TPU v7x, 32 devices: a whole 2x2x4 slice. The times are simulated.
32 devices in a mesh: groups: 2 (over x), dp: 16 (over z, y, core).
Axes of the slice: x: 2, y: 2, z: 4, core: 2. Of those that a mesh axis runs over, the one named last changes fastest.
Arguments:
- activations: bfloat16 [8192, 8192], P(('groups', 'dp')), parts along dimension 0, may hold values from -6 to 6
- key_grad: bfloat16 [8192, 1024], P(('groups', 'dp')), parts along dimension 0
- proj_basis: bfloat16 [16384, 512], P(('groups', 'dp')), parts along dimension 0
- master_weight: float32 [16384, 1024], P(('groups', 'dp')), parts along dimension 0, may hold values from -0.0625 to 0.0625
- first_moment: float32 [1024, 1024], P(('groups', 'dp')), parts along dimension 0, may hold values from -3 to 3
- second_moment: float32 [1024, 1024], P(('groups', 'dp')), parts along dimension 0, may hold values from 0.1 to 1
Outputs:
- activation_grad: bfloat16 [8192, 8192], P(('groups', 'dp')), parts along dimension 0
- new_master: float32 [16384, 1024], P(('groups', 'dp')), parts along dimension 0
- new_first: float32 [1024, 1024], P(('groups', 'dp')), parts along dimension 0
- new_second: float32 [1024, 1024], P(('groups', 'dp')), parts along dimension 0
There are 2 independent parts, one for each index of `groups`. A program takes and returns all parts, laid end to end along the dimension named above; each array names one. Nothing has to cross between parts.
All inputs are finite; a program needn't handle non-finite values.
Results may differ from a plain program's by a relative error of at most 0.0049.
Values may be sent and summed in bfloat16 or wider, within the bound.
No kernel may reach another device: no remote copies, remote signals or barrier semaphores. Data moves between devices by JAX's collectives and lax.ppermute only.
A program may use at most 128 MiB of HBM per device.

v0:
```python
import jax
import jax.numpy as jnp
from jax import lax
from jax.sharding import PartitionSpec as P

clip_total = 512.0
step_size = 0.01
first_fix = 1.0 - 0.9**10
second_fix = 1.0 - 0.99**10


def per_device(activations, key_grad, proj_basis, master_weight, first_moment, second_moment):
    weight_bf16 = master_weight.astype(jnp.bfloat16)
    grad_cols = jnp.dot(
        key_grad,
        lax.all_gather(weight_bf16, "dp", axis=0, tiled=True).T,
        preferred_element_type=jnp.float32,
    ).astype(jnp.bfloat16)
    projected_sum = jnp.dot(
        activations,
        lax.all_gather(proj_basis, "dp", axis=0, tiled=True),
        preferred_element_type=jnp.float32,
    )
    projected = projected_sum.astype(jnp.bfloat16)
    partial_grad = lax.dot_general(
        projected, key_grad, (((0,), (0,)), ((), ())), preferred_element_type=jnp.float32
    )
    owned_rows = lax.psum_scatter(partial_grad, "dp", scatter_dimension=0, tiled=True)
    square_sum = lax.psum(jnp.sum(owned_rows * owned_rows), "dp")
    grad_norm = jnp.sqrt(square_sum)
    factor = jnp.minimum(1.0, clip_total / (grad_norm + 1e-06))
    clipped = owned_rows * factor
    new_first = 0.9 * first_moment + 0.1 * clipped
    new_second = 0.99 * second_moment + 0.01 * clipped * clipped
    update = new_first / first_fix / (jnp.sqrt(new_second / second_fix) + 1e-08)
    basis_float = proj_basis.astype(jnp.float32)
    back_step = jnp.zeros(master_weight.shape, jnp.float32) + jnp.dot(
        basis_float,
        lax.all_gather(update.astype(jnp.bfloat16), "dp", axis=0, tiled=True).astype(jnp.float32),
        precision=lax.Precision.HIGHEST,
    )
    new_master = master_weight - step_size * back_step
    return (grad_cols, new_master, new_first, new_second)


def solution(mesh):
    placed = (
        P(("groups", "dp"), None),
        P(("groups", "dp"), None),
        P(("groups", "dp"), None),
        P(("groups", "dp"), None),
        P(("groups", "dp"), None),
        P(("groups", "dp"), None),
    )
    return jax.shard_map(
        per_device,
        mesh=mesh,
        in_specs=placed,
        out_specs=(
            P(("groups", "dp"), None),
            P(("groups", "dp"), None),
            P(("groups", "dp"), None),
            P(("groups", "dp"), None),
        ),
        check_vma=False,
    )
```

profile of v0, /device:TPU:0, one launch (start us, length us, event | category | flops | bytes accessed | tf_op | source)
XLA Modules:
  0.0 370.6 jit_solution(156581201575859890)
XLA Ops:
  7.2 0.0 copy-start
  7.2 0.0 all-gather.6.cloned.1.call-start
  7.2 0.7 all-gather.6.cloned.1.call-update
  7.9 0.0 copy-start.3
  7.9 0.0 copy-start.4
  7.9 0.0 reduce-scatter.2.cloned.1.call-start
  8.0 79.8 %all-gather.6.cloned.1.call-done = bf16[8192,512]{1,0:T(8,128)(2,1)} async-done(((bf16[512,512]{1,0:T(8,128)(2,1)}), bf16[8192,512]{1,0:T(8,128)(2,1)}) %all-gather.6.cloned.1.call-update) | async-done | bytes 8388624 | tf_op jit(solution)/shard_map/all_gather | solution.py:21
  87.8 0.0 copy-done
  87.8 8.8 %fusion = f32[512,1024]{1,0:T(8,128)} fusion(bf16[256,1024]{1,0:T(8,128)(2,1)S(1)} %copy-done, bf16[256,8192]{1,0:T(8,128)(2,1)} %param.6, bf16[8192,512]{1,0:T(8,128)(2,1)} %all-gather.6.cloned.1.call-done), kind=kOutput, calls=%fused_computation.3 | convolution fusion | flops 2416050176 | bytes 15204352 | tf_op jit(solution)/shard_map/dot_general | solution.py:25
  96.6 0.0 copy-start.1
  96.6 0.0 reduce-scatter.2.cloned.1.call-update
  96.6 0.0 all-gather.8.cloned.1.call-start
  96.6 59.9 %reduce-scatter.2.cloned.1.call-done = f32[32,1024]{1,0:T(8,128)} async-done(((f32[512,1024]{1,0:T(8,128)}), f32[32,1024]{1,0:T(8,128)}) %reduce-scatter.2.cloned.1.call-update) | async-done | bytes 131088 | tf_op jit(solution)/shard_map/reduce_scatter | solution.py:28
  156.6 1.5 multiply_reduce_fusion
  158.1 30.1 %psum.7 = f32[]{:T(128)} all-reduce(f32[]{:T(128)} %multiply_reduce_fusion), channel_id=1, replica_groups=mesh['groups'=2,'dp'=16] {'dp'}, use_global_device_ids=true, to_apply=%region_2.0 | all-reduce | flops 1 | bytes 8 | tf_op jit(solution)/shard_map/psum | solution.py:29
  189.0 0.0 copy-done.3
  189.0 0.0 copy-done.4
  189.0 1.7 divide_convert_fusion
  190.6 0.0 all-gather.8.cloned.1.call-update
  190.7 0.0 copy-start.2
  190.7 0.0 all-gather.4.cloned.1.call-start
  190.7 0.0 copy-done.1
  190.7 1.1 convert_element_type.14
  191.9 0.0 all-gather.4.cloned.1.call-update
  191.9 1.8 copy.10
  193.7 32.3 %all-gather.8.cloned.1.call-done = bf16[512,1024]{1,0:T(8,128)(2,1)} async-done(((bf16[32,1024]{1,0:T(8,128)(2,1)}), bf16[512,1024]{1,0:T(8,128)(2,1)}) %all-gather.8.cloned.1.call-update) | async-done | bytes 1048592 | tf_op jit(solution)/shard_map/all_gather | solution.py:39
  226.0 0.0 copy-done.2
  226.0 2.7 bitcast_subtract_fusion
  228.7 1.8 copy.11
  230.5 124.2 %all-gather.4.cloned.1.call-done = bf16[8192,1024]{1,0:T(8,128)(2,1)} async-done(((bf16[512,1024]{1,0:T(8,128)(2,1)}), bf16[8192,1024]{1,0:T(8,128)(2,1)}) %all-gather.4.cloned.1.call-update) | async-done | bytes 16777232 | tf_op jit(solution)/shard_map/all_gather | solution.py:16
  354.6 9.5 %convolution_convert_fusion = bf16[256,8192]{1,0:T(8,128)(2,1)} fusion(bf16[256,1024]{1,0:T(8,128)(2,1)S(1)} %copy-done, bf16[8192,1024]{1,0:T(8,128)(2,1)} %all-gather.4.cloned.1.call-done), kind=kOutput, calls=%fused_computation | convolution fusion | flops 4297064448 | bytes 21495808 | tf_op jit(solution)/shard_map/dot_general | solution.py:14
Async XLA Ops:
  7.2 80.6 %copy-start = (bf16[256,1024]{1,0:T(8,128)(2,1)S(1)}, bf16[256,1024]{1,0:T(8,128)(2,1)}, u32[]{:S(2)}) copy-start(bf16[256,1024]{1,0:T(8,128)(2,1)} %param.7) | copy-start | bytes 1572868
  7.2 80.6 %all-gather.6.cloned.1.call-start = ((), (), s32[]{:S(2)}) async-start(), calls=%async_computation.2 | async-start | bytes 8912896 | tf_op jit(solution)/shard_map/all_gather | solution.py:21
  7.9 181.0 %copy-start.3 = (f32[32,1024]{1,0:T(8,128)S(1)}, f32[32,1024]{1,0:T(8,128)}, u32[]{:S(2)}) copy-start(f32[32,1024]{1,0:T(8,128)} %param.10) | copy-start | bytes 393220
  7.9 181.0 %copy-start.4 = (f32[32,1024]{1,0:T(8,128)S(1)}, f32[32,1024]{1,0:T(8,128)}, u32[]{:S(2)}) copy-start(f32[32,1024]{1,0:T(8,128)} %param.11) | copy-start | bytes 393220
  7.9 148.6 %reduce-scatter.2.cloned.1.call-start = ((), (), s32[]{:S(2)}) async-start(), calls=%async_computation.3 | async-start | bytes 2228224 | tf_op jit(solution)/shard_map/reduce_scatter | solution.py:28
  96.6 94.2 %copy-start.1 = (f32[512,1024]{1,0:T(8,128)S(1)}, f32[512,1024]{1,0:T(8,128)}, u32[]{:S(2)}) copy-start(f32[512,1024]{1,0:T(8,128)} %param.9) | copy-start | bytes 6291460
  96.6 129.4 %all-gather.8.cloned.1.call-start = ((), (), s32[]{:S(2)}) async-start(), calls=%async_computation.4 | async-start | bytes 1114112 | tf_op jit(solution)/shard_map/all_gather | solution.py:39
  190.7 35.3 %copy-start.2 = (bf16[512,512]{1,0:T(8,128)(2,1)S(1)}, bf16[512,512]{1,0:T(8,128)(2,1)}, u32[]{:S(2)}) copy-start(bf16[512,512]{1,0:T(8,128)(2,1)} %param.8) | copy-start | bytes 1572868
  190.7 164.0 %all-gather.4.cloned.1.call-start = ((), (), s32[]{:S(2)}) async-start(), calls=%async_computation.1 | async-start | bytes 17825792 | tf_op jit(solution)/shard_map/all_gather | solution.py:16
Sparse Core Ops, SparseCore 0:
  10.2 77.5 all-gather.5
  96.7 59.8 reduce-scatter.1
  190.8 35.1 all-gather.7
  228.8 125.7 all-gather.3
where the time goes:
time: 371 us
  waiting for transfers between devices  297 us (80%)
  blocking collectives  30.1 us (8%)
  matrix products  20.9 us (6%)
  between operations  14.6 us (4%)
  other arithmetic  4.34 us (1%)
    all_gather x1, waiting for transfers between devices, per_device(): lax.all_gather(weight_bf16, 'dp', axis=0, tiled=True)  124 us
    all_gather x1, waiting for transfers between devices, per_device(): lax.all_gather(proj_basis, 'dp', axis=0, tiled=True)  79.8 us
    reduce_scatter x1, waiting for transfers between devices, per_device(): lax.psum_scatter(partial_grad, 'dp', scatter_dimension=0, tiled=True)  59.9 us
    all_gather x1, waiting for transfers between devices, per_device(): lax.all_gather(update.astype(jnp.bfloat16), 'dp', axis=0, tiled=True)  32.3 us
    psum x1, blocking collectives, per_device(): square_sum = lax.psum(jnp.sum(owned_rows * owned_rows), 'dp')  30.1 us
    dot_general x1, matrix products, per_device(): jnp.dot(key_grad, lax.all_gather(weight_bf16, 'dp', axis=0, tiled=True).T...  9.46 us
    dot_general x1, matrix products, per_device(): lax.dot_general(projected, key_grad, (((0,), (0,)), ((), ())), preferred_...  8.75 us
  transfers between devices with their start and end apart: 4, of which 4 were waited for; matrix products, arithmetic and copies ran while one was open for 2% of the time, Pallas kernels for 0%

commit v1 on v0

v1 whole, which is shorter than its diff:
```python
import jax
import jax.numpy as jnp
from jax import lax
from jax.sharding import PartitionSpec as P

clip_total = 512.0
step_size = 0.01
first_fix = 1.0 - 0.9**10
second_fix = 1.0 - 0.99**10

f32 = jnp.float32
bf16 = jnp.bfloat16


def after(value, *others):
    return lax.optimization_barrier((value,) + others)[0]


def make_per_device(n):
    members = 4 if n == 16 else 2
    ring = n // members
    order = [0, 1, 3, 2] if ring == 4 else list(range(ring))
    forward = [
        (order[k] * members + m, order[(k + 1) % ring] * members + m)
        for k in range(ring)
        for m in range(members)
    ]

    def send_xor(value, bit):
        return lax.ppermute(value, "dp", [(i, i ^ bit) for i in range(n)])

    def per_device(activations, key_grad, proj_basis, master_weight, first_moment, second_moment):
        tokens, width = activations.shape
        rows, rank = proj_basis.shape
        outs = key_grad.shape[1]
        index = lax.axis_index("dp")
        member = index % members
        place = jnp.asarray([order.index(z) for z in range(ring)], jnp.int32)[index // members]
        source = [
            jnp.asarray(order, jnp.int32)[(place - s + ring) % ring] for s in range(ring)
        ]

        if members == 4:
            far = send_xor(key_grad, 2)
            near = send_xor(jnp.concatenate([key_grad, far], axis=0), 1)
            plane_grad = jnp.concatenate(
                [key_grad, near[:tokens], far, near[tokens:]], axis=0
            )
        else:
            plane_grad = jnp.concatenate([key_grad, send_xor(key_grad, 1)], axis=0)

        def columns(m):
            return jnp.concatenate(
                [
                    lax.dynamic_slice(
                        activations, (0, (source[s] * members + m) * rows), (tokens, rows)
                    )
                    for s in range(ring)
                ],
                axis=1,
            )

        plane_act = [columns(member)]
        for x in range(1, members):
            plane_act.append(send_xor(columns(member ^ x), x))
        plane_act = jnp.concatenate(plane_act, axis=0)

        basis = [proj_basis]
        for s in range(1, ring):
            basis.append(lax.ppermute(basis[-1], "dp", forward))
        ring_basis = jnp.concatenate(basis, axis=0)

        projected = jnp.dot(plane_act, ring_basis, preferred_element_type=f32).astype(bf16)
        partial_grad = lax.dot_general(
            projected, plane_grad, (((0,), (0,)), ((), ())), preferred_element_type=f32
        )

        weight = master_weight.astype(bf16)
        weight = after(weight, basis[ring - 2])
        activation_grad = jnp.zeros((tokens, width), bf16)
        for s in range(ring):
            if s > 0:
                weight = lax.ppermute(weight, "dp", forward)
            block = lax.dot_general(
                plane_grad, weight, (((1,), (1,)), ((), ())), preferred_element_type=f32
            ).astype(bf16)
            for x in range(members):
                piece = block[x * tokens : (x + 1) * tokens]
                if x > 0:
                    piece = send_xor(piece, x)
                activation_grad = lax.dynamic_update_slice(
                    activation_grad, piece, (0, (source[s] * members + (member ^ x)) * rows)
                )

        owned = rank // n
        bits = [1 << b for b in range(n.bit_length() - 1)]
        total = partial_grad.reshape(n, owned, outs)
        for bit in bits:
            mine = (index // bit) % 2
            total = total.reshape(total.shape[0] // 2, 2, owned, outs)
            kept = lax.dynamic_index_in_dim(total, mine, 1, keepdims=False)
            given = lax.dynamic_index_in_dim(total, 1 - mine, 1, keepdims=False)
            total = kept + send_xor(given.astype(bf16), bit).astype(f32)
        owned_rows = total.reshape(owned, outs)

        square_sum = jnp.broadcast_to(jnp.sum(owned_rows * owned_rows), (8, 128))
        for bit in reversed(bits):
            square_sum = square_sum + send_xor(square_sum, bit)
        grad_norm = jnp.sqrt(square_sum[0, 0])
        factor = jnp.minimum(1.0, clip_total / (grad_norm + 1e-06))
        clipped = owned_rows * factor
        new_first = 0.9 * first_moment + 0.1 * clipped
        new_second = 0.99 * second_moment + 0.01 * clipped * clipped
        update = new_first / first_fix / (jnp.sqrt(new_second / second_fix) + 1e-08)

        whole = update.astype(bf16).reshape(1, owned, outs)
        for bit in reversed(bits):
            other = send_xor(whole, bit)
            pair = jnp.where(
                (index // bit) % 2 == 0,
                jnp.stack([whole, other], axis=1),
                jnp.stack([other, whole], axis=1),
            )
            whole = pair.reshape(2 * whole.shape[0], owned, outs)
        back_step = jnp.dot(
            proj_basis, whole.reshape(rank, outs), preferred_element_type=f32
        )
        new_master = master_weight - step_size * back_step
        return (activation_grad, new_master, new_first, new_second)

    return per_device


def solution(mesh):
    spec = P(("groups", "dp"), None)
    return jax.shard_map(
        make_per_device(mesh.shape["dp"]),
        mesh=mesh,
        in_specs=(spec,) * 6,
        out_specs=(spec,) * 4,
        check_vma=False,
    )
```

time: 371 us -> 203 us (0.55)
  waiting for transfers between devices: 297 us -> 102 us
  local copies, waits for them, and re-layouts: 3.66 us -> 36.4 us
  blocking collectives: 30.1 us -> 0 us
  starting transfers between devices: 0.16 us -> 26.9 us
  between operations: 14.6 us -> 7.1 us
  other arithmetic: 4.34 us -> 9.85 us
    all_gather x3 -> x0, waiting for transfers between devices: 236 us -> none  [the longest x1 124 us: per_device(): lax.all_gather(weight_bf16, 'dp', axis=0, tiled=True)]
    ppermute x0 -> x35, waiting for transfers between devices: none -> 102 us  [the longest x29 78.1 us: send_xor(): return lax.ppermute(value, 'dp', [(i, i ^ bit) for i in range(n)])]
    reduce_scatter x1 -> x0, waiting for transfers between devices: 59.9 us -> none  [per_device(): lax.psum_scatter(partial_grad, 'dp', scatter_dimension=0, tiled=True)]
    psum x1 -> x0, blocking collectives: 30.1 us -> none  [per_device(): square_sum = lax.psum(jnp.sum(owned_rows * owned_rows), 'dp')]
    ppermute x0 -> x35, starting transfers between devices: none -> 26.9 us  [the longest x29 20.3 us: send_xor(): return lax.ppermute(value, 'dp', [(i, i ^ bit) for i in range(n)])]
    dynamic_update_slice x0 -> x12, local copies, waits for them, and re-layouts: none -> 14.5 us  [per_device(): lax.dynamic_update_slice(activation_grad, piece, (0, (source[s] * members...]
    slice x0 -> x6, local copies, waits for them, and re-layouts: none -> 6.74 us  [the longest x4 3.55 us: per_device(): piece = block[x * tokens:(x + 1) * tokens]]
    dynamic_slice x0 -> x3, local copies, waits for them, and re-layouts: none -> 6.16 us  [the longest x1 3.51 us: columns(): lax.dynamic_slice(activations, (0, (source[s] * members + m) * rows), (to...]
  transfers between devices with their start and end apart: 4 -> 35, of which waited for: 4 -> 20; matrix products, arithmetic and copies ran while one was open for 2% -> 26% of each run, Pallas kernels for 0% -> 0%
where the time goes in v1:
time: 203 us
  waiting for transfers between devices  102 us (50%)
  local copies, waits for them, and re-layouts  36.4 us (18%)
  starting transfers between devices  26.9 us (13%)
  matrix products  20.1 us (10%)
  other arithmetic  9.85 us (5%)
  between operations  7.1 us (3%)
    ppermute x29, waiting for transfers between devices, send_xor(): return lax.ppermute(value, 'dp', [(i, i ^ bit) for i in range(n)])  78.1 us
    ppermute x3, waiting for transfers between devices, per_device(): basis.append(lax.ppermute(basis[-1], 'dp', forward))  23.3 us
    ppermute x29, starting transfers between devices, send_xor(): return lax.ppermute(value, 'dp', [(i, i ^ bit) for i in range(n)])  20.3 us
    dynamic_update_slice x12, local copies, waits for them, and re-layouts, per_device(): lax.dynamic_update_slice(activation_grad, piece, (0, (source[s] * members...  14.5 us
    dot_general x4, matrix products, per_device(): lax.dot_general(plane_grad, weight, (((1,), (1,)), ((), ())), preferred_e...  11.3 us
    dot_general x1, matrix products, per_device(): lax.dot_general(projected, plane_grad, (((0,), (0,)), ((), ())), preferre...  8.06 us
  transfers between devices with their start and end apart: 35, of which 20 were waited for; matrix products, arithmetic and copies ran while one was open for 26% of the time, Pallas kernels for 0%

profile of v1, /device:TPU:0, one launch (start us, length us, event | category | flops | bytes accessed | tf_op | source)
XLA Modules:
  0.0 202.5 jit_solution(2209734477026991128)
XLA Ops:
  0.6 3.0 %collective-permute-start = (bf16[256,1024]{1,0:T(8,128)(2,1)}, bf16[256,1024]{1,0:T(8,128)(2,1)S(1)}, u32[]{:S(2)}, u32[]{:S(2)}) collective-permute-start(bf16[256,1024]{1,0:T(8,128)(2,1)} %param.12), channel_id=1, source_target_pairs={{0,2},{1,3},{2,0},{3,1},{4,6},{5,7},{6,4},{7,5},{8,10},{9,11},{10,... | collective-permute-start | bytes 1572872 | tf_op jit(solution)/shard_map/ppermute | solution.py:30
  3.7 1.2 dynamic_slice.87
  7.6 1.4 fusion.45
  11.7 3.5 %constant_dynamic-slice_fusion.15 = (bf16[256,512]{1,0:T(8,128)(2,1)S(1)}, bf16[256,512]{1,0:T(8,128)(2,1)S(1)}, bf16[256,512]{1,0:T(8,128)(2,1)S(1)}, bf16[256,...) fusion(bf16[256,8192]{1,0:T(8,128)(2,1)} %param.11, ...), kind=kLoop, calls=%fused_computation.74 | loop fusion | bytes 8388672 | tf_op jit(solution)/shard_map/dynamic_slice | solution.py:55
  16.4 1.6 collective-permute-start.2
  22.0 9.6 %collective-permute-done.2 = bf16[512,512]{1,0:T(8,128)(2,1)S(1)} collective-permute-done((bf16[512,512]{1,0:T(8,128)(2,1)S(1)}, bf16[512,512]{1,0:T(8,128)(2,1)S(1)}, u32[]{:S(2)}, u32[]{:S(2)}) %collective-permute-start.2) | collective-permute-done | bytes 524320 | tf_op jit(solution)/shard_map/ppermute | solution.py:70
  32.4 13.8 %collective-permute-done.3 = bf16[512,512]{1,0:T(8,128)(2,1)} collective-permute-done((bf16[512,512]{1,0:T(8,128)(2,1)S(1)}, bf16[512,512]{1,0:T(8,128)(2,1)}, u32[]{:S(2)}, u32[]{:S(2)}) %collective-permute-start.3) | collective-permute-done | bytes 524320 | tf_op jit(solution)/shard_map/ppermute | solution.py:70
  47.1 2.7 %fusion.44 = (bf16[256,1024]{1,0:T(8,128)(2,1)}, bf16[256,1024]{1,0:T(8,128)(2,1)}) fusion(bf16[512,1024]{1,0:T(8,128)(2,1)} %collective-permute-done.1), kind=kLoop, calls=%fused_computation.93 | loop fusion | bytes 2097152 | tf_op jit(solution)/shard_map/slice | solution.py:47
  49.7 18.2 %collective-permute-done.21 = bf16[256,2048]{1,0:T(8,128)(2,1)} collective-permute-done((bf16[256,2048]{1,0:T(8,128)(2,1)}, bf16[256,2048]{1,0:T(8,128)(2,1)}, u32[]{:S(2)}, u32[]{:S(2)}) %collective-permute-start.21) | collective-permute-done | bytes 1048608 | tf_op jit(solution)/shard_map/ppermute | solution.py:30
  67.9 8.1 %fusion.28 = f32[512,1024]{1,0:T(8,128)} fusion(bf16[512,512]{1,0:T(8,128)(2,1)} %collective-permute-done.22, bf16[512,512]{1,0:T(8,128)(2,1)} %collective-permute-done.3, bf16[512,512]{1,0:T(8,128)(2,1)} %copy-done.14, bf16[512,512]{1,0:T(8,128)(2,1)} %param.13, bf16[256,2048]{1,0:T(8,128)(2,1)} %collective-permute-done.21, ...), kind=kOutput, calls=%fused_computation.35 | convolution fusion | flops 3267887104 | bytes 10485760 | tf_op jit(solution)/shard_map/dot_general | solution.py:74
  76.0 1.3 fusion.31
  77.8 2.8 %convolution_convert_fusion.3 = bf16[1024,512]{1,0:T(8,128)(2,1)S(1)} fusion(bf16[512,1024]{1,0:T(8,128)(2,1)S(1)} %convert_element_type.56, bf16[256,1024]{1,0:T(8,128)(2,1)} %get-tuple-element.58, bf16[256,1024]{1,0:T(8,128)(2,1)} %copy-done.7, bf16[256,1024]{1,0:T(8,128)(2,1)} %get-tuple-element.57, bf16[256,1024]{1,0:T(8,128)(2,1)} %param.12), kind=kOutput, calls=%fused_computation.27 | convolution fusion | flops 1082654720 | bytes 4194304 | tf_op jit(solution)/shard_map/dot_general | solution.py:84
  80.6 2.5 %broadcast_in_dim.6 = bf16[256,8192]{1,0:T(8,128)(2,1)} broadcast(bf16[]{:T(256)} %constant.169.clone.1), dimensions={} | broadcast | bytes 4194306 | tf_op jit(solution)/shard_map/broadcast_in_dim | solution.py:80
  85.5 2.6 %collective-permute-start.7 = (bf16[512,1024]{1,0:T(8,128)(2,1)}, bf16[512,1024]{1,0:T(8,128)(2,1)}, u32[]{:S(2)}, u32[]{:S(2)}) collective-permute-start(bf16[512,1024]{1,0:T(8,128)(2,1)} %copy-done.3), channel_id=1, source_target_pairs={{0,4},{1,5},{2,6},{3,7},{4,12},{5,13},{6,14},{7,15},{12,8},{13,9},... | collective-permute-start | bytes 3145736 | tf_op jit(solution)/shard_map/ppermute | solution.py:83
  88.1 1.5 collective-permute-start.5
  89.6 1.7 constant_dynamic-update-slice_fusion.11
  91.3 3.1 %collective-permute-done.24 = bf16[4,32,1024]{2,1,0:T(8,128)(2,1)} collective-permute-done((bf16[4,32,1024]{2,1,0:T(8,128)(2,1)}, bf16[4,32,1024]{2,1,0:T(8,128)(2,1)}, u32[]{:S(2)}, u32[]{:S(2)}) %collective-permute-start.24) | collective-permute-done | bytes 262176 | tf_op jit(solution)/shard_map/ppermute | solution.py:30
  95.5 2.7 %collective-permute-start.25 = (bf16[2,32,1024]{2,1,0:T(8,128)(2,1)S(1)}, bf16[2,32,1024]{2,1,0:T(8,128)(2,1)S(1)}, u32[]{:S(2)}, u32[]{:S(2)}) collective-permute-start(bf16[2,32,1024]{2,1,0:T(8,128)(2,1)S(1)} %fusion.34), channel_id=1, source_target_pairs={{0,4},{1,5},{2,6},{3,7},{4,0},{5,1},{6,2},{7,3},{8,12},{9,13},{10,... | collective-permute-start | bytes 393224 | tf_op jit(solution)/shard_map/ppermute | solution.py:30
  98.1 1.8 collective-permute-done.5
  100.6 4.0 %collective-permute-done.6 = bf16[256,512]{1,0:T(8,128)(2,1)S(1)} collective-permute-done((bf16[256,512]{1,0:T(8,128)(2,1)S(1)}, bf16[256,512]{1,0:T(8,128)(2,1)S(1)}, u32[]{:S(2)}, u32[]{:S(2)}) %collective-permute-start.6) | collective-permute-done | bytes 262176 | tf_op jit(solution)/shard_map/ppermute | solution.py:30
  105.4 9.3 %collective-permute-done.25 = bf16[2,32,1024]{2,1,0:T(8,128)(2,1)S(1)} collective-permute-done((bf16[2,32,1024]{2,1,0:T(8,128)(2,1)S(1)}, bf16[2,32,1024]{2,1,0:T(8,128)(2,1)S(1)}, u32[]{:S(2)}, u32[]{:S(2)}) %collective-permute-start.25) | collective-permute-done | bytes 131104 | tf_op jit(solution)/shard_map/ppermute | solution.py:30
  115.6 3.1 %convolution_convert_fusion.2 = bf16[1024,512]{1,0:T(8,128)(2,1)S(1)} fusion(bf16[512,1024]{1,0:T(8,128)(2,1)} %collective-permute-done.7, bf16[256,1024]{1,0:T(8,128)(2,1)} %get-tuple-element.58, bf16[256,1024]{1,0:T(8,128)(2,1)} %copy-done.7, bf16[256,1024]{1,0:T(8,128)(2,1)} %get-tuple-element.57, bf16[256,1024]{1,0:T(8,128)(2,1)} %param.12), kind=kOutput, calls=%fused_computation.26 | convolution fusion | flops 1082654720 | bytes 4194304 | tf_op jit(solution)/shard_map/dot_general | solution.py:84
  118.7 1.7 collective-permute-done.26
  123.2 3.0 %collective-permute-done.27 = f32[8,128]{1,0:T(8,128)S(1)} collective-permute-done((f32[8,128]{1,0:T(8,128)S(1)}, f32[8,128]{1,0:T(8,128)S(1)}, u32[]{:S(2)}, u32[]{:S(2)}) %collective-permute-start.27) | collective-permute-done | bytes 4128 | tf_op jit(solution)/shard_map/ppermute | solution.py:30
  126.9 1.3 collective-permute-start.28
  129.0 1.6 collective-permute-done.28
  131.3 2.0 collective-permute-start.29
  133.4 1.7 collective-permute-done.29
  135.4 1.7 constant_dynamic-update-slice_fusion.8
  138.3 1.8 divide_convert_fusion
  140.9 1.3 collective-permute-done.9
  142.9 13.0 %collective-permute-done.31 = bf16[1,32,1024]{2,1,0:T(8,128)(2,1)S(1)} collective-permute-done((bf16[1,32,1024]{2,1,0:T(8,128)(2,1)S(1)}, bf16[1,32,1024]{2,1,0:T(8,128)(2,1)S(1)}, u32[]{:S(2)}, u32[]{:S(2)}) %collective-permute-start.31) | collective-permute-done | bytes 65568 | tf_op jit(solution)/shard_map/ppermute | solution.py:30
  156.7 4.2 %collective-permute-done.32 = bf16[2,32,1024]{2,1,0:T(8,128)(2,1)S(1)} collective-permute-done((bf16[2,32,1024]{2,1,0:T(8,128)(2,1)S(1)}, bf16[2,32,1024]{2,1,0:T(8,128)(2,1)S(1)}, u32[]{:S(2)}, u32[]{:S(2)}) %collective-permute-start.32) | collective-permute-done | bytes 131104 | tf_op jit(solution)/shard_map/ppermute | solution.py:30
  161.0 1.4 collective-permute-start.33
  162.6 2.8 %convolution_convert_fusion.1 = bf16[1024,512]{1,0:T(8,128)(2,1)S(1)} fusion(bf16[512,1024]{1,0:T(8,128)(2,1)} %collective-permute-done.11, bf16[256,1024]{1,0:T(8,128)(2,1)} %get-tuple-element.58, bf16[256,1024]{1,0:T(8,128)(2,1)S(1)} %copy-done.8, bf16[256,1024]{1,0:T(8,128)(2,1)} %get-tuple-element.57, bf16[256,1024]{1,0:T(8,128)(2,1)S(1)} %copy-done.5), kind=kOutput, calls=%fused_computation.25 | convolution fusion | flops 1082654720 | bytes 4194304 | tf_op jit(solution)/shard_map/dot_general | solution.py:84
  167.6 1.4 collective-permute-start.13
  169.5 1.8 copy.34
  171.3 1.8 constant_dynamic-update-slice_fusion.5
  173.1 4.0 %collective-permute-done.13 = bf16[256,512]{1,0:T(8,128)(2,1)} collective-permute-done((bf16[256,512]{1,0:T(8,128)(2,1)}, bf16[256,512]{1,0:T(8,128)(2,1)}, u32[]{:S(2)}, u32[]{:S(2)}) %collective-permute-start.13) | collective-permute-done | bytes 262176 | tf_op jit(solution)/shard_map/ppermute | solution.py:30
  177.1 1.7 constant_dynamic-update-slice_fusion.4
  178.8 3.0 %collective-permute-done.14 = bf16[256,512]{1,0:T(8,128)(2,1)} collective-permute-done((bf16[256,512]{1,0:T(8,128)(2,1)S(1)}, bf16[256,512]{1,0:T(8,128)(2,1)}, u32[]{:S(2)}, u32[]{:S(2)}) %collective-permute-start.14) | collective-permute-done | bytes 262176 | tf_op jit(solution)/shard_map/ppermute | solution.py:30
  181.8 1.7 constant_dynamic-update-slice_fusion.3
  184.5 2.6 %convolution_convert_fusion = bf16[1024,512]{1,0:T(8,128)(2,1)S(1)} fusion(bf16[512,1024]{1,0:T(8,128)(2,1)} %collective-permute-done.15, bf16[256,1024]{1,0:T(8,128)(2,1)S(1)} %copy-done.11, bf16[256,1024]{1,0:T(8,128)(2,1)S(1)} %copy-done.9, bf16[256,1024]{1,0:T(8,128)(2,1)S(1)} %copy-done.10, bf16[256,1024]{1,0:T(8,128)(2,1)S(1)} %copy-done.6), kind=kOutput, calls=%fused_computation.24 | convolution fusion | flops 1082654720 | bytes 4194304 | tf_op jit(solution)/shard_map/dot_general | solution.py:84
  187.9 1.3 collective-permute-start.17
  190.5 1.8 copy.35
  192.3 1.7 constant_dynamic-update-slice_fusion.2
  194.0 3.0 %collective-permute-done.17 = bf16[256,512]{1,0:T(8,128)(2,1)S(1)} collective-permute-done((bf16[256,512]{1,0:T(8,128)(2,1)S(1)}, bf16[256,512]{1,0:T(8,128)(2,1)S(1)}, u32[]{:S(2)}, u32[]{:S(2)}) %collective-permute-start.17) | collective-permute-done | bytes 262176 | tf_op jit(solution)/shard_map/ppermute | solution.py:30
  197.7 4.1 %collective-permute-done.18 = bf16[256,512]{1,0:T(8,128)(2,1)S(1)} collective-permute-done((bf16[256,512]{1,0:T(8,128)(2,1)S(1)}, bf16[256,512]{1,0:T(8,128)(2,1)S(1)}, u32[]{:S(2)}, u32[]{:S(2)}) %collective-permute-start.18) | collective-permute-done | bytes 262176 | tf_op jit(solution)/shard_map/ppermute | solution.py:30
  (109 shorter events, 28.8 us)
Async XLA Ops:
  0.6 17.3 %collective-permute-start = (bf16[256,1024]{1,0:T(8,128)(2,1)}, bf16[256,1024]{1,0:T(8,128)(2,1)S(1)}, u32[]{:S(2)}, u32[]{:S(2)}) collective-permute-start(bf16[256,1024]{1,0:T(8,128)(2,1)} %param.12), channel_id=1, source_target_pairs={{0,2},{1,3},{2,0},{3,1},{4,6},{5,7},{6,4},{7,5},{8,10},{9,11},{10,... | collective-permute-start | bytes 1572872 | tf_op jit(solution)/shard_map/ppermute | solution.py:30
  11.7 6.2 %copy-start.4 = (bf16[256,1024]{1,0:T(8,128)(2,1)S(1)}, bf16[256,1024]{1,0:T(8,128)(2,1)}, u32[]{:S(2)}) copy-start(bf16[256,1024]{1,0:T(8,128)(2,1)} %param.12) | copy-start | bytes 1572868
  15.2 31.6 %copy-start = (f32[512,1024]{1,0:T(8,128)S(1)}, f32[512,1024]{1,0:T(8,128)}, u32[]{:S(2)}) copy-start(f32[512,1024]{1,0:T(8,128)} %param.14) | copy-start | bytes 6291460
  16.4 33.4 %collective-permute-start.19 = (bf16[256,2048]{1,0:T(8,128)(2,1)}, bf16[256,2048]{1,0:T(8,128)(2,1)}, u32[]{:S(2)}, u32[]{:S(2)}) collective-permute-start(bf16[256,2048]{1,0:T(8,128)(2,1)} %pad_maximum_fusion.2), channel_id=1, source_target_pairs={{0,1},{1,0},{2,3},{3,2},{4,5},{5,4},{6,7},{7,6},{8,9},{9,8},{10,11... | collective-permute-start | bytes 3145736 | tf_op jit(solution)/shard_map/ppermute | solution.py:30
  16.4 15.2 %collective-permute-start.2 = (bf16[512,512]{1,0:T(8,128)(2,1)S(1)}, bf16[512,512]{1,0:T(8,128)(2,1)S(1)}, u32[]{:S(2)}, u32[]{:S(2)}) collective-permute-start(bf16[512,512]{1,0:T(8,128)(2,1)S(1)} %copy-done.12), channel_id=1, source_target_pairs={{0,4},{1,5},{2,6},{3,7},{4,12},{5,13},{6,14},{7,15},{12,8},{13,9},... | collective-permute-start | bytes 1572872 | tf_op jit(solution)/shard_map/ppermute | solution.py:70
  17.9 28.9 %copy-start.7 = (bf16[256,1024]{1,0:T(8,128)(2,1)}, bf16[256,1024]{1,0:T(8,128)(2,1)S(1)}, u32[]{:S(2)}) copy-start(bf16[256,1024]{1,0:T(8,128)(2,1)S(1)} %collective-permute-done) | copy-start | bytes 1572868
  19.1 28.0 %collective-permute-start.1 = (bf16[512,1024]{1,0:T(8,128)(2,1)}, bf16[512,1024]{1,0:T(8,128)(2,1)}, u32[]{:S(2)}, u32[]{:S(2)}) collective-permute-start(bf16[512,1024]{1,0:T(8,128)(2,1)} %pad_maximum_fusion.1), channel_id=1, source_target_pairs={{0,1},{1,0},{2,3},{3,2},{4,5},{5,4},{6,7},{7,6},{8,9},{9,8},{10,11... | collective-permute-start | bytes 3145736 | tf_op jit(solution)/shard_map/ppermute | solution.py:30
  20.4 29.3 %collective-permute-start.20 = (bf16[256,2048]{1,0:T(8,128)(2,1)}, bf16[256,2048]{1,0:T(8,128)(2,1)}, u32[]{:S(2)}, u32[]{:S(2)}) collective-permute-start(bf16[256,2048]{1,0:T(8,128)(2,1)} %pad_maximum_fusion.3), channel_id=1, source_target_pairs={{0,2},{1,3},{2,0},{3,1},{4,6},{5,7},{6,4},{7,5},{8,10},{9,11},{10,... | collective-permute-start | bytes 3145736 | tf_op jit(solution)/shard_map/ppermute | solution.py:30
  31.6 15.2 %copy-start.14 = (bf16[512,512]{1,0:T(8,128)(2,1)}, bf16[512,512]{1,0:T(8,128)(2,1)S(1)}, u32[]{:S(2)}) copy-start(bf16[512,512]{1,0:T(8,128)(2,1)S(1)} %collective-permute-done.2) | copy-start | bytes 1572868
  31.6 14.6 %collective-permute-start.3 = (bf16[512,512]{1,0:T(8,128)(2,1)S(1)}, bf16[512,512]{1,0:T(8,128)(2,1)}, u32[]{:S(2)}, u32[]{:S(2)}) collective-permute-start(bf16[512,512]{1,0:T(8,128)(2,1)S(1)} %collective-permute-done.2), channel_id=1, source_target_pairs={{0,4},{1,5},{2,6},{3,7},{4,12},{5,13},{6,14},{7,15},{12,8},{13,9},... | collective-permute-start | bytes 1572872 | tf_op jit(solution)/shard_map/ppermute | solution.py:70
  32.4 35.5 %collective-permute-start.21 = (bf16[256,2048]{1,0:T(8,128)(2,1)}, bf16[256,2048]{1,0:T(8,128)(2,1)}, u32[]{:S(2)}, u32[]{:S(2)}) collective-permute-start(bf16[256,2048]{1,0:T(8,128)(2,1)} %pad_maximum_fusion.4), channel_id=1, source_target_pairs={{0,3},{1,2},{2,1},{3,0},{4,7},{5,6},{6,5},{7,4},{8,11},{9,10},{10,... | collective-permute-start | bytes 3145736 | tf_op jit(solution)/shard_map/ppermute | solution.py:30
  46.2 21.7 %collective-permute-start.22 = (bf16[512,512]{1,0:T(8,128)(2,1)}, bf16[512,512]{1,0:T(8,128)(2,1)}, u32[]{:S(2)}, u32[]{:S(2)}) collective-permute-start(bf16[512,512]{1,0:T(8,128)(2,1)} %collective-permute-done.3), channel_id=1, source_target_pairs={{0,4},{1,5},{2,6},{3,7},{4,12},{5,13},{6,14},{7,15},{12,8},{13,9},... | collective-permute-start | bytes 1572872 | tf_op jit(solution)/shard_map/ppermute | solution.py:70
  47.0 30.8 %copy-start.3 = (bf16[512,1024]{1,0:T(8,128)(2,1)}, bf16[512,1024]{1,0:T(8,128)(2,1)S(1)}, u32[]{:S(2)}) copy-start(bf16[512,1024]{1,0:T(8,128)(2,1)S(1)} %convert_element_type.56) | copy-start | bytes 3145732
  77.3 6.8 %collective-permute-start.23 = (bf16[8,32,1024]{2,1,0:T(8,128)(2,1)S(1)}, bf16[8,32,1024]{2,1,0:T(8,128)(2,1)S(1)}, u32[]{:S(2)}, u32[]{:S(2)}) collective-permute-start(bf16[8,32,1024]{2,1,0:T(8,128)(2,1)S(1)} %fusion.31), channel_id=1, source_target_pairs={{0,1},{1,0},{2,3},{3,2},{4,5},{5,4},{6,7},{7,6},{8,9},{9,8},{10,11... | collective-permute-start | bytes 1572872 | tf_op jit(solution)/shard_map/ppermute | solution.py:30
  84.0 5.6 %collective-permute-start.4 = (bf16[256,512]{1,0:T(8,128)(2,1)}, bf16[256,512]{1,0:T(8,128)(2,1)}, u32[]{:S(2)}, u32[]{:S(2)}) collective-permute-start(bf16[256,512]{1,0:T(8,128)(2,1)} %get-tuple-element.55), channel_id=1, source_target_pairs={{0,1},{1,0},{2,3},{3,2},{4,5},{5,4},{6,7},{7,6},{8,9},{9,8},{10,11... | collective-permute-start | bytes 786440 | tf_op jit(solution)/shard_map/ppermute | solution.py:30
  85.0 9.4 %collective-permute-start.24 = (bf16[4,32,1024]{2,1,0:T(8,128)(2,1)}, bf16[4,32,1024]{2,1,0:T(8,128)(2,1)}, u32[]{:S(2)}, u32[]{:S(2)}) collective-permute-start(bf16[4,32,1024]{2,1,0:T(8,128)(2,1)} %fusion.32), channel_id=1, source_target_pairs={{0,2},{1,3},{2,0},{3,1},{4,6},{5,7},{6,4},{7,5},{8,10},{9,11},{10,... | collective-permute-start | bytes 786440 | tf_op jit(solution)/shard_map/ppermute | solution.py:30
  85.5 30.1 %collective-permute-start.7 = (bf16[512,1024]{1,0:T(8,128)(2,1)}, bf16[512,1024]{1,0:T(8,128)(2,1)}, u32[]{:S(2)}, u32[]{:S(2)}) collective-permute-start(bf16[512,1024]{1,0:T(8,128)(2,1)} %copy-done.3), channel_id=1, source_target_pairs={{0,4},{1,5},{2,6},{3,7},{4,12},{5,13},{6,14},{7,15},{12,8},{13,9},... | collective-permute-start | bytes 3145736 | tf_op jit(solution)/shard_map/ppermute | solution.py:83
  88.1 11.8 %collective-permute-start.5 = (bf16[256,512]{1,0:T(8,128)(2,1)}, bf16[256,512]{1,0:T(8,128)(2,1)S(1)}, u32[]{:S(2)}, u32[]{:S(2)}) collective-permute-start(bf16[256,512]{1,0:T(8,128)(2,1)} %get-tuple-element.54), channel_id=1, source_target_pairs={{0,2},{1,3},{2,0},{3,1},{4,6},{5,7},{6,4},{7,5},{8,10},{9,11},{10,... | collective-permute-start | bytes 786440 | tf_op jit(solution)/shard_map/ppermute | solution.py:30
  89.6 15.1 %collective-permute-start.6 = (bf16[256,512]{1,0:T(8,128)(2,1)S(1)}, bf16[256,512]{1,0:T(8,128)(2,1)S(1)}, u32[]{:S(2)}, u32[]{:S(2)}) collective-permute-start(bf16[256,512]{1,0:T(8,128)(2,1)S(1)} %get-tuple-element.53), channel_id=1, source_target_pairs={{0,3},{1,2},{2,1},{3,0},{4,7},{5,6},{6,5},{7,4},{8,11},{9,10},{10,... | collective-permute-start | bytes 786440 | tf_op jit(solution)/shard_map/ppermute | solution.py:30
  95.5 19.2 %collective-permute-start.25 = (bf16[2,32,1024]{2,1,0:T(8,128)(2,1)S(1)}, bf16[2,32,1024]{2,1,0:T(8,128)(2,1)S(1)}, u32[]{:S(2)}, u32[]{:S(2)}) collective-permute-start(bf16[2,32,1024]{2,1,0:T(8,128)(2,1)S(1)} %fusion.34), channel_id=1, source_target_pairs={{0,4},{1,5},{2,6},{3,7},{4,0},{5,1},{6,2},{7,3},{8,12},{9,13},{10,... | collective-permute-start | bytes 393224 | tf_op jit(solution)/shard_map/ppermute | solution.py:30
  114.7 5.7 %collective-permute-start.26 = (bf16[1,32,1024]{2,1,0:T(8,128)(2,1)S(1)}, bf16[1,32,1024]{2,1,0:T(8,128)(2,1)S(1)}, u32[]{:S(2)}, u32[]{:S(2)}) collective-permute-start(bf16[1,32,1024]{2,1,0:T(8,128)(2,1)S(1)} %dynamic-slice_convert_fusion.2), channel_id=1, source_target_pairs={{0,8},{1,9},{2,10},{3,11},{4,12},{5,13},{6,14},{7,15},{8,0},{9,1},... | collective-permute-start | bytes 196616 | tf_op jit(solution)/shard_map/ppermute | solution.py:30
  118.7 43.9 %copy-start.5 = (bf16[256,1024]{1,0:T(8,128)(2,1)S(1)}, bf16[256,1024]{1,0:T(8,128)(2,1)}, u32[]{:S(2)}) copy-start(bf16[256,1024]{1,0:T(8,128)(2,1)} %param.12) | copy-start | bytes 1572868
  118.7 43.9 %copy-start.8 = (bf16[256,1024]{1,0:T(8,128)(2,1)S(1)}, bf16[256,1024]{1,0:T(8,128)(2,1)}, u32[]{:S(2)}) copy-start(bf16[256,1024]{1,0:T(8,128)(2,1)} %copy-done.7) | copy-start | bytes 1572868
  121.7 4.6 %collective-permute-start.27 = (f32[8,128]{1,0:T(8,128)S(1)}, f32[8,128]{1,0:T(8,128)S(1)}, u32[]{:S(2)}, u32[]{:S(2)}) collective-permute-start(f32[8,128]{1,0:T(8,128)S(1)} %broadcast_in_dim.7), channel_id=1, source_target_pairs={{0,8},{1,9},{2,10},{3,11},{4,12},{5,13},{6,14},{7,15},{8,0},{9,1},... | collective-permute-start | bytes 12296 | tf_op jit(solution)/shard_map/ppermute | solution.py:30
  123.2 12.2 %collective-permute-start.8 = (bf16[256,512]{1,0:T(8,128)(2,1)}, bf16[256,512]{1,0:T(8,128)(2,1)}, u32[]{:S(2)}, u32[]{:S(2)}) collective-permute-start(bf16[256,512]{1,0:T(8,128)(2,1)} %get-tuple-element.51), channel_id=1, source_target_pairs={{0,1},{1,0},{2,3},{3,2},{4,5},{5,4},{6,7},{7,6},{8,9},{9,8},{10,11... | collective-permute-start | bytes 786440 | tf_op jit(solution)/shard_map/ppermute | solution.py:30
  126.9 3.7 %collective-permute-start.28 = (f32[8,128]{1,0:T(8,128)S(1)}, f32[8,128]{1,0:T(8,128)S(1)}, u32[]{:S(2)}, u32[]{:S(2)}) collective-permute-start(f32[8,128]{1,0:T(8,128)S(1)} %broadcast_add_fusion), channel_id=1, source_target_pairs={{0,4},{1,5},{2,6},{3,7},{4,0},{5,1},{6,2},{7,3},{8,12},{9,13},{10,... | collective-permute-start | bytes 12296 | tf_op jit(solution)/shard_map/ppermute | solution.py:30
  128.2 34.1 %collective-permute-start.11 = (bf16[512,1024]{1,0:T(8,128)(2,1)}, bf16[512,1024]{1,0:T(8,128)(2,1)}, u32[]{:S(2)}, u32[]{:S(2)}) collective-permute-start(bf16[512,1024]{1,0:T(8,128)(2,1)} %collective-permute-done.7), channel_id=1, source_target_pairs={{0,4},{1,5},{2,6},{3,7},{4,12},{5,13},{6,14},{7,15},{12,8},{13,9},... | collective-permute-start | bytes 3145736 | tf_op jit(solution)/shard_map/ppermute | solution.py:83
  131.3 3.8 %collective-permute-start.29 = (f32[8,128]{1,0:T(8,128)S(1)}, f32[8,128]{1,0:T(8,128)S(1)}, u32[]{:S(2)}, u32[]{:S(2)}) collective-permute-start(f32[8,128]{1,0:T(8,128)S(1)} %fusion.52), channel_id=1, source_target_pairs={{0,2},{1,3},{2,0},{3,1},{4,6},{5,7},{6,4},{7,5},{8,10},{9,11},{10,... | collective-permute-start | bytes 12296 | tf_op jit(solution)/shard_map/ppermute | solution.py:30
  133.2 8.9 %collective-permute-start.9 = (bf16[256,512]{1,0:T(8,128)(2,1)}, bf16[256,512]{1,0:T(8,128)(2,1)S(1)}, u32[]{:S(2)}, u32[]{:S(2)}) collective-permute-start(bf16[256,512]{1,0:T(8,128)(2,1)} %get-tuple-element.50), channel_id=1, source_target_pairs={{0,2},{1,3},{2,0},{3,1},{4,6},{5,7},{6,4},{7,5},{8,10},{9,11},{10,... | collective-permute-start | bytes 786440 | tf_op jit(solution)/shard_map/ppermute | solution.py:30
  133.4 22.6 %collective-permute-start.10 = (bf16[256,512]{1,0:T(8,128)(2,1)}, bf16[256,512]{1,0:T(8,128)(2,1)S(1)}, u32[]{:S(2)}, u32[]{:S(2)}) collective-permute-start(bf16[256,512]{1,0:T(8,128)(2,1)} %get-tuple-element.49), channel_id=1, source_target_pairs={{0,3},{1,2},{2,1},{3,0},{4,7},{5,6},{6,5},{7,4},{8,11},{9,10},{10,... | collective-permute-start | bytes 786440 | tf_op jit(solution)/shard_map/ppermute | solution.py:30
  135.0 2.0 collective-permute-start.30
  140.1 15.8 %collective-permute-start.31 = (bf16[1,32,1024]{2,1,0:T(8,128)(2,1)S(1)}, bf16[1,32,1024]{2,1,0:T(8,128)(2,1)S(1)}, u32[]{:S(2)}, u32[]{:S(2)}) collective-permute-start(bf16[1,32,1024]{2,1,0:T(8,128)(2,1)S(1)} %bitcast.65), channel_id=1, source_target_pairs={{0,8},{1,9},{2,10},{3,11},{4,12},{5,13},{6,14},{7,15},{8,0},{9,1},... | collective-permute-start | bytes 196616 | tf_op jit(solution)/shard_map/ppermute | solution.py:30
  155.9 5.0 %collective-permute-start.32 = (bf16[2,32,1024]{2,1,0:T(8,128)(2,1)S(1)}, bf16[2,32,1024]{2,1,0:T(8,128)(2,1)S(1)}, u32[]{:S(2)}, u32[]{:S(2)}) collective-permute-start(bf16[2,32,1024]{2,1,0:T(8,128)(2,1)S(1)} %maximum_select_fusion.4), channel_id=1, source_target_pairs={{0,4},{1,5},{2,6},{3,7},{4,0},{5,1},{6,2},{7,3},{8,12},{9,13},{10,... | collective-permute-start | bytes 393224 | tf_op jit(solution)/shard_map/ppermute | solution.py:30
  161.0 6.4 %collective-permute-start.33 = (bf16[4,32,1024]{2,1,0:T(8,128)(2,1)S(1)}, bf16[4,32,1024]{2,1,0:T(8,128)(2,1)S(1)}, u32[]{:S(2)}, u32[]{:S(2)}) collective-permute-start(bf16[4,32,1024]{2,1,0:T(8,128)(2,1)S(1)} %bitcast.63), channel_id=1, source_target_pairs={{0,2},{1,3},{2,0},{3,1},{4,6},{5,7},{6,4},{7,5},{8,10},{9,11},{10,... | collective-permute-start | bytes 786440 | tf_op jit(solution)/shard_map/ppermute | solution.py:30
  162.4 22.1 %collective-permute-start.15 = (bf16[512,1024]{1,0:T(8,128)(2,1)}, bf16[512,1024]{1,0:T(8,128)(2,1)}, u32[]{:S(2)}, u32[]{:S(2)}) collective-permute-start(bf16[512,1024]{1,0:T(8,128)(2,1)} %collective-permute-done.11), channel_id=1, source_target_pairs={{0,4},{1,5},{2,6},{3,7},{4,12},{5,13},{6,14},{7,15},{12,8},{13,9},... | collective-permute-start | bytes 3145736 | tf_op jit(solution)/shard_map/ppermute | solution.py:83
  166.3 5.0 %collective-permute-start.12 = (bf16[256,512]{1,0:T(8,128)(2,1)}, bf16[256,512]{1,0:T(8,128)(2,1)}, u32[]{:S(2)}, u32[]{:S(2)}) collective-permute-start(bf16[256,512]{1,0:T(8,128)(2,1)} %get-tuple-element.47), channel_id=1, source_target_pairs={{0,1},{1,0},{2,3},{3,2},{4,5},{5,4},{6,7},{7,6},{8,9},{9,8},{10,11... | collective-permute-start | bytes 786440 | tf_op jit(solution)/shard_map/ppermute | solution.py:30
  167.6 16.0 %collective-permute-start.34 = (bf16[8,32,1024]{2,1,0:T(8,128)(2,1)S(1)}, bf16[8,32,1024]{2,1,0:T(8,128)(2,1)S(1)}, u32[]{:S(2)}, u32[]{:S(2)}) collective-permute-start(bf16[8,32,1024]{2,1,0:T(8,128)(2,1)S(1)} %bitcast.57), channel_id=1, source_target_pairs={{0,1},{1,0},{2,3},{3,2},{4,5},{5,4},{6,7},{7,6},{8,9},{9,8},{10,11... | collective-permute-start | bytes 1572872 | tf_op jit(solution)/shard_map/ppermute | solution.py:30
  167.6 9.5 %collective-permute-start.13 = (bf16[256,512]{1,0:T(8,128)(2,1)}, bf16[256,512]{1,0:T(8,128)(2,1)}, u32[]{:S(2)}, u32[]{:S(2)}) collective-permute-start(bf16[256,512]{1,0:T(8,128)(2,1)} %get-tuple-element.46), channel_id=1, source_target_pairs={{0,2},{1,3},{2,0},{3,1},{4,6},{5,7},{6,4},{7,5},{8,10},{9,11},{10,... | collective-permute-start | bytes 786440 | tf_op jit(solution)/shard_map/ppermute | solution.py:30
  169.0 12.8 %collective-permute-start.14 = (bf16[256,512]{1,0:T(8,128)(2,1)S(1)}, bf16[256,512]{1,0:T(8,128)(2,1)}, u32[]{:S(2)}, u32[]{:S(2)}) collective-permute-start(bf16[256,512]{1,0:T(8,128)(2,1)S(1)} %get-tuple-element.45), channel_id=1, source_target_pairs={{0,3},{1,2},{2,1},{3,0},{4,7},{5,6},{6,5},{7,4},{8,11},{9,10},{10,... | collective-permute-start | bytes 786440 | tf_op jit(solution)/shard_map/ppermute | solution.py:30
  171.3 13.2 %copy-start.6 = (bf16[256,1024]{1,0:T(8,128)(2,1)S(1)}, bf16[256,1024]{1,0:T(8,128)(2,1)}, u32[]{:S(2)}) copy-start(bf16[256,1024]{1,0:T(8,128)(2,1)} %param.12) | copy-start | bytes 1572868
  171.3 13.2 %copy-start.9 = (bf16[256,1024]{1,0:T(8,128)(2,1)S(1)}, bf16[256,1024]{1,0:T(8,128)(2,1)}, u32[]{:S(2)}) copy-start(bf16[256,1024]{1,0:T(8,128)(2,1)} %copy-done.7) | copy-start | bytes 1572868
  171.3 13.2 %copy-start.10 = (bf16[256,1024]{1,0:T(8,128)(2,1)S(1)}, bf16[256,1024]{1,0:T(8,128)(2,1)}, u32[]{:S(2)}) copy-start(bf16[256,1024]{1,0:T(8,128)(2,1)} %get-tuple-element.57) | copy-start | bytes 1572868
  171.3 13.2 %copy-start.11 = (bf16[256,1024]{1,0:T(8,128)(2,1)S(1)}, bf16[256,1024]{1,0:T(8,128)(2,1)}, u32[]{:S(2)}) copy-start(bf16[256,1024]{1,0:T(8,128)(2,1)} %get-tuple-element.58) | copy-start | bytes 1572868
  183.8 6.0 %copy-start.1 = (f32[512,1024]{0,1:T(8,128)S(1)}, f32[512,1024]{0,1:T(8,128)}, u32[]{:S(2)}) copy-start(f32[512,1024]{0,1:T(8,128)} %copy.34) | copy-start | bytes 6291460
  183.8 6.0 %copy-start.13 = (bf16[512,512]{1,0:T(8,128)(2,1)S(1)}, bf16[512,512]{1,0:T(8,128)(2,1)}, u32[]{:S(2)}) copy-start(bf16[512,512]{1,0:T(8,128)(2,1)} %param.13) | copy-start | bytes 1572868
  187.9 4.5 %collective-permute-start.16 = (bf16[256,512]{1,0:T(8,128)(2,1)S(1)}, bf16[256,512]{1,0:T(8,128)(2,1)}, u32[]{:S(2)}, u32[]{:S(2)}) collective-permute-start(bf16[256,512]{1,0:T(8,128)(2,1)S(1)} %get-tuple-element.43), channel_id=1, source_target_pairs={{0,1},{1,0},{2,3},{3,2},{4,5},{5,4},{6,7},{7,6},{8,9},{9,8},{10,11... | collective-permute-start | bytes 786440 | tf_op jit(solution)/shard_map/ppermute | solution.py:30
  187.9 9.1 %collective-permute-start.17 = (bf16[256,512]{1,0:T(8,128)(2,1)S(1)}, bf16[256,512]{1,0:T(8,128)(2,1)S(1)}, u32[]{:S(2)}, u32[]{:S(2)}) collective-permute-start(bf16[256,512]{1,0:T(8,128)(2,1)S(1)} %get-tuple-element.42), channel_id=1, source_target_pairs={{0,2},{1,3},{2,0},{3,1},{4,6},{5,7},{6,4},{7,5},{8,10},{9,11},{10,... | collective-permute-start | bytes 786440 | tf_op jit(solution)/shard_map/ppermute | solution.py:30
  189.2 12.6 %collective-permute-start.18 = (bf16[256,512]{1,0:T(8,128)(2,1)S(1)}, bf16[256,512]{1,0:T(8,128)(2,1)S(1)}, u32[]{:S(2)}, u32[]{:S(2)}) collective-permute-start(bf16[256,512]{1,0:T(8,128)(2,1)S(1)} %get-tuple-element.41), channel_id=1, source_target_pairs={{0,3},{1,2},{2,1},{3,0},{4,7},{5,6},{6,5},{7,4},{8,11},{9,10},{10,... | collective-permute-start | bytes 786440 | tf_op jit(solution)/shard_map/ppermute | solution.py:30
  (2 other events, 8.1 us)

commit v2 on v1

v2 whole, which is shorter than its diff:
```python
import jax
import jax.numpy as jnp
from jax import lax
from jax.sharding import PartitionSpec as P

clip_total = 512.0
step_size = 0.01
first_fix = 1.0 - 0.9**10
second_fix = 1.0 - 0.99**10

f32 = jnp.float32
bf16 = jnp.bfloat16


def after(value, *others):
    return lax.optimization_barrier((value,) + others)[0]


def make_per_device(n):
    sides = 2 if n == 16 else 1
    ring = n // (2 * sides)
    order = [0, 1, 3, 2] if ring == 4 else list(range(ring))
    forward = [
        ((order[k] * 2 * sides) + m, order[(k + 1) % ring] * 2 * sides + m)
        for k in range(ring)
        for m in range(2 * sides)
    ]
    rounds = [(1, 2)]
    bit = 2
    if sides == 2:
        rounds.append((2, 2))
        bit = 4
    while bit < n:
        radix = 4 if 2 * bit < n else 2
        rounds.append((bit, radix))
        bit *= radix

    def swap(value, bit):
        return lax.ppermute(value, "dp", [(i, i ^ bit) for i in range(n)])

    def onward(value):
        return lax.ppermute(value, "dp", forward)

    def per_device(activations, key_grad, proj_basis, master_weight, first_moment, second_moment):
        tokens = activations.shape[0]
        rows, rank = proj_basis.shape
        outs = key_grad.shape[1]
        half = rows // 2
        index = lax.axis_index("dp")
        core = index & 1
        side = (index >> 1) & (sides - 1)
        zplace = lax.shift_right_logical(index, 1 if sides == 1 else 2)
        if ring == 4:
            place = zplace ^ (zplace >> 1)
        else:
            place = zplace

        def source(s):
            k = (place - s) & (ring - 1)
            return k ^ (k >> 1) if ring == 4 else k

        def block_at(s, side_):
            return (source(s) * sides + side_) * (2 * rows)

        def pair(mine, theirs):
            return jnp.where(
                core == 0,
                jnp.concatenate([mine, theirs], axis=0),
                jnp.concatenate([theirs, mine], axis=0),
            )

        def act_columns(s, side_):
            return lax.dynamic_slice(activations, (0, block_at(s, side_)), (tokens, 2 * rows))

        basis = [proj_basis]
        for s in range(1, ring):
            basis.append(onward(basis[-1]))
        basis_pair = [pair(b, swap(b, 1)) for b in basis]

        weight = master_weight.astype(bf16)
        low, high = [weight[:half]], [weight[half:]]
        for s in range(1, ring):
            low.append(onward(after(low[-1], basis[ring - 1]) if s == 2 else low[-1]))
        for s in range(1, ring):
            high.append(onward(after(high[-1], basis[ring - 2]) if s == 1 else high[-1]))

        grads = [key_grad]
        acts = [[act_columns(s, side) for s in range(ring)]]
        if sides == 2:
            acts.append([swap(act_columns(s, 1 - side), 2) for s in range(ring)])
            grads.append(swap(key_grad, 2))

        partial_grad = 0.0
        for x in range(sides):
            projected = 0.0
            for s in range(ring):
                projected = projected + jnp.dot(
                    acts[x][s], basis_pair[s], preferred_element_type=f32
                )
            partial_grad = partial_grad + lax.dot_general(
                projected.astype(bf16),
                grads[x],
                (((0,), (0,)), ((), ())),
                preferred_element_type=f32,
            )

        activation_grad = jnp.zeros(activations.shape, bf16)
        for s in range(ring):
            wide = pair(
                jnp.concatenate([low[s], high[s]], axis=0),
                jnp.concatenate([swap(low[s], 1), swap(high[s], 1)], axis=0),
            )
            for x in reversed(range(sides)):
                block = lax.dot_general(
                    grads[x], wide, (((1,), (1,)), ((), ())), preferred_element_type=f32
                ).astype(bf16)
                if x > 0:
                    block = swap(block, 2)
                activation_grad = lax.dynamic_update_slice(
                    activation_grad, block, (0, block_at(s, side ^ x))
                )

        owned = rank // n
        total = partial_grad.reshape(n, owned, outs)
        for bit, radix in rounds:
            digit = (index // bit) & (radix - 1)
            total = total.reshape(total.shape[0] // radix, radix, owned, outs)
            kept = lax.dynamic_index_in_dim(total, digit, 1, keepdims=False)
            for j in range(1, radix):
                given = lax.dynamic_index_in_dim(total, digit ^ j, 1, keepdims=False)
                kept = kept + swap(given.astype(bf16), j * bit).astype(f32)
            total = kept
        owned_rows = total.reshape(owned, outs)

        square_sum = jnp.broadcast_to(jnp.sum(owned_rows * owned_rows), (8, 128))
        for bit, radix in reversed(rounds):
            square_sum = sum([swap(square_sum, j * bit) for j in range(1, radix)], square_sum)
        grad_norm = jnp.sqrt(square_sum[0, 0])
        factor = jnp.minimum(1.0, clip_total / (grad_norm + 1e-06))
        clipped = owned_rows * factor
        new_first = 0.9 * first_moment + 0.1 * clipped
        new_second = 0.99 * second_moment + 0.01 * clipped * clipped
        update = new_first / first_fix / (jnp.sqrt(new_second / second_fix) + 1e-08)

        whole = update.astype(bf16).reshape(1, owned, outs)
        for bit, radix in reversed(rounds):
            digit = (index // bit) & (radix - 1)
            found = [whole] + [swap(whole, j * bit) for j in range(1, radix)]
            ordered = []
            for d in range(radix):
                pick = found[d]
                for j in range(radix):
                    if j != d:
                        pick = jnp.where(digit == (d ^ j), found[j], pick)
                ordered.append(pick)
            whole = jnp.stack(ordered, axis=1).reshape(radix * whole.shape[0], owned, outs)
        back_step = jnp.dot(
            proj_basis, whole.reshape(rank, outs), preferred_element_type=f32
        )
        new_master = master_weight - step_size * back_step
        return (activation_grad, new_master, new_first, new_second)

    return per_device


def solution(mesh):
    spec = P(("groups", "dp"), None)
    return jax.shard_map(
        make_per_device(mesh.shape["dp"]),
        mesh=mesh,
        in_specs=(spec,) * 6,
        out_specs=(spec,) * 4,
        check_vma=False,
    )
```

time: 203 us -> 187 us (0.921)
  waiting for transfers between devices: 102 us -> 66.9 us
  matrix products: 20.1 us -> 42 us
  starting transfers between devices: 26.9 us -> 39.8 us
  local copies, waits for them, and re-layouts: 36.4 us -> 24.4 us
  between operations: 7.1 us -> 1.83 us
    ppermute x35 -> x45, waiting for transfers between devices: 102 us -> 66.9 us  [the longest x36 36.7 us: swap(): return lax.ppermute(value, 'dp', [(i, i ^ bit) for i in range(n)])]
    dot_general x5 -> x16, matrix products: 19.4 us -> 40.2 us  [the longest x8 16.4 us: per_device(): lax.dot_general(grads[x], wide, (((1,), (1,)), ((), ())), preferred_eleme...]
    ppermute x35 -> x45, starting transfers between devices: 26.9 us -> 39.8 us  [the longest x36 28.1 us: swap(): return lax.ppermute(value, 'dp', [(i, i ^ bit) for i in range(n)])]
    dynamic_update_slice x12 -> x8, local copies, waits for them, and re-layouts: 14.5 us -> 5.07 us  [per_device(): lax.dynamic_update_slice(activation_grad, block, (0, block_at(s, side ^ x)))]
    select_n x5 -> x3, other arithmetic: 0.3 us -> 5.75 us  [pair(): jnp.where(core == 0, jnp.concatenate([mine, theirs], axis=0), jnp.concate...]
    slice x5 -> x1, local copies, waits for them, and re-layouts: 6.23 us -> 1.05 us  [per_device(): low, high = ([weight[:half]], [weight[half:]])]
    concatenate x4 -> x0, other arithmetic: 4.46 us -> none  [the longest x3 3.35 us: columns(): jnp.concatenate([lax.dynamic_slice(activations, (0, (source[s] * members...]
    unnamed x32 -> x38, local copies, waits for them, and re-layouts: 3.69 us -> 7.67 us
  transfers between devices with their start and end apart: 35 -> 45, of which waited for: 20 -> 20; matrix products, arithmetic and copies ran while one was open for 26% -> 37% of each run, Pallas kernels for 0% -> 0%
where the time goes in v2:
time: 187 us; the launch traced here: 186 us
  waiting for transfers between devices  66.9 us (36%)
  matrix products  42 us (22%)
  starting transfers between devices  39.8 us (21%)
  local copies, waits for them, and re-layouts  24.4 us (13%)
  other arithmetic  11.2 us (6%)
    ppermute x36, waiting for transfers between devices, swap(): return lax.ppermute(value, 'dp', [(i, i ^ bit) for i in range(n)])  36.7 us
    ppermute x9, waiting for transfers between devices, onward(): return lax.ppermute(value, 'dp', forward)  30.2 us
    ppermute x36, starting transfers between devices, swap(): return lax.ppermute(value, 'dp', [(i, i ^ bit) for i in range(n)])  28.1 us
    dot_general x8, matrix products, per_device(): lax.dot_general(grads[x], wide, (((1,), (1,)), ((), ())), preferred_eleme...  16.4 us
    dot_general x6, matrix products, per_device(): jnp.dot(acts[x][s], basis_pair[s], preferred_element_type=f32)  15.9 us
    ppermute x9, starting transfers between devices, onward(): return lax.ppermute(value, 'dp', forward)  11.7 us
    dot_general x2, matrix products, per_device(): lax.dot_general(projected.astype(bf16), grads[x], (((0,), (0,)), ((), ())...  7.78 us
    unnamed x38, local copies, waits for them, and re-layouts  7.67 us
  transfers between devices with their start and end apart: 45, of which 20 were waited for; matrix products, arithmetic and copies ran while one was open for 37% of the time, Pallas kernels for 0%

profile of v2, /device:TPU:0, one launch (start us, length us, event | category | flops | bytes accessed | tf_op | source)
XLA Modules:
  0.0 186.1 jit_solution(7086472256596260888)
XLA Ops:
  0.6 3.0 %collective-permute-start.2 = (bf16[256,1024]{1,0:T(8,128)(2,1)}, bf16[256,1024]{1,0:T(8,128)(2,1)}, u32[]{:S(2)}, u32[]{:S(2)}) collective-permute-start(bf16[256,1024]{1,0:T(8,128)(2,1)} %param.7), channel_id=1, source_target_pairs={{0,2},{1,3},{2,0},{3,1},{4,6},{5,7},{6,4},{7,5},{8,10},{9,11},{10,... | collective-permute-start | bytes 1572872 | tf_op jit(solution)/shard_map/ppermute | solution.py:39
  3.7 1.7 convert_element_type.102
  7.0 1.6 collective-permute-start.5
  8.6 3.1 %constant_dynamic-slice_fusion.3 = (bf16[256,1024]{1,0:T(8,128)(2,1)}, bf16[256,1024]{1,0:T(8,128)(2,1)}, bf16[256,1024]{1,0:T(8,128)(2,1)}, bf16[256,1024]{1,0:T(8,128)(2,1)}) fusion(bf16[256,8192]{1,0:T(8,128)(2,1)} %param.6, s32[]{:T(128)S(6)} %select_n.222, s32[]{:T(128)S(6)} %select_n.223, s32[]{:T(128)S(6)} %select_n.225, s32[]{:T(128)S(6)} %select_n.224), kind=kLoop, calls=%fused_computation.74 | loop fusion | bytes 4194320 | tf_op jit(solution)/shard_map/dynamic_slice | solution.py:73
  11.7 1.8 copy.31
  13.5 2.4 %collective-permute-done.2 = bf16[256,1024]{1,0:T(8,128)(2,1)} collective-permute-done((bf16[256,1024]{1,0:T(8,128)(2,1)}, bf16[256,1024]{1,0:T(8,128)(2,1)}, u32[]{:S(2)}, u32[]{:S(2)}) %collective-permute-start.2) | collective-permute-done | bytes 524320 | tf_op jit(solution)/shard_map/ppermute | solution.py:39
  15.9 1.7 collective-permute-start.27
  17.7 3.3 %fusion.1 = bf16[256,1024]{0,1:T(8,128)(2,1)} fusion(bf16[256,1024]{1,0:T(8,128)(2,1)} %collective-permute-done.2, bf16[256,1024]{1,0:T(8,128)(2,1)} %collective-permute-done.1, bf16[256,1024]{1,0:T(8,128)(2,1)} %collective-permute-done, bf16[512,1024]{1,0:T(8,128)(2,1)S(1)} %convert_element_type.102, pred[]{:T(512)S(6)} %eq.12), kind=kOutput, calls=%fused_computation.19 | convolution fusion | flops 550764544 | bytes 3145729 | tf_op jit(solution)/shard_map/dot_general | solution.py:114
  23.3 2.4 %fusion.2 = bf16[256,1024]{0,1:T(8,128)(2,1)S(1)} fusion(bf16[256,1024]{1,0:T(8,128)(2,1)S(1)} %copy-done.11, bf16[256,1024]{1,0:T(8,128)(2,1)} %collective-permute-done.1, bf16[256,1024]{1,0:T(8,128)(2,1)} %collective-permute-done, bf16[512,1024]{1,0:T(8,128)(2,1)S(1)} %convert_element_type.102, pred[]{:T(512)S(6)} %eq.12), kind=kOutput, calls=%fused_computation.20 | convolution fusion | flops 550764544 | bytes 3145729 | tf_op jit(solution)/shard_map/dot_general | solution.py:114
  25.9 3.4 %collective-permute-start.4 = (bf16[256,1024]{1,0:T(8,128)(2,1)}, bf16[256,1024]{1,0:T(8,128)(2,1)}, u32[]{:S(2)}, u32[]{:S(2)}) collective-permute-start(bf16[256,1024]{1,0:T(8,128)(2,1)} %get-tuple-element.27), channel_id=1, source_target_pairs={{0,4},{1,5},{2,6},{3,7},{4,12},{5,13},{6,14},{7,15},{12,8},{13,9},... | collective-permute-start | bytes 1572872 | tf_op jit(solution)/shard_map/ppermute | solution.py:42
  29.3 2.9 %fusion.18 = f32[256,512]{1,0:T(8,128)} fusion(bf16[256,8192]{1,0:T(8,128)(2,1)} %param.6, s32[]{:T(128)S(6)} %select_n.202, bf16[512,512]{1,0:T(8,128)(2,1)} %collective-permute-done.22, bf16[512,512]{1,0:T(8,128)(2,1)} %param.8, pred[]{:T(512)S(6)} %eq.12), kind=kOutput, calls=%fused_computation.47 | convolution fusion | flops 273154048 | bytes 2097157 | tf_op jit(solution)/shard_map/dot_general | solution.py:97
  32.9 5.4 %collective-permute-done.6 = bf16[512,512]{1,0:T(8,128)(2,1)S(1)} collective-permute-done((bf16[512,512]{1,0:T(8,128)(2,1)}, bf16[512,512]{1,0:T(8,128)(2,1)S(1)}, u32[]{:S(2)}, u32[]{:S(2)}) %collective-permute-start.6) | collective-permute-done | bytes 524320 | tf_op jit(solution)/shard_map/ppermute | solution.py:42
  39.3 2.9 %fusion.23 = f32[256,512]{1,0:T(8,128)} fusion(bf16[256,1024]{1,0:T(8,128)(2,1)} %collective-permute-done.27, bf16[512,512]{1,0:T(8,128)(2,1)} %collective-permute-done.23, bf16[512,512]{1,0:T(8,128)(2,1)} %collective-permute-done.5, pred[]{:T(512)S(6)} %eq.12), kind=kOutput, calls=%fused_computation.56 | convolution fusion | flops 273154048 | bytes 2097153 | tf_op jit(solution)/shard_map/dot_general | solution.py:97
  42.2 1.7 collective-permute-start.29
  45.2 2.2 %convolution_add_fusion.4 = f32[256,512]{1,0:T(8,128)S(1)} fusion(f32[256,512]{1,0:T(8,128)S(1)} %copy-done.17, bf16[256,8192]{1,0:T(8,128)(2,1)} %param.6, s32[]{:T(128)S(6)} %select_n.205, bf16[512,512]{1,0:T(8,128)(2,1)} %collective-permute-done.23, bf16[512,512]{1,0:T(8,128)(2,1)} %collective-permute-done.5, pred[]{:T(512)S(6)} %eq.12), kind=kOutput, calls=%fused_computation.17 | convolution fusion | flops 273285120 | bytes 2621445 | tf_op jit(solution)/shard_map/dot_general | solution.py:97
  47.4 2.3 %collective-permute-done.4 = bf16[256,1024]{1,0:T(8,128)(2,1)} collective-permute-done((bf16[256,1024]{1,0:T(8,128)(2,1)}, bf16[256,1024]{1,0:T(8,128)(2,1)}, u32[]{:S(2)}, u32[]{:S(2)}) %collective-permute-start.4) | collective-permute-done | bytes 524320 | tf_op jit(solution)/shard_map/ppermute | solution.py:42
  50.5 10.4 %collective-permute-done.11 = bf16[512,512]{1,0:T(8,128)(2,1)} collective-permute-done((bf16[512,512]{1,0:T(8,128)(2,1)S(1)}, bf16[512,512]{1,0:T(8,128)(2,1)}, u32[]{:S(2)}, u32[]{:S(2)}) %collective-permute-start.11) | collective-permute-done | bytes 524320 | tf_op jit(solution)/shard_map/ppermute | solution.py:42
  61.8 3.3 %fusion.22 = f32[256,512]{1,0:T(8,128)} fusion(bf16[256,1024]{1,0:T(8,128)(2,1)} %collective-permute-done.28, bf16[512,512]{1,0:T(8,128)(2,1)} %collective-permute-done.24, bf16[512,512]{1,0:T(8,128)(2,1)S(1)} %collective-permute-done.6, pred[]{:T(512)S(6)} %eq.12), kind=kOutput, calls=%fused_computation.55 | convolution fusion | flops 273154048 | bytes 2097153 | tf_op jit(solution)/shard_map/dot_general | solution.py:97
  65.1 1.9 %convolution_add_fusion.3 = f32[256,512]{1,0:T(8,128)S(1)} fusion(f32[256,512]{1,0:T(8,128)S(1)} %convolution_add_fusion.4, bf16[256,8192]{1,0:T(8,128)(2,1)} %param.6, s32[]{:T(128)S(6)} %select_n.208, bf16[512,512]{1,0:T(8,128)(2,1)} %collective-permute-done.24, bf16[512,512]{1,0:T(8,128)(2,1)S(1)} %collective-permute-done.6, pred[]{:T(512)S(6)} %eq.12), kind=kOutput, calls=%fused_computation.16 | convolution fusion | flops 273285120 | bytes 2621445 | tf_op jit(solution)/shard_map/dot_general | solution.py:97
  67.7 4.5 %collective-permute-done.7 = bf16[256,1024]{1,0:T(8,128)(2,1)} collective-permute-done((bf16[256,1024]{1,0:T(8,128)(2,1)}, bf16[256,1024]{1,0:T(8,128)(2,1)}, u32[]{:S(2)}, u32[]{:S(2)}) %collective-permute-start.7) | collective-permute-done | bytes 524320 | tf_op jit(solution)/shard_map/ppermute | solution.py:42
  73.7 2.7 %fusion.21 = f32[256,512]{1,0:T(8,128)} fusion(bf16[256,1024]{1,0:T(8,128)(2,1)} %collective-permute-done.29, bf16[512,512]{1,0:T(8,128)(2,1)S(1)} %collective-permute-done.25, bf16[512,512]{1,0:T(8,128)(2,1)} %collective-permute-done.11, pred[]{:T(512)S(6)} %eq.12), kind=kOutput, calls=%fused_computation.54 | convolution fusion | flops 273154048 | bytes 2097153 | tf_op jit(solution)/shard_map/dot_general | solution.py:97
  76.5 4.0 %fusion.12 = f32[512,1024]{1,0:T(8,128)} fusion(bf16[256,1024]{1,0:T(8,128)(2,1)S(1)} %copy-done.12, f32[256,512]{1,0:T(8,128)S(1)} %convolution_add_fusion.3, bf16[256,8192]{1,0:T(8,128)(2,1)} %param.6, s32[]{:T(128)S(6)} %select_n.211, bf16[512,512]{1,0:T(8,128)(2,1)} %copy-done.16, bf16[512,512]{1,0:T(8,128)(2,1)} %collective-permute-done.11, pred[]{:T(512)S(6)} %eq.12), kind=kOutput, calls=%fused_computation.30 | convolution fusion | flops 541851648 | bytes 4718597 | tf_op jit(solution)/shard_map/dot_general | solution.py:100
  80.4 3.8 %convolution_add_fusion = f32[512,1024]{1,0:T(8,128)S(1)} fusion(f32[512,1024]{1,0:T(8,128)} %fusion.12, bf16[256,1024]{1,0:T(8,128)(2,1)} %collective-permute-done.2, f32[256,512]{1,0:T(8,128)} %fusion.21, f32[256,512]{1,0:T(8,128)} %fusion.22, f32[256,512]{1,0:T(8,128)S(1)} %copy-done.5, bf16[256,1024]{1,0:T(8,128)(2,1)} %collective-permute-done.26, ...), kind=kOutput, calls=%fused_computation.5 | convolution fusion | flops 542638080 | bytes 7864321 | tf_op jit(solution)/shard_map/dot_general | solution.py:100
  85.2 2.6 %maximum_select_fusion.1 = bf16[1024,1024]{1,0:T(8,128)(2,1)S(1)} fusion(bf16[256,1024]{1,0:T(8,128)(2,1)} %collective-permute-done.9, bf16[256,1024]{1,0:T(8,128)(2,1)} %collective-permute-done.8, bf16[256,1024]{1,0:T(8,128)(2,1)} %collective-permute-done.7, bf16[256,1024]{1,0:T(8,128)(2,1)} %collective-permute-done.4, pred[]{:T(512)S(6)} %eq.12), kind=kLoop, calls=%fused_computation.1 | loop fusion | flops 17825792 | bytes 4194305 | tf_op jit(solution)/shard_map/jit(_where)/select_n | solution.py:66
  89.1 1.6 fusion.4
  91.9 2.4 %collective-permute-done.13 = bf16[256,1024]{1,0:T(8,128)(2,1)} collective-permute-done((bf16[256,1024]{1,0:T(8,128)(2,1)}, bf16[256,1024]{1,0:T(8,128)(2,1)}, u32[]{:S(2)}, u32[]{:S(2)}) %collective-permute-start.13) | collective-permute-done | bytes 524320 | tf_op jit(solution)/shard_map/ppermute | solution.py:42
  96.6 1.8 fusion.3
  98.4 1.6 collective-permute-start.10
  101.2 4.1 %collective-permute-done.31 = bf16[4,32,1024]{2,1,0:T(8,128)(2,1)S(1)} collective-permute-done((bf16[4,32,1024]{2,1,0:T(8,128)(2,1)S(1)}, bf16[4,32,1024]{2,1,0:T(8,128)(2,1)S(1)}, u32[]{:S(2)}, u32[]{:S(2)}) %collective-permute-start.31) | collective-permute-done | bytes 262176 | tf_op jit(solution)/shard_map/ppermute | solution.py:39
  106.6 2.6 %collective-permute-start.34 = (bf16[1,32,1024]{2,1,0:T(8,128)(2,1)S(1)}, bf16[1,32,1024]{2,1,0:T(8,128)(2,1)S(1)}, u32[]{:S(2)}, u32[]{:S(2)}) collective-permute-start(bf16[1,32,1024]{2,1,0:T(8,128)(2,1)S(1)} %get-tuple-element.32), channel_id=1, source_target_pairs={{0,12},{1,13},{2,14},{3,15},{4,8},{5,9},{6,10},{7,11},{8,4},{9,5},... | collective-permute-start | bytes 196616 | tf_op jit(solution)/shard_map/ppermute | solution.py:39
  109.7 2.0 %maximum_select_fusion.2 = bf16[1024,1024]{1,0:T(8,128)(2,1)S(1)} fusion(bf16[256,1024]{1,0:T(8,128)(2,1)S(1)} %collective-permute-done.15, bf16[256,1024]{1,0:T(8,128)(2,1)S(1)} %collective-permute-done.14, bf16[256,1024]{1,0:T(8,128)(2,1)} %collective-permute-done.13, bf16[256,1024]{1,0:T(8,128)(2,1)S(1)} %collective-permute-done.12, pred[]{:T(512)S(6)} %eq.12), kind=kLoop, calls=%fused_computation.2 | loop fusion | flops 17825792 | bytes 4194305 | tf_op jit(solution)/shard_map/jit(_where)/select_n | solution.py:66
  111.8 5.4 %collective-permute-done.32 = bf16[1,32,1024]{2,1,0:T(8,128)(2,1)S(1)} collective-permute-done((bf16[1,32,1024]{2,1,0:T(8,128)(2,1)S(1)}, bf16[1,32,1024]{2,1,0:T(8,128)(2,1)S(1)}, u32[]{:S(2)}, u32[]{:S(2)}) %collective-permute-start.32) | collective-permute-done | bytes 65568 | tf_op jit(solution)/shard_map/ppermute | solution.py:39
  117.2 1.8 collective-permute-done.34
  121.4 2.1 %collective-permute-start.36 = (f32[8,128]{1,0:T(8,128)S(1)}, f32[8,128]{1,0:T(8,128)S(1)}, u32[]{:S(2)}, u32[]{:S(2)}) collective-permute-start(f32[8,128]{1,0:T(8,128)S(1)} %broadcast_in_dim.7), channel_id=1, source_target_pairs={{0,8},{1,9},{2,10},{3,11},{4,12},{5,13},{6,14},{7,15},{8,0},{9,1},... | collective-permute-start | bytes 12296 | tf_op jit(solution)/shard_map/ppermute | solution.py:39
  123.4 1.7 collective-permute-start.37
  125.6 1.5 fusion.6
  127.1 1.5 collective-permute-start.17
  130.4 2.6 %fusion.5 = bf16[256,1024]{0,1:T(8,128)(2,1)} fusion(bf16[1024,1024]{1,0:T(8,128)(2,1)S(1)} %maximum_select_fusion.2, bf16[256,1024]{1,0:T(8,128)(2,1)} %collective-permute-done.2), kind=kOutput, calls=%fused_computation.23 | convolution fusion | flops 537133056 | bytes 3145728 | tf_op jit(solution)/shard_map/dot_general | solution.py:114
  136.1 3.8 %collective-permute-done.17 = bf16[256,1024]{1,0:T(8,128)(2,1)S(1)} collective-permute-done((bf16[256,1024]{1,0:T(8,128)(2,1)S(1)}, bf16[256,1024]{1,0:T(8,128)(2,1)S(1)}, u32[]{:S(2)}, u32[]{:S(2)}) %collective-permute-start.17) | collective-permute-done | bytes 524320 | tf_op jit(solution)/shard_map/ppermute | solution.py:42
  142.5 2.6 %collective-permute-start.41 = (bf16[1,32,1024]{2,1,0:T(8,128)(2,1)S(1)}, bf16[1,32,1024]{2,1,0:T(8,128)(2,1)S(1)}, u32[]{:S(2)}, u32[]{:S(2)}) collective-permute-start(bf16[1,32,1024]{2,1,0:T(8,128)(2,1)S(1)} %get-tuple-element.16), channel_id=1, source_target_pairs={{0,8},{1,9},{2,10},{3,11},{4,12},{5,13},{6,14},{7,15},{8,0},{9,1},... | collective-permute-start | bytes 196616 | tf_op jit(solution)/shard_map/ppermute | solution.py:39
  148.1 1.4 collective-permute-done.41
  149.5 1.7 collective-permute-done.40
  153.1 2.6 %fusion.7 = bf16[256,1024]{0,1:T(8,128)(2,1)} fusion(bf16[1024,1024]{1,0:T(8,128)(2,1)S(1)} %maximum_select_fusion.3, bf16[256,1024]{1,0:T(8,128)(2,1)} %collective-permute-done.2), kind=kOutput, calls=%fused_computation.25 | convolution fusion | flops 537133056 | bytes 3145728 | tf_op jit(solution)/shard_map/dot_general | solution.py:114
  155.7 1.5 collective-permute-start.21
  157.1 11.1 %collective-permute-done.43 = bf16[4,32,1024]{2,1,0:T(8,128)(2,1)S(1)} collective-permute-done((bf16[4,32,1024]{2,1,0:T(8,128)(2,1)S(1)}, bf16[4,32,1024]{2,1,0:T(8,128)(2,1)S(1)}, u32[]{:S(2)}, u32[]{:S(2)}) %collective-permute-start.43) | collective-permute-done | bytes 262176 | tf_op jit(solution)/shard_map/ppermute | solution.py:39
  171.4 6.5 %collective-permute-done.21 = bf16[256,1024]{0,1:T(8,128)(2,1)} collective-permute-done((bf16[256,1024]{0,1:T(8,128)(2,1)}, bf16[256,1024]{0,1:T(8,128)(2,1)}, u32[]{:S(2)}, u32[]{:S(2)}) %collective-permute-start.21) | collective-permute-done | bytes 524320 | tf_op jit(solution)/shard_map/ppermute | solution.py:39
  182.5 1.8 bitcast_subtract_fusion
  184.3 1.8 copy.32
  (140 shorter events, 41.5 us)
Async XLA Ops:
  0.6 15.3 %collective-permute-start.2 = (bf16[256,1024]{1,0:T(8,128)(2,1)}, bf16[256,1024]{1,0:T(8,128)(2,1)}, u32[]{:S(2)}, u32[]{:S(2)}) collective-permute-start(bf16[256,1024]{1,0:T(8,128)(2,1)} %param.7), channel_id=1, source_target_pairs={{0,2},{1,3},{2,0},{3,1},{4,6},{5,7},{6,4},{7,5},{8,10},{9,11},{10,... | collective-permute-start | bytes 1572872 | tf_op jit(solution)/shard_map/ppermute | solution.py:39
  6.5 11.2 %collective-permute-start = (bf16[256,1024]{1,0:T(8,128)(2,1)}, bf16[256,1024]{1,0:T(8,128)(2,1)}, u32[]{:S(2)}, u32[]{:S(2)}) collective-permute-start(bf16[256,1024]{1,0:T(8,128)(2,1)} %get-tuple-element.27), channel_id=1, source_target_pairs={{0,1},{1,0},{2,3},{3,2},{4,5},{5,4},{6,7},{7,6},{8,9},{9,8},{10,11... | collective-permute-start | bytes 1572872 | tf_op jit(solution)/shard_map/ppermute | solution.py:39
  6.5 11.2 %collective-permute-start.1 = (bf16[256,1024]{1,0:T(8,128)(2,1)}, bf16[256,1024]{1,0:T(8,128)(2,1)}, u32[]{:S(2)}, u32[]{:S(2)}) collective-permute-start(bf16[256,1024]{1,0:T(8,128)(2,1)} %get-tuple-element.6), channel_id=1, source_target_pairs={{0,1},{1,0},{2,3},{3,2},{4,5},{5,4},{6,7},{7,6},{8,9},{9,8},{10,11... | collective-permute-start | bytes 1572872 | tf_op jit(solution)/shard_map/ppermute | solution.py:39
  7.0 18.9 %collective-permute-start.22 = (bf16[512,512]{1,0:T(8,128)(2,1)}, bf16[512,512]{1,0:T(8,128)(2,1)}, u32[]{:S(2)}, u32[]{:S(2)}) collective-permute-start(bf16[512,512]{1,0:T(8,128)(2,1)} %param.8), channel_id=1, source_target_pairs={{0,1},{1,0},{2,3},{3,2},{4,5},{5,4},{6,7},{7,6},{8,9},{9,8},{10,11... | collective-permute-start | bytes 1572872 | tf_op jit(solution)/shard_map/ppermute | solution.py:39
  7.0 15.6 %collective-permute-start.5 = (bf16[512,512]{1,0:T(8,128)(2,1)}, bf16[512,512]{1,0:T(8,128)(2,1)}, u32[]{:S(2)}, u32[]{:S(2)}) collective-permute-start(bf16[512,512]{1,0:T(8,128)(2,1)} %param.8), channel_id=1, source_target_pairs={{0,4},{1,5},{2,6},{3,7},{4,12},{5,13},{6,14},{7,15},{12,8},{13,9},... | collective-permute-start | bytes 1572872 | tf_op jit(solution)/shard_map/ppermute | solution.py:42
  15.9 16.4 %collective-permute-start.27 = (bf16[256,1024]{1,0:T(8,128)(2,1)}, bf16[256,1024]{1,0:T(8,128)(2,1)}, u32[]{:S(2)}, u32[]{:S(2)}) collective-permute-start(bf16[256,1024]{1,0:T(8,128)(2,1)} %get-tuple-element.22), channel_id=1, source_target_pairs={{0,2},{1,3},{2,0},{3,1},{4,6},{5,7},{6,4},{7,5},{8,10},{9,11},{10,... | collective-permute-start | bytes 1572872 | tf_op jit(solution)/shard_map/ppermute | solution.py:39
  20.9 21.3 %collective-permute-start.3 = (bf16[256,1024]{0,1:T(8,128)(2,1)}, bf16[256,1024]{0,1:T(8,128)(2,1)S(1)}, u32[]{:S(2)}, u32[]{:S(2)}) collective-permute-start(bf16[256,1024]{0,1:T(8,128)(2,1)} %fusion.1), channel_id=1, source_target_pairs={{0,2},{1,3},{2,0},{3,1},{4,6},{5,7},{6,4},{7,5},{8,10},{9,11},{10,... | collective-permute-start | bytes 1572872 | tf_op jit(solution)/shard_map/ppermute | solution.py:39
  22.5 15.8 %collective-permute-start.23 = (bf16[512,512]{1,0:T(8,128)(2,1)}, bf16[512,512]{1,0:T(8,128)(2,1)}, u32[]{:S(2)}, u32[]{:S(2)}) collective-permute-start(bf16[512,512]{1,0:T(8,128)(2,1)} %collective-permute-done.5), channel_id=1, source_target_pairs={{0,1},{1,0},{2,3},{3,2},{4,5},{5,4},{6,7},{7,6},{8,9},{9,8},{10,11... | collective-permute-start | bytes 1572872 | tf_op jit(solution)/shard_map/ppermute | solution.py:39
  22.5 15.8 %collective-permute-start.6 = (bf16[512,512]{1,0:T(8,128)(2,1)}, bf16[512,512]{1,0:T(8,128)(2,1)S(1)}, u32[]{:S(2)}, u32[]{:S(2)}) collective-permute-start(bf16[512,512]{1,0:T(8,128)(2,1)} %collective-permute-done.5), channel_id=1, source_target_pairs={{0,4},{1,5},{2,6},{3,7},{4,12},{5,13},{6,14},{7,15},{12,8},{13,9},... | collective-permute-start | bytes 1572872 | tf_op jit(solution)/shard_map/ppermute | solution.py:42
  25.9 23.8 %collective-permute-start.4 = (bf16[256,1024]{1,0:T(8,128)(2,1)}, bf16[256,1024]{1,0:T(8,128)(2,1)}, u32[]{:S(2)}, u32[]{:S(2)}) collective-permute-start(bf16[256,1024]{1,0:T(8,128)(2,1)} %get-tuple-element.27), channel_id=1, source_target_pairs={{0,4},{1,5},{2,6},{3,7},{4,12},{5,13},{6,14},{7,15},{12,8},{13,9},... | collective-permute-start | bytes 1572872 | tf_op jit(solution)/shard_map/ppermute | solution.py:42
  32.3 28.7 %collective-permute-start.28 = (bf16[256,1024]{1,0:T(8,128)(2,1)S(1)}, bf16[256,1024]{1,0:T(8,128)(2,1)}, u32[]{:S(2)}, u32[]{:S(2)}) collective-permute-start(bf16[256,1024]{1,0:T(8,128)(2,1)S(1)} %copy-done.8), channel_id=1, source_target_pairs={{0,2},{1,3},{2,0},{3,1},{4,6},{5,7},{6,4},{7,5},{8,10},{9,11},{10,... | collective-permute-start | bytes 1572872 | tf_op jit(solution)/shard_map/ppermute | solution.py:39
  38.4 23.2 %collective-permute-start.24 = (bf16[512,512]{1,0:T(8,128)(2,1)S(1)}, bf16[512,512]{1,0:T(8,128)(2,1)}, u32[]{:S(2)}, u32[]{:S(2)}) collective-permute-start(bf16[512,512]{1,0:T(8,128)(2,1)S(1)} %collective-permute-done.6), channel_id=1, source_target_pairs={{0,1},{1,0},{2,3},{3,2},{4,5},{5,4},{6,7},{7,6},{8,9},{9,8},{10,11... | collective-permute-start | bytes 1572872 | tf_op jit(solution)/shard_map/ppermute | solution.py:39
  38.4 22.6 %collective-permute-start.11 = (bf16[512,512]{1,0:T(8,128)(2,1)S(1)}, bf16[512,512]{1,0:T(8,128)(2,1)}, u32[]{:S(2)}, u32[]{:S(2)}) collective-permute-start(bf16[512,512]{1,0:T(8,128)(2,1)S(1)} %collective-permute-done.6), channel_id=1, source_target_pairs={{0,4},{1,5},{2,6},{3,7},{4,12},{5,13},{6,14},{7,15},{12,8},{13,9},... | collective-permute-start | bytes 1572872 | tf_op jit(solution)/shard_map/ppermute | solution.py:42
  42.2 24.8 %collective-permute-start.29 = (bf16[256,1024]{1,0:T(8,128)(2,1)S(1)}, bf16[256,1024]{1,0:T(8,128)(2,1)}, u32[]{:S(2)}, u32[]{:S(2)}) collective-permute-start(bf16[256,1024]{1,0:T(8,128)(2,1)S(1)} %copy-done.7), channel_id=1, source_target_pairs={{0,2},{1,3},{2,0},{3,1},{4,6},{5,7},{6,4},{7,5},{8,10},{9,11},{10,... | collective-permute-start | bytes 1572872 | tf_op jit(solution)/shard_map/ppermute | solution.py:39
  45.2 15.8 %copy-start.6 = (bf16[256,1024]{1,0:T(8,128)(2,1)S(1)}, bf16[256,1024]{1,0:T(8,128)(2,1)}, u32[]{:S(2)}) copy-start(bf16[256,1024]{1,0:T(8,128)(2,1)} %get-tuple-element.21) | copy-start | bytes 1572868
  49.7 22.5 %collective-permute-start.7 = (bf16[256,1024]{1,0:T(8,128)(2,1)}, bf16[256,1024]{1,0:T(8,128)(2,1)}, u32[]{:S(2)}, u32[]{:S(2)}) collective-permute-start(bf16[256,1024]{1,0:T(8,128)(2,1)} %get-tuple-element.6), channel_id=1, source_target_pairs={{0,4},{1,5},{2,6},{3,7},{4,12},{5,13},{6,14},{7,15},{12,8},{13,9},... | collective-permute-start | bytes 1572872 | tf_op jit(solution)/shard_map/ppermute | solution.py:42
  60.9 12.0 %collective-permute-start.25 = (bf16[512,512]{1,0:T(8,128)(2,1)}, bf16[512,512]{1,0:T(8,128)(2,1)S(1)}, u32[]{:S(2)}, u32[]{:S(2)}) collective-permute-start(bf16[512,512]{1,0:T(8,128)(2,1)} %collective-permute-done.11), channel_id=1, source_target_pairs={{0,1},{1,0},{2,3},{3,2},{4,5},{5,4},{6,7},{7,6},{8,9},{9,8},{10,11... | collective-permute-start | bytes 1572872 | tf_op jit(solution)/shard_map/ppermute | solution.py:39
  61.0 19.4 %collective-permute-start.26 = (bf16[256,1024]{1,0:T(8,128)(2,1)S(1)}, bf16[256,1024]{1,0:T(8,128)(2,1)}, u32[]{:S(2)}, u32[]{:S(2)}) collective-permute-start(bf16[256,1024]{1,0:T(8,128)(2,1)S(1)} %copy-done.6), channel_id=1, source_target_pairs={{0,2},{1,3},{2,0},{3,1},{4,6},{5,7},{6,4},{7,5},{8,10},{9,11},{10,... | collective-permute-start | bytes 1572872 | tf_op jit(solution)/shard_map/ppermute | solution.py:39
  61.6 23.6 %collective-permute-start.8 = (bf16[256,1024]{1,0:T(8,128)(2,1)}, bf16[256,1024]{1,0:T(8,128)(2,1)}, u32[]{:S(2)}, u32[]{:S(2)}) collective-permute-start(bf16[256,1024]{1,0:T(8,128)(2,1)} %collective-permute-done.4), channel_id=1, source_target_pairs={{0,1},{1,0},{2,3},{3,2},{4,5},{5,4},{6,7},{7,6},{8,9},{9,8},{10,11... | collective-permute-start | bytes 1572872 | tf_op jit(solution)/shard_map/ppermute | solution.py:39
  67.0 27.3 %collective-permute-start.12 = (bf16[256,1024]{1,0:T(8,128)(2,1)}, bf16[256,1024]{1,0:T(8,128)(2,1)S(1)}, u32[]{:S(2)}, u32[]{:S(2)}) collective-permute-start(bf16[256,1024]{1,0:T(8,128)(2,1)} %collective-permute-done.4), channel_id=1, source_target_pairs={{0,4},{1,5},{2,6},{3,7},{4,12},{5,13},{6,14},{7,15},{12,8},{13,9},... | collective-permute-start | bytes 1572872 | tf_op jit(solution)/shard_map/ppermute | solution.py:42
  72.2 22.1 %collective-permute-start.13 = (bf16[256,1024]{1,0:T(8,128)(2,1)}, bf16[256,1024]{1,0:T(8,128)(2,1)}, u32[]{:S(2)}, u32[]{:S(2)}) collective-permute-start(bf16[256,1024]{1,0:T(8,128)(2,1)} %collective-permute-done.7), channel_id=1, source_target_pairs={{0,4},{1,5},{2,6},{3,7},{4,12},{5,13},{6,14},{7,15},{12,8},{13,9},... | collective-permute-start | bytes 1572872 | tf_op jit(solution)/shard_map/ppermute | solution.py:42
  73.0 12.2 %collective-permute-start.9 = (bf16[256,1024]{1,0:T(8,128)(2,1)}, bf16[256,1024]{1,0:T(8,128)(2,1)}, u32[]{:S(2)}, u32[]{:S(2)}) collective-permute-start(bf16[256,1024]{1,0:T(8,128)(2,1)} %collective-permute-done.7), channel_id=1, source_target_pairs={{0,1},{1,0},{2,3},{3,2},{4,5},{5,4},{6,7},{7,6},{8,9},{9,8},{10,11... | collective-permute-start | bytes 1572872 | tf_op jit(solution)/shard_map/ppermute | solution.py:39
  85.2 9.6 %collective-permute-start.30 = (bf16[8,32,1024]{2,1,0:T(8,128)(2,1)}, bf16[8,32,1024]{2,1,0:T(8,128)(2,1)}, u32[]{:S(2)}, u32[]{:S(2)}) collective-permute-start(bf16[8,32,1024]{2,1,0:T(8,128)(2,1)} %fusion.13), channel_id=1, source_target_pairs={{0,1},{1,0},{2,3},{3,2},{4,5},{5,4},{6,7},{7,6},{8,9},{9,8},{10,11... | collective-permute-start | bytes 1572872 | tf_op jit(solution)/shard_map/ppermute | solution.py:39
  94.3 12.3 %collective-permute-start.15 = (bf16[256,1024]{1,0:T(8,128)(2,1)}, bf16[256,1024]{1,0:T(8,128)(2,1)S(1)}, u32[]{:S(2)}, u32[]{:S(2)}) collective-permute-start(bf16[256,1024]{1,0:T(8,128)(2,1)} %collective-permute-done.13), channel_id=1, source_target_pairs={{0,1},{1,0},{2,3},{3,2},{4,5},{5,4},{6,7},{7,6},{8,9},{9,8},{10,11... | collective-permute-start | bytes 1572872 | tf_op jit(solution)/shard_map/ppermute | solution.py:39
  94.3 14.9 %collective-permute-start.14 = (bf16[256,1024]{1,0:T(8,128)(2,1)S(1)}, bf16[256,1024]{1,0:T(8,128)(2,1)S(1)}, u32[]{:S(2)}, u32[]{:S(2)}) collective-permute-start(bf16[256,1024]{1,0:T(8,128)(2,1)S(1)} %collective-permute-done.12), channel_id=1, source_target_pairs={{0,1},{1,0},{2,3},{3,2},{4,5},{5,4},{6,7},{7,6},{8,9},{9,8},{10,11... | collective-permute-start | bytes 1572872 | tf_op jit(solution)/shard_map/ppermute | solution.py:39
  96.1 9.2 %collective-permute-start.31 = (bf16[4,32,1024]{2,1,0:T(8,128)(2,1)S(1)}, bf16[4,32,1024]{2,1,0:T(8,128)(2,1)S(1)}, u32[]{:S(2)}, u32[]{:S(2)}) collective-permute-start(bf16[4,32,1024]{2,1,0:T(8,128)(2,1)S(1)} %fusion.20), channel_id=1, source_target_pairs={{0,2},{1,3},{2,0},{3,1},{4,6},{5,7},{6,4},{7,5},{8,10},{9,11},{10,... | collective-permute-start | bytes 786440 | tf_op jit(solution)/shard_map/ppermute | solution.py:39
  98.4 34.6 %collective-permute-start.10 = (bf16[256,1024]{0,1:T(8,128)(2,1)S(1)}, bf16[256,1024]{0,1:T(8,128)(2,1)S(1)}, u32[]{:S(2)}, u32[]{:S(2)}) collective-permute-start(bf16[256,1024]{0,1:T(8,128)(2,1)S(1)} %fusion.3), channel_id=1, source_target_pairs={{0,2},{1,3},{2,0},{3,1},{4,6},{5,7},{6,4},{7,5},{8,10},{9,11},{10,... | collective-permute-start | bytes 1572872 | tf_op jit(solution)/shard_map/ppermute | solution.py:39
  100.0 35.5 %collective-permute-start.18 = (bf16[256,1024]{1,0:T(8,128)(2,1)}, bf16[256,1024]{1,0:T(8,128)(2,1)S(1)}, u32[]{:S(2)}, u32[]{:S(2)}) collective-permute-start(bf16[256,1024]{1,0:T(8,128)(2,1)} %collective-permute-done.13), channel_id=1, source_target_pairs={{0,4},{1,5},{2,6},{3,7},{4,12},{5,13},{6,14},{7,15},{12,8},{13,9},... | collective-permute-start | bytes 1572872 | tf_op jit(solution)/shard_map/ppermute | solution.py:42
  105.4 11.8 %collective-permute-start.32 = (bf16[1,32,1024]{2,1,0:T(8,128)(2,1)S(1)}, bf16[1,32,1024]{2,1,0:T(8,128)(2,1)S(1)}, u32[]{:S(2)}, u32[]{:S(2)}) collective-permute-start(bf16[1,32,1024]{2,1,0:T(8,128)(2,1)S(1)} %get-tuple-element.31), channel_id=1, source_target_pairs={{0,4},{1,5},{2,6},{3,7},{4,0},{5,1},{6,2},{7,3},{8,12},{9,13},{10,... | collective-permute-start | bytes 196616 | tf_op jit(solution)/shard_map/ppermute | solution.py:39
  106.6 12.4 %collective-permute-start.34 = (bf16[1,32,1024]{2,1,0:T(8,128)(2,1)S(1)}, bf16[1,32,1024]{2,1,0:T(8,128)(2,1)S(1)}, u32[]{:S(2)}, u32[]{:S(2)}) collective-permute-start(bf16[1,32,1024]{2,1,0:T(8,128)(2,1)S(1)} %get-tuple-element.32), channel_id=1, source_target_pairs={{0,12},{1,13},{2,14},{3,15},{4,8},{5,9},{6,10},{7,11},{8,4},{9,5},... | collective-permute-start | bytes 196616 | tf_op jit(solution)/shard_map/ppermute | solution.py:39
  109.2 16.4 %copy-start.14 = (bf16[256,1024]{1,0:T(8,128)(2,1)S(1)}, bf16[256,1024]{1,0:T(8,128)(2,1)}, u32[]{:S(2)}) copy-start(bf16[256,1024]{1,0:T(8,128)(2,1)} %param.7) | copy-start | bytes 1572868
  109.2 10.9 %collective-permute-start.33 = (bf16[1,32,1024]{2,1,0:T(8,128)(2,1)S(1)}, bf16[1,32,1024]{2,1,0:T(8,128)(2,1)S(1)}, u32[]{:S(2)}, u32[]{:S(2)}) collective-permute-start(bf16[1,32,1024]{2,1,0:T(8,128)(2,1)S(1)} %get-tuple-element.33), channel_id=1, source_target_pairs={{0,8},{1,9},{2,10},{3,11},{4,12},{5,13},{6,14},{7,15},{8,0},{9,1},... | collective-permute-start | bytes 196616 | tf_op jit(solution)/shard_map/ppermute | solution.py:39
  121.4 5.8 %collective-permute-start.36 = (f32[8,128]{1,0:T(8,128)S(1)}, f32[8,128]{1,0:T(8,128)S(1)}, u32[]{:S(2)}, u32[]{:S(2)}) collective-permute-start(f32[8,128]{1,0:T(8,128)S(1)} %broadcast_in_dim.7), channel_id=1, source_target_pairs={{0,8},{1,9},{2,10},{3,11},{4,12},{5,13},{6,14},{7,15},{8,0},{9,1},... | collective-permute-start | bytes 12296 | tf_op jit(solution)/shard_map/ppermute | solution.py:39
  123.4 5.5 %collective-permute-start.37 = (f32[8,128]{1,0:T(8,128)S(1)}, f32[8,128]{1,0:T(8,128)S(1)}, u32[]{:S(2)}, u32[]{:S(2)}) collective-permute-start(f32[8,128]{1,0:T(8,128)S(1)} %broadcast_in_dim.7), channel_id=1, source_target_pairs={{0,12},{1,13},{2,14},{3,15},{4,8},{5,9},{6,10},{7,11},{8,4},{9,5},... | collective-permute-start | bytes 12296 | tf_op jit(solution)/shard_map/ppermute | solution.py:39
  125.1 4.0 %collective-permute-start.35 = (f32[8,128]{1,0:T(8,128)S(1)}, f32[8,128]{1,0:T(8,128)S(1)}, u32[]{:S(2)}, u32[]{:S(2)}) collective-permute-start(f32[8,128]{1,0:T(8,128)S(1)} %broadcast_in_dim.7), channel_id=1, source_target_pairs={{0,4},{1,5},{2,6},{3,7},{4,0},{5,1},{6,2},{7,3},{8,12},{9,13},{10,... | collective-permute-start | bytes 12296 | tf_op jit(solution)/shard_map/ppermute | solution.py:39
  127.1 12.8 %collective-permute-start.17 = (bf16[256,1024]{1,0:T(8,128)(2,1)S(1)}, bf16[256,1024]{1,0:T(8,128)(2,1)S(1)}, u32[]{:S(2)}, u32[]{:S(2)}) collective-permute-start(bf16[256,1024]{1,0:T(8,128)(2,1)S(1)} %collective-permute-done.12), channel_id=1, source_target_pairs={{0,4},{1,5},{2,6},{3,7},{4,12},{5,13},{6,14},{7,15},{12,8},{13,9},... | collective-permute-start | bytes 1572872 | tf_op jit(solution)/shard_map/ppermute | solution.py:42
  129.8 3.7 %collective-permute-start.38 = (f32[8,128]{1,0:T(8,128)S(1)}, f32[8,128]{1,0:T(8,128)S(1)}, u32[]{:S(2)}, u32[]{:S(2)}) collective-permute-start(f32[8,128]{1,0:T(8,128)S(1)} %add_add_fusion), channel_id=1, source_target_pairs={{0,2},{1,3},{2,0},{3,1},{4,6},{5,7},{6,4},{7,5},{8,10},{9,11},{10,... | collective-permute-start | bytes 12296 | tf_op jit(solution)/shard_map/ppermute | solution.py:39
  133.4 6.5 %collective-permute-start.39 = (f32[8,128]{1,0:T(8,128)S(1)}, f32[8,128]{1,0:T(8,128)S(1)}, u32[]{:S(2)}, u32[]{:S(2)}) collective-permute-start(f32[8,128]{1,0:T(8,128)S(1)} %add.227), channel_id=1, source_target_pairs={{0,1},{1,0},{2,3},{3,2},{4,5},{5,4},{6,7},{7,6},{8,9},{9,8},{10,11... | collective-permute-start | bytes 12296 | tf_op jit(solution)/shard_map/ppermute | solution.py:39
  135.5 16.4 %collective-permute-start.20 = (bf16[256,1024]{1,0:T(8,128)(2,1)S(1)}, bf16[256,1024]{1,0:T(8,128)(2,1)S(1)}, u32[]{:S(2)}, u32[]{:S(2)}) collective-permute-start(bf16[256,1024]{1,0:T(8,128)(2,1)S(1)} %collective-permute-done.18), channel_id=1, source_target_pairs={{0,1},{1,0},{2,3},{3,2},{4,5},{5,4},{6,7},{7,6},{8,9},{9,8},{10,11... | collective-permute-start | bytes 1572872 | tf_op jit(solution)/shard_map/ppermute | solution.py:39
  140.0 12.0 %collective-permute-start.19 = (bf16[256,1024]{1,0:T(8,128)(2,1)S(1)}, bf16[256,1024]{1,0:T(8,128)(2,1)S(1)}, u32[]{:S(2)}, u32[]{:S(2)}) collective-permute-start(bf16[256,1024]{1,0:T(8,128)(2,1)S(1)} %collective-permute-done.17), channel_id=1, source_target_pairs={{0,1},{1,0},{2,3},{3,2},{4,5},{5,4},{6,7},{7,6},{8,9},{9,8},{10,11... | collective-permute-start | bytes 1572872 | tf_op jit(solution)/shard_map/ppermute | solution.py:39
  142.0 5.6 %collective-permute-start.42 = (bf16[1,32,1024]{2,1,0:T(8,128)(2,1)S(1)}, bf16[1,32,1024]{2,1,0:T(8,128)(2,1)S(1)}, u32[]{:S(2)}, u32[]{:S(2)}) collective-permute-start(bf16[1,32,1024]{2,1,0:T(8,128)(2,1)S(1)} %get-tuple-element.16), channel_id=1, source_target_pairs={{0,4},{1,5},{2,6},{3,7},{4,0},{5,1},{6,2},{7,3},{8,12},{9,13},{10,... | collective-permute-start | bytes 196616 | tf_op jit(solution)/shard_map/ppermute | solution.py:39
  142.5 7.0 %collective-permute-start.41 = (bf16[1,32,1024]{2,1,0:T(8,128)(2,1)S(1)}, bf16[1,32,1024]{2,1,0:T(8,128)(2,1)S(1)}, u32[]{:S(2)}, u32[]{:S(2)}) collective-permute-start(bf16[1,32,1024]{2,1,0:T(8,128)(2,1)S(1)} %get-tuple-element.16), channel_id=1, source_target_pairs={{0,8},{1,9},{2,10},{3,11},{4,12},{5,13},{6,14},{7,15},{8,0},{9,1},... | collective-permute-start | bytes 196616 | tf_op jit(solution)/shard_map/ppermute | solution.py:39
  145.1 6.1 %collective-permute-start.40 = (bf16[1,32,1024]{2,1,0:T(8,128)(2,1)S(1)}, bf16[1,32,1024]{2,1,0:T(8,128)(2,1)S(1)}, u32[]{:S(2)}, u32[]{:S(2)}) collective-permute-start(bf16[1,32,1024]{2,1,0:T(8,128)(2,1)S(1)} %get-tuple-element.16), channel_id=1, source_target_pairs={{0,12},{1,13},{2,14},{3,15},{4,8},{5,9},{6,10},{7,11},{8,4},{9,5},... | collective-permute-start | bytes 196616 | tf_op jit(solution)/shard_map/ppermute | solution.py:39
  147.6 21.9 %collective-permute-start.16 = (bf16[256,1024]{0,1:T(8,128)(2,1)}, bf16[256,1024]{0,1:T(8,128)(2,1)S(1)}, u32[]{:S(2)}, u32[]{:S(2)}) collective-permute-start(bf16[256,1024]{0,1:T(8,128)(2,1)} %fusion.5), channel_id=1, source_target_pairs={{0,2},{1,3},{2,0},{3,1},{4,6},{5,7},{6,4},{7,5},{8,10},{9,11},{10,... | collective-permute-start | bytes 1572872 | tf_op jit(solution)/shard_map/ppermute | solution.py:39
  151.3 17.0 %collective-permute-start.43 = (bf16[4,32,1024]{2,1,0:T(8,128)(2,1)S(1)}, bf16[4,32,1024]{2,1,0:T(8,128)(2,1)S(1)}, u32[]{:S(2)}, u32[]{:S(2)}) collective-permute-start(bf16[4,32,1024]{2,1,0:T(8,128)(2,1)S(1)} %maximum_bitcast_fusion), channel_id=1, source_target_pairs={{0,2},{1,3},{2,0},{3,1},{4,6},{5,7},{6,4},{7,5},{8,10},{9,11},{10,... | collective-permute-start | bytes 786440 | tf_op jit(solution)/shard_map/ppermute | solution.py:39
  155.7 12.9 %copy-start.15 = (bf16[256,1024]{1,0:T(8,128)(2,1)S(1)}, bf16[256,1024]{1,0:T(8,128)(2,1)}, u32[]{:S(2)}) copy-start(bf16[256,1024]{1,0:T(8,128)(2,1)} %param.7) | copy-start | bytes 1572868
  155.7 22.2 %collective-permute-start.21 = (bf16[256,1024]{0,1:T(8,128)(2,1)}, bf16[256,1024]{0,1:T(8,128)(2,1)}, u32[]{:S(2)}, u32[]{:S(2)}) collective-permute-start(bf16[256,1024]{0,1:T(8,128)(2,1)} %fusion.7), channel_id=1, source_target_pairs={{0,2},{1,3},{2,0},{3,1},{4,6},{5,7},{6,4},{7,5},{8,10},{9,11},{10,... | collective-permute-start | bytes 1572872 | tf_op jit(solution)/shard_map/ppermute | solution.py:39
  168.4 12.4 %collective-permute-start.44 = (bf16[8,32,1024]{2,1,0:T(8,128)(2,1)S(1)}, bf16[8,32,1024]{2,1,0:T(8,128)(2,1)S(1)}, u32[]{:S(2)}, u32[]{:S(2)}) collective-permute-start(bf16[8,32,1024]{2,1,0:T(8,128)(2,1)S(1)} %bitcast.95), channel_id=1, source_target_pairs={{0,1},{1,0},{2,3},{3,2},{4,5},{5,4},{6,7},{7,6},{8,9},{9,8},{10,11... | collective-permute-start | bytes 1572872 | tf_op jit(solution)/shard_map/ppermute | solution.py:39
  (15 other events, 74.3 us)

commit v3 on v0

v3 whole, which is shorter than its diff:
```python
import functools
import jax
import jax.numpy as jnp
from jax import lax
from jax.experimental import pallas as pl
from jax.experimental.pallas import tpu as pltpu
from jax.sharding import PartitionSpec as P

clip_total = 512.0
step_size = 0.01
first_fix = 1.0 - 0.9**10
second_fix = 1.0 - 0.99**10

f32 = jnp.float32
bf16 = jnp.bfloat16
HBM = pl.BlockSpec(memory_space=pl.ANY)
VMEM = pl.BlockSpec(memory_space=pltpu.VMEM)
PARAMS = pltpu.CompilerParams(vmem_limit_bytes=40 * 2**20)


def after(value, *others):
    return lax.optimization_barrier((value,) + others)[0]


class Layout:
    def __init__(self, n):
        self.n = n
        self.sides = 2 if n == 16 else 1
        self.members = 2 * self.sides
        self.ring = n // self.members
        ring, members = self.ring, self.members
        order = [0, 1, 3, 2] if ring == 4 else list(range(ring))
        self.forward = [
            (order[k] * members + m, order[(k + 1) % ring] * members + m)
            for k in range(ring)
            for m in range(members)
        ]
        self.rounds = [(1, 2)]
        bit = 2
        if self.sides == 2:
            self.rounds.append((2, 2))
            bit = 4
        while bit < n:
            radix = 4 if 2 * bit < n else 2
            self.rounds.append((bit, radix))
            bit *= radix

    def swap(self, value, bit):
        return lax.ppermute(value, "dp", [(i, i ^ bit) for i in range(self.n)])

    def onward(self, value):
        return lax.ppermute(value, "dp", self.forward)

    def source(self, index, s):
        z = index // self.members
        if self.ring != 4:
            return (z - s + self.ring) % self.ring
        k = (z + z // 2 * (5 - 2 * z) - s + 4) % 4
        return k + k // 2 * (5 - 2 * k)


def flip(value, bit):
    return value + bit - 2 * bit * ((value // bit) % 2)


def cut_kernel(lay, rows, act, *refs):
    pieces, sems = refs[:-1], refs[-1]
    index = lax.axis_index("dp")
    member = index % lay.members
    copies = []
    for x in reversed(range(lay.members)):
        owner = member
        for bit in (1, 2):
            if x & bit:
                owner = flip(owner, bit)
        for s in range(lay.ring):
            start = pl.multiple_of((lay.source(index, s) * lay.members + owner) * rows, rows)
            copies.append(
                pltpu.make_async_copy(
                    act.at[:, pl.ds(start, rows)],
                    pieces[x].at[:, pl.ds(s * rows, rows)],
                    sems.at[x * lay.ring + s],
                )
            )
    for copy in copies:
        copy.start()
    for copy in copies:
        copy.wait()


def project_kernel(lay, owned, *refs):
    members, ring = lay.members, lay.ring
    acts, refs = refs[:members], refs[members:]
    basis, refs = refs[:ring], refs[ring:]
    grads, refs = refs[:members], refs[members:]
    kept, given, grad = refs
    rows = basis[0].shape[0]
    core = lax.axis_index("dp") % 2
    for x in range(members):
        total = jnp.dot(acts[x][:, :rows], basis[0][...], preferred_element_type=f32)
        for s in range(1, ring):
            total += jnp.dot(
                acts[x][:, s * rows : (s + 1) * rows],
                basis[s][...],
                preferred_element_type=f32,
            )
        term = lax.dot_general(
            total.astype(bf16),
            grads[x][...],
            (((0,), (0,)), ((), ())),
            preferred_element_type=f32,
        )
        if x == 0:
            grad[...] = term
        else:
            grad[...] += term
    for i in range(lay.n // 2):
        kept[i] = grad[pl.ds(pl.multiple_of((2 * i + core) * owned, owned), owned), :]
        given[i] = grad[pl.ds(pl.multiple_of((2 * i + 1 - core) * owned, owned), owned), :].astype(bf16)


def place(lay, s, side, low, width, rows, source, out, sems):
    index = lax.axis_index("dp")
    core = index % 2
    chip = lay.source(index, s) * lay.sides + side
    copies = []
    for k, owner in enumerate((core, 1 - core)):
        start = pl.multiple_of((chip * 2 + owner) * rows + low, width)
        copies.append(
            pltpu.make_async_copy(
                source.at[:, pl.ds(k * width, width)],
                out.at[:, pl.ds(start, width)],
                sems.at[k],
            )
        )
    return copies


def weight_kernel(lay, rows, s, low, parts, came, first, *refs):
    sides = lay.sides
    mine, refs = refs[:parts], refs[parts:]
    theirs, refs = refs[:parts], refs[parts:]
    grads, refs = refs[:sides], refs[sides:]
    if came is not None:
        arrived, refs = refs[0], refs[1:]
    if not first:
        refs = refs[1:]
    out, refs = refs[0], refs[1:]
    if sides == 2:
        far, refs = refs[0], refs[1:]
    own, sems, came_sems = refs
    height = mine[0].shape[0]
    width = parts * height
    side = (lax.axis_index("dp") // 2) % sides
    copies = []
    if came is not None:
        copies = place(
            lay, came[0], 1 - side, came[1], arrived.shape[1] // 2, rows, arrived, out, came_sems
        )
        for copy in copies:
            copy.start()
    for x in reversed(range(sides)):
        target = own if x == 0 else far
        for k, group in enumerate((mine, theirs)):
            for p, piece in enumerate(group):
                target[:, k * width + p * height : k * width + (p + 1) * height] = lax.dot_general(
                    grads[x][...],
                    piece[...],
                    (((1,), (1,)), ((), ())),
                    preferred_element_type=f32,
                ).astype(bf16)
    owns = place(lay, s, side, low, width, rows, own, out, sems)
    for copy in owns:
        copy.start()
    for copy in owns + copies:
        copy.wait()


def last_kernel(lay, rows, s, low, arrived, before, out, sems):
    side = (lax.axis_index("dp") // 2) % lay.sides
    copies = place(lay, s, 1 - side, low, arrived.shape[1] // 2, rows, arrived, out, sems)
    for copy in copies:
        copy.start()
    for copy in copies:
        copy.wait()


def back_kernel(lay, owned, basis, near, other, master, out, update):
    index = lax.axis_index("dp")
    half = lay.n // 2
    for j in range(lay.n):
        owner = index
        for bit in [1 << b for b in range(lay.n.bit_length() - 1)]:
            if slot_to_xor(lay, j) & bit:
                owner = flip(owner, bit)
        piece = near[j] if j < half else other[j - half]
        update[pl.ds(pl.multiple_of(owner * owned, owned), owned), :] = piece.astype(f32)
    out[...] = master[...] - step_size * jnp.dot(
        basis[...], update[...].astype(bf16), preferred_element_type=f32
    )


def slot_to_xor(lay, j):
    xor = 0
    for bit, radix in reversed(lay.rounds):
        xor += (j % radix) * bit
        j //= radix
    return xor


def make_per_device(n):
    lay = Layout(n)
    sides, members, ring, rounds = lay.sides, lay.members, lay.ring, lay.rounds
    swap, onward = lay.swap, lay.onward

    def per_device(activations, key_grad, proj_basis, master_weight, first_moment, second_moment):
        tokens = activations.shape[0]
        rows, rank = proj_basis.shape
        outs = key_grad.shape[1]
        index = lax.axis_index("dp")
        owned = rank // n
        parts = 2 if rows % 256 == 0 else 1
        height = rows // parts

        cut = pl.pallas_call(
            functools.partial(cut_kernel, lay, rows),
            name="cut",
            out_shape=[jax.ShapeDtypeStruct((tokens, ring * rows), bf16)] * members,
            in_specs=[HBM],
            out_specs=[VMEM] * members,
            scratch_shapes=[pltpu.SemaphoreType.DMA((members * ring,))],
            compiler_params=PARAMS,
            cost_estimate=pl.CostEstimate(
                flops=0, bytes_accessed=4 * tokens * ring * rows * members, transcendentals=0
            ),
        )(activations)
        acts = [cut[0]] + [swap(cut[x], x) for x in range(1, members)]

        weight = master_weight.astype(bf16)
        basis = [proj_basis]
        mine = [[weight[p * height : (p + 1) * height] for p in range(parts)]]
        for s in range(1, ring):
            value = basis[-1]
            if s == 2:
                value = started = after(value, cut[1])
            if s == 3:
                value = after(value, first_part)
            basis.append(onward(value))
            if s == 1:
                first_part = onward(mine[0][0])
        for s in range(1, ring):
            step = []
            for p in range(parts):
                value = mine[-1][p]
                if s == 1 and p == 0:
                    step.append(first_part)
                    continue
                if s == 1:
                    value = after(value, basis[ring - 2])
                if s == 2 and p == 0:
                    value = after(value, basis[ring - 1])
                step.append(onward(value))
            mine.append(step)
        theirs = [[swap(piece, 1) for piece in step] for step in mine]

        grads = [key_grad]
        if sides == 2:
            far_grad = swap(key_grad, 2)
            near = swap(
                jnp.concatenate([key_grad, after(far_grad, started)], axis=0), 1
            )
            grads = [key_grad, near[:tokens], far_grad, near[tokens:]]
        else:
            grads = [key_grad, swap(key_grad, 1)]

        total, given = pl.pallas_call(
            functools.partial(project_kernel, lay, owned),
            name="project",
            out_shape=[
                jax.ShapeDtypeStruct((n // 2, owned, outs), f32),
                jax.ShapeDtypeStruct((n // 2, owned, outs), bf16),
            ],
            in_specs=[VMEM] * (2 * members + ring),
            out_specs=[VMEM] * 2,
            scratch_shapes=[pltpu.VMEM((rank, outs), f32)],
            compiler_params=PARAMS,
            cost_estimate=pl.CostEstimate(
                flops=2 * tokens * members * rank * (ring * rows + outs),
                bytes_accessed=12 * 2**20,
                transcendentals=0,
            ),
        )(*acts, *basis, *grads)

        side_grads = [key_grad, far_grad] if sides == 2 else [key_grad]
        activation_grad = None
        waiting = None
        for s in range(ring):
            groups = [range(parts)] if s < ring - 1 else [[p] for p in range(parts)]
            for group in groups:
                low = group[0] * height
                width = len(group) * height
                args = [mine[s][p] for p in group] + [theirs[s][p] for p in group] + side_grads
                specs = [VMEM] * len(args)
                came = None
                if waiting is not None:
                    came = waiting[:2]
                    args.append(waiting[2])
                    specs.append(VMEM)
                first = activation_grad is None
                if not first:
                    args.append(activation_grad)
                    specs.append(HBM)
                shapes = [jax.ShapeDtypeStruct(activations.shape, bf16)]
                out_specs = [HBM]
                if sides == 2:
                    shapes.append(jax.ShapeDtypeStruct((tokens, 2 * width), bf16))
                    out_specs.append(VMEM)
                result = pl.pallas_call(
                    functools.partial(
                        weight_kernel, lay, rows, s, low, len(group), came, first
                    ),
                    name="weight",
                    out_shape=shapes,
                    in_specs=specs,
                    out_specs=out_specs,
                    scratch_shapes=[
                        pltpu.VMEM((tokens, 2 * width), bf16),
                        pltpu.SemaphoreType.DMA((2,)),
                        pltpu.SemaphoreType.DMA((2,)),
                    ],
                    input_output_aliases={} if first else {len(args) - 1: 0},
                    compiler_params=PARAMS,
                    cost_estimate=pl.CostEstimate(
                        flops=4 * sides * tokens * width * outs,
                        bytes_accessed=8 * 2**20,
                        transcendentals=0,
                    ),
                )(*args)
                activation_grad = result[0]
                if sides == 2:
                    waiting = (s, low, swap(result[1], 2))
        if waiting is not None:
            activation_grad = pl.pallas_call(
                functools.partial(last_kernel, lay, rows, waiting[0], waiting[1]),
                name="last",
                out_shape=jax.ShapeDtypeStruct(activations.shape, bf16),
                in_specs=[VMEM, HBM],
                out_specs=HBM,
                scratch_shapes=[pltpu.SemaphoreType.DMA((2,))],
                input_output_aliases={1: 0},
                compiler_params=PARAMS,
            )(waiting[2], activation_grad)

        for bit, radix in rounds:
            digit = (index // bit) % radix
            if bit == 1:
                total = total + swap(after(given, mine[1][-1]), 1).astype(f32)
                continue
            if bit == members:
                total = after(total, mine[2][0])
            total = total.reshape(total.shape[0] // radix, radix, owned, outs)
            kept = lax.dynamic_index_in_dim(total, digit, 1, keepdims=False)
            for j in range(1, radix):
                give = lax.dynamic_index_in_dim(total, digit ^ j, 1, keepdims=False)
                kept = kept + swap(give.astype(bf16), j * bit).astype(f32)
            total = kept
        owned_rows = total.reshape(owned, outs)

        square_sum = jnp.broadcast_to(jnp.sum(owned_rows * owned_rows), (8, 128))
        for bit, radix in reversed(rounds):
            square_sum = sum([swap(square_sum, j * bit) for j in range(1, radix)], square_sum)
        grad_norm = jnp.sqrt(square_sum[0, 0])
        factor = jnp.minimum(1.0, clip_total / (grad_norm + 1e-06))
        clipped = owned_rows * factor
        new_first = 0.9 * first_moment + 0.1 * clipped
        new_second = 0.99 * second_moment + 0.01 * clipped * clipped
        update = new_first / first_fix / (jnp.sqrt(new_second / second_fix) + 1e-08)

        whole = after(update.astype(bf16).reshape(1, owned, outs), mine[2][-1])
        for bit, radix in reversed(rounds[1:]):
            whole = jnp.concatenate(
                [whole] + [swap(whole, j * bit) for j in range(1, radix)], axis=0
            )
        new_master = pl.pallas_call(
            functools.partial(back_kernel, lay, owned),
            name="back",
            out_shape=jax.ShapeDtypeStruct(master_weight.shape, f32),
            in_specs=[VMEM] * 4,
            out_specs=VMEM,
            scratch_shapes=[pltpu.VMEM((rank, outs), f32)],
            compiler_params=PARAMS,
            cost_estimate=pl.CostEstimate(
                flops=2 * rows * rank * outs, bytes_accessed=8 * 2**20, transcendentals=0
            ),
        )(proj_basis, whole, swap(whole, 1), master_weight)
        return (activation_grad, new_master, new_first, new_second)

    return per_device


def solution(mesh):
    spec = P(("groups", "dp"), None)
    return jax.shard_map(
        make_per_device(mesh.shape["dp"]),
        mesh=mesh,
        in_specs=(spec,) * 6,
        out_specs=(spec,) * 4,
        check_vma=False,
    )
```

time: 371 us -> 180 us (0.49)
  waiting for transfers between devices: 297 us -> 100 us
  starting transfers between devices: 0.16 us -> 46.6 us
  blocking collectives: 30.1 us -> 0 us
  Pallas kernels: 0 us -> 21.3 us
  matrix products: 20.9 us -> 0 us
  between operations: 14.6 us -> 1.81 us
    all_gather x3 -> x0, waiting for transfers between devices: 236 us -> none  [the longest x1 124 us: per_device(): lax.all_gather(weight_bf16, 'dp', axis=0, tiled=True)]
    ppermute x0 -> x42, waiting for transfers between devices: none -> 100 us  [the longest x33 70.2 us: swap(): return lax.ppermute(value, 'dp', [(i, i ^ bit) for i in range(self.n)])]
    reduce_scatter x1 -> x0, waiting for transfers between devices: 59.9 us -> none  [per_device(): lax.psum_scatter(partial_grad, 'dp', scatter_dimension=0, tiled=True)]
    ppermute x0 -> x42, starting transfers between devices: none -> 46.6 us  [the longest x33 30 us: swap(): return lax.ppermute(value, 'dp', [(i, i ^ bit) for i in range(self.n)])]
    psum x1 -> x0, blocking collectives: 30.1 us -> none  [per_device(): square_sum = lax.psum(jnp.sum(owned_rows * owned_rows), 'dp')]
    pallas_call x0 -> x9, Pallas kernels: none -> 21.3 us  [the longest x5 12.7 us: per_device(): pl.pallas_call(functools.partial(weight_kernel, lay, rows, s, low, len(gr...]
    dot_general x3 -> x0, matrix products: 20.9 us -> none  [the longest x1 9.46 us: per_device(): jnp.dot(key_grad, lax.all_gather(weight_bf16, 'dp', axis=0, tiled=True).T...]
    add x0 -> x5, other arithmetic: none -> 3.9 us  [the longest x1 2.15 us: per_device(): total = total + swap(after(given, mine[1][-1]), 1).astype(f32)]
  transfers between devices with their start and end apart: 4 -> 42, of which waited for: 4 -> 19; matrix products, arithmetic and copies ran while one was open for 2% -> 5% of each run, Pallas kernels for 0% -> 11%
where the time goes in v3:
time: 180 us
  waiting for transfers between devices  100 us (56%)
  starting transfers between devices  46.6 us (26%)
  Pallas kernels  21.3 us (12%)
  other arithmetic  7.17 us (4%)
  local copies, waits for them, and re-layouts  2.47 us (1%)
  between operations  1.81 us (1%)
    ppermute x33, waiting for transfers between devices, swap(): return lax.ppermute(value, 'dp', [(i, i ^ bit) for i in range(self.n)])  70.2 us
    ppermute x9, waiting for transfers between devices, onward(): return lax.ppermute(value, 'dp', self.forward)  30.1 us
    ppermute x33, starting transfers between devices, swap(): return lax.ppermute(value, 'dp', [(i, i ^ bit) for i in range(self.n)])  30 us
    ppermute x9, starting transfers between devices, onward(): return lax.ppermute(value, 'dp', self.forward)  16.6 us
    pallas_call x5, Pallas kernels, per_device(): pl.pallas_call(functools.partial(weight_kernel, lay, rows, s, low, len(gr...  12.7 us
    pallas_call x1, Pallas kernels, per_device(): pl.pallas_call(functools.partial(project_kernel, lay, owned), name='proje...  5.13 us
  transfers between devices with their start and end apart: 42, of which 19 were waited for; matrix products, arithmetic and copies ran while one was open for 5% of the time, Pallas kernels for 11%

profile of v3, /device:TPU:0, one launch (start us, length us, event | category | flops | bytes accessed | tf_op | source)
XLA Modules:
  0.0 179.7 jit_solution(15073973048645753492)
XLA Ops:
  0.7 3.1 %collective-permute-start = (bf16[512,512]{1,0:T(8,128)(2,1)}, bf16[512,512]{1,0:T(8,128)(2,1)S(1)}, u32[]{:S(2)}, u32[]{:S(2)}) collective-permute-start(bf16[512,512]{1,0:T(8,128)(2,1)} %basis.1), channel_id=1, source_target_pairs={{0,4},{1,5},{2,6},{3,7},{4,12},{5,13},{6,14},{7,15},{12,8},{13,9},... | collective-permute-start | bytes 1572872 | tf_op jit(solution)/shard_map/ppermute | solution.py:52
  3.7 1.5 collective-permute-start.6
  5.2 1.7 convert_element_type.42
  7.1 2.6 %collective-permute-start.7 = (bf16[256,1024]{1,0:T(8,128)(2,1)S(1)}, bf16[256,1024]{1,0:T(8,128)(2,1)}, u32[]{:S(2)}, u32[]{:S(2)}) collective-permute-start(bf16[256,1024]{1,0:T(8,128)(2,1)S(1)} %get-tuple-element.59.refs_0_), channel_id=1, source_target_pairs={{0,4},{1,5},{2,6},{3,7},{4,12},{5,13},{6,14},{7,15},{12,8},{13,9},... | collective-permute-start | bytes 1572872 | tf_op jit(solution)/shard_map/ppermute | solution.py:52
  10.3 7.4 %collective-permute-done.refs_5_ = bf16[512,512]{1,0:T(8,128)(2,1)S(1)} collective-permute-done((bf16[512,512]{1,0:T(8,128)(2,1)}, bf16[512,512]{1,0:T(8,128)(2,1)S(1)}, u32[]{:S(2)}, u32[]{:S(2)}) %collective-permute-start) | collective-permute-done | bytes 524320 | tf_op jit(solution)/shard_map/ppermute | solution.py:52
  18.4 1.9 %collective-permute-start.24 = (bf16[256,2048]{1,0:T(8,128)(2,1)S(1)}, bf16[256,2048]{1,0:T(8,128)(2,1)S(1)}, u32[]{:S(2)}, u32[]{:S(2)}) collective-permute-start(bf16[256,2048]{1,0:T(8,128)(2,1)S(1)} %get-tuple-element.44), channel_id=1, source_target_pairs={{0,2},{1,3},{2,0},{3,1},{4,6},{5,7},{6,4},{7,5},{8,10},{9,11},{10,... | collective-permute-start | bytes 3145736 | tf_op jit(solution)/shard_map/ppermute | solution.py:49
  20.2 1.8 %collective-permute-start.1 = (bf16[512,512]{1,0:T(8,128)(2,1)S(1)}, bf16[512,512]{1,0:T(8,128)(2,1)S(1)}, u32[]{:S(2)}, u32[]{:S(2)}) collective-permute-start(bf16[512,512]{1,0:T(8,128)(2,1)S(1)} %collective-permute-done.refs_5_), channel_id=1, source_target_pairs={{0,4},{1,5},{2,6},{3,7},{4,12},{5,13},{6,14},{7,15},{12,8},{13,9},... | collective-permute-start | bytes 1572872 | tf_op jit(solution)/shard_map/ppermute | solution.py:52
  22.1 7.0 %collective-permute-done.7.refs_0_ = bf16[256,1024]{1,0:T(8,128)(2,1)} collective-permute-done((bf16[256,1024]{1,0:T(8,128)(2,1)S(1)}, bf16[256,1024]{1,0:T(8,128)(2,1)}, u32[]{:S(2)}, u32[]{:S(2)}) %collective-permute-start.7) | collective-permute-done | bytes 524320 | tf_op jit(solution)/shard_map/ppermute | solution.py:52
  29.0 10.3 %collective-permute-done.1.refs_6_ = bf16[512,512]{1,0:T(8,128)(2,1)S(1)} collective-permute-done((bf16[512,512]{1,0:T(8,128)(2,1)S(1)}, bf16[512,512]{1,0:T(8,128)(2,1)S(1)}, u32[]{:S(2)}, u32[]{:S(2)}) %collective-permute-start.1) | collective-permute-done | bytes 524320 | tf_op jit(solution)/shard_map/ppermute | solution.py:52
  39.3 0.8 collective-permute-start.8
  40.2 3.4 %collective-permute-start.2 = (bf16[256,1024]{1,0:T(8,128)(2,1)S(1)}, bf16[256,1024]{1,0:T(8,128)(2,1)}, u32[]{:S(2)}, u32[]{:S(2)}) collective-permute-start(bf16[256,1024]{1,0:T(8,128)(2,1)S(1)} %get-tuple-element.30.refs_1_), channel_id=1, source_target_pairs={{0,4},{1,5},{2,6},{3,7},{4,12},{5,13},{6,14},{7,15},{12,8},{13,9},... | collective-permute-start | bytes 1572872 | tf_op jit(solution)/shard_map/ppermute | solution.py:52
  44.4 21.0 %collective-permute-done.25.refs_3_ = bf16[256,2048]{1,0:T(8,128)(2,1)S(1)} collective-permute-done((bf16[256,2048]{1,0:T(8,128)(2,1)S(1)}, bf16[256,2048]{1,0:T(8,128)(2,1)S(1)}, u32[]{:S(2)}, u32[]{:S(2)}) %collective-permute-start.25) | collective-permute-done | bytes 1048608 | tf_op jit(solution)/shard_map/ppermute | solution.py:49
  65.4 5.1 %project.1 = (f32[8,32,1024]{2,1,0:T(8,128)S(1)}, bf16[8,32,1024]{2,1,0:T(8,128)(2,1)}) custom-call(bf16[256,2048]{1,0:T(8,128)(2,1)S(1)} %get-tuple-element.43.refs_0_, bf16[256,2048]{1,0:T(8,128)(2,1)S(1)} %collective-permute-done.23.refs_1_, bf16[256,2048]{1,0:T(8,128)(2,1)S(1)} %collective-permute-done.24.refs_2_, ...), custom_call_target="tpu_custom_call" | custom-call | flops 3221225472 | bytes 12582912 | tf_op jit(solution)/shard_map/project/pallas_call | solution.py:276
  71.6 2.1 %collective-permute-done.27 = bf16[8,32,1024]{2,1,0:T(8,128)(2,1)} collective-permute-done((bf16[8,32,1024]{2,1,0:T(8,128)(2,1)}, bf16[8,32,1024]{2,1,0:T(8,128)(2,1)}, u32[]{:S(2)}, u32[]{:S(2)}) %collective-permute-start.27) | collective-permute-done | bytes 524320 | tf_op jit(solution)/shard_map/ppermute | solution.py:49
  73.7 2.1 %convert_add_fusion = f32[8,32,1024]{2,1,0:T(8,128)} fusion(f32[8,32,1024]{2,1,0:T(8,128)S(1)} %get-tuple-element.47, bf16[8,32,1024]{2,1,0:T(8,128)(2,1)} %collective-permute-done.27), kind=kLoop, calls=%fused_computation.1 | loop fusion | flops 524288 | bytes 2621440 | tf_op jit(solution)/shard_map/add | solution.py:357
  75.8 1.1 fusion
  76.9 1.8 %collective-permute-start.28 = (bf16[4,32,1024]{2,1,0:T(8,128)(2,1)S(1)}, bf16[4,32,1024]{2,1,0:T(8,128)(2,1)S(1)}, u32[]{:S(2)}, u32[]{:S(2)}) collective-permute-start(bf16[4,32,1024]{2,1,0:T(8,128)(2,1)S(1)} %fusion), channel_id=1, source_target_pairs={{0,2},{1,3},{2,0},{3,1},{4,6},{5,7},{6,4},{7,5},{8,10},{9,11},{10,... | collective-permute-start | bytes 786440 | tf_op jit(solution)/shard_map/ppermute | solution.py:49
  78.7 1.8 %collective-permute-start.9 = (bf16[256,1024]{1,0:T(8,128)(2,1)}, bf16[256,1024]{1,0:T(8,128)(2,1)S(1)}, u32[]{:S(2)}, u32[]{:S(2)}) collective-permute-start(bf16[256,1024]{1,0:T(8,128)(2,1)} %collective-permute-done.7.refs_0_), channel_id=1, source_target_pairs={{0,4},{1,5},{2,6},{3,7},{4,12},{5,13},{6,14},{7,15},{12,8},{13,9},... | collective-permute-start | bytes 1572872 | tf_op jit(solution)/shard_map/ppermute | solution.py:52
  80.6 4.1 %weight.5 = (bf16[256,8192]{1,0:T(8,128)(2,1)}, bf16[256,1024]{1,0:T(8,128)(2,1)}) custom-call(bf16[256,1024]{1,0:T(8,128)(2,1)S(1)} %get-tuple-element.59.refs_0_, bf16[256,1024]{1,0:T(8,128)(2,1)S(1)} %get-tuple-element.30.refs_1_, bf16[256,1024]{1,0:T(8,128)(2,1)} %collective-permute-done.16.refs_2_, bf16[256,1024]{1,0:T(8,128)(2,1)} %collective-permute-done.17.refs_3_, ...), custom_call_target="tpu_custom_call" | custom-call | flops 1073741824 | bytes 8388608 | tf_op jit(solution)/shard_map/weight/pallas_call | solution.py:318
  85.8 2.3 %collective-permute-start.3 = (bf16[256,1024]{1,0:T(8,128)(2,1)}, bf16[256,1024]{1,0:T(8,128)(2,1)S(1)}, u32[]{:S(2)}, u32[]{:S(2)}) collective-permute-start(bf16[256,1024]{1,0:T(8,128)(2,1)} %collective-permute-done.2.refs_1_), channel_id=1, source_target_pairs={{0,4},{1,5},{2,6},{3,7},{4,12},{5,13},{6,14},{7,15},{12,8},{13,9},... | collective-permute-start | bytes 1572872 | tf_op jit(solution)/shard_map/ppermute | solution.py:52
  88.1 1.1 bitcast_add_fusion
  89.2 5.4 %collective-permute-done.9.refs_0_ = bf16[256,1024]{1,0:T(8,128)(2,1)S(1)} collective-permute-done((bf16[256,1024]{1,0:T(8,128)(2,1)}, bf16[256,1024]{1,0:T(8,128)(2,1)S(1)}, u32[]{:S(2)}, u32[]{:S(2)}) %collective-permute-start.9) | collective-permute-done | bytes 524320 | tf_op jit(solution)/shard_map/ppermute | solution.py:52
  94.6 1.0 collective-permute-start.29
  95.6 2.9 %collective-permute-done.18.refs_6_ = bf16[256,1024]{1,0:T(8,128)(2,1)S(1)} collective-permute-done((bf16[256,1024]{1,0:T(8,128)(2,1)}, bf16[256,1024]{1,0:T(8,128)(2,1)S(1)}, u32[]{:S(2)}, u32[]{:S(2)}) %collective-permute-start.18) | collective-permute-done | bytes 524320 | tf_op jit(solution)/shard_map/ppermute | solution.py:49
  98.6 1.1 collective-permute-start.30
  99.7 3.6 %collective-permute-start.31 = (bf16[1,32,1024]{2,1,0:T(8,128)(2,1)S(1)}, bf16[1,32,1024]{2,1,0:T(8,128)(2,1)S(1)}, u32[]{:S(2)}, u32[]{:S(2)}) collective-permute-start(bf16[1,32,1024]{2,1,0:T(8,128)(2,1)S(1)} %get-tuple-element.62), channel_id=1, source_target_pairs={{0,12},{1,13},{2,14},{3,15},{4,8},{5,9},{6,10},{7,11},{8,4},{9,5},... | collective-permute-start | bytes 196616 | tf_op jit(solution)/shard_map/ppermute | solution.py:49
  103.3 3.5 %weight.6 = (bf16[256,8192]{1,0:T(8,128)(2,1)}, bf16[256,1024]{1,0:T(8,128)(2,1)S(1)}) custom-call(bf16[256,1024]{1,0:T(8,128)(2,1)} %collective-permute-done.7.refs_0_, bf16[256,1024]{1,0:T(8,128)(2,1)} %collective-permute-done.2.refs_1_, bf16[256,1024]{1,0:T(8,128)(2,1)S(1)} %collective-permute-done.14.refs_2_, ...), custom_call_target="tpu_custom_call", output_to_operand_aliasing={{0}: (7, {})} | custom-call | flops 1073741824 | bytes 8388608 | tf_op jit(solution)/shard_map/weight/pallas_call | solution.py:318
  107.9 2.3 %collective-permute-done.31 = bf16[1,32,1024]{2,1,0:T(8,128)(2,1)S(1)} collective-permute-done((bf16[1,32,1024]{2,1,0:T(8,128)(2,1)S(1)}, bf16[1,32,1024]{2,1,0:T(8,128)(2,1)S(1)}, u32[]{:S(2)}, u32[]{:S(2)}) %collective-permute-start.31) | collective-permute-done | bytes 65568 | tf_op jit(solution)/shard_map/ppermute | solution.py:49
  111.5 1.2 collective-permute-start.32
  112.8 2.7 %collective-permute-start.33 = (f32[8,128]{1,0:T(8,128)S(1)}, f32[8,128]{1,0:T(8,128)S(1)}, u32[]{:S(2)}, u32[]{:S(2)}) collective-permute-start(f32[8,128]{1,0:T(8,128)S(1)} %broadcast_in_dim.3), channel_id=1, source_target_pairs={{0,8},{1,9},{2,10},{3,11},{4,12},{5,13},{6,14},{7,15},{8,0},{9,1},... | collective-permute-start | bytes 12296 | tf_op jit(solution)/shard_map/ppermute | solution.py:49
  115.5 3.0 %collective-permute-start.34 = (f32[8,128]{1,0:T(8,128)S(1)}, f32[8,128]{1,0:T(8,128)S(1)}, u32[]{:S(2)}, u32[]{:S(2)}) collective-permute-start(f32[8,128]{1,0:T(8,128)S(1)} %broadcast_in_dim.3), channel_id=1, source_target_pairs={{0,12},{1,13},{2,14},{3,15},{4,8},{5,9},{6,10},{7,11},{8,4},{9,5},... | collective-permute-start | bytes 12296 | tf_op jit(solution)/shard_map/ppermute | solution.py:49
  118.9 2.1 %collective-permute-done.34 = f32[8,128]{1,0:T(8,128)S(1)} collective-permute-done((f32[8,128]{1,0:T(8,128)S(1)}, f32[8,128]{1,0:T(8,128)S(1)}, u32[]{:S(2)}, u32[]{:S(2)}) %collective-permute-start.34) | collective-permute-done | bytes 4128 | tf_op jit(solution)/shard_map/ppermute | solution.py:49
  122.2 3.1 %collective-permute-done.35 = f32[8,128]{1,0:T(8,128)S(1)} collective-permute-done((f32[8,128]{1,0:T(8,128)S(1)}, f32[8,128]{1,0:T(8,128)S(1)}, u32[]{:S(2)}, u32[]{:S(2)}) %collective-permute-start.35) | collective-permute-done | bytes 4128 | tf_op jit(solution)/shard_map/ppermute | solution.py:49
  125.3 1.2 collective-permute-done.36
  128.0 0.8 fusion.3
  128.8 3.4 %collective-permute-start.37 = (bf16[1,32,1024]{2,1,0:T(8,128)(2,1)S(1)}, bf16[1,32,1024]{2,1,0:T(8,128)(2,1)S(1)}, u32[]{:S(2)}, u32[]{:S(2)}) collective-permute-start(bf16[1,32,1024]{2,1,0:T(8,128)(2,1)S(1)} %get-tuple-element.51), channel_id=1, source_target_pairs={{0,4},{1,5},{2,6},{3,7},{4,0},{5,1},{6,2},{7,3},{8,12},{9,13},{10,... | collective-permute-start | bytes 196616 | tf_op jit(solution)/shard_map/ppermute | solution.py:49
  132.2 2.4 %collective-permute-start.39 = (bf16[1,32,1024]{2,1,0:T(8,128)(2,1)S(1)}, bf16[1,32,1024]{2,1,0:T(8,128)(2,1)S(1)}, u32[]{:S(2)}, u32[]{:S(2)}) collective-permute-start(bf16[1,32,1024]{2,1,0:T(8,128)(2,1)S(1)} %get-tuple-element.51), channel_id=1, source_target_pairs={{0,12},{1,13},{2,14},{3,15},{4,8},{5,9},{6,10},{7,11},{8,4},{9,5},... | collective-permute-start | bytes 196616 | tf_op jit(solution)/shard_map/ppermute | solution.py:49
  134.6 2.1 %weight.7 = (bf16[256,8192]{1,0:T(8,128)(2,1)}, bf16[256,1024]{1,0:T(8,128)(2,1)S(1)}) custom-call(bf16[256,1024]{1,0:T(8,128)(2,1)S(1)} %collective-permute-done.9.refs_0_, bf16[256,1024]{1,0:T(8,128)(2,1)S(1)} %collective-permute-done.3.refs_1_, bf16[256,1024]{1,0:T(8,128)(2,1)S(1)} %collective-permute-done.12.refs_2_, ...), custom_call_target="tpu_custom_call", output_to_operand_aliasing={{0}: (7, {})} | custom-call | flops 1073741824 | bytes 8388608 | tf_op jit(solution)/shard_map/weight/pallas_call | solution.py:318
  136.7 8.0 %collective-permute-done.37 = bf16[1,32,1024]{2,1,0:T(8,128)(2,1)S(1)} collective-permute-done((bf16[1,32,1024]{2,1,0:T(8,128)(2,1)S(1)}, bf16[1,32,1024]{2,1,0:T(8,128)(2,1)S(1)}, u32[]{:S(2)}, u32[]{:S(2)}) %collective-permute-start.37) | collective-permute-done | bytes 65568 | tf_op jit(solution)/shard_map/ppermute | solution.py:49
  145.3 2.4 %collective-permute-done.38 = bf16[1,32,1024]{2,1,0:T(8,128)(2,1)S(1)} collective-permute-done((bf16[1,32,1024]{2,1,0:T(8,128)(2,1)S(1)}, bf16[1,32,1024]{2,1,0:T(8,128)(2,1)S(1)}, u32[]{:S(2)}, u32[]{:S(2)}) %collective-permute-start.38) | collective-permute-done | bytes 65568 | tf_op jit(solution)/shard_map/ppermute | solution.py:49
  148.4 11.2 %collective-permute-done.20.refs_4_ = bf16[256,1024]{1,0:T(8,128)(2,1)S(1)} collective-permute-done((bf16[256,1024]{1,0:T(8,128)(2,1)S(1)}, bf16[256,1024]{1,0:T(8,128)(2,1)S(1)}, u32[]{:S(2)}, u32[]{:S(2)}) %collective-permute-start.20) | collective-permute-done | bytes 524320 | tf_op jit(solution)/shard_map/ppermute | solution.py:49
  159.5 1.5 weight.8
  161.6 3.5 %collective-permute-done.40 = bf16[4,32,1024]{2,1,0:T(8,128)(2,1)S(1)} collective-permute-done((bf16[4,32,1024]{2,1,0:T(8,128)(2,1)S(1)}, bf16[4,32,1024]{2,1,0:T(8,128)(2,1)S(1)}, u32[]{:S(2)}, u32[]{:S(2)}) %collective-permute-start.40) | collective-permute-done | bytes 262176 | tf_op jit(solution)/shard_map/ppermute | solution.py:49
  165.3 4.6 %collective-permute-done.21.refs_4_ = bf16[256,512]{1,0:T(8,128)(2,1)S(1)} collective-permute-done((bf16[256,512]{1,0:T(8,128)(2,1)S(1)}, bf16[256,512]{1,0:T(8,128)(2,1)S(1)}, u32[]{:S(2)}, u32[]{:S(2)}) %collective-permute-start.21) | collective-permute-done | bytes 262176 | tf_op jit(solution)/shard_map/ppermute | solution.py:49
  169.8 1.5 weight.9
  171.9 2.2 %back.1 = f32[512,1024]{1,0:T(8,128)} custom-call(bf16[512,512]{1,0:T(8,128)(2,1)S(1)} %copy-done.4, bf16[8,32,1024]{2,1,0:T(8,128)(2,1)S(1)} %constant_dynamic-update-slice_fusion.near, bf16[8,32,1024]{2,1,0:T(8,128)(2,1)S(1)} %collective-permute-done.41.other, f32[512,1024]{1,0:T(8,128)S(1)} %copy-done.1), custom_call_target="tpu_custom_call" | custom-call | flops 536870912 | bytes 8388608 | tf_op jit(solution)/shard_map/back/pallas_call | solution.py:384
  174.1 4.7 %collective-permute-done.22.arrived = bf16[256,512]{1,0:T(8,128)(2,1)S(1)} collective-permute-done((bf16[256,512]{1,0:T(8,128)(2,1)S(1)}, bf16[256,512]{1,0:T(8,128)(2,1)S(1)}, u32[]{:S(2)}, u32[]{:S(2)}) %collective-permute-start.22) | collective-permute-done | bytes 262176 | tf_op jit(solution)/shard_map/ppermute | solution.py:49
  178.8 0.7 last.1
  (80 shorter events, 11.4 us)
Async XLA Ops:
  0.6 17.1 %copy-start = (bf16[256,1024]{1,0:T(8,128)(2,1)S(1)}, bf16[256,1024]{1,0:T(8,128)(2,1)}, u32[]{:S(2)}) copy-start(bf16[256,1024]{1,0:T(8,128)(2,1)} %refs_8_.1) | copy-start | bytes 1572868
  0.7 17.1 %collective-permute-start = (bf16[512,512]{1,0:T(8,128)(2,1)}, bf16[512,512]{1,0:T(8,128)(2,1)S(1)}, u32[]{:S(2)}, u32[]{:S(2)}) collective-permute-start(bf16[512,512]{1,0:T(8,128)(2,1)} %basis.1), channel_id=1, source_target_pairs={{0,4},{1,5},{2,6},{3,7},{4,12},{5,13},{6,14},{7,15},{12,8},{13,9},... | collective-permute-start | bytes 1572872 | tf_op jit(solution)/shard_map/ppermute | solution.py:52
  3.7 14.0 %collective-permute-start.6 = (bf16[256,1024]{1,0:T(8,128)(2,1)}, bf16[256,1024]{1,0:T(8,128)(2,1)S(1)}, u32[]{:S(2)}, u32[]{:S(2)}) collective-permute-start(bf16[256,1024]{1,0:T(8,128)(2,1)} %refs_8_.1), channel_id=1, source_target_pairs={{0,2},{1,3},{2,0},{3,1},{4,6},{5,7},{6,4},{7,5},{8,10},{9,11},{10,... | collective-permute-start | bytes 1572872 | tf_op jit(solution)/shard_map/ppermute | solution.py:49
  7.1 58.3 %copy-start.3 = (bf16[512,512]{1,0:T(8,128)(2,1)S(1)}, bf16[512,512]{1,0:T(8,128)(2,1)}, u32[]{:S(2)}) copy-start(bf16[512,512]{1,0:T(8,128)(2,1)} %basis.1) | copy-start | bytes 1572868
  7.1 22.0 %collective-permute-start.7 = (bf16[256,1024]{1,0:T(8,128)(2,1)S(1)}, bf16[256,1024]{1,0:T(8,128)(2,1)}, u32[]{:S(2)}, u32[]{:S(2)}) collective-permute-start(bf16[256,1024]{1,0:T(8,128)(2,1)S(1)} %get-tuple-element.59.refs_0_), channel_id=1, source_target_pairs={{0,4},{1,5},{2,6},{3,7},{4,12},{5,13},{6,14},{7,15},{12,8},{13,9},... | collective-permute-start | bytes 1572872 | tf_op jit(solution)/shard_map/ppermute | solution.py:52
  17.8 22.4 %collective-permute-start.26 = (bf16[512,1024]{1,0:T(8,128)(2,1)S(1)}, bf16[512,1024]{1,0:T(8,128)(2,1)S(1)}, u32[]{:S(2)}, u32[]{:S(2)}) collective-permute-start(bf16[512,1024]{1,0:T(8,128)(2,1)S(1)} %pad_maximum_fusion), channel_id=1, source_target_pairs={{0,1},{1,0},{2,3},{3,2},{4,5},{5,4},{6,7},{7,6},{8,9},{9,8},{10,11... | collective-permute-start | bytes 3145736 | tf_op jit(solution)/shard_map/ppermute | solution.py:49
  17.9 25.8 %collective-permute-start.23 = (bf16[256,2048]{1,0:T(8,128)(2,1)S(1)}, bf16[256,2048]{1,0:T(8,128)(2,1)S(1)}, u32[]{:S(2)}, u32[]{:S(2)}) collective-permute-start(bf16[256,2048]{1,0:T(8,128)(2,1)S(1)} %get-tuple-element.28), channel_id=1, source_target_pairs={{0,1},{1,0},{2,3},{3,2},{4,5},{5,4},{6,7},{7,6},{8,9},{9,8},{10,11... | collective-permute-start | bytes 3145736 | tf_op jit(solution)/shard_map/ppermute | solution.py:49
  18.4 26.0 %collective-permute-start.24 = (bf16[256,2048]{1,0:T(8,128)(2,1)S(1)}, bf16[256,2048]{1,0:T(8,128)(2,1)S(1)}, u32[]{:S(2)}, u32[]{:S(2)}) collective-permute-start(bf16[256,2048]{1,0:T(8,128)(2,1)S(1)} %get-tuple-element.44), channel_id=1, source_target_pairs={{0,2},{1,3},{2,0},{3,1},{4,6},{5,7},{6,4},{7,5},{8,10},{9,11},{10,... | collective-permute-start | bytes 3145736 | tf_op jit(solution)/shard_map/ppermute | solution.py:49
  20.2 19.1 %collective-permute-start.1 = (bf16[512,512]{1,0:T(8,128)(2,1)S(1)}, bf16[512,512]{1,0:T(8,128)(2,1)S(1)}, u32[]{:S(2)}, u32[]{:S(2)}) collective-permute-start(bf16[512,512]{1,0:T(8,128)(2,1)S(1)} %collective-permute-done.refs_5_), channel_id=1, source_target_pairs={{0,4},{1,5},{2,6},{3,7},{4,12},{5,13},{6,14},{7,15},{12,8},{13,9},... | collective-permute-start | bytes 1572872 | tf_op jit(solution)/shard_map/ppermute | solution.py:52
  29.0 36.4 %collective-permute-start.25 = (bf16[256,2048]{1,0:T(8,128)(2,1)S(1)}, bf16[256,2048]{1,0:T(8,128)(2,1)S(1)}, u32[]{:S(2)}, u32[]{:S(2)}) collective-permute-start(bf16[256,2048]{1,0:T(8,128)(2,1)S(1)} %get-tuple-element.45), channel_id=1, source_target_pairs={{0,3},{1,2},{2,1},{3,0},{4,7},{5,6},{6,5},{7,4},{8,11},{9,10},{10,... | collective-permute-start | bytes 3145736 | tf_op jit(solution)/shard_map/ppermute | solution.py:49
  39.3 26.1 %collective-permute-start.8 = (bf16[512,512]{1,0:T(8,128)(2,1)S(1)}, bf16[512,512]{1,0:T(8,128)(2,1)S(1)}, u32[]{:S(2)}, u32[]{:S(2)}) collective-permute-start(bf16[512,512]{1,0:T(8,128)(2,1)S(1)} %collective-permute-done.1.refs_6_), channel_id=1, source_target_pairs={{0,4},{1,5},{2,6},{3,7},{4,12},{5,13},{6,14},{7,15},{12,8},{13,9},... | collective-permute-start | bytes 1572872 | tf_op jit(solution)/shard_map/ppermute | solution.py:52
  40.2 30.4 %collective-permute-start.2 = (bf16[256,1024]{1,0:T(8,128)(2,1)S(1)}, bf16[256,1024]{1,0:T(8,128)(2,1)}, u32[]{:S(2)}, u32[]{:S(2)}) collective-permute-start(bf16[256,1024]{1,0:T(8,128)(2,1)S(1)} %get-tuple-element.30.refs_1_), channel_id=1, source_target_pairs={{0,4},{1,5},{2,6},{3,7},{4,12},{5,13},{6,14},{7,15},{12,8},{13,9},... | collective-permute-start | bytes 1572872 | tf_op jit(solution)/shard_map/ppermute | solution.py:52
  70.5 3.1 %collective-permute-start.27 = (bf16[8,32,1024]{2,1,0:T(8,128)(2,1)}, bf16[8,32,1024]{2,1,0:T(8,128)(2,1)}, u32[]{:S(2)}, u32[]{:S(2)}) collective-permute-start(bf16[8,32,1024]{2,1,0:T(8,128)(2,1)} %get-tuple-element.49), channel_id=1, source_target_pairs={{0,1},{1,0},{2,3},{3,2},{4,5},{5,4},{6,7},{7,6},{8,9},{9,8},{10,11... | collective-permute-start | bytes 1572872 | tf_op jit(solution)/shard_map/ppermute | solution.py:49
  71.1 9.5 %collective-permute-start.16 = (bf16[256,1024]{1,0:T(8,128)(2,1)S(1)}, bf16[256,1024]{1,0:T(8,128)(2,1)}, u32[]{:S(2)}, u32[]{:S(2)}) collective-permute-start(bf16[256,1024]{1,0:T(8,128)(2,1)S(1)} %get-tuple-element.59.refs_0_), channel_id=1, source_target_pairs={{0,1},{1,0},{2,3},{3,2},{4,5},{5,4},{6,7},{7,6},{8,9},{9,8},{10,11... | collective-permute-start | bytes 1572872 | tf_op jit(solution)/shard_map/ppermute | solution.py:49
  71.1 9.5 %collective-permute-start.17 = (bf16[256,1024]{1,0:T(8,128)(2,1)S(1)}, bf16[256,1024]{1,0:T(8,128)(2,1)}, u32[]{:S(2)}, u32[]{:S(2)}) collective-permute-start(bf16[256,1024]{1,0:T(8,128)(2,1)S(1)} %get-tuple-element.30.refs_1_), channel_id=1, source_target_pairs={{0,1},{1,0},{2,3},{3,2},{4,5},{5,4},{6,7},{7,6},{8,9},{9,8},{10,11... | collective-permute-start | bytes 1572872 | tf_op jit(solution)/shard_map/ppermute | solution.py:49
  76.9 8.9 %collective-permute-start.28 = (bf16[4,32,1024]{2,1,0:T(8,128)(2,1)S(1)}, bf16[4,32,1024]{2,1,0:T(8,128)(2,1)S(1)}, u32[]{:S(2)}, u32[]{:S(2)}) collective-permute-start(bf16[4,32,1024]{2,1,0:T(8,128)(2,1)S(1)} %fusion), channel_id=1, source_target_pairs={{0,2},{1,3},{2,0},{3,1},{4,6},{5,7},{6,4},{7,5},{8,10},{9,11},{10,... | collective-permute-start | bytes 786440 | tf_op jit(solution)/shard_map/ppermute | solution.py:49
  78.7 15.9 %collective-permute-start.9 = (bf16[256,1024]{1,0:T(8,128)(2,1)}, bf16[256,1024]{1,0:T(8,128)(2,1)S(1)}, u32[]{:S(2)}, u32[]{:S(2)}) collective-permute-start(bf16[256,1024]{1,0:T(8,128)(2,1)} %collective-permute-done.7.refs_0_), channel_id=1, source_target_pairs={{0,4},{1,5},{2,6},{3,7},{4,12},{5,13},{6,14},{7,15},{12,8},{13,9},... | collective-permute-start | bytes 1572872 | tf_op jit(solution)/shard_map/ppermute | solution.py:52
  84.7 13.9 %collective-permute-start.18 = (bf16[256,1024]{1,0:T(8,128)(2,1)}, bf16[256,1024]{1,0:T(8,128)(2,1)S(1)}, u32[]{:S(2)}, u32[]{:S(2)}) collective-permute-start(bf16[256,1024]{1,0:T(8,128)(2,1)} %get-tuple-element.33), channel_id=1, source_target_pairs={{0,2},{1,3},{2,0},{3,1},{4,6},{5,7},{6,4},{7,5},{8,10},{9,11},{10,... | collective-permute-start | bytes 1572872 | tf_op jit(solution)/shard_map/ppermute | solution.py:49
  85.2 14.4 %collective-permute-start.14 = (bf16[256,1024]{1,0:T(8,128)(2,1)}, bf16[256,1024]{1,0:T(8,128)(2,1)S(1)}, u32[]{:S(2)}, u32[]{:S(2)}) collective-permute-start(bf16[256,1024]{1,0:T(8,128)(2,1)} %collective-permute-done.7.refs_0_), channel_id=1, source_target_pairs={{0,1},{1,0},{2,3},{3,2},{4,5},{5,4},{6,7},{7,6},{8,9},{9,8},{10,11... | collective-permute-start | bytes 1572872 | tf_op jit(solution)/shard_map/ppermute | solution.py:49
  85.2 18.0 %collective-permute-start.15 = (bf16[256,1024]{1,0:T(8,128)(2,1)}, bf16[256,1024]{1,0:T(8,128)(2,1)}, u32[]{:S(2)}, u32[]{:S(2)}) collective-permute-start(bf16[256,1024]{1,0:T(8,128)(2,1)} %collective-permute-done.2.refs_1_), channel_id=1, source_target_pairs={{0,1},{1,0},{2,3},{3,2},{4,5},{5,4},{6,7},{7,6},{8,9},{9,8},{10,11... | collective-permute-start | bytes 1572872 | tf_op jit(solution)/shard_map/ppermute | solution.py:49
  85.8 21.6 %collective-permute-start.3 = (bf16[256,1024]{1,0:T(8,128)(2,1)}, bf16[256,1024]{1,0:T(8,128)(2,1)S(1)}, u32[]{:S(2)}, u32[]{:S(2)}) collective-permute-start(bf16[256,1024]{1,0:T(8,128)(2,1)} %collective-permute-done.2.refs_1_), channel_id=1, source_target_pairs={{0,4},{1,5},{2,6},{3,7},{4,12},{5,13},{6,14},{7,15},{12,8},{13,9},... | collective-permute-start | bytes 1572872 | tf_op jit(solution)/shard_map/ppermute | solution.py:52
  94.6 13.1 %collective-permute-start.29 = (bf16[1,32,1024]{2,1,0:T(8,128)(2,1)S(1)}, bf16[1,32,1024]{2,1,0:T(8,128)(2,1)S(1)}, u32[]{:S(2)}, u32[]{:S(2)}) collective-permute-start(bf16[1,32,1024]{2,1,0:T(8,128)(2,1)S(1)} %get-tuple-element.61), channel_id=1, source_target_pairs={{0,4},{1,5},{2,6},{3,7},{4,0},{5,1},{6,2},{7,3},{8,12},{9,13},{10,... | collective-permute-start | bytes 196616 | tf_op jit(solution)/shard_map/ppermute | solution.py:49
  98.6 9.3 %collective-permute-start.30 = (bf16[1,32,1024]{2,1,0:T(8,128)(2,1)S(1)}, bf16[1,32,1024]{2,1,0:T(8,128)(2,1)S(1)}, u32[]{:S(2)}, u32[]{:S(2)}) collective-permute-start(bf16[1,32,1024]{2,1,0:T(8,128)(2,1)S(1)} %get-tuple-element.63), channel_id=1, source_target_pairs={{0,8},{1,9},{2,10},{3,11},{4,12},{5,13},{6,14},{7,15},{8,0},{9,1},... | collective-permute-start | bytes 196616 | tf_op jit(solution)/shard_map/ppermute | solution.py:49
  99.7 10.6 %collective-permute-start.31 = (bf16[1,32,1024]{2,1,0:T(8,128)(2,1)S(1)}, bf16[1,32,1024]{2,1,0:T(8,128)(2,1)S(1)}, u32[]{:S(2)}, u32[]{:S(2)}) collective-permute-start(bf16[1,32,1024]{2,1,0:T(8,128)(2,1)S(1)} %get-tuple-element.62), channel_id=1, source_target_pairs={{0,12},{1,13},{2,14},{3,15},{4,8},{5,9},{6,10},{7,11},{8,4},{9,5},... | collective-permute-start | bytes 196616 | tf_op jit(solution)/shard_map/ppermute | solution.py:49
  103.3 24.7 %copy-start.5 = (f32[32,1024]{1,0:T(8,128)S(1)}, f32[32,1024]{1,0:T(8,128)}, u32[]{:S(2)}) copy-start(f32[32,1024]{1,0:T(8,128)} %param.10) | copy-start | bytes 393220
  103.3 24.7 %copy-start.6 = (f32[32,1024]{1,0:T(8,128)S(1)}, f32[32,1024]{1,0:T(8,128)}, u32[]{:S(2)}) copy-start(f32[32,1024]{1,0:T(8,128)} %param.11) | copy-start | bytes 393220
  106.8 22.0 %collective-permute-start.19 = (bf16[256,1024]{1,0:T(8,128)(2,1)S(1)}, bf16[256,1024]{1,0:T(8,128)(2,1)S(1)}, u32[]{:S(2)}, u32[]{:S(2)}) collective-permute-start(bf16[256,1024]{1,0:T(8,128)(2,1)S(1)} %get-tuple-element.35), channel_id=1, source_target_pairs={{0,2},{1,3},{2,0},{3,1},{4,6},{5,7},{6,4},{7,5},{8,10},{9,11},{10,... | collective-permute-start | bytes 1572872 | tf_op jit(solution)/shard_map/ppermute | solution.py:49
  107.4 24.8 %collective-permute-start.12 = (bf16[256,1024]{1,0:T(8,128)(2,1)S(1)}, bf16[256,1024]{1,0:T(8,128)(2,1)S(1)}, u32[]{:S(2)}, u32[]{:S(2)}) collective-permute-start(bf16[256,1024]{1,0:T(8,128)(2,1)S(1)} %collective-permute-done.9.refs_0_), channel_id=1, source_target_pairs={{0,1},{1,0},{2,3},{3,2},{4,5},{5,4},{6,7},{7,6},{8,9},{9,8},{10,11... | collective-permute-start | bytes 1572872 | tf_op jit(solution)/shard_map/ppermute | solution.py:49
  107.8 24.4 %collective-permute-start.13 = (bf16[256,1024]{1,0:T(8,128)(2,1)S(1)}, bf16[256,1024]{1,0:T(8,128)(2,1)S(1)}, u32[]{:S(2)}, u32[]{:S(2)}) collective-permute-start(bf16[256,1024]{1,0:T(8,128)(2,1)S(1)} %collective-permute-done.3.refs_1_), channel_id=1, source_target_pairs={{0,1},{1,0},{2,3},{3,2},{4,5},{5,4},{6,7},{7,6},{8,9},{9,8},{10,11... | collective-permute-start | bytes 1572872 | tf_op jit(solution)/shard_map/ppermute | solution.py:49
  111.5 3.9 %collective-permute-start.32 = (f32[8,128]{1,0:T(8,128)S(1)}, f32[8,128]{1,0:T(8,128)S(1)}, u32[]{:S(2)}, u32[]{:S(2)}) collective-permute-start(f32[8,128]{1,0:T(8,128)S(1)} %broadcast_in_dim.3), channel_id=1, source_target_pairs={{0,4},{1,5},{2,6},{3,7},{4,0},{5,1},{6,2},{7,3},{8,12},{9,13},{10,... | collective-permute-start | bytes 12296 | tf_op jit(solution)/shard_map/ppermute | solution.py:49
  112.8 5.7 %collective-permute-start.33 = (f32[8,128]{1,0:T(8,128)S(1)}, f32[8,128]{1,0:T(8,128)S(1)}, u32[]{:S(2)}, u32[]{:S(2)}) collective-permute-start(f32[8,128]{1,0:T(8,128)S(1)} %broadcast_in_dim.3), channel_id=1, source_target_pairs={{0,8},{1,9},{2,10},{3,11},{4,12},{5,13},{6,14},{7,15},{8,0},{9,1},... | collective-permute-start | bytes 12296 | tf_op jit(solution)/shard_map/ppermute | solution.py:49
  115.5 5.5 %collective-permute-start.34 = (f32[8,128]{1,0:T(8,128)S(1)}, f32[8,128]{1,0:T(8,128)S(1)}, u32[]{:S(2)}, u32[]{:S(2)}) collective-permute-start(f32[8,128]{1,0:T(8,128)S(1)} %broadcast_in_dim.3), channel_id=1, source_target_pairs={{0,12},{1,13},{2,14},{3,15},{4,8},{5,9},{6,10},{7,11},{8,4},{9,5},... | collective-permute-start | bytes 12296 | tf_op jit(solution)/shard_map/ppermute | solution.py:49
  118.5 26.7 %collective-permute-start.10 = (bf16[256,1024]{1,0:T(8,128)(2,1)S(1)}, bf16[256,1024]{1,0:T(8,128)(2,1)S(1)}, u32[]{:S(2)}, u32[]{:S(2)}) collective-permute-start(bf16[256,1024]{1,0:T(8,128)(2,1)S(1)} %collective-permute-done.9.refs_0_), channel_id=1, source_target_pairs={{0,4},{1,5},{2,6},{3,7},{4,12},{5,13},{6,14},{7,15},{12,8},{13,9},... | collective-permute-start | bytes 1572872 | tf_op jit(solution)/shard_map/ppermute | solution.py:52
  121.6 3.7 %collective-permute-start.35 = (f32[8,128]{1,0:T(8,128)S(1)}, f32[8,128]{1,0:T(8,128)S(1)}, u32[]{:S(2)}, u32[]{:S(2)}) collective-permute-start(f32[8,128]{1,0:T(8,128)S(1)} %add_add_fusion), channel_id=1, source_target_pairs={{0,2},{1,3},{2,0},{3,1},{4,6},{5,7},{6,4},{7,5},{8,10},{9,11},{10,... | collective-permute-start | bytes 12296 | tf_op jit(solution)/shard_map/ppermute | solution.py:49
  125.3 1.2 collective-permute-start.36
  126.5 21.8 %collective-permute-start.4 = (bf16[256,1024]{1,0:T(8,128)(2,1)S(1)}, bf16[256,1024]{1,0:T(8,128)(2,1)S(1)}, u32[]{:S(2)}, u32[]{:S(2)}) collective-permute-start(bf16[256,1024]{1,0:T(8,128)(2,1)S(1)} %collective-permute-done.3.refs_1_), channel_id=1, source_target_pairs={{0,4},{1,5},{2,6},{3,7},{4,12},{5,13},{6,14},{7,15},{12,8},{13,9},... | collective-permute-start | bytes 1572872 | tf_op jit(solution)/shard_map/ppermute | solution.py:52
  128.8 16.0 %collective-permute-start.37 = (bf16[1,32,1024]{2,1,0:T(8,128)(2,1)S(1)}, bf16[1,32,1024]{2,1,0:T(8,128)(2,1)S(1)}, u32[]{:S(2)}, u32[]{:S(2)}) collective-permute-start(bf16[1,32,1024]{2,1,0:T(8,128)(2,1)S(1)} %get-tuple-element.51), channel_id=1, source_target_pairs={{0,4},{1,5},{2,6},{3,7},{4,0},{5,1},{6,2},{7,3},{8,12},{9,13},{10,... | collective-permute-start | bytes 196616 | tf_op jit(solution)/shard_map/ppermute | solution.py:49
  132.1 15.5 %collective-permute-start.38 = (bf16[1,32,1024]{2,1,0:T(8,128)(2,1)S(1)}, bf16[1,32,1024]{2,1,0:T(8,128)(2,1)S(1)}, u32[]{:S(2)}, u32[]{:S(2)}) collective-permute-start(bf16[1,32,1024]{2,1,0:T(8,128)(2,1)S(1)} %get-tuple-element.51), channel_id=1, source_target_pairs={{0,8},{1,9},{2,10},{3,11},{4,12},{5,13},{6,14},{7,15},{8,0},{9,1},... | collective-permute-start | bytes 196616 | tf_op jit(solution)/shard_map/ppermute | solution.py:49
  132.2 15.5 %collective-permute-start.39 = (bf16[1,32,1024]{2,1,0:T(8,128)(2,1)S(1)}, bf16[1,32,1024]{2,1,0:T(8,128)(2,1)S(1)}, u32[]{:S(2)}, u32[]{:S(2)}) collective-permute-start(bf16[1,32,1024]{2,1,0:T(8,128)(2,1)S(1)} %get-tuple-element.51), channel_id=1, source_target_pairs={{0,12},{1,13},{2,14},{3,15},{4,8},{5,9},{6,10},{7,11},{8,4},{9,5},... | collective-permute-start | bytes 196616 | tf_op jit(solution)/shard_map/ppermute | solution.py:49
  144.7 14.8 %collective-permute-start.20 = (bf16[256,1024]{1,0:T(8,128)(2,1)S(1)}, bf16[256,1024]{1,0:T(8,128)(2,1)S(1)}, u32[]{:S(2)}, u32[]{:S(2)}) collective-permute-start(bf16[256,1024]{1,0:T(8,128)(2,1)S(1)} %get-tuple-element.37), channel_id=1, source_target_pairs={{0,2},{1,3},{2,0},{3,1},{4,6},{5,7},{6,4},{7,5},{8,10},{9,11},{10,... | collective-permute-start | bytes 1572872 | tf_op jit(solution)/shard_map/ppermute | solution.py:49
  145.3 14.3 %collective-permute-start.11 = (bf16[256,1024]{1,0:T(8,128)(2,1)S(1)}, bf16[256,1024]{1,0:T(8,128)(2,1)S(1)}, u32[]{:S(2)}, u32[]{:S(2)}) collective-permute-start(bf16[256,1024]{1,0:T(8,128)(2,1)S(1)} %collective-permute-done.10.refs_0_), channel_id=1, source_target_pairs={{0,1},{1,0},{2,3},{3,2},{4,5},{5,4},{6,7},{7,6},{8,9},{9,8},{10,11... | collective-permute-start | bytes 1572872 | tf_op jit(solution)/shard_map/ppermute | solution.py:49
  147.7 17.5 %collective-permute-start.40 = (bf16[4,32,1024]{2,1,0:T(8,128)(2,1)S(1)}, bf16[4,32,1024]{2,1,0:T(8,128)(2,1)S(1)}, u32[]{:S(2)}, u32[]{:S(2)}) collective-permute-start(bf16[4,32,1024]{2,1,0:T(8,128)(2,1)S(1)} %pad_maximum_fusion.1), channel_id=1, source_target_pairs={{0,2},{1,3},{2,0},{3,1},{4,6},{5,7},{6,4},{7,5},{8,10},{9,11},{10,... | collective-permute-start | bytes 786440 | tf_op jit(solution)/shard_map/ppermute | solution.py:49
  148.3 17.0 %collective-permute-start.5 = (bf16[256,1024]{1,0:T(8,128)(2,1)S(1)}, bf16[256,1024]{1,0:T(8,128)(2,1)S(1)}, u32[]{:S(2)}, u32[]{:S(2)}) collective-permute-start(bf16[256,1024]{1,0:T(8,128)(2,1)S(1)} %collective-permute-done.4.refs_0_), channel_id=1, source_target_pairs={{0,1},{1,0},{2,3},{3,2},{4,5},{5,4},{6,7},{7,6},{8,9},{9,8},{10,11... | collective-permute-start | bytes 1572872 | tf_op jit(solution)/shard_map/ppermute | solution.py:49
  161.0 10.9 %copy-start.1 = (f32[512,1024]{1,0:T(8,128)S(1)}, f32[512,1024]{1,0:T(8,128)}, u32[]{:S(2)}) copy-start(f32[512,1024]{1,0:T(8,128)} %master.1) | copy-start | bytes 6291460
  161.0 10.9 %copy-start.4 = (bf16[512,512]{1,0:T(8,128)(2,1)S(1)}, bf16[512,512]{1,0:T(8,128)(2,1)}, u32[]{:S(2)}) copy-start(bf16[512,512]{1,0:T(8,128)(2,1)} %basis.1) | copy-start | bytes 1572868
  161.1 8.8 %collective-permute-start.21 = (bf16[256,512]{1,0:T(8,128)(2,1)S(1)}, bf16[256,512]{1,0:T(8,128)(2,1)S(1)}, u32[]{:S(2)}, u32[]{:S(2)}) collective-permute-start(bf16[256,512]{1,0:T(8,128)(2,1)S(1)} %get-tuple-element.39), channel_id=1, source_target_pairs={{0,2},{1,3},{2,0},{3,1},{4,6},{5,7},{6,4},{7,5},{8,10},{9,11},{10,... | collective-permute-start | bytes 786440 | tf_op jit(solution)/shard_map/ppermute | solution.py:49
  165.2 6.7 %collective-permute-start.41 = (bf16[8,32,1024]{2,1,0:T(8,128)(2,1)S(1)}, bf16[8,32,1024]{2,1,0:T(8,128)(2,1)S(1)}, u32[]{:S(2)}, u32[]{:S(2)}) collective-permute-start(bf16[8,32,1024]{2,1,0:T(8,128)(2,1)S(1)} %constant_dynamic-update-slice_fusion.near), channel_id=1, source_target_pairs={{0,1},{1,0},{2,3},{3,2},{4,5},{5,4},{6,7},{7,6},{8,9},{9,8},{10,11... | collective-permute-start | bytes 1572872 | tf_op jit(solution)/shard_map/ppermute | solution.py:49
  171.3 7.5 %collective-permute-start.22 = (bf16[256,512]{1,0:T(8,128)(2,1)S(1)}, bf16[256,512]{1,0:T(8,128)(2,1)S(1)}, u32[]{:S(2)}, u32[]{:S(2)}) collective-permute-start(bf16[256,512]{1,0:T(8,128)(2,1)S(1)} %get-tuple-element.41), channel_id=1, source_target_pairs={{0,2},{1,3},{2,0},{3,1},{4,6},{5,7},{6,4},{7,5},{8,10},{9,11},{10,... | collective-permute-start | bytes 786440 | tf_op jit(solution)/shard_map/ppermute | solution.py:49
  (1 other events, 9.1 us)

commit v4 on v3

v4 whole, which is shorter than its diff:
```python
import functools
import jax
import jax.numpy as jnp
from jax import lax
from jax.experimental import pallas as pl
from jax.experimental.pallas import tpu as pltpu
from jax.sharding import PartitionSpec as P

clip_total = 512.0
step_size = 0.01
first_fix = 1.0 - 0.9**10
second_fix = 1.0 - 0.99**10

f32 = jnp.float32
bf16 = jnp.bfloat16
HBM = pl.BlockSpec(memory_space=pl.ANY)
VMEM = pl.BlockSpec(memory_space=pltpu.VMEM)
PARAMS = pltpu.CompilerParams(vmem_limit_bytes=40 * 2**20)


def after(value, *others):
    return lax.optimization_barrier((value,) + others)[0]


class Layout:
    def __init__(self, n):
        self.n = n
        self.sides = 2 if n == 16 else 1
        self.members = 2 * self.sides
        self.ring = n // self.members
        ring, members = self.ring, self.members
        order = [0, 1, 3, 2] if ring == 4 else list(range(ring))
        self.forward = [
            (order[k] * members + m, order[(k + 1) % ring] * members + m)
            for k in range(ring)
            for m in range(members)
        ]
        self.rounds = [(1, 2)]
        bit = 2
        if self.sides == 2:
            self.rounds.append((2, 2))
            bit = 4
        while bit < n:
            radix = 4 if 2 * bit < n else 2
            self.rounds.append((bit, radix))
            bit *= radix

    def swap(self, value, bit):
        return lax.ppermute(value, "dp", [(i, i ^ bit) for i in range(self.n)])

    def onward(self, value):
        return lax.ppermute(value, "dp", self.forward)

    def source(self, index, s):
        z = index // self.members
        if self.ring != 4:
            return (z - s + self.ring) % self.ring
        k = (z + z // 2 * (5 - 2 * z) - s + 4) % 4
        return k + k // 2 * (5 - 2 * k)


def flip(value, bit):
    return value + bit - 2 * bit * ((value // bit) % 2)


def cut_kernel(lay, rows, plan, act, *refs):
    pieces, sems = refs[:-1], refs[-1]
    index = lax.axis_index("dp")
    member = index % lay.members
    copies = []
    for (x, first, count), piece in zip(plan, pieces):
        owner = member
        for bit in (1, 2):
            if x & bit:
                owner = flip(owner, bit)
        for s in range(first, first + count):
            start = pl.multiple_of((lay.source(index, s) * lay.members + owner) * rows, rows)
            copies.append(
                pltpu.make_async_copy(
                    act.at[:, pl.ds(start, rows)],
                    piece.at[:, pl.ds((s - first) * rows, rows)],
                    sems.at[len(copies)],
                )
            )
    for copy in copies:
        copy.start()
    for copy in copies:
        copy.wait()


def project_kernel(lay, owned, plan, *refs):
    members, ring = lay.members, lay.ring
    acts, refs = refs[: len(plan)], refs[len(plan) :]
    basis, refs = refs[:ring], refs[ring:]
    grads, refs = refs[:members], refs[members:]
    kept, given, grad = refs
    rows = basis[0].shape[0]
    core = lax.axis_index("dp") % 2
    for x in range(members):
        total = None
        for (x_, first, count), piece in zip(plan, acts):
            if x_ != x:
                continue
            for s in range(first, first + count):
                term = jnp.dot(
                    piece[:, (s - first) * rows : (s - first + 1) * rows],
                    basis[s][...],
                    preferred_element_type=f32,
                )
                total = term if total is None else total + term
        term = lax.dot_general(
            total.astype(bf16),
            grads[x][...],
            (((0,), (0,)), ((), ())),
            preferred_element_type=f32,
        )
        if x == 0:
            grad[...] = term
        else:
            grad[...] += term
    for i in range(lay.n // 2):
        kept[i] = grad[pl.ds(pl.multiple_of((2 * i + core) * owned, owned), owned), :]
        given[i] = grad[pl.ds(pl.multiple_of((2 * i + 1 - core) * owned, owned), owned), :].astype(bf16)


def fold_kernel(bit, radix, came, *refs):
    kept, arrived, outs = refs[0], refs[1 : 1 + came], refs[1 + came :]
    digit = (lax.axis_index("dp") // bit) % radix

    def block(i):
        total = kept[i]
        for piece in arrived:
            total = total + piece[i].astype(f32)
        return total

    for i in range(kept.shape[0] // radix):
        for j in range(radix):
            other = digit
            for b in (1, 2):
                if j & b:
                    other = flip(other, b)
            value = block(i * radix + other)
            outs[j][i] = value.astype(outs[j].dtype)


def square_kernel(came, *refs):
    kept, arrived, (owned, square) = refs[0], refs[1 : 1 + came], refs[1 + came :]
    total = kept[0]
    for piece in arrived:
        total = total + piece[0].astype(f32)
    owned[...] = total
    square[...] = jnp.full(square.shape, jnp.sum(total * total), f32)


def moment_kernel(count, *refs):
    squares, (owned, first, second, new_first, new_second, update) = refs[:count], refs[count:]
    total = squares[0][...]
    for square in squares[1:]:
        total = total + square[...]
    factor = jnp.minimum(1.0, clip_total / (jnp.sqrt(total) + 1e-06))[0:1, 0:1]
    clipped = owned[...] * factor
    one = 0.9 * first[...] + 0.1 * clipped
    two = 0.99 * second[...] + 0.01 * clipped * clipped
    new_first[...] = one
    new_second[...] = two
    update[0] = (one / first_fix / (jnp.sqrt(two / second_fix) + 1e-08)).astype(bf16)


def place(lay, s, side, low, width, rows, source, out, sems):
    index = lax.axis_index("dp")
    core = index % 2
    chip = lay.source(index, s) * lay.sides + side
    copies = []
    for k, owner in enumerate((core, 1 - core)):
        start = pl.multiple_of((chip * 2 + owner) * rows + low, width)
        copies.append(
            pltpu.make_async_copy(
                source.at[:, pl.ds(k * width, width)],
                out.at[:, pl.ds(start, width)],
                sems.at[k],
            )
        )
    return copies


def weight_kernel(lay, rows, s, low, parts, came, first, *refs):
    sides = lay.sides
    mine, refs = refs[:parts], refs[parts:]
    theirs, refs = refs[:parts], refs[parts:]
    grads, refs = refs[:sides], refs[sides:]
    if came is not None:
        arrived, refs = refs[0], refs[1:]
    if not first:
        refs = refs[1:]
    out, refs = refs[0], refs[1:]
    if sides == 2:
        far, refs = refs[0], refs[1:]
    own, sems, came_sems = refs
    height = mine[0].shape[0]
    width = parts * height
    side = (lax.axis_index("dp") // 2) % sides
    copies = []
    if came is not None:
        copies = place(
            lay, came[0], 1 - side, came[1], arrived.shape[1] // 2, rows, arrived, out, came_sems
        )
        for copy in copies:
            copy.start()
    for x in reversed(range(sides)):
        target = own if x == 0 else far
        for k, group in enumerate((mine, theirs)):
            for p, piece in enumerate(group):
                target[:, k * width + p * height : k * width + (p + 1) * height] = lax.dot_general(
                    grads[x][...],
                    piece[...],
                    (((1,), (1,)), ((), ())),
                    preferred_element_type=f32,
                ).astype(bf16)
    owns = place(lay, s, side, low, width, rows, own, out, sems)
    for copy in owns:
        copy.start()
    for copy in owns + copies:
        copy.wait()


def last_kernel(lay, rows, s, low, arrived, before, out, sems):
    side = (lax.axis_index("dp") // 2) % lay.sides
    copies = place(lay, s, 1 - side, low, arrived.shape[1] // 2, rows, arrived, out, sems)
    for copy in copies:
        copy.start()
    for copy in copies:
        copy.wait()


def back_kernel(lay, owned, basis, near, other, master, out, update):
    index = lax.axis_index("dp")
    half = lay.n // 2
    for j in range(lay.n):
        owner = index
        for bit in [1 << b for b in range(lay.n.bit_length() - 1)]:
            if slot_to_xor(lay, j) & bit:
                owner = flip(owner, bit)
        piece = near[j] if j < half else other[j - half]
        update[pl.ds(pl.multiple_of(owner * owned, owned), owned), :] = piece.astype(f32)
    out[...] = master[...] - step_size * jnp.dot(
        basis[...], update[...].astype(bf16), preferred_element_type=f32
    )


def slot_to_xor(lay, j):
    xor = 0
    for bit, radix in reversed(lay.rounds):
        xor += (j % radix) * bit
        j //= radix
    return xor


class Queue:
    def __init__(self):
        self.results = []

    def send(self, move, value):
        if len(self.results) >= 2:
            value = after(value, self.results[-2])
        self.results.append(move(value))
        return self.results[-1]


def call(kernel, name, shapes, args, in_specs=None, out_specs=None, scratch=(), flops=0, moved=2**20, **more):
    return pl.pallas_call(
        kernel,
        name=name,
        out_shape=[jax.ShapeDtypeStruct(shape, dtype) for shape, dtype in shapes],
        in_specs=in_specs or [VMEM] * len(args),
        out_specs=out_specs or [VMEM] * len(shapes),
        scratch_shapes=list(scratch),
        compiler_params=PARAMS,
        cost_estimate=pl.CostEstimate(flops=flops, bytes_accessed=moved, transcendentals=0),
        **more,
    )(*args)


def make_per_device(n):
    lay = Layout(n)
    sides, members, ring, rounds = lay.sides, lay.members, lay.ring, lay.rounds
    swap, onward = lay.swap, lay.onward

    def per_device(activations, key_grad, proj_basis, master_weight, first_moment, second_moment):
        tokens, width = activations.shape
        rows, rank = proj_basis.shape
        outs = key_grad.shape[1]
        owned = rank // n
        parts = 2 if rows % 256 == 0 else 1
        height = rows // parts
        z_queue, y_queue = Queue(), Queue()

        def swap_side(value):
            return y_queue.send(lambda v: swap(v, 2), value)

        def go_on(value):
            return z_queue.send(onward, value)

        plan = [(0, 0, ring), (1, 0, ring)]
        for x in range(2, members):
            plan += [(x, 0, ring // 2), (x, ring // 2, ring // 2)]
        cut = call(
            functools.partial(cut_kernel, lay, rows, plan),
            "cut",
            [((tokens, count * rows), bf16) for x, first, count in plan],
            [activations],
            in_specs=[HBM],
            scratch=[pltpu.SemaphoreType.DMA((members * ring,))],
            moved=4 * tokens * ring * rows * members,
        )

        weight = master_weight.astype(bf16)
        basis = [proj_basis]
        mine = [[weight[p * height : (p + 1) * height] for p in range(parts)]]
        mine += [[None] * parts for s in range(1, ring)]
        far_grad = swap_side(key_grad) if sides == 2 else None
        sends = []
        for s in range(1, ring):
            sends.append((s, None))
            if s <= parts:
                sends.append((1, s - 1))
        sends += [(s, p) for s in range(2, ring) for p in range(parts)]
        early = [send for send in sends if send[1] is None or send[0] <= 2]
        for s, p in early:
            if p is None:
                basis.append(go_on(basis[-1]))
            else:
                mine[s][p] = go_on(mine[s - 1][p])

        acts = list(cut)
        for k, (x, first, count) in enumerate(plan):
            if x >= 2:
                swap_x = functools.partial(swap, bit=x)
                acts[k] = y_queue.send(swap_x, cut[k])
        acts[1] = swap(after(cut[1], basis[1]), 1)
        if sides == 2:
            near = swap(jnp.concatenate([key_grad, after(far_grad, basis[1])], axis=0), 1)
            grads = [key_grad, near[:tokens], far_grad, near[tokens:]]
        else:
            grads = [key_grad, swap(key_grad, 1)]

        side_grads = [key_grad, far_grad] if sides == 2 else [key_grad]
        state = {"out": None, "waiting": None}

        def multiply(s, group, gate=None):
            low = group[0] * height
            wide = len(group) * height
            args = [mine[s][p] for p in group] + [swap(mine[s][p], 1) for p in group] + side_grads
            if gate is not None:
                args[0] = after(args[0], gate)
            in_specs = [VMEM] * len(args)
            came = None
            if state["waiting"] is not None:
                came = state["waiting"][:2]
                args.append(state["waiting"][2])
                in_specs.append(VMEM)
            first = state["out"] is None
            if not first:
                args.append(state["out"])
                in_specs.append(HBM)
            shapes, out_specs = [((tokens, width), bf16)], [HBM]
            if sides == 2:
                shapes.append(((tokens, 2 * wide), bf16))
                out_specs.append(VMEM)
            result = call(
                functools.partial(weight_kernel, lay, rows, s, low, len(group), came, first),
                "weight",
                shapes,
                args,
                in_specs,
                out_specs,
                scratch=[
                    pltpu.VMEM((tokens, 2 * wide), bf16),
                    pltpu.SemaphoreType.DMA((2,)),
                    pltpu.SemaphoreType.DMA((2,)),
                ],
                flops=4 * sides * tokens * wide * outs,
                moved=6 * 2**20,
                input_output_aliases={} if first else {len(args) - 1: 0},
            )
            state["out"] = result[0]
            state["waiting"] = None
            return result[1] if sides == 2 else None

        def give_back(s, group, block, gate=None):
            if sides == 2:
                if gate is not None:
                    block = after(block, gate)
                state["waiting"] = (s, group[0] * height, swap_side(block))

        everything = list(range(parts))
        block = multiply(0, everything)
        give_back(0, everything, block)
        block = multiply(1, everything)

        total, *gives = call(
            functools.partial(project_kernel, lay, owned, plan),
            "project",
            [((n // 2, owned, outs), f32), ((n // 2, owned, outs), bf16)],
            [after(acts[0], state["out"])] + acts[1:] + basis + grads,
            scratch=[pltpu.VMEM((rank, outs), f32)],
            flops=2 * tokens * members * rank * (ring * rows + outs),
            moved=12 * 2**20,
        )

        for k, (bit, radix) in enumerate(rounds):
            if bit == members:
                gives = [after(give, mine[2][0]) for give in gives]
            came = [swap(give, j * bit) for j, give in zip(range(1, radix), gives)]
            if k == len(rounds) - 1:
                break
            next_bit, next_radix = rounds[k + 1]
            shape = (total.shape[0] // next_radix, owned, outs)
            total, *gives = call(
                functools.partial(fold_kernel, next_bit, next_radix, len(came)),
                "fold",
                [(shape, f32)] + [(shape, bf16)] * (next_radix - 1),
                [total] + came,
                moved=4 * total.size,
            )
            if bit == 2 and sides == 2:
                give_back(1, everything, block, total)
        owned_rows, square = call(
            functools.partial(square_kernel, len(came)),
            "square",
            [((owned, outs), f32), ((8, 128), f32)],
            [total] + came,
        )
        for bit, radix in reversed(rounds):
            if bit >= members:
                square = sum([swap(square, j * bit) for j in range(1, radix)], square)
        squares = [square] + [swap(square, x) for x in range(1, members)]
        if sides == 1:
            give_back(1, everything, block)
        for s, p in sends:
            if (s, p) not in early and p == 0 and s == 3:
                mine[s][p] = go_on(after(mine[s - 1][p], square))
        if ring > 2:
            block = multiply(2, everything, square)
        new_first, new_second, update = call(
            functools.partial(moment_kernel, members),
            "moment",
            [((owned, outs), f32), ((owned, outs), f32), ((1, owned, outs), bf16)],
            squares + [owned_rows, first_moment, second_moment],
        )
        if ring > 2:
            give_back(2, everything, block, squares[-1])
        for s, p in sends:
            if p is not None and mine[s][p] is None:
                mine[s][p] = go_on(after(mine[s - 1][p], update))

        whole = update
        for bit, radix in reversed(rounds[1:]):
            whole = jnp.concatenate(
                [whole] + [swap(whole, j * bit) for j in range(1, radix)], axis=0
            )
        (new_master,) = call(
            functools.partial(back_kernel, lay, owned),
            "back",
            [(master_weight.shape, f32)],
            [proj_basis, whole, swap(whole, 1), master_weight],
            scratch=[pltpu.VMEM((rank, outs), f32)],
            flops=2 * rows * rank * outs,
            moved=8 * 2**20,
        )

        for s in range(3, ring):
            groups = [everything] if s < ring - 1 else [[p] for p in everything]
            for group in groups:
                block = multiply(s, group)
                give_back(s, group, block, whole if s == 3 and group[0] == 0 else None)
        activation_grad = state["out"]
        if state["waiting"] is not None:
            s, low, arrived = state["waiting"]
            (activation_grad,) = call(
                functools.partial(last_kernel, lay, rows, s, low),
                "last",
                [((tokens, width), bf16)],
                [arrived, activation_grad],
                [VMEM, HBM],
                [HBM],
                scratch=[pltpu.SemaphoreType.DMA((2,))],
                input_output_aliases={1: 0},
            )
        return (activation_grad, new_master, new_first, new_second)

    return per_device


def solution(mesh):
    spec = P(("groups", "dp"), None)
    return jax.shard_map(
        make_per_device(mesh.shape["dp"]),
        mesh=mesh,
        in_specs=(spec,) * 6,
        out_specs=(spec,) * 4,
        check_vma=False,
    )
```

time: 180 us -> 192 us (1.067)
  waiting for transfers between devices: 100 us -> 123 us
  other arithmetic: 7.17 us -> 0.27 us
  Pallas kernels: 21.3 us -> 18.2 us
    ppermute x33 -> x36, waiting for transfers between devices: 70.2 us -> 106 us  [swap(): return lax.ppermute(value, 'dp', [(i, i ^ bit) for i in range(self.n)])]
    ppermute x9, waiting for transfers between devices: 30.1 us -> 16.6 us  [onward(): return lax.ppermute(value, 'dp', self.forward)]
    add x5 -> x1, other arithmetic: 3.9 us -> 0.01 us  [per_device(): square = sum([swap(square, j * bit) for j in range(1, radix)], square)]
    pallas_call x9 -> x13, Pallas kernels: 21.3 us -> 18.2 us  [call(): pl.pallas_call(kernel, name=name, out_shape=[jax.ShapeDtypeStruct(shape,...]
    unnamed x18 -> x16, local copies, waits for them, and re-layouts: 0.06 us -> 2.37 us
    ppermute x33 -> x36, starting transfers between devices: 30 us -> 31.4 us  [swap(): return lax.ppermute(value, 'dp', [(i, i ^ bit) for i in range(self.n)])]
  transfers between devices with their start and end apart: 42 -> 45, of which waited for: 19 -> 23; matrix products, arithmetic and copies ran while one was open for 5% -> 0% of each run, Pallas kernels for 11% -> 7%
where the time goes in v4:
time: 192 us
  waiting for transfers between devices  123 us (64%)
  starting transfers between devices  46.9 us (24%)
  Pallas kernels  18.2 us (9%)
  local copies, waits for them, and re-layouts  2.53 us (1%)
    ppermute x36, waiting for transfers between devices, swap(): return lax.ppermute(value, 'dp', [(i, i ^ bit) for i in range(self.n)])  106 us
    ppermute x36, starting transfers between devices, swap(): return lax.ppermute(value, 'dp', [(i, i ^ bit) for i in range(self.n)])  31.4 us
    pallas_call x13, Pallas kernels, call(): pl.pallas_call(kernel, name=name, out_shape=[jax.ShapeDtypeStruct(shape,...  18.2 us
    ppermute x9, waiting for transfers between devices, onward(): return lax.ppermute(value, 'dp', self.forward)  16.6 us
    ppermute x9, starting transfers between devices, onward(): return lax.ppermute(value, 'dp', self.forward)  15.4 us
  transfers between devices with their start and end apart: 45, of which 23 were waited for; matrix products, arithmetic and copies ran while one was open for 0% of the time, Pallas kernels for 7%

profile of v4, /device:TPU:0, one launch (start us, length us, event | category | flops | bytes accessed | tf_op | source)
XLA Modules:
  0.0 192.0 jit_solution(16986396485445563994)
XLA Ops:
  0.7 2.3 %copy-done.2 = bf16[256,8192]{1,0:T(8,128)(2,1)S(1)} copy-done((bf16[256,8192]{1,0:T(8,128)(2,1)S(1)}, bf16[256,8192]{1,0:T(8,128)(2,1)}, u32[]{:S(2)}) %copy-start.2) | copy-done | bytes 4194328
  3.5 3.0 %collective-permute-start.11 = (bf16[256,1024]{1,0:T(8,128)(2,1)S(1)}, bf16[256,1024]{1,0:T(8,128)(2,1)S(1)}, u32[]{:S(2)}, u32[]{:S(2)}) collective-permute-start(bf16[256,1024]{1,0:T(8,128)(2,1)S(1)} %get-tuple-element.66), channel_id=1, source_target_pairs={{0,2},{1,3},{2,0},{3,1},{4,6},{5,7},{6,4},{7,5},{8,10},{9,11},{10,... | collective-permute-start | bytes 1572872 | tf_op jit(solution)/shard_map/ppermute | solution.py:49
  6.8 1.6 collective-permute-start
  8.9 2.6 %collective-permute-start.2 = (bf16[512,512]{1,0:T(8,128)(2,1)S(1)}, bf16[512,512]{1,0:T(8,128)(2,1)S(1)}, u32[]{:S(2)}, u32[]{:S(2)}) collective-permute-start(bf16[512,512]{1,0:T(8,128)(2,1)S(1)} %copy-done.3), channel_id=1, source_target_pairs={{0,4},{1,5},{2,6},{3,7},{4,12},{5,13},{6,14},{7,15},{12,8},{13,9},... | collective-permute-start | bytes 1572872 | tf_op jit(solution)/shard_map/ppermute | solution.py:52
  11.5 7.8 %collective-permute-done.11.refs_2_ = bf16[256,1024]{1,0:T(8,128)(2,1)S(1)} collective-permute-done((bf16[256,1024]{1,0:T(8,128)(2,1)S(1)}, bf16[256,1024]{1,0:T(8,128)(2,1)S(1)}, u32[]{:S(2)}, u32[]{:S(2)}) %collective-permute-start.11) | collective-permute-done | bytes 524320 | tf_op jit(solution)/shard_map/ppermute | solution.py:49
  19.3 3.3 %collective-permute-done.refs_0_ = bf16[256,1024]{1,0:T(8,128)(2,1)S(1)} collective-permute-done((bf16[256,1024]{1,0:T(8,128)(2,1)S(1)}, bf16[256,1024]{1,0:T(8,128)(2,1)S(1)}, u32[]{:S(2)}, u32[]{:S(2)}) %collective-permute-start) | collective-permute-done | bytes 524320 | tf_op jit(solution)/shard_map/ppermute | solution.py:52
  22.6 7.9 %collective-permute-done.8.refs_5_.refs_12_.refs_3_ = bf16[256,1024]{1,0:T(8,128)(2,1)S(1)} collective-permute-done((bf16[256,1024]{1,0:T(8,128)(2,1)S(1)}, bf16[256,1024]{1,0:T(8,128)(2,1)S(1)}, u32[]{:S(2)}, u32[]{:S(2)}) %collective-permute-start.8) | collective-permute-done | bytes 524320 | tf_op jit(solution)/shard_map/ppermute | solution.py:49
  30.5 2.1 %collective-permute-start.1 = (bf16[256,1024]{1,0:T(8,128)(2,1)S(1)}, bf16[256,1024]{1,0:T(8,128)(2,1)S(1)}, u32[]{:S(2)}, u32[]{:S(2)}) collective-permute-start(bf16[256,1024]{1,0:T(8,128)(2,1)S(1)} %get-tuple-element.59.refs_1_), channel_id=1, source_target_pairs={{0,4},{1,5},{2,6},{3,7},{4,12},{5,13},{6,14},{7,15},{12,8},{13,9},... | collective-permute-start | bytes 1572872 | tf_op jit(solution)/shard_map/ppermute | solution.py:52
  32.7 1.5 collective-permute-start.15
  34.2 2.6 %collective-permute-start.3 = (bf16[512,512]{1,0:T(8,128)(2,1)S(1)}, bf16[512,512]{1,0:T(8,128)(2,1)S(1)}, u32[]{:S(2)}, u32[]{:S(2)}) collective-permute-start(bf16[512,512]{1,0:T(8,128)(2,1)S(1)} %collective-permute-done.2.refs_7_), channel_id=1, source_target_pairs={{0,4},{1,5},{2,6},{3,7},{4,12},{5,13},{6,14},{7,15},{12,8},{13,9},... | collective-permute-start | bytes 1572872 | tf_op jit(solution)/shard_map/ppermute | solution.py:52
  36.9 2.1 %weight.5 = (bf16[256,8192]{1,0:T(8,128)(2,1)}, bf16[256,1024]{1,0:T(8,128)(2,1)S(1)}) custom-call(bf16[256,1024]{1,0:T(8,128)(2,1)S(1)} %get-tuple-element.116.refs_0_, bf16[256,1024]{1,0:T(8,128)(2,1)S(1)} %get-tuple-element.59.refs_1_, bf16[256,1024]{1,0:T(8,128)(2,1)S(1)} %collective-permute-done.9.refs_2_, ...), custom_call_target="tpu_custom_call" | custom-call | flops 1073741824 | bytes 6291456 | tf_op jit(solution)/shard_map/weight/pallas_call | solution.py:270
  39.1 2.3 %collective-permute-done.12.refs_4_ = bf16[256,1024]{1,0:T(8,128)(2,1)S(1)} collective-permute-done((bf16[256,1024]{1,0:T(8,128)(2,1)S(1)}, bf16[256,1024]{1,0:T(8,128)(2,1)S(1)}, u32[]{:S(2)}, u32[]{:S(2)}) %collective-permute-start.12) | collective-permute-done | bytes 524320 | tf_op jit(solution)/shard_map/ppermute | solution.py:49
  41.9 4.6 %collective-permute-done.1.refs_1_ = bf16[256,1024]{1,0:T(8,128)(2,1)S(1)} collective-permute-done((bf16[256,1024]{1,0:T(8,128)(2,1)S(1)}, bf16[256,1024]{1,0:T(8,128)(2,1)S(1)}, u32[]{:S(2)}, u32[]{:S(2)}) %collective-permute-start.1) | collective-permute-done | bytes 524320 | tf_op jit(solution)/shard_map/ppermute | solution.py:52
  46.5 1.9 collective-permute-start.13
  48.4 4.7 %collective-permute-done.15.refs_3_ = bf16[256,1024]{1,0:T(8,128)(2,1)S(1)} collective-permute-done((bf16[256,1024]{1,0:T(8,128)(2,1)S(1)}, bf16[256,1024]{1,0:T(8,128)(2,1)S(1)}, u32[]{:S(2)}, u32[]{:S(2)}) %collective-permute-start.15) | collective-permute-done | bytes 524320 | tf_op jit(solution)/shard_map/ppermute | solution.py:49
  53.0 1.9 %collective-permute-done.3.refs_8_ = bf16[512,512]{1,0:T(8,128)(2,1)S(1)} collective-permute-done((bf16[512,512]{1,0:T(8,128)(2,1)S(1)}, bf16[512,512]{1,0:T(8,128)(2,1)S(1)}, u32[]{:S(2)}, u32[]{:S(2)}) %collective-permute-start.3) | collective-permute-done | bytes 524320 | tf_op jit(solution)/shard_map/ppermute | solution.py:52
  55.0 1.5 collective-permute-start.16
  56.5 7.8 %collective-permute-done.13.refs_6_ = bf16[256,1024]{1,0:T(8,128)(2,1)S(1)} collective-permute-done((bf16[256,1024]{1,0:T(8,128)(2,1)S(1)}, bf16[256,1024]{1,0:T(8,128)(2,1)S(1)}, u32[]{:S(2)}, u32[]{:S(2)}) %collective-permute-start.13) | collective-permute-done | bytes 524320 | tf_op jit(solution)/shard_map/ppermute | solution.py:49
  64.2 2.1 %collective-permute-start.4 = (bf16[512,512]{1,0:T(8,128)(2,1)S(1)}, bf16[512,512]{1,0:T(8,128)(2,1)S(1)}, u32[]{:S(2)}, u32[]{:S(2)}) collective-permute-start(bf16[512,512]{1,0:T(8,128)(2,1)S(1)} %collective-permute-done.3.refs_8_), channel_id=1, source_target_pairs={{0,4},{1,5},{2,6},{3,7},{4,12},{5,13},{6,14},{7,15},{12,8},{13,9},... | collective-permute-start | bytes 1572872 | tf_op jit(solution)/shard_map/ppermute | solution.py:52
  66.4 2.1 %weight.6 = (bf16[256,8192]{1,0:T(8,128)(2,1)}, bf16[256,1024]{1,0:T(8,128)(2,1)S(1)}) custom-call(bf16[256,1024]{1,0:T(8,128)(2,1)S(1)} %collective-permute-done.refs_0_, bf16[256,1024]{1,0:T(8,128)(2,1)S(1)} %collective-permute-done.1.refs_1_, bf16[256,1024]{1,0:T(8,128)(2,1)S(1)} %collective-permute-done.6.refs_2_, ...), custom_call_target="tpu_custom_call", output_to_operand_aliasing={{0}: (7, {})} | custom-call | flops 1073741824 | bytes 6291456 | tf_op jit(solution)/shard_map/weight/pallas_call | solution.py:270
  68.6 5.3 %collective-permute-done.16.refs_5_ = bf16[256,1024]{1,0:T(8,128)(2,1)S(1)} collective-permute-done((bf16[256,1024]{1,0:T(8,128)(2,1)S(1)}, bf16[256,1024]{1,0:T(8,128)(2,1)S(1)}, u32[]{:S(2)}, u32[]{:S(2)}) %collective-permute-start.16) | collective-permute-done | bytes 524320 | tf_op jit(solution)/shard_map/ppermute | solution.py:49
  73.9 3.5 %collective-permute-done.4.refs_9_ = bf16[512,512]{1,0:T(8,128)(2,1)S(1)} collective-permute-done((bf16[512,512]{1,0:T(8,128)(2,1)S(1)}, bf16[512,512]{1,0:T(8,128)(2,1)S(1)}, u32[]{:S(2)}, u32[]{:S(2)}) %collective-permute-start.4) | collective-permute-done | bytes 524320 | tf_op jit(solution)/shard_map/ppermute | solution.py:52
  77.4 4.3 %project.1 = (f32[8,32,1024]{2,1,0:T(8,128)S(1)}, bf16[8,32,1024]{2,1,0:T(8,128)(2,1)S(1)}) custom-call(bf16[256,2048]{1,0:T(8,128)(2,1)S(1)} %get-tuple-element.71.refs_0_, bf16[256,2048]{1,0:T(8,128)(2,1)S(1)} %collective-permute-done.14.refs_1_, bf16[256,1024]{1,0:T(8,128)(2,1)S(1)} %collective-permute-done.11.refs_2_, ...), custom_call_target="tpu_custom_call" | custom-call | flops 3221225472 | bytes 12582912 | tf_op jit(solution)/shard_map/project/pallas_call | solution.py:270
  82.6 3.4 %collective-permute-start.5 = (bf16[256,1024]{1,0:T(8,128)(2,1)S(1)}, bf16[256,1024]{1,0:T(8,128)(2,1)S(1)}, u32[]{:S(2)}, u32[]{:S(2)}) collective-permute-start(bf16[256,1024]{1,0:T(8,128)(2,1)S(1)} %collective-permute-done.1.refs_1_), channel_id=1, source_target_pairs={{0,4},{1,5},{2,6},{3,7},{4,12},{5,13},{6,14},{7,15},{12,8},{13,9},... | collective-permute-start | bytes 1572872 | tf_op jit(solution)/shard_map/ppermute | solution.py:52
  86.1 1.6 collective-permute-start.19
  87.6 6.6 %collective-permute-done.19.refs_1_ = bf16[4,32,1024]{2,1,0:T(8,128)(2,1)S(1)} collective-permute-done((bf16[4,32,1024]{2,1,0:T(8,128)(2,1)S(1)}, bf16[4,32,1024]{2,1,0:T(8,128)(2,1)S(1)}, u32[]{:S(2)}, u32[]{:S(2)}) %collective-permute-start.19) | collective-permute-done | bytes 262176 | tf_op jit(solution)/shard_map/ppermute | solution.py:49
  94.3 3.2 %collective-permute-done.20.refs_0_ = bf16[256,1024]{1,0:T(8,128)(2,1)S(1)} collective-permute-done((bf16[256,1024]{1,0:T(8,128)(2,1)S(1)}, bf16[256,1024]{1,0:T(8,128)(2,1)S(1)}, u32[]{:S(2)}, u32[]{:S(2)}) %collective-permute-start.20) | collective-permute-done | bytes 524320 | tf_op jit(solution)/shard_map/ppermute | solution.py:52
  97.5 3.5 %collective-permute-start.23 = (bf16[1,32,1024]{2,1,0:T(8,128)(2,1)S(1)}, bf16[1,32,1024]{2,1,0:T(8,128)(2,1)S(1)}, u32[]{:S(2)}, u32[]{:S(2)}) collective-permute-start(bf16[1,32,1024]{2,1,0:T(8,128)(2,1)S(1)} %get-tuple-element.90), channel_id=1, source_target_pairs={{0,12},{1,13},{2,14},{3,15},{4,8},{5,9},{6,10},{7,11},{8,4},{9,5},... | collective-permute-start | bytes 196616 | tf_op jit(solution)/shard_map/ppermute | solution.py:49
  101.9 9.0 %collective-permute-done.23.refs_3_ = bf16[1,32,1024]{2,1,0:T(8,128)(2,1)S(1)} collective-permute-done((bf16[1,32,1024]{2,1,0:T(8,128)(2,1)S(1)}, bf16[1,32,1024]{2,1,0:T(8,128)(2,1)S(1)}, u32[]{:S(2)}, u32[]{:S(2)}) %collective-permute-start.23) | collective-permute-done | bytes 65568 | tf_op jit(solution)/shard_map/ppermute | solution.py:49
  110.9 3.0 %collective-permute-done.22.refs_2_ = bf16[1,32,1024]{2,1,0:T(8,128)(2,1)S(1)} collective-permute-done((bf16[1,32,1024]{2,1,0:T(8,128)(2,1)S(1)}, bf16[1,32,1024]{2,1,0:T(8,128)(2,1)S(1)}, u32[]{:S(2)}, u32[]{:S(2)}) %collective-permute-start.22) | collective-permute-done | bytes 65568 | tf_op jit(solution)/shard_map/ppermute | solution.py:49
  114.9 3.4 %collective-permute-start.25 = (f32[8,128]{1,0:T(8,128)S(1)}, f32[8,128]{1,0:T(8,128)S(1)}, u32[]{:S(2)}, u32[]{:S(2)}) collective-permute-start(f32[8,128]{1,0:T(8,128)S(1)} %get-tuple-element.91), channel_id=1, source_target_pairs={{0,8},{1,9},{2,10},{3,11},{4,12},{5,13},{6,14},{7,15},{8,0},{9,1},... | collective-permute-start | bytes 12296 | tf_op jit(solution)/shard_map/ppermute | solution.py:49
  119.1 1.4 collective-permute-start.36
  120.5 3.2 %collective-permute-done.26 = f32[8,128]{1,0:T(8,128)S(1)} collective-permute-done((f32[8,128]{1,0:T(8,128)S(1)}, f32[8,128]{1,0:T(8,128)S(1)}, u32[]{:S(2)}, u32[]{:S(2)}) %collective-permute-start.26) | collective-permute-done | bytes 4128 | tf_op jit(solution)/shard_map/ppermute | solution.py:49
  123.8 1.2 collective-permute-done.27.refs_1_
  124.9 1.5 collective-permute-start.28
  126.5 6.7 %collective-permute-done.28.refs_2_ = f32[8,128]{1,0:T(8,128)S(1)} collective-permute-done((f32[8,128]{1,0:T(8,128)S(1)}, f32[8,128]{1,0:T(8,128)S(1)}, u32[]{:S(2)}, u32[]{:S(2)}) %collective-permute-start.28) | collective-permute-done | bytes 4128 | tf_op jit(solution)/shard_map/ppermute | solution.py:49
  133.4 2.8 %collective-permute-done.29.refs_3_ = f32[8,128]{1,0:T(8,128)S(1)} collective-permute-done((f32[8,128]{1,0:T(8,128)S(1)}, f32[8,128]{1,0:T(8,128)S(1)}, u32[]{:S(2)}, u32[]{:S(2)}) %collective-permute-start.29) | collective-permute-done | bytes 4128 | tf_op jit(solution)/shard_map/ppermute | solution.py:49
  137.2 3.9 %collective-permute-start.38 = (bf16[1,32,1024]{2,1,0:T(8,128)(2,1)S(1)}, bf16[1,32,1024]{2,1,0:T(8,128)(2,1)S(1)}, u32[]{:S(2)}, u32[]{:S(2)}) collective-permute-start(bf16[1,32,1024]{2,1,0:T(8,128)(2,1)S(1)} %get-tuple-element.93), channel_id=1, source_target_pairs={{0,4},{1,5},{2,6},{3,7},{4,0},{5,1},{6,2},{7,3},{8,12},{9,13},{10,... | collective-permute-start | bytes 196616 | tf_op jit(solution)/shard_map/ppermute | solution.py:49
  141.1 2.4 %collective-permute-start.40 = (bf16[1,32,1024]{2,1,0:T(8,128)(2,1)S(1)}, bf16[1,32,1024]{2,1,0:T(8,128)(2,1)S(1)}, u32[]{:S(2)}, u32[]{:S(2)}) collective-permute-start(bf16[1,32,1024]{2,1,0:T(8,128)(2,1)S(1)} %get-tuple-element.93), channel_id=1, source_target_pairs={{0,12},{1,13},{2,14},{3,15},{4,8},{5,9},{6,10},{7,11},{8,4},{9,5},... | collective-permute-start | bytes 196616 | tf_op jit(solution)/shard_map/ppermute | solution.py:49
  143.6 2.1 %weight.7 = (bf16[256,8192]{1,0:T(8,128)(2,1)}, bf16[256,1024]{1,0:T(8,128)(2,1)S(1)}) custom-call(bf16[256,1024]{1,0:T(8,128)(2,1)S(1)} %collective-permute-done.20.refs_0_, bf16[256,1024]{1,0:T(8,128)(2,1)S(1)} %collective-permute-done.5.refs_1_, bf16[256,1024]{1,0:T(8,128)(2,1)S(1)} %collective-permute-done.34.refs_2_, ...), custom_call_target="tpu_custom_call", output_to_operand_aliasing={{0}: (7, {})} | custom-call | flops 1073741824 | bytes 6291456 | tf_op jit(solution)/shard_map/weight/pallas_call | solution.py:270
  145.7 8.9 %collective-permute-done.38 = bf16[1,32,1024]{2,1,0:T(8,128)(2,1)S(1)} collective-permute-done((bf16[1,32,1024]{2,1,0:T(8,128)(2,1)S(1)}, bf16[1,32,1024]{2,1,0:T(8,128)(2,1)S(1)}, u32[]{:S(2)}, u32[]{:S(2)}) %collective-permute-start.38) | collective-permute-done | bytes 65568 | tf_op jit(solution)/shard_map/ppermute | solution.py:49
  154.6 2.4 %collective-permute-done.40 = bf16[1,32,1024]{2,1,0:T(8,128)(2,1)S(1)} collective-permute-done((bf16[1,32,1024]{2,1,0:T(8,128)(2,1)S(1)}, bf16[1,32,1024]{2,1,0:T(8,128)(2,1)S(1)}, u32[]{:S(2)}, u32[]{:S(2)}) %collective-permute-start.40) | collective-permute-done | bytes 65568 | tf_op jit(solution)/shard_map/ppermute | solution.py:49
  157.8 16.2 %collective-permute-done.41 = bf16[4,32,1024]{2,1,0:T(8,128)(2,1)S(1)} collective-permute-done((bf16[4,32,1024]{2,1,0:T(8,128)(2,1)S(1)}, bf16[4,32,1024]{2,1,0:T(8,128)(2,1)S(1)}, u32[]{:S(2)}, u32[]{:S(2)}) %collective-permute-start.41) | collective-permute-done | bytes 262176 | tf_op jit(solution)/shard_map/ppermute | solution.py:49
  174.1 1.5 weight.8
  176.0 7.1 %collective-permute-done.42.refs_4_ = bf16[256,512]{1,0:T(8,128)(2,1)S(1)} collective-permute-done((bf16[256,512]{1,0:T(8,128)(2,1)S(1)}, bf16[256,512]{1,0:T(8,128)(2,1)S(1)}, u32[]{:S(2)}, u32[]{:S(2)}) %collective-permute-start.42) | collective-permute-done | bytes 262176 | tf_op jit(solution)/shard_map/ppermute | solution.py:49
  183.1 1.5 weight.9
  185.2 2.2 %back.1 = f32[512,1024]{1,0:T(8,128)} custom-call(bf16[512,512]{1,0:T(8,128)(2,1)S(1)} %copy-done.3, bf16[8,32,1024]{2,1,0:T(8,128)(2,1)S(1)} %constant_dynamic-update-slice_fusion.near, bf16[8,32,1024]{2,1,0:T(8,128)(2,1)S(1)} %collective-permute-done.44.other, f32[512,1024]{1,0:T(8,128)S(1)} %copy-done.1), custom_call_target="tpu_custom_call" | custom-call | flops 536870912 | bytes 8388608 | tf_op jit(solution)/shard_map/back/pallas_call | solution.py:270
  187.4 3.7 %collective-permute-done.43.arrived = bf16[256,512]{1,0:T(8,128)(2,1)S(1)} collective-permute-done((bf16[256,512]{1,0:T(8,128)(2,1)S(1)}, bf16[256,512]{1,0:T(8,128)(2,1)S(1)}, u32[]{:S(2)}, u32[]{:S(2)}) %collective-permute-start.43) | collective-permute-done | bytes 262176 | tf_op jit(solution)/shard_map/ppermute | solution.py:49
  (78 shorter events, 9.6 us)
Async XLA Ops:
  0.6 7.8 %copy-start = (bf16[256,1024]{1,0:T(8,128)(2,1)S(1)}, bf16[256,1024]{1,0:T(8,128)(2,1)}, u32[]{:S(2)}) copy-start(bf16[256,1024]{1,0:T(8,128)(2,1)} %refs_2_.3) | copy-start | bytes 1572868
  3.5 15.8 %collective-permute-start.11 = (bf16[256,1024]{1,0:T(8,128)(2,1)S(1)}, bf16[256,1024]{1,0:T(8,128)(2,1)S(1)}, u32[]{:S(2)}, u32[]{:S(2)}) collective-permute-start(bf16[256,1024]{1,0:T(8,128)(2,1)S(1)} %get-tuple-element.66), channel_id=1, source_target_pairs={{0,2},{1,3},{2,0},{3,1},{4,6},{5,7},{6,4},{7,5},{8,10},{9,11},{10,... | collective-permute-start | bytes 1572872 | tf_op jit(solution)/shard_map/ppermute | solution.py:49
  6.8 15.8 %collective-permute-start = (bf16[256,1024]{1,0:T(8,128)(2,1)S(1)}, bf16[256,1024]{1,0:T(8,128)(2,1)S(1)}, u32[]{:S(2)}, u32[]{:S(2)}) collective-permute-start(bf16[256,1024]{1,0:T(8,128)(2,1)S(1)} %get-tuple-element.116.refs_0_), channel_id=1, source_target_pairs={{0,4},{1,5},{2,6},{3,7},{4,12},{5,13},{6,14},{7,15},{12,8},{13,9},... | collective-permute-start | bytes 1572872 | tf_op jit(solution)/shard_map/ppermute | solution.py:52
  8.4 22.1 %collective-permute-start.8 = (bf16[256,1024]{1,0:T(8,128)(2,1)S(1)}, bf16[256,1024]{1,0:T(8,128)(2,1)S(1)}, u32[]{:S(2)}, u32[]{:S(2)}) collective-permute-start(bf16[256,1024]{1,0:T(8,128)(2,1)S(1)} %copy-done), channel_id=1, source_target_pairs={{0,2},{1,3},{2,0},{3,1},{4,6},{5,7},{6,4},{7,5},{8,10},{9,11},{10,... | collective-permute-start | bytes 1572872 | tf_op jit(solution)/shard_map/ppermute | solution.py:49
  8.9 23.7 %collective-permute-start.2 = (bf16[512,512]{1,0:T(8,128)(2,1)S(1)}, bf16[512,512]{1,0:T(8,128)(2,1)S(1)}, u32[]{:S(2)}, u32[]{:S(2)}) collective-permute-start(bf16[512,512]{1,0:T(8,128)(2,1)S(1)} %copy-done.3), channel_id=1, source_target_pairs={{0,4},{1,5},{2,6},{3,7},{4,12},{5,13},{6,14},{7,15},{12,8},{13,9},... | collective-permute-start | bytes 1572872 | tf_op jit(solution)/shard_map/ppermute | solution.py:52
  11.5 22.7 %collective-permute-start.10 = (bf16[256,1024]{1,0:T(8,128)(2,1)S(1)}, bf16[256,1024]{1,0:T(8,128)(2,1)S(1)}, u32[]{:S(2)}, u32[]{:S(2)}) collective-permute-start(bf16[256,1024]{1,0:T(8,128)(2,1)S(1)} %get-tuple-element.59.refs_1_), channel_id=1, source_target_pairs={{0,1},{1,0},{2,3},{3,2},{4,5},{5,4},{6,7},{7,6},{8,9},{9,8},{10,11... | collective-permute-start | bytes 1572872 | tf_op jit(solution)/shard_map/ppermute | solution.py:49
  19.3 17.5 %collective-permute-start.9 = (bf16[256,1024]{1,0:T(8,128)(2,1)S(1)}, bf16[256,1024]{1,0:T(8,128)(2,1)S(1)}, u32[]{:S(2)}, u32[]{:S(2)}) collective-permute-start(bf16[256,1024]{1,0:T(8,128)(2,1)S(1)} %get-tuple-element.116.refs_0_), channel_id=1, source_target_pairs={{0,1},{1,0},{2,3},{3,2},{4,5},{5,4},{6,7},{7,6},{8,9},{9,8},{10,11... | collective-permute-start | bytes 1572872 | tf_op jit(solution)/shard_map/ppermute | solution.py:49
  22.6 18.7 %collective-permute-start.12 = (bf16[256,1024]{1,0:T(8,128)(2,1)S(1)}, bf16[256,1024]{1,0:T(8,128)(2,1)S(1)}, u32[]{:S(2)}, u32[]{:S(2)}) collective-permute-start(bf16[256,1024]{1,0:T(8,128)(2,1)S(1)} %get-tuple-element.67), channel_id=1, source_target_pairs={{0,3},{1,2},{2,1},{3,0},{4,7},{5,6},{6,5},{7,4},{8,11},{9,10},{10,... | collective-permute-start | bytes 1572872 | tf_op jit(solution)/shard_map/ppermute | solution.py:49
  30.5 16.0 %collective-permute-start.1 = (bf16[256,1024]{1,0:T(8,128)(2,1)S(1)}, bf16[256,1024]{1,0:T(8,128)(2,1)S(1)}, u32[]{:S(2)}, u32[]{:S(2)}) collective-permute-start(bf16[256,1024]{1,0:T(8,128)(2,1)S(1)} %get-tuple-element.59.refs_1_), channel_id=1, source_target_pairs={{0,4},{1,5},{2,6},{3,7},{4,12},{5,13},{6,14},{7,15},{12,8},{13,9},... | collective-permute-start | bytes 1572872 | tf_op jit(solution)/shard_map/ppermute | solution.py:52
  32.7 20.3 %collective-permute-start.15 = (bf16[256,1024]{1,0:T(8,128)(2,1)S(1)}, bf16[256,1024]{1,0:T(8,128)(2,1)S(1)}, u32[]{:S(2)}, u32[]{:S(2)}) collective-permute-start(bf16[256,1024]{1,0:T(8,128)(2,1)S(1)} %get-tuple-element.75), channel_id=1, source_target_pairs={{0,2},{1,3},{2,0},{3,1},{4,6},{5,7},{6,4},{7,5},{8,10},{9,11},{10,... | collective-permute-start | bytes 1572872 | tf_op jit(solution)/shard_map/ppermute | solution.py:49
  34.2 20.7 %collective-permute-start.3 = (bf16[512,512]{1,0:T(8,128)(2,1)S(1)}, bf16[512,512]{1,0:T(8,128)(2,1)S(1)}, u32[]{:S(2)}, u32[]{:S(2)}) collective-permute-start(bf16[512,512]{1,0:T(8,128)(2,1)S(1)} %collective-permute-done.2.refs_7_), channel_id=1, source_target_pairs={{0,4},{1,5},{2,6},{3,7},{4,12},{5,13},{6,14},{7,15},{12,8},{13,9},... | collective-permute-start | bytes 1572872 | tf_op jit(solution)/shard_map/ppermute | solution.py:52
  36.9 31.6 %collective-permute-start.17 = (bf16[512,1024]{1,0:T(8,128)(2,1)S(1)}, bf16[512,1024]{1,0:T(8,128)(2,1)S(1)}, u32[]{:S(2)}, u32[]{:S(2)}) collective-permute-start(bf16[512,1024]{1,0:T(8,128)(2,1)S(1)} %pad_maximum_fusion), channel_id=1, source_target_pairs={{0,1},{1,0},{2,3},{3,2},{4,5},{5,4},{6,7},{7,6},{8,9},{9,8},{10,11... | collective-permute-start | bytes 3145736 | tf_op jit(solution)/shard_map/ppermute | solution.py:49
  41.4 13.6 %collective-permute-start.6 = (bf16[256,1024]{1,0:T(8,128)(2,1)S(1)}, bf16[256,1024]{1,0:T(8,128)(2,1)S(1)}, u32[]{:S(2)}, u32[]{:S(2)}) collective-permute-start(bf16[256,1024]{1,0:T(8,128)(2,1)S(1)} %collective-permute-done.refs_0_), channel_id=1, source_target_pairs={{0,1},{1,0},{2,3},{3,2},{4,5},{5,4},{6,7},{7,6},{8,9},{9,8},{10,11... | collective-permute-start | bytes 1572872 | tf_op jit(solution)/shard_map/ppermute | solution.py:49
  46.5 17.7 %collective-permute-start.13 = (bf16[256,1024]{1,0:T(8,128)(2,1)S(1)}, bf16[256,1024]{1,0:T(8,128)(2,1)S(1)}, u32[]{:S(2)}, u32[]{:S(2)}) collective-permute-start(bf16[256,1024]{1,0:T(8,128)(2,1)S(1)} %get-tuple-element.68), channel_id=1, source_target_pairs={{0,2},{1,3},{2,0},{3,1},{4,6},{5,7},{6,4},{7,5},{8,10},{9,11},{10,... | collective-permute-start | bytes 1572872 | tf_op jit(solution)/shard_map/ppermute | solution.py:49
  53.0 20.9 %collective-permute-start.14 = (bf16[256,2048]{1,0:T(8,128)(2,1)S(1)}, bf16[256,2048]{1,0:T(8,128)(2,1)S(1)}, u32[]{:S(2)}, u32[]{:S(2)}) collective-permute-start(bf16[256,2048]{1,0:T(8,128)(2,1)S(1)} %get-tuple-element.73), channel_id=1, source_target_pairs={{0,1},{1,0},{2,3},{3,2},{4,5},{5,4},{6,7},{7,6},{8,9},{9,8},{10,11... | collective-permute-start | bytes 3145736 | tf_op jit(solution)/shard_map/ppermute | solution.py:49
  54.9 11.4 %collective-permute-start.7 = (bf16[256,1024]{1,0:T(8,128)(2,1)S(1)}, bf16[256,1024]{1,0:T(8,128)(2,1)S(1)}, u32[]{:S(2)}, u32[]{:S(2)}) collective-permute-start(bf16[256,1024]{1,0:T(8,128)(2,1)S(1)} %collective-permute-done.1.refs_1_), channel_id=1, source_target_pairs={{0,1},{1,0},{2,3},{3,2},{4,5},{5,4},{6,7},{7,6},{8,9},{9,8},{10,11... | collective-permute-start | bytes 1572872 | tf_op jit(solution)/shard_map/ppermute | solution.py:49
  55.0 19.0 %collective-permute-start.16 = (bf16[256,1024]{1,0:T(8,128)(2,1)S(1)}, bf16[256,1024]{1,0:T(8,128)(2,1)S(1)}, u32[]{:S(2)}, u32[]{:S(2)}) collective-permute-start(bf16[256,1024]{1,0:T(8,128)(2,1)S(1)} %get-tuple-element.77), channel_id=1, source_target_pairs={{0,3},{1,2},{2,1},{3,0},{4,7},{5,6},{6,5},{7,4},{8,11},{9,10},{10,... | collective-permute-start | bytes 1572872 | tf_op jit(solution)/shard_map/ppermute | solution.py:49
  64.2 13.2 %collective-permute-start.4 = (bf16[512,512]{1,0:T(8,128)(2,1)S(1)}, bf16[512,512]{1,0:T(8,128)(2,1)S(1)}, u32[]{:S(2)}, u32[]{:S(2)}) collective-permute-start(bf16[512,512]{1,0:T(8,128)(2,1)S(1)} %collective-permute-done.3.refs_8_), channel_id=1, source_target_pairs={{0,4},{1,5},{2,6},{3,7},{4,12},{5,13},{6,14},{7,15},{12,8},{13,9},... | collective-permute-start | bytes 1572872 | tf_op jit(solution)/shard_map/ppermute | solution.py:52
  77.4 58.7 %copy-start.4 = (f32[32,1024]{1,0:T(8,128)S(1)}, f32[32,1024]{1,0:T(8,128)}, u32[]{:S(2)}) copy-start(f32[32,1024]{1,0:T(8,128)} %refs_5_.1) | copy-start | bytes 393220
  77.4 58.7 %copy-start.5 = (f32[32,1024]{1,0:T(8,128)S(1)}, f32[32,1024]{1,0:T(8,128)}, u32[]{:S(2)}) copy-start(f32[32,1024]{1,0:T(8,128)} %refs_6_.3) | copy-start | bytes 393220
  81.8 4.2 %collective-permute-start.18 = (bf16[8,32,1024]{2,1,0:T(8,128)(2,1)S(1)}, bf16[8,32,1024]{2,1,0:T(8,128)(2,1)S(1)}, u32[]{:S(2)}, u32[]{:S(2)}) collective-permute-start(bf16[8,32,1024]{2,1,0:T(8,128)(2,1)S(1)} %get-tuple-element.80), channel_id=1, source_target_pairs={{0,1},{1,0},{2,3},{3,2},{4,5},{5,4},{6,7},{7,6},{8,9},{9,8},{10,11... | collective-permute-start | bytes 1572872 | tf_op jit(solution)/shard_map/ppermute | solution.py:49
  81.8 15.7 %collective-permute-start.20 = (bf16[256,1024]{1,0:T(8,128)(2,1)S(1)}, bf16[256,1024]{1,0:T(8,128)(2,1)S(1)}, u32[]{:S(2)}, u32[]{:S(2)}) collective-permute-start(bf16[256,1024]{1,0:T(8,128)(2,1)S(1)} %collective-permute-done.refs_0_), channel_id=1, source_target_pairs={{0,4},{1,5},{2,6},{3,7},{4,12},{5,13},{6,14},{7,15},{12,8},{13,9},... | collective-permute-start | bytes 1572872 | tf_op jit(solution)/shard_map/ppermute | solution.py:52
  82.6 36.0 %collective-permute-start.5 = (bf16[256,1024]{1,0:T(8,128)(2,1)S(1)}, bf16[256,1024]{1,0:T(8,128)(2,1)S(1)}, u32[]{:S(2)}, u32[]{:S(2)}) collective-permute-start(bf16[256,1024]{1,0:T(8,128)(2,1)S(1)} %collective-permute-done.1.refs_1_), channel_id=1, source_target_pairs={{0,4},{1,5},{2,6},{3,7},{4,12},{5,13},{6,14},{7,15},{12,8},{13,9},... | collective-permute-start | bytes 1572872 | tf_op jit(solution)/shard_map/ppermute | solution.py:52
  86.1 8.2 %collective-permute-start.19 = (bf16[4,32,1024]{2,1,0:T(8,128)(2,1)S(1)}, bf16[4,32,1024]{2,1,0:T(8,128)(2,1)S(1)}, u32[]{:S(2)}, u32[]{:S(2)}) collective-permute-start(bf16[4,32,1024]{2,1,0:T(8,128)(2,1)S(1)} %get-tuple-element.82), channel_id=1, source_target_pairs={{0,2},{1,3},{2,0},{3,1},{4,6},{5,7},{6,4},{7,5},{8,10},{9,11},{10,... | collective-permute-start | bytes 786440 | tf_op jit(solution)/shard_map/ppermute | solution.py:49
  97.5 13.4 %collective-permute-start.23 = (bf16[1,32,1024]{2,1,0:T(8,128)(2,1)S(1)}, bf16[1,32,1024]{2,1,0:T(8,128)(2,1)S(1)}, u32[]{:S(2)}, u32[]{:S(2)}) collective-permute-start(bf16[1,32,1024]{2,1,0:T(8,128)(2,1)S(1)} %get-tuple-element.90), channel_id=1, source_target_pairs={{0,12},{1,13},{2,14},{3,15},{4,8},{5,9},{6,10},{7,11},{8,4},{9,5},... | collective-permute-start | bytes 196616 | tf_op jit(solution)/shard_map/ppermute | solution.py:49
  101.0 12.9 %collective-permute-start.22 = (bf16[1,32,1024]{2,1,0:T(8,128)(2,1)S(1)}, bf16[1,32,1024]{2,1,0:T(8,128)(2,1)S(1)}, u32[]{:S(2)}, u32[]{:S(2)}) collective-permute-start(bf16[1,32,1024]{2,1,0:T(8,128)(2,1)S(1)} %get-tuple-element.88), channel_id=1, source_target_pairs={{0,8},{1,9},{2,10},{3,11},{4,12},{5,13},{6,14},{7,15},{8,0},{9,1},... | collective-permute-start | bytes 196616 | tf_op jit(solution)/shard_map/ppermute | solution.py:49
  101.0 12.9 %collective-permute-start.21 = (bf16[1,32,1024]{2,1,0:T(8,128)(2,1)S(1)}, bf16[1,32,1024]{2,1,0:T(8,128)(2,1)S(1)}, u32[]{:S(2)}, u32[]{:S(2)}) collective-permute-start(bf16[1,32,1024]{2,1,0:T(8,128)(2,1)S(1)} %get-tuple-element.86), channel_id=1, source_target_pairs={{0,4},{1,5},{2,6},{3,7},{4,0},{5,1},{6,2},{7,3},{8,12},{9,13},{10,... | collective-permute-start | bytes 196616 | tf_op jit(solution)/shard_map/ppermute | solution.py:49
  114.2 5.0 %collective-permute-start.24 = (f32[8,128]{1,0:T(8,128)S(1)}, f32[8,128]{1,0:T(8,128)S(1)}, u32[]{:S(2)}, u32[]{:S(2)}) collective-permute-start(f32[8,128]{1,0:T(8,128)S(1)} %get-tuple-element.91), channel_id=1, source_target_pairs={{0,4},{1,5},{2,6},{3,7},{4,0},{5,1},{6,2},{7,3},{8,12},{9,13},{10,... | collective-permute-start | bytes 12296 | tf_op jit(solution)/shard_map/ppermute | solution.py:49
  114.9 5.6 %collective-permute-start.25 = (f32[8,128]{1,0:T(8,128)S(1)}, f32[8,128]{1,0:T(8,128)S(1)}, u32[]{:S(2)}, u32[]{:S(2)}) collective-permute-start(f32[8,128]{1,0:T(8,128)S(1)} %get-tuple-element.91), channel_id=1, source_target_pairs={{0,8},{1,9},{2,10},{3,11},{4,12},{5,13},{6,14},{7,15},{8,0},{9,1},... | collective-permute-start | bytes 12296 | tf_op jit(solution)/shard_map/ppermute | solution.py:49
  118.3 5.4 %collective-permute-start.26 = (f32[8,128]{1,0:T(8,128)S(1)}, f32[8,128]{1,0:T(8,128)S(1)}, u32[]{:S(2)}, u32[]{:S(2)}) collective-permute-start(f32[8,128]{1,0:T(8,128)S(1)} %get-tuple-element.91), channel_id=1, source_target_pairs={{0,12},{1,13},{2,14},{3,15},{4,8},{5,9},{6,10},{7,11},{8,4},{9,5},... | collective-permute-start | bytes 12296 | tf_op jit(solution)/shard_map/ppermute | solution.py:49
  118.6 18.6 %collective-permute-start.34 = (bf16[256,1024]{1,0:T(8,128)(2,1)S(1)}, bf16[256,1024]{1,0:T(8,128)(2,1)S(1)}, u32[]{:S(2)}, u32[]{:S(2)}) collective-permute-start(bf16[256,1024]{1,0:T(8,128)(2,1)S(1)} %collective-permute-done.20.refs_0_), channel_id=1, source_target_pairs={{0,1},{1,0},{2,3},{3,2},{4,5},{5,4},{6,7},{7,6},{8,9},{9,8},{10,11... | collective-permute-start | bytes 1572872 | tf_op jit(solution)/shard_map/ppermute | solution.py:49
  118.6 22.5 %collective-permute-start.35 = (bf16[256,1024]{1,0:T(8,128)(2,1)S(1)}, bf16[256,1024]{1,0:T(8,128)(2,1)S(1)}, u32[]{:S(2)}, u32[]{:S(2)}) collective-permute-start(bf16[256,1024]{1,0:T(8,128)(2,1)S(1)} %collective-permute-done.5.refs_1_), channel_id=1, source_target_pairs={{0,1},{1,0},{2,3},{3,2},{4,5},{5,4},{6,7},{7,6},{8,9},{9,8},{10,11... | collective-permute-start | bytes 1572872 | tf_op jit(solution)/shard_map/ppermute | solution.py:49
  119.1 22.0 %collective-permute-start.36 = (bf16[256,1024]{1,0:T(8,128)(2,1)S(1)}, bf16[256,1024]{1,0:T(8,128)(2,1)S(1)}, u32[]{:S(2)}, u32[]{:S(2)}) collective-permute-start(bf16[256,1024]{1,0:T(8,128)(2,1)S(1)} %get-tuple-element.100), channel_id=1, source_target_pairs={{0,2},{1,3},{2,0},{3,1},{4,6},{5,7},{6,4},{7,5},{8,10},{9,11},{10,... | collective-permute-start | bytes 1572872 | tf_op jit(solution)/shard_map/ppermute | solution.py:49
  123.7 30.9 %collective-permute-start.32 = (bf16[256,1024]{1,0:T(8,128)(2,1)S(1)}, bf16[256,1024]{1,0:T(8,128)(2,1)S(1)}, u32[]{:S(2)}, u32[]{:S(2)}) collective-permute-start(bf16[256,1024]{1,0:T(8,128)(2,1)S(1)} %collective-permute-done.20.refs_0_), channel_id=1, source_target_pairs={{0,4},{1,5},{2,6},{3,7},{4,12},{5,13},{6,14},{7,15},{12,8},{13,9},... | collective-permute-start | bytes 1572872 | tf_op jit(solution)/shard_map/ppermute | solution.py:52
  123.7 1.2 collective-permute-start.27
  124.9 8.2 %collective-permute-start.28 = (f32[8,128]{1,0:T(8,128)S(1)}, f32[8,128]{1,0:T(8,128)S(1)}, u32[]{:S(2)}, u32[]{:S(2)}) collective-permute-start(f32[8,128]{1,0:T(8,128)S(1)} %add_add_fusion.refs_0_), channel_id=1, source_target_pairs={{0,2},{1,3},{2,0},{3,1},{4,6},{5,7},{6,4},{7,5},{8,10},{9,11},{10,... | collective-permute-start | bytes 12296 | tf_op jit(solution)/shard_map/ppermute | solution.py:49
  133.1 3.0 %collective-permute-start.29 = (f32[8,128]{1,0:T(8,128)S(1)}, f32[8,128]{1,0:T(8,128)S(1)}, u32[]{:S(2)}, u32[]{:S(2)}) collective-permute-start(f32[8,128]{1,0:T(8,128)S(1)} %add_add_fusion.refs_0_), channel_id=1, source_target_pairs={{0,3},{1,2},{2,1},{3,0},{4,7},{5,6},{6,5},{7,4},{8,11},{9,10},{10,... | collective-permute-start | bytes 12296 | tf_op jit(solution)/shard_map/ppermute | solution.py:49
  136.9 20.8 %collective-permute-start.30 = (bf16[256,1024]{1,0:T(8,128)(2,1)S(1)}, bf16[256,1024]{1,0:T(8,128)(2,1)S(1)}, u32[]{:S(2)}, u32[]{:S(2)}) collective-permute-start(bf16[256,1024]{1,0:T(8,128)(2,1)S(1)} %collective-permute-done.5.refs_1_), channel_id=1, source_target_pairs={{0,4},{1,5},{2,6},{3,7},{4,12},{5,13},{6,14},{7,15},{12,8},{13,9},... | collective-permute-start | bytes 1572872 | tf_op jit(solution)/shard_map/ppermute | solution.py:52
  137.2 17.4 %collective-permute-start.38 = (bf16[1,32,1024]{2,1,0:T(8,128)(2,1)S(1)}, bf16[1,32,1024]{2,1,0:T(8,128)(2,1)S(1)}, u32[]{:S(2)}, u32[]{:S(2)}) collective-permute-start(bf16[1,32,1024]{2,1,0:T(8,128)(2,1)S(1)} %get-tuple-element.93), channel_id=1, source_target_pairs={{0,4},{1,5},{2,6},{3,7},{4,0},{5,1},{6,2},{7,3},{8,12},{9,13},{10,... | collective-permute-start | bytes 196616 | tf_op jit(solution)/shard_map/ppermute | solution.py:49
  141.1 13.5 %collective-permute-start.39 = (bf16[1,32,1024]{2,1,0:T(8,128)(2,1)S(1)}, bf16[1,32,1024]{2,1,0:T(8,128)(2,1)S(1)}, u32[]{:S(2)}, u32[]{:S(2)}) collective-permute-start(bf16[1,32,1024]{2,1,0:T(8,128)(2,1)S(1)} %get-tuple-element.93), channel_id=1, source_target_pairs={{0,8},{1,9},{2,10},{3,11},{4,12},{5,13},{6,14},{7,15},{8,0},{9,1},... | collective-permute-start | bytes 196616 | tf_op jit(solution)/shard_map/ppermute | solution.py:49
  141.1 15.9 %collective-permute-start.40 = (bf16[1,32,1024]{2,1,0:T(8,128)(2,1)S(1)}, bf16[1,32,1024]{2,1,0:T(8,128)(2,1)S(1)}, u32[]{:S(2)}, u32[]{:S(2)}) collective-permute-start(bf16[1,32,1024]{2,1,0:T(8,128)(2,1)S(1)} %get-tuple-element.93), channel_id=1, source_target_pairs={{0,12},{1,13},{2,14},{3,15},{4,8},{5,9},{6,10},{7,11},{8,4},{9,5},... | collective-permute-start | bytes 196616 | tf_op jit(solution)/shard_map/ppermute | solution.py:49
  154.6 19.5 %collective-permute-start.37 = (bf16[256,1024]{1,0:T(8,128)(2,1)S(1)}, bf16[256,1024]{1,0:T(8,128)(2,1)S(1)}, u32[]{:S(2)}, u32[]{:S(2)}) collective-permute-start(bf16[256,1024]{1,0:T(8,128)(2,1)S(1)} %get-tuple-element.103), channel_id=1, source_target_pairs={{0,2},{1,3},{2,0},{3,1},{4,6},{5,7},{6,4},{7,5},{8,10},{9,11},{10,... | collective-permute-start | bytes 1572872 | tf_op jit(solution)/shard_map/ppermute | solution.py:49
  154.6 19.5 %collective-permute-start.33 = (bf16[256,1024]{1,0:T(8,128)(2,1)S(1)}, bf16[256,1024]{1,0:T(8,128)(2,1)S(1)}, u32[]{:S(2)}, u32[]{:S(2)}) collective-permute-start(bf16[256,1024]{1,0:T(8,128)(2,1)S(1)} %collective-permute-done.32.refs_0_), channel_id=1, source_target_pairs={{0,1},{1,0},{2,3},{3,2},{4,5},{5,4},{6,7},{7,6},{8,9},{9,8},{10,11... | collective-permute-start | bytes 1572872 | tf_op jit(solution)/shard_map/ppermute | solution.py:49
  157.0 17.0 %collective-permute-start.41 = (bf16[4,32,1024]{2,1,0:T(8,128)(2,1)S(1)}, bf16[4,32,1024]{2,1,0:T(8,128)(2,1)S(1)}, u32[]{:S(2)}, u32[]{:S(2)}) collective-permute-start(bf16[4,32,1024]{2,1,0:T(8,128)(2,1)S(1)} %pad_maximum_fusion.1), channel_id=1, source_target_pairs={{0,2},{1,3},{2,0},{3,1},{4,6},{5,7},{6,4},{7,5},{8,10},{9,11},{10,... | collective-permute-start | bytes 786440 | tf_op jit(solution)/shard_map/ppermute | solution.py:49
  157.7 18.2 %collective-permute-start.31 = (bf16[256,1024]{1,0:T(8,128)(2,1)S(1)}, bf16[256,1024]{1,0:T(8,128)(2,1)S(1)}, u32[]{:S(2)}, u32[]{:S(2)}) collective-permute-start(bf16[256,1024]{1,0:T(8,128)(2,1)S(1)} %collective-permute-done.30.refs_0_), channel_id=1, source_target_pairs={{0,1},{1,0},{2,3},{3,2},{4,5},{5,4},{6,7},{7,6},{8,9},{9,8},{10,11... | collective-permute-start | bytes 1572872 | tf_op jit(solution)/shard_map/ppermute | solution.py:49
  175.6 7.5 %collective-permute-start.42 = (bf16[256,512]{1,0:T(8,128)(2,1)S(1)}, bf16[256,512]{1,0:T(8,128)(2,1)S(1)}, u32[]{:S(2)}, u32[]{:S(2)}) collective-permute-start(bf16[256,512]{1,0:T(8,128)(2,1)S(1)} %get-tuple-element.107), channel_id=1, source_target_pairs={{0,2},{1,3},{2,0},{3,1},{4,6},{5,7},{6,4},{7,5},{8,10},{9,11},{10,... | collective-permute-start | bytes 786440 | tf_op jit(solution)/shard_map/ppermute | solution.py:49
  175.9 9.3 %collective-permute-start.44 = (bf16[8,32,1024]{2,1,0:T(8,128)(2,1)S(1)}, bf16[8,32,1024]{2,1,0:T(8,128)(2,1)S(1)}, u32[]{:S(2)}, u32[]{:S(2)}) collective-permute-start(bf16[8,32,1024]{2,1,0:T(8,128)(2,1)S(1)} %constant_dynamic-update-slice_fusion.near), channel_id=1, source_target_pairs={{0,1},{1,0},{2,3},{3,2},{4,5},{5,4},{6,7},{7,6},{8,9},{9,8},{10,11... | collective-permute-start | bytes 1572872 | tf_op jit(solution)/shard_map/ppermute | solution.py:49
  184.5 6.5 %collective-permute-start.43 = (bf16[256,512]{1,0:T(8,128)(2,1)S(1)}, bf16[256,512]{1,0:T(8,128)(2,1)S(1)}, u32[]{:S(2)}, u32[]{:S(2)}) collective-permute-start(bf16[256,512]{1,0:T(8,128)(2,1)S(1)} %get-tuple-element.110), channel_id=1, source_target_pairs={{0,2},{1,3},{2,0},{3,1},{4,6},{5,7},{6,4},{7,5},{8,10},{9,11},{10,... | collective-permute-start | bytes 786440 | tf_op jit(solution)/shard_map/ppermute | solution.py:49
  (3 other events, 14.2 us)

commit v5 on v4

--- a/solution.py
+++ b/solution.py
@@ -166,28 +166,26 @@
     update[0] = (one / first_fix / (jnp.sqrt(two / second_fix) + 1e-08)).astype(bf16)
 
 
-def place(lay, s, side, low, width, rows, source, out, sems):
-    index = lax.axis_index("dp")
-    core = index % 2
-    chip = lay.source(index, s) * lay.sides + side
+def place(lay, side, rows, low, source, out, sems):
+    height = source.shape[1] // (2 * lay.ring)
     copies = []
-    for k, owner in enumerate((core, 1 - core)):
-        start = pl.multiple_of((chip * 2 + owner) * rows + low, width)
-        copies.append(
-            pltpu.make_async_copy(
-                source.at[:, pl.ds(k * width, width)],
-                out.at[:, pl.ds(start, width)],
-                sems.at[k],
-            )
-        )
+    for z in range(lay.ring):
+        for core in range(2):
+            k = 2 * z + core
+            start = pl.multiple_of(((z * lay.sides + side) * 2 + core) * rows + low, height)
+            copies.append(
+                pltpu.make_async_copy(
+                    source.at[:, pl.ds(k * height, height)],
+                    out.at[:, pl.ds(start, height)],
+                    sems.at[k],
+                )
+            )
     return copies
 
 
-def weight_kernel(lay, rows, s, low, parts, came, first, *refs):
+def weight_kernel(lay, rows, low, came, first, *refs):
     sides = lay.sides
-    mine, refs = refs[:parts], refs[parts:]
-    theirs, refs = refs[:parts], refs[parts:]
-    grads, refs = refs[:sides], refs[sides:]
+    weight, grads, refs = refs[0], refs[1 : 1 + sides], refs[1 + sides :]
     if came is not None:
         arrived, refs = refs[0], refs[1:]
     if not first:
@@ -196,36 +194,27 @@
     if sides == 2:
         far, refs = refs[0], refs[1:]
     own, sems, came_sems = refs
-    height = mine[0].shape[0]
-    width = parts * height
     side = (lax.axis_index("dp") // 2) % sides
     copies = []
     if came is not None:
-        copies = place(
-            lay, came[0], 1 - side, came[1], arrived.shape[1] // 2, rows, arrived, out, came_sems
-        )
+        copies = place(lay, 1 - side, rows, came, arrived, out, came_sems)
         for copy in copies:
             copy.start()
     for x in reversed(range(sides)):
         target = own if x == 0 else far
-        for k, group in enumerate((mine, theirs)):
-            for p, piece in enumerate(group):
-                target[:, k * width + p * height : k * width + (p + 1) * height] = lax.dot_general(
-                    grads[x][...],
-                    piece[...],
-                    (((1,), (1,)), ((), ())),
-                    preferred_element_type=f32,
-                ).astype(bf16)
-    owns = place(lay, s, side, low, width, rows, own, out, sems)
+        target[...] = lax.dot_general(
+            grads[x][...], weight[...], (((1,), (1,)), ((), ())), preferred_element_type=f32
+        ).astype(bf16)
+    owns = place(lay, side, rows, low, own, out, sems)
     for copy in owns:
         copy.start()
     for copy in owns + copies:
         copy.wait()
 
 
-def last_kernel(lay, rows, s, low, arrived, before, out, sems):
+def last_kernel(lay, rows, low, arrived, before, out, sems):
     side = (lax.axis_index("dp") // 2) % lay.sides
-    copies = place(lay, s, 1 - side, low, arrived.shape[1] // 2, rows, arrived, out, sems)
+    copies = place(lay, 1 - side, rows, low, arrived, out, sems)
     for copy in copies:
         copy.start()
     for copy in copies:
@@ -255,17 +244,6 @@
     return xor
 
 
-class Queue:
-    def __init__(self):
-        self.results = []
-
-    def send(self, move, value):
-        if len(self.results) >= 2:
-            value = after(value, self.results[-2])
-        self.results.append(move(value))
-        return self.results[-1]
-
-
 def call(kernel, name, shapes, args, in_specs=None, out_specs=None, scratch=(), flops=0, moved=2**20, **more):
     return pl.pallas_call(
         kernel,
@@ -290,19 +268,12 @@
         rows, rank = proj_basis.shape
         outs = key_grad.shape[1]
         owned = rank // n
-        parts = 2 if rows % 256 == 0 else 1
-        height = rows // parts
-        z_queue, y_queue = Queue(), Queue()
-
-        def swap_side(value):
-            return y_queue.send(lambda v: swap(v, 2), value)
-
-        def go_on(value):
-            return z_queue.send(onward, value)
-
-        plan = [(0, 0, ring), (1, 0, ring)]
-        for x in range(2, members):
-            plan += [(x, 0, ring // 2), (x, ring // 2, ring // 2)]
+        height = 128 if rows % 128 == 0 else rows
+        parts = rows // height
+
+        plan = [(x, 0, ring) for x in range(min(members, 3))]
+        if sides == 2:
+            plan += [(3, 0, ring // 2), (3, ring // 2, ring // 2)]
         cut = call(
             functools.partial(cut_kernel, lay, rows, plan),
             "cut",
@@ -313,50 +284,52 @@
             moved=4 * tokens * ring * rows * members,
         )
 
-        weight = master_weight.astype(bf16)
-        basis = [proj_basis]
-        mine = [[weight[p * height : (p + 1) * height] for p in range(parts)]]
-        mine += [[None] * parts for s in range(1, ring)]
-        far_grad = swap_side(key_grad) if sides == 2 else None
-        sends = []
+        basis = [after(proj_basis, cut[0])]
+        acts = list(cut)
+        if sides == 2:
+            far_grad = swap(key_grad, 2)
+            acts[2] = swap(cut[2], 2)
+            acts[3] = swap(after(cut[3], far_grad), 3)
+            acts[4] = swap(after(cut[4], acts[2]), 3)
         for s in range(1, ring):
-            sends.append((s, None))
-            if s <= parts:
-                sends.append((1, s - 1))
-        sends += [(s, p) for s in range(2, ring) for p in range(parts)]
-        early = [send for send in sends if send[1] is None or send[0] <= 2]
-        for s, p in early:
-            if p is None:
-                basis.append(go_on(basis[-1]))
-            else:
-                mine[s][p] = go_on(mine[s - 1][p])
-
-        acts = list(cut)
-        for k, (x, first, count) in enumerate(plan):
-            if x >= 2:
-                swap_x = functools.partial(swap, bit=x)
-                acts[k] = y_queue.send(swap_x, cut[k])
+            value = basis[-1]
+            if s == 2 and sides == 2:
+                value = after(value, far_grad)
+            basis.append(onward(value))
         acts[1] = swap(after(cut[1], basis[1]), 1)
         if sides == 2:
-            near = swap(jnp.concatenate([key_grad, after(far_grad, basis[1])], axis=0), 1)
+            near = swap(jnp.concatenate([key_grad, far_grad], axis=0), 1)
             grads = [key_grad, near[:tokens], far_grad, near[tokens:]]
         else:
             grads = [key_grad, swap(key_grad, 1)]
 
+        weight = master_weight.astype(bf16)
+        groups = None
+        if sides == 2:
+            groups = [
+                [(z * sides + side) * 2 + core for z in range(ring) for core in range(2)]
+                for side in range(sides)
+            ]
+        chunks = []
+        for p in range(parts):
+            chunk = weight[p * height : (p + 1) * height]
+            if p > 0:
+                chunk = after(chunk, basis[min(p + 1, ring - 1)], acts[p + 1])
+            chunks.append(
+                lax.all_gather(chunk, "dp", axis=0, tiled=True, axis_index_groups=groups)
+            )
+
         side_grads = [key_grad, far_grad] if sides == 2 else [key_grad]
         state = {"out": None, "waiting": None}
-
-        def multiply(s, group, gate=None):
-            low = group[0] * height
-            wide = len(group) * height
-            args = [mine[s][p] for p in group] + [swap(mine[s][p], 1) for p in group] + side_grads
-            if gate is not None:
-                args[0] = after(args[0], gate)
+        wide = 2 * ring * height
+
+        def multiply(p, gate=None):
+            args = [chunks[p] if gate is None else after(chunks[p], gate)] + side_grads
             in_specs = [VMEM] * len(args)
             came = None
             if state["waiting"] is not None:
-                came = state["waiting"][:2]
-                args.append(state["waiting"][2])
+                came = state["waiting"][0]
+                args.append(state["waiting"][1])
                 in_specs.append(VMEM)
             first = state["out"] is None
             if not first:
@@ -364,21 +337,21 @@
                 in_specs.append(HBM)
             shapes, out_specs = [((tokens, width), bf16)], [HBM]
             if sides == 2:
-                shapes.append(((tokens, 2 * wide), bf16))
+                shapes.append(((tokens, wide), bf16))
                 out_specs.append(VMEM)
             result = call(
-                functools.partial(weight_kernel, lay, rows, s, low, len(group), came, first),
+                functools.partial(weight_kernel, lay, rows, p * height, came, first),
                 "weight",
                 shapes,
                 args,
                 in_specs,
                 out_specs,
                 scratch=[
-                    pltpu.VMEM((tokens, 2 * wide), bf16),
-                    pltpu.SemaphoreType.DMA((2,)),
-                    pltpu.SemaphoreType.DMA((2,)),
+                    pltpu.VMEM((tokens, wide), bf16),
+                    pltpu.SemaphoreType.DMA((2 * ring,)),
+                    pltpu.SemaphoreType.DMA((2 * ring,)),
                 ],
-                flops=4 * sides * tokens * wide * outs,
+                flops=2 * sides * tokens * wide * outs,
                 moved=6 * 2**20,
                 input_output_aliases={} if first else {len(args) - 1: 0},
             )
@@ -386,30 +359,26 @@
             state["waiting"] = None
             return result[1] if sides == 2 else None
 
-        def give_back(s, group, block, gate=None):
+        def give_back(p, block, gate=None):
             if sides == 2:
                 if gate is not None:
                     block = after(block, gate)
-                state["waiting"] = (s, group[0] * height, swap_side(block))
-
-        everything = list(range(parts))
-        block = multiply(0, everything)
-        give_back(0, everything, block)
-        block = multiply(1, everything)
+                state["waiting"] = (p * height, swap(block, 2))
+
+        block = multiply(0)
+        give_back(0, block, acts[-1])
 
         total, *gives = call(
             functools.partial(project_kernel, lay, owned, plan),
             "project",
             [((n // 2, owned, outs), f32), ((n // 2, owned, outs), bf16)],
-            [after(acts[0], state["out"])] + acts[1:] + basis + grads,
+            [after(acts[0], block if sides == 2 else acts[0])] + acts[1:] + basis + grads,
             scratch=[pltpu.VMEM((rank, outs), f32)],
             flops=2 * tokens * members * rank * (ring * rows + outs),
             moved=12 * 2**20,
         )
 
         for k, (bit, radix) in enumerate(rounds):
-            if bit == members:
-                gives = [after(give, mine[2][0]) for give in gives]
             came = [swap(give, j * bit) for j, give in zip(range(1, radix), gives)]
             if k == len(rounds) - 1:
                 break
@@ -422,8 +391,9 @@
                 [total] + came,
                 moved=4 * total.size,
             )
-            if bit == 2 and sides == 2:
-                give_back(1, everything, block, total)
+        if parts > 1:
+            block = multiply(1, total)
+            give_back(1, block)
         owned_rows, square = call(
             functools.partial(square_kernel, len(came)),
             "square",
@@ -434,24 +404,15 @@
             if bit >= members:
                 square = sum([swap(square, j * bit) for j in range(1, radix)], square)
         squares = [square] + [swap(square, x) for x in range(1, members)]
-        if sides == 1:
-            give_back(1, everything, block)
-        for s, p in sends:
-            if (s, p) not in early and p == 0 and s == 3:
-                mine[s][p] = go_on(after(mine[s - 1][p], square))
-        if ring > 2:
-            block = multiply(2, everything, square)
         new_first, new_second, update = call(
             functools.partial(moment_kernel, members),
             "moment",
             [((owned, outs), f32), ((owned, outs), f32), ((1, owned, outs), bf16)],
             squares + [owned_rows, first_moment, second_moment],
         )
-        if ring > 2:
-            give_back(2, everything, block, squares[-1])
-        for s, p in sends:
-            if p is not None and mine[s][p] is None:
-                mine[s][p] = go_on(after(mine[s - 1][p], update))
+        if parts > 2:
+            block = multiply(2, update)
+            give_back(2, block)
 
         whole = update
         for bit, radix in reversed(rounds[1:]):
@@ -468,22 +429,20 @@
             moved=8 * 2**20,
         )
 
-        for s in range(3, ring):
-            groups = [everything] if s < ring - 1 else [[p] for p in everything]
-            for group in groups:
-                block = multiply(s, group)
-                give_back(s, group, block, whole if s == 3 and group[0] == 0 else None)
+        for p in range(3, parts):
+            block = multiply(p, whole)
+            give_back(p, block)
         activation_grad = state["out"]
         if state["waiting"] is not None:
-            s, low, arrived = state["waiting"]
+            low, arrived = state["waiting"]
             (activation_grad,) = call(
-                functools.partial(last_kernel, lay, rows, s, low),
+                functools.partial(last_kernel, lay, rows, low),
                 "last",
                 [((tokens, width), bf16)],
                 [arrived, activation_grad],
                 [VMEM, HBM],
                 [HBM],
-                scratch=[pltpu.SemaphoreType.DMA((2,))],
+                scratch=[pltpu.SemaphoreType.DMA((2 * ring,))],
                 input_output_aliases={1: 0},
             )
         return (activation_grad, new_master, new_first, new_second)

time: 192 us -> 230 us (1.20)
  local copies, waits for them, and re-layouts: 2.53 us -> 17.7 us
  between operations: 1.06 us -> 14.1 us
  starting transfers between devices: 46.9 us -> 52.3 us
  Pallas kernels: 18.2 us -> 22.4 us
  other arithmetic: 0.27 us -> 2.83 us
    ppermute x36 -> x26, waiting for transfers between devices: 106 us -> 81 us  [swap(): return lax.ppermute(value, 'dp', [(i, i ^ bit) for i in range(self.n)])]
    ppermute x9 -> x3, waiting for transfers between devices: 16.6 us -> 39.6 us  [onward(): return lax.ppermute(value, 'dp', self.forward)]
    unnamed x16 -> x52, local copies, waits for them, and re-layouts: 2.37 us -> 15.4 us
    ppermute x36 -> x26, starting transfers between devices: 31.4 us -> 40.8 us  [swap(): return lax.ppermute(value, 'dp', [(i, i ^ bit) for i in range(self.n)])]
    pallas_call x13 -> x12, Pallas kernels: 18.2 us -> 22.4 us  [call(): pl.pallas_call(kernel, name=name, out_shape=[jax.ShapeDtypeStruct(shape,...]
    ppermute x9 -> x3, starting transfers between devices: 15.4 us -> 11.3 us  [onward(): return lax.ppermute(value, 'dp', self.forward)]
  transfers between devices with their start and end apart: 45 -> 33, of which waited for: 23 -> 14; matrix products, arithmetic and copies ran while one was open for 0% -> 1% of each run, Pallas kernels for 7% -> 9%
where the time goes in v5:
time: 230 us
  waiting for transfers between devices  121 us (53%)
  starting transfers between devices  52.3 us (23%)
  Pallas kernels  22.4 us (10%)
  local copies, waits for them, and re-layouts  17.7 us (8%)
  between operations  14.1 us (6%)
  other arithmetic  2.83 us (1%)
    ppermute x26, waiting for transfers between devices, swap(): return lax.ppermute(value, 'dp', [(i, i ^ bit) for i in range(self.n)])  81 us
    ppermute x26, starting transfers between devices, swap(): return lax.ppermute(value, 'dp', [(i, i ^ bit) for i in range(self.n)])  40.8 us
    ppermute x3, waiting for transfers between devices, onward(): return lax.ppermute(value, 'dp', self.forward)  39.6 us
    pallas_call x12, Pallas kernels, call(): pl.pallas_call(kernel, name=name, out_shape=[jax.ShapeDtypeStruct(shape,...  22.4 us
    unnamed x52, local copies, waits for them, and re-layouts  15.4 us
    ppermute x3, starting transfers between devices, onward(): return lax.ppermute(value, 'dp', self.forward)  11.3 us
  transfers between devices with their start and end apart: 33, of which 14 were waited for; matrix products, arithmetic and copies ran while one was open for 1% of the time, Pallas kernels for 9%

profile of v5, /device:TPU:0, one launch (start us, length us, event | category | flops | bytes accessed | tf_op | source)
XLA Modules:
  0.0 230.1 jit_solution(4611102450045495911)
XLA Ops:
  7.2 1.7 convert_element_type.3
  9.0 1.0 fusion
  10.1 2.2 copy-done.2
  12.3 1.5 cut.1
  16.3 3.0 %collective-permute-start = (bf16[512,512]{1,0:T(8,128)(2,1)S(1)}, bf16[512,512]{1,0:T(8,128)(2,1)S(1)}, u32[]{:S(2)}, u32[]{:S(2)}) collective-permute-start(bf16[512,512]{1,0:T(8,128)(2,1)S(1)} %copy-done.6), channel_id=1, source_target_pairs={{0,4},{1,5},{2,6},{3,7},{4,12},{5,13},{6,14},{7,15},{12,8},{13,9},... | collective-permute-start | bytes 1572872 | tf_op jit(solution)/shard_map/ppermute | solution.py:52
  19.4 1.5 collective-permute-start.1
  21.4 24.3 %collective-permute-done.refs_6_ = bf16[512,512]{1,0:T(8,128)(2,1)S(1)} collective-permute-done((bf16[512,512]{1,0:T(8,128)(2,1)S(1)}, bf16[512,512]{1,0:T(8,128)(2,1)S(1)}, u32[]{:S(2)}, u32[]{:S(2)}) %collective-permute-start) | collective-permute-done | bytes 524320 | tf_op jit(solution)/shard_map/ppermute | solution.py:52
  45.7 4.4 %collective-permute-start.2 = (bf16[512,512]{1,0:T(8,128)(2,1)S(1)}, bf16[512,512]{1,0:T(8,128)(2,1)S(1)}, u32[]{:S(2)}, u32[]{:S(2)}) collective-permute-start(bf16[512,512]{1,0:T(8,128)(2,1)S(1)} %collective-permute-done.refs_6_), channel_id=1, source_target_pairs={{0,4},{1,5},{2,6},{3,7},{4,12},{5,13},{6,14},{7,15},{12,8},{13,9},... | collective-permute-start | bytes 1572872 | tf_op jit(solution)/shard_map/ppermute | solution.py:52
  50.0 10.4 %collective-permute-done.2.refs_7_ = bf16[512,512]{1,0:T(8,128)(2,1)S(1)} collective-permute-done((bf16[512,512]{1,0:T(8,128)(2,1)S(1)}, bf16[512,512]{1,0:T(8,128)(2,1)S(1)}, u32[]{:S(2)}, u32[]{:S(2)}) %collective-permute-start.2) | collective-permute-done | bytes 524320 | tf_op jit(solution)/shard_map/ppermute | solution.py:52
  61.4 3.9 %collective-permute-start.3 = (bf16[512,512]{1,0:T(8,128)(2,1)}, bf16[512,512]{1,0:T(8,128)(2,1)S(1)}, u32[]{:S(2)}, u32[]{:S(2)}) collective-permute-start(bf16[512,512]{1,0:T(8,128)(2,1)} %copy-done.14), channel_id=1, source_target_pairs={{0,4},{1,5},{2,6},{3,7},{4,12},{5,13},{6,14},{7,15},{12,8},{13,9},... | collective-permute-start | bytes 1572872 | tf_op jit(solution)/shard_map/ppermute | solution.py:52
  65.3 10.4 %collective-permute-done.7.refs_3_ = bf16[256,1024]{1,0:T(8,128)(2,1)S(1)} collective-permute-done((bf16[256,1024]{1,0:T(8,128)(2,1)}, bf16[256,1024]{1,0:T(8,128)(2,1)S(1)}, u32[]{:S(2)}, u32[]{:S(2)}) %collective-permute-start.7) | collective-permute-done | bytes 524320 | tf_op jit(solution)/shard_map/ppermute | solution.py:49
  76.5 4.9 %collective-permute-done.3.refs_8_ = bf16[512,512]{1,0:T(8,128)(2,1)S(1)} collective-permute-done((bf16[512,512]{1,0:T(8,128)(2,1)}, bf16[512,512]{1,0:T(8,128)(2,1)S(1)}, u32[]{:S(2)}, u32[]{:S(2)}) %collective-permute-start.3) | collective-permute-done | bytes 524320 | tf_op jit(solution)/shard_map/ppermute | solution.py:52
  82.3 2.3 collective-permute-start.5
  84.5 1.0 pad_maximum_fusion
  85.6 10.9 %collective-permute-done.5.refs_4_ = bf16[256,1024]{1,0:T(8,128)(2,1)S(1)} collective-permute-done((bf16[256,1024]{1,0:T(8,128)(2,1)}, bf16[256,1024]{1,0:T(8,128)(2,1)S(1)}, u32[]{:S(2)}, u32[]{:S(2)}) %collective-permute-start.5) | collective-permute-done | bytes 524320 | tf_op jit(solution)/shard_map/ppermute | solution.py:49
  97.9 1.3 fusion.1
  99.2 1.6 copy-done.9
  100.8 3.0 %weight.4 = (bf16[256,8192]{1,0:T(8,128)(2,1)}, bf16[256,1024]{1,0:T(8,128)(2,1)}) custom-call(bf16[1024,1024]{1,0:T(8,128)(2,1)S(1)} %copy-done.9, bf16[256,1024]{1,0:T(8,128)(2,1)S(1)} %copy-done.1, bf16[256,1024]{1,0:T(8,128)(2,1)S(1)} %collective-permute-done.1.refs_2_.refs_11_), custom_call_target="tpu_custom_call" | custom-call | flops 1073741824 | bytes 6291456 | tf_op jit(solution)/shard_map/weight/pallas_call | solution.py:248
  103.9 1.0 copy-done.22
  105.0 5.6 %project.1 = (f32[8,32,1024]{2,1,0:T(8,128)S(1)}, bf16[8,32,1024]{2,1,0:T(8,128)(2,1)S(1)}) custom-call(bf16[256,2048]{1,0:T(8,128)(2,1)S(1)} %copy-done.11, bf16[256,2048]{1,0:T(8,128)(2,1)} %collective-permute-done.6.refs_1_, bf16[256,2048]{1,0:T(8,128)(2,1)S(1)} %copy-done.13, bf16[256,1024]{1,0:T(8,128)(2,1)S(1)} %copy-done.18, ...), custom_call_target="tpu_custom_call" | custom-call | flops 3221225472 | bytes 12582912 | tf_op jit(solution)/shard_map/project/pallas_call | solution.py:248
  110.6 1.8 collective-permute-start.24
  112.6 1.8 collective-permute-start.10
  114.4 16.4 %collective-permute-done.10.refs_1_ = bf16[4,32,1024]{2,1,0:T(8,128)(2,1)S(1)} collective-permute-done((bf16[4,32,1024]{2,1,0:T(8,128)(2,1)S(1)}, bf16[4,32,1024]{2,1,0:T(8,128)(2,1)S(1)}, u32[]{:S(2)}, u32[]{:S(2)}) %collective-permute-start.10) | collective-permute-done | bytes 262176 | tf_op jit(solution)/shard_map/ppermute | solution.py:49
  130.9 1.6 copy-done.5
  132.5 3.0 %weight.5 = (bf16[256,8192]{1,0:T(8,128)(2,1)}, bf16[256,1024]{1,0:T(8,128)(2,1)}) custom-call(bf16[1024,1024]{1,0:T(8,128)(2,1)S(1)} %copy-done.5, bf16[256,1024]{1,0:T(8,128)(2,1)S(1)} %copy-done.1, bf16[256,1024]{1,0:T(8,128)(2,1)S(1)} %collective-permute-done.1.refs_2_.refs_11_, ...), custom_call_target="tpu_custom_call", output_to_operand_aliasing={{0}: (4, {})} | custom-call | flops 1073741824 | bytes 6291456 | tf_op jit(solution)/shard_map/weight/pallas_call | solution.py:248
  135.5 1.8 collective-permute-start.25
  137.3 10.3 %collective-permute-start.11 = (bf16[1,32,1024]{2,1,0:T(8,128)(2,1)S(1)}, bf16[1,32,1024]{2,1,0:T(8,128)(2,1)S(1)}, u32[]{:S(2)}, u32[]{:S(2)}) collective-permute-start(bf16[1,32,1024]{2,1,0:T(8,128)(2,1)S(1)} %get-tuple-element.61), channel_id=1, source_target_pairs={{0,4},{1,5},{2,6},{3,7},{4,0},{5,1},{6,2},{7,3},{8,12},{9,13},{10,... | collective-permute-start | bytes 196616 | tf_op jit(solution)/shard_map/ppermute | solution.py:49
  147.6 4.4 %collective-permute-start.12 = (bf16[1,32,1024]{2,1,0:T(8,128)(2,1)S(1)}, bf16[1,32,1024]{2,1,0:T(8,128)(2,1)S(1)}, u32[]{:S(2)}, u32[]{:S(2)}) collective-permute-start(bf16[1,32,1024]{2,1,0:T(8,128)(2,1)S(1)} %get-tuple-element.62), channel_id=1, source_target_pairs={{0,8},{1,9},{2,10},{3,11},{4,12},{5,13},{6,14},{7,15},{8,0},{9,1},... | collective-permute-start | bytes 196616 | tf_op jit(solution)/shard_map/ppermute | solution.py:49
  152.0 2.8 %collective-permute-done.11.refs_1_ = bf16[1,32,1024]{2,1,0:T(8,128)(2,1)S(1)} collective-permute-done((bf16[1,32,1024]{2,1,0:T(8,128)(2,1)S(1)}, bf16[1,32,1024]{2,1,0:T(8,128)(2,1)S(1)}, u32[]{:S(2)}, u32[]{:S(2)}) %collective-permute-start.11) | collective-permute-done | bytes 65568 | tf_op jit(solution)/shard_map/ppermute | solution.py:49
  154.8 6.7 %collective-permute-done.12.refs_2_ = bf16[1,32,1024]{2,1,0:T(8,128)(2,1)S(1)} collective-permute-done((bf16[1,32,1024]{2,1,0:T(8,128)(2,1)S(1)}, bf16[1,32,1024]{2,1,0:T(8,128)(2,1)S(1)}, u32[]{:S(2)}, u32[]{:S(2)}) %collective-permute-start.12) | collective-permute-done | bytes 65568 | tf_op jit(solution)/shard_map/ppermute | solution.py:49
  161.7 2.4 %collective-permute-start.16 = (f32[8,128]{1,0:T(8,128)S(1)}, f32[8,128]{1,0:T(8,128)S(1)}, u32[]{:S(2)}, u32[]{:S(2)}) collective-permute-start(f32[8,128]{1,0:T(8,128)S(1)} %get-tuple-element.64), channel_id=1, source_target_pairs={{0,12},{1,13},{2,14},{3,15},{4,8},{5,9},{6,10},{7,11},{8,4},{9,5},... | collective-permute-start | bytes 12296 | tf_op jit(solution)/shard_map/ppermute | solution.py:49
  164.1 3.7 %collective-permute-start.15 = (f32[8,128]{1,0:T(8,128)S(1)}, f32[8,128]{1,0:T(8,128)S(1)}, u32[]{:S(2)}, u32[]{:S(2)}) collective-permute-start(f32[8,128]{1,0:T(8,128)S(1)} %get-tuple-element.64), channel_id=1, source_target_pairs={{0,8},{1,9},{2,10},{3,11},{4,12},{5,13},{6,14},{7,15},{8,0},{9,1},... | collective-permute-start | bytes 12296 | tf_op jit(solution)/shard_map/ppermute | solution.py:49
  167.8 1.6 collective-permute-done.15
  169.4 2.0 collective-permute-done.14
  171.4 1.1 collective-permute-start.18
  173.3 1.8 collective-permute-done.18.refs_2_
  176.6 1.9 collective-permute-start.21
  178.6 2.2 collective-permute-start.22
  180.8 1.6 copy-done.4
  182.3 3.0 %weight.6 = (bf16[256,8192]{1,0:T(8,128)(2,1)}, bf16[256,1024]{1,0:T(8,128)(2,1)}) custom-call(bf16[1024,1024]{1,0:T(8,128)(2,1)S(1)} %copy-done.4, bf16[256,1024]{1,0:T(8,128)(2,1)S(1)} %copy-done.1, bf16[256,1024]{1,0:T(8,128)(2,1)S(1)} %collective-permute-done.1.refs_2_.refs_11_, ...), custom_call_target="tpu_custom_call", output_to_operand_aliasing={{0}: (4, {})} | custom-call | flops 1073741824 | bytes 6291456 | tf_op jit(solution)/shard_map/weight/pallas_call | solution.py:248
  185.3 1.1 collective-permute-start.26
  186.5 1.1 collective-permute-start.23
  187.6 16.8 %collective-permute-done.23 = bf16[4,32,1024]{2,1,0:T(8,128)(2,1)S(1)} collective-permute-done((bf16[4,32,1024]{2,1,0:T(8,128)(2,1)S(1)}, bf16[4,32,1024]{2,1,0:T(8,128)(2,1)S(1)}, u32[]{:S(2)}, u32[]{:S(2)}) %collective-permute-start.23) | collective-permute-done | bytes 262176 | tf_op jit(solution)/shard_map/ppermute | solution.py:49
  204.5 1.6 copy-done.3
  206.1 2.2 weight.7
  208.4 1.1 collective-permute-start.27
  209.4 2.2 back.1
  211.6 11.1 %collective-permute-done.27.arrived = bf16[256,1024]{1,0:T(8,128)(2,1)S(1)} collective-permute-done((bf16[256,1024]{1,0:T(8,128)(2,1)S(1)}, bf16[256,1024]{1,0:T(8,128)(2,1)S(1)}, u32[]{:S(2)}, u32[]{:S(2)}) %collective-permute-start.27) | collective-permute-done | bytes 524320 | tf_op jit(solution)/shard_map/ppermute | solution.py:49
  (93 shorter events, 11.1 us)
Async XLA Ops:
  7.2 92.1 %all-gather.7.cloned.1.call-start = ((), (), s32[]{:S(2)}) async-start(), calls=%async_computation.1 | async-start | bytes 2359296 | tf_op jit(solution)/shard_map/all_gather | solution.py:319
  10.0 9.4 %copy-start.1 = (bf16[256,1024]{1,0:T(8,128)(2,1)S(1)}, bf16[256,1024]{1,0:T(8,128)(2,1)}, u32[]{:S(2)}) copy-start(bf16[256,1024]{1,0:T(8,128)(2,1)} %refs_1_.7) | copy-start | bytes 1572868
  10.0 120.9 %all-gather.11.cloned.1.call-start = ((), (), s32[]{:S(2)}) async-start(), calls=%async_computation.3 | async-start | bytes 2359296 | tf_op jit(solution)/shard_map/all_gather | solution.py:319
  10.0 2.2 copy-start.2
  12.3 4.1 %copy-start.6 = (bf16[512,512]{1,0:T(8,128)(2,1)S(1)}, bf16[512,512]{1,0:T(8,128)(2,1)}, u32[]{:S(2)}) copy-start(bf16[512,512]{1,0:T(8,128)(2,1)} %basis.1) | copy-start | bytes 1572868
  16.3 29.3 %collective-permute-start = (bf16[512,512]{1,0:T(8,128)(2,1)S(1)}, bf16[512,512]{1,0:T(8,128)(2,1)S(1)}, u32[]{:S(2)}, u32[]{:S(2)}) collective-permute-start(bf16[512,512]{1,0:T(8,128)(2,1)S(1)} %copy-done.6), channel_id=1, source_target_pairs={{0,4},{1,5},{2,6},{3,7},{4,12},{5,13},{6,14},{7,15},{12,8},{13,9},... | collective-permute-start | bytes 1572872 | tf_op jit(solution)/shard_map/ppermute | solution.py:52
  19.4 26.3 %collective-permute-start.1 = (bf16[256,1024]{1,0:T(8,128)(2,1)S(1)}, bf16[256,1024]{1,0:T(8,128)(2,1)S(1)}, u32[]{:S(2)}, u32[]{:S(2)}) collective-permute-start(bf16[256,1024]{1,0:T(8,128)(2,1)S(1)} %copy-done.1), channel_id=1, source_target_pairs={{0,2},{1,3},{2,0},{3,1},{4,6},{5,7},{6,4},{7,5},{8,10},{9,11},{10,... | collective-permute-start | bytes 1572872 | tf_op jit(solution)/shard_map/ppermute | solution.py:49
  20.9 39.5 %collective-permute-start.4 = (bf16[256,2048]{1,0:T(8,128)(2,1)S(1)}, bf16[256,2048]{1,0:T(8,128)(2,1)S(1)}, u32[]{:S(2)}, u32[]{:S(2)}) collective-permute-start(bf16[256,2048]{1,0:T(8,128)(2,1)S(1)} %get-tuple-element.47), channel_id=1, source_target_pairs={{0,2},{1,3},{2,0},{3,1},{4,6},{5,7},{6,4},{7,5},{8,10},{9,11},{10,... | collective-permute-start | bytes 3145736 | tf_op jit(solution)/shard_map/ppermute | solution.py:49
  45.7 14.8 %collective-permute-start.2 = (bf16[512,512]{1,0:T(8,128)(2,1)S(1)}, bf16[512,512]{1,0:T(8,128)(2,1)S(1)}, u32[]{:S(2)}, u32[]{:S(2)}) collective-permute-start(bf16[512,512]{1,0:T(8,128)(2,1)S(1)} %collective-permute-done.refs_6_), channel_id=1, source_target_pairs={{0,4},{1,5},{2,6},{3,7},{4,12},{5,13},{6,14},{7,15},{12,8},{13,9},... | collective-permute-start | bytes 1572872 | tf_op jit(solution)/shard_map/ppermute | solution.py:52
  61.2 36.7 %copy-start.12 = (bf16[256,2048]{1,0:T(8,128)(2,1)}, bf16[256,2048]{1,0:T(8,128)(2,1)S(1)}, u32[]{:S(2)}) copy-start(bf16[256,2048]{1,0:T(8,128)(2,1)S(1)} %collective-permute-done.4.refs_2_) | copy-start | bytes 3145732
  61.3 119.5 %all-gather.9.cloned.1.call-start = ((), (), s32[]{:S(2)}) async-start(), calls=%async_computation.2 | async-start | bytes 2359296 | tf_op jit(solution)/shard_map/all_gather | solution.py:319
  61.3 14.4 %collective-permute-start.7 = (bf16[256,1024]{1,0:T(8,128)(2,1)}, bf16[256,1024]{1,0:T(8,128)(2,1)S(1)}, u32[]{:S(2)}, u32[]{:S(2)}) collective-permute-start(bf16[256,1024]{1,0:T(8,128)(2,1)} %copy-done.23), channel_id=1, source_target_pairs={{0,3},{1,2},{2,1},{3,0},{4,7},{5,6},{6,5},{7,4},{8,11},{9,10},{10,... | collective-permute-start | bytes 1572872 | tf_op jit(solution)/shard_map/ppermute | solution.py:49
  61.4 20.0 %collective-permute-start.3 = (bf16[512,512]{1,0:T(8,128)(2,1)}, bf16[512,512]{1,0:T(8,128)(2,1)S(1)}, u32[]{:S(2)}, u32[]{:S(2)}) collective-permute-start(bf16[512,512]{1,0:T(8,128)(2,1)} %copy-done.14), channel_id=1, source_target_pairs={{0,4},{1,5},{2,6},{3,7},{4,12},{5,13},{6,14},{7,15},{12,8},{13,9},... | collective-permute-start | bytes 1572872 | tf_op jit(solution)/shard_map/ppermute | solution.py:52
  82.2 122.3 %all-gather.5.cloned.1.call-start = ((), (), s32[]{:S(2)}) async-start(), calls=%async_computation | async-start | bytes 2359296 | tf_op jit(solution)/shard_map/all_gather | solution.py:319
  82.3 14.3 %collective-permute-start.5 = (bf16[256,1024]{1,0:T(8,128)(2,1)}, bf16[256,1024]{1,0:T(8,128)(2,1)S(1)}, u32[]{:S(2)}, u32[]{:S(2)}) collective-permute-start(bf16[256,1024]{1,0:T(8,128)(2,1)} %copy-done.16), channel_id=1, source_target_pairs={{0,3},{1,2},{2,1},{3,0},{4,7},{5,6},{6,5},{7,4},{8,11},{9,10},{10,... | collective-permute-start | bytes 1572872 | tf_op jit(solution)/shard_map/ppermute | solution.py:49
  85.6 12.4 %collective-permute-start.8 = (bf16[512,1024]{1,0:T(8,128)(2,1)}, bf16[512,1024]{1,0:T(8,128)(2,1)}, u32[]{:S(2)}, u32[]{:S(2)}) collective-permute-start(bf16[512,1024]{1,0:T(8,128)(2,1)} %pad_maximum_fusion), channel_id=1, source_target_pairs={{0,1},{1,0},{2,3},{3,2},{4,5},{5,4},{6,7},{7,6},{8,9},{9,8},{10,11... | collective-permute-start | bytes 3145736 | tf_op jit(solution)/shard_map/ppermute | solution.py:49
  97.4 6.5 %collective-permute-start.6 = (bf16[256,2048]{1,0:T(8,128)(2,1)}, bf16[256,2048]{1,0:T(8,128)(2,1)}, u32[]{:S(2)}, u32[]{:S(2)}) collective-permute-start(bf16[256,2048]{1,0:T(8,128)(2,1)} %get-tuple-element.53), channel_id=1, source_target_pairs={{0,1},{1,0},{2,3},{3,2},{4,5},{5,4},{6,7},{7,6},{8,9},{9,8},{10,11... | collective-permute-start | bytes 3145736 | tf_op jit(solution)/shard_map/ppermute | solution.py:49
  99.2 1.6 copy-start.9
  100.8 3.1 %copy-start.11 = (bf16[256,2048]{1,0:T(8,128)(2,1)S(1)}, bf16[256,2048]{1,0:T(8,128)(2,1)}, u32[]{:S(2)}) copy-start(bf16[256,2048]{1,0:T(8,128)(2,1)} %copy-done.10) | copy-start | bytes 3145732
  100.8 3.1 %copy-start.13 = (bf16[256,2048]{1,0:T(8,128)(2,1)S(1)}, bf16[256,2048]{1,0:T(8,128)(2,1)}, u32[]{:S(2)}) copy-start(bf16[256,2048]{1,0:T(8,128)(2,1)} %copy-done.12) | copy-start | bytes 3145732
  100.8 3.1 %copy-start.15 = (bf16[512,512]{1,0:T(8,128)(2,1)S(1)}, bf16[512,512]{1,0:T(8,128)(2,1)}, u32[]{:S(2)}) copy-start(bf16[512,512]{1,0:T(8,128)(2,1)} %copy-done.14) | copy-start | bytes 1572868
  100.8 3.1 %copy-start.18 = (bf16[256,1024]{1,0:T(8,128)(2,1)S(1)}, bf16[256,1024]{1,0:T(8,128)(2,1)}, u32[]{:S(2)}) copy-start(bf16[256,1024]{1,0:T(8,128)(2,1)} %copy-done.17) | copy-start | bytes 1572868
  100.8 3.1 %copy-start.20 = (bf16[512,512]{1,0:T(8,128)(2,1)S(1)}, bf16[512,512]{1,0:T(8,128)(2,1)}, u32[]{:S(2)}) copy-start(bf16[512,512]{1,0:T(8,128)(2,1)} %copy-done.19) | copy-start | bytes 1572868
  110.5 2.0 collective-permute-start.9
  110.6 20.2 %collective-permute-start.24 = (bf16[256,1024]{1,0:T(8,128)(2,1)}, bf16[256,1024]{1,0:T(8,128)(2,1)S(1)}, u32[]{:S(2)}, u32[]{:S(2)}) collective-permute-start(bf16[256,1024]{1,0:T(8,128)(2,1)} %get-tuple-element.72), channel_id=1, source_target_pairs={{0,2},{1,3},{2,0},{3,1},{4,6},{5,7},{6,4},{7,5},{8,10},{9,11},{10,... | collective-permute-start | bytes 1572872 | tf_op jit(solution)/shard_map/ppermute | solution.py:49
  112.6 18.2 %collective-permute-start.10 = (bf16[4,32,1024]{2,1,0:T(8,128)(2,1)S(1)}, bf16[4,32,1024]{2,1,0:T(8,128)(2,1)S(1)}, u32[]{:S(2)}, u32[]{:S(2)}) collective-permute-start(bf16[4,32,1024]{2,1,0:T(8,128)(2,1)S(1)} %get-tuple-element.59), channel_id=1, source_target_pairs={{0,2},{1,3},{2,0},{3,1},{4,6},{5,7},{6,4},{7,5},{8,10},{9,11},{10,... | collective-permute-start | bytes 786440 | tf_op jit(solution)/shard_map/ppermute | solution.py:49
  130.9 1.6 copy-start.5
  132.5 43.1 %copy-start.7 = (f32[32,1024]{1,0:T(8,128)S(1)}, f32[32,1024]{1,0:T(8,128)}, u32[]{:S(2)}) copy-start(f32[32,1024]{1,0:T(8,128)} %refs_5_.2) | copy-start | bytes 393220
  132.5 43.1 %copy-start.8 = (f32[32,1024]{1,0:T(8,128)S(1)}, f32[32,1024]{1,0:T(8,128)}, u32[]{:S(2)}) copy-start(f32[32,1024]{1,0:T(8,128)} %refs_6_.1) | copy-start | bytes 393220
  135.5 45.3 %collective-permute-start.25 = (bf16[256,1024]{1,0:T(8,128)(2,1)}, bf16[256,1024]{1,0:T(8,128)(2,1)S(1)}, u32[]{:S(2)}, u32[]{:S(2)}) collective-permute-start(bf16[256,1024]{1,0:T(8,128)(2,1)} %get-tuple-element.74), channel_id=1, source_target_pairs={{0,2},{1,3},{2,0},{3,1},{4,6},{5,7},{6,4},{7,5},{8,10},{9,11},{10,... | collective-permute-start | bytes 1572872 | tf_op jit(solution)/shard_map/ppermute | solution.py:49
  137.3 17.6 %collective-permute-start.11 = (bf16[1,32,1024]{2,1,0:T(8,128)(2,1)S(1)}, bf16[1,32,1024]{2,1,0:T(8,128)(2,1)S(1)}, u32[]{:S(2)}, u32[]{:S(2)}) collective-permute-start(bf16[1,32,1024]{2,1,0:T(8,128)(2,1)S(1)} %get-tuple-element.61), channel_id=1, source_target_pairs={{0,4},{1,5},{2,6},{3,7},{4,0},{5,1},{6,2},{7,3},{8,12},{9,13},{10,... | collective-permute-start | bytes 196616 | tf_op jit(solution)/shard_map/ppermute | solution.py:49
  147.6 14.0 %collective-permute-start.12 = (bf16[1,32,1024]{2,1,0:T(8,128)(2,1)S(1)}, bf16[1,32,1024]{2,1,0:T(8,128)(2,1)S(1)}, u32[]{:S(2)}, u32[]{:S(2)}) collective-permute-start(bf16[1,32,1024]{2,1,0:T(8,128)(2,1)S(1)} %get-tuple-element.62), channel_id=1, source_target_pairs={{0,8},{1,9},{2,10},{3,11},{4,12},{5,13},{6,14},{7,15},{8,0},{9,1},... | collective-permute-start | bytes 196616 | tf_op jit(solution)/shard_map/ppermute | solution.py:49
  152.0 9.6 %collective-permute-start.13 = (bf16[1,32,1024]{2,1,0:T(8,128)(2,1)S(1)}, bf16[1,32,1024]{2,1,0:T(8,128)(2,1)S(1)}, u32[]{:S(2)}, u32[]{:S(2)}) collective-permute-start(bf16[1,32,1024]{2,1,0:T(8,128)(2,1)S(1)} %get-tuple-element.63), channel_id=1, source_target_pairs={{0,12},{1,13},{2,14},{3,15},{4,8},{5,9},{6,10},{7,11},{8,4},{9,5},... | collective-permute-start | bytes 196616 | tf_op jit(solution)/shard_map/ppermute | solution.py:49
  161.7 6.1 %collective-permute-start.16 = (f32[8,128]{1,0:T(8,128)S(1)}, f32[8,128]{1,0:T(8,128)S(1)}, u32[]{:S(2)}, u32[]{:S(2)}) collective-permute-start(f32[8,128]{1,0:T(8,128)S(1)} %get-tuple-element.64), channel_id=1, source_target_pairs={{0,12},{1,13},{2,14},{3,15},{4,8},{5,9},{6,10},{7,11},{8,4},{9,5},... | collective-permute-start | bytes 12296 | tf_op jit(solution)/shard_map/ppermute | solution.py:49
  164.1 5.3 %collective-permute-start.15 = (f32[8,128]{1,0:T(8,128)S(1)}, f32[8,128]{1,0:T(8,128)S(1)}, u32[]{:S(2)}, u32[]{:S(2)}) collective-permute-start(f32[8,128]{1,0:T(8,128)S(1)} %get-tuple-element.64), channel_id=1, source_target_pairs={{0,8},{1,9},{2,10},{3,11},{4,12},{5,13},{6,14},{7,15},{8,0},{9,1},... | collective-permute-start | bytes 12296 | tf_op jit(solution)/shard_map/ppermute | solution.py:49
  167.8 3.6 %collective-permute-start.14 = (f32[8,128]{1,0:T(8,128)S(1)}, f32[8,128]{1,0:T(8,128)S(1)}, u32[]{:S(2)}, u32[]{:S(2)}) collective-permute-start(f32[8,128]{1,0:T(8,128)S(1)} %get-tuple-element.64), channel_id=1, source_target_pairs={{0,4},{1,5},{2,6},{3,7},{4,0},{5,1},{6,2},{7,3},{8,12},{9,13},{10,... | collective-permute-start | bytes 12296 | tf_op jit(solution)/shard_map/ppermute | solution.py:49
  171.4 1.9 collective-permute-start.17
  171.4 3.7 %collective-permute-start.18 = (f32[8,128]{1,0:T(8,128)S(1)}, f32[8,128]{1,0:T(8,128)S(1)}, u32[]{:S(2)}, u32[]{:S(2)}) collective-permute-start(f32[8,128]{1,0:T(8,128)S(1)} %add_add_fusion.refs_0_), channel_id=1, source_target_pairs={{0,2},{1,3},{2,0},{3,1},{4,6},{5,7},{6,4},{7,5},{8,10},{9,11},{10,... | collective-permute-start | bytes 12296 | tf_op jit(solution)/shard_map/ppermute | solution.py:49
  172.5 3.0 %collective-permute-start.19 = (f32[8,128]{1,0:T(8,128)S(1)}, f32[8,128]{1,0:T(8,128)S(1)}, u32[]{:S(2)}, u32[]{:S(2)}) collective-permute-start(f32[8,128]{1,0:T(8,128)S(1)} %add_add_fusion.refs_0_), channel_id=1, source_target_pairs={{0,3},{1,2},{2,1},{3,0},{4,7},{5,6},{6,5},{7,4},{8,11},{9,10},{10,... | collective-permute-start | bytes 12296 | tf_op jit(solution)/shard_map/ppermute | solution.py:49
  176.3 10.1 %collective-permute-start.20 = (bf16[1,32,1024]{2,1,0:T(8,128)(2,1)S(1)}, bf16[1,32,1024]{2,1,0:T(8,128)(2,1)S(1)}, u32[]{:S(2)}, u32[]{:S(2)}) collective-permute-start(bf16[1,32,1024]{2,1,0:T(8,128)(2,1)S(1)} %get-tuple-element.66), channel_id=1, source_target_pairs={{0,4},{1,5},{2,6},{3,7},{4,0},{5,1},{6,2},{7,3},{8,12},{9,13},{10,... | collective-permute-start | bytes 196616 | tf_op jit(solution)/shard_map/ppermute | solution.py:49
  176.6 9.8 %collective-permute-start.21 = (bf16[1,32,1024]{2,1,0:T(8,128)(2,1)S(1)}, bf16[1,32,1024]{2,1,0:T(8,128)(2,1)S(1)}, u32[]{:S(2)}, u32[]{:S(2)}) collective-permute-start(bf16[1,32,1024]{2,1,0:T(8,128)(2,1)S(1)} %get-tuple-element.66), channel_id=1, source_target_pairs={{0,8},{1,9},{2,10},{3,11},{4,12},{5,13},{6,14},{7,15},{8,0},{9,1},... | collective-permute-start | bytes 196616 | tf_op jit(solution)/shard_map/ppermute | solution.py:49
  178.6 7.9 %collective-permute-start.22 = (bf16[1,32,1024]{2,1,0:T(8,128)(2,1)S(1)}, bf16[1,32,1024]{2,1,0:T(8,128)(2,1)S(1)}, u32[]{:S(2)}, u32[]{:S(2)}) collective-permute-start(bf16[1,32,1024]{2,1,0:T(8,128)(2,1)S(1)} %get-tuple-element.66), channel_id=1, source_target_pairs={{0,12},{1,13},{2,14},{3,15},{4,8},{5,9},{6,10},{7,11},{8,4},{9,5},... | collective-permute-start | bytes 196616 | tf_op jit(solution)/shard_map/ppermute | solution.py:49
  180.7 1.6 copy-start.4
  185.3 19.2 %collective-permute-start.26 = (bf16[256,1024]{1,0:T(8,128)(2,1)}, bf16[256,1024]{1,0:T(8,128)(2,1)S(1)}, u32[]{:S(2)}, u32[]{:S(2)}) collective-permute-start(bf16[256,1024]{1,0:T(8,128)(2,1)} %get-tuple-element.76), channel_id=1, source_target_pairs={{0,2},{1,3},{2,0},{3,1},{4,6},{5,7},{6,4},{7,5},{8,10},{9,11},{10,... | collective-permute-start | bytes 1572872 | tf_op jit(solution)/shard_map/ppermute | solution.py:49
  186.5 17.9 %collective-permute-start.23 = (bf16[4,32,1024]{2,1,0:T(8,128)(2,1)S(1)}, bf16[4,32,1024]{2,1,0:T(8,128)(2,1)S(1)}, u32[]{:S(2)}, u32[]{:S(2)}) collective-permute-start(bf16[4,32,1024]{2,1,0:T(8,128)(2,1)S(1)} %pad_maximum_fusion.1), channel_id=1, source_target_pairs={{0,2},{1,3},{2,0},{3,1},{4,6},{5,7},{6,4},{7,5},{8,10},{9,11},{10,... | collective-permute-start | bytes 786440 | tf_op jit(solution)/shard_map/ppermute | solution.py:49
  204.4 5.0 %collective-permute-start.28 = (bf16[8,32,1024]{2,1,0:T(8,128)(2,1)S(1)}, bf16[8,32,1024]{2,1,0:T(8,128)(2,1)S(1)}, u32[]{:S(2)}, u32[]{:S(2)}) collective-permute-start(bf16[8,32,1024]{2,1,0:T(8,128)(2,1)S(1)} %constant_dynamic-update-slice_fusion.near), channel_id=1, source_target_pairs={{0,1},{1,0},{2,3},{3,2},{4,5},{5,4},{6,7},{7,6},{8,9},{9,8},{10,11... | collective-permute-start | bytes 1572872 | tf_op jit(solution)/shard_map/ppermute | solution.py:49
  206.1 3.3 %copy-start = (f32[512,1024]{1,0:T(8,128)S(1)}, f32[512,1024]{1,0:T(8,128)}, u32[]{:S(2)}) copy-start(f32[512,1024]{1,0:T(8,128)} %master.1) | copy-start | bytes 6291460
  208.4 14.4 %collective-permute-start.27 = (bf16[256,1024]{1,0:T(8,128)(2,1)S(1)}, bf16[256,1024]{1,0:T(8,128)(2,1)S(1)}, u32[]{:S(2)}, u32[]{:S(2)}) collective-permute-start(bf16[256,1024]{1,0:T(8,128)(2,1)S(1)} %get-tuple-element.78), channel_id=1, source_target_pairs={{0,2},{1,3},{2,0},{3,1},{4,6},{5,7},{6,4},{7,5},{8,10},{9,11},{10,... | collective-permute-start | bytes 1572872 | tf_op jit(solution)/shard_map/ppermute | solution.py:49
  (9 other events, 8.4 us)
Sparse Core Ops, SparseCore 0:
  10.1 41.2 all-gather.6
  61.4 36.0 all-gather.10
  99.1 31.9 all-gather.8
  132.6 34.8 all-gather.4

commit v6 on v5

--- a/solution.py
+++ b/solution.py
@@ -166,26 +166,26 @@
     update[0] = (one / first_fix / (jnp.sqrt(two / second_fix) + 1e-08)).astype(bf16)
 
 
-def place(lay, side, rows, low, source, out, sems):
-    height = source.shape[1] // (2 * lay.ring)
+def place(lay, s, side, rows, source, out, sems):
+    index = lax.axis_index("dp")
+    core = index % 2
+    chip = lay.source(index, s) * lay.sides + side
     copies = []
-    for z in range(lay.ring):
-        for core in range(2):
-            k = 2 * z + core
-            start = pl.multiple_of(((z * lay.sides + side) * 2 + core) * rows + low, height)
-            copies.append(
-                pltpu.make_async_copy(
-                    source.at[:, pl.ds(k * height, height)],
-                    out.at[:, pl.ds(start, height)],
-                    sems.at[k],
-                )
-            )
+    for k, owner in enumerate((core, 1 - core)):
+        start = pl.multiple_of((chip * 2 + owner) * rows, rows)
+        copies.append(
+            pltpu.make_async_copy(
+                source.at[:, pl.ds(k * rows, rows)],
+                out.at[:, pl.ds(start, rows)],
+                sems.at[k],
+            )
+        )
     return copies
 
 
-def weight_kernel(lay, rows, low, came, first, *refs):
+def weight_kernel(lay, rows, s, came, first, *refs):
     sides = lay.sides
-    weight, grads, refs = refs[0], refs[1 : 1 + sides], refs[1 + sides :]
+    mine, theirs, grads, refs = refs[0], refs[1], refs[2 : 2 + sides], refs[2 + sides :]
     if came is not None:
         arrived, refs = refs[0], refs[1:]
     if not first:
@@ -197,24 +197,31 @@
     side = (lax.axis_index("dp") // 2) % sides
     copies = []
     if came is not None:
-        copies = place(lay, 1 - side, rows, came, arrived, out, came_sems)
+        copies = place(lay, came, 1 - side, rows, arrived, out, came_sems)
         for copy in copies:
             copy.start()
     for x in reversed(range(sides)):
         target = own if x == 0 else far
-        target[...] = lax.dot_general(
-            grads[x][...], weight[...], (((1,), (1,)), ((), ())), preferred_element_type=f32
-        ).astype(bf16)
-    owns = place(lay, side, rows, low, own, out, sems)
+        for k, piece in enumerate((mine, theirs)):
+            target[:, k * rows : (k + 1) * rows] = lax.dot_general(
+                grads[x][...],
+                piece[...],
+                (((1,), (1,)), ((), ())),
+                preferred_element_type=f32,
+            ).astype(bf16)
+    owns = place(lay, s, side, rows, own, out, sems)
     for copy in owns:
         copy.start()
     for copy in owns + copies:
         copy.wait()
 
 
-def last_kernel(lay, rows, low, arrived, before, out, sems):
+def last_kernel(lay, rows, steps, *refs):
+    arrived, (before, out, sems) = refs[: len(steps)], refs[len(steps) :]
     side = (lax.axis_index("dp") // 2) % lay.sides
-    copies = place(lay, 1 - side, rows, low, arrived, out, sems)
+    copies = []
+    for k, s in enumerate(steps):
+        copies += place(lay, s, 1 - side, rows, arrived[k], out, sems.at[k])
     for copy in copies:
         copy.start()
     for copy in copies:
@@ -268,8 +275,6 @@
         rows, rank = proj_basis.shape
         outs = key_grad.shape[1]
         owned = rank // n
-        height = 128 if rows % 128 == 0 else rows
-        parts = rows // height
 
         plan = [(x, 0, ring) for x in range(min(members, 3))]
         if sides == 2:
@@ -284,52 +289,44 @@
             moved=4 * tokens * ring * rows * members,
         )
 
-        basis = [after(proj_basis, cut[0])]
         acts = list(cut)
+        far_grad = None
         if sides == 2:
             far_grad = swap(key_grad, 2)
             acts[2] = swap(cut[2], 2)
             acts[3] = swap(after(cut[3], far_grad), 3)
             acts[4] = swap(after(cut[4], acts[2]), 3)
+        weight = [master_weight.astype(bf16)]
+        basis = [after(proj_basis, cut[0])]
         for s in range(1, ring):
             value = basis[-1]
             if s == 2 and sides == 2:
                 value = after(value, far_grad)
+            if s == 3:
+                value = after(value, weight[1])
             basis.append(onward(value))
+            if s == 1:
+                weight.append(onward(weight[0]))
         acts[1] = swap(after(cut[1], basis[1]), 1)
         if sides == 2:
             near = swap(jnp.concatenate([key_grad, far_grad], axis=0), 1)
             grads = [key_grad, near[:tokens], far_grad, near[tokens:]]
         else:
             grads = [key_grad, swap(key_grad, 1)]
-
-        weight = master_weight.astype(bf16)
-        groups = None
-        if sides == 2:
-            groups = [
-                [(z * sides + side) * 2 + core for z in range(ring) for core in range(2)]
-                for side in range(sides)
-            ]
-        chunks = []
-        for p in range(parts):
-            chunk = weight[p * height : (p + 1) * height]
-            if p > 0:
-                chunk = after(chunk, basis[min(p + 1, ring - 1)], acts[p + 1])
-            chunks.append(
-                lax.all_gather(chunk, "dp", axis=0, tiled=True, axis_index_groups=groups)
-            )
+        weight.append(onward(after(weight[1], basis[-1])))
 
         side_grads = [key_grad, far_grad] if sides == 2 else [key_grad]
-        state = {"out": None, "waiting": None}
-        wide = 2 * ring * height
-
-        def multiply(p, gate=None):
-            args = [chunks[p] if gate is None else after(chunks[p], gate)] + side_grads
+        state = {"out": None}
+        waiting = []
+
+        def multiply(s, gate=None):
+            args = [weight[s] if gate is None else after(weight[s], gate), swap(weight[s], 1)]
+            args += side_grads
             in_specs = [VMEM] * len(args)
             came = None
-            if state["waiting"] is not None:
-                came = state["waiting"][0]
-                args.append(state["waiting"][1])
+            if len(waiting) > 1:
+                came, block = waiting.pop(0)
+                args.append(block)
                 in_specs.append(VMEM)
             first = state["out"] is None
             if not first:
@@ -337,48 +334,48 @@
                 in_specs.append(HBM)
             shapes, out_specs = [((tokens, width), bf16)], [HBM]
             if sides == 2:
-                shapes.append(((tokens, wide), bf16))
+                shapes.append(((tokens, 2 * rows), bf16))
                 out_specs.append(VMEM)
             result = call(
-                functools.partial(weight_kernel, lay, rows, p * height, came, first),
+                functools.partial(weight_kernel, lay, rows, s, came, first),
                 "weight",
                 shapes,
                 args,
                 in_specs,
                 out_specs,
                 scratch=[
-                    pltpu.VMEM((tokens, wide), bf16),
-                    pltpu.SemaphoreType.DMA((2 * ring,)),
-                    pltpu.SemaphoreType.DMA((2 * ring,)),
+                    pltpu.VMEM((tokens, 2 * rows), bf16),
+                    pltpu.SemaphoreType.DMA((2,)),
+                    pltpu.SemaphoreType.DMA((2,)),
                 ],
-                flops=2 * sides * tokens * wide * outs,
+                flops=4 * sides * tokens * rows * outs,
                 moved=6 * 2**20,
                 input_output_aliases={} if first else {len(args) - 1: 0},
             )
             state["out"] = result[0]
-            state["waiting"] = None
-            return result[1] if sides == 2 else None
-
-        def give_back(p, block, gate=None):
-            if sides == 2:
-                if gate is not None:
-                    block = after(block, gate)
-                state["waiting"] = (p * height, swap(block, 2))
-
-        block = multiply(0)
-        give_back(0, block, acts[-1])
+            return result[1] if sides == 2 else result[0]
+
+        def give_back(s, block, *gates):
+            if sides == 1:
+                return block
+            waiting.append((s, swap(after(block, *gates) if gates else block, 2)))
+            return waiting[-1][1]
+
+        first_block = multiply(0)
 
         total, *gives = call(
             functools.partial(project_kernel, lay, owned, plan),
             "project",
             [((n // 2, owned, outs), f32), ((n // 2, owned, outs), bf16)],
-            [after(acts[0], block if sides == 2 else acts[0])] + acts[1:] + basis + grads,
+            [after(acts[0], first_block)] + acts[1:] + basis + grads,
             scratch=[pltpu.VMEM((rank, outs), f32)],
             flops=2 * tokens * members * rank * (ring * rows + outs),
             moved=12 * 2**20,
         )
 
         for k, (bit, radix) in enumerate(rounds):
+            if bit == members:
+                gives = [after(give, weight[2], block) for give in gives]
             came = [swap(give, j * bit) for j, give in zip(range(1, radix), gives)]
             if k == len(rounds) - 1:
                 break
@@ -391,31 +388,42 @@
                 [total] + came,
                 moved=4 * total.size,
             )
-        if parts > 1:
-            block = multiply(1, total)
-            give_back(1, block)
+            if bit == 1:
+                block = multiply(1, total)
+            if bit == 2:
+                sent = give_back(0, first_block, total)
+                later = give_back(1, block, total)
         owned_rows, square = call(
             functools.partial(square_kernel, len(came)),
             "square",
             [((owned, outs), f32), ((8, 128), f32)],
             [total] + came,
         )
+        square = after(square, sent)
         for bit, radix in reversed(rounds):
             if bit >= members:
                 square = sum([swap(square, j * bit) for j in range(1, radix)], square)
+        if ring > 3:
+            weight.append(onward(after(weight[2], square)))
+        block = multiply(2, owned_rows)
+        square = after(square, later)
         squares = [square] + [swap(square, x) for x in range(1, members)]
         new_first, new_second, update = call(
             functools.partial(moment_kernel, members),
             "moment",
             [((owned, outs), f32), ((owned, outs), f32), ((1, owned, outs), bf16)],
-            squares + [owned_rows, first_moment, second_moment],
-        )
-        if parts > 2:
-            block = multiply(2, update)
-            give_back(2, block)
+            squares + [after(owned_rows, block), first_moment, second_moment],
+        )
+        sent = give_back(2, block, update)
+        if ring > 3:
+            weight[3] = after(weight[3], update)
 
         whole = update
         for bit, radix in reversed(rounds[1:]):
+            if bit >= members and 2 * bit >= n // 2 and ring > 3:
+                whole = after(whole, weight[3])
+            if bit == 2 and sides == 2:
+                whole = after(whole, sent)
             whole = jnp.concatenate(
                 [whole] + [swap(whole, j * bit) for j in range(1, radix)], axis=0
             )
@@ -429,21 +437,21 @@
             moved=8 * 2**20,
         )
 
-        for p in range(3, parts):
-            block = multiply(p, whole)
-            give_back(p, block)
+        for s in range(3, ring):
+            if s > 3:
+                weight.append(onward(weight[s - 1]))
+            give_back(s, multiply(s))
         activation_grad = state["out"]
-        if state["waiting"] is not None:
-            low, arrived = state["waiting"]
+        if waiting:
             (activation_grad,) = call(
-                functools.partial(last_kernel, lay, rows, low),
+                functools.partial(last_kernel, lay, rows, [s for s, block in waiting]),
                 "last",
                 [((tokens, width), bf16)],
-                [arrived, activation_grad],
-                [VMEM, HBM],
+                [block for s, block in waiting] + [activation_grad],
+                [VMEM] * len(waiting) + [HBM],
                 [HBM],
-                scratch=[pltpu.SemaphoreType.DMA((2 * ring,))],
-                input_output_aliases={1: 0},
+                scratch=[pltpu.SemaphoreType.DMA((len(waiting), 2))],
+                input_output_aliases={len(waiting): 0},
             )
         return (activation_grad, new_master, new_first, new_second)
 

time: 230 us -> 191 us (0.83)
  local copies, waits for them, and re-layouts: 17.7 us -> 2.97 us
  between operations: 14.1 us -> 1.01 us
  starting transfers between devices: 52.3 us -> 39.4 us
  waiting for transfers between devices: 121 us -> 129 us
  Pallas kernels: 22.4 us -> 17.6 us
  other arithmetic: 2.83 us -> 0.27 us
    ppermute x3 -> x6, waiting for transfers between devices: 39.6 us -> 59 us  [onward(): return lax.ppermute(value, 'dp', self.forward)]
    unnamed x52 -> x13, local copies, waits for them, and re-layouts: 15.4 us -> 2.88 us
    ppermute x26 -> x30, starting transfers between devices: 40.8 us -> 29.6 us  [swap(): return lax.ppermute(value, 'dp', [(i, i ^ bit) for i in range(self.n)])]
    ppermute x26 -> x30, waiting for transfers between devices: 81 us -> 70.3 us  [swap(): return lax.ppermute(value, 'dp', [(i, i ^ bit) for i in range(self.n)])]
    pallas_call x12, Pallas kernels: 22.4 us -> 17.6 us  [call(): pl.pallas_call(kernel, name=name, out_shape=[jax.ShapeDtypeStruct(shape,...]
    ppermute x3 -> x6, starting transfers between devices: 11.3 us -> 9.88 us  [onward(): return lax.ppermute(value, 'dp', self.forward)]
  transfers between devices with their start and end apart: 33 -> 36, of which waited for: 14 -> 22; matrix products, arithmetic and copies ran while one was open for 1% -> 0% of each run, Pallas kernels for 9% -> 6%
where the time goes in v6:
time: 191 us
  waiting for transfers between devices  129 us (68%)
  starting transfers between devices  39.4 us (21%)
  Pallas kernels  17.6 us (9%)
  local copies, waits for them, and re-layouts  2.97 us (2%)
    ppermute x30, waiting for transfers between devices, swap(): return lax.ppermute(value, 'dp', [(i, i ^ bit) for i in range(self.n)])  70.3 us
    ppermute x6, waiting for transfers between devices, onward(): return lax.ppermute(value, 'dp', self.forward)  59 us
    ppermute x30, starting transfers between devices, swap(): return lax.ppermute(value, 'dp', [(i, i ^ bit) for i in range(self.n)])  29.6 us
    pallas_call x12, Pallas kernels, call(): pl.pallas_call(kernel, name=name, out_shape=[jax.ShapeDtypeStruct(shape,...  17.6 us
    ppermute x6, starting transfers between devices, onward(): return lax.ppermute(value, 'dp', self.forward)  9.88 us
  transfers between devices with their start and end apart: 36, of which 22 were waited for; matrix products, arithmetic and copies ran while one was open for 0% of the time, Pallas kernels for 6%

profile of v6, /device:TPU:0, one launch (start us, length us, event | category | flops | bytes accessed | tf_op | source)
XLA Modules:
  0.0 190.6 jit_solution(14330964863571008520)
XLA Ops:
  0.7 2.3 %copy-done.2 = bf16[256,8192]{1,0:T(8,128)(2,1)S(1)} copy-done((bf16[256,8192]{1,0:T(8,128)(2,1)S(1)}, bf16[256,8192]{1,0:T(8,128)(2,1)}, u32[]{:S(2)}) %copy-start.2) | copy-done | bytes 4194328
  4.0 3.0 %collective-permute-start.1 = (bf16[512,512]{1,0:T(8,128)(2,1)S(1)}, bf16[512,512]{1,0:T(8,128)(2,1)S(1)}, u32[]{:S(2)}, u32[]{:S(2)}) collective-permute-start(bf16[512,512]{1,0:T(8,128)(2,1)S(1)} %copy-done.3), channel_id=1, source_target_pairs={{0,4},{1,5},{2,6},{3,7},{4,12},{5,13},{6,14},{7,15},{12,8},{13,9},... | collective-permute-start | bytes 1572872 | tf_op jit(solution)/shard_map/ppermute | solution.py:52
  7.1 1.5 collective-permute-start.2
  8.7 2.6 %collective-permute-start = (bf16[512,1024]{1,0:T(8,128)(2,1)S(1)}, bf16[512,1024]{1,0:T(8,128)(2,1)S(1)}, u32[]{:S(2)}, u32[]{:S(2)}) collective-permute-start(bf16[512,1024]{1,0:T(8,128)(2,1)S(1)} %convert_element_type.3.refs_0_), channel_id=1, source_target_pairs={{0,4},{1,5},{2,6},{3,7},{4,12},{5,13},{6,14},{7,15},{12,8},{13,9},... | collective-permute-start | bytes 3145736 | tf_op jit(solution)/shard_map/ppermute | solution.py:52
  11.9 8.9 %collective-permute-done.1.refs_6_ = bf16[512,512]{1,0:T(8,128)(2,1)S(1)} collective-permute-done((bf16[512,512]{1,0:T(8,128)(2,1)S(1)}, bf16[512,512]{1,0:T(8,128)(2,1)S(1)}, u32[]{:S(2)}, u32[]{:S(2)}) %collective-permute-start.1) | collective-permute-done | bytes 524320 | tf_op jit(solution)/shard_map/ppermute | solution.py:52
  20.8 1.1 collective-permute-done.2.refs_3_.refs_11_
  21.9 2.6 %collective-permute-start.3 = (bf16[512,512]{1,0:T(8,128)(2,1)S(1)}, bf16[512,512]{1,0:T(8,128)(2,1)S(1)}, u32[]{:S(2)}, u32[]{:S(2)}) collective-permute-start(bf16[512,512]{1,0:T(8,128)(2,1)S(1)} %collective-permute-done.1.refs_6_), channel_id=1, source_target_pairs={{0,4},{1,5},{2,6},{3,7},{4,12},{5,13},{6,14},{7,15},{12,8},{13,9},... | collective-permute-start | bytes 1572872 | tf_op jit(solution)/shard_map/ppermute | solution.py:52
  25.1 28.5 %collective-permute-done.3.refs_7_ = bf16[512,512]{1,0:T(8,128)(2,1)S(1)} collective-permute-done((bf16[512,512]{1,0:T(8,128)(2,1)S(1)}, bf16[512,512]{1,0:T(8,128)(2,1)S(1)}, u32[]{:S(2)}, u32[]{:S(2)}) %collective-permute-start.3) | collective-permute-done | bytes 524320 | tf_op jit(solution)/shard_map/ppermute | solution.py:52
  53.7 1.7 collective-permute-start.9
  55.4 0.8 collective-permute-start.4
  56.2 2.1 %weight.4 = (bf16[256,8192]{1,0:T(8,128)(2,1)}, bf16[256,1024]{1,0:T(8,128)(2,1)S(1)}) custom-call(bf16[512,1024]{1,0:T(8,128)(2,1)S(1)} %convert_element_type.3.refs_0_, bf16[512,1024]{1,0:T(8,128)(2,1)S(1)} %collective-permute-done.6.refs_1_, bf16[256,1024]{1,0:T(8,128)(2,1)S(1)} %copy-done.1, bf16[256,1024]{1,0:T(8,128)(2,1)S(1)} %collective-permute-done.2.refs_3_.refs_11_), custom_call_target="tpu_custom_call" | custom-call | flops 1073741824 | bytes 6291456 | tf_op jit(solution)/shard_map/weight/pallas_call | solution.py:255
  58.4 9.3 %collective-permute-done.9.refs_3_ = bf16[256,1024]{1,0:T(8,128)(2,1)S(1)} collective-permute-done((bf16[256,1024]{1,0:T(8,128)(2,1)S(1)}, bf16[256,1024]{1,0:T(8,128)(2,1)S(1)}, u32[]{:S(2)}, u32[]{:S(2)}) %collective-permute-start.9) | collective-permute-done | bytes 524320 | tf_op jit(solution)/shard_map/ppermute | solution.py:49
  67.7 2.5 %collective-permute-done.4.refs_8_ = bf16[512,512]{1,0:T(8,128)(2,1)S(1)} collective-permute-done((bf16[512,512]{1,0:T(8,128)(2,1)S(1)}, bf16[512,512]{1,0:T(8,128)(2,1)S(1)}, u32[]{:S(2)}, u32[]{:S(2)}) %collective-permute-start.4) | collective-permute-done | bytes 524320 | tf_op jit(solution)/shard_map/ppermute | solution.py:52
  70.1 8.4 %collective-permute-done.10.refs_4_ = bf16[256,1024]{1,0:T(8,128)(2,1)S(1)} collective-permute-done((bf16[256,1024]{1,0:T(8,128)(2,1)S(1)}, bf16[256,1024]{1,0:T(8,128)(2,1)S(1)}, u32[]{:S(2)}, u32[]{:S(2)}) %collective-permute-start.10) | collective-permute-done | bytes 524320 | tf_op jit(solution)/shard_map/ppermute | solution.py:49
  78.5 4.3 %project.1 = (f32[8,32,1024]{2,1,0:T(8,128)S(1)}, bf16[8,32,1024]{2,1,0:T(8,128)(2,1)S(1)}) custom-call(bf16[256,2048]{1,0:T(8,128)(2,1)S(1)} %get-tuple-element.59.refs_0_, bf16[256,2048]{1,0:T(8,128)(2,1)S(1)} %collective-permute-done.7.refs_1_, bf16[256,2048]{1,0:T(8,128)(2,1)S(1)} %collective-permute-done.8.refs_2_, ...), custom_call_target="tpu_custom_call" | custom-call | flops 3221225472 | bytes 12582912 | tf_op jit(solution)/shard_map/project/pallas_call | solution.py:255
  83.5 0.8 collective-permute-start.5
  85.0 1.7 collective-permute-start.13
  86.7 7.0 %collective-permute-done.13.refs_1_ = bf16[4,32,1024]{2,1,0:T(8,128)(2,1)S(1)} collective-permute-done((bf16[4,32,1024]{2,1,0:T(8,128)(2,1)S(1)}, bf16[4,32,1024]{2,1,0:T(8,128)(2,1)S(1)}, u32[]{:S(2)}, u32[]{:S(2)}) %collective-permute-start.13) | collective-permute-done | bytes 262176 | tf_op jit(solution)/shard_map/ppermute | solution.py:49
  93.7 1.6 collective-permute-start.19
  95.4 2.1 %weight.5 = (bf16[256,8192]{1,0:T(8,128)(2,1)}, bf16[256,1024]{1,0:T(8,128)(2,1)S(1)}) custom-call(bf16[512,1024]{1,0:T(8,128)(2,1)S(1)} %collective-permute-done.refs_0_, bf16[512,1024]{1,0:T(8,128)(2,1)S(1)} %collective-permute-done.14.refs_1_, bf16[256,1024]{1,0:T(8,128)(2,1)S(1)} %copy-done.1, ...), custom_call_target="tpu_custom_call", output_to_operand_aliasing={{0}: (4, {})} | custom-call | flops 1073741824 | bytes 6291456 | tf_op jit(solution)/shard_map/weight/pallas_call | solution.py:255
  97.5 12.4 %collective-permute-done.5.refs_0_ = bf16[512,1024]{1,0:T(8,128)(2,1)S(1)} collective-permute-done((bf16[512,1024]{1,0:T(8,128)(2,1)S(1)}, bf16[512,1024]{1,0:T(8,128)(2,1)S(1)}, u32[]{:S(2)}, u32[]{:S(2)}) %collective-permute-start.5) | collective-permute-done | bytes 1048608 | tf_op jit(solution)/shard_map/ppermute | solution.py:52
  109.9 3.7 %collective-permute-start.17 = (bf16[1,32,1024]{2,1,0:T(8,128)(2,1)S(1)}, bf16[1,32,1024]{2,1,0:T(8,128)(2,1)S(1)}, u32[]{:S(2)}, u32[]{:S(2)}) collective-permute-start(bf16[1,32,1024]{2,1,0:T(8,128)(2,1)S(1)} %get-tuple-element.80), channel_id=1, source_target_pairs={{0,12},{1,13},{2,14},{3,15},{4,8},{5,9},{6,10},{7,11},{8,4},{9,5},... | collective-permute-start | bytes 196616 | tf_op jit(solution)/shard_map/ppermute | solution.py:49
  114.3 2.1 %collective-permute-done.17.refs_3_ = bf16[1,32,1024]{2,1,0:T(8,128)(2,1)S(1)} collective-permute-done((bf16[1,32,1024]{2,1,0:T(8,128)(2,1)S(1)}, bf16[1,32,1024]{2,1,0:T(8,128)(2,1)S(1)}, u32[]{:S(2)}, u32[]{:S(2)}) %collective-permute-start.17) | collective-permute-done | bytes 65568 | tf_op jit(solution)/shard_map/ppermute | solution.py:49
  116.4 2.4 %collective-permute-done.16.refs_2_ = bf16[1,32,1024]{2,1,0:T(8,128)(2,1)S(1)} collective-permute-done((bf16[1,32,1024]{2,1,0:T(8,128)(2,1)S(1)}, bf16[1,32,1024]{2,1,0:T(8,128)(2,1)S(1)}, u32[]{:S(2)}, u32[]{:S(2)}) %collective-permute-start.16) | collective-permute-done | bytes 65568 | tf_op jit(solution)/shard_map/ppermute | solution.py:49
  119.4 0.9 collective-permute-start.20
  120.3 1.7 collective-permute-start.21
  121.9 1.9 collective-permute-start.22
  123.8 0.9 collective-permute-done.21
  124.8 2.6 %collective-permute-done.22 = f32[8,128]{1,0:T(8,128)S(1)} collective-permute-done((f32[8,128]{1,0:T(8,128)S(1)}, f32[8,128]{1,0:T(8,128)S(1)}, u32[]{:S(2)}, u32[]{:S(2)}) %collective-permute-start.22) | collective-permute-done | bytes 4128 | tf_op jit(solution)/shard_map/ppermute | solution.py:49
  127.3 1.6 collective-permute-start.23
  128.9 9.6 %collective-permute-done.23.refs_4_ = bf16[256,1024]{1,0:T(8,128)(2,1)S(1)} collective-permute-done((bf16[256,1024]{1,0:T(8,128)(2,1)S(1)}, bf16[256,1024]{1,0:T(8,128)(2,1)S(1)}, u32[]{:S(2)}, u32[]{:S(2)}) %collective-permute-start.23) | collective-permute-done | bytes 524320 | tf_op jit(solution)/shard_map/ppermute | solution.py:49
  138.5 1.5 collective-permute-start.25
  140.4 2.1 %weight.6 = (bf16[256,8192]{1,0:T(8,128)(2,1)}, bf16[256,1024]{1,0:T(8,128)(2,1)S(1)}) custom-call(bf16[512,1024]{1,0:T(8,128)(2,1)S(1)} %collective-permute-done.5.refs_0_, bf16[512,1024]{1,0:T(8,128)(2,1)S(1)} %collective-permute-done.18.refs_1_, bf16[256,1024]{1,0:T(8,128)(2,1)S(1)} %copy-done.1, ...), custom_call_target="tpu_custom_call", output_to_operand_aliasing={{0}: (5, {})} | custom-call | flops 1073741824 | bytes 6291456 | tf_op jit(solution)/shard_map/weight/pallas_call | solution.py:255
  143.0 0.8 moment.1
  143.8 6.7 %collective-permute-done.28.refs_0_ = bf16[512,1024]{1,0:T(8,128)(2,1)S(1)} collective-permute-done((bf16[512,1024]{1,0:T(8,128)(2,1)S(1)}, bf16[512,1024]{1,0:T(8,128)(2,1)S(1)}, u32[]{:S(2)}, u32[]{:S(2)}) %collective-permute-start.28) | collective-permute-done | bytes 1048608 | tf_op jit(solution)/shard_map/ppermute | solution.py:52
  150.6 1.5 collective-permute-start.27
  152.1 2.5 %collective-permute-start.32 = (bf16[1,32,1024]{2,1,0:T(8,128)(2,1)S(1)}, bf16[1,32,1024]{2,1,0:T(8,128)(2,1)S(1)}, u32[]{:S(2)}, u32[]{:S(2)}) collective-permute-start(bf16[1,32,1024]{2,1,0:T(8,128)(2,1)S(1)} %get-tuple-element.98), channel_id=1, source_target_pairs={{0,8},{1,9},{2,10},{3,11},{4,12},{5,13},{6,14},{7,15},{8,0},{9,1},... | collective-permute-start | bytes 196616 | tf_op jit(solution)/shard_map/ppermute | solution.py:49
  154.6 1.9 collective-permute-start.33
  156.5 0.9 collective-permute-done.31
  157.3 3.4 %collective-permute-done.32 = bf16[1,32,1024]{2,1,0:T(8,128)(2,1)S(1)} collective-permute-done((bf16[1,32,1024]{2,1,0:T(8,128)(2,1)S(1)}, bf16[1,32,1024]{2,1,0:T(8,128)(2,1)S(1)}, u32[]{:S(2)}, u32[]{:S(2)}) %collective-permute-start.32) | collective-permute-done | bytes 65568 | tf_op jit(solution)/shard_map/ppermute | solution.py:49
  160.8 4.1 %collective-permute-done.27.refs_0_ = bf16[256,1024]{1,0:T(8,128)(2,1)S(1)} collective-permute-done((bf16[256,1024]{1,0:T(8,128)(2,1)S(1)}, bf16[256,1024]{1,0:T(8,128)(2,1)S(1)}, u32[]{:S(2)}, u32[]{:S(2)}) %collective-permute-start.27) | collective-permute-done | bytes 524320 | tf_op jit(solution)/shard_map/ppermute | solution.py:49
  164.9 1.5 collective-permute-start.34
  166.4 6.4 %collective-permute-done.34 = bf16[4,32,1024]{2,1,0:T(8,128)(2,1)S(1)} collective-permute-done((bf16[4,32,1024]{2,1,0:T(8,128)(2,1)S(1)}, bf16[4,32,1024]{2,1,0:T(8,128)(2,1)S(1)}, u32[]{:S(2)}, u32[]{:S(2)}) %collective-permute-start.34) | collective-permute-done | bytes 262176 | tf_op jit(solution)/shard_map/ppermute | solution.py:49
  172.9 2.1 %weight.7 = (bf16[256,8192]{1,0:T(8,128)(2,1)}, bf16[256,1024]{1,0:T(8,128)(2,1)S(1)}) custom-call(bf16[512,1024]{1,0:T(8,128)(2,1)S(1)} %collective-permute-done.28.refs_0_, bf16[512,1024]{1,0:T(8,128)(2,1)S(1)} %collective-permute-done.29.refs_1_, bf16[256,1024]{1,0:T(8,128)(2,1)S(1)} %copy-done.1, ...), custom_call_target="tpu_custom_call", output_to_operand_aliasing={{0}: (5, {})} | custom-call | flops 1073741824 | bytes 6291456 | tf_op jit(solution)/shard_map/weight/pallas_call | solution.py:255
  175.1 1.6 collective-permute-start.30
  176.7 2.2 %back.1 = f32[512,1024]{1,0:T(8,128)} custom-call(bf16[512,512]{1,0:T(8,128)(2,1)S(1)} %copy-done.3, bf16[8,32,1024]{2,1,0:T(8,128)(2,1)S(1)} %constant_dynamic-update-slice_fusion.near, bf16[8,32,1024]{2,1,0:T(8,128)(2,1)S(1)} %collective-permute-done.35.other, f32[512,1024]{1,0:T(8,128)S(1)} %copy-done), custom_call_target="tpu_custom_call" | custom-call | flops 536870912 | bytes 8388608 | tf_op jit(solution)/shard_map/back/pallas_call | solution.py:255
  178.9 10.6 %collective-permute-done.30.refs_1_ = bf16[256,1024]{1,0:T(8,128)(2,1)S(1)} collective-permute-done((bf16[256,1024]{1,0:T(8,128)(2,1)S(1)}, bf16[256,1024]{1,0:T(8,128)(2,1)S(1)}, u32[]{:S(2)}, u32[]{:S(2)}) %collective-permute-start.30) | collective-permute-done | bytes 524320 | tf_op jit(solution)/shard_map/ppermute | solution.py:49
  189.5 1.0 last.1
  (55 shorter events, 6.2 us)
Async XLA Ops:
  0.6 6.4 %copy-start.1 = (bf16[256,1024]{1,0:T(8,128)(2,1)S(1)}, bf16[256,1024]{1,0:T(8,128)(2,1)}, u32[]{:S(2)}) copy-start(bf16[256,1024]{1,0:T(8,128)(2,1)} %refs_2_.7) | copy-start | bytes 1572868
  0.6 7.9 %copy-start = (f32[512,1024]{1,0:T(8,128)S(1)}, f32[512,1024]{1,0:T(8,128)}, u32[]{:S(2)}) copy-start(f32[512,1024]{1,0:T(8,128)} %master.1) | copy-start | bytes 6291460
  0.7 2.3 %copy-start.2 = (bf16[256,8192]{1,0:T(8,128)(2,1)S(1)}, bf16[256,8192]{1,0:T(8,128)(2,1)}, u32[]{:S(2)}) copy-start(bf16[256,8192]{1,0:T(8,128)(2,1)} %act.1) | copy-start | bytes 12582916
  3.0 1.0 copy-start.3
  4.0 16.8 %collective-permute-start.1 = (bf16[512,512]{1,0:T(8,128)(2,1)S(1)}, bf16[512,512]{1,0:T(8,128)(2,1)S(1)}, u32[]{:S(2)}, u32[]{:S(2)}) collective-permute-start(bf16[512,512]{1,0:T(8,128)(2,1)S(1)} %copy-done.3), channel_id=1, source_target_pairs={{0,4},{1,5},{2,6},{3,7},{4,12},{5,13},{6,14},{7,15},{12,8},{13,9},... | collective-permute-start | bytes 1572872 | tf_op jit(solution)/shard_map/ppermute | solution.py:52
  7.1 14.8 %collective-permute-start.2 = (bf16[256,1024]{1,0:T(8,128)(2,1)S(1)}, bf16[256,1024]{1,0:T(8,128)(2,1)S(1)}, u32[]{:S(2)}, u32[]{:S(2)}) collective-permute-start(bf16[256,1024]{1,0:T(8,128)(2,1)S(1)} %copy-done.1), channel_id=1, source_target_pairs={{0,2},{1,3},{2,0},{3,1},{4,6},{5,7},{6,4},{7,5},{8,10},{9,11},{10,... | collective-permute-start | bytes 1572872 | tf_op jit(solution)/shard_map/ppermute | solution.py:49
  8.7 45.0 %collective-permute-start = (bf16[512,1024]{1,0:T(8,128)(2,1)S(1)}, bf16[512,1024]{1,0:T(8,128)(2,1)S(1)}, u32[]{:S(2)}, u32[]{:S(2)}) collective-permute-start(bf16[512,1024]{1,0:T(8,128)(2,1)S(1)} %convert_element_type.3.refs_0_), channel_id=1, source_target_pairs={{0,4},{1,5},{2,6},{3,7},{4,12},{5,13},{6,14},{7,15},{12,8},{13,9},... | collective-permute-start | bytes 3145736 | tf_op jit(solution)/shard_map/ppermute | solution.py:52
  11.4 44.0 %collective-permute-start.8 = (bf16[256,2048]{1,0:T(8,128)(2,1)S(1)}, bf16[256,2048]{1,0:T(8,128)(2,1)S(1)}, u32[]{:S(2)}, u32[]{:S(2)}) collective-permute-start(bf16[256,2048]{1,0:T(8,128)(2,1)S(1)} %get-tuple-element.62), channel_id=1, source_target_pairs={{0,2},{1,3},{2,0},{3,1},{4,6},{5,7},{6,4},{7,5},{8,10},{9,11},{10,... | collective-permute-start | bytes 3145736 | tf_op jit(solution)/shard_map/ppermute | solution.py:49
  21.9 31.8 %collective-permute-start.3 = (bf16[512,512]{1,0:T(8,128)(2,1)S(1)}, bf16[512,512]{1,0:T(8,128)(2,1)S(1)}, u32[]{:S(2)}, u32[]{:S(2)}) collective-permute-start(bf16[512,512]{1,0:T(8,128)(2,1)S(1)} %collective-permute-done.1.refs_6_), channel_id=1, source_target_pairs={{0,4},{1,5},{2,6},{3,7},{4,12},{5,13},{6,14},{7,15},{12,8},{13,9},... | collective-permute-start | bytes 1572872 | tf_op jit(solution)/shard_map/ppermute | solution.py:52
  24.5 31.7 %collective-permute-start.6 = (bf16[512,1024]{1,0:T(8,128)(2,1)S(1)}, bf16[512,1024]{1,0:T(8,128)(2,1)S(1)}, u32[]{:S(2)}, u32[]{:S(2)}) collective-permute-start(bf16[512,1024]{1,0:T(8,128)(2,1)S(1)} %convert_element_type.3.refs_0_), channel_id=1, source_target_pairs={{0,1},{1,0},{2,3},{3,2},{4,5},{5,4},{6,7},{7,6},{8,9},{9,8},{10,11... | collective-permute-start | bytes 3145736 | tf_op jit(solution)/shard_map/ppermute | solution.py:49
  24.6 33.7 %collective-permute-start.11 = (bf16[512,1024]{1,0:T(8,128)(2,1)S(1)}, bf16[512,1024]{1,0:T(8,128)(2,1)S(1)}, u32[]{:S(2)}, u32[]{:S(2)}) collective-permute-start(bf16[512,1024]{1,0:T(8,128)(2,1)S(1)} %pad_maximum_fusion), channel_id=1, source_target_pairs={{0,1},{1,0},{2,3},{3,2},{4,5},{5,4},{6,7},{7,6},{8,9},{9,8},{10,11... | collective-permute-start | bytes 3145736 | tf_op jit(solution)/shard_map/ppermute | solution.py:49
  53.7 16.4 %collective-permute-start.7 = (bf16[256,2048]{1,0:T(8,128)(2,1)S(1)}, bf16[256,2048]{1,0:T(8,128)(2,1)S(1)}, u32[]{:S(2)}, u32[]{:S(2)}) collective-permute-start(bf16[256,2048]{1,0:T(8,128)(2,1)S(1)} %get-tuple-element.61), channel_id=1, source_target_pairs={{0,1},{1,0},{2,3},{3,2},{4,5},{5,4},{6,7},{7,6},{8,9},{9,8},{10,11... | collective-permute-start | bytes 3145736 | tf_op jit(solution)/shard_map/ppermute | solution.py:49
  53.7 14.0 %collective-permute-start.9 = (bf16[256,1024]{1,0:T(8,128)(2,1)S(1)}, bf16[256,1024]{1,0:T(8,128)(2,1)S(1)}, u32[]{:S(2)}, u32[]{:S(2)}) collective-permute-start(bf16[256,1024]{1,0:T(8,128)(2,1)S(1)} %get-tuple-element.64), channel_id=1, source_target_pairs={{0,3},{1,2},{2,1},{3,0},{4,7},{5,6},{6,5},{7,4},{8,11},{9,10},{10,... | collective-permute-start | bytes 1572872 | tf_op jit(solution)/shard_map/ppermute | solution.py:49
  55.4 14.7 %collective-permute-start.4 = (bf16[512,512]{1,0:T(8,128)(2,1)S(1)}, bf16[512,512]{1,0:T(8,128)(2,1)S(1)}, u32[]{:S(2)}, u32[]{:S(2)}) collective-permute-start(bf16[512,512]{1,0:T(8,128)(2,1)S(1)} %collective-permute-done.3.refs_7_), channel_id=1, source_target_pairs={{0,4},{1,5},{2,6},{3,7},{4,12},{5,13},{6,14},{7,15},{12,8},{13,9},... | collective-permute-start | bytes 1572872 | tf_op jit(solution)/shard_map/ppermute | solution.py:52
  56.2 22.3 %collective-permute-start.10 = (bf16[256,1024]{1,0:T(8,128)(2,1)S(1)}, bf16[256,1024]{1,0:T(8,128)(2,1)S(1)}, u32[]{:S(2)}, u32[]{:S(2)}) collective-permute-start(bf16[256,1024]{1,0:T(8,128)(2,1)S(1)} %get-tuple-element.66), channel_id=1, source_target_pairs={{0,3},{1,2},{2,1},{3,0},{4,7},{5,6},{6,5},{7,4},{8,11},{9,10},{10,... | collective-permute-start | bytes 1572872 | tf_op jit(solution)/shard_map/ppermute | solution.py:49
  82.8 2.1 %collective-permute-start.12 = (bf16[8,32,1024]{2,1,0:T(8,128)(2,1)S(1)}, bf16[8,32,1024]{2,1,0:T(8,128)(2,1)S(1)}, u32[]{:S(2)}, u32[]{:S(2)}) collective-permute-start(bf16[8,32,1024]{2,1,0:T(8,128)(2,1)S(1)} %get-tuple-element.68), channel_id=1, source_target_pairs={{0,1},{1,0},{2,3},{3,2},{4,5},{5,4},{6,7},{7,6},{8,9},{9,8},{10,11... | collective-permute-start | bytes 1572872 | tf_op jit(solution)/shard_map/ppermute | solution.py:49
  83.4 12.0 %collective-permute-start.14 = (bf16[512,1024]{1,0:T(8,128)(2,1)S(1)}, bf16[512,1024]{1,0:T(8,128)(2,1)S(1)}, u32[]{:S(2)}, u32[]{:S(2)}) collective-permute-start(bf16[512,1024]{1,0:T(8,128)(2,1)S(1)} %collective-permute-done.refs_0_), channel_id=1, source_target_pairs={{0,1},{1,0},{2,3},{3,2},{4,5},{5,4},{6,7},{7,6},{8,9},{9,8},{10,11... | collective-permute-start | bytes 3145736 | tf_op jit(solution)/shard_map/ppermute | solution.py:49
  83.5 26.4 %collective-permute-start.5 = (bf16[512,1024]{1,0:T(8,128)(2,1)S(1)}, bf16[512,1024]{1,0:T(8,128)(2,1)S(1)}, u32[]{:S(2)}, u32[]{:S(2)}) collective-permute-start(bf16[512,1024]{1,0:T(8,128)(2,1)S(1)} %collective-permute-done.refs_0_), channel_id=1, source_target_pairs={{0,4},{1,5},{2,6},{3,7},{4,12},{5,13},{6,14},{7,15},{12,8},{13,9},... | collective-permute-start | bytes 3145736 | tf_op jit(solution)/shard_map/ppermute | solution.py:52
  85.0 8.7 %collective-permute-start.13 = (bf16[4,32,1024]{2,1,0:T(8,128)(2,1)S(1)}, bf16[4,32,1024]{2,1,0:T(8,128)(2,1)S(1)}, u32[]{:S(2)}, u32[]{:S(2)}) collective-permute-start(bf16[4,32,1024]{2,1,0:T(8,128)(2,1)S(1)} %get-tuple-element.70), channel_id=1, source_target_pairs={{0,2},{1,3},{2,0},{3,1},{4,6},{5,7},{6,4},{7,5},{8,10},{9,11},{10,... | collective-permute-start | bytes 786440 | tf_op jit(solution)/shard_map/ppermute | solution.py:49
  93.7 25.6 %collective-permute-start.19 = (bf16[256,1024]{1,0:T(8,128)(2,1)S(1)}, bf16[256,1024]{1,0:T(8,128)(2,1)S(1)}, u32[]{:S(2)}, u32[]{:S(2)}) collective-permute-start(bf16[256,1024]{1,0:T(8,128)(2,1)S(1)} %get-tuple-element.83), channel_id=1, source_target_pairs={{0,2},{1,3},{2,0},{3,1},{4,6},{5,7},{6,4},{7,5},{8,10},{9,11},{10,... | collective-permute-start | bytes 1572872 | tf_op jit(solution)/shard_map/ppermute | solution.py:49
  97.5 45.6 %copy-start.4 = (f32[32,1024]{1,0:T(8,128)S(1)}, f32[32,1024]{1,0:T(8,128)}, u32[]{:S(2)}) copy-start(f32[32,1024]{1,0:T(8,128)} %refs_5_.2) | copy-start | bytes 393220
  97.5 45.6 %copy-start.5 = (f32[32,1024]{1,0:T(8,128)S(1)}, f32[32,1024]{1,0:T(8,128)}, u32[]{:S(2)}) copy-start(f32[32,1024]{1,0:T(8,128)} %refs_6_.1) | copy-start | bytes 393220
  109.9 6.5 %collective-permute-start.17 = (bf16[1,32,1024]{2,1,0:T(8,128)(2,1)S(1)}, bf16[1,32,1024]{2,1,0:T(8,128)(2,1)S(1)}, u32[]{:S(2)}, u32[]{:S(2)}) collective-permute-start(bf16[1,32,1024]{2,1,0:T(8,128)(2,1)S(1)} %get-tuple-element.80), channel_id=1, source_target_pairs={{0,12},{1,13},{2,14},{3,15},{4,8},{5,9},{6,10},{7,11},{8,4},{9,5},... | collective-permute-start | bytes 196616 | tf_op jit(solution)/shard_map/ppermute | solution.py:49
  113.5 5.2 %collective-permute-start.16 = (bf16[1,32,1024]{2,1,0:T(8,128)(2,1)S(1)}, bf16[1,32,1024]{2,1,0:T(8,128)(2,1)S(1)}, u32[]{:S(2)}, u32[]{:S(2)}) collective-permute-start(bf16[1,32,1024]{2,1,0:T(8,128)(2,1)S(1)} %get-tuple-element.78), channel_id=1, source_target_pairs={{0,8},{1,9},{2,10},{3,11},{4,12},{5,13},{6,14},{7,15},{8,0},{9,1},... | collective-permute-start | bytes 196616 | tf_op jit(solution)/shard_map/ppermute | solution.py:49
  113.5 5.6 %collective-permute-start.15 = (bf16[1,32,1024]{2,1,0:T(8,128)(2,1)S(1)}, bf16[1,32,1024]{2,1,0:T(8,128)(2,1)S(1)}, u32[]{:S(2)}, u32[]{:S(2)}) collective-permute-start(bf16[1,32,1024]{2,1,0:T(8,128)(2,1)S(1)} %get-tuple-element.76), channel_id=1, source_target_pairs={{0,4},{1,5},{2,6},{3,7},{4,0},{5,1},{6,2},{7,3},{8,12},{9,13},{10,... | collective-permute-start | bytes 196616 | tf_op jit(solution)/shard_map/ppermute | solution.py:49
  119.4 4.5 %collective-permute-start.20 = (f32[8,128]{1,0:T(8,128)S(1)}, f32[8,128]{1,0:T(8,128)S(1)}, u32[]{:S(2)}, u32[]{:S(2)}) collective-permute-start(f32[8,128]{1,0:T(8,128)S(1)} %get-tuple-element.87), channel_id=1, source_target_pairs={{0,4},{1,5},{2,6},{3,7},{4,0},{5,1},{6,2},{7,3},{8,12},{9,13},{10,... | collective-permute-start | bytes 12296 | tf_op jit(solution)/shard_map/ppermute | solution.py:49
  120.3 4.5 %collective-permute-start.21 = (f32[8,128]{1,0:T(8,128)S(1)}, f32[8,128]{1,0:T(8,128)S(1)}, u32[]{:S(2)}, u32[]{:S(2)}) collective-permute-start(f32[8,128]{1,0:T(8,128)S(1)} %get-tuple-element.87), channel_id=1, source_target_pairs={{0,8},{1,9},{2,10},{3,11},{4,12},{5,13},{6,14},{7,15},{8,0},{9,1},... | collective-permute-start | bytes 12296 | tf_op jit(solution)/shard_map/ppermute | solution.py:49
  121.9 5.4 %collective-permute-start.22 = (f32[8,128]{1,0:T(8,128)S(1)}, f32[8,128]{1,0:T(8,128)S(1)}, u32[]{:S(2)}, u32[]{:S(2)}) collective-permute-start(f32[8,128]{1,0:T(8,128)S(1)} %get-tuple-element.87), channel_id=1, source_target_pairs={{0,12},{1,13},{2,14},{3,15},{4,8},{5,9},{6,10},{7,11},{8,4},{9,5},... | collective-permute-start | bytes 12296 | tf_op jit(solution)/shard_map/ppermute | solution.py:49
  123.8 16.5 %collective-permute-start.18 = (bf16[512,1024]{1,0:T(8,128)(2,1)S(1)}, bf16[512,1024]{1,0:T(8,128)(2,1)S(1)}, u32[]{:S(2)}, u32[]{:S(2)}) collective-permute-start(bf16[512,1024]{1,0:T(8,128)(2,1)S(1)} %collective-permute-done.5.refs_0_), channel_id=1, source_target_pairs={{0,1},{1,0},{2,3},{3,2},{4,5},{5,4},{6,7},{7,6},{8,9},{9,8},{10,11... | collective-permute-start | bytes 3145736 | tf_op jit(solution)/shard_map/ppermute | solution.py:49
  127.3 23.2 %collective-permute-start.28 = (bf16[512,1024]{1,0:T(8,128)(2,1)S(1)}, bf16[512,1024]{1,0:T(8,128)(2,1)S(1)}, u32[]{:S(2)}, u32[]{:S(2)}) collective-permute-start(bf16[512,1024]{1,0:T(8,128)(2,1)S(1)} %collective-permute-done.5.refs_0_), channel_id=1, source_target_pairs={{0,4},{1,5},{2,6},{3,7},{4,12},{5,13},{6,14},{7,15},{12,8},{13,9},... | collective-permute-start | bytes 3145736 | tf_op jit(solution)/shard_map/ppermute | solution.py:52
  127.3 11.2 %collective-permute-start.23 = (bf16[256,1024]{1,0:T(8,128)(2,1)S(1)}, bf16[256,1024]{1,0:T(8,128)(2,1)S(1)}, u32[]{:S(2)}, u32[]{:S(2)}) collective-permute-start(bf16[256,1024]{1,0:T(8,128)(2,1)S(1)} %get-tuple-element.88), channel_id=1, source_target_pairs={{0,2},{1,3},{2,0},{3,1},{4,6},{5,7},{6,4},{7,5},{8,10},{9,11},{10,... | collective-permute-start | bytes 1572872 | tf_op jit(solution)/shard_map/ppermute | solution.py:49
  138.5 4.0 %collective-permute-start.24 = (f32[8,128]{1,0:T(8,128)S(1)}, f32[8,128]{1,0:T(8,128)S(1)}, u32[]{:S(2)}, u32[]{:S(2)}) collective-permute-start(f32[8,128]{1,0:T(8,128)S(1)} %add_add_fusion.refs_0_), channel_id=1, source_target_pairs={{0,1},{1,0},{2,3},{3,2},{4,5},{5,4},{6,7},{7,6},{8,9},{9,8},{10,11... | collective-permute-start | bytes 12296 | tf_op jit(solution)/shard_map/ppermute | solution.py:49
  138.5 4.0 %collective-permute-start.25 = (f32[8,128]{1,0:T(8,128)S(1)}, f32[8,128]{1,0:T(8,128)S(1)}, u32[]{:S(2)}, u32[]{:S(2)}) collective-permute-start(f32[8,128]{1,0:T(8,128)S(1)} %add_add_fusion.refs_0_), channel_id=1, source_target_pairs={{0,2},{1,3},{2,0},{3,1},{4,6},{5,7},{6,4},{7,5},{8,10},{9,11},{10,... | collective-permute-start | bytes 12296 | tf_op jit(solution)/shard_map/ppermute | solution.py:49
  140.0 3.0 %collective-permute-start.26 = (f32[8,128]{1,0:T(8,128)S(1)}, f32[8,128]{1,0:T(8,128)S(1)}, u32[]{:S(2)}, u32[]{:S(2)}) collective-permute-start(f32[8,128]{1,0:T(8,128)S(1)} %add_add_fusion.refs_0_), channel_id=1, source_target_pairs={{0,3},{1,2},{2,1},{3,0},{4,7},{5,6},{6,5},{7,4},{8,11},{9,10},{10,... | collective-permute-start | bytes 12296 | tf_op jit(solution)/shard_map/ppermute | solution.py:49
  150.5 22.4 %collective-permute-start.29 = (bf16[512,1024]{1,0:T(8,128)(2,1)S(1)}, bf16[512,1024]{1,0:T(8,128)(2,1)S(1)}, u32[]{:S(2)}, u32[]{:S(2)}) collective-permute-start(bf16[512,1024]{1,0:T(8,128)(2,1)S(1)} %collective-permute-done.28.refs_0_), channel_id=1, source_target_pairs={{0,1},{1,0},{2,3},{3,2},{4,5},{5,4},{6,7},{7,6},{8,9},{9,8},{10,11... | collective-permute-start | bytes 3145736 | tf_op jit(solution)/shard_map/ppermute | solution.py:49
  150.6 14.3 %collective-permute-start.27 = (bf16[256,1024]{1,0:T(8,128)(2,1)S(1)}, bf16[256,1024]{1,0:T(8,128)(2,1)S(1)}, u32[]{:S(2)}, u32[]{:S(2)}) collective-permute-start(bf16[256,1024]{1,0:T(8,128)(2,1)S(1)} %get-tuple-element.92), channel_id=1, source_target_pairs={{0,2},{1,3},{2,0},{3,1},{4,6},{5,7},{6,4},{7,5},{8,10},{9,11},{10,... | collective-permute-start | bytes 1572872 | tf_op jit(solution)/shard_map/ppermute | solution.py:49
  152.1 5.2 %collective-permute-start.31 = (bf16[1,32,1024]{2,1,0:T(8,128)(2,1)S(1)}, bf16[1,32,1024]{2,1,0:T(8,128)(2,1)S(1)}, u32[]{:S(2)}, u32[]{:S(2)}) collective-permute-start(bf16[1,32,1024]{2,1,0:T(8,128)(2,1)S(1)} %get-tuple-element.98), channel_id=1, source_target_pairs={{0,4},{1,5},{2,6},{3,7},{4,0},{5,1},{6,2},{7,3},{8,12},{9,13},{10,... | collective-permute-start | bytes 196616 | tf_op jit(solution)/shard_map/ppermute | solution.py:49
  152.1 8.7 %collective-permute-start.32 = (bf16[1,32,1024]{2,1,0:T(8,128)(2,1)S(1)}, bf16[1,32,1024]{2,1,0:T(8,128)(2,1)S(1)}, u32[]{:S(2)}, u32[]{:S(2)}) collective-permute-start(bf16[1,32,1024]{2,1,0:T(8,128)(2,1)S(1)} %get-tuple-element.98), channel_id=1, source_target_pairs={{0,8},{1,9},{2,10},{3,11},{4,12},{5,13},{6,14},{7,15},{8,0},{9,1},... | collective-permute-start | bytes 196616 | tf_op jit(solution)/shard_map/ppermute | solution.py:49
  154.6 6.2 %collective-permute-start.33 = (bf16[1,32,1024]{2,1,0:T(8,128)(2,1)S(1)}, bf16[1,32,1024]{2,1,0:T(8,128)(2,1)S(1)}, u32[]{:S(2)}, u32[]{:S(2)}) collective-permute-start(bf16[1,32,1024]{2,1,0:T(8,128)(2,1)S(1)} %get-tuple-element.98), channel_id=1, source_target_pairs={{0,12},{1,13},{2,14},{3,15},{4,8},{5,9},{6,10},{7,11},{8,4},{9,5},... | collective-permute-start | bytes 196616 | tf_op jit(solution)/shard_map/ppermute | solution.py:49
  164.9 7.9 %collective-permute-start.34 = (bf16[4,32,1024]{2,1,0:T(8,128)(2,1)S(1)}, bf16[4,32,1024]{2,1,0:T(8,128)(2,1)S(1)}, u32[]{:S(2)}, u32[]{:S(2)}) collective-permute-start(bf16[4,32,1024]{2,1,0:T(8,128)(2,1)S(1)} %pad_maximum_fusion.1), channel_id=1, source_target_pairs={{0,2},{1,3},{2,0},{3,1},{4,6},{5,7},{6,4},{7,5},{8,10},{9,11},{10,... | collective-permute-start | bytes 786440 | tf_op jit(solution)/shard_map/ppermute | solution.py:49
  172.8 3.8 %collective-permute-start.35 = (bf16[8,32,1024]{2,1,0:T(8,128)(2,1)S(1)}, bf16[8,32,1024]{2,1,0:T(8,128)(2,1)S(1)}, u32[]{:S(2)}, u32[]{:S(2)}) collective-permute-start(bf16[8,32,1024]{2,1,0:T(8,128)(2,1)S(1)} %constant_dynamic-update-slice_fusion.near), channel_id=1, source_target_pairs={{0,1},{1,0},{2,3},{3,2},{4,5},{5,4},{6,7},{7,6},{8,9},{9,8},{10,11... | collective-permute-start | bytes 1572872 | tf_op jit(solution)/shard_map/ppermute | solution.py:49
  175.1 14.4 %collective-permute-start.30 = (bf16[256,1024]{1,0:T(8,128)(2,1)S(1)}, bf16[256,1024]{1,0:T(8,128)(2,1)S(1)}, u32[]{:S(2)}, u32[]{:S(2)}) collective-permute-start(bf16[256,1024]{1,0:T(8,128)(2,1)S(1)} %get-tuple-element.96), channel_id=1, source_target_pairs={{0,2},{1,3},{2,0},{3,1},{4,6},{5,7},{6,4},{7,5},{8,10},{9,11},{10,... | collective-permute-start | bytes 1572872 | tf_op jit(solution)/shard_map/ppermute | solution.py:49

commit v7 on v6

--- a/solution.py
+++ b/solution.py
@@ -94,7 +94,7 @@
     basis, refs = refs[:ring], refs[ring:]
     grads, refs = refs[:members], refs[members:]
     kept, given, grad = refs
-    rows = basis[0].shape[0]
+    rows = acts[0].shape[1] // ring
     core = lax.axis_index("dp") % 2
     for x in range(members):
         total = None
@@ -104,7 +104,7 @@
             for s in range(first, first + count):
                 term = jnp.dot(
                     piece[:, (s - first) * rows : (s - first + 1) * rows],
-                    basis[s][...],
+                    basis[s][:rows, :],
                     preferred_element_type=f32,
                 )
                 total = term if total is None else total + term
@@ -143,49 +143,98 @@
             outs[j][i] = value.astype(outs[j].dtype)
 
 
-def square_kernel(came, *refs):
-    kept, arrived, (owned, square) = refs[0], refs[1 : 1 + came], refs[1 + came :]
+def square_kernel(came, lines, *refs):
+    kept, arrived, (owned, message) = refs[0], refs[1 : 1 + came], refs[1 + came :]
     total = kept[0]
     for piece in arrived:
         total = total + piece[0].astype(f32)
     owned[...] = total
-    square[...] = jnp.full(square.shape, jnp.sum(total * total), f32)
-
-
-def moment_kernel(count, *refs):
-    squares, (owned, first, second, new_first, new_second, update) = refs[:count], refs[count:]
+    count = total.shape[0]
+    square = jnp.full((16, total.shape[1]), jnp.sum(total * total), f32)
+    first = square.astype(bf16).astype(f32)
+    second = (square - first).astype(bf16).astype(f32)
+    third = square - first - second
+    row = lax.broadcasted_iota(jnp.int32, square.shape, 0)
+    terms = jnp.where(row == 0, first, jnp.where(row == 1, second, jnp.where(row == 2, third, 0.0)))
+    if count < lines:
+        total = jnp.concatenate([total, jnp.zeros((lines - count, total.shape[1]), f32)], axis=0)
+    message[0, :lines, :] = total.astype(bf16)
+    message[0, lines:, :] = terms.astype(bf16)
+
+
+def gathered_kernel(messages, square):
+    lines = messages.shape[1] - 16
+    total = jnp.zeros((16, 128), f32)
+    for j in range(messages.shape[0]):
+        total = total + messages[j, lines:, 0:128].astype(f32)
+    square[...] = jnp.full(square.shape, jnp.sum(total[:, 0:1]), f32)
+
+
+def moment_kernel(lay, rows, *refs):
+    squares, refs = refs[: lay.members], refs[lay.members :]
+    basis, refs = refs[: lay.ring], refs[lay.ring :]
+    owned, first, second, messages, new_first, new_second, update = refs
     total = squares[0][...]
     for square in squares[1:]:
         total = total + square[...]
     factor = jnp.minimum(1.0, clip_total / (jnp.sqrt(total) + 1e-06))[0:1, 0:1]
-    clipped = owned[...] * factor
-    one = 0.9 * first[...] + 0.1 * clipped
-    two = 0.99 * second[...] + 0.01 * clipped * clipped
+
+    def advance(gradient, one, two):
+        clipped = gradient * factor
+        one = 0.9 * one + 0.1 * clipped
+        two = 0.99 * two + 0.01 * clipped * clipped
+        return one, two
+
+    one, two = advance(owned[...], first[...], second[...])
     new_first[...] = one
     new_second[...] = two
-    update[0] = (one / first_fix / (jnp.sqrt(two / second_fix) + 1e-08)).astype(bf16)
-
-
-def place(lay, s, side, rows, source, out, sems):
+    count = owned.shape[0]
+    half = owned.shape[1] // 2
+    index = lax.axis_index("dp")
+    for s in range(lay.ring):
+        xor = lax.bitwise_xor(lay.source(index, s), index // lay.members)
+        slot = place_slot(lay, xor)
+        for k in range(2):
+            low = rows + k * 2 * count
+            moments = basis[s][low : low + 2 * count, :].astype(f32)
+            gradient = messages[slot, :, k * half : (k + 1) * half].astype(f32)[:count]
+            one, two = advance(gradient, moments[:count], moments[count:])
+            update[slot, :, k * half : (k + 1) * half] = (
+                one / first_fix / (jnp.sqrt(two / second_fix) + 1e-08)
+            ).astype(bf16)
+
+
+def place_slot(lay, xor):
+    slot, scale = 0, 1
+    for bit, radix in reversed(lay.rounds):
+        if bit >= lay.members:
+            slot = slot + scale * ((xor // (bit // lay.members)) % radix)
+            scale *= radix
+    return slot
+
+
+def place(lay, s, side, low, width, rows, source, out, sems):
     index = lax.axis_index("dp")
     core = index % 2
     chip = lay.source(index, s) * lay.sides + side
     copies = []
     for k, owner in enumerate((core, 1 - core)):
-        start = pl.multiple_of((chip * 2 + owner) * rows, rows)
+        start = pl.multiple_of((chip * 2 + owner) * rows + low, width)
         copies.append(
             pltpu.make_async_copy(
-                source.at[:, pl.ds(k * rows, rows)],
-                out.at[:, pl.ds(start, rows)],
+                source.at[:, pl.ds(k * width, width)],
+                out.at[:, pl.ds(start, width)],
                 sems.at[k],
             )
         )
     return copies
 
 
-def weight_kernel(lay, rows, s, came, first, *refs):
+def weight_kernel(lay, rows, s, low, parts, came, first, *refs):
     sides = lay.sides
-    mine, theirs, grads, refs = refs[0], refs[1], refs[2 : 2 + sides], refs[2 + sides :]
+    mine, refs = refs[:parts], refs[parts:]
+    theirs, refs = refs[:parts], refs[parts:]
+    grads, refs = refs[:sides], refs[sides:]
     if came is not None:
         arrived, refs = refs[0], refs[1:]
     if not first:
@@ -194,34 +243,40 @@
     if sides == 2:
         far, refs = refs[0], refs[1:]
     own, sems, came_sems = refs
+    height = mine[0].shape[0]
+    width = parts * height
     side = (lax.axis_index("dp") // 2) % sides
     copies = []
     if came is not None:
-        copies = place(lay, came, 1 - side, rows, arrived, out, came_sems)
+        copies = place(
+            lay, came[0], 1 - side, came[1], arrived.shape[1] // 2, rows, arrived, out, came_sems
+        )
         for copy in copies:
             copy.start()
     for x in reversed(range(sides)):
         target = own if x == 0 else far
-        for k, piece in enumerate((mine, theirs)):
-            target[:, k * rows : (k + 1) * rows] = lax.dot_general(
-                grads[x][...],
-                piece[...],
-                (((1,), (1,)), ((), ())),
-                preferred_element_type=f32,
-            ).astype(bf16)
-    owns = place(lay, s, side, rows, own, out, sems)
+        for k, group in enumerate((mine, theirs)):
+            for p, piece in enumerate(group):
+                target[:, k * width + p * height : k * width + (p + 1) * height] = lax.dot_general(
+                    grads[x][...],
+                    piece[...],
+                    (((1,), (1,)), ((), ())),
+                    preferred_element_type=f32,
+                ).astype(bf16)
+    owns = place(lay, s, side, low, width, rows, own, out, sems)
     for copy in owns:
         copy.start()
     for copy in owns + copies:
         copy.wait()
 
 
-def last_kernel(lay, rows, steps, *refs):
-    arrived, (before, out, sems) = refs[: len(steps)], refs[len(steps) :]
+def last_kernel(lay, rows, blocks, *refs):
+    arrived, (before, out, sems) = refs[: len(blocks)], refs[len(blocks) :]
     side = (lax.axis_index("dp") // 2) % lay.sides
     copies = []
-    for k, s in enumerate(steps):
-        copies += place(lay, s, 1 - side, rows, arrived[k], out, sems.at[k])
+    for k, (s, low) in enumerate(blocks):
+        wide = arrived[k].shape[1] // 2
+        copies += place(lay, s, 1 - side, low, wide, rows, arrived[k], out, sems.at[k])
     for copy in copies:
         copy.start()
     for copy in copies:
@@ -275,6 +330,9 @@
         rows, rank = proj_basis.shape
         outs = key_grad.shape[1]
         owned = rank // n
+        lines = -(-owned // 16) * 16
+        parts = 2 if rows % 256 == 0 else 1
+        height = rows // parts
 
         plan = [(x, 0, ring) for x in range(min(members, 3))]
         if sides == 2:
@@ -296,36 +354,41 @@
             acts[2] = swap(cut[2], 2)
             acts[3] = swap(after(cut[3], far_grad), 3)
             acts[4] = swap(after(cut[4], acts[2]), 3)
+        moments = jnp.concatenate([first_moment, second_moment], axis=0).astype(bf16)
+        folded = [moments[:, k * rank : (k + 1) * rank] for k in range(outs // rank)]
+        basis = [after(jnp.concatenate([proj_basis] + folded, axis=0), cut[0])]
         weight = [master_weight.astype(bf16)]
-        basis = [after(proj_basis, cut[0])]
         for s in range(1, ring):
             value = basis[-1]
             if s == 2 and sides == 2:
                 value = after(value, far_grad)
-            if s == 3:
-                value = after(value, weight[1])
+            if s == 3 and sides == 2:
+                value = after(value, acts[2])
             basis.append(onward(value))
             if s == 1:
-                weight.append(onward(weight[0]))
-        acts[1] = swap(after(cut[1], basis[1]), 1)
+                weight.append(onward(after(weight[0], basis[1])))
+        weight.append(onward(after(weight[1], basis[-1], acts[-1])))
+
+        acts[1] = swap(cut[1], 1)
         if sides == 2:
-            near = swap(jnp.concatenate([key_grad, far_grad], axis=0), 1)
+            near = swap(jnp.concatenate([after(key_grad, acts[1]), far_grad], axis=0), 1)
             grads = [key_grad, near[:tokens], far_grad, near[tokens:]]
         else:
-            grads = [key_grad, swap(key_grad, 1)]
-        weight.append(onward(after(weight[1], basis[-1])))
+            near = swap(key_grad, 1)
+            grads = [key_grad, near]
+        theirs = [swap(after(weight[0], near, acts[min(members, 3) - 1]), 1)]
 
         side_grads = [key_grad, far_grad] if sides == 2 else [key_grad]
         state = {"out": None}
         waiting = []
 
-        def multiply(s, gate=None):
-            args = [weight[s] if gate is None else after(weight[s], gate), swap(weight[s], 1)]
-            args += side_grads
+        def multiply(s, mine, theirs, low=0, gate=None):
+            args = [mine if gate is None else after(mine, gate), theirs] + side_grads
             in_specs = [VMEM] * len(args)
+            wide = mine.shape[0]
             came = None
             if len(waiting) > 1:
-                came, block = waiting.pop(0)
+                (came, block) = waiting.pop(0)
                 args.append(block)
                 in_specs.append(VMEM)
             first = state["out"] is None
@@ -334,34 +397,35 @@
                 in_specs.append(HBM)
             shapes, out_specs = [((tokens, width), bf16)], [HBM]
             if sides == 2:
-                shapes.append(((tokens, 2 * rows), bf16))
+                shapes.append(((tokens, 2 * wide), bf16))
                 out_specs.append(VMEM)
             result = call(
-                functools.partial(weight_kernel, lay, rows, s, came, first),
+                functools.partial(weight_kernel, lay, rows, s, low, 1, came, first),
                 "weight",
                 shapes,
                 args,
                 in_specs,
                 out_specs,
                 scratch=[
-                    pltpu.VMEM((tokens, 2 * rows), bf16),
+                    pltpu.VMEM((tokens, 2 * wide), bf16),
                     pltpu.SemaphoreType.DMA((2,)),
                     pltpu.SemaphoreType.DMA((2,)),
                 ],
-                flops=4 * sides * tokens * rows * outs,
+                flops=4 * sides * tokens * wide * outs,
                 moved=6 * 2**20,
                 input_output_aliases={} if first else {len(args) - 1: 0},
             )
             state["out"] = result[0]
             return result[1] if sides == 2 else result[0]
 
-        def give_back(s, block, *gates):
+        def give_back(s, block, low=0, gate=None):
             if sides == 1:
                 return block
-            waiting.append((s, swap(after(block, *gates) if gates else block, 2)))
+            waiting.append(((s, low), swap(block if gate is None else after(block, gate), 2)))
             return waiting[-1][1]
 
-        first_block = multiply(0)
+        first_block = multiply(0, weight[0], theirs[0], gate=acts[-2])
+        theirs.append(swap(after(weight[1], theirs[0]), 1))
 
         total, *gives = call(
             functools.partial(project_kernel, lay, owned, plan),
@@ -372,8 +436,11 @@
             flops=2 * tokens * members * rank * (ring * rows + outs),
             moved=12 * 2**20,
         )
+        sent = give_back(0, first_block, gate=acts[-1])
 
         for k, (bit, radix) in enumerate(rounds):
+            if bit == 2 and sides == 2:
+                gives = [after(give, sent) for give in gives]
             if bit == members:
                 gives = [after(give, weight[2], block) for give in gives]
             came = [swap(give, j * bit) for j, give in zip(range(1, radix), gives)]
@@ -389,44 +456,50 @@
                 moved=4 * total.size,
             )
             if bit == 1:
-                block = multiply(1, total)
+                block = multiply(1, weight[1], theirs[1], gate=total)
             if bit == 2:
-                sent = give_back(0, first_block, total)
-                later = give_back(1, block, total)
-        owned_rows, square = call(
-            functools.partial(square_kernel, len(came)),
+                later = give_back(1, block, gate=total)
+
+        split = [weight[2][p * height : (p + 1) * height] for p in range(parts)] if ring == 4 else []
+        last = []
+        if split:
+            last.append(onward(after(split[0], *came)))
+        owned_rows, message = call(
+            functools.partial(square_kernel, len(came), lines),
             "square",
-            [((owned, outs), f32), ((8, 128), f32)],
+            [((owned, outs), f32), ((1, lines + 16, outs), bf16)],
             [total] + came,
         )
-        square = after(square, sent)
+        block = multiply(2, weight[2], swap(weight[2], 1), gate=owned_rows)
+        messages = after(message, last[0], block) if split else message
         for bit, radix in reversed(rounds):
             if bit >= members:
-                square = sum([swap(square, j * bit) for j in range(1, radix)], square)
-        if ring > 3:
-            weight.append(onward(after(weight[2], square)))
-        block = multiply(2, owned_rows)
-        square = after(square, later)
+                came = [swap(messages, j * bit) for j in range(1, radix)]
+                messages = jnp.concatenate([messages] + came, axis=0)
+        for p in range(1, len(split)):
+            last.append(onward(after(split[p], *came)))
+        (square,) = call(gathered_kernel, "gathered", [((8, 128), f32)], [messages])
+        if sides == 2:
+            sent = give_back(2, block, gate=later)
+            square = after(square, sent)
         squares = [square] + [swap(square, x) for x in range(1, members)]
-        new_first, new_second, update = call(
-            functools.partial(moment_kernel, members),
+        new_first, new_second, whole = call(
+            functools.partial(moment_kernel, lay, rows),
             "moment",
-            [((owned, outs), f32), ((owned, outs), f32), ((1, owned, outs), bf16)],
-            squares + [after(owned_rows, block), first_moment, second_moment],
-        )
-        sent = give_back(2, block, update)
-        if ring > 3:
-            weight[3] = after(weight[3], update)
-
-        whole = update
+            [((owned, outs), f32), ((owned, outs), f32), ((ring, owned, outs), bf16)],
+            squares + basis + [owned_rows, first_moment, second_moment, messages],
+        )
+        blocks = []
+        if split:
+            block = multiply(3, last[0], swap(last[0], 1), 0, squares[0])
+            sent = give_back(3, after(block, *squares), 0)
+
         for bit, radix in reversed(rounds[1:]):
-            if bit >= members and 2 * bit >= n // 2 and ring > 3:
-                whole = after(whole, weight[3])
-            if bit == 2 and sides == 2:
+            if bit < members:
                 whole = after(whole, sent)
-            whole = jnp.concatenate(
-                [whole] + [swap(whole, j * bit) for j in range(1, radix)], axis=0
-            )
+                whole = jnp.concatenate(
+                    [whole] + [swap(whole, j * bit) for j in range(1, radix)], axis=0
+                )
         (new_master,) = call(
             functools.partial(back_kernel, lay, owned),
             "back",
@@ -437,17 +510,19 @@
             moved=8 * 2**20,
         )
 
-        for s in range(3, ring):
-            if s > 3:
+        for p in range(1, len(split)):
+            give_back(3, multiply(3, last[p], swap(last[p], 1), p * height), p * height)
+        if not split:
+            for s in range(3, ring):
                 weight.append(onward(weight[s - 1]))
-            give_back(s, multiply(s))
+                give_back(s, multiply(s, weight[s], swap(weight[s], 1)))
         activation_grad = state["out"]
         if waiting:
             (activation_grad,) = call(
-                functools.partial(last_kernel, lay, rows, [s for s, block in waiting]),
+                functools.partial(last_kernel, lay, rows, [spot for spot, block in waiting]),
                 "last",
                 [((tokens, width), bf16)],
-                [block for s, block in waiting] + [activation_grad],
+                [block for spot, block in waiting] + [activation_grad],
                 [VMEM] * len(waiting) + [HBM],
                 [HBM],
                 scratch=[pltpu.SemaphoreType.DMA((len(waiting), 2))],

time: 191 us -> 179 us (0.937)
  waiting for transfers between devices: 129 us -> 119 us
  starting transfers between devices: 39.4 us -> 37.2 us
    ppermute x6 -> x7, waiting for transfers between devices: 59 us -> 25.4 us  [onward(): return lax.ppermute(value, 'dp', self.forward)]
    ppermute x30 -> x29, waiting for transfers between devices: 70.3 us -> 94.1 us  [swap(): return lax.ppermute(value, 'dp', [(i, i ^ bit) for i in range(self.n)])]
    ppermute x30 -> x29, starting transfers between devices: 29.6 us -> 26.8 us  [swap(): return lax.ppermute(value, 'dp', [(i, i ^ bit) for i in range(self.n)])]
    pallas_call x12 -> x14, Pallas kernels: 17.6 us -> 18.8 us  [call(): pl.pallas_call(kernel, name=name, out_shape=[jax.ShapeDtypeStruct(shape,...]
    ppermute x6 -> x7, starting transfers between devices: 9.88 us -> 10.4 us  [onward(): return lax.ppermute(value, 'dp', self.forward)]
  transfers between devices with their start and end apart: 36 -> 36, of which waited for: 22 -> 20; matrix products, arithmetic and copies ran while one was open for 0% -> 0% of each run, Pallas kernels for 6% -> 9%
where the time goes in v7:
time: 179 us
  waiting for transfers between devices  119 us (66%)
  starting transfers between devices  37.2 us (21%)
  Pallas kernels  18.8 us (11%)
  local copies, waits for them, and re-layouts  2.46 us (1%)
    ppermute x29, waiting for transfers between devices, swap(): return lax.ppermute(value, 'dp', [(i, i ^ bit) for i in range(self.n)])  94.1 us
    ppermute x29, starting transfers between devices, swap(): return lax.ppermute(value, 'dp', [(i, i ^ bit) for i in range(self.n)])  26.8 us
    ppermute x7, waiting for transfers between devices, onward(): return lax.ppermute(value, 'dp', self.forward)  25.4 us
    pallas_call x14, Pallas kernels, call(): pl.pallas_call(kernel, name=name, out_shape=[jax.ShapeDtypeStruct(shape,...  18.8 us
    ppermute x7, starting transfers between devices, onward(): return lax.ppermute(value, 'dp', self.forward)  10.4 us
  transfers between devices with their start and end apart: 36, of which 20 were waited for; matrix products, arithmetic and copies ran while one was open for 0% of the time, Pallas kernels for 9%

profile of v7, /device:TPU:0, one launch (start us, length us, event | category | flops | bytes accessed | tf_op | source)
XLA Modules:
  0.0 179.1 jit_solution(14485380022229233614)
XLA Ops:
  0.7 2.2 %copy-done.2 = bf16[256,8192]{1,0:T(8,128)(2,1)S(1)} copy-done((bf16[256,8192]{1,0:T(8,128)(2,1)S(1)}, bf16[256,8192]{1,0:T(8,128)(2,1)}, u32[]{:S(2)}) %copy-start.2) | copy-done | bytes 4194328
  4.0 2.6 %collective-permute-start.2 = (bf16[256,1024]{1,0:T(8,128)(2,1)S(1)}, bf16[256,1024]{1,0:T(8,128)(2,1)S(1)}, u32[]{:S(2)}, u32[]{:S(2)}) collective-permute-start(bf16[256,1024]{1,0:T(8,128)(2,1)S(1)} %copy-done), channel_id=1, source_target_pairs={{0,2},{1,3},{2,0},{3,1},{4,6},{5,7},{6,4},{7,5},{8,10},{9,11},{10,... | collective-permute-start | bytes 1572872 | tf_op jit(solution)/shard_map/ppermute | solution.py:49
  6.8 2.0 %collective-permute-start = (bf16[640,512]{1,0:T(8,128)(2,1)S(1)}, bf16[640,512]{1,0:T(8,128)(2,1)S(1)}, u32[]{:S(2)}, u32[]{:S(2)}) collective-permute-start(bf16[640,512]{1,0:T(8,128)(2,1)S(1)} %fusion.refs_5_.refs_4_), channel_id=1, source_target_pairs={{0,4},{1,5},{2,6},{3,7},{4,12},{5,13},{6,14},{7,15},{12,8},{13,9},... | collective-permute-start | bytes 1966088 | tf_op jit(solution)/shard_map/ppermute | solution.py:52
  8.8 10.5 %collective-permute-done.2.refs_3_.refs_11_ = bf16[256,1024]{1,0:T(8,128)(2,1)S(1)} collective-permute-done((bf16[256,1024]{1,0:T(8,128)(2,1)S(1)}, bf16[256,1024]{1,0:T(8,128)(2,1)S(1)}, u32[]{:S(2)}, u32[]{:S(2)}) %collective-permute-start.2) | collective-permute-done | bytes 524320 | tf_op jit(solution)/shard_map/ppermute | solution.py:49
  19.5 5.1 %collective-permute-done.refs_6_.refs_5_ = bf16[640,512]{1,0:T(8,128)(2,1)S(1)} collective-permute-done((bf16[640,512]{1,0:T(8,128)(2,1)S(1)}, bf16[640,512]{1,0:T(8,128)(2,1)S(1)}, u32[]{:S(2)}, u32[]{:S(2)}) %collective-permute-start) | collective-permute-done | bytes 655392 | tf_op jit(solution)/shard_map/ppermute | solution.py:52
  24.6 0.8 collective-permute-start.3
  25.6 3.4 %collective-permute-start.1 = (bf16[512,1024]{1,0:T(8,128)(2,1)S(1)}, bf16[512,1024]{1,0:T(8,128)(2,1)S(1)}, u32[]{:S(2)}, u32[]{:S(2)}) collective-permute-start(bf16[512,1024]{1,0:T(8,128)(2,1)S(1)} %convert_element_type.4.refs_0_), channel_id=1, source_target_pairs={{0,4},{1,5},{2,6},{3,7},{4,12},{5,13},{6,14},{7,15},{12,8},{13,9},... | collective-permute-start | bytes 3145736 | tf_op jit(solution)/shard_map/ppermute | solution.py:52
  29.0 12.5 %collective-permute-done.4.refs_2_ = bf16[256,2048]{1,0:T(8,128)(2,1)S(1)} collective-permute-done((bf16[256,2048]{1,0:T(8,128)(2,1)S(1)}, bf16[256,2048]{1,0:T(8,128)(2,1)S(1)}, u32[]{:S(2)}, u32[]{:S(2)}) %collective-permute-start.4) | collective-permute-done | bytes 1048608 | tf_op jit(solution)/shard_map/ppermute | solution.py:49
  41.5 1.6 collective-permute-done.3.refs_7_.refs_6_
  43.2 0.8 collective-permute-start.5
  44.0 0.7 collective-permute-start.8
  44.7 1.0 collective-permute-start.6
  45.8 12.4 %collective-permute-done.8.refs_3_ = bf16[256,1024]{1,0:T(8,128)(2,1)S(1)} collective-permute-done((bf16[256,1024]{1,0:T(8,128)(2,1)S(1)}, bf16[256,1024]{1,0:T(8,128)(2,1)S(1)}, u32[]{:S(2)}, u32[]{:S(2)}) %collective-permute-start.8) | collective-permute-done | bytes 524320 | tf_op jit(solution)/shard_map/ppermute | solution.py:49
  58.2 11.2 %collective-permute-done.6.refs_4_ = bf16[256,1024]{1,0:T(8,128)(2,1)S(1)} collective-permute-done((bf16[256,1024]{1,0:T(8,128)(2,1)S(1)}, bf16[256,1024]{1,0:T(8,128)(2,1)S(1)}, u32[]{:S(2)}, u32[]{:S(2)}) %collective-permute-start.6) | collective-permute-done | bytes 524320 | tf_op jit(solution)/shard_map/ppermute | solution.py:49
  69.4 8.6 %collective-permute-done.5.refs_8_.refs_7_ = bf16[640,512]{1,0:T(8,128)(2,1)S(1)} collective-permute-done((bf16[640,512]{1,0:T(8,128)(2,1)S(1)}, bf16[640,512]{1,0:T(8,128)(2,1)S(1)}, u32[]{:S(2)}, u32[]{:S(2)}) %collective-permute-start.5) | collective-permute-done | bytes 655392 | tf_op jit(solution)/shard_map/ppermute | solution.py:52
  78.6 2.1 %weight.5 = (bf16[256,8192]{1,0:T(8,128)(2,1)}, bf16[256,1024]{1,0:T(8,128)(2,1)S(1)}) custom-call(bf16[512,1024]{1,0:T(8,128)(2,1)S(1)} %convert_element_type.4.refs_0_, bf16[512,1024]{1,0:T(8,128)(2,1)S(1)} %collective-permute-done.11.refs_1_, bf16[256,1024]{1,0:T(8,128)(2,1)S(1)} %copy-done, bf16[256,1024]{1,0:T(8,128)(2,1)S(1)} %collective-permute-done.2.refs_3_.refs_11_), custom_call_target="tpu_custom_call" | custom-call | flops 1073741824 | bytes 6291456 | tf_op jit(solution)/shard_map/weight/pallas_call | solution.py:310
  80.8 4.3 %project.1 = (f32[8,32,1024]{2,1,0:T(8,128)S(1)}, bf16[8,32,1024]{2,1,0:T(8,128)(2,1)S(1)}) custom-call(bf16[256,2048]{1,0:T(8,128)(2,1)S(1)} %get-tuple-element.76.refs_0_, bf16[256,2048]{1,0:T(8,128)(2,1)S(1)} %collective-permute-done.9.refs_1_, bf16[256,2048]{1,0:T(8,128)(2,1)S(1)} %collective-permute-done.4.refs_2_, ...), custom_call_target="tpu_custom_call" | custom-call | flops 3221225472 | bytes 12582912 | tf_op jit(solution)/shard_map/project/pallas_call | solution.py:310
  85.7 1.5 collective-permute-start.13
  87.3 12.3 %collective-permute-done.13.refs_4_ = bf16[256,1024]{1,0:T(8,128)(2,1)S(1)} collective-permute-done((bf16[256,1024]{1,0:T(8,128)(2,1)S(1)}, bf16[256,1024]{1,0:T(8,128)(2,1)S(1)}, u32[]{:S(2)}, u32[]{:S(2)}) %collective-permute-start.13) | collective-permute-done | bytes 524320 | tf_op jit(solution)/shard_map/ppermute | solution.py:49
  99.6 1.5 collective-permute-start.14
  101.1 1.2 collective-permute-done.7.refs_0_
  102.4 4.7 %collective-permute-done.14.refs_1_ = bf16[4,32,1024]{2,1,0:T(8,128)(2,1)S(1)} collective-permute-done((bf16[4,32,1024]{2,1,0:T(8,128)(2,1)S(1)}, bf16[4,32,1024]{2,1,0:T(8,128)(2,1)S(1)}, u32[]{:S(2)}, u32[]{:S(2)}) %collective-permute-start.14) | collective-permute-done | bytes 262176 | tf_op jit(solution)/shard_map/ppermute | solution.py:49
  107.1 2.1 %weight.6 = (bf16[256,8192]{1,0:T(8,128)(2,1)}, bf16[256,1024]{1,0:T(8,128)(2,1)S(1)}) custom-call(bf16[512,1024]{1,0:T(8,128)(2,1)S(1)} %collective-permute-done.1.refs_0_, bf16[512,1024]{1,0:T(8,128)(2,1)S(1)} %collective-permute-done.15.refs_1_, bf16[256,1024]{1,0:T(8,128)(2,1)S(1)} %copy-done, ...), custom_call_target="tpu_custom_call", output_to_operand_aliasing={{0}: (4, {})} | custom-call | flops 1073741824 | bytes 6291456 | tf_op jit(solution)/shard_map/weight/pallas_call | solution.py:310
  109.2 1.6 collective-permute-start.24
  110.8 2.8 %collective-permute-start.18 = (bf16[1,32,1024]{2,1,0:T(8,128)(2,1)S(1)}, bf16[1,32,1024]{2,1,0:T(8,128)(2,1)S(1)}, u32[]{:S(2)}, u32[]{:S(2)}) collective-permute-start(bf16[1,32,1024]{2,1,0:T(8,128)(2,1)S(1)} %get-tuple-element.92), channel_id=1, source_target_pairs={{0,12},{1,13},{2,14},{3,15},{4,8},{5,9},{6,10},{7,11},{8,4},{9,5},... | collective-permute-start | bytes 196616 | tf_op jit(solution)/shard_map/ppermute | solution.py:49
  113.6 2.0 %collective-permute-start.17 = (bf16[1,32,1024]{2,1,0:T(8,128)(2,1)S(1)}, bf16[1,32,1024]{2,1,0:T(8,128)(2,1)S(1)}, u32[]{:S(2)}, u32[]{:S(2)}) collective-permute-start(bf16[1,32,1024]{2,1,0:T(8,128)(2,1)S(1)} %get-tuple-element.90), channel_id=1, source_target_pairs={{0,8},{1,9},{2,10},{3,11},{4,12},{5,13},{6,14},{7,15},{8,0},{9,1},... | collective-permute-start | bytes 196616 | tf_op jit(solution)/shard_map/ppermute | solution.py:49
  115.7 1.8 collective-permute-done.18.refs_3_
  117.5 2.0 %collective-permute-done.17.refs_2_ = bf16[1,32,1024]{2,1,0:T(8,128)(2,1)S(1)} collective-permute-done((bf16[1,32,1024]{2,1,0:T(8,128)(2,1)S(1)}, bf16[1,32,1024]{2,1,0:T(8,128)(2,1)S(1)}, u32[]{:S(2)}, u32[]{:S(2)}) %collective-permute-start.17) | collective-permute-done | bytes 65568 | tf_op jit(solution)/shard_map/ppermute | solution.py:49
  119.5 0.7 collective-permute-done.16.refs_1_
  120.9 2.1 %weight.7 = (bf16[256,8192]{1,0:T(8,128)(2,1)}, bf16[256,1024]{1,0:T(8,128)(2,1)S(1)}) custom-call(bf16[512,1024]{1,0:T(8,128)(2,1)S(1)} %collective-permute-done.7.refs_0_, bf16[512,1024]{1,0:T(8,128)(2,1)S(1)} %collective-permute-done.20.refs_1_, bf16[256,1024]{1,0:T(8,128)(2,1)S(1)} %copy-done, ...), custom_call_target="tpu_custom_call", output_to_operand_aliasing={{0}: (5, {})} | custom-call | flops 1073741824 | bytes 6291456 | tf_op jit(solution)/shard_map/weight/pallas_call | solution.py:310
  123.6 8.8 %collective-permute-done.19.refs_0_ = bf16[256,1024]{1,0:T(8,128)(2,1)S(1)} collective-permute-done((bf16[256,1024]{1,0:T(8,128)(2,1)S(1)}, bf16[256,1024]{1,0:T(8,128)(2,1)S(1)}, u32[]{:S(2)}, u32[]{:S(2)}) %collective-permute-start.19) | collective-permute-done | bytes 524320 | tf_op jit(solution)/shard_map/ppermute | solution.py:52
  132.4 1.3 collective-permute-start.22
  133.7 3.1 %collective-permute-start.23 = (bf16[1,48,1024]{2,1,0:T(8,128)(2,1)S(1)}, bf16[1,48,1024]{2,1,0:T(8,128)(2,1)S(1)}, u32[]{:S(2)}, u32[]{:S(2)}) collective-permute-start(bf16[1,48,1024]{2,1,0:T(8,128)(2,1)S(1)} %get-tuple-element.100), channel_id=1, source_target_pairs={{0,12},{1,13},{2,14},{3,15},{4,8},{5,9},{6,10},{7,11},{8,4},{9,5},... | collective-permute-start | bytes 294920 | tf_op jit(solution)/shard_map/ppermute | solution.py:49
  136.8 2.0 %collective-permute-done.21 = bf16[1,48,1024]{2,1,0:T(8,128)(2,1)S(1)} collective-permute-done((bf16[1,48,1024]{2,1,0:T(8,128)(2,1)S(1)}, bf16[1,48,1024]{2,1,0:T(8,128)(2,1)S(1)}, u32[]{:S(2)}, u32[]{:S(2)}) %collective-permute-start.21) | collective-permute-done | bytes 98336 | tf_op jit(solution)/shard_map/ppermute | solution.py:49
  138.8 4.3 %collective-permute-done.22 = bf16[1,48,1024]{2,1,0:T(8,128)(2,1)S(1)} collective-permute-done((bf16[1,48,1024]{2,1,0:T(8,128)(2,1)S(1)}, bf16[1,48,1024]{2,1,0:T(8,128)(2,1)S(1)}, u32[]{:S(2)}, u32[]{:S(2)}) %collective-permute-start.22) | collective-permute-done | bytes 98336 | tf_op jit(solution)/shard_map/ppermute | solution.py:49
  143.1 2.3 %collective-permute-start.31 = (bf16[256,1024]{1,0:T(8,128)(2,1)S(1)}, bf16[256,1024]{1,0:T(8,128)(2,1)S(1)}, u32[]{:S(2)}, u32[]{:S(2)}) collective-permute-start(bf16[256,1024]{1,0:T(8,128)(2,1)S(1)} %get-tuple-element.108), channel_id=1, source_target_pairs={{0,4},{1,5},{2,6},{3,7},{4,12},{5,13},{6,14},{7,15},{12,8},{13,9},... | collective-permute-start | bytes 1572872 | tf_op jit(solution)/shard_map/ppermute | solution.py:52
  146.2 1.3 collective-permute-start.29
  147.5 1.5 weight.8
  149.3 1.4 collective-permute-start.30
  150.8 1.1 moment.1
  151.9 6.0 %collective-permute-done.30.refs_0_ = bf16[256,512]{1,0:T(8,128)(2,1)S(1)} collective-permute-done((bf16[256,512]{1,0:T(8,128)(2,1)S(1)}, bf16[256,512]{1,0:T(8,128)(2,1)S(1)}, u32[]{:S(2)}, u32[]{:S(2)}) %collective-permute-start.30) | collective-permute-done | bytes 262176 | tf_op jit(solution)/shard_map/ppermute | solution.py:49
  158.0 1.5 collective-permute-start.34
  159.5 6.2 %collective-permute-done.34 = bf16[4,32,1024]{2,1,0:T(8,128)(2,1)S(1)} collective-permute-done((bf16[4,32,1024]{2,1,0:T(8,128)(2,1)S(1)}, bf16[4,32,1024]{2,1,0:T(8,128)(2,1)S(1)}, u32[]{:S(2)}, u32[]{:S(2)}) %collective-permute-start.34) | collective-permute-done | bytes 262176 | tf_op jit(solution)/shard_map/ppermute | solution.py:49
  165.8 1.5 weight.9
  167.3 1.7 collective-permute-start.33
  169.0 7.1 %collective-permute-done.33.refs_1_ = bf16[256,512]{1,0:T(8,128)(2,1)S(1)} collective-permute-done((bf16[256,512]{1,0:T(8,128)(2,1)S(1)}, bf16[256,512]{1,0:T(8,128)(2,1)S(1)}, u32[]{:S(2)}, u32[]{:S(2)}) %collective-permute-start.33) | collective-permute-done | bytes 262176 | tf_op jit(solution)/shard_map/ppermute | solution.py:49
  176.1 0.8 last.1
  176.9 2.2 %back.1 = f32[512,1024]{1,0:T(8,128)} custom-call(bf16[512,512]{1,0:T(8,128)(2,1)S(1)} %copy-done.3, bf16[8,32,1024]{2,1,0:T(8,128)(2,1)S(1)} %constant_dynamic-update-slice_fusion.4.near, bf16[8,32,1024]{2,1,0:T(8,128)(2,1)S(1)} %collective-permute-done.35.other, f32[512,1024]{1,0:T(8,128)S(1)} %copy-done.1), custom_call_target="tpu_custom_call" | custom-call | flops 536870912 | bytes 8388608 | tf_op jit(solution)/shard_map/back/pallas_call | solution.py:310
  (64 shorter events, 5.4 us)
Async XLA Ops:
  0.6 3.3 %copy-start = (bf16[256,1024]{1,0:T(8,128)(2,1)S(1)}, bf16[256,1024]{1,0:T(8,128)(2,1)}, u32[]{:S(2)}) copy-start(bf16[256,1024]{1,0:T(8,128)(2,1)} %refs_2_.9) | copy-start | bytes 1572868
  0.6 2.2 %copy-start.2 = (bf16[256,8192]{1,0:T(8,128)(2,1)S(1)}, bf16[256,8192]{1,0:T(8,128)(2,1)}, u32[]{:S(2)}) copy-start(bf16[256,8192]{1,0:T(8,128)(2,1)} %act.1) | copy-start | bytes 12582916
  2.9 3.8 %copy-start.5 = (f32[32,1024]{1,0:T(8,128)S(1)}, f32[32,1024]{1,0:T(8,128)}, u32[]{:S(2)}) copy-start(f32[32,1024]{1,0:T(8,128)} %refs_9_.3) | copy-start | bytes 393220
  2.9 3.8 %copy-start.4 = (f32[32,1024]{1,0:T(8,128)S(1)}, f32[32,1024]{1,0:T(8,128)}, u32[]{:S(2)}) copy-start(f32[32,1024]{1,0:T(8,128)} %refs_10_.1) | copy-start | bytes 393220
  2.9 3.8 %copy-start.3 = (bf16[512,512]{1,0:T(8,128)(2,1)S(1)}, bf16[512,512]{1,0:T(8,128)(2,1)}, u32[]{:S(2)}) copy-start(bf16[512,512]{1,0:T(8,128)(2,1)} %basis.1) | copy-start | bytes 1572868
  3.4 22.0 %copy-start.1 = (f32[512,1024]{1,0:T(8,128)S(1)}, f32[512,1024]{1,0:T(8,128)}, u32[]{:S(2)}) copy-start(f32[512,1024]{1,0:T(8,128)} %master.1) | copy-start | bytes 6291460
  3.4 5.4 %collective-permute-start.9 = (bf16[256,2048]{1,0:T(8,128)(2,1)S(1)}, bf16[256,2048]{1,0:T(8,128)(2,1)S(1)}, u32[]{:S(2)}, u32[]{:S(2)}) collective-permute-start(bf16[256,2048]{1,0:T(8,128)(2,1)S(1)} %get-tuple-element.72), channel_id=1, source_target_pairs={{0,1},{1,0},{2,3},{3,2},{4,5},{5,4},{6,7},{7,6},{8,9},{9,8},{10,11... | collective-permute-start | bytes 3145736 | tf_op jit(solution)/shard_map/ppermute | solution.py:49
  4.0 15.4 %collective-permute-start.2 = (bf16[256,1024]{1,0:T(8,128)(2,1)S(1)}, bf16[256,1024]{1,0:T(8,128)(2,1)S(1)}, u32[]{:S(2)}, u32[]{:S(2)}) collective-permute-start(bf16[256,1024]{1,0:T(8,128)(2,1)S(1)} %copy-done), channel_id=1, source_target_pairs={{0,2},{1,3},{2,0},{3,1},{4,6},{5,7},{6,4},{7,5},{8,10},{9,11},{10,... | collective-permute-start | bytes 1572872 | tf_op jit(solution)/shard_map/ppermute | solution.py:49
  6.6 35.0 %collective-permute-start.4 = (bf16[256,2048]{1,0:T(8,128)(2,1)S(1)}, bf16[256,2048]{1,0:T(8,128)(2,1)S(1)}, u32[]{:S(2)}, u32[]{:S(2)}) collective-permute-start(bf16[256,2048]{1,0:T(8,128)(2,1)S(1)} %get-tuple-element.64), channel_id=1, source_target_pairs={{0,2},{1,3},{2,0},{3,1},{4,6},{5,7},{6,4},{7,5},{8,10},{9,11},{10,... | collective-permute-start | bytes 3145736 | tf_op jit(solution)/shard_map/ppermute | solution.py:49
  6.8 17.8 %collective-permute-start = (bf16[640,512]{1,0:T(8,128)(2,1)S(1)}, bf16[640,512]{1,0:T(8,128)(2,1)S(1)}, u32[]{:S(2)}, u32[]{:S(2)}) collective-permute-start(bf16[640,512]{1,0:T(8,128)(2,1)S(1)} %fusion.refs_5_.refs_4_), channel_id=1, source_target_pairs={{0,4},{1,5},{2,6},{3,7},{4,12},{5,13},{6,14},{7,15},{12,8},{13,9},... | collective-permute-start | bytes 1966088 | tf_op jit(solution)/shard_map/ppermute | solution.py:52
  19.4 22.1 %collective-permute-start.10 = (bf16[512,1024]{1,0:T(8,128)(2,1)S(1)}, bf16[512,1024]{1,0:T(8,128)(2,1)S(1)}, u32[]{:S(2)}, u32[]{:S(2)}) collective-permute-start(bf16[512,1024]{1,0:T(8,128)(2,1)S(1)} %pad_maximum_fusion), channel_id=1, source_target_pairs={{0,1},{1,0},{2,3},{3,2},{4,5},{5,4},{6,7},{7,6},{8,9},{9,8},{10,11... | collective-permute-start | bytes 3145736 | tf_op jit(solution)/shard_map/ppermute | solution.py:49
  24.6 18.6 %collective-permute-start.3 = (bf16[640,512]{1,0:T(8,128)(2,1)S(1)}, bf16[640,512]{1,0:T(8,128)(2,1)S(1)}, u32[]{:S(2)}, u32[]{:S(2)}) collective-permute-start(bf16[640,512]{1,0:T(8,128)(2,1)S(1)} %collective-permute-done.refs_6_.refs_5_), channel_id=1, source_target_pairs={{0,4},{1,5},{2,6},{3,7},{4,12},{5,13},{6,14},{7,15},{12,8},{13,9},... | collective-permute-start | bytes 1966088 | tf_op jit(solution)/shard_map/ppermute | solution.py:52
  25.6 43.8 %collective-permute-start.1 = (bf16[512,1024]{1,0:T(8,128)(2,1)S(1)}, bf16[512,1024]{1,0:T(8,128)(2,1)S(1)}, u32[]{:S(2)}, u32[]{:S(2)}) collective-permute-start(bf16[512,1024]{1,0:T(8,128)(2,1)S(1)} %convert_element_type.4.refs_0_), channel_id=1, source_target_pairs={{0,4},{1,5},{2,6},{3,7},{4,12},{5,13},{6,14},{7,15},{12,8},{13,9},... | collective-permute-start | bytes 3145736 | tf_op jit(solution)/shard_map/ppermute | solution.py:52
  41.5 37.0 %collective-permute-start.11 = (bf16[512,1024]{1,0:T(8,128)(2,1)S(1)}, bf16[512,1024]{1,0:T(8,128)(2,1)S(1)}, u32[]{:S(2)}, u32[]{:S(2)}) collective-permute-start(bf16[512,1024]{1,0:T(8,128)(2,1)S(1)} %convert_element_type.4.refs_0_), channel_id=1, source_target_pairs={{0,1},{1,0},{2,3},{3,2},{4,5},{5,4},{6,7},{7,6},{8,9},{9,8},{10,11... | collective-permute-start | bytes 3145736 | tf_op jit(solution)/shard_map/ppermute | solution.py:49
  43.2 34.8 %collective-permute-start.5 = (bf16[640,512]{1,0:T(8,128)(2,1)S(1)}, bf16[640,512]{1,0:T(8,128)(2,1)S(1)}, u32[]{:S(2)}, u32[]{:S(2)}) collective-permute-start(bf16[640,512]{1,0:T(8,128)(2,1)S(1)} %collective-permute-done.3.refs_7_.refs_6_), channel_id=1, source_target_pairs={{0,4},{1,5},{2,6},{3,7},{4,12},{5,13},{6,14},{7,15},{12,8},{13,9},... | collective-permute-start | bytes 1966088 | tf_op jit(solution)/shard_map/ppermute | solution.py:52
  44.0 14.1 %collective-permute-start.8 = (bf16[256,1024]{1,0:T(8,128)(2,1)S(1)}, bf16[256,1024]{1,0:T(8,128)(2,1)S(1)}, u32[]{:S(2)}, u32[]{:S(2)}) collective-permute-start(bf16[256,1024]{1,0:T(8,128)(2,1)S(1)} %get-tuple-element.70), channel_id=1, source_target_pairs={{0,3},{1,2},{2,1},{3,0},{4,7},{5,6},{6,5},{7,4},{8,11},{9,10},{10,... | collective-permute-start | bytes 1572872 | tf_op jit(solution)/shard_map/ppermute | solution.py:49
  44.7 24.7 %collective-permute-start.6 = (bf16[256,1024]{1,0:T(8,128)(2,1)S(1)}, bf16[256,1024]{1,0:T(8,128)(2,1)S(1)}, u32[]{:S(2)}, u32[]{:S(2)}) collective-permute-start(bf16[256,1024]{1,0:T(8,128)(2,1)S(1)} %get-tuple-element.67), channel_id=1, source_target_pairs={{0,3},{1,2},{2,1},{3,0},{4,7},{5,6},{6,5},{7,4},{8,11},{9,10},{10,... | collective-permute-start | bytes 1572872 | tf_op jit(solution)/shard_map/ppermute | solution.py:49
  78.0 24.4 %collective-permute-start.7 = (bf16[512,1024]{1,0:T(8,128)(2,1)S(1)}, bf16[512,1024]{1,0:T(8,128)(2,1)S(1)}, u32[]{:S(2)}, u32[]{:S(2)}) collective-permute-start(bf16[512,1024]{1,0:T(8,128)(2,1)S(1)} %collective-permute-done.1.refs_0_), channel_id=1, source_target_pairs={{0,4},{1,5},{2,6},{3,7},{4,12},{5,13},{6,14},{7,15},{12,8},{13,9},... | collective-permute-start | bytes 3145736 | tf_op jit(solution)/shard_map/ppermute | solution.py:52
  80.7 26.4 %collective-permute-start.15 = (bf16[512,1024]{1,0:T(8,128)(2,1)S(1)}, bf16[512,1024]{1,0:T(8,128)(2,1)S(1)}, u32[]{:S(2)}, u32[]{:S(2)}) collective-permute-start(bf16[512,1024]{1,0:T(8,128)(2,1)S(1)} %collective-permute-done.1.refs_0_), channel_id=1, source_target_pairs={{0,1},{1,0},{2,3},{3,2},{4,5},{5,4},{6,7},{7,6},{8,9},{9,8},{10,11... | collective-permute-start | bytes 3145736 | tf_op jit(solution)/shard_map/ppermute | solution.py:49
  85.1 2.1 %collective-permute-start.12 = (bf16[8,32,1024]{2,1,0:T(8,128)(2,1)S(1)}, bf16[8,32,1024]{2,1,0:T(8,128)(2,1)S(1)}, u32[]{:S(2)}, u32[]{:S(2)}) collective-permute-start(bf16[8,32,1024]{2,1,0:T(8,128)(2,1)S(1)} %get-tuple-element.78), channel_id=1, source_target_pairs={{0,1},{1,0},{2,3},{3,2},{4,5},{5,4},{6,7},{7,6},{8,9},{9,8},{10,11... | collective-permute-start | bytes 1572872 | tf_op jit(solution)/shard_map/ppermute | solution.py:49
  85.7 13.9 %collective-permute-start.13 = (bf16[256,1024]{1,0:T(8,128)(2,1)S(1)}, bf16[256,1024]{1,0:T(8,128)(2,1)S(1)}, u32[]{:S(2)}, u32[]{:S(2)}) collective-permute-start(bf16[256,1024]{1,0:T(8,128)(2,1)S(1)} %get-tuple-element.81), channel_id=1, source_target_pairs={{0,2},{1,3},{2,0},{3,1},{4,6},{5,7},{6,4},{7,5},{8,10},{9,11},{10,... | collective-permute-start | bytes 1572872 | tf_op jit(solution)/shard_map/ppermute | solution.py:49
  99.6 7.4 %collective-permute-start.14 = (bf16[4,32,1024]{2,1,0:T(8,128)(2,1)S(1)}, bf16[4,32,1024]{2,1,0:T(8,128)(2,1)S(1)}, u32[]{:S(2)}, u32[]{:S(2)}) collective-permute-start(bf16[4,32,1024]{2,1,0:T(8,128)(2,1)S(1)} %get-tuple-element.82), channel_id=1, source_target_pairs={{0,2},{1,3},{2,0},{3,1},{4,6},{5,7},{6,4},{7,5},{8,10},{9,11},{10,... | collective-permute-start | bytes 786440 | tf_op jit(solution)/shard_map/ppermute | solution.py:49
  102.4 18.5 %collective-permute-start.20 = (bf16[512,1024]{1,0:T(8,128)(2,1)S(1)}, bf16[512,1024]{1,0:T(8,128)(2,1)S(1)}, u32[]{:S(2)}, u32[]{:S(2)}) collective-permute-start(bf16[512,1024]{1,0:T(8,128)(2,1)S(1)} %collective-permute-done.7.refs_0_), channel_id=1, source_target_pairs={{0,1},{1,0},{2,3},{3,2},{4,5},{5,4},{6,7},{7,6},{8,9},{9,8},{10,11... | collective-permute-start | bytes 3145736 | tf_op jit(solution)/shard_map/ppermute | solution.py:49
  109.2 13.8 %collective-permute-start.24 = (bf16[256,1024]{1,0:T(8,128)(2,1)S(1)}, bf16[256,1024]{1,0:T(8,128)(2,1)S(1)}, u32[]{:S(2)}, u32[]{:S(2)}) collective-permute-start(bf16[256,1024]{1,0:T(8,128)(2,1)S(1)} %get-tuple-element.101), channel_id=1, source_target_pairs={{0,2},{1,3},{2,0},{3,1},{4,6},{5,7},{6,4},{7,5},{8,10},{9,11},{10,... | collective-permute-start | bytes 1572872 | tf_op jit(solution)/shard_map/ppermute | solution.py:49
  110.8 6.7 %collective-permute-start.18 = (bf16[1,32,1024]{2,1,0:T(8,128)(2,1)S(1)}, bf16[1,32,1024]{2,1,0:T(8,128)(2,1)S(1)}, u32[]{:S(2)}, u32[]{:S(2)}) collective-permute-start(bf16[1,32,1024]{2,1,0:T(8,128)(2,1)S(1)} %get-tuple-element.92), channel_id=1, source_target_pairs={{0,12},{1,13},{2,14},{3,15},{4,8},{5,9},{6,10},{7,11},{8,4},{9,5},... | collective-permute-start | bytes 196616 | tf_op jit(solution)/shard_map/ppermute | solution.py:49
  113.6 5.9 %collective-permute-start.17 = (bf16[1,32,1024]{2,1,0:T(8,128)(2,1)S(1)}, bf16[1,32,1024]{2,1,0:T(8,128)(2,1)S(1)}, u32[]{:S(2)}, u32[]{:S(2)}) collective-permute-start(bf16[1,32,1024]{2,1,0:T(8,128)(2,1)S(1)} %get-tuple-element.90), channel_id=1, source_target_pairs={{0,8},{1,9},{2,10},{3,11},{4,12},{5,13},{6,14},{7,15},{8,0},{9,1},... | collective-permute-start | bytes 196616 | tf_op jit(solution)/shard_map/ppermute | solution.py:49
  115.7 4.5 %collective-permute-start.16 = (bf16[1,32,1024]{2,1,0:T(8,128)(2,1)S(1)}, bf16[1,32,1024]{2,1,0:T(8,128)(2,1)S(1)}, u32[]{:S(2)}, u32[]{:S(2)}) collective-permute-start(bf16[1,32,1024]{2,1,0:T(8,128)(2,1)S(1)} %get-tuple-element.88), channel_id=1, source_target_pairs={{0,4},{1,5},{2,6},{3,7},{4,0},{5,1},{6,2},{7,3},{8,12},{9,13},{10,... | collective-permute-start | bytes 196616 | tf_op jit(solution)/shard_map/ppermute | solution.py:49
  120.2 12.2 %collective-permute-start.19 = (bf16[256,1024]{1,0:T(8,128)(2,1)S(1)}, bf16[256,1024]{1,0:T(8,128)(2,1)S(1)}, u32[]{:S(2)}, u32[]{:S(2)}) collective-permute-start(bf16[256,1024]{1,0:T(8,128)(2,1)S(1)} %get-tuple-element.93), channel_id=1, source_target_pairs={{0,4},{1,5},{2,6},{3,7},{4,12},{5,13},{6,14},{7,15},{12,8},{13,9},... | collective-permute-start | bytes 1572872 | tf_op jit(solution)/shard_map/ppermute | solution.py:52
  123.0 22.6 %collective-permute-start.25 = (bf16[256,1024]{1,0:T(8,128)(2,1)S(1)}, bf16[256,1024]{1,0:T(8,128)(2,1)S(1)}, u32[]{:S(2)}, u32[]{:S(2)}) collective-permute-start(bf16[256,1024]{1,0:T(8,128)(2,1)S(1)} %get-tuple-element.102), channel_id=1, source_target_pairs={{0,2},{1,3},{2,0},{3,1},{4,6},{5,7},{6,4},{7,5},{8,10},{9,11},{10,... | collective-permute-start | bytes 1572872 | tf_op jit(solution)/shard_map/ppermute | solution.py:49
  132.4 15.2 %collective-permute-start.26 = (bf16[256,1024]{1,0:T(8,128)(2,1)S(1)}, bf16[256,1024]{1,0:T(8,128)(2,1)S(1)}, u32[]{:S(2)}, u32[]{:S(2)}) collective-permute-start(bf16[256,1024]{1,0:T(8,128)(2,1)S(1)} %collective-permute-done.19.refs_0_), channel_id=1, source_target_pairs={{0,1},{1,0},{2,3},{3,2},{4,5},{5,4},{6,7},{7,6},{8,9},{9,8},{10,11... | collective-permute-start | bytes 1572872 | tf_op jit(solution)/shard_map/ppermute | solution.py:49
  132.4 6.4 %collective-permute-start.21 = (bf16[1,48,1024]{2,1,0:T(8,128)(2,1)S(1)}, bf16[1,48,1024]{2,1,0:T(8,128)(2,1)S(1)}, u32[]{:S(2)}, u32[]{:S(2)}) collective-permute-start(bf16[1,48,1024]{2,1,0:T(8,128)(2,1)S(1)} %get-tuple-element.100), channel_id=1, source_target_pairs={{0,4},{1,5},{2,6},{3,7},{4,0},{5,1},{6,2},{7,3},{8,12},{9,13},{10,... | collective-permute-start | bytes 294920 | tf_op jit(solution)/shard_map/ppermute | solution.py:49
  132.4 10.8 %collective-permute-start.22 = (bf16[1,48,1024]{2,1,0:T(8,128)(2,1)S(1)}, bf16[1,48,1024]{2,1,0:T(8,128)(2,1)S(1)}, u32[]{:S(2)}, u32[]{:S(2)}) collective-permute-start(bf16[1,48,1024]{2,1,0:T(8,128)(2,1)S(1)} %get-tuple-element.100), channel_id=1, source_target_pairs={{0,8},{1,9},{2,10},{3,11},{4,12},{5,13},{6,14},{7,15},{8,0},{9,1},... | collective-permute-start | bytes 294920 | tf_op jit(solution)/shard_map/ppermute | solution.py:49
  133.7 9.5 %collective-permute-start.23 = (bf16[1,48,1024]{2,1,0:T(8,128)(2,1)S(1)}, bf16[1,48,1024]{2,1,0:T(8,128)(2,1)S(1)}, u32[]{:S(2)}, u32[]{:S(2)}) collective-permute-start(bf16[1,48,1024]{2,1,0:T(8,128)(2,1)S(1)} %get-tuple-element.100), channel_id=1, source_target_pairs={{0,12},{1,13},{2,14},{3,15},{4,8},{5,9},{6,10},{7,11},{8,4},{9,5},... | collective-permute-start | bytes 294920 | tf_op jit(solution)/shard_map/ppermute | solution.py:49
  143.1 16.3 %collective-permute-start.31 = (bf16[256,1024]{1,0:T(8,128)(2,1)S(1)}, bf16[256,1024]{1,0:T(8,128)(2,1)S(1)}, u32[]{:S(2)}, u32[]{:S(2)}) collective-permute-start(bf16[256,1024]{1,0:T(8,128)(2,1)S(1)} %get-tuple-element.108), channel_id=1, source_target_pairs={{0,4},{1,5},{2,6},{3,7},{4,12},{5,13},{6,14},{7,15},{12,8},{13,9},... | collective-permute-start | bytes 1572872 | tf_op jit(solution)/shard_map/ppermute | solution.py:52
  145.6 3.5 %collective-permute-start.27 = (f32[8,128]{1,0:T(8,128)S(1)}, f32[8,128]{1,0:T(8,128)S(1)}, u32[]{:S(2)}, u32[]{:S(2)}) collective-permute-start(f32[8,128]{1,0:T(8,128)S(1)} %gathered.1.refs_0_), channel_id=1, source_target_pairs={{0,1},{1,0},{2,3},{3,2},{4,5},{5,4},{6,7},{7,6},{8,9},{9,8},{10,11... | collective-permute-start | bytes 12296 | tf_op jit(solution)/shard_map/ppermute | solution.py:49
  145.7 3.7 %collective-permute-start.28 = (f32[8,128]{1,0:T(8,128)S(1)}, f32[8,128]{1,0:T(8,128)S(1)}, u32[]{:S(2)}, u32[]{:S(2)}) collective-permute-start(f32[8,128]{1,0:T(8,128)S(1)} %gathered.1.refs_0_), channel_id=1, source_target_pairs={{0,2},{1,3},{2,0},{3,1},{4,6},{5,7},{6,4},{7,5},{8,10},{9,11},{10,... | collective-permute-start | bytes 12296 | tf_op jit(solution)/shard_map/ppermute | solution.py:49
  146.2 3.1 %collective-permute-start.29 = (f32[8,128]{1,0:T(8,128)S(1)}, f32[8,128]{1,0:T(8,128)S(1)}, u32[]{:S(2)}, u32[]{:S(2)}) collective-permute-start(f32[8,128]{1,0:T(8,128)S(1)} %gathered.1.refs_0_), channel_id=1, source_target_pairs={{0,3},{1,2},{2,1},{3,0},{4,7},{5,6},{6,5},{7,4},{8,11},{9,10},{10,... | collective-permute-start | bytes 12296 | tf_op jit(solution)/shard_map/ppermute | solution.py:49
  149.3 8.6 %collective-permute-start.30 = (bf16[256,512]{1,0:T(8,128)(2,1)S(1)}, bf16[256,512]{1,0:T(8,128)(2,1)S(1)}, u32[]{:S(2)}, u32[]{:S(2)}) collective-permute-start(bf16[256,512]{1,0:T(8,128)(2,1)S(1)} %get-tuple-element.107), channel_id=1, source_target_pairs={{0,2},{1,3},{2,0},{3,1},{4,6},{5,7},{6,4},{7,5},{8,10},{9,11},{10,... | collective-permute-start | bytes 786440 | tf_op jit(solution)/shard_map/ppermute | solution.py:49
  158.0 7.8 %collective-permute-start.34 = (bf16[4,32,1024]{2,1,0:T(8,128)(2,1)S(1)}, bf16[4,32,1024]{2,1,0:T(8,128)(2,1)S(1)}, u32[]{:S(2)}, u32[]{:S(2)}) collective-permute-start(bf16[4,32,1024]{2,1,0:T(8,128)(2,1)S(1)} %get-tuple-element.113), channel_id=1, source_target_pairs={{0,2},{1,3},{2,0},{3,1},{4,6},{5,7},{6,4},{7,5},{8,10},{9,11},{10,... | collective-permute-start | bytes 786440 | tf_op jit(solution)/shard_map/ppermute | solution.py:49
  159.5 6.4 %collective-permute-start.32 = (bf16[256,1024]{1,0:T(8,128)(2,1)S(1)}, bf16[256,1024]{1,0:T(8,128)(2,1)S(1)}, u32[]{:S(2)}, u32[]{:S(2)}) collective-permute-start(bf16[256,1024]{1,0:T(8,128)(2,1)S(1)} %collective-permute-done.31.refs_0_), channel_id=1, source_target_pairs={{0,1},{1,0},{2,3},{3,2},{4,5},{5,4},{6,7},{7,6},{8,9},{9,8},{10,11... | collective-permute-start | bytes 1572872 | tf_op jit(solution)/shard_map/ppermute | solution.py:49
  165.7 11.2 %collective-permute-start.35 = (bf16[8,32,1024]{2,1,0:T(8,128)(2,1)S(1)}, bf16[8,32,1024]{2,1,0:T(8,128)(2,1)S(1)}, u32[]{:S(2)}, u32[]{:S(2)}) collective-permute-start(bf16[8,32,1024]{2,1,0:T(8,128)(2,1)S(1)} %constant_dynamic-update-slice_fusion.4.near), channel_id=1, source_target_pairs={{0,1},{1,0},{2,3},{3,2},{4,5},{5,4},{6,7},{7,6},{8,9},{9,8},{10,11... | collective-permute-start | bytes 1572872 | tf_op jit(solution)/shard_map/ppermute | solution.py:49
  167.3 8.8 %collective-permute-start.33 = (bf16[256,512]{1,0:T(8,128)(2,1)S(1)}, bf16[256,512]{1,0:T(8,128)(2,1)S(1)}, u32[]{:S(2)}, u32[]{:S(2)}) collective-permute-start(bf16[256,512]{1,0:T(8,128)(2,1)S(1)} %get-tuple-element.110), channel_id=1, source_target_pairs={{0,2},{1,3},{2,0},{3,1},{4,6},{5,7},{6,4},{7,5},{8,10},{9,11},{10,... | collective-permute-start | bytes 786440 | tf_op jit(solution)/shard_map/ppermute | solution.py:49

commit v8 on v7

--- a/solution.py
+++ b/solution.py
@@ -358,16 +358,13 @@
         folded = [moments[:, k * rank : (k + 1) * rank] for k in range(outs // rank)]
         basis = [after(jnp.concatenate([proj_basis] + folded, axis=0), cut[0])]
         weight = [master_weight.astype(bf16)]
+        halves = [weight[0][p * height : (p + 1) * height] for p in range(parts)]
         for s in range(1, ring):
             value = basis[-1]
             if s == 2 and sides == 2:
                 value = after(value, far_grad)
-            if s == 3 and sides == 2:
-                value = after(value, acts[2])
             basis.append(onward(value))
-            if s == 1:
-                weight.append(onward(after(weight[0], basis[1])))
-        weight.append(onward(after(weight[1], basis[-1], acts[-1])))
+        halves = [onward(half if p == 0 else after(half, acts[-2])) for p, half in enumerate(halves)]
 
         acts[1] = swap(cut[1], 1)
         if sides == 2:
@@ -425,8 +422,6 @@
             return waiting[-1][1]
 
         first_block = multiply(0, weight[0], theirs[0], gate=acts[-2])
-        theirs.append(swap(after(weight[1], theirs[0]), 1))
-
         total, *gives = call(
             functools.partial(project_kernel, lay, owned, plan),
             "project",
@@ -436,13 +431,14 @@
             flops=2 * tokens * members * rank * (ring * rows + outs),
             moved=12 * 2**20,
         )
-        sent = give_back(0, first_block, gate=acts[-1])
+        halves[-1] = after(halves[-1], total)
+        weight.append(jnp.concatenate(halves, axis=0))
+        weight.append(onward(weight[1]))
+        theirs.append(swap(weight[1], 1))
 
         for k, (bit, radix) in enumerate(rounds):
-            if bit == 2 and sides == 2:
-                gives = [after(give, sent) for give in gives]
             if bit == members:
-                gives = [after(give, weight[2], block) for give in gives]
+                gives = [after(give, weight[2], sent if sides == 2 else block) for give in gives]
             came = [swap(give, j * bit) for j, give in zip(range(1, radix), gives)]
             if k == len(rounds) - 1:
                 break
@@ -458,7 +454,9 @@
             if bit == 1:
                 block = multiply(1, weight[1], theirs[1], gate=total)
             if bit == 2:
+                sent = give_back(0, first_block, gate=total)
                 later = give_back(1, block, gate=total)
+                weight[2] = after(weight[2], total)
 
         split = [weight[2][p * height : (p + 1) * height] for p in range(parts)] if ring == 4 else []
         last = []
@@ -522,7 +520,7 @@
                 functools.partial(last_kernel, lay, rows, [spot for spot, block in waiting]),
                 "last",
                 [((tokens, width), bf16)],
-                [block for spot, block in waiting] + [activation_grad],
+                [after(block, new_master) for spot, block in waiting] + [activation_grad],
                 [VMEM] * len(waiting) + [HBM],
                 [HBM],
                 scratch=[pltpu.SemaphoreType.DMA((len(waiting), 2))],

time: 179 us -> 189 us (1.056)
  waiting for transfers between devices: 119 us -> 130 us
    ppermute x7 -> x8, waiting for transfers between devices: 25.4 us -> 75.8 us  [onward(): return lax.ppermute(value, 'dp', self.forward)]
    ppermute x29, waiting for transfers between devices: 94.1 us -> 54.1 us  [swap(): return lax.ppermute(value, 'dp', [(i, i ^ bit) for i in range(self.n)])]
    ppermute x7 -> x8, starting transfers between devices: 10.4 us -> 10.7 us  [onward(): return lax.ppermute(value, 'dp', self.forward)]
  transfers between devices with their start and end apart: 36 -> 37, of which waited for: 20 -> 22; matrix products, arithmetic and copies ran while one was open for 0% -> 0% of each run, Pallas kernels for 9% -> 9%
where the time goes in v8:
time: 189 us
  waiting for transfers between devices  130 us (69%)
  starting transfers between devices  36.5 us (19%)
  Pallas kernels  18.8 us (10%)
  local copies, waits for them, and re-layouts  2.61 us (1%)
    ppermute x8, waiting for transfers between devices, onward(): return lax.ppermute(value, 'dp', self.forward)  75.8 us
    ppermute x29, waiting for transfers between devices, swap(): return lax.ppermute(value, 'dp', [(i, i ^ bit) for i in range(self.n)])  54.1 us
    ppermute x29, starting transfers between devices, swap(): return lax.ppermute(value, 'dp', [(i, i ^ bit) for i in range(self.n)])  25.8 us
    pallas_call x14, Pallas kernels, call(): pl.pallas_call(kernel, name=name, out_shape=[jax.ShapeDtypeStruct(shape,...  18.8 us
    ppermute x8, starting transfers between devices, onward(): return lax.ppermute(value, 'dp', self.forward)  10.7 us
  transfers between devices with their start and end apart: 37, of which 22 were waited for; matrix products, arithmetic and copies ran while one was open for 0% of the time, Pallas kernels for 9%

profile of v8, /device:TPU:0, one launch (start us, length us, event | category | flops | bytes accessed | tf_op | source)
XLA Modules:
  0.0 189.1 jit_solution(18394410007781999829)
XLA Ops:
  0.7 2.2 %copy-done.2 = bf16[256,8192]{1,0:T(8,128)(2,1)S(1)} copy-done((bf16[256,8192]{1,0:T(8,128)(2,1)S(1)}, bf16[256,8192]{1,0:T(8,128)(2,1)}, u32[]{:S(2)}) %copy-start.2) | copy-done | bytes 4194328
  4.0 2.6 %collective-permute-start.1 = (bf16[256,1024]{1,0:T(8,128)(2,1)S(1)}, bf16[256,1024]{1,0:T(8,128)(2,1)S(1)}, u32[]{:S(2)}, u32[]{:S(2)}) collective-permute-start(bf16[256,1024]{1,0:T(8,128)(2,1)S(1)} %copy-done), channel_id=1, source_target_pairs={{0,2},{1,3},{2,0},{3,1},{4,6},{5,7},{6,4},{7,5},{8,10},{9,11},{10,... | collective-permute-start | bytes 1572872 | tf_op jit(solution)/shard_map/ppermute | solution.py:49
  6.7 12.7 %collective-permute-done.1.refs_3_.refs_11_ = bf16[256,1024]{1,0:T(8,128)(2,1)S(1)} collective-permute-done((bf16[256,1024]{1,0:T(8,128)(2,1)S(1)}, bf16[256,1024]{1,0:T(8,128)(2,1)S(1)}, u32[]{:S(2)}, u32[]{:S(2)}) %collective-permute-start.1) | collective-permute-done | bytes 524320 | tf_op jit(solution)/shard_map/ppermute | solution.py:49
  19.6 2.1 %collective-permute-start.9 = (bf16[640,512]{1,0:T(8,128)(2,1)S(1)}, bf16[640,512]{1,0:T(8,128)(2,1)S(1)}, u32[]{:S(2)}, u32[]{:S(2)}) collective-permute-start(bf16[640,512]{1,0:T(8,128)(2,1)S(1)} %fusion.refs_5_.refs_4_), channel_id=1, source_target_pairs={{0,4},{1,5},{2,6},{3,7},{4,12},{5,13},{6,14},{7,15},{12,8},{13,9},... | collective-permute-start | bytes 1966088 | tf_op jit(solution)/shard_map/ppermute | solution.py:52
  21.7 16.4 %collective-permute-done.9.refs_6_.refs_5_ = bf16[640,512]{1,0:T(8,128)(2,1)S(1)} collective-permute-done((bf16[640,512]{1,0:T(8,128)(2,1)S(1)}, bf16[640,512]{1,0:T(8,128)(2,1)S(1)}, u32[]{:S(2)}, u32[]{:S(2)}) %collective-permute-start.9) | collective-permute-done | bytes 655392 | tf_op jit(solution)/shard_map/ppermute | solution.py:52
  38.1 0.8 collective-permute-start.10
  39.1 2.5 %collective-permute-done.6.refs_2_ = bf16[256,2048]{1,0:T(8,128)(2,1)S(1)} collective-permute-done((bf16[256,2048]{1,0:T(8,128)(2,1)S(1)}, bf16[256,2048]{1,0:T(8,128)(2,1)S(1)}, u32[]{:S(2)}, u32[]{:S(2)}) %collective-permute-start.6) | collective-permute-done | bytes 1048608 | tf_op jit(solution)/shard_map/ppermute | solution.py:49
  41.6 1.9 collective-permute-start
  43.5 1.4 collective-permute-start.2
  44.8 11.7 %collective-permute-done.10.refs_7_.refs_6_ = bf16[640,512]{1,0:T(8,128)(2,1)S(1)} collective-permute-done((bf16[640,512]{1,0:T(8,128)(2,1)S(1)}, bf16[640,512]{1,0:T(8,128)(2,1)S(1)}, u32[]{:S(2)}, u32[]{:S(2)}) %collective-permute-start.10) | collective-permute-done | bytes 655392 | tf_op jit(solution)/shard_map/ppermute | solution.py:52
  56.6 0.9 collective-permute-start.11
  57.5 10.4 %collective-permute-done = bf16[256,1024]{1,0:T(8,128)(2,1)S(1)} collective-permute-done((bf16[256,1024]{1,0:T(8,128)(2,1)S(1)}, bf16[256,1024]{1,0:T(8,128)(2,1)S(1)}, u32[]{:S(2)}, u32[]{:S(2)}) %collective-permute-start) | collective-permute-done | bytes 524320 | tf_op jit(solution)/shard_map/ppermute | solution.py:52
  67.9 0.9 collective-permute-start.3
  68.9 2.1 %weight.5 = (bf16[256,8192]{1,0:T(8,128)(2,1)}, bf16[256,1024]{1,0:T(8,128)(2,1)S(1)}) custom-call(bf16[512,1024]{1,0:T(8,128)(2,1)S(1)} %convert_element_type.4.refs_0_, bf16[512,1024]{1,0:T(8,128)(2,1)S(1)} %collective-permute-done.7.refs_1_, bf16[256,1024]{1,0:T(8,128)(2,1)S(1)} %copy-done, bf16[256,1024]{1,0:T(8,128)(2,1)S(1)} %collective-permute-done.1.refs_3_.refs_11_), custom_call_target="tpu_custom_call" | custom-call | flops 1073741824 | bytes 6291456 | tf_op jit(solution)/shard_map/weight/pallas_call | solution.py:310
  71.6 10.3 %collective-permute-done.11.refs_8_.refs_7_ = bf16[640,512]{1,0:T(8,128)(2,1)S(1)} collective-permute-done((bf16[640,512]{1,0:T(8,128)(2,1)S(1)}, bf16[640,512]{1,0:T(8,128)(2,1)S(1)}, u32[]{:S(2)}, u32[]{:S(2)}) %collective-permute-start.11) | collective-permute-done | bytes 655392 | tf_op jit(solution)/shard_map/ppermute | solution.py:52
  81.9 4.3 %project.1 = (f32[8,32,1024]{2,1,0:T(8,128)S(1)}, bf16[8,32,1024]{2,1,0:T(8,128)(2,1)S(1)}) custom-call(bf16[256,2048]{1,0:T(8,128)(2,1)S(1)} %get-tuple-element.70.refs_0_, bf16[256,2048]{1,0:T(8,128)(2,1)S(1)} %collective-permute-done.4.refs_1_, bf16[256,2048]{1,0:T(8,128)(2,1)S(1)} %collective-permute-done.6.refs_2_, ...), custom_call_target="tpu_custom_call" | custom-call | flops 3221225472 | bytes 12582912 | tf_op jit(solution)/shard_map/project/pallas_call | solution.py:310
  86.2 5.8 %collective-permute-done.3 = bf16[256,1024]{1,0:T(8,128)(2,1)S(1)} collective-permute-done((bf16[256,1024]{1,0:T(8,128)(2,1)S(1)}, bf16[256,1024]{1,0:T(8,128)(2,1)S(1)}, u32[]{:S(2)}, u32[]{:S(2)}) %collective-permute-start.3) | collective-permute-done | bytes 524320 | tf_op jit(solution)/shard_map/ppermute | solution.py:52
  93.3 1.4 collective-permute-done.13.refs_1_
  94.8 1.6 collective-permute-start.14
  96.4 6.8 %collective-permute-done.14.refs_1_ = bf16[4,32,1024]{2,1,0:T(8,128)(2,1)S(1)} collective-permute-done((bf16[4,32,1024]{2,1,0:T(8,128)(2,1)S(1)}, bf16[4,32,1024]{2,1,0:T(8,128)(2,1)S(1)}, u32[]{:S(2)}, u32[]{:S(2)}) %collective-permute-start.14) | collective-permute-done | bytes 262176 | tf_op jit(solution)/shard_map/ppermute | solution.py:49
  103.2 1.6 collective-permute-start.15
  104.8 12.3 %collective-permute-done.12.refs_0_ = bf16[512,1024]{1,0:T(8,128)(2,1)S(1)} collective-permute-done((bf16[512,1024]{1,0:T(8,128)(2,1)S(1)}, bf16[512,1024]{1,0:T(8,128)(2,1)S(1)}, u32[]{:S(2)}, u32[]{:S(2)}) %collective-permute-start.12) | collective-permute-done | bytes 1048608 | tf_op jit(solution)/shard_map/ppermute | solution.py:52
  117.1 2.1 %weight.6 = (bf16[256,8192]{1,0:T(8,128)(2,1)}, bf16[256,1024]{1,0:T(8,128)(2,1)S(1)}) custom-call(bf16[512,1024]{1,0:T(8,128)(2,1)S(1)} %constant_dynamic-update-slice_fusion.refs_0_, bf16[512,1024]{1,0:T(8,128)(2,1)S(1)} %collective-permute-done.21.refs_1_, bf16[256,1024]{1,0:T(8,128)(2,1)S(1)} %copy-done, ...), custom_call_target="tpu_custom_call", output_to_operand_aliasing={{0}: (4, {})} | custom-call | flops 1073741824 | bytes 6291456 | tf_op jit(solution)/shard_map/weight/pallas_call | solution.py:310
  119.3 1.2 collective-permute-start.25
  120.5 3.6 %collective-permute-start.18 = (bf16[1,32,1024]{2,1,0:T(8,128)(2,1)S(1)}, bf16[1,32,1024]{2,1,0:T(8,128)(2,1)S(1)}, u32[]{:S(2)}, u32[]{:S(2)}) collective-permute-start(bf16[1,32,1024]{2,1,0:T(8,128)(2,1)S(1)} %get-tuple-element.88), channel_id=1, source_target_pairs={{0,12},{1,13},{2,14},{3,15},{4,8},{5,9},{6,10},{7,11},{8,4},{9,5},... | collective-permute-start | bytes 196616 | tf_op jit(solution)/shard_map/ppermute | solution.py:49
  124.9 2.3 %collective-permute-done.18.refs_3_ = bf16[1,32,1024]{2,1,0:T(8,128)(2,1)S(1)} collective-permute-done((bf16[1,32,1024]{2,1,0:T(8,128)(2,1)S(1)}, bf16[1,32,1024]{2,1,0:T(8,128)(2,1)S(1)}, u32[]{:S(2)}, u32[]{:S(2)}) %collective-permute-start.18) | collective-permute-done | bytes 65568 | tf_op jit(solution)/shard_map/ppermute | solution.py:49
  127.2 2.3 %collective-permute-done.17.refs_2_ = bf16[1,32,1024]{2,1,0:T(8,128)(2,1)S(1)} collective-permute-done((bf16[1,32,1024]{2,1,0:T(8,128)(2,1)S(1)}, bf16[1,32,1024]{2,1,0:T(8,128)(2,1)S(1)}, u32[]{:S(2)}, u32[]{:S(2)}) %collective-permute-start.17) | collective-permute-done | bytes 65568 | tf_op jit(solution)/shard_map/ppermute | solution.py:49
  129.7 1.4 collective-permute-start.19
  131.4 2.1 %weight.7 = (bf16[256,8192]{1,0:T(8,128)(2,1)}, bf16[256,1024]{1,0:T(8,128)(2,1)S(1)}) custom-call(bf16[512,1024]{1,0:T(8,128)(2,1)S(1)} %collective-permute-done.12.refs_0_, bf16[512,1024]{1,0:T(8,128)(2,1)S(1)} %collective-permute-done.20.refs_1_, bf16[256,1024]{1,0:T(8,128)(2,1)S(1)} %copy-done, ...), custom_call_target="tpu_custom_call", output_to_operand_aliasing={{0}: (5, {})} | custom-call | flops 1073741824 | bytes 6291456 | tf_op jit(solution)/shard_map/weight/pallas_call | solution.py:310
  133.7 1.1 collective-permute-start.26
  134.8 8.8 %collective-permute-done.19.refs_0_ = bf16[256,1024]{1,0:T(8,128)(2,1)S(1)} collective-permute-done((bf16[256,1024]{1,0:T(8,128)(2,1)S(1)}, bf16[256,1024]{1,0:T(8,128)(2,1)S(1)}, u32[]{:S(2)}, u32[]{:S(2)}) %collective-permute-start.19) | collective-permute-done | bytes 524320 | tf_op jit(solution)/shard_map/ppermute | solution.py:52
  144.4 2.8 %collective-permute-start.23 = (bf16[1,48,1024]{2,1,0:T(8,128)(2,1)S(1)}, bf16[1,48,1024]{2,1,0:T(8,128)(2,1)S(1)}, u32[]{:S(2)}, u32[]{:S(2)}) collective-permute-start(bf16[1,48,1024]{2,1,0:T(8,128)(2,1)S(1)} %get-tuple-element.97), channel_id=1, source_target_pairs={{0,8},{1,9},{2,10},{3,11},{4,12},{5,13},{6,14},{7,15},{8,0},{9,1},... | collective-permute-start | bytes 294920 | tf_op jit(solution)/shard_map/ppermute | solution.py:49
  147.1 0.9 collective-permute-start.24
  148.0 2.5 %collective-permute-done.22 = bf16[1,48,1024]{2,1,0:T(8,128)(2,1)S(1)} collective-permute-done((bf16[1,48,1024]{2,1,0:T(8,128)(2,1)S(1)}, bf16[1,48,1024]{2,1,0:T(8,128)(2,1)S(1)}, u32[]{:S(2)}, u32[]{:S(2)}) %collective-permute-start.22) | collective-permute-done | bytes 98336 | tf_op jit(solution)/shard_map/ppermute | solution.py:49
  150.5 4.6 %collective-permute-done.23 = bf16[1,48,1024]{2,1,0:T(8,128)(2,1)S(1)} collective-permute-done((bf16[1,48,1024]{2,1,0:T(8,128)(2,1)S(1)}, bf16[1,48,1024]{2,1,0:T(8,128)(2,1)S(1)}, u32[]{:S(2)}, u32[]{:S(2)}) %collective-permute-start.23) | collective-permute-done | bytes 98336 | tf_op jit(solution)/shard_map/ppermute | solution.py:49
  155.2 2.1 %collective-permute-start.34 = (bf16[256,1024]{1,0:T(8,128)(2,1)S(1)}, bf16[256,1024]{1,0:T(8,128)(2,1)S(1)}, u32[]{:S(2)}, u32[]{:S(2)}) collective-permute-start(bf16[256,1024]{1,0:T(8,128)(2,1)S(1)} %get-tuple-element.109), channel_id=1, source_target_pairs={{0,4},{1,5},{2,6},{3,7},{4,12},{5,13},{6,14},{7,15},{12,8},{13,9},... | collective-permute-start | bytes 1572872 | tf_op jit(solution)/shard_map/ppermute | solution.py:52
  158.2 1.2 collective-permute-start.30
  159.4 1.5 weight.8
  161.2 1.4 collective-permute-start.31
  162.6 1.1 moment.1
  163.7 6.1 %collective-permute-done.31.refs_0_ = bf16[256,512]{1,0:T(8,128)(2,1)S(1)} collective-permute-done((bf16[256,512]{1,0:T(8,128)(2,1)S(1)}, bf16[256,512]{1,0:T(8,128)(2,1)S(1)}, u32[]{:S(2)}, u32[]{:S(2)}) %collective-permute-start.31) | collective-permute-done | bytes 262176 | tf_op jit(solution)/shard_map/ppermute | solution.py:49
  169.9 1.4 collective-permute-start.32
  171.3 6.4 %collective-permute-done.32 = bf16[4,32,1024]{2,1,0:T(8,128)(2,1)S(1)} collective-permute-done((bf16[4,32,1024]{2,1,0:T(8,128)(2,1)S(1)}, bf16[4,32,1024]{2,1,0:T(8,128)(2,1)S(1)}, u32[]{:S(2)}, u32[]{:S(2)}) %collective-permute-start.32) | collective-permute-done | bytes 262176 | tf_op jit(solution)/shard_map/ppermute | solution.py:49
  177.9 1.5 weight.9
  179.4 1.5 collective-permute-start.36
  180.9 2.2 %back.1 = f32[512,1024]{1,0:T(8,128)} custom-call(bf16[512,512]{1,0:T(8,128)(2,1)S(1)} %copy-done.3, bf16[8,32,1024]{2,1,0:T(8,128)(2,1)S(1)} %constant_dynamic-update-slice_fusion.6.near, bf16[8,32,1024]{2,1,0:T(8,128)(2,1)S(1)} %collective-permute-done.33.other, f32[512,1024]{1,0:T(8,128)S(1)} %copy-done.1), custom_call_target="tpu_custom_call" | custom-call | flops 536870912 | bytes 8388608 | tf_op jit(solution)/shard_map/back/pallas_call | solution.py:310
  183.1 5.1 %collective-permute-done.36.refs_1_ = bf16[256,512]{1,0:T(8,128)(2,1)S(1)} collective-permute-done((bf16[256,512]{1,0:T(8,128)(2,1)S(1)}, bf16[256,512]{1,0:T(8,128)(2,1)S(1)}, u32[]{:S(2)}, u32[]{:S(2)}) %collective-permute-start.36) | collective-permute-done | bytes 262176 | tf_op jit(solution)/shard_map/ppermute | solution.py:49
  188.1 0.8 last.1
  (69 shorter events, 7.3 us)
Async XLA Ops:
  0.6 3.3 %copy-start = (bf16[256,1024]{1,0:T(8,128)(2,1)S(1)}, bf16[256,1024]{1,0:T(8,128)(2,1)}, u32[]{:S(2)}) copy-start(bf16[256,1024]{1,0:T(8,128)(2,1)} %refs_2_.9) | copy-start | bytes 1572868
  0.6 2.2 %copy-start.2 = (bf16[256,8192]{1,0:T(8,128)(2,1)S(1)}, bf16[256,8192]{1,0:T(8,128)(2,1)}, u32[]{:S(2)}) copy-start(bf16[256,8192]{1,0:T(8,128)(2,1)} %act.1) | copy-start | bytes 12582916
  2.9 16.6 %copy-start.5 = (f32[32,1024]{1,0:T(8,128)S(1)}, f32[32,1024]{1,0:T(8,128)}, u32[]{:S(2)}) copy-start(f32[32,1024]{1,0:T(8,128)} %refs_9_.3) | copy-start | bytes 393220
  2.9 16.6 %copy-start.4 = (f32[32,1024]{1,0:T(8,128)S(1)}, f32[32,1024]{1,0:T(8,128)}, u32[]{:S(2)}) copy-start(f32[32,1024]{1,0:T(8,128)} %refs_10_.1) | copy-start | bytes 393220
  3.4 16.1 %copy-start.3 = (bf16[512,512]{1,0:T(8,128)(2,1)S(1)}, bf16[512,512]{1,0:T(8,128)(2,1)}, u32[]{:S(2)}) copy-start(bf16[512,512]{1,0:T(8,128)(2,1)} %basis.1) | copy-start | bytes 1572868
  3.4 35.5 %copy-start.1 = (f32[512,1024]{1,0:T(8,128)S(1)}, f32[512,1024]{1,0:T(8,128)}, u32[]{:S(2)}) copy-start(f32[512,1024]{1,0:T(8,128)} %master.1) | copy-start | bytes 6291460
  3.4 3.2 %collective-permute-start.4 = (bf16[256,2048]{1,0:T(8,128)(2,1)S(1)}, bf16[256,2048]{1,0:T(8,128)(2,1)S(1)}, u32[]{:S(2)}, u32[]{:S(2)}) collective-permute-start(bf16[256,2048]{1,0:T(8,128)(2,1)S(1)} %get-tuple-element.65), channel_id=1, source_target_pairs={{0,1},{1,0},{2,3},{3,2},{4,5},{5,4},{6,7},{7,6},{8,9},{9,8},{10,11... | collective-permute-start | bytes 3145736 | tf_op jit(solution)/shard_map/ppermute | solution.py:49
  4.0 15.4 %collective-permute-start.1 = (bf16[256,1024]{1,0:T(8,128)(2,1)S(1)}, bf16[256,1024]{1,0:T(8,128)(2,1)S(1)}, u32[]{:S(2)}, u32[]{:S(2)}) collective-permute-start(bf16[256,1024]{1,0:T(8,128)(2,1)S(1)} %copy-done), channel_id=1, source_target_pairs={{0,2},{1,3},{2,0},{3,1},{4,6},{5,7},{6,4},{7,5},{8,10},{9,11},{10,... | collective-permute-start | bytes 1572872 | tf_op jit(solution)/shard_map/ppermute | solution.py:49
  6.6 35.0 %collective-permute-start.6 = (bf16[256,2048]{1,0:T(8,128)(2,1)S(1)}, bf16[256,2048]{1,0:T(8,128)(2,1)S(1)}, u32[]{:S(2)}, u32[]{:S(2)}) collective-permute-start(bf16[256,2048]{1,0:T(8,128)(2,1)S(1)} %get-tuple-element.67), channel_id=1, source_target_pairs={{0,2},{1,3},{2,0},{3,1},{4,6},{5,7},{6,4},{7,5},{8,10},{9,11},{10,... | collective-permute-start | bytes 3145736 | tf_op jit(solution)/shard_map/ppermute | solution.py:49
  19.4 22.1 %collective-permute-start.5 = (bf16[512,1024]{1,0:T(8,128)(2,1)S(1)}, bf16[512,1024]{1,0:T(8,128)(2,1)S(1)}, u32[]{:S(2)}, u32[]{:S(2)}) collective-permute-start(bf16[512,1024]{1,0:T(8,128)(2,1)S(1)} %pad_maximum_fusion), channel_id=1, source_target_pairs={{0,1},{1,0},{2,3},{3,2},{4,5},{5,4},{6,7},{7,6},{8,9},{9,8},{10,11... | collective-permute-start | bytes 3145736 | tf_op jit(solution)/shard_map/ppermute | solution.py:49
  19.6 18.5 %collective-permute-start.9 = (bf16[640,512]{1,0:T(8,128)(2,1)S(1)}, bf16[640,512]{1,0:T(8,128)(2,1)S(1)}, u32[]{:S(2)}, u32[]{:S(2)}) collective-permute-start(bf16[640,512]{1,0:T(8,128)(2,1)S(1)} %fusion.refs_5_.refs_4_), channel_id=1, source_target_pairs={{0,4},{1,5},{2,6},{3,7},{4,12},{5,13},{6,14},{7,15},{12,8},{13,9},... | collective-permute-start | bytes 1966088 | tf_op jit(solution)/shard_map/ppermute | solution.py:52
  38.1 18.5 %collective-permute-start.10 = (bf16[640,512]{1,0:T(8,128)(2,1)S(1)}, bf16[640,512]{1,0:T(8,128)(2,1)S(1)}, u32[]{:S(2)}, u32[]{:S(2)}) collective-permute-start(bf16[640,512]{1,0:T(8,128)(2,1)S(1)} %collective-permute-done.9.refs_6_.refs_5_), channel_id=1, source_target_pairs={{0,4},{1,5},{2,6},{3,7},{4,12},{5,13},{6,14},{7,15},{12,8},{13,9},... | collective-permute-start | bytes 1966088 | tf_op jit(solution)/shard_map/ppermute | solution.py:52
  41.6 27.3 %collective-permute-start.7 = (bf16[512,1024]{1,0:T(8,128)(2,1)S(1)}, bf16[512,1024]{1,0:T(8,128)(2,1)S(1)}, u32[]{:S(2)}, u32[]{:S(2)}) collective-permute-start(bf16[512,1024]{1,0:T(8,128)(2,1)S(1)} %convert_element_type.4.refs_0_), channel_id=1, source_target_pairs={{0,1},{1,0},{2,3},{3,2},{4,5},{5,4},{6,7},{7,6},{8,9},{9,8},{10,11... | collective-permute-start | bytes 3145736 | tf_op jit(solution)/shard_map/ppermute | solution.py:49
  41.6 26.2 %collective-permute-start = (bf16[256,1024]{1,0:T(8,128)(2,1)S(1)}, bf16[256,1024]{1,0:T(8,128)(2,1)S(1)}, u32[]{:S(2)}, u32[]{:S(2)}) collective-permute-start(bf16[256,1024]{1,0:T(8,128)(2,1)S(1)} %get-tuple-element.121), channel_id=1, source_target_pairs={{0,4},{1,5},{2,6},{3,7},{4,12},{5,13},{6,14},{7,15},{12,8},{13,9},... | collective-permute-start | bytes 1572872 | tf_op jit(solution)/shard_map/ppermute | solution.py:52
  43.5 24.4 %collective-permute-start.2 = (bf16[256,1024]{1,0:T(8,128)(2,1)S(1)}, bf16[256,1024]{1,0:T(8,128)(2,1)S(1)}, u32[]{:S(2)}, u32[]{:S(2)}) collective-permute-start(bf16[256,1024]{1,0:T(8,128)(2,1)S(1)} %get-tuple-element.61), channel_id=1, source_target_pairs={{0,3},{1,2},{2,1},{3,0},{4,7},{5,6},{6,5},{7,4},{8,11},{9,10},{10,... | collective-permute-start | bytes 1572872 | tf_op jit(solution)/shard_map/ppermute | solution.py:49
  56.6 25.3 %collective-permute-start.11 = (bf16[640,512]{1,0:T(8,128)(2,1)S(1)}, bf16[640,512]{1,0:T(8,128)(2,1)S(1)}, u32[]{:S(2)}, u32[]{:S(2)}) collective-permute-start(bf16[640,512]{1,0:T(8,128)(2,1)S(1)} %collective-permute-done.10.refs_7_.refs_6_), channel_id=1, source_target_pairs={{0,4},{1,5},{2,6},{3,7},{4,12},{5,13},{6,14},{7,15},{12,8},{13,9},... | collective-permute-start | bytes 1966088 | tf_op jit(solution)/shard_map/ppermute | solution.py:52
  57.5 14.1 %collective-permute-start.8 = (bf16[256,1024]{1,0:T(8,128)(2,1)S(1)}, bf16[256,1024]{1,0:T(8,128)(2,1)S(1)}, u32[]{:S(2)}, u32[]{:S(2)}) collective-permute-start(bf16[256,1024]{1,0:T(8,128)(2,1)S(1)} %get-tuple-element.72), channel_id=1, source_target_pairs={{0,3},{1,2},{2,1},{3,0},{4,7},{5,6},{6,5},{7,4},{8,11},{9,10},{10,... | collective-permute-start | bytes 1572872 | tf_op jit(solution)/shard_map/ppermute | solution.py:49
  67.9 24.2 %collective-permute-start.3 = (bf16[256,1024]{1,0:T(8,128)(2,1)S(1)}, bf16[256,1024]{1,0:T(8,128)(2,1)S(1)}, u32[]{:S(2)}, u32[]{:S(2)}) collective-permute-start(bf16[256,1024]{1,0:T(8,128)(2,1)S(1)} %get-tuple-element.62), channel_id=1, source_target_pairs={{0,4},{1,5},{2,6},{3,7},{4,12},{5,13},{6,14},{7,15},{12,8},{13,9},... | collective-permute-start | bytes 1572872 | tf_op jit(solution)/shard_map/ppermute | solution.py:52
  92.1 25.1 %collective-permute-start.12 = (bf16[512,1024]{1,0:T(8,128)(2,1)S(1)}, bf16[512,1024]{1,0:T(8,128)(2,1)S(1)}, u32[]{:S(2)}, u32[]{:S(2)}) collective-permute-start(bf16[512,1024]{1,0:T(8,128)(2,1)S(1)} %constant_dynamic-update-slice_fusion.refs_0_), channel_id=1, source_target_pairs={{0,4},{1,5},{2,6},{3,7},{4,12},{5,13},{6,14},{7,15},{12,8},{13,9},... | collective-permute-start | bytes 3145736 | tf_op jit(solution)/shard_map/ppermute | solution.py:52
  92.8 1.9 %collective-permute-start.13 = (bf16[8,32,1024]{2,1,0:T(8,128)(2,1)S(1)}, bf16[8,32,1024]{2,1,0:T(8,128)(2,1)S(1)}, u32[]{:S(2)}, u32[]{:S(2)}) collective-permute-start(bf16[8,32,1024]{2,1,0:T(8,128)(2,1)S(1)} %get-tuple-element.77), channel_id=1, source_target_pairs={{0,1},{1,0},{2,3},{3,2},{4,5},{5,4},{6,7},{7,6},{8,9},{9,8},{10,11... | collective-permute-start | bytes 1572872 | tf_op jit(solution)/shard_map/ppermute | solution.py:49
  92.8 24.4 %collective-permute-start.21 = (bf16[512,1024]{1,0:T(8,128)(2,1)S(1)}, bf16[512,1024]{1,0:T(8,128)(2,1)S(1)}, u32[]{:S(2)}, u32[]{:S(2)}) collective-permute-start(bf16[512,1024]{1,0:T(8,128)(2,1)S(1)} %constant_dynamic-update-slice_fusion.refs_0_), channel_id=1, source_target_pairs={{0,1},{1,0},{2,3},{3,2},{4,5},{5,4},{6,7},{7,6},{8,9},{9,8},{10,11... | collective-permute-start | bytes 3145736 | tf_op jit(solution)/shard_map/ppermute | solution.py:49
  94.8 8.4 %collective-permute-start.14 = (bf16[4,32,1024]{2,1,0:T(8,128)(2,1)S(1)}, bf16[4,32,1024]{2,1,0:T(8,128)(2,1)S(1)}, u32[]{:S(2)}, u32[]{:S(2)}) collective-permute-start(bf16[4,32,1024]{2,1,0:T(8,128)(2,1)S(1)} %get-tuple-element.79), channel_id=1, source_target_pairs={{0,2},{1,3},{2,0},{3,1},{4,6},{5,7},{6,4},{7,5},{8,10},{9,11},{10,... | collective-permute-start | bytes 786440 | tf_op jit(solution)/shard_map/ppermute | solution.py:49
  103.2 17.2 %collective-permute-start.15 = (bf16[256,1024]{1,0:T(8,128)(2,1)S(1)}, bf16[256,1024]{1,0:T(8,128)(2,1)S(1)}, u32[]{:S(2)}, u32[]{:S(2)}) collective-permute-start(bf16[256,1024]{1,0:T(8,128)(2,1)S(1)} %get-tuple-element.83), channel_id=1, source_target_pairs={{0,2},{1,3},{2,0},{3,1},{4,6},{5,7},{6,4},{7,5},{8,10},{9,11},{10,... | collective-permute-start | bytes 1572872 | tf_op jit(solution)/shard_map/ppermute | solution.py:49
  117.1 14.2 %collective-permute-start.20 = (bf16[512,1024]{1,0:T(8,128)(2,1)S(1)}, bf16[512,1024]{1,0:T(8,128)(2,1)S(1)}, u32[]{:S(2)}, u32[]{:S(2)}) collective-permute-start(bf16[512,1024]{1,0:T(8,128)(2,1)S(1)} %collective-permute-done.12.refs_0_), channel_id=1, source_target_pairs={{0,1},{1,0},{2,3},{3,2},{4,5},{5,4},{6,7},{7,6},{8,9},{9,8},{10,11... | collective-permute-start | bytes 3145736 | tf_op jit(solution)/shard_map/ppermute | solution.py:49
  119.3 14.4 %collective-permute-start.25 = (bf16[256,1024]{1,0:T(8,128)(2,1)S(1)}, bf16[256,1024]{1,0:T(8,128)(2,1)S(1)}, u32[]{:S(2)}, u32[]{:S(2)}) collective-permute-start(bf16[256,1024]{1,0:T(8,128)(2,1)S(1)} %get-tuple-element.99), channel_id=1, source_target_pairs={{0,2},{1,3},{2,0},{3,1},{4,6},{5,7},{6,4},{7,5},{8,10},{9,11},{10,... | collective-permute-start | bytes 1572872 | tf_op jit(solution)/shard_map/ppermute | solution.py:49
  120.5 6.7 %collective-permute-start.18 = (bf16[1,32,1024]{2,1,0:T(8,128)(2,1)S(1)}, bf16[1,32,1024]{2,1,0:T(8,128)(2,1)S(1)}, u32[]{:S(2)}, u32[]{:S(2)}) collective-permute-start(bf16[1,32,1024]{2,1,0:T(8,128)(2,1)S(1)} %get-tuple-element.88), channel_id=1, source_target_pairs={{0,12},{1,13},{2,14},{3,15},{4,8},{5,9},{6,10},{7,11},{8,4},{9,5},... | collective-permute-start | bytes 196616 | tf_op jit(solution)/shard_map/ppermute | solution.py:49
  124.1 5.4 %collective-permute-start.17 = (bf16[1,32,1024]{2,1,0:T(8,128)(2,1)S(1)}, bf16[1,32,1024]{2,1,0:T(8,128)(2,1)S(1)}, u32[]{:S(2)}, u32[]{:S(2)}) collective-permute-start(bf16[1,32,1024]{2,1,0:T(8,128)(2,1)S(1)} %get-tuple-element.86), channel_id=1, source_target_pairs={{0,8},{1,9},{2,10},{3,11},{4,12},{5,13},{6,14},{7,15},{8,0},{9,1},... | collective-permute-start | bytes 196616 | tf_op jit(solution)/shard_map/ppermute | solution.py:49
  124.1 5.7 %collective-permute-start.16 = (bf16[1,32,1024]{2,1,0:T(8,128)(2,1)S(1)}, bf16[1,32,1024]{2,1,0:T(8,128)(2,1)S(1)}, u32[]{:S(2)}, u32[]{:S(2)}) collective-permute-start(bf16[1,32,1024]{2,1,0:T(8,128)(2,1)S(1)} %get-tuple-element.84), channel_id=1, source_target_pairs={{0,4},{1,5},{2,6},{3,7},{4,0},{5,1},{6,2},{7,3},{8,12},{9,13},{10,... | collective-permute-start | bytes 196616 | tf_op jit(solution)/shard_map/ppermute | solution.py:49
  129.7 13.9 %collective-permute-start.19 = (bf16[256,1024]{1,0:T(8,128)(2,1)S(1)}, bf16[256,1024]{1,0:T(8,128)(2,1)S(1)}, u32[]{:S(2)}, u32[]{:S(2)}) collective-permute-start(bf16[256,1024]{1,0:T(8,128)(2,1)S(1)} %get-tuple-element.89), channel_id=1, source_target_pairs={{0,4},{1,5},{2,6},{3,7},{4,12},{5,13},{6,14},{7,15},{12,8},{13,9},... | collective-permute-start | bytes 1572872 | tf_op jit(solution)/shard_map/ppermute | solution.py:52
  133.7 23.8 %collective-permute-start.26 = (bf16[256,1024]{1,0:T(8,128)(2,1)S(1)}, bf16[256,1024]{1,0:T(8,128)(2,1)S(1)}, u32[]{:S(2)}, u32[]{:S(2)}) collective-permute-start(bf16[256,1024]{1,0:T(8,128)(2,1)S(1)} %get-tuple-element.100), channel_id=1, source_target_pairs={{0,2},{1,3},{2,0},{3,1},{4,6},{5,7},{6,4},{7,5},{8,10},{9,11},{10,... | collective-permute-start | bytes 1572872 | tf_op jit(solution)/shard_map/ppermute | solution.py:49
  143.6 15.7 %collective-permute-start.27 = (bf16[256,1024]{1,0:T(8,128)(2,1)S(1)}, bf16[256,1024]{1,0:T(8,128)(2,1)S(1)}, u32[]{:S(2)}, u32[]{:S(2)}) collective-permute-start(bf16[256,1024]{1,0:T(8,128)(2,1)S(1)} %collective-permute-done.19.refs_0_), channel_id=1, source_target_pairs={{0,1},{1,0},{2,3},{3,2},{4,5},{5,4},{6,7},{7,6},{8,9},{9,8},{10,11... | collective-permute-start | bytes 1572872 | tf_op jit(solution)/shard_map/ppermute | solution.py:49
  143.6 6.9 %collective-permute-start.22 = (bf16[1,48,1024]{2,1,0:T(8,128)(2,1)S(1)}, bf16[1,48,1024]{2,1,0:T(8,128)(2,1)S(1)}, u32[]{:S(2)}, u32[]{:S(2)}) collective-permute-start(bf16[1,48,1024]{2,1,0:T(8,128)(2,1)S(1)} %get-tuple-element.97), channel_id=1, source_target_pairs={{0,4},{1,5},{2,6},{3,7},{4,0},{5,1},{6,2},{7,3},{8,12},{9,13},{10,... | collective-permute-start | bytes 294920 | tf_op jit(solution)/shard_map/ppermute | solution.py:49
  144.4 10.8 %collective-permute-start.23 = (bf16[1,48,1024]{2,1,0:T(8,128)(2,1)S(1)}, bf16[1,48,1024]{2,1,0:T(8,128)(2,1)S(1)}, u32[]{:S(2)}, u32[]{:S(2)}) collective-permute-start(bf16[1,48,1024]{2,1,0:T(8,128)(2,1)S(1)} %get-tuple-element.97), channel_id=1, source_target_pairs={{0,8},{1,9},{2,10},{3,11},{4,12},{5,13},{6,14},{7,15},{8,0},{9,1},... | collective-permute-start | bytes 294920 | tf_op jit(solution)/shard_map/ppermute | solution.py:49
  147.1 8.0 %collective-permute-start.24 = (bf16[1,48,1024]{2,1,0:T(8,128)(2,1)S(1)}, bf16[1,48,1024]{2,1,0:T(8,128)(2,1)S(1)}, u32[]{:S(2)}, u32[]{:S(2)}) collective-permute-start(bf16[1,48,1024]{2,1,0:T(8,128)(2,1)S(1)} %get-tuple-element.97), channel_id=1, source_target_pairs={{0,12},{1,13},{2,14},{3,15},{4,8},{5,9},{6,10},{7,11},{8,4},{9,5},... | collective-permute-start | bytes 294920 | tf_op jit(solution)/shard_map/ppermute | solution.py:49
  155.2 16.2 %collective-permute-start.34 = (bf16[256,1024]{1,0:T(8,128)(2,1)S(1)}, bf16[256,1024]{1,0:T(8,128)(2,1)S(1)}, u32[]{:S(2)}, u32[]{:S(2)}) collective-permute-start(bf16[256,1024]{1,0:T(8,128)(2,1)S(1)} %get-tuple-element.109), channel_id=1, source_target_pairs={{0,4},{1,5},{2,6},{3,7},{4,12},{5,13},{6,14},{7,15},{12,8},{13,9},... | collective-permute-start | bytes 1572872 | tf_op jit(solution)/shard_map/ppermute | solution.py:52
  157.4 3.4 %collective-permute-start.28 = (f32[8,128]{1,0:T(8,128)S(1)}, f32[8,128]{1,0:T(8,128)S(1)}, u32[]{:S(2)}, u32[]{:S(2)}) collective-permute-start(f32[8,128]{1,0:T(8,128)S(1)} %gathered.1.refs_0_), channel_id=1, source_target_pairs={{0,1},{1,0},{2,3},{3,2},{4,5},{5,4},{6,7},{7,6},{8,9},{9,8},{10,11... | collective-permute-start | bytes 12296 | tf_op jit(solution)/shard_map/ppermute | solution.py:49
  157.5 3.7 %collective-permute-start.29 = (f32[8,128]{1,0:T(8,128)S(1)}, f32[8,128]{1,0:T(8,128)S(1)}, u32[]{:S(2)}, u32[]{:S(2)}) collective-permute-start(f32[8,128]{1,0:T(8,128)S(1)} %gathered.1.refs_0_), channel_id=1, source_target_pairs={{0,2},{1,3},{2,0},{3,1},{4,6},{5,7},{6,4},{7,5},{8,10},{9,11},{10,... | collective-permute-start | bytes 12296 | tf_op jit(solution)/shard_map/ppermute | solution.py:49
  158.2 3.0 %collective-permute-start.30 = (f32[8,128]{1,0:T(8,128)S(1)}, f32[8,128]{1,0:T(8,128)S(1)}, u32[]{:S(2)}, u32[]{:S(2)}) collective-permute-start(f32[8,128]{1,0:T(8,128)S(1)} %gathered.1.refs_0_), channel_id=1, source_target_pairs={{0,3},{1,2},{2,1},{3,0},{4,7},{5,6},{6,5},{7,4},{8,11},{9,10},{10,... | collective-permute-start | bytes 12296 | tf_op jit(solution)/shard_map/ppermute | solution.py:49
  161.2 8.7 %collective-permute-start.31 = (bf16[256,512]{1,0:T(8,128)(2,1)S(1)}, bf16[256,512]{1,0:T(8,128)(2,1)S(1)}, u32[]{:S(2)}, u32[]{:S(2)}) collective-permute-start(bf16[256,512]{1,0:T(8,128)(2,1)S(1)} %get-tuple-element.105), channel_id=1, source_target_pairs={{0,2},{1,3},{2,0},{3,1},{4,6},{5,7},{6,4},{7,5},{8,10},{9,11},{10,... | collective-permute-start | bytes 786440 | tf_op jit(solution)/shard_map/ppermute | solution.py:49
  169.9 7.9 %collective-permute-start.32 = (bf16[4,32,1024]{2,1,0:T(8,128)(2,1)S(1)}, bf16[4,32,1024]{2,1,0:T(8,128)(2,1)S(1)}, u32[]{:S(2)}, u32[]{:S(2)}) collective-permute-start(bf16[4,32,1024]{2,1,0:T(8,128)(2,1)S(1)} %get-tuple-element.107), channel_id=1, source_target_pairs={{0,2},{1,3},{2,0},{3,1},{4,6},{5,7},{6,4},{7,5},{8,10},{9,11},{10,... | collective-permute-start | bytes 786440 | tf_op jit(solution)/shard_map/ppermute | solution.py:49
  171.3 6.6 %collective-permute-start.35 = (bf16[256,1024]{1,0:T(8,128)(2,1)S(1)}, bf16[256,1024]{1,0:T(8,128)(2,1)S(1)}, u32[]{:S(2)}, u32[]{:S(2)}) collective-permute-start(bf16[256,1024]{1,0:T(8,128)(2,1)S(1)} %collective-permute-done.34.refs_0_), channel_id=1, source_target_pairs={{0,1},{1,0},{2,3},{3,2},{4,5},{5,4},{6,7},{7,6},{8,9},{9,8},{10,11... | collective-permute-start | bytes 1572872 | tf_op jit(solution)/shard_map/ppermute | solution.py:49
  177.8 3.1 %collective-permute-start.33 = (bf16[8,32,1024]{2,1,0:T(8,128)(2,1)S(1)}, bf16[8,32,1024]{2,1,0:T(8,128)(2,1)S(1)}, u32[]{:S(2)}, u32[]{:S(2)}) collective-permute-start(bf16[8,32,1024]{2,1,0:T(8,128)(2,1)S(1)} %constant_dynamic-update-slice_fusion.6.near), channel_id=1, source_target_pairs={{0,1},{1,0},{2,3},{3,2},{4,5},{5,4},{6,7},{7,6},{8,9},{9,8},{10,11... | collective-permute-start | bytes 1572872 | tf_op jit(solution)/shard_map/ppermute | solution.py:49
  179.4 8.8 %collective-permute-start.36 = (bf16[256,512]{1,0:T(8,128)(2,1)S(1)}, bf16[256,512]{1,0:T(8,128)(2,1)S(1)}, u32[]{:S(2)}, u32[]{:S(2)}) collective-permute-start(bf16[256,512]{1,0:T(8,128)(2,1)S(1)} %get-tuple-element.111), channel_id=1, source_target_pairs={{0,2},{1,3},{2,0},{3,1},{4,6},{5,7},{6,4},{7,5},{8,10},{9,11},{10,... | collective-permute-start | bytes 786440 | tf_op jit(solution)/shard_map/ppermute | solution.py:49

commit v9 on v8

--- a/solution.py
+++ b/solution.py
@@ -63,7 +63,7 @@
     return value + bit - 2 * bit * ((value // bit) % 2)
 
 
-def cut_kernel(lay, rows, plan, act, *refs):
+def cut_kernel(lay, rows, plan, act, key_grad, *refs):
     pieces, sems = refs[:-1], refs[-1]
     index = lax.axis_index("dp")
     member = index % lay.members
@@ -82,6 +82,14 @@
                     sems.at[len(copies)],
                 )
             )
+    if lay.sides == 2:
+        copies.append(
+            pltpu.make_async_copy(
+                key_grad,
+                pieces[2].at[:, pl.ds(lay.ring * rows, key_grad.shape[1])],
+                sems.at[len(copies)],
+            )
+        )
     for copy in copies:
         copy.start()
     for copy in copies:
@@ -334,46 +342,35 @@
         parts = 2 if rows % 256 == 0 else 1
         height = rows // parts
 
-        plan = [(x, 0, ring) for x in range(min(members, 3))]
-        if sides == 2:
-            plan += [(3, 0, ring // 2), (3, ring // 2, ring // 2)]
+        plan = [(x, 0, ring) for x in range(members)]
+        wides = [ring * rows + (outs if x == 2 else 0) for x in range(members)]
         cut = call(
             functools.partial(cut_kernel, lay, rows, plan),
             "cut",
-            [((tokens, count * rows), bf16) for x, first, count in plan],
-            [activations],
-            in_specs=[HBM],
-            scratch=[pltpu.SemaphoreType.DMA((members * ring,))],
+            [((tokens, wide), bf16) for wide in wides],
+            [activations, key_grad],
+            in_specs=[HBM, HBM],
+            scratch=[pltpu.SemaphoreType.DMA((members * ring + 1,))],
             moved=4 * tokens * ring * rows * members,
         )
 
-        acts = list(cut)
-        far_grad = None
-        if sides == 2:
-            far_grad = swap(key_grad, 2)
-            acts[2] = swap(cut[2], 2)
-            acts[3] = swap(after(cut[3], far_grad), 3)
-            acts[4] = swap(after(cut[4], acts[2]), 3)
+        acts = [cut[0]] + [swap(cut[x], x) for x in range(1, members)]
         moments = jnp.concatenate([first_moment, second_moment], axis=0).astype(bf16)
         folded = [moments[:, k * rank : (k + 1) * rank] for k in range(outs // rank)]
         basis = [after(jnp.concatenate([proj_basis] + folded, axis=0), cut[0])]
+        for s in range(1, ring):
+            basis.append(onward(basis[-1]))
         weight = [master_weight.astype(bf16)]
-        halves = [weight[0][p * height : (p + 1) * height] for p in range(parts)]
-        for s in range(1, ring):
-            value = basis[-1]
-            if s == 2 and sides == 2:
-                value = after(value, far_grad)
-            basis.append(onward(value))
-        halves = [onward(half if p == 0 else after(half, acts[-2])) for p, half in enumerate(halves)]
-
-        acts[1] = swap(cut[1], 1)
+        weight.append(onward(after(weight[0], basis[-1])))
+
         if sides == 2:
-            near = swap(jnp.concatenate([after(key_grad, acts[1]), far_grad], axis=0), 1)
+            far_grad = acts[2][:, ring * rows :]
+            near = swap(jnp.concatenate([key_grad, far_grad], axis=0), 1)
             grads = [key_grad, near[:tokens], far_grad, near[tokens:]]
         else:
             near = swap(key_grad, 1)
             grads = [key_grad, near]
-        theirs = [swap(after(weight[0], near, acts[min(members, 3) - 1]), 1)]
+        theirs = [swap(after(weight[0], basis[1]), 1)]
 
         side_grads = [key_grad, far_grad] if sides == 2 else [key_grad]
         state = {"out": None}
@@ -421,7 +418,7 @@
             waiting.append(((s, low), swap(block if gate is None else after(block, gate), 2)))
             return waiting[-1][1]
 
-        first_block = multiply(0, weight[0], theirs[0], gate=acts[-2])
+        first_block = multiply(0, weight[0], theirs[0])
         total, *gives = call(
             functools.partial(project_kernel, lay, owned, plan),
             "project",
@@ -431,8 +428,6 @@
             flops=2 * tokens * members * rank * (ring * rows + outs),
             moved=12 * 2**20,
         )
-        halves[-1] = after(halves[-1], total)
-        weight.append(jnp.concatenate(halves, axis=0))
         weight.append(onward(weight[1]))
         theirs.append(swap(weight[1], 1))
 

time: 189 us -> 173 us (0.915)
  waiting for transfers between devices: 130 us -> 119 us
  starting transfers between devices: 36.5 us -> 30 us
    ppermute x8 -> x7, waiting for transfers between devices: 75.8 us -> 63.8 us  [onward(): return lax.ppermute(value, 'dp', self.forward)]
    ppermute x8 -> x7, starting transfers between devices: 10.7 us -> 7.42 us  [onward(): return lax.ppermute(value, 'dp', self.forward)]
    ppermute x29 -> x27, starting transfers between devices: 25.8 us -> 22.5 us  [swap(): return lax.ppermute(value, 'dp', [(i, i ^ bit) for i in range(self.n)])]
    ppermute x29 -> x27, waiting for transfers between devices: 54.1 us -> 54.8 us  [swap(): return lax.ppermute(value, 'dp', [(i, i ^ bit) for i in range(self.n)])]
  transfers between devices with their start and end apart: 37 -> 34, of which waited for: 22 -> 20; matrix products, arithmetic and copies ran while one was open for 0% -> 0% of each run, Pallas kernels for 9% -> 10%
where the time goes in v9:
time: 173 us; the launch traced here: 172 us
  waiting for transfers between devices  119 us (69%)
  starting transfers between devices  30 us (17%)
  Pallas kernels  18.9 us (11%)
  local copies, waits for them, and re-layouts  3.48 us (2%)
    ppermute x7, waiting for transfers between devices, onward(): return lax.ppermute(value, 'dp', self.forward)  63.8 us
    ppermute x27, waiting for transfers between devices, swap(): return lax.ppermute(value, 'dp', [(i, i ^ bit) for i in range(self.n)])  54.8 us
    ppermute x27, starting transfers between devices, swap(): return lax.ppermute(value, 'dp', [(i, i ^ bit) for i in range(self.n)])  22.5 us
    pallas_call x14, Pallas kernels, call(): pl.pallas_call(kernel, name=name, out_shape=[jax.ShapeDtypeStruct(shape,...  18.9 us
    ppermute x7, starting transfers between devices, onward(): return lax.ppermute(value, 'dp', self.forward)  7.42 us
  transfers between devices with their start and end apart: 34, of which 20 were waited for; matrix products, arithmetic and copies ran while one was open for 0% of the time, Pallas kernels for 10%

profile of v9, /device:TPU:0, one launch (start us, length us, event | category | flops | bytes accessed | tf_op | source)
XLA Modules:
  0.0 172.4 jit_solution(4841386081779324011)
XLA Ops:
  0.6 1.0 copy-done
  1.7 2.2 %copy-done.3 = bf16[256,8192]{1,0:T(8,128)(2,1)S(1)} copy-done((bf16[256,8192]{1,0:T(8,128)(2,1)S(1)}, bf16[256,8192]{1,0:T(8,128)(2,1)}, u32[]{:S(2)}) %copy-start.3) | copy-done | bytes 4194328
  3.9 0.7 cut.1
  4.5 3.0 %collective-permute-start.6 = (bf16[256,3072]{1,0:T(8,128)(2,1)S(1)}, bf16[256,3072]{1,0:T(8,128)(2,1)S(1)}, u32[]{:S(2)}, u32[]{:S(2)}) collective-permute-start(bf16[256,3072]{1,0:T(8,128)(2,1)S(1)} %get-tuple-element.57), channel_id=1, source_target_pairs={{0,2},{1,3},{2,0},{3,1},{4,6},{5,7},{6,4},{7,5},{8,10},{9,11},{10,... | collective-permute-start | bytes 4718600 | tf_op jit(solution)/shard_map/ppermute | solution.py:49
  7.7 1.6 collective-permute-start
  9.3 15.5 %collective-permute-done.refs_5_ = bf16[640,512]{1,0:T(8,128)(2,1)S(1)} collective-permute-done((bf16[640,512]{1,0:T(8,128)(2,1)S(1)}, bf16[640,512]{1,0:T(8,128)(2,1)S(1)}, u32[]{:S(2)}, u32[]{:S(2)}) %collective-permute-start) | collective-permute-done | bytes 655392 | tf_op jit(solution)/shard_map/ppermute | solution.py:52
  24.8 0.8 collective-permute-start.1
  25.9 15.1 %collective-permute-done.1.refs_6_ = bf16[640,512]{1,0:T(8,128)(2,1)S(1)} collective-permute-done((bf16[640,512]{1,0:T(8,128)(2,1)S(1)}, bf16[640,512]{1,0:T(8,128)(2,1)S(1)}, u32[]{:S(2)}, u32[]{:S(2)}) %collective-permute-start.1) | collective-permute-done | bytes 655392 | tf_op jit(solution)/shard_map/ppermute | solution.py:52
  41.0 0.8 collective-permute-start.2
  42.2 0.5 collective-permute-start.7
  42.7 1.4 collective-permute-start.8
  44.1 12.2 %collective-permute-done.2.refs_7_ = bf16[640,512]{1,0:T(8,128)(2,1)S(1)} collective-permute-done((bf16[640,512]{1,0:T(8,128)(2,1)S(1)}, bf16[640,512]{1,0:T(8,128)(2,1)S(1)}, u32[]{:S(2)}, u32[]{:S(2)}) %collective-permute-start.2) | collective-permute-done | bytes 655392 | tf_op jit(solution)/shard_map/ppermute | solution.py:52
  56.3 0.8 collective-permute-start.3
  57.1 2.1 %weight.5 = (bf16[256,8192]{1,0:T(8,128)(2,1)}, bf16[256,1024]{1,0:T(8,128)(2,1)S(1)}) custom-call(bf16[512,1024]{1,0:T(8,128)(2,1)S(1)} %convert_element_type.4.refs_0_, bf16[512,1024]{1,0:T(8,128)(2,1)S(1)} %collective-permute-done.5.refs_1_, bf16[256,1024]{1,0:T(8,128)(2,1)S(1)} %copy-done, bf16[256,1024]{1,0:T(8,128)(2,1)S(1)} %slice.30.refs_3_.refs_10_), custom_call_target="tpu_custom_call" | custom-call | flops 1073741824 | bytes 6291456 | tf_op jit(solution)/shard_map/weight/pallas_call | solution.py:318
  59.3 8.5 %collective-permute-done.8.refs_3_ = bf16[256,2048]{1,0:T(8,128)(2,1)S(1)} collective-permute-done((bf16[256,2048]{1,0:T(8,128)(2,1)S(1)}, bf16[256,2048]{1,0:T(8,128)(2,1)S(1)}, u32[]{:S(2)}, u32[]{:S(2)}) %collective-permute-start.8) | collective-permute-done | bytes 1048608 | tf_op jit(solution)/shard_map/ppermute | solution.py:49
  67.8 4.3 %project.1 = (f32[8,32,1024]{2,1,0:T(8,128)S(1)}, bf16[8,32,1024]{2,1,0:T(8,128)(2,1)S(1)}) custom-call(bf16[256,2048]{1,0:T(8,128)(2,1)S(1)} %get-tuple-element.59.refs_0_, bf16[256,2048]{1,0:T(8,128)(2,1)S(1)} %collective-permute-done.7.refs_1_, bf16[256,3072]{1,0:T(8,128)(2,1)S(1)} %collective-permute-done.6.refs_2_, ...), custom_call_target="tpu_custom_call" | custom-call | flops 3221225472 | bytes 12582912 | tf_op jit(solution)/shard_map/project/pallas_call | solution.py:318
  72.6 6.9 %collective-permute-done.3.refs_0_ = bf16[512,1024]{1,0:T(8,128)(2,1)S(1)} collective-permute-done((bf16[512,1024]{1,0:T(8,128)(2,1)S(1)}, bf16[512,1024]{1,0:T(8,128)(2,1)S(1)}, u32[]{:S(2)}, u32[]{:S(2)}) %collective-permute-start.3) | collective-permute-done | bytes 1048608 | tf_op jit(solution)/shard_map/ppermute | solution.py:52
  79.6 0.8 collective-permute-start.4
  80.5 1.0 collective-permute-start.11
  81.5 7.7 %collective-permute-done.11.refs_1_ = bf16[4,32,1024]{2,1,0:T(8,128)(2,1)S(1)} collective-permute-done((bf16[4,32,1024]{2,1,0:T(8,128)(2,1)S(1)}, bf16[4,32,1024]{2,1,0:T(8,128)(2,1)S(1)}, u32[]{:S(2)}, u32[]{:S(2)}) %collective-permute-start.11) | collective-permute-done | bytes 262176 | tf_op jit(solution)/shard_map/ppermute | solution.py:49
  89.3 1.0 collective-permute-start.12
  90.3 11.1 %collective-permute-done.4.refs_0_ = bf16[512,1024]{1,0:T(8,128)(2,1)S(1)} collective-permute-done((bf16[512,1024]{1,0:T(8,128)(2,1)S(1)}, bf16[512,1024]{1,0:T(8,128)(2,1)S(1)}, u32[]{:S(2)}, u32[]{:S(2)}) %collective-permute-start.4) | collective-permute-done | bytes 1048608 | tf_op jit(solution)/shard_map/ppermute | solution.py:52
  101.5 1.4 collective-permute-done.12.refs_4_
  102.9 2.8 %collective-permute-start.15 = (bf16[1,32,1024]{2,1,0:T(8,128)(2,1)S(1)}, bf16[1,32,1024]{2,1,0:T(8,128)(2,1)S(1)}, u32[]{:S(2)}, u32[]{:S(2)}) collective-permute-start(bf16[1,32,1024]{2,1,0:T(8,128)(2,1)S(1)} %get-tuple-element.74), channel_id=1, source_target_pairs={{0,12},{1,13},{2,14},{3,15},{4,8},{5,9},{6,10},{7,11},{8,4},{9,5},... | collective-permute-start | bytes 196616 | tf_op jit(solution)/shard_map/ppermute | solution.py:49
  105.7 2.0 %collective-permute-start.14 = (bf16[1,32,1024]{2,1,0:T(8,128)(2,1)S(1)}, bf16[1,32,1024]{2,1,0:T(8,128)(2,1)S(1)}, u32[]{:S(2)}, u32[]{:S(2)}) collective-permute-start(bf16[1,32,1024]{2,1,0:T(8,128)(2,1)S(1)} %get-tuple-element.72), channel_id=1, source_target_pairs={{0,8},{1,9},{2,10},{3,11},{4,12},{5,13},{6,14},{7,15},{8,0},{9,1},... | collective-permute-start | bytes 196616 | tf_op jit(solution)/shard_map/ppermute | solution.py:49
  107.8 2.1 %weight.6 = (bf16[256,8192]{1,0:T(8,128)(2,1)}, bf16[256,1024]{1,0:T(8,128)(2,1)S(1)}) custom-call(bf16[512,1024]{1,0:T(8,128)(2,1)S(1)} %collective-permute-done.3.refs_0_, bf16[512,1024]{1,0:T(8,128)(2,1)S(1)} %collective-permute-done.18.refs_1_, bf16[256,1024]{1,0:T(8,128)(2,1)S(1)} %copy-done.1, ...), custom_call_target="tpu_custom_call", output_to_operand_aliasing={{0}: (4, {})} | custom-call | flops 1073741824 | bytes 6291456 | tf_op jit(solution)/shard_map/weight/pallas_call | solution.py:318
  109.9 1.0 collective-permute-start.22
  111.0 1.3 collective-permute-done.14.refs_2_
  113.3 2.1 %weight.7 = (bf16[256,8192]{1,0:T(8,128)(2,1)}, bf16[256,1024]{1,0:T(8,128)(2,1)S(1)}) custom-call(bf16[512,1024]{1,0:T(8,128)(2,1)S(1)} %collective-permute-done.4.refs_0_, bf16[512,1024]{1,0:T(8,128)(2,1)S(1)} %collective-permute-done.17.refs_1_, bf16[256,1024]{1,0:T(8,128)(2,1)S(1)} %copy-done.1, ...), custom_call_target="tpu_custom_call", output_to_operand_aliasing={{0}: (5, {})} | custom-call | flops 1073741824 | bytes 6291456 | tf_op jit(solution)/shard_map/weight/pallas_call | solution.py:318
  115.5 6.6 %collective-permute-done.22.refs_4_ = bf16[256,1024]{1,0:T(8,128)(2,1)S(1)} collective-permute-done((bf16[256,1024]{1,0:T(8,128)(2,1)S(1)}, bf16[256,1024]{1,0:T(8,128)(2,1)S(1)}, u32[]{:S(2)}, u32[]{:S(2)}) %collective-permute-start.22) | collective-permute-done | bytes 524320 | tf_op jit(solution)/shard_map/ppermute | solution.py:49
  122.1 1.1 collective-permute-start.23
  123.2 2.9 %collective-permute-done.16.refs_0_ = bf16[256,1024]{1,0:T(8,128)(2,1)S(1)} collective-permute-done((bf16[256,1024]{1,0:T(8,128)(2,1)S(1)}, bf16[256,1024]{1,0:T(8,128)(2,1)S(1)}, u32[]{:S(2)}, u32[]{:S(2)}) %collective-permute-start.16) | collective-permute-done | bytes 524320 | tf_op jit(solution)/shard_map/ppermute | solution.py:52
  126.1 1.6 collective-permute-start.20
  127.7 2.8 %collective-permute-start.21 = (bf16[1,48,1024]{2,1,0:T(8,128)(2,1)S(1)}, bf16[1,48,1024]{2,1,0:T(8,128)(2,1)S(1)}, u32[]{:S(2)}, u32[]{:S(2)}) collective-permute-start(bf16[1,48,1024]{2,1,0:T(8,128)(2,1)S(1)} %get-tuple-element.83), channel_id=1, source_target_pairs={{0,12},{1,13},{2,14},{3,15},{4,8},{5,9},{6,10},{7,11},{8,4},{9,5},... | collective-permute-start | bytes 294920 | tf_op jit(solution)/shard_map/ppermute | solution.py:49
  130.5 2.0 %collective-permute-done.19 = bf16[1,48,1024]{2,1,0:T(8,128)(2,1)S(1)} collective-permute-done((bf16[1,48,1024]{2,1,0:T(8,128)(2,1)S(1)}, bf16[1,48,1024]{2,1,0:T(8,128)(2,1)S(1)}, u32[]{:S(2)}, u32[]{:S(2)}) %collective-permute-start.19) | collective-permute-done | bytes 98336 | tf_op jit(solution)/shard_map/ppermute | solution.py:49
  132.5 4.3 %collective-permute-done.20 = bf16[1,48,1024]{2,1,0:T(8,128)(2,1)S(1)} collective-permute-done((bf16[1,48,1024]{2,1,0:T(8,128)(2,1)S(1)}, bf16[1,48,1024]{2,1,0:T(8,128)(2,1)S(1)}, u32[]{:S(2)}, u32[]{:S(2)}) %collective-permute-start.20) | collective-permute-done | bytes 98336 | tf_op jit(solution)/shard_map/ppermute | solution.py:49
  136.9 2.3 %collective-permute-start.31 = (bf16[256,1024]{1,0:T(8,128)(2,1)S(1)}, bf16[256,1024]{1,0:T(8,128)(2,1)S(1)}, u32[]{:S(2)}, u32[]{:S(2)}) collective-permute-start(bf16[256,1024]{1,0:T(8,128)(2,1)S(1)} %get-tuple-element.95), channel_id=1, source_target_pairs={{0,4},{1,5},{2,6},{3,7},{4,12},{5,13},{6,14},{7,15},{12,8},{13,9},... | collective-permute-start | bytes 1572872 | tf_op jit(solution)/shard_map/ppermute | solution.py:52
  139.4 2.0 %collective-permute-start.26 = (f32[8,128]{1,0:T(8,128)S(1)}, f32[8,128]{1,0:T(8,128)S(1)}, u32[]{:S(2)}, u32[]{:S(2)}) collective-permute-start(f32[8,128]{1,0:T(8,128)S(1)} %gathered.1.refs_0_), channel_id=1, source_target_pairs={{0,2},{1,3},{2,0},{3,1},{4,6},{5,7},{6,4},{7,5},{8,10},{9,11},{10,... | collective-permute-start | bytes 12296 | tf_op jit(solution)/shard_map/ppermute | solution.py:49
  141.5 1.5 weight.8
  143.1 1.4 collective-permute-done.27.refs_3_
  144.4 0.6 collective-permute-start.28
  145.0 1.1 moment.1
  146.1 7.0 %collective-permute-done.28.refs_0_ = bf16[256,512]{1,0:T(8,128)(2,1)S(1)} collective-permute-done((bf16[256,512]{1,0:T(8,128)(2,1)S(1)}, bf16[256,512]{1,0:T(8,128)(2,1)S(1)}, u32[]{:S(2)}, u32[]{:S(2)}) %collective-permute-start.28) | collective-permute-done | bytes 262176 | tf_op jit(solution)/shard_map/ppermute | solution.py:49
  153.4 7.6 %collective-permute-done.29 = bf16[4,32,1024]{2,1,0:T(8,128)(2,1)S(1)} collective-permute-done((bf16[4,32,1024]{2,1,0:T(8,128)(2,1)S(1)}, bf16[4,32,1024]{2,1,0:T(8,128)(2,1)S(1)}, u32[]{:S(2)}, u32[]{:S(2)}) %collective-permute-start.29) | collective-permute-done | bytes 262176 | tf_op jit(solution)/shard_map/ppermute | solution.py:49
  161.1 1.5 weight.9
  163.0 2.2 %back.1 = f32[512,1024]{1,0:T(8,128)} custom-call(bf16[512,512]{1,0:T(8,128)(2,1)S(1)} %copy-done.4, bf16[8,32,1024]{2,1,0:T(8,128)(2,1)S(1)} %constant_dynamic-update-slice_fusion.4.near, bf16[8,32,1024]{2,1,0:T(8,128)(2,1)S(1)} %collective-permute-done.30.other, f32[512,1024]{1,0:T(8,128)S(1)} %copy-done.2), custom_call_target="tpu_custom_call" | custom-call | flops 536870912 | bytes 8388608 | tf_op jit(solution)/shard_map/back/pallas_call | solution.py:318
  165.2 6.2 %collective-permute-done.33.refs_1_ = bf16[256,512]{1,0:T(8,128)(2,1)S(1)} collective-permute-done((bf16[256,512]{1,0:T(8,128)(2,1)S(1)}, bf16[256,512]{1,0:T(8,128)(2,1)S(1)}, u32[]{:S(2)}, u32[]{:S(2)}) %collective-permute-start.33) | collective-permute-done | bytes 262176 | tf_op jit(solution)/shard_map/ppermute | solution.py:49
  171.4 0.8 last.1
  (63 shorter events, 3.6 us)
Async XLA Ops:
  0.6 1.0 copy-start
  1.7 2.2 %copy-start.3 = (bf16[256,8192]{1,0:T(8,128)(2,1)S(1)}, bf16[256,8192]{1,0:T(8,128)(2,1)}, u32[]{:S(2)}) copy-start(bf16[256,8192]{1,0:T(8,128)(2,1)} %act.1) | copy-start | bytes 12582916
  3.9 3.7 %copy-start.6 = (f32[32,1024]{1,0:T(8,128)S(1)}, f32[32,1024]{1,0:T(8,128)}, u32[]{:S(2)}) copy-start(f32[32,1024]{1,0:T(8,128)} %refs_9_.1) | copy-start | bytes 393220
  3.9 3.7 %copy-start.5 = (f32[32,1024]{1,0:T(8,128)S(1)}, f32[32,1024]{1,0:T(8,128)}, u32[]{:S(2)}) copy-start(f32[32,1024]{1,0:T(8,128)} %refs_10_.1) | copy-start | bytes 393220
  3.9 3.8 %copy-start.4 = (bf16[512,512]{1,0:T(8,128)(2,1)S(1)}, bf16[512,512]{1,0:T(8,128)(2,1)}, u32[]{:S(2)}) copy-start(bf16[512,512]{1,0:T(8,128)(2,1)} %basis.1) | copy-start | bytes 1572868
  3.9 21.7 %copy-start.2 = (f32[512,1024]{1,0:T(8,128)S(1)}, f32[512,1024]{1,0:T(8,128)}, u32[]{:S(2)}) copy-start(f32[512,1024]{1,0:T(8,128)} %master.1) | copy-start | bytes 6291460
  4.5 37.4 %collective-permute-start.6 = (bf16[256,3072]{1,0:T(8,128)(2,1)S(1)}, bf16[256,3072]{1,0:T(8,128)(2,1)S(1)}, u32[]{:S(2)}, u32[]{:S(2)}) collective-permute-start(bf16[256,3072]{1,0:T(8,128)(2,1)S(1)} %get-tuple-element.57), channel_id=1, source_target_pairs={{0,2},{1,3},{2,0},{3,1},{4,6},{5,7},{6,4},{7,5},{8,10},{9,11},{10,... | collective-permute-start | bytes 4718600 | tf_op jit(solution)/shard_map/ppermute | solution.py:49
  7.7 17.1 %collective-permute-start = (bf16[640,512]{1,0:T(8,128)(2,1)S(1)}, bf16[640,512]{1,0:T(8,128)(2,1)S(1)}, u32[]{:S(2)}, u32[]{:S(2)}) collective-permute-start(bf16[640,512]{1,0:T(8,128)(2,1)S(1)} %fusion.refs_4_), channel_id=1, source_target_pairs={{0,4},{1,5},{2,6},{3,7},{4,12},{5,13},{6,14},{7,15},{12,8},{13,9},... | collective-permute-start | bytes 1966088 | tf_op jit(solution)/shard_map/ppermute | solution.py:52
  24.8 16.2 %collective-permute-start.1 = (bf16[640,512]{1,0:T(8,128)(2,1)S(1)}, bf16[640,512]{1,0:T(8,128)(2,1)S(1)}, u32[]{:S(2)}, u32[]{:S(2)}) collective-permute-start(bf16[640,512]{1,0:T(8,128)(2,1)S(1)} %collective-permute-done.refs_5_), channel_id=1, source_target_pairs={{0,4},{1,5},{2,6},{3,7},{4,12},{5,13},{6,14},{7,15},{12,8},{13,9},... | collective-permute-start | bytes 1966088 | tf_op jit(solution)/shard_map/ppermute | solution.py:52
  25.8 31.3 %collective-permute-start.5 = (bf16[512,1024]{1,0:T(8,128)(2,1)S(1)}, bf16[512,1024]{1,0:T(8,128)(2,1)S(1)}, u32[]{:S(2)}, u32[]{:S(2)}) collective-permute-start(bf16[512,1024]{1,0:T(8,128)(2,1)S(1)} %convert_element_type.4.refs_0_), channel_id=1, source_target_pairs={{0,1},{1,0},{2,3},{3,2},{4,5},{5,4},{6,7},{7,6},{8,9},{9,8},{10,11... | collective-permute-start | bytes 3145736 | tf_op jit(solution)/shard_map/ppermute | solution.py:49
  41.0 15.3 %collective-permute-start.2 = (bf16[640,512]{1,0:T(8,128)(2,1)S(1)}, bf16[640,512]{1,0:T(8,128)(2,1)S(1)}, u32[]{:S(2)}, u32[]{:S(2)}) collective-permute-start(bf16[640,512]{1,0:T(8,128)(2,1)S(1)} %collective-permute-done.1.refs_6_), channel_id=1, source_target_pairs={{0,4},{1,5},{2,6},{3,7},{4,12},{5,13},{6,14},{7,15},{12,8},{13,9},... | collective-permute-start | bytes 1966088 | tf_op jit(solution)/shard_map/ppermute | solution.py:52
  42.1 17.1 %collective-permute-start.9 = (bf16[512,1024]{1,0:T(8,128)(2,1)S(1)}, bf16[512,1024]{1,0:T(8,128)(2,1)S(1)}, u32[]{:S(2)}, u32[]{:S(2)}) collective-permute-start(bf16[512,1024]{1,0:T(8,128)(2,1)S(1)} %pad_maximum_fusion), channel_id=1, source_target_pairs={{0,1},{1,0},{2,3},{3,2},{4,5},{5,4},{6,7},{7,6},{8,9},{9,8},{10,11... | collective-permute-start | bytes 3145736 | tf_op jit(solution)/shard_map/ppermute | solution.py:49
  42.2 17.1 %collective-permute-start.7 = (bf16[256,2048]{1,0:T(8,128)(2,1)S(1)}, bf16[256,2048]{1,0:T(8,128)(2,1)S(1)}, u32[]{:S(2)}, u32[]{:S(2)}) collective-permute-start(bf16[256,2048]{1,0:T(8,128)(2,1)S(1)} %get-tuple-element.60), channel_id=1, source_target_pairs={{0,1},{1,0},{2,3},{3,2},{4,5},{5,4},{6,7},{7,6},{8,9},{9,8},{10,11... | collective-permute-start | bytes 3145736 | tf_op jit(solution)/shard_map/ppermute | solution.py:49
  42.7 25.2 %copy-start.1 = (bf16[256,1024]{1,0:T(8,128)(2,1)S(1)}, bf16[256,1024]{1,0:T(8,128)(2,1)}, u32[]{:S(2)}) copy-start(bf16[256,1024]{1,0:T(8,128)(2,1)} %refs_2_.9) | copy-start | bytes 1572868
  42.7 25.2 %collective-permute-start.8 = (bf16[256,2048]{1,0:T(8,128)(2,1)S(1)}, bf16[256,2048]{1,0:T(8,128)(2,1)S(1)}, u32[]{:S(2)}, u32[]{:S(2)}) collective-permute-start(bf16[256,2048]{1,0:T(8,128)(2,1)S(1)} %get-tuple-element.61), channel_id=1, source_target_pairs={{0,3},{1,2},{2,1},{3,0},{4,7},{5,6},{6,5},{7,4},{8,11},{9,10},{10,... | collective-permute-start | bytes 3145736 | tf_op jit(solution)/shard_map/ppermute | solution.py:49
  56.3 23.3 %collective-permute-start.3 = (bf16[512,1024]{1,0:T(8,128)(2,1)S(1)}, bf16[512,1024]{1,0:T(8,128)(2,1)S(1)}, u32[]{:S(2)}, u32[]{:S(2)}) collective-permute-start(bf16[512,1024]{1,0:T(8,128)(2,1)S(1)} %convert_element_type.4.refs_0_), channel_id=1, source_target_pairs={{0,4},{1,5},{2,6},{3,7},{4,12},{5,13},{6,14},{7,15},{12,8},{13,9},... | collective-permute-start | bytes 3145736 | tf_op jit(solution)/shard_map/ppermute | solution.py:52
  72.2 8.2 %collective-permute-start.10 = (bf16[8,32,1024]{2,1,0:T(8,128)(2,1)S(1)}, bf16[8,32,1024]{2,1,0:T(8,128)(2,1)S(1)}, u32[]{:S(2)}, u32[]{:S(2)}) collective-permute-start(bf16[8,32,1024]{2,1,0:T(8,128)(2,1)S(1)} %get-tuple-element.63), channel_id=1, source_target_pairs={{0,1},{1,0},{2,3},{3,2},{4,5},{5,4},{6,7},{7,6},{8,9},{9,8},{10,11... | collective-permute-start | bytes 1572872 | tf_op jit(solution)/shard_map/ppermute | solution.py:49
  79.6 21.9 %collective-permute-start.4 = (bf16[512,1024]{1,0:T(8,128)(2,1)S(1)}, bf16[512,1024]{1,0:T(8,128)(2,1)S(1)}, u32[]{:S(2)}, u32[]{:S(2)}) collective-permute-start(bf16[512,1024]{1,0:T(8,128)(2,1)S(1)} %collective-permute-done.3.refs_0_), channel_id=1, source_target_pairs={{0,4},{1,5},{2,6},{3,7},{4,12},{5,13},{6,14},{7,15},{12,8},{13,9},... | collective-permute-start | bytes 3145736 | tf_op jit(solution)/shard_map/ppermute | solution.py:52
  80.4 27.4 %collective-permute-start.18 = (bf16[512,1024]{1,0:T(8,128)(2,1)S(1)}, bf16[512,1024]{1,0:T(8,128)(2,1)S(1)}, u32[]{:S(2)}, u32[]{:S(2)}) collective-permute-start(bf16[512,1024]{1,0:T(8,128)(2,1)S(1)} %collective-permute-done.3.refs_0_), channel_id=1, source_target_pairs={{0,1},{1,0},{2,3},{3,2},{4,5},{5,4},{6,7},{7,6},{8,9},{9,8},{10,11... | collective-permute-start | bytes 3145736 | tf_op jit(solution)/shard_map/ppermute | solution.py:49
  80.5 8.8 %collective-permute-start.11 = (bf16[4,32,1024]{2,1,0:T(8,128)(2,1)S(1)}, bf16[4,32,1024]{2,1,0:T(8,128)(2,1)S(1)}, u32[]{:S(2)}, u32[]{:S(2)}) collective-permute-start(bf16[4,32,1024]{2,1,0:T(8,128)(2,1)S(1)} %get-tuple-element.65), channel_id=1, source_target_pairs={{0,2},{1,3},{2,0},{3,1},{4,6},{5,7},{6,4},{7,5},{8,10},{9,11},{10,... | collective-permute-start | bytes 786440 | tf_op jit(solution)/shard_map/ppermute | solution.py:49
  89.3 13.6 %collective-permute-start.12 = (bf16[256,1024]{1,0:T(8,128)(2,1)S(1)}, bf16[256,1024]{1,0:T(8,128)(2,1)S(1)}, u32[]{:S(2)}, u32[]{:S(2)}) collective-permute-start(bf16[256,1024]{1,0:T(8,128)(2,1)S(1)} %get-tuple-element.69), channel_id=1, source_target_pairs={{0,2},{1,3},{2,0},{3,1},{4,6},{5,7},{6,4},{7,5},{8,10},{9,11},{10,... | collective-permute-start | bytes 1572872 | tf_op jit(solution)/shard_map/ppermute | solution.py:49
  101.5 11.8 %collective-permute-start.17 = (bf16[512,1024]{1,0:T(8,128)(2,1)S(1)}, bf16[512,1024]{1,0:T(8,128)(2,1)S(1)}, u32[]{:S(2)}, u32[]{:S(2)}) collective-permute-start(bf16[512,1024]{1,0:T(8,128)(2,1)S(1)} %collective-permute-done.4.refs_0_), channel_id=1, source_target_pairs={{0,1},{1,0},{2,3},{3,2},{4,5},{5,4},{6,7},{7,6},{8,9},{9,8},{10,11... | collective-permute-start | bytes 3145736 | tf_op jit(solution)/shard_map/ppermute | solution.py:49
  102.9 8.1 %collective-permute-start.15 = (bf16[1,32,1024]{2,1,0:T(8,128)(2,1)S(1)}, bf16[1,32,1024]{2,1,0:T(8,128)(2,1)S(1)}, u32[]{:S(2)}, u32[]{:S(2)}) collective-permute-start(bf16[1,32,1024]{2,1,0:T(8,128)(2,1)S(1)} %get-tuple-element.74), channel_id=1, source_target_pairs={{0,12},{1,13},{2,14},{3,15},{4,8},{5,9},{6,10},{7,11},{8,4},{9,5},... | collective-permute-start | bytes 196616 | tf_op jit(solution)/shard_map/ppermute | solution.py:49
  105.7 6.6 %collective-permute-start.14 = (bf16[1,32,1024]{2,1,0:T(8,128)(2,1)S(1)}, bf16[1,32,1024]{2,1,0:T(8,128)(2,1)S(1)}, u32[]{:S(2)}, u32[]{:S(2)}) collective-permute-start(bf16[1,32,1024]{2,1,0:T(8,128)(2,1)S(1)} %get-tuple-element.72), channel_id=1, source_target_pairs={{0,8},{1,9},{2,10},{3,11},{4,12},{5,13},{6,14},{7,15},{8,0},{9,1},... | collective-permute-start | bytes 196616 | tf_op jit(solution)/shard_map/ppermute | solution.py:49
  107.8 5.0 %collective-permute-start.13 = (bf16[1,32,1024]{2,1,0:T(8,128)(2,1)S(1)}, bf16[1,32,1024]{2,1,0:T(8,128)(2,1)S(1)}, u32[]{:S(2)}, u32[]{:S(2)}) collective-permute-start(bf16[1,32,1024]{2,1,0:T(8,128)(2,1)S(1)} %get-tuple-element.70), channel_id=1, source_target_pairs={{0,4},{1,5},{2,6},{3,7},{4,0},{5,1},{6,2},{7,3},{8,12},{9,13},{10,... | collective-permute-start | bytes 196616 | tf_op jit(solution)/shard_map/ppermute | solution.py:49
  109.9 12.2 %collective-permute-start.22 = (bf16[256,1024]{1,0:T(8,128)(2,1)S(1)}, bf16[256,1024]{1,0:T(8,128)(2,1)S(1)}, u32[]{:S(2)}, u32[]{:S(2)}) collective-permute-start(bf16[256,1024]{1,0:T(8,128)(2,1)S(1)} %get-tuple-element.85), channel_id=1, source_target_pairs={{0,2},{1,3},{2,0},{3,1},{4,6},{5,7},{6,4},{7,5},{8,10},{9,11},{10,... | collective-permute-start | bytes 1572872 | tf_op jit(solution)/shard_map/ppermute | solution.py:49
  112.8 13.3 %collective-permute-start.16 = (bf16[256,1024]{1,0:T(8,128)(2,1)S(1)}, bf16[256,1024]{1,0:T(8,128)(2,1)S(1)}, u32[]{:S(2)}, u32[]{:S(2)}) collective-permute-start(bf16[256,1024]{1,0:T(8,128)(2,1)S(1)} %get-tuple-element.75), channel_id=1, source_target_pairs={{0,4},{1,5},{2,6},{3,7},{4,12},{5,13},{6,14},{7,15},{12,8},{13,9},... | collective-permute-start | bytes 1572872 | tf_op jit(solution)/shard_map/ppermute | solution.py:52
  122.1 17.3 %collective-permute-start.23 = (bf16[256,1024]{1,0:T(8,128)(2,1)S(1)}, bf16[256,1024]{1,0:T(8,128)(2,1)S(1)}, u32[]{:S(2)}, u32[]{:S(2)}) collective-permute-start(bf16[256,1024]{1,0:T(8,128)(2,1)S(1)} %get-tuple-element.86), channel_id=1, source_target_pairs={{0,2},{1,3},{2,0},{3,1},{4,6},{5,7},{6,4},{7,5},{8,10},{9,11},{10,... | collective-permute-start | bytes 1572872 | tf_op jit(solution)/shard_map/ppermute | solution.py:49
  126.1 15.4 %collective-permute-start.24 = (bf16[256,1024]{1,0:T(8,128)(2,1)S(1)}, bf16[256,1024]{1,0:T(8,128)(2,1)S(1)}, u32[]{:S(2)}, u32[]{:S(2)}) collective-permute-start(bf16[256,1024]{1,0:T(8,128)(2,1)S(1)} %collective-permute-done.16.refs_0_), channel_id=1, source_target_pairs={{0,1},{1,0},{2,3},{3,2},{4,5},{5,4},{6,7},{7,6},{8,9},{9,8},{10,11... | collective-permute-start | bytes 1572872 | tf_op jit(solution)/shard_map/ppermute | solution.py:49
  126.1 6.4 %collective-permute-start.19 = (bf16[1,48,1024]{2,1,0:T(8,128)(2,1)S(1)}, bf16[1,48,1024]{2,1,0:T(8,128)(2,1)S(1)}, u32[]{:S(2)}, u32[]{:S(2)}) collective-permute-start(bf16[1,48,1024]{2,1,0:T(8,128)(2,1)S(1)} %get-tuple-element.83), channel_id=1, source_target_pairs={{0,4},{1,5},{2,6},{3,7},{4,0},{5,1},{6,2},{7,3},{8,12},{9,13},{10,... | collective-permute-start | bytes 294920 | tf_op jit(solution)/shard_map/ppermute | solution.py:49
  126.1 10.8 %collective-permute-start.20 = (bf16[1,48,1024]{2,1,0:T(8,128)(2,1)S(1)}, bf16[1,48,1024]{2,1,0:T(8,128)(2,1)S(1)}, u32[]{:S(2)}, u32[]{:S(2)}) collective-permute-start(bf16[1,48,1024]{2,1,0:T(8,128)(2,1)S(1)} %get-tuple-element.83), channel_id=1, source_target_pairs={{0,8},{1,9},{2,10},{3,11},{4,12},{5,13},{6,14},{7,15},{8,0},{9,1},... | collective-permute-start | bytes 294920 | tf_op jit(solution)/shard_map/ppermute | solution.py:49
  127.7 9.2 %collective-permute-start.21 = (bf16[1,48,1024]{2,1,0:T(8,128)(2,1)S(1)}, bf16[1,48,1024]{2,1,0:T(8,128)(2,1)S(1)}, u32[]{:S(2)}, u32[]{:S(2)}) collective-permute-start(bf16[1,48,1024]{2,1,0:T(8,128)(2,1)S(1)} %get-tuple-element.83), channel_id=1, source_target_pairs={{0,12},{1,13},{2,14},{3,15},{4,8},{5,9},{6,10},{7,11},{8,4},{9,5},... | collective-permute-start | bytes 294920 | tf_op jit(solution)/shard_map/ppermute | solution.py:49
  136.9 16.6 %collective-permute-start.31 = (bf16[256,1024]{1,0:T(8,128)(2,1)S(1)}, bf16[256,1024]{1,0:T(8,128)(2,1)S(1)}, u32[]{:S(2)}, u32[]{:S(2)}) collective-permute-start(bf16[256,1024]{1,0:T(8,128)(2,1)S(1)} %get-tuple-element.95), channel_id=1, source_target_pairs={{0,4},{1,5},{2,6},{3,7},{4,12},{5,13},{6,14},{7,15},{12,8},{13,9},... | collective-permute-start | bytes 1572872 | tf_op jit(solution)/shard_map/ppermute | solution.py:52
  139.3 3.7 %collective-permute-start.25 = (f32[8,128]{1,0:T(8,128)S(1)}, f32[8,128]{1,0:T(8,128)S(1)}, u32[]{:S(2)}, u32[]{:S(2)}) collective-permute-start(f32[8,128]{1,0:T(8,128)S(1)} %gathered.1.refs_0_), channel_id=1, source_target_pairs={{0,1},{1,0},{2,3},{3,2},{4,5},{5,4},{6,7},{7,6},{8,9},{9,8},{10,11... | collective-permute-start | bytes 12296 | tf_op jit(solution)/shard_map/ppermute | solution.py:49
  139.4 3.7 %collective-permute-start.26 = (f32[8,128]{1,0:T(8,128)S(1)}, f32[8,128]{1,0:T(8,128)S(1)}, u32[]{:S(2)}, u32[]{:S(2)}) collective-permute-start(f32[8,128]{1,0:T(8,128)S(1)} %gathered.1.refs_0_), channel_id=1, source_target_pairs={{0,2},{1,3},{2,0},{3,1},{4,6},{5,7},{6,4},{7,5},{8,10},{9,11},{10,... | collective-permute-start | bytes 12296 | tf_op jit(solution)/shard_map/ppermute | solution.py:49
  141.4 3.0 %collective-permute-start.27 = (f32[8,128]{1,0:T(8,128)S(1)}, f32[8,128]{1,0:T(8,128)S(1)}, u32[]{:S(2)}, u32[]{:S(2)}) collective-permute-start(f32[8,128]{1,0:T(8,128)S(1)} %gathered.1.refs_0_), channel_id=1, source_target_pairs={{0,3},{1,2},{2,1},{3,0},{4,7},{5,6},{6,5},{7,4},{8,11},{9,10},{10,... | collective-permute-start | bytes 12296 | tf_op jit(solution)/shard_map/ppermute | solution.py:49
  144.4 8.7 %collective-permute-start.28 = (bf16[256,512]{1,0:T(8,128)(2,1)S(1)}, bf16[256,512]{1,0:T(8,128)(2,1)S(1)}, u32[]{:S(2)}, u32[]{:S(2)}) collective-permute-start(bf16[256,512]{1,0:T(8,128)(2,1)S(1)} %get-tuple-element.91), channel_id=1, source_target_pairs={{0,2},{1,3},{2,0},{3,1},{4,6},{5,7},{6,4},{7,5},{8,10},{9,11},{10,... | collective-permute-start | bytes 786440 | tf_op jit(solution)/shard_map/ppermute | solution.py:49
  153.1 7.9 %collective-permute-start.29 = (bf16[4,32,1024]{2,1,0:T(8,128)(2,1)S(1)}, bf16[4,32,1024]{2,1,0:T(8,128)(2,1)S(1)}, u32[]{:S(2)}, u32[]{:S(2)}) collective-permute-start(bf16[4,32,1024]{2,1,0:T(8,128)(2,1)S(1)} %get-tuple-element.93), channel_id=1, source_target_pairs={{0,2},{1,3},{2,0},{3,1},{4,6},{5,7},{6,4},{7,5},{8,10},{9,11},{10,... | collective-permute-start | bytes 786440 | tf_op jit(solution)/shard_map/ppermute | solution.py:49
  153.4 7.7 %collective-permute-start.32 = (bf16[256,1024]{1,0:T(8,128)(2,1)S(1)}, bf16[256,1024]{1,0:T(8,128)(2,1)S(1)}, u32[]{:S(2)}, u32[]{:S(2)}) collective-permute-start(bf16[256,1024]{1,0:T(8,128)(2,1)S(1)} %collective-permute-done.31.refs_0_), channel_id=1, source_target_pairs={{0,1},{1,0},{2,3},{3,2},{4,5},{5,4},{6,7},{7,6},{8,9},{9,8},{10,11... | collective-permute-start | bytes 1572872 | tf_op jit(solution)/shard_map/ppermute | solution.py:49
  161.0 2.0 %collective-permute-start.30 = (bf16[8,32,1024]{2,1,0:T(8,128)(2,1)S(1)}, bf16[8,32,1024]{2,1,0:T(8,128)(2,1)S(1)}, u32[]{:S(2)}, u32[]{:S(2)}) collective-permute-start(bf16[8,32,1024]{2,1,0:T(8,128)(2,1)S(1)} %constant_dynamic-update-slice_fusion.4.near), channel_id=1, source_target_pairs={{0,1},{1,0},{2,3},{3,2},{4,5},{5,4},{6,7},{7,6},{8,9},{9,8},{10,11... | collective-permute-start | bytes 1572872 | tf_op jit(solution)/shard_map/ppermute | solution.py:49
  162.6 8.8 %collective-permute-start.33 = (bf16[256,512]{1,0:T(8,128)(2,1)S(1)}, bf16[256,512]{1,0:T(8,128)(2,1)S(1)}, u32[]{:S(2)}, u32[]{:S(2)}) collective-permute-start(bf16[256,512]{1,0:T(8,128)(2,1)S(1)} %get-tuple-element.97), channel_id=1, source_target_pairs={{0,2},{1,3},{2,0},{3,1},{4,6},{5,7},{6,4},{7,5},{8,10},{9,11},{10,... | collective-permute-start | bytes 786440 | tf_op jit(solution)/shard_map/ppermute | solution.py:49

commit v10 on v9

--- a/solution.py
+++ b/solution.py
@@ -357,11 +357,11 @@
         acts = [cut[0]] + [swap(cut[x], x) for x in range(1, members)]
         moments = jnp.concatenate([first_moment, second_moment], axis=0).astype(bf16)
         folded = [moments[:, k * rank : (k + 1) * rank] for k in range(outs // rank)]
-        basis = [after(jnp.concatenate([proj_basis] + folded, axis=0), cut[0])]
+        basis = [jnp.concatenate([proj_basis] + folded, axis=0)]
         for s in range(1, ring):
             basis.append(onward(basis[-1]))
-        weight = [master_weight.astype(bf16)]
-        weight.append(onward(after(weight[0], basis[-1])))
+        whole_weight = master_weight.astype(bf16)
+        next_weight = onward(after(whole_weight, basis[-1]))
 
         if sides == 2:
             far_grad = acts[2][:, ring * rows :]
@@ -370,16 +370,18 @@
         else:
             near = swap(key_grad, 1)
             grads = [key_grad, near]
-        theirs = [swap(after(weight[0], basis[1]), 1)]
+        their_weight = swap(after(whole_weight, basis[1]), 1)
 
         side_grads = [key_grad, far_grad] if sides == 2 else [key_grad]
         state = {"out": None}
         waiting = []
 
         def multiply(s, mine, theirs, low=0, gate=None):
-            args = [mine if gate is None else after(mine, gate), theirs] + side_grads
+            if gate is not None:
+                mine = [after(mine[0], gate)] + mine[1:]
+            args = mine + theirs + side_grads
             in_specs = [VMEM] * len(args)
-            wide = mine.shape[0]
+            wide = sum(piece.shape[0] for piece in mine)
             came = None
             if len(waiting) > 1:
                 (came, block) = waiting.pop(0)
@@ -394,7 +396,7 @@
                 shapes.append(((tokens, 2 * wide), bf16))
                 out_specs.append(VMEM)
             result = call(
-                functools.partial(weight_kernel, lay, rows, s, low, 1, came, first),
+                functools.partial(weight_kernel, lay, rows, s, low, len(mine), came, first),
                 "weight",
                 shapes,
                 args,
@@ -418,7 +420,11 @@
             waiting.append(((s, low), swap(block if gate is None else after(block, gate), 2)))
             return waiting[-1][1]
 
-        first_block = multiply(0, weight[0], theirs[0])
+        def core_swap(pieces):
+            return [swap(piece, 1) for piece in pieces]
+
+        first_block = multiply(0, [whole_weight], [their_weight])
+
         total, *gives = call(
             functools.partial(project_kernel, lay, owned, plan),
             "project",
@@ -428,12 +434,9 @@
             flops=2 * tokens * members * rank * (ring * rows + outs),
             moved=12 * 2**20,
         )
-        weight.append(onward(weight[1]))
-        theirs.append(swap(weight[1], 1))
-
         for k, (bit, radix) in enumerate(rounds):
             if bit == members:
-                gives = [after(give, weight[2], sent if sides == 2 else block) for give in gives]
+                gives = [after(give, weight[2][0]) for give in gives]
             came = [swap(give, j * bit) for j, give in zip(range(1, radix), gives)]
             if k == len(rounds) - 1:
                 break
@@ -447,34 +450,44 @@
                 moved=4 * total.size,
             )
             if bit == 1:
-                block = multiply(1, weight[1], theirs[1], gate=total)
-            if bit == 2:
-                sent = give_back(0, first_block, gate=total)
-                later = give_back(1, block, gate=total)
-                weight[2] = after(weight[2], total)
-
-        split = [weight[2][p * height : (p + 1) * height] for p in range(parts)] if ring == 4 else []
-        last = []
-        if split:
-            last.append(onward(after(split[0], *came)))
+                next_weight = after(next_weight, total)
+                weight = [None, [next_weight[p * height : (p + 1) * height] for p in range(parts)]]
+                weight.append([onward(weight[1][0])])
+                block = multiply(1, [next_weight], core_swap([next_weight]))
+            if bit == 2 and sides == 2:
+                both = jnp.concatenate([first_block, block], axis=1)
+                sent = swap(after(both, total), 2)
+                waiting.append(((0, 0), sent[:, : 2 * rows]))
+                waiting.append(((1, 0), sent[:, 2 * rows :]))
+        if sides == 1:
+            sent = block
+        for p in range(1, parts):
+            weight[2].append(onward(after(weight[1][p], *came)))
+        if ring == 4:
+            weight.append([onward(after(weight[2][0], *came))])
         owned_rows, message = call(
             functools.partial(square_kernel, len(came), lines),
             "square",
             [((owned, outs), f32), ((1, lines + 16, outs), bf16)],
-            [total] + came,
-        )
-        block = multiply(2, weight[2], swap(weight[2], 1), gate=owned_rows)
-        messages = after(message, last[0], block) if split else message
+            [after(total, sent)] + came,
+        )
+
+        their_half = swap(weight[2][0], 1)
+        messages = after(message, weight[3][0]) if ring == 4 else message
         for bit, radix in reversed(rounds):
             if bit >= members:
                 came = [swap(messages, j * bit) for j in range(1, radix)]
                 messages = jnp.concatenate([messages] + came, axis=0)
-        for p in range(1, len(split)):
-            last.append(onward(after(split[p], *came)))
+        if ring == 4:
+            for p in range(1, parts):
+                weight[3].append(onward(after(weight[2][p], *came)))
         (square,) = call(gathered_kernel, "gathered", [((8, 128), f32)], [messages])
-        if sides == 2:
-            sent = give_back(2, block, gate=later)
-            square = after(square, sent)
+        block = multiply(2, weight[2][:1], [their_half], 0, owned_rows)
+        sent = give_back(2, block, 0)
+        for p in range(1, parts):
+            block = multiply(2, weight[2][p:], core_swap(weight[2][p:]), p * height, owned_rows)
+            sent = give_back(2, block, p * height)
+        square = after(square, sent)
         squares = [square] + [swap(square, x) for x in range(1, members)]
         new_first, new_second, whole = call(
             functools.partial(moment_kernel, lay, rows),
@@ -482,10 +495,10 @@
             [((owned, outs), f32), ((owned, outs), f32), ((ring, owned, outs), bf16)],
             squares + basis + [owned_rows, first_moment, second_moment, messages],
         )
-        blocks = []
-        if split:
-            block = multiply(3, last[0], swap(last[0], 1), 0, squares[0])
-            sent = give_back(3, after(block, *squares), 0)
+        if ring == 4:
+            pieces = weight[3][:1]
+            block = multiply(3, pieces, core_swap(pieces))
+            sent = give_back(3, block)
 
         for bit, radix in reversed(rounds[1:]):
             if bit < members:
@@ -503,12 +516,12 @@
             moved=8 * 2**20,
         )
 
-        for p in range(1, len(split)):
-            give_back(3, multiply(3, last[p], swap(last[p], 1), p * height), p * height)
-        if not split:
-            for s in range(3, ring):
-                weight.append(onward(weight[s - 1]))
-                give_back(s, multiply(s, weight[s], swap(weight[s], 1)))
+        for s in range(3, ring):
+            if len(weight) <= s:
+                weight.append([onward(piece) for piece in weight[s - 1]])
+            for p in range(1 if ring == 4 else 0, parts):
+                pieces = weight[s][p : p + 1]
+                give_back(s, multiply(s, pieces, core_swap(pieces), p * height), p * height)
         activation_grad = state["out"]
         if waiting:
             (activation_grad,) = call(

time: 173 us -> 189 us (1.092)
  waiting for transfers between devices: 119 us -> 131 us
  starting transfers between devices: 30 us -> 33.3 us
    ppermute x27 -> x28, waiting for transfers between devices: 54.8 us -> 61 us  [swap(): return lax.ppermute(value, 'dp', [(i, i ^ bit) for i in range(self.n)])]
    ppermute x7 -> x8, waiting for transfers between devices: 63.8 us -> 69.7 us  [onward(): return lax.ppermute(value, 'dp', self.forward)]
    ppermute x7 -> x8, starting transfers between devices: 7.42 us -> 9.95 us  [onward(): return lax.ppermute(value, 'dp', self.forward)]
    ppermute x27 -> x28, starting transfers between devices: 22.5 us -> 23.4 us  [swap(): return lax.ppermute(value, 'dp', [(i, i ^ bit) for i in range(self.n)])]
    pallas_call x14 -> x15, Pallas kernels: 18.9 us -> 19.7 us  [call(): pl.pallas_call(kernel, name=name, out_shape=[jax.ShapeDtypeStruct(shape,...]
  transfers between devices with their start and end apart: 34 -> 36, of which waited for: 20 -> 19; matrix products, arithmetic and copies ran while one was open for 0% -> 0% of each run, Pallas kernels for 10% -> 10%
where the time goes in v10:
time: 189 us
  waiting for transfers between devices  131 us (69%)
  starting transfers between devices  33.3 us (18%)
  Pallas kernels  19.7 us (10%)
  local copies, waits for them, and re-layouts  3.56 us (2%)
    ppermute x8, waiting for transfers between devices, onward(): return lax.ppermute(value, 'dp', self.forward)  69.7 us
    ppermute x28, waiting for transfers between devices, swap(): return lax.ppermute(value, 'dp', [(i, i ^ bit) for i in range(self.n)])  61 us
    ppermute x28, starting transfers between devices, swap(): return lax.ppermute(value, 'dp', [(i, i ^ bit) for i in range(self.n)])  23.4 us
    pallas_call x15, Pallas kernels, call(): pl.pallas_call(kernel, name=name, out_shape=[jax.ShapeDtypeStruct(shape,...  19.7 us
    ppermute x8, starting transfers between devices, onward(): return lax.ppermute(value, 'dp', self.forward)  9.95 us
  transfers between devices with their start and end apart: 36, of which 19 were waited for; matrix products, arithmetic and copies ran while one was open for 0% of the time, Pallas kernels for 10%

profile of v10, /device:TPU:0, one launch (start us, length us, event | category | flops | bytes accessed | tf_op | source)
XLA Modules:
  0.0 188.8 jit_solution(4733855078536506183)
XLA Ops:
  0.6 1.0 copy-done
  1.7 2.2 %copy-done.3 = bf16[256,8192]{1,0:T(8,128)(2,1)S(1)} copy-done((bf16[256,8192]{1,0:T(8,128)(2,1)S(1)}, bf16[256,8192]{1,0:T(8,128)(2,1)}, u32[]{:S(2)}) %copy-start.3) | copy-done | bytes 4194328
  4.5 3.0 %collective-permute-start.5 = (bf16[256,3072]{1,0:T(8,128)(2,1)S(1)}, bf16[256,3072]{1,0:T(8,128)(2,1)S(1)}, u32[]{:S(2)}, u32[]{:S(2)}) collective-permute-start(bf16[256,3072]{1,0:T(8,128)(2,1)S(1)} %get-tuple-element.55), channel_id=1, source_target_pairs={{0,2},{1,3},{2,0},{3,1},{4,6},{5,7},{6,4},{7,5},{8,10},{9,11},{10,... | collective-permute-start | bytes 4718600 | tf_op jit(solution)/shard_map/ppermute | solution.py:49
  7.7 1.6 collective-permute-start
  9.3 15.5 %collective-permute-done.refs_5_ = bf16[640,512]{1,0:T(8,128)(2,1)S(1)} collective-permute-done((bf16[640,512]{1,0:T(8,128)(2,1)S(1)}, bf16[640,512]{1,0:T(8,128)(2,1)S(1)}, u32[]{:S(2)}, u32[]{:S(2)}) %collective-permute-start) | collective-permute-done | bytes 655392 | tf_op jit(solution)/shard_map/ppermute | solution.py:52
  24.8 0.8 collective-permute-start.1
  25.9 16.1 %collective-permute-done.5.refs_2_ = bf16[256,3072]{1,0:T(8,128)(2,1)S(1)} collective-permute-done((bf16[256,3072]{1,0:T(8,128)(2,1)S(1)}, bf16[256,3072]{1,0:T(8,128)(2,1)S(1)}, u32[]{:S(2)}, u32[]{:S(2)}) %collective-permute-start.5) | collective-permute-done | bytes 1572896 | tf_op jit(solution)/shard_map/ppermute | solution.py:49
  42.7 1.4 collective-permute-start.7
  44.1 1.6 collective-permute-start.2
  45.7 2.1 %weight.6 = (bf16[256,8192]{1,0:T(8,128)(2,1)}, bf16[256,1024]{1,0:T(8,128)(2,1)S(1)}) custom-call(bf16[512,1024]{1,0:T(8,128)(2,1)S(1)} %convert_element_type.4.refs_0_, bf16[512,1024]{1,0:T(8,128)(2,1)S(1)} %collective-permute-done.4.refs_1_, bf16[256,1024]{1,0:T(8,128)(2,1)S(1)} %copy-done, bf16[256,1024]{1,0:T(8,128)(2,1)S(1)} %slice.38.refs_3_.refs_10_), custom_call_target="tpu_custom_call" | custom-call | flops 1073741824 | bytes 6291456 | tf_op jit(solution)/shard_map/weight/pallas_call | solution.py:318
  47.8 14.3 %collective-permute-done.2.refs_7_ = bf16[640,512]{1,0:T(8,128)(2,1)S(1)} collective-permute-done((bf16[640,512]{1,0:T(8,128)(2,1)S(1)}, bf16[640,512]{1,0:T(8,128)(2,1)S(1)}, u32[]{:S(2)}, u32[]{:S(2)}) %collective-permute-start.2) | collective-permute-done | bytes 655392 | tf_op jit(solution)/shard_map/ppermute | solution.py:52
  62.1 0.8 collective-permute-start.3
  62.9 4.9 %collective-permute-done.7.refs_3_ = bf16[256,2048]{1,0:T(8,128)(2,1)S(1)} collective-permute-done((bf16[256,2048]{1,0:T(8,128)(2,1)S(1)}, bf16[256,2048]{1,0:T(8,128)(2,1)S(1)}, u32[]{:S(2)}, u32[]{:S(2)}) %collective-permute-start.7) | collective-permute-done | bytes 1048608 | tf_op jit(solution)/shard_map/ppermute | solution.py:49
  67.8 4.3 %project.1 = (f32[8,32,1024]{2,1,0:T(8,128)S(1)}, bf16[8,32,1024]{2,1,0:T(8,128)(2,1)S(1)}) custom-call(bf16[256,2048]{1,0:T(8,128)(2,1)S(1)} %get-tuple-element.57.refs_0_, bf16[256,2048]{1,0:T(8,128)(2,1)S(1)} %collective-permute-done.6.refs_1_, bf16[256,3072]{1,0:T(8,128)(2,1)S(1)} %collective-permute-done.5.refs_2_, ...), custom_call_target="tpu_custom_call" | custom-call | flops 3221225472 | bytes 12582912 | tf_op jit(solution)/shard_map/project/pallas_call | solution.py:318
  72.6 1.5 collective-permute-done.9.refs_1_
  74.3 13.4 %collective-permute-done.3.refs_0_ = bf16[512,1024]{1,0:T(8,128)(2,1)S(1)} collective-permute-done((bf16[512,1024]{1,0:T(8,128)(2,1)S(1)}, bf16[512,1024]{1,0:T(8,128)(2,1)S(1)}, u32[]{:S(2)}, u32[]{:S(2)}) %collective-permute-start.3) | collective-permute-done | bytes 1048608 | tf_op jit(solution)/shard_map/ppermute | solution.py:52
  88.3 0.8 collective-permute-start.10
  89.1 7.3 %collective-permute-done.11.refs_1_ = bf16[4,32,1024]{2,1,0:T(8,128)(2,1)S(1)} collective-permute-done((bf16[4,32,1024]{2,1,0:T(8,128)(2,1)S(1)}, bf16[4,32,1024]{2,1,0:T(8,128)(2,1)S(1)}, u32[]{:S(2)}, u32[]{:S(2)}) %collective-permute-start.11) | collective-permute-done | bytes 262176 | tf_op jit(solution)/shard_map/ppermute | solution.py:49
  96.5 2.1 %weight.7 = (bf16[256,8192]{1,0:T(8,128)(2,1)}, bf16[256,1024]{1,0:T(8,128)(2,1)S(1)}) custom-call(bf16[512,1024]{1,0:T(8,128)(2,1)S(1)} %collective-permute-done.3.refs_0_, bf16[512,1024]{1,0:T(8,128)(2,1)S(1)} %collective-permute-done.17.refs_1_, bf16[256,1024]{1,0:T(8,128)(2,1)S(1)} %copy-done.1, ...), custom_call_target="tpu_custom_call", output_to_operand_aliasing={{0}: (4, {})} | custom-call | flops 1073741824 | bytes 6291456 | tf_op jit(solution)/shard_map/weight/pallas_call | solution.py:318
  99.3 4.0 %collective-permute-done.10.refs_0_ = bf16[256,1024]{1,0:T(8,128)(2,1)S(1)} collective-permute-done((bf16[256,1024]{1,0:T(8,128)(2,1)S(1)}, bf16[256,1024]{1,0:T(8,128)(2,1)S(1)}, u32[]{:S(2)}, u32[]{:S(2)}) %collective-permute-start.10) | collective-permute-done | bytes 524320 | tf_op jit(solution)/shard_map/ppermute | solution.py:52
  103.3 3.6 %collective-permute-start.14 = (bf16[1,32,1024]{2,1,0:T(8,128)(2,1)S(1)}, bf16[1,32,1024]{2,1,0:T(8,128)(2,1)S(1)}, u32[]{:S(2)}, u32[]{:S(2)}) collective-permute-start(bf16[1,32,1024]{2,1,0:T(8,128)(2,1)S(1)} %get-tuple-element.70), channel_id=1, source_target_pairs={{0,12},{1,13},{2,14},{3,15},{4,8},{5,9},{6,10},{7,11},{8,4},{9,5},... | collective-permute-start | bytes 196616 | tf_op jit(solution)/shard_map/ppermute | solution.py:49
  106.9 0.8 collective-permute-start.12
  107.7 1.8 collective-permute-done.14.refs_3_
  109.5 2.6 %collective-permute-done.13.refs_2_ = bf16[1,32,1024]{2,1,0:T(8,128)(2,1)S(1)} collective-permute-done((bf16[1,32,1024]{2,1,0:T(8,128)(2,1)S(1)}, bf16[1,32,1024]{2,1,0:T(8,128)(2,1)S(1)}, u32[]{:S(2)}, u32[]{:S(2)}) %collective-permute-start.13) | collective-permute-done | bytes 65568 | tf_op jit(solution)/shard_map/ppermute | solution.py:49
  112.4 0.7 collective-permute-start.21
  113.1 1.7 collective-permute-start.15
  114.8 13.4 %collective-permute-done.21.refs_0_ = bf16[256,1024]{1,0:T(8,128)(2,1)S(1)} collective-permute-done((bf16[256,1024]{1,0:T(8,128)(2,1)S(1)}, bf16[256,1024]{1,0:T(8,128)(2,1)S(1)}, u32[]{:S(2)}, u32[]{:S(2)}) %collective-permute-start.21) | collective-permute-done | bytes 524320 | tf_op jit(solution)/shard_map/ppermute | solution.py:52
  128.1 9.0 %collective-permute-done.15.refs_0_ = bf16[256,1024]{1,0:T(8,128)(2,1)S(1)} collective-permute-done((bf16[256,1024]{1,0:T(8,128)(2,1)S(1)}, bf16[256,1024]{1,0:T(8,128)(2,1)S(1)}, u32[]{:S(2)}, u32[]{:S(2)}) %collective-permute-start.15) | collective-permute-done | bytes 524320 | tf_op jit(solution)/shard_map/ppermute | solution.py:52
  137.6 1.5 weight.8
  139.1 1.6 collective-permute-start.20
  140.6 1.6 collective-permute-start.25
  142.6 2.4 %collective-permute-start.26 = (bf16[1,48,1024]{2,1,0:T(8,128)(2,1)S(1)}, bf16[1,48,1024]{2,1,0:T(8,128)(2,1)S(1)}, u32[]{:S(2)}, u32[]{:S(2)}) collective-permute-start(bf16[1,48,1024]{2,1,0:T(8,128)(2,1)S(1)} %get-tuple-element.87), channel_id=1, source_target_pairs={{0,12},{1,13},{2,14},{3,15},{4,8},{5,9},{6,10},{7,11},{8,4},{9,5},... | collective-permute-start | bytes 294920 | tf_op jit(solution)/shard_map/ppermute | solution.py:49
  145.0 6.4 %collective-permute-done.25 = bf16[1,48,1024]{2,1,0:T(8,128)(2,1)S(1)} collective-permute-done((bf16[1,48,1024]{2,1,0:T(8,128)(2,1)S(1)}, bf16[1,48,1024]{2,1,0:T(8,128)(2,1)S(1)}, u32[]{:S(2)}, u32[]{:S(2)}) %collective-permute-start.25) | collective-permute-done | bytes 98336 | tf_op jit(solution)/shard_map/ppermute | solution.py:49
  151.4 2.0 %collective-permute-start.33 = (bf16[256,1024]{1,0:T(8,128)(2,1)S(1)}, bf16[256,1024]{1,0:T(8,128)(2,1)S(1)}, u32[]{:S(2)}, u32[]{:S(2)}) collective-permute-start(bf16[256,1024]{1,0:T(8,128)(2,1)S(1)} %collective-permute-done.21.refs_0_), channel_id=1, source_target_pairs={{0,4},{1,5},{2,6},{3,7},{4,12},{5,13},{6,14},{7,15},{12,8},{13,9},... | collective-permute-start | bytes 1572872 | tf_op jit(solution)/shard_map/ppermute | solution.py:52
  153.4 1.5 weight.9
  155.4 1.5 weight.10
  156.9 1.6 collective-permute-start.23
  158.7 5.5 %collective-permute-done.27.refs_4_ = bf16[256,512]{1,0:T(8,128)(2,1)S(1)} collective-permute-done((bf16[256,512]{1,0:T(8,128)(2,1)S(1)}, bf16[256,512]{1,0:T(8,128)(2,1)S(1)}, u32[]{:S(2)}, u32[]{:S(2)}) %collective-permute-start.27) | collective-permute-done | bytes 262176 | tf_op jit(solution)/shard_map/ppermute | solution.py:49
  164.7 1.3 collective-permute-start.30
  166.0 2.0 %collective-permute-done.29.refs_2_ = f32[8,128]{1,0:T(8,128)S(1)} collective-permute-done((f32[8,128]{1,0:T(8,128)S(1)}, f32[8,128]{1,0:T(8,128)S(1)}, u32[]{:S(2)}, u32[]{:S(2)}) %collective-permute-start.29) | collective-permute-done | bytes 4128 | tf_op jit(solution)/shard_map/ppermute | solution.py:49
  168.0 1.1 moment.1
  169.1 1.2 collective-permute-start.31
  170.4 7.1 %collective-permute-done.31 = bf16[4,32,1024]{2,1,0:T(8,128)(2,1)S(1)} collective-permute-done((bf16[4,32,1024]{2,1,0:T(8,128)(2,1)S(1)}, bf16[4,32,1024]{2,1,0:T(8,128)(2,1)S(1)}, u32[]{:S(2)}, u32[]{:S(2)}) %collective-permute-start.31) | collective-permute-done | bytes 262176 | tf_op jit(solution)/shard_map/ppermute | solution.py:49
  177.6 1.5 weight.11
  179.0 1.4 collective-permute-start.35
  180.5 2.2 %back.1 = f32[512,1024]{1,0:T(8,128)} custom-call(bf16[512,512]{1,0:T(8,128)(2,1)S(1)} %copy-done.4, bf16[8,32,1024]{2,1,0:T(8,128)(2,1)S(1)} %constant_dynamic-update-slice_fusion.4.near, bf16[8,32,1024]{2,1,0:T(8,128)(2,1)S(1)} %collective-permute-done.32.other, f32[512,1024]{1,0:T(8,128)S(1)} %copy-done.2), custom_call_target="tpu_custom_call" | custom-call | flops 536870912 | bytes 8388608 | tf_op jit(solution)/shard_map/back/pallas_call | solution.py:318
  182.7 5.2 %collective-permute-done.35.refs_1_ = bf16[256,512]{1,0:T(8,128)(2,1)S(1)} collective-permute-done((bf16[256,512]{1,0:T(8,128)(2,1)S(1)}, bf16[256,512]{1,0:T(8,128)(2,1)S(1)}, u32[]{:S(2)}, u32[]{:S(2)}) %collective-permute-start.35) | collective-permute-done | bytes 262176 | tf_op jit(solution)/shard_map/ppermute | solution.py:49
  187.8 0.8 last.1
  (70 shorter events, 6.0 us)
Async XLA Ops:
  0.6 1.0 copy-start
  1.7 2.2 %copy-start.3 = (bf16[256,8192]{1,0:T(8,128)(2,1)S(1)}, bf16[256,8192]{1,0:T(8,128)(2,1)}, u32[]{:S(2)}) copy-start(bf16[256,8192]{1,0:T(8,128)(2,1)} %act.1) | copy-start | bytes 12582916
  3.9 3.7 %copy-start.6 = (f32[32,1024]{1,0:T(8,128)S(1)}, f32[32,1024]{1,0:T(8,128)}, u32[]{:S(2)}) copy-start(f32[32,1024]{1,0:T(8,128)} %refs_9_.1) | copy-start | bytes 393220
  3.9 3.7 %copy-start.5 = (f32[32,1024]{1,0:T(8,128)S(1)}, f32[32,1024]{1,0:T(8,128)}, u32[]{:S(2)}) copy-start(f32[32,1024]{1,0:T(8,128)} %refs_10_.1) | copy-start | bytes 393220
  3.9 3.8 %copy-start.4 = (bf16[512,512]{1,0:T(8,128)(2,1)S(1)}, bf16[512,512]{1,0:T(8,128)(2,1)}, u32[]{:S(2)}) copy-start(bf16[512,512]{1,0:T(8,128)(2,1)} %basis.1) | copy-start | bytes 1572868
  3.9 21.7 %copy-start.2 = (f32[512,1024]{1,0:T(8,128)S(1)}, f32[512,1024]{1,0:T(8,128)}, u32[]{:S(2)}) copy-start(f32[512,1024]{1,0:T(8,128)} %master.1) | copy-start | bytes 6291460
  4.5 37.4 %collective-permute-start.5 = (bf16[256,3072]{1,0:T(8,128)(2,1)S(1)}, bf16[256,3072]{1,0:T(8,128)(2,1)S(1)}, u32[]{:S(2)}, u32[]{:S(2)}) collective-permute-start(bf16[256,3072]{1,0:T(8,128)(2,1)S(1)} %get-tuple-element.55), channel_id=1, source_target_pairs={{0,2},{1,3},{2,0},{3,1},{4,6},{5,7},{6,4},{7,5},{8,10},{9,11},{10,... | collective-permute-start | bytes 4718600 | tf_op jit(solution)/shard_map/ppermute | solution.py:49
  7.7 17.1 %collective-permute-start = (bf16[640,512]{1,0:T(8,128)(2,1)S(1)}, bf16[640,512]{1,0:T(8,128)(2,1)S(1)}, u32[]{:S(2)}, u32[]{:S(2)}) collective-permute-start(bf16[640,512]{1,0:T(8,128)(2,1)S(1)} %fusion.refs_4_), channel_id=1, source_target_pairs={{0,4},{1,5},{2,6},{3,7},{4,12},{5,13},{6,14},{7,15},{12,8},{13,9},... | collective-permute-start | bytes 1966088 | tf_op jit(solution)/shard_map/ppermute | solution.py:52
  24.8 19.2 %collective-permute-start.1 = (bf16[640,512]{1,0:T(8,128)(2,1)S(1)}, bf16[640,512]{1,0:T(8,128)(2,1)S(1)}, u32[]{:S(2)}, u32[]{:S(2)}) collective-permute-start(bf16[640,512]{1,0:T(8,128)(2,1)S(1)} %collective-permute-done.refs_5_), channel_id=1, source_target_pairs={{0,4},{1,5},{2,6},{3,7},{4,12},{5,13},{6,14},{7,15},{12,8},{13,9},... | collective-permute-start | bytes 1966088 | tf_op jit(solution)/shard_map/ppermute | solution.py:52
  25.8 19.9 %collective-permute-start.4 = (bf16[512,1024]{1,0:T(8,128)(2,1)S(1)}, bf16[512,1024]{1,0:T(8,128)(2,1)S(1)}, u32[]{:S(2)}, u32[]{:S(2)}) collective-permute-start(bf16[512,1024]{1,0:T(8,128)(2,1)S(1)} %convert_element_type.4.refs_0_), channel_id=1, source_target_pairs={{0,1},{1,0},{2,3},{3,2},{4,5},{5,4},{6,7},{7,6},{8,9},{9,8},{10,11... | collective-permute-start | bytes 3145736 | tf_op jit(solution)/shard_map/ppermute | solution.py:49
  42.1 20.8 %collective-permute-start.8 = (bf16[512,1024]{1,0:T(8,128)(2,1)S(1)}, bf16[512,1024]{1,0:T(8,128)(2,1)S(1)}, u32[]{:S(2)}, u32[]{:S(2)}) collective-permute-start(bf16[512,1024]{1,0:T(8,128)(2,1)S(1)} %pad_maximum_fusion), channel_id=1, source_target_pairs={{0,1},{1,0},{2,3},{3,2},{4,5},{5,4},{6,7},{7,6},{8,9},{9,8},{10,11... | collective-permute-start | bytes 3145736 | tf_op jit(solution)/shard_map/ppermute | solution.py:49
  42.2 20.8 %collective-permute-start.6 = (bf16[256,2048]{1,0:T(8,128)(2,1)S(1)}, bf16[256,2048]{1,0:T(8,128)(2,1)S(1)}, u32[]{:S(2)}, u32[]{:S(2)}) collective-permute-start(bf16[256,2048]{1,0:T(8,128)(2,1)S(1)} %get-tuple-element.58), channel_id=1, source_target_pairs={{0,1},{1,0},{2,3},{3,2},{4,5},{5,4},{6,7},{7,6},{8,9},{9,8},{10,11... | collective-permute-start | bytes 3145736 | tf_op jit(solution)/shard_map/ppermute | solution.py:49
  42.7 25.2 %copy-start.1 = (bf16[256,1024]{1,0:T(8,128)(2,1)S(1)}, bf16[256,1024]{1,0:T(8,128)(2,1)}, u32[]{:S(2)}) copy-start(bf16[256,1024]{1,0:T(8,128)(2,1)} %refs_2_.11) | copy-start | bytes 1572868
  42.7 25.2 %collective-permute-start.7 = (bf16[256,2048]{1,0:T(8,128)(2,1)S(1)}, bf16[256,2048]{1,0:T(8,128)(2,1)S(1)}, u32[]{:S(2)}, u32[]{:S(2)}) collective-permute-start(bf16[256,2048]{1,0:T(8,128)(2,1)S(1)} %get-tuple-element.59), channel_id=1, source_target_pairs={{0,3},{1,2},{2,1},{3,0},{4,7},{5,6},{6,5},{7,4},{8,11},{9,10},{10,... | collective-permute-start | bytes 3145736 | tf_op jit(solution)/shard_map/ppermute | solution.py:49
  44.1 18.0 %collective-permute-start.2 = (bf16[640,512]{1,0:T(8,128)(2,1)S(1)}, bf16[640,512]{1,0:T(8,128)(2,1)S(1)}, u32[]{:S(2)}, u32[]{:S(2)}) collective-permute-start(bf16[640,512]{1,0:T(8,128)(2,1)S(1)} %collective-permute-done.1.refs_6_), channel_id=1, source_target_pairs={{0,4},{1,5},{2,6},{3,7},{4,12},{5,13},{6,14},{7,15},{12,8},{13,9},... | collective-permute-start | bytes 1966088 | tf_op jit(solution)/shard_map/ppermute | solution.py:52
  62.1 25.6 %collective-permute-start.3 = (bf16[512,1024]{1,0:T(8,128)(2,1)S(1)}, bf16[512,1024]{1,0:T(8,128)(2,1)S(1)}, u32[]{:S(2)}, u32[]{:S(2)}) collective-permute-start(bf16[512,1024]{1,0:T(8,128)(2,1)S(1)} %convert_element_type.4.refs_0_), channel_id=1, source_target_pairs={{0,4},{1,5},{2,6},{3,7},{4,12},{5,13},{6,14},{7,15},{12,8},{13,9},... | collective-permute-start | bytes 3145736 | tf_op jit(solution)/shard_map/ppermute | solution.py:52
  72.2 2.0 %collective-permute-start.9 = (bf16[8,32,1024]{2,1,0:T(8,128)(2,1)S(1)}, bf16[8,32,1024]{2,1,0:T(8,128)(2,1)S(1)}, u32[]{:S(2)}, u32[]{:S(2)}) collective-permute-start(bf16[8,32,1024]{2,1,0:T(8,128)(2,1)S(1)} %get-tuple-element.61), channel_id=1, source_target_pairs={{0,1},{1,0},{2,3},{3,2},{4,5},{5,4},{6,7},{7,6},{8,9},{9,8},{10,11... | collective-permute-start | bytes 1572872 | tf_op jit(solution)/shard_map/ppermute | solution.py:49
  87.7 8.8 %collective-permute-start.17 = (bf16[512,1024]{1,0:T(8,128)(2,1)S(1)}, bf16[512,1024]{1,0:T(8,128)(2,1)S(1)}, u32[]{:S(2)}, u32[]{:S(2)}) collective-permute-start(bf16[512,1024]{1,0:T(8,128)(2,1)S(1)} %collective-permute-done.3.refs_0_), channel_id=1, source_target_pairs={{0,1},{1,0},{2,3},{3,2},{4,5},{5,4},{6,7},{7,6},{8,9},{9,8},{10,11... | collective-permute-start | bytes 3145736 | tf_op jit(solution)/shard_map/ppermute | solution.py:49
  87.7 8.7 %collective-permute-start.11 = (bf16[4,32,1024]{2,1,0:T(8,128)(2,1)S(1)}, bf16[4,32,1024]{2,1,0:T(8,128)(2,1)S(1)}, u32[]{:S(2)}, u32[]{:S(2)}) collective-permute-start(bf16[4,32,1024]{2,1,0:T(8,128)(2,1)S(1)} %get-tuple-element.64), channel_id=1, source_target_pairs={{0,2},{1,3},{2,0},{3,1},{4,6},{5,7},{6,4},{7,5},{8,10},{9,11},{10,... | collective-permute-start | bytes 786440 | tf_op jit(solution)/shard_map/ppermute | solution.py:49
  88.3 15.0 %collective-permute-start.10 = (bf16[256,1024]{1,0:T(8,128)(2,1)S(1)}, bf16[256,1024]{1,0:T(8,128)(2,1)S(1)}, u32[]{:S(2)}, u32[]{:S(2)}) collective-permute-start(bf16[256,1024]{1,0:T(8,128)(2,1)S(1)} %get-tuple-element.103), channel_id=1, source_target_pairs={{0,4},{1,5},{2,6},{3,7},{4,12},{5,13},{6,14},{7,15},{12,8},{13,9},... | collective-permute-start | bytes 1572872 | tf_op jit(solution)/shard_map/ppermute | solution.py:52
  98.7 38.5 %collective-permute-start.18 = (bf16[256,2048]{1,0:T(8,128)(2,1)S(1)}, bf16[256,2048]{1,0:T(8,128)(2,1)S(1)}, u32[]{:S(2)}, u32[]{:S(2)}) collective-permute-start(bf16[256,2048]{1,0:T(8,128)(2,1)S(1)} %pad_maximum_fusion.1), channel_id=1, source_target_pairs={{0,2},{1,3},{2,0},{3,1},{4,6},{5,7},{6,4},{7,5},{8,10},{9,11},{10,... | collective-permute-start | bytes 3145736 | tf_op jit(solution)/shard_map/ppermute | solution.py:49
  103.3 6.2 %collective-permute-start.14 = (bf16[1,32,1024]{2,1,0:T(8,128)(2,1)S(1)}, bf16[1,32,1024]{2,1,0:T(8,128)(2,1)S(1)}, u32[]{:S(2)}, u32[]{:S(2)}) collective-permute-start(bf16[1,32,1024]{2,1,0:T(8,128)(2,1)S(1)} %get-tuple-element.70), channel_id=1, source_target_pairs={{0,12},{1,13},{2,14},{3,15},{4,8},{5,9},{6,10},{7,11},{8,4},{9,5},... | collective-permute-start | bytes 196616 | tf_op jit(solution)/shard_map/ppermute | solution.py:49
  106.9 5.2 %collective-permute-start.13 = (bf16[1,32,1024]{2,1,0:T(8,128)(2,1)S(1)}, bf16[1,32,1024]{2,1,0:T(8,128)(2,1)S(1)}, u32[]{:S(2)}, u32[]{:S(2)}) collective-permute-start(bf16[1,32,1024]{2,1,0:T(8,128)(2,1)S(1)} %get-tuple-element.68), channel_id=1, source_target_pairs={{0,8},{1,9},{2,10},{3,11},{4,12},{5,13},{6,14},{7,15},{8,0},{9,1},... | collective-permute-start | bytes 196616 | tf_op jit(solution)/shard_map/ppermute | solution.py:49
  106.9 5.5 %collective-permute-start.12 = (bf16[1,32,1024]{2,1,0:T(8,128)(2,1)S(1)}, bf16[1,32,1024]{2,1,0:T(8,128)(2,1)S(1)}, u32[]{:S(2)}, u32[]{:S(2)}) collective-permute-start(bf16[1,32,1024]{2,1,0:T(8,128)(2,1)S(1)} %get-tuple-element.66), channel_id=1, source_target_pairs={{0,4},{1,5},{2,6},{3,7},{4,0},{5,1},{6,2},{7,3},{8,12},{9,13},{10,... | collective-permute-start | bytes 196616 | tf_op jit(solution)/shard_map/ppermute | solution.py:49
  112.4 15.8 %collective-permute-start.21 = (bf16[256,1024]{1,0:T(8,128)(2,1)S(1)}, bf16[256,1024]{1,0:T(8,128)(2,1)S(1)}, u32[]{:S(2)}, u32[]{:S(2)}) collective-permute-start(bf16[256,1024]{1,0:T(8,128)(2,1)S(1)} %get-tuple-element.81), channel_id=1, source_target_pairs={{0,4},{1,5},{2,6},{3,7},{4,12},{5,13},{6,14},{7,15},{12,8},{13,9},... | collective-permute-start | bytes 1572872 | tf_op jit(solution)/shard_map/ppermute | solution.py:52
  113.1 24.1 %collective-permute-start.15 = (bf16[256,1024]{1,0:T(8,128)(2,1)S(1)}, bf16[256,1024]{1,0:T(8,128)(2,1)S(1)}, u32[]{:S(2)}, u32[]{:S(2)}) collective-permute-start(bf16[256,1024]{1,0:T(8,128)(2,1)S(1)} %collective-permute-done.10.refs_0_), channel_id=1, source_target_pairs={{0,4},{1,5},{2,6},{3,7},{4,12},{5,13},{6,14},{7,15},{12,8},{13,9},... | collective-permute-start | bytes 1572872 | tf_op jit(solution)/shard_map/ppermute | solution.py:52
  114.8 22.8 %collective-permute-start.19 = (bf16[256,1024]{1,0:T(8,128)(2,1)S(1)}, bf16[256,1024]{1,0:T(8,128)(2,1)S(1)}, u32[]{:S(2)}, u32[]{:S(2)}) collective-permute-start(bf16[256,1024]{1,0:T(8,128)(2,1)S(1)} %collective-permute-done.10.refs_0_), channel_id=1, source_target_pairs={{0,1},{1,0},{2,3},{3,2},{4,5},{5,4},{6,7},{7,6},{8,9},{9,8},{10,11... | collective-permute-start | bytes 1572872 | tf_op jit(solution)/shard_map/ppermute | solution.py:49
  128.1 25.2 %collective-permute-start.22 = (bf16[256,1024]{1,0:T(8,128)(2,1)S(1)}, bf16[256,1024]{1,0:T(8,128)(2,1)S(1)}, u32[]{:S(2)}, u32[]{:S(2)}) collective-permute-start(bf16[256,1024]{1,0:T(8,128)(2,1)S(1)} %collective-permute-done.21.refs_0_), channel_id=1, source_target_pairs={{0,1},{1,0},{2,3},{3,2},{4,5},{5,4},{6,7},{7,6},{8,9},{9,8},{10,11... | collective-permute-start | bytes 1572872 | tf_op jit(solution)/shard_map/ppermute | solution.py:49
  137.2 18.3 %collective-permute-start.16 = (bf16[256,1024]{1,0:T(8,128)(2,1)S(1)}, bf16[256,1024]{1,0:T(8,128)(2,1)S(1)}, u32[]{:S(2)}, u32[]{:S(2)}) collective-permute-start(bf16[256,1024]{1,0:T(8,128)(2,1)S(1)} %collective-permute-done.15.refs_0_), channel_id=1, source_target_pairs={{0,1},{1,0},{2,3},{3,2},{4,5},{5,4},{6,7},{7,6},{8,9},{9,8},{10,11... | collective-permute-start | bytes 1572872 | tf_op jit(solution)/shard_map/ppermute | solution.py:49
  137.4 5.3 %collective-permute-start.24 = (bf16[1,48,1024]{2,1,0:T(8,128)(2,1)S(1)}, bf16[1,48,1024]{2,1,0:T(8,128)(2,1)S(1)}, u32[]{:S(2)}, u32[]{:S(2)}) collective-permute-start(bf16[1,48,1024]{2,1,0:T(8,128)(2,1)S(1)} %get-tuple-element.87), channel_id=1, source_target_pairs={{0,4},{1,5},{2,6},{3,7},{4,0},{5,1},{6,2},{7,3},{8,12},{9,13},{10,... | collective-permute-start | bytes 294920 | tf_op jit(solution)/shard_map/ppermute | solution.py:49
  139.1 16.4 %collective-permute-start.20 = (bf16[256,512]{1,0:T(8,128)(2,1)S(1)}, bf16[256,512]{1,0:T(8,128)(2,1)S(1)}, u32[]{:S(2)}, u32[]{:S(2)}) collective-permute-start(bf16[256,512]{1,0:T(8,128)(2,1)S(1)} %get-tuple-element.80), channel_id=1, source_target_pairs={{0,2},{1,3},{2,0},{3,1},{4,6},{5,7},{6,4},{7,5},{8,10},{9,11},{10,... | collective-permute-start | bytes 786440 | tf_op jit(solution)/shard_map/ppermute | solution.py:49
  140.6 10.7 %collective-permute-start.25 = (bf16[1,48,1024]{2,1,0:T(8,128)(2,1)S(1)}, bf16[1,48,1024]{2,1,0:T(8,128)(2,1)S(1)}, u32[]{:S(2)}, u32[]{:S(2)}) collective-permute-start(bf16[1,48,1024]{2,1,0:T(8,128)(2,1)S(1)} %get-tuple-element.87), channel_id=1, source_target_pairs={{0,8},{1,9},{2,10},{3,11},{4,12},{5,13},{6,14},{7,15},{8,0},{9,1},... | collective-permute-start | bytes 294920 | tf_op jit(solution)/shard_map/ppermute | solution.py:49
  142.6 8.7 %collective-permute-start.26 = (bf16[1,48,1024]{2,1,0:T(8,128)(2,1)S(1)}, bf16[1,48,1024]{2,1,0:T(8,128)(2,1)S(1)}, u32[]{:S(2)}, u32[]{:S(2)}) collective-permute-start(bf16[1,48,1024]{2,1,0:T(8,128)(2,1)S(1)} %get-tuple-element.87), channel_id=1, source_target_pairs={{0,12},{1,13},{2,14},{3,15},{4,8},{5,9},{6,10},{7,11},{8,4},{9,5},... | collective-permute-start | bytes 294920 | tf_op jit(solution)/shard_map/ppermute | solution.py:49
  151.4 19.0 %collective-permute-start.33 = (bf16[256,1024]{1,0:T(8,128)(2,1)S(1)}, bf16[256,1024]{1,0:T(8,128)(2,1)S(1)}, u32[]{:S(2)}, u32[]{:S(2)}) collective-permute-start(bf16[256,1024]{1,0:T(8,128)(2,1)S(1)} %collective-permute-done.21.refs_0_), channel_id=1, source_target_pairs={{0,4},{1,5},{2,6},{3,7},{4,12},{5,13},{6,14},{7,15},{12,8},{13,9},... | collective-permute-start | bytes 1572872 | tf_op jit(solution)/shard_map/ppermute | solution.py:52
  154.9 9.3 %collective-permute-start.27 = (bf16[256,512]{1,0:T(8,128)(2,1)S(1)}, bf16[256,512]{1,0:T(8,128)(2,1)S(1)}, u32[]{:S(2)}, u32[]{:S(2)}) collective-permute-start(bf16[256,512]{1,0:T(8,128)(2,1)S(1)} %get-tuple-element.88), channel_id=1, source_target_pairs={{0,2},{1,3},{2,0},{3,1},{4,6},{5,7},{6,4},{7,5},{8,10},{9,11},{10,... | collective-permute-start | bytes 786440 | tf_op jit(solution)/shard_map/ppermute | solution.py:49
  156.9 12.2 %collective-permute-start.23 = (bf16[256,512]{1,0:T(8,128)(2,1)S(1)}, bf16[256,512]{1,0:T(8,128)(2,1)S(1)}, u32[]{:S(2)}, u32[]{:S(2)}) collective-permute-start(bf16[256,512]{1,0:T(8,128)(2,1)S(1)} %get-tuple-element.85), channel_id=1, source_target_pairs={{0,2},{1,3},{2,0},{3,1},{4,6},{5,7},{6,4},{7,5},{8,10},{9,11},{10,... | collective-permute-start | bytes 786440 | tf_op jit(solution)/shard_map/ppermute | solution.py:49
  164.2 1.9 collective-permute-start.28
  164.2 3.8 %collective-permute-start.29 = (f32[8,128]{1,0:T(8,128)S(1)}, f32[8,128]{1,0:T(8,128)S(1)}, u32[]{:S(2)}, u32[]{:S(2)}) collective-permute-start(f32[8,128]{1,0:T(8,128)S(1)} %gathered.1.refs_0_), channel_id=1, source_target_pairs={{0,2},{1,3},{2,0},{3,1},{4,6},{5,7},{6,4},{7,5},{8,10},{9,11},{10,... | collective-permute-start | bytes 12296 | tf_op jit(solution)/shard_map/ppermute | solution.py:49
  164.7 3.3 %collective-permute-start.30 = (f32[8,128]{1,0:T(8,128)S(1)}, f32[8,128]{1,0:T(8,128)S(1)}, u32[]{:S(2)}, u32[]{:S(2)}) collective-permute-start(f32[8,128]{1,0:T(8,128)S(1)} %gathered.1.refs_0_), channel_id=1, source_target_pairs={{0,3},{1,2},{2,1},{3,0},{4,7},{5,6},{6,5},{7,4},{8,11},{9,10},{10,... | collective-permute-start | bytes 12296 | tf_op jit(solution)/shard_map/ppermute | solution.py:49
  169.1 8.3 %collective-permute-start.31 = (bf16[4,32,1024]{2,1,0:T(8,128)(2,1)S(1)}, bf16[4,32,1024]{2,1,0:T(8,128)(2,1)S(1)}, u32[]{:S(2)}, u32[]{:S(2)}) collective-permute-start(bf16[4,32,1024]{2,1,0:T(8,128)(2,1)S(1)} %get-tuple-element.91), channel_id=1, source_target_pairs={{0,2},{1,3},{2,0},{3,1},{4,6},{5,7},{6,4},{7,5},{8,10},{9,11},{10,... | collective-permute-start | bytes 786440 | tf_op jit(solution)/shard_map/ppermute | solution.py:49
  170.3 7.2 %collective-permute-start.34 = (bf16[256,1024]{1,0:T(8,128)(2,1)S(1)}, bf16[256,1024]{1,0:T(8,128)(2,1)S(1)}, u32[]{:S(2)}, u32[]{:S(2)}) collective-permute-start(bf16[256,1024]{1,0:T(8,128)(2,1)S(1)} %collective-permute-done.33.refs_0_), channel_id=1, source_target_pairs={{0,1},{1,0},{2,3},{3,2},{4,5},{5,4},{6,7},{7,6},{8,9},{9,8},{10,11... | collective-permute-start | bytes 1572872 | tf_op jit(solution)/shard_map/ppermute | solution.py:49
  177.5 3.0 %collective-permute-start.32 = (bf16[8,32,1024]{2,1,0:T(8,128)(2,1)S(1)}, bf16[8,32,1024]{2,1,0:T(8,128)(2,1)S(1)}, u32[]{:S(2)}, u32[]{:S(2)}) collective-permute-start(bf16[8,32,1024]{2,1,0:T(8,128)(2,1)S(1)} %constant_dynamic-update-slice_fusion.4.near), channel_id=1, source_target_pairs={{0,1},{1,0},{2,3},{3,2},{4,5},{5,4},{6,7},{7,6},{8,9},{9,8},{10,11... | collective-permute-start | bytes 1572872 | tf_op jit(solution)/shard_map/ppermute | solution.py:49
  179.0 8.8 %collective-permute-start.35 = (bf16[256,512]{1,0:T(8,128)(2,1)S(1)}, bf16[256,512]{1,0:T(8,128)(2,1)S(1)}, u32[]{:S(2)}, u32[]{:S(2)}) collective-permute-start(bf16[256,512]{1,0:T(8,128)(2,1)S(1)} %get-tuple-element.95), channel_id=1, source_target_pairs={{0,2},{1,3},{2,0},{3,1},{4,6},{5,7},{6,4},{7,5},{8,10},{9,11},{10,... | collective-permute-start | bytes 786440 | tf_op jit(solution)/shard_map/ppermute | solution.py:49

commit v11 on v9

--- a/solution.py
+++ b/solution.py
@@ -428,12 +428,13 @@
             flops=2 * tokens * members * rank * (ring * rows + outs),
             moved=12 * 2**20,
         )
+        weight[1] = after(weight[1], total)
         weight.append(onward(weight[1]))
         theirs.append(swap(weight[1], 1))
 
         for k, (bit, radix) in enumerate(rounds):
             if bit == members:
-                gives = [after(give, weight[2], sent if sides == 2 else block) for give in gives]
+                gives = [after(give, weight[2], block, sent if sides == 2 else block) for give in gives]
             came = [swap(give, j * bit) for j, give in zip(range(1, radix), gives)]
             if k == len(rounds) - 1:
                 break
@@ -451,45 +452,39 @@
             if bit == 2:
                 sent = give_back(0, first_block, gate=total)
                 later = give_back(1, block, gate=total)
-                weight[2] = after(weight[2], total)
-
-        split = [weight[2][p * height : (p + 1) * height] for p in range(parts)] if ring == 4 else []
-        last = []
-        if split:
-            last.append(onward(after(split[0], *came)))
+                weight[2] = after(weight[2], total, sent)
+
         owned_rows, message = call(
             functools.partial(square_kernel, len(came), lines),
             "square",
             [((owned, outs), f32), ((1, lines + 16, outs), bf16)],
             [total] + came,
         )
-        block = multiply(2, weight[2], swap(weight[2], 1), gate=owned_rows)
-        messages = after(message, last[0], block) if split else message
+        their_step = swap(weight[2], 1)
+        messages = message
         for bit, radix in reversed(rounds):
             if bit >= members:
                 came = [swap(messages, j * bit) for j in range(1, radix)]
                 messages = jnp.concatenate([messages] + came, axis=0)
-        for p in range(1, len(split)):
-            last.append(onward(after(split[p], *came)))
+
+        split = [weight[2][p * height : (p + 1) * height] for p in range(parts)] if ring == 4 else []
+        last = [onward(after(piece, *came)) for piece in split[:1]]
+        block = multiply(2, weight[2], their_step, gate=owned_rows)
         (square,) = call(gathered_kernel, "gathered", [((8, 128), f32)], [messages])
         if sides == 2:
             sent = give_back(2, block, gate=later)
             square = after(square, sent)
         squares = [square] + [swap(square, x) for x in range(1, members)]
-        new_first, new_second, whole = call(
+        last += [onward(after(piece, square)) for piece in split[1:]]
+        new_first, new_second, update = call(
             functools.partial(moment_kernel, lay, rows),
             "moment",
             [((owned, outs), f32), ((owned, outs), f32), ((ring, owned, outs), bf16)],
             squares + basis + [owned_rows, first_moment, second_moment, messages],
         )
-        blocks = []
-        if split:
-            block = multiply(3, last[0], swap(last[0], 1), 0, squares[0])
-            sent = give_back(3, after(block, *squares), 0)
-
+        whole = update
         for bit, radix in reversed(rounds[1:]):
             if bit < members:
-                whole = after(whole, sent)
                 whole = jnp.concatenate(
                     [whole] + [swap(whole, j * bit) for j in range(1, radix)], axis=0
                 )
@@ -503,8 +498,10 @@
             moved=8 * 2**20,
         )
 
-        for p in range(1, len(split)):
-            give_back(3, multiply(3, last[p], swap(last[p], 1), p * height), p * height)
+        for p in range(len(split)):
+            piece = after(last[p], update if p == 0 else sent)
+            block = multiply(3, piece, swap(piece, 1), p * height)
+            sent = give_back(3, block, p * height)
         if not split:
             for s in range(3, ring):
                 weight.append(onward(weight[s - 1]))

time: 173 us -> 177 us (1.023)
  starting transfers between devices: 30 us -> 33.7 us
    ppermute x27, waiting for transfers between devices: 54.8 us -> 61.6 us  [swap(): return lax.ppermute(value, 'dp', [(i, i ^ bit) for i in range(self.n)])]
    ppermute x7, waiting for transfers between devices: 63.8 us -> 58.2 us  [onward(): return lax.ppermute(value, 'dp', self.forward)]
    ppermute x27, starting transfers between devices: 22.5 us -> 24.7 us  [swap(): return lax.ppermute(value, 'dp', [(i, i ^ bit) for i in range(self.n)])]
where the time goes in v11:
time: 177 us
  waiting for transfers between devices  120 us (68%)
  starting transfers between devices  33.7 us (19%)
  Pallas kernels  18.9 us (11%)
  local copies, waits for them, and re-layouts  3.49 us (2%)
    ppermute x27, waiting for transfers between devices, swap(): return lax.ppermute(value, 'dp', [(i, i ^ bit) for i in range(self.n)])  61.6 us
    ppermute x7, waiting for transfers between devices, onward(): return lax.ppermute(value, 'dp', self.forward)  58.2 us
    ppermute x27, starting transfers between devices, swap(): return lax.ppermute(value, 'dp', [(i, i ^ bit) for i in range(self.n)])  24.7 us
    pallas_call x14, Pallas kernels, call(): pl.pallas_call(kernel, name=name, out_shape=[jax.ShapeDtypeStruct(shape,...  18.9 us
    ppermute x7, starting transfers between devices, onward(): return lax.ppermute(value, 'dp', self.forward)  9.02 us
  transfers between devices with their start and end apart: 34, of which 20 were waited for; matrix products, arithmetic and copies ran while one was open for 0% of the time, Pallas kernels for 10%

profile of v11, /device:TPU:0, one launch (start us, length us, event | category | flops | bytes accessed | tf_op | source)
XLA Modules:
  0.0 177.2 jit_solution(5687918402776035883)
XLA Ops:
  0.6 1.0 copy-done
  1.7 2.2 %copy-done.3 = bf16[256,8192]{1,0:T(8,128)(2,1)S(1)} copy-done((bf16[256,8192]{1,0:T(8,128)(2,1)S(1)}, bf16[256,8192]{1,0:T(8,128)(2,1)}, u32[]{:S(2)}) %copy-start.3) | copy-done | bytes 4194328
  4.5 3.0 %collective-permute-start.5 = (bf16[256,3072]{1,0:T(8,128)(2,1)S(1)}, bf16[256,3072]{1,0:T(8,128)(2,1)S(1)}, u32[]{:S(2)}, u32[]{:S(2)}) collective-permute-start(bf16[256,3072]{1,0:T(8,128)(2,1)S(1)} %get-tuple-element.56), channel_id=1, source_target_pairs={{0,2},{1,3},{2,0},{3,1},{4,6},{5,7},{6,4},{7,5},{8,10},{9,11},{10,... | collective-permute-start | bytes 4718600 | tf_op jit(solution)/shard_map/ppermute | solution.py:49
  7.7 1.6 collective-permute-start
  9.3 15.5 %collective-permute-done.refs_5_ = bf16[640,512]{1,0:T(8,128)(2,1)S(1)} collective-permute-done((bf16[640,512]{1,0:T(8,128)(2,1)S(1)}, bf16[640,512]{1,0:T(8,128)(2,1)S(1)}, u32[]{:S(2)}, u32[]{:S(2)}) %collective-permute-start) | collective-permute-done | bytes 655392 | tf_op jit(solution)/shard_map/ppermute | solution.py:52
  24.8 0.8 collective-permute-start.1
  25.9 16.1 %collective-permute-done.5.refs_2_ = bf16[256,3072]{1,0:T(8,128)(2,1)S(1)} collective-permute-done((bf16[256,3072]{1,0:T(8,128)(2,1)S(1)}, bf16[256,3072]{1,0:T(8,128)(2,1)S(1)}, u32[]{:S(2)}, u32[]{:S(2)}) %collective-permute-start.5) | collective-permute-done | bytes 1572896 | tf_op jit(solution)/shard_map/ppermute | solution.py:49
  42.2 1.9 %collective-permute-start.2 = (bf16[640,512]{1,0:T(8,128)(2,1)S(1)}, bf16[640,512]{1,0:T(8,128)(2,1)S(1)}, u32[]{:S(2)}, u32[]{:S(2)}) collective-permute-start(bf16[640,512]{1,0:T(8,128)(2,1)S(1)} %collective-permute-done.1.refs_6_), channel_id=1, source_target_pairs={{0,4},{1,5},{2,6},{3,7},{4,12},{5,13},{6,14},{7,15},{12,8},{13,9},... | collective-permute-start | bytes 1966088 | tf_op jit(solution)/shard_map/ppermute | solution.py:52
  44.2 1.5 collective-permute-start.7
  45.7 14.7 %collective-permute-done.2.refs_7_ = bf16[640,512]{1,0:T(8,128)(2,1)S(1)} collective-permute-done((bf16[640,512]{1,0:T(8,128)(2,1)S(1)}, bf16[640,512]{1,0:T(8,128)(2,1)S(1)}, u32[]{:S(2)}, u32[]{:S(2)}) %collective-permute-start.2) | collective-permute-done | bytes 655392 | tf_op jit(solution)/shard_map/ppermute | solution.py:52
  60.4 0.8 collective-permute-start.3
  61.2 2.1 %weight.5 = (bf16[256,8192]{1,0:T(8,128)(2,1)}, bf16[256,1024]{1,0:T(8,128)(2,1)S(1)}) custom-call(bf16[512,1024]{1,0:T(8,128)(2,1)S(1)} %convert_element_type.4.refs_0_, bf16[512,1024]{1,0:T(8,128)(2,1)S(1)} %collective-permute-done.4.refs_1_, bf16[256,1024]{1,0:T(8,128)(2,1)S(1)} %copy-done, bf16[256,1024]{1,0:T(8,128)(2,1)S(1)} %slice.30.refs_3_.refs_10_), custom_call_target="tpu_custom_call" | custom-call | flops 1073741824 | bytes 6291456 | tf_op jit(solution)/shard_map/weight/pallas_call | solution.py:318
  63.4 5.7 %collective-permute-done.7.refs_3_ = bf16[256,2048]{1,0:T(8,128)(2,1)S(1)} collective-permute-done((bf16[256,2048]{1,0:T(8,128)(2,1)S(1)}, bf16[256,2048]{1,0:T(8,128)(2,1)S(1)}, u32[]{:S(2)}, u32[]{:S(2)}) %collective-permute-start.7) | collective-permute-done | bytes 1048608 | tf_op jit(solution)/shard_map/ppermute | solution.py:49
  69.2 4.3 %project.1 = (f32[8,32,1024]{2,1,0:T(8,128)S(1)}, bf16[8,32,1024]{2,1,0:T(8,128)(2,1)S(1)}) custom-call(bf16[256,2048]{1,0:T(8,128)(2,1)S(1)} %get-tuple-element.58.refs_0_, bf16[256,2048]{1,0:T(8,128)(2,1)S(1)} %collective-permute-done.6.refs_1_, bf16[256,3072]{1,0:T(8,128)(2,1)S(1)} %collective-permute-done.5.refs_2_, ...), custom_call_target="tpu_custom_call" | custom-call | flops 3221225472 | bytes 12582912 | tf_op jit(solution)/shard_map/project/pallas_call | solution.py:318
  74.2 12.0 %collective-permute-done.3.refs_0_ = bf16[512,1024]{1,0:T(8,128)(2,1)S(1)} collective-permute-done((bf16[512,1024]{1,0:T(8,128)(2,1)S(1)}, bf16[512,1024]{1,0:T(8,128)(2,1)S(1)}, u32[]{:S(2)}, u32[]{:S(2)}) %collective-permute-start.3) | collective-permute-done | bytes 1048608 | tf_op jit(solution)/shard_map/ppermute | solution.py:52
  86.9 1.6 collective-permute-start.11
  88.5 5.2 %collective-permute-done.11.refs_1_ = bf16[4,32,1024]{2,1,0:T(8,128)(2,1)S(1)} collective-permute-done((bf16[4,32,1024]{2,1,0:T(8,128)(2,1)S(1)}, bf16[4,32,1024]{2,1,0:T(8,128)(2,1)S(1)}, u32[]{:S(2)}, u32[]{:S(2)}) %collective-permute-start.11) | collective-permute-done | bytes 262176 | tf_op jit(solution)/shard_map/ppermute | solution.py:49
  93.7 1.6 collective-permute-start.12
  95.3 9.9 %collective-permute-done.12.refs_4_ = bf16[256,1024]{1,0:T(8,128)(2,1)S(1)} collective-permute-done((bf16[256,1024]{1,0:T(8,128)(2,1)S(1)}, bf16[256,1024]{1,0:T(8,128)(2,1)S(1)}, u32[]{:S(2)}, u32[]{:S(2)}) %collective-permute-start.12) | collective-permute-done | bytes 524320 | tf_op jit(solution)/shard_map/ppermute | solution.py:49
  105.1 6.0 %collective-permute-done.9.refs_0_ = bf16[512,1024]{1,0:T(8,128)(2,1)S(1)} collective-permute-done((bf16[512,1024]{1,0:T(8,128)(2,1)S(1)}, bf16[512,1024]{1,0:T(8,128)(2,1)S(1)}, u32[]{:S(2)}, u32[]{:S(2)}) %collective-permute-start.9) | collective-permute-done | bytes 1048608 | tf_op jit(solution)/shard_map/ppermute | solution.py:52
  111.1 2.1 %weight.6 = (bf16[256,8192]{1,0:T(8,128)(2,1)}, bf16[256,1024]{1,0:T(8,128)(2,1)S(1)}) custom-call(bf16[512,1024]{1,0:T(8,128)(2,1)S(1)} %collective-permute-done.3.refs_0_, bf16[512,1024]{1,0:T(8,128)(2,1)S(1)} %collective-permute-done.13.refs_1_, bf16[256,1024]{1,0:T(8,128)(2,1)S(1)} %copy-done.1, ...), custom_call_target="tpu_custom_call", output_to_operand_aliasing={{0}: (4, {})} | custom-call | flops 1073741824 | bytes 6291456 | tf_op jit(solution)/shard_map/weight/pallas_call | solution.py:318
  113.2 1.2 collective-permute-start.22
  114.4 3.6 %collective-permute-start.16 = (bf16[1,32,1024]{2,1,0:T(8,128)(2,1)S(1)}, bf16[1,32,1024]{2,1,0:T(8,128)(2,1)S(1)}, u32[]{:S(2)}, u32[]{:S(2)}) collective-permute-start(bf16[1,32,1024]{2,1,0:T(8,128)(2,1)S(1)} %get-tuple-element.77), channel_id=1, source_target_pairs={{0,12},{1,13},{2,14},{3,15},{4,8},{5,9},{6,10},{7,11},{8,4},{9,5},... | collective-permute-start | bytes 196616 | tf_op jit(solution)/shard_map/ppermute | solution.py:49
  118.0 0.8 collective-permute-start.14
  118.8 2.3 %collective-permute-done.16.refs_3_ = bf16[1,32,1024]{2,1,0:T(8,128)(2,1)S(1)} collective-permute-done((bf16[1,32,1024]{2,1,0:T(8,128)(2,1)S(1)}, bf16[1,32,1024]{2,1,0:T(8,128)(2,1)S(1)}, u32[]{:S(2)}, u32[]{:S(2)}) %collective-permute-start.16) | collective-permute-done | bytes 65568 | tf_op jit(solution)/shard_map/ppermute | solution.py:49
  121.1 2.3 %collective-permute-done.15.refs_2_ = bf16[1,32,1024]{2,1,0:T(8,128)(2,1)S(1)} collective-permute-done((bf16[1,32,1024]{2,1,0:T(8,128)(2,1)S(1)}, bf16[1,32,1024]{2,1,0:T(8,128)(2,1)S(1)}, u32[]{:S(2)}, u32[]{:S(2)}) %collective-permute-start.15) | collective-permute-done | bytes 65568 | tf_op jit(solution)/shard_map/ppermute | solution.py:49
  123.9 1.5 collective-permute-start.17
  125.4 1.6 collective-permute-start.18
  127.0 1.4 collective-permute-start.19
  128.4 2.1 %weight.7 = (bf16[256,8192]{1,0:T(8,128)(2,1)}, bf16[256,1024]{1,0:T(8,128)(2,1)S(1)}) custom-call(bf16[512,1024]{1,0:T(8,128)(2,1)S(1)} %collective-permute-done.9.refs_0_, bf16[512,1024]{1,0:T(8,128)(2,1)S(1)} %collective-permute-done.21.refs_1_, bf16[256,1024]{1,0:T(8,128)(2,1)S(1)} %copy-done.1, ...), custom_call_target="tpu_custom_call", output_to_operand_aliasing={{0}: (5, {})} | custom-call | flops 1073741824 | bytes 6291456 | tf_op jit(solution)/shard_map/weight/pallas_call | solution.py:318
  130.5 0.7 collective-permute-start.23
  131.3 3.9 %collective-permute-done.18 = bf16[1,48,1024]{2,1,0:T(8,128)(2,1)S(1)} collective-permute-done((bf16[1,48,1024]{2,1,0:T(8,128)(2,1)S(1)}, bf16[1,48,1024]{2,1,0:T(8,128)(2,1)S(1)}, u32[]{:S(2)}, u32[]{:S(2)}) %collective-permute-start.18) | collective-permute-done | bytes 98336 | tf_op jit(solution)/shard_map/ppermute | solution.py:49
  135.2 1.8 %collective-permute-start.20 = (bf16[256,1024]{1,0:T(8,128)(2,1)S(1)}, bf16[256,1024]{1,0:T(8,128)(2,1)S(1)}, u32[]{:S(2)}, u32[]{:S(2)}) collective-permute-start(bf16[256,1024]{1,0:T(8,128)(2,1)S(1)} %get-tuple-element.79), channel_id=1, source_target_pairs={{0,4},{1,5},{2,6},{3,7},{4,12},{5,13},{6,14},{7,15},{12,8},{13,9},... | collective-permute-start | bytes 1572872 | tf_op jit(solution)/shard_map/ppermute | solution.py:52
  137.2 5.6 %collective-permute-done.23.refs_4_ = bf16[256,1024]{1,0:T(8,128)(2,1)S(1)} collective-permute-done((bf16[256,1024]{1,0:T(8,128)(2,1)S(1)}, bf16[256,1024]{1,0:T(8,128)(2,1)S(1)}, u32[]{:S(2)}, u32[]{:S(2)}) %collective-permute-start.23) | collective-permute-done | bytes 524320 | tf_op jit(solution)/shard_map/ppermute | solution.py:49
  142.7 1.2 collective-permute-start.25
  144.6 1.7 collective-permute-done.25.refs_2_
  146.9 1.1 moment.1
  148.6 1.5 collective-permute-start.31
  150.2 1.5 weight.8
  151.7 0.9 collective-permute-start.28
  152.5 1.2 collective-permute-start.29
  153.8 9.7 %collective-permute-done.31.refs_0_ = bf16[256,1024]{1,0:T(8,128)(2,1)S(1)} collective-permute-done((bf16[256,1024]{1,0:T(8,128)(2,1)S(1)}, bf16[256,1024]{1,0:T(8,128)(2,1)S(1)}, u32[]{:S(2)}, u32[]{:S(2)}) %collective-permute-start.31) | collective-permute-done | bytes 524320 | tf_op jit(solution)/shard_map/ppermute | solution.py:52
  163.5 2.3 %collective-permute-done.29 = bf16[4,32,1024]{2,1,0:T(8,128)(2,1)S(1)} collective-permute-done((bf16[4,32,1024]{2,1,0:T(8,128)(2,1)S(1)}, bf16[4,32,1024]{2,1,0:T(8,128)(2,1)S(1)}, u32[]{:S(2)}, u32[]{:S(2)}) %collective-permute-start.29) | collective-permute-done | bytes 262176 | tf_op jit(solution)/shard_map/ppermute | solution.py:49
  166.0 1.5 weight.9
  167.5 0.9 collective-permute-start.33
  168.4 2.2 %back.1 = f32[512,1024]{1,0:T(8,128)} custom-call(bf16[512,512]{1,0:T(8,128)(2,1)S(1)} %copy-done.4, bf16[8,32,1024]{2,1,0:T(8,128)(2,1)S(1)} %constant_dynamic-update-slice_fusion.4.near, bf16[8,32,1024]{2,1,0:T(8,128)(2,1)S(1)} %collective-permute-done.30.other, f32[512,1024]{1,0:T(8,128)S(1)} %copy-done.2), custom_call_target="tpu_custom_call" | custom-call | flops 536870912 | bytes 8388608 | tf_op jit(solution)/shard_map/back/pallas_call | solution.py:318
  170.6 5.6 %collective-permute-done.33.refs_1_ = bf16[256,512]{1,0:T(8,128)(2,1)S(1)} collective-permute-done((bf16[256,512]{1,0:T(8,128)(2,1)S(1)}, bf16[256,512]{1,0:T(8,128)(2,1)S(1)}, u32[]{:S(2)}, u32[]{:S(2)}) %collective-permute-start.33) | collective-permute-done | bytes 262176 | tf_op jit(solution)/shard_map/ppermute | solution.py:49
  176.2 0.8 last.1
  (63 shorter events, 5.6 us)
Async XLA Ops:
  0.6 1.0 copy-start
  1.7 2.2 %copy-start.3 = (bf16[256,8192]{1,0:T(8,128)(2,1)S(1)}, bf16[256,8192]{1,0:T(8,128)(2,1)}, u32[]{:S(2)}) copy-start(bf16[256,8192]{1,0:T(8,128)(2,1)} %act.1) | copy-start | bytes 12582916
  3.9 3.7 %copy-start.6 = (f32[32,1024]{1,0:T(8,128)S(1)}, f32[32,1024]{1,0:T(8,128)}, u32[]{:S(2)}) copy-start(f32[32,1024]{1,0:T(8,128)} %refs_9_.1) | copy-start | bytes 393220
  3.9 3.7 %copy-start.5 = (f32[32,1024]{1,0:T(8,128)S(1)}, f32[32,1024]{1,0:T(8,128)}, u32[]{:S(2)}) copy-start(f32[32,1024]{1,0:T(8,128)} %refs_10_.1) | copy-start | bytes 393220
  3.9 3.8 %copy-start.4 = (bf16[512,512]{1,0:T(8,128)(2,1)S(1)}, bf16[512,512]{1,0:T(8,128)(2,1)}, u32[]{:S(2)}) copy-start(bf16[512,512]{1,0:T(8,128)(2,1)} %basis.1) | copy-start | bytes 1572868
  3.9 21.7 %copy-start.2 = (f32[512,1024]{1,0:T(8,128)S(1)}, f32[512,1024]{1,0:T(8,128)}, u32[]{:S(2)}) copy-start(f32[512,1024]{1,0:T(8,128)} %master.1) | copy-start | bytes 6291460
  4.5 37.4 %collective-permute-start.5 = (bf16[256,3072]{1,0:T(8,128)(2,1)S(1)}, bf16[256,3072]{1,0:T(8,128)(2,1)S(1)}, u32[]{:S(2)}, u32[]{:S(2)}) collective-permute-start(bf16[256,3072]{1,0:T(8,128)(2,1)S(1)} %get-tuple-element.56), channel_id=1, source_target_pairs={{0,2},{1,3},{2,0},{3,1},{4,6},{5,7},{6,4},{7,5},{8,10},{9,11},{10,... | collective-permute-start | bytes 4718600 | tf_op jit(solution)/shard_map/ppermute | solution.py:49
  7.7 17.1 %collective-permute-start = (bf16[640,512]{1,0:T(8,128)(2,1)S(1)}, bf16[640,512]{1,0:T(8,128)(2,1)S(1)}, u32[]{:S(2)}, u32[]{:S(2)}) collective-permute-start(bf16[640,512]{1,0:T(8,128)(2,1)S(1)} %fusion.refs_4_), channel_id=1, source_target_pairs={{0,4},{1,5},{2,6},{3,7},{4,12},{5,13},{6,14},{7,15},{12,8},{13,9},... | collective-permute-start | bytes 1966088 | tf_op jit(solution)/shard_map/ppermute | solution.py:52
  24.8 17.3 %collective-permute-start.1 = (bf16[640,512]{1,0:T(8,128)(2,1)S(1)}, bf16[640,512]{1,0:T(8,128)(2,1)S(1)}, u32[]{:S(2)}, u32[]{:S(2)}) collective-permute-start(bf16[640,512]{1,0:T(8,128)(2,1)S(1)} %collective-permute-done.refs_5_), channel_id=1, source_target_pairs={{0,4},{1,5},{2,6},{3,7},{4,12},{5,13},{6,14},{7,15},{12,8},{13,9},... | collective-permute-start | bytes 1966088 | tf_op jit(solution)/shard_map/ppermute | solution.py:52
  25.8 35.4 %collective-permute-start.4 = (bf16[512,1024]{1,0:T(8,128)(2,1)S(1)}, bf16[512,1024]{1,0:T(8,128)(2,1)S(1)}, u32[]{:S(2)}, u32[]{:S(2)}) collective-permute-start(bf16[512,1024]{1,0:T(8,128)(2,1)S(1)} %convert_element_type.4.refs_0_), channel_id=1, source_target_pairs={{0,1},{1,0},{2,3},{3,2},{4,5},{5,4},{6,7},{7,6},{8,9},{9,8},{10,11... | collective-permute-start | bytes 3145736 | tf_op jit(solution)/shard_map/ppermute | solution.py:49
  42.1 21.2 %collective-permute-start.8 = (bf16[512,1024]{1,0:T(8,128)(2,1)S(1)}, bf16[512,1024]{1,0:T(8,128)(2,1)S(1)}, u32[]{:S(2)}, u32[]{:S(2)}) collective-permute-start(bf16[512,1024]{1,0:T(8,128)(2,1)S(1)} %pad_maximum_fusion), channel_id=1, source_target_pairs={{0,1},{1,0},{2,3},{3,2},{4,5},{5,4},{6,7},{7,6},{8,9},{9,8},{10,11... | collective-permute-start | bytes 3145736 | tf_op jit(solution)/shard_map/ppermute | solution.py:49
  42.2 18.2 %collective-permute-start.2 = (bf16[640,512]{1,0:T(8,128)(2,1)S(1)}, bf16[640,512]{1,0:T(8,128)(2,1)S(1)}, u32[]{:S(2)}, u32[]{:S(2)}) collective-permute-start(bf16[640,512]{1,0:T(8,128)(2,1)S(1)} %collective-permute-done.1.refs_6_), channel_id=1, source_target_pairs={{0,4},{1,5},{2,6},{3,7},{4,12},{5,13},{6,14},{7,15},{12,8},{13,9},... | collective-permute-start | bytes 1966088 | tf_op jit(solution)/shard_map/ppermute | solution.py:52
  44.0 19.4 %collective-permute-start.6 = (bf16[256,2048]{1,0:T(8,128)(2,1)S(1)}, bf16[256,2048]{1,0:T(8,128)(2,1)S(1)}, u32[]{:S(2)}, u32[]{:S(2)}) collective-permute-start(bf16[256,2048]{1,0:T(8,128)(2,1)S(1)} %get-tuple-element.59), channel_id=1, source_target_pairs={{0,1},{1,0},{2,3},{3,2},{4,5},{5,4},{6,7},{7,6},{8,9},{9,8},{10,11... | collective-permute-start | bytes 3145736 | tf_op jit(solution)/shard_map/ppermute | solution.py:49
  44.2 25.0 %copy-start.1 = (bf16[256,1024]{1,0:T(8,128)(2,1)S(1)}, bf16[256,1024]{1,0:T(8,128)(2,1)}, u32[]{:S(2)}) copy-start(bf16[256,1024]{1,0:T(8,128)(2,1)} %refs_2_.9) | copy-start | bytes 1572868
  44.2 25.0 %collective-permute-start.7 = (bf16[256,2048]{1,0:T(8,128)(2,1)S(1)}, bf16[256,2048]{1,0:T(8,128)(2,1)S(1)}, u32[]{:S(2)}, u32[]{:S(2)}) collective-permute-start(bf16[256,2048]{1,0:T(8,128)(2,1)S(1)} %get-tuple-element.60), channel_id=1, source_target_pairs={{0,3},{1,2},{2,1},{3,0},{4,7},{5,6},{6,5},{7,4},{8,11},{9,10},{10,... | collective-permute-start | bytes 3145736 | tf_op jit(solution)/shard_map/ppermute | solution.py:49
  60.4 25.8 %collective-permute-start.3 = (bf16[512,1024]{1,0:T(8,128)(2,1)S(1)}, bf16[512,1024]{1,0:T(8,128)(2,1)S(1)}, u32[]{:S(2)}, u32[]{:S(2)}) collective-permute-start(bf16[512,1024]{1,0:T(8,128)(2,1)S(1)} %convert_element_type.4.refs_0_), channel_id=1, source_target_pairs={{0,4},{1,5},{2,6},{3,7},{4,12},{5,13},{6,14},{7,15},{12,8},{13,9},... | collective-permute-start | bytes 3145736 | tf_op jit(solution)/shard_map/ppermute | solution.py:52
  73.5 13.3 %collective-permute-start.10 = (bf16[8,32,1024]{2,1,0:T(8,128)(2,1)S(1)}, bf16[8,32,1024]{2,1,0:T(8,128)(2,1)S(1)}, u32[]{:S(2)}, u32[]{:S(2)}) collective-permute-start(bf16[8,32,1024]{2,1,0:T(8,128)(2,1)S(1)} %get-tuple-element.63), channel_id=1, source_target_pairs={{0,1},{1,0},{2,3},{3,2},{4,5},{5,4},{6,7},{7,6},{8,9},{9,8},{10,11... | collective-permute-start | bytes 1572872 | tf_op jit(solution)/shard_map/ppermute | solution.py:49
  86.2 24.9 %collective-permute-start.9 = (bf16[512,1024]{1,0:T(8,128)(2,1)S(1)}, bf16[512,1024]{1,0:T(8,128)(2,1)S(1)}, u32[]{:S(2)}, u32[]{:S(2)}) collective-permute-start(bf16[512,1024]{1,0:T(8,128)(2,1)S(1)} %collective-permute-done.3.refs_0_), channel_id=1, source_target_pairs={{0,4},{1,5},{2,6},{3,7},{4,12},{5,13},{6,14},{7,15},{12,8},{13,9},... | collective-permute-start | bytes 3145736 | tf_op jit(solution)/shard_map/ppermute | solution.py:52
  86.9 6.7 %collective-permute-start.11 = (bf16[4,32,1024]{2,1,0:T(8,128)(2,1)S(1)}, bf16[4,32,1024]{2,1,0:T(8,128)(2,1)S(1)}, u32[]{:S(2)}, u32[]{:S(2)}) collective-permute-start(bf16[4,32,1024]{2,1,0:T(8,128)(2,1)S(1)} %get-tuple-element.65), channel_id=1, source_target_pairs={{0,2},{1,3},{2,0},{3,1},{4,6},{5,7},{6,4},{7,5},{8,10},{9,11},{10,... | collective-permute-start | bytes 786440 | tf_op jit(solution)/shard_map/ppermute | solution.py:49
  93.7 11.4 %collective-permute-start.12 = (bf16[256,1024]{1,0:T(8,128)(2,1)S(1)}, bf16[256,1024]{1,0:T(8,128)(2,1)S(1)}, u32[]{:S(2)}, u32[]{:S(2)}) collective-permute-start(bf16[256,1024]{1,0:T(8,128)(2,1)S(1)} %get-tuple-element.67), channel_id=1, source_target_pairs={{0,2},{1,3},{2,0},{3,1},{4,6},{5,7},{6,4},{7,5},{8,10},{9,11},{10,... | collective-permute-start | bytes 1572872 | tf_op jit(solution)/shard_map/ppermute | solution.py:49
  95.3 15.8 %collective-permute-start.13 = (bf16[512,1024]{1,0:T(8,128)(2,1)S(1)}, bf16[512,1024]{1,0:T(8,128)(2,1)S(1)}, u32[]{:S(2)}, u32[]{:S(2)}) collective-permute-start(bf16[512,1024]{1,0:T(8,128)(2,1)S(1)} %collective-permute-done.3.refs_0_), channel_id=1, source_target_pairs={{0,1},{1,0},{2,3},{3,2},{4,5},{5,4},{6,7},{7,6},{8,9},{9,8},{10,11... | collective-permute-start | bytes 3145736 | tf_op jit(solution)/shard_map/ppermute | solution.py:49
  111.1 17.3 %collective-permute-start.21 = (bf16[512,1024]{1,0:T(8,128)(2,1)S(1)}, bf16[512,1024]{1,0:T(8,128)(2,1)S(1)}, u32[]{:S(2)}, u32[]{:S(2)}) collective-permute-start(bf16[512,1024]{1,0:T(8,128)(2,1)S(1)} %collective-permute-done.9.refs_0_), channel_id=1, source_target_pairs={{0,1},{1,0},{2,3},{3,2},{4,5},{5,4},{6,7},{7,6},{8,9},{9,8},{10,11... | collective-permute-start | bytes 3145736 | tf_op jit(solution)/shard_map/ppermute | solution.py:49
  113.2 17.3 %collective-permute-start.22 = (bf16[256,1024]{1,0:T(8,128)(2,1)S(1)}, bf16[256,1024]{1,0:T(8,128)(2,1)S(1)}, u32[]{:S(2)}, u32[]{:S(2)}) collective-permute-start(bf16[256,1024]{1,0:T(8,128)(2,1)S(1)} %get-tuple-element.84), channel_id=1, source_target_pairs={{0,2},{1,3},{2,0},{3,1},{4,6},{5,7},{6,4},{7,5},{8,10},{9,11},{10,... | collective-permute-start | bytes 1572872 | tf_op jit(solution)/shard_map/ppermute | solution.py:49
  114.4 6.7 %collective-permute-start.16 = (bf16[1,32,1024]{2,1,0:T(8,128)(2,1)S(1)}, bf16[1,32,1024]{2,1,0:T(8,128)(2,1)S(1)}, u32[]{:S(2)}, u32[]{:S(2)}) collective-permute-start(bf16[1,32,1024]{2,1,0:T(8,128)(2,1)S(1)} %get-tuple-element.77), channel_id=1, source_target_pairs={{0,12},{1,13},{2,14},{3,15},{4,8},{5,9},{6,10},{7,11},{8,4},{9,5},... | collective-permute-start | bytes 196616 | tf_op jit(solution)/shard_map/ppermute | solution.py:49
  118.0 5.4 %collective-permute-start.15 = (bf16[1,32,1024]{2,1,0:T(8,128)(2,1)S(1)}, bf16[1,32,1024]{2,1,0:T(8,128)(2,1)S(1)}, u32[]{:S(2)}, u32[]{:S(2)}) collective-permute-start(bf16[1,32,1024]{2,1,0:T(8,128)(2,1)S(1)} %get-tuple-element.75), channel_id=1, source_target_pairs={{0,8},{1,9},{2,10},{3,11},{4,12},{5,13},{6,14},{7,15},{8,0},{9,1},... | collective-permute-start | bytes 196616 | tf_op jit(solution)/shard_map/ppermute | solution.py:49
  118.0 5.7 %collective-permute-start.14 = (bf16[1,32,1024]{2,1,0:T(8,128)(2,1)S(1)}, bf16[1,32,1024]{2,1,0:T(8,128)(2,1)S(1)}, u32[]{:S(2)}, u32[]{:S(2)}) collective-permute-start(bf16[1,32,1024]{2,1,0:T(8,128)(2,1)S(1)} %get-tuple-element.73), channel_id=1, source_target_pairs={{0,4},{1,5},{2,6},{3,7},{4,0},{5,1},{6,2},{7,3},{8,12},{9,13},{10,... | collective-permute-start | bytes 196616 | tf_op jit(solution)/shard_map/ppermute | solution.py:49
  123.9 7.4 %collective-permute-start.17 = (bf16[1,48,1024]{2,1,0:T(8,128)(2,1)S(1)}, bf16[1,48,1024]{2,1,0:T(8,128)(2,1)S(1)}, u32[]{:S(2)}, u32[]{:S(2)}) collective-permute-start(bf16[1,48,1024]{2,1,0:T(8,128)(2,1)S(1)} %get-tuple-element.78), channel_id=1, source_target_pairs={{0,4},{1,5},{2,6},{3,7},{4,0},{5,1},{6,2},{7,3},{8,12},{9,13},{10,... | collective-permute-start | bytes 294920 | tf_op jit(solution)/shard_map/ppermute | solution.py:49
  125.4 9.8 %collective-permute-start.18 = (bf16[1,48,1024]{2,1,0:T(8,128)(2,1)S(1)}, bf16[1,48,1024]{2,1,0:T(8,128)(2,1)S(1)}, u32[]{:S(2)}, u32[]{:S(2)}) collective-permute-start(bf16[1,48,1024]{2,1,0:T(8,128)(2,1)S(1)} %get-tuple-element.78), channel_id=1, source_target_pairs={{0,8},{1,9},{2,10},{3,11},{4,12},{5,13},{6,14},{7,15},{8,0},{9,1},... | collective-permute-start | bytes 294920 | tf_op jit(solution)/shard_map/ppermute | solution.py:49
  127.0 8.2 %collective-permute-start.19 = (bf16[1,48,1024]{2,1,0:T(8,128)(2,1)S(1)}, bf16[1,48,1024]{2,1,0:T(8,128)(2,1)S(1)}, u32[]{:S(2)}, u32[]{:S(2)}) collective-permute-start(bf16[1,48,1024]{2,1,0:T(8,128)(2,1)S(1)} %get-tuple-element.78), channel_id=1, source_target_pairs={{0,12},{1,13},{2,14},{3,15},{4,8},{5,9},{6,10},{7,11},{8,4},{9,5},... | collective-permute-start | bytes 294920 | tf_op jit(solution)/shard_map/ppermute | solution.py:49
  130.5 12.2 %collective-permute-start.23 = (bf16[256,1024]{1,0:T(8,128)(2,1)S(1)}, bf16[256,1024]{1,0:T(8,128)(2,1)S(1)}, u32[]{:S(2)}, u32[]{:S(2)}) collective-permute-start(bf16[256,1024]{1,0:T(8,128)(2,1)S(1)} %get-tuple-element.85), channel_id=1, source_target_pairs={{0,2},{1,3},{2,0},{3,1},{4,6},{5,7},{6,4},{7,5},{8,10},{9,11},{10,... | collective-permute-start | bytes 1572872 | tf_op jit(solution)/shard_map/ppermute | solution.py:49
  135.2 13.1 %collective-permute-start.20 = (bf16[256,1024]{1,0:T(8,128)(2,1)S(1)}, bf16[256,1024]{1,0:T(8,128)(2,1)S(1)}, u32[]{:S(2)}, u32[]{:S(2)}) collective-permute-start(bf16[256,1024]{1,0:T(8,128)(2,1)S(1)} %get-tuple-element.79), channel_id=1, source_target_pairs={{0,4},{1,5},{2,6},{3,7},{4,12},{5,13},{6,14},{7,15},{12,8},{13,9},... | collective-permute-start | bytes 1572872 | tf_op jit(solution)/shard_map/ppermute | solution.py:52
  142.7 1.9 %collective-permute-start.24 = (f32[8,128]{1,0:T(8,128)S(1)}, f32[8,128]{1,0:T(8,128)S(1)}, u32[]{:S(2)}, u32[]{:S(2)}) collective-permute-start(f32[8,128]{1,0:T(8,128)S(1)} %gathered.1.refs_0_), channel_id=1, source_target_pairs={{0,1},{1,0},{2,3},{3,2},{4,5},{5,4},{6,7},{7,6},{8,9},{9,8},{10,11... | collective-permute-start | bytes 12296 | tf_op jit(solution)/shard_map/ppermute | solution.py:49
  142.7 3.6 %collective-permute-start.25 = (f32[8,128]{1,0:T(8,128)S(1)}, f32[8,128]{1,0:T(8,128)S(1)}, u32[]{:S(2)}, u32[]{:S(2)}) collective-permute-start(f32[8,128]{1,0:T(8,128)S(1)} %gathered.1.refs_0_), channel_id=1, source_target_pairs={{0,2},{1,3},{2,0},{3,1},{4,6},{5,7},{6,4},{7,5},{8,10},{9,11},{10,... | collective-permute-start | bytes 12296 | tf_op jit(solution)/shard_map/ppermute | solution.py:49
  143.9 3.0 %collective-permute-start.26 = (f32[8,128]{1,0:T(8,128)S(1)}, f32[8,128]{1,0:T(8,128)S(1)}, u32[]{:S(2)}, u32[]{:S(2)}) collective-permute-start(f32[8,128]{1,0:T(8,128)S(1)} %gathered.1.refs_0_), channel_id=1, source_target_pairs={{0,3},{1,2},{2,1},{3,0},{4,7},{5,6},{6,5},{7,4},{8,11},{9,10},{10,... | collective-permute-start | bytes 12296 | tf_op jit(solution)/shard_map/ppermute | solution.py:49
  148.3 1.9 %collective-permute-start.27 = (bf16[256,1024]{1,0:T(8,128)(2,1)S(1)}, bf16[256,1024]{1,0:T(8,128)(2,1)S(1)}, u32[]{:S(2)}, u32[]{:S(2)}) collective-permute-start(bf16[256,1024]{1,0:T(8,128)(2,1)S(1)} %collective-permute-done.20.refs_0_), channel_id=1, source_target_pairs={{0,1},{1,0},{2,3},{3,2},{4,5},{5,4},{6,7},{7,6},{8,9},{9,8},{10,11... | collective-permute-start | bytes 1572872 | tf_op jit(solution)/shard_map/ppermute | solution.py:49
  148.6 14.9 %collective-permute-start.31 = (bf16[256,1024]{1,0:T(8,128)(2,1)S(1)}, bf16[256,1024]{1,0:T(8,128)(2,1)S(1)}, u32[]{:S(2)}, u32[]{:S(2)}) collective-permute-start(bf16[256,1024]{1,0:T(8,128)(2,1)S(1)} %get-tuple-element.92), channel_id=1, source_target_pairs={{0,4},{1,5},{2,6},{3,7},{4,12},{5,13},{6,14},{7,15},{12,8},{13,9},... | collective-permute-start | bytes 1572872 | tf_op jit(solution)/shard_map/ppermute | solution.py:52
  151.7 11.8 %collective-permute-start.28 = (bf16[256,512]{1,0:T(8,128)(2,1)S(1)}, bf16[256,512]{1,0:T(8,128)(2,1)S(1)}, u32[]{:S(2)}, u32[]{:S(2)}) collective-permute-start(bf16[256,512]{1,0:T(8,128)(2,1)S(1)} %get-tuple-element.90), channel_id=1, source_target_pairs={{0,2},{1,3},{2,0},{3,1},{4,6},{5,7},{6,4},{7,5},{8,10},{9,11},{10,... | collective-permute-start | bytes 786440 | tf_op jit(solution)/shard_map/ppermute | solution.py:49
  152.5 13.3 %collective-permute-start.29 = (bf16[4,32,1024]{2,1,0:T(8,128)(2,1)S(1)}, bf16[4,32,1024]{2,1,0:T(8,128)(2,1)S(1)}, u32[]{:S(2)}, u32[]{:S(2)}) collective-permute-start(bf16[4,32,1024]{2,1,0:T(8,128)(2,1)S(1)} %get-tuple-element.87), channel_id=1, source_target_pairs={{0,2},{1,3},{2,0},{3,1},{4,6},{5,7},{6,4},{7,5},{8,10},{9,11},{10,... | collective-permute-start | bytes 786440 | tf_op jit(solution)/shard_map/ppermute | solution.py:49
  163.5 2.5 %collective-permute-start.32 = (bf16[256,1024]{1,0:T(8,128)(2,1)S(1)}, bf16[256,1024]{1,0:T(8,128)(2,1)S(1)}, u32[]{:S(2)}, u32[]{:S(2)}) collective-permute-start(bf16[256,1024]{1,0:T(8,128)(2,1)S(1)} %collective-permute-done.31.refs_0_), channel_id=1, source_target_pairs={{0,1},{1,0},{2,3},{3,2},{4,5},{5,4},{6,7},{7,6},{8,9},{9,8},{10,11... | collective-permute-start | bytes 1572872 | tf_op jit(solution)/shard_map/ppermute | solution.py:49
  165.9 2.5 %collective-permute-start.30 = (bf16[8,32,1024]{2,1,0:T(8,128)(2,1)S(1)}, bf16[8,32,1024]{2,1,0:T(8,128)(2,1)S(1)}, u32[]{:S(2)}, u32[]{:S(2)}) collective-permute-start(bf16[8,32,1024]{2,1,0:T(8,128)(2,1)S(1)} %constant_dynamic-update-slice_fusion.4.near), channel_id=1, source_target_pairs={{0,1},{1,0},{2,3},{3,2},{4,5},{5,4},{6,7},{7,6},{8,9},{9,8},{10,11... | collective-permute-start | bytes 1572872 | tf_op jit(solution)/shard_map/ppermute | solution.py:49
  167.5 8.8 %collective-permute-start.33 = (bf16[256,512]{1,0:T(8,128)(2,1)S(1)}, bf16[256,512]{1,0:T(8,128)(2,1)S(1)}, u32[]{:S(2)}, u32[]{:S(2)}) collective-permute-start(bf16[256,512]{1,0:T(8,128)(2,1)S(1)} %get-tuple-element.95), channel_id=1, source_target_pairs={{0,2},{1,3},{2,0},{3,1},{4,6},{5,7},{6,4},{7,5},{8,10},{9,11},{10,... | collective-permute-start | bytes 786440 | tf_op jit(solution)/shard_map/ppermute | solution.py:49

commit v12 on v9

--- a/solution.py
+++ b/solution.py
@@ -487,12 +487,14 @@
             block = multiply(3, last[0], swap(last[0], 1), 0, squares[0])
             sent = give_back(3, after(block, *squares), 0)
 
+        for p in range(1, len(split)):
+            piece = after(last[p], sent)
+            block = multiply(3, piece, swap(piece, 1), p * height)
+            sent = give_back(3, block, p * height)
+
         for bit, radix in reversed(rounds[1:]):
             if bit < members:
-                whole = after(whole, sent)
-                whole = jnp.concatenate(
-                    [whole] + [swap(whole, j * bit) for j in range(1, radix)], axis=0
-                )
+                whole = jnp.concatenate([whole, after(swap(whole, bit), block)], axis=0)
         (new_master,) = call(
             functools.partial(back_kernel, lay, owned),
             "back",
@@ -503,8 +505,6 @@
             moved=8 * 2**20,
         )
 
-        for p in range(1, len(split)):
-            give_back(3, multiply(3, last[p], swap(last[p], 1), p * height), p * height)
         if not split:
             for s in range(3, ring):
                 weight.append(onward(weight[s - 1]))

time: 173 us -> 173 us (level)
    ppermute x7, waiting for transfers between devices: 63.8 us -> 69.8 us  [onward(): return lax.ppermute(value, 'dp', self.forward)]
    ppermute x27, waiting for transfers between devices: 54.8 us -> 49.3 us  [swap(): return lax.ppermute(value, 'dp', [(i, i ^ bit) for i in range(self.n)])]
  transfers between devices with their start and end apart: 34 -> 34, of which waited for: 20 -> 23; matrix products, arithmetic and copies ran while one was open for 0% -> 0% of each run, Pallas kernels for 10% -> 10%
where the time goes in v12:
time: 173 us
  waiting for transfers between devices  119 us (69%)
  starting transfers between devices  30 us (17%)
  Pallas kernels  18.9 us (11%)
  local copies, waits for them, and re-layouts  3.48 us (2%)
    ppermute x7, waiting for transfers between devices, onward(): return lax.ppermute(value, 'dp', self.forward)  69.8 us
    ppermute x27, waiting for transfers between devices, swap(): return lax.ppermute(value, 'dp', [(i, i ^ bit) for i in range(self.n)])  49.3 us
    ppermute x27, starting transfers between devices, swap(): return lax.ppermute(value, 'dp', [(i, i ^ bit) for i in range(self.n)])  22.6 us
    pallas_call x14, Pallas kernels, call(): pl.pallas_call(kernel, name=name, out_shape=[jax.ShapeDtypeStruct(shape,...  18.9 us
    ppermute x7, starting transfers between devices, onward(): return lax.ppermute(value, 'dp', self.forward)  7.42 us
  transfers between devices with their start and end apart: 34, of which 23 were waited for; matrix products, arithmetic and copies ran while one was open for 0% of the time, Pallas kernels for 10%

profile of v12, /device:TPU:0, one launch (start us, length us, event | category | flops | bytes accessed | tf_op | source)
XLA Modules:
  0.0 172.8 jit_solution(8740367610261748330)
XLA Ops:
  0.6 1.0 copy-done
  1.7 2.2 %copy-done.3 = bf16[256,8192]{1,0:T(8,128)(2,1)S(1)} copy-done((bf16[256,8192]{1,0:T(8,128)(2,1)S(1)}, bf16[256,8192]{1,0:T(8,128)(2,1)}, u32[]{:S(2)}) %copy-start.3) | copy-done | bytes 4194328
  3.9 0.7 cut.1
  4.5 3.0 %collective-permute-start.6 = (bf16[256,3072]{1,0:T(8,128)(2,1)S(1)}, bf16[256,3072]{1,0:T(8,128)(2,1)S(1)}, u32[]{:S(2)}, u32[]{:S(2)}) collective-permute-start(bf16[256,3072]{1,0:T(8,128)(2,1)S(1)} %get-tuple-element.58), channel_id=1, source_target_pairs={{0,2},{1,3},{2,0},{3,1},{4,6},{5,7},{6,4},{7,5},{8,10},{9,11},{10,... | collective-permute-start | bytes 4718600 | tf_op jit(solution)/shard_map/ppermute | solution.py:49
  7.7 1.6 collective-permute-start
  9.3 15.5 %collective-permute-done.refs_5_ = bf16[640,512]{1,0:T(8,128)(2,1)S(1)} collective-permute-done((bf16[640,512]{1,0:T(8,128)(2,1)S(1)}, bf16[640,512]{1,0:T(8,128)(2,1)S(1)}, u32[]{:S(2)}, u32[]{:S(2)}) %collective-permute-start) | collective-permute-done | bytes 655392 | tf_op jit(solution)/shard_map/ppermute | solution.py:52
  24.8 0.8 collective-permute-start.1
  25.9 15.1 %collective-permute-done.1.refs_6_ = bf16[640,512]{1,0:T(8,128)(2,1)S(1)} collective-permute-done((bf16[640,512]{1,0:T(8,128)(2,1)S(1)}, bf16[640,512]{1,0:T(8,128)(2,1)S(1)}, u32[]{:S(2)}, u32[]{:S(2)}) %collective-permute-start.1) | collective-permute-done | bytes 655392 | tf_op jit(solution)/shard_map/ppermute | solution.py:52
  41.0 0.8 collective-permute-start.2
  42.7 1.4 collective-permute-start.8
  44.1 12.2 %collective-permute-done.2.refs_7_ = bf16[640,512]{1,0:T(8,128)(2,1)S(1)} collective-permute-done((bf16[640,512]{1,0:T(8,128)(2,1)S(1)}, bf16[640,512]{1,0:T(8,128)(2,1)S(1)}, u32[]{:S(2)}, u32[]{:S(2)}) %collective-permute-start.2) | collective-permute-done | bytes 655392 | tf_op jit(solution)/shard_map/ppermute | solution.py:52
  56.3 0.8 collective-permute-start.3
  57.1 2.1 %weight.5 = (bf16[256,8192]{1,0:T(8,128)(2,1)}, bf16[256,1024]{1,0:T(8,128)(2,1)S(1)}) custom-call(bf16[512,1024]{1,0:T(8,128)(2,1)S(1)} %convert_element_type.4.refs_0_, bf16[512,1024]{1,0:T(8,128)(2,1)S(1)} %collective-permute-done.5.refs_1_, bf16[256,1024]{1,0:T(8,128)(2,1)S(1)} %copy-done, bf16[256,1024]{1,0:T(8,128)(2,1)S(1)} %slice.30.refs_3_.refs_10_), custom_call_target="tpu_custom_call" | custom-call | flops 1073741824 | bytes 6291456 | tf_op jit(solution)/shard_map/weight/pallas_call | solution.py:318
  59.3 8.5 %collective-permute-done.8.refs_3_ = bf16[256,2048]{1,0:T(8,128)(2,1)S(1)} collective-permute-done((bf16[256,2048]{1,0:T(8,128)(2,1)S(1)}, bf16[256,2048]{1,0:T(8,128)(2,1)S(1)}, u32[]{:S(2)}, u32[]{:S(2)}) %collective-permute-start.8) | collective-permute-done | bytes 1048608 | tf_op jit(solution)/shard_map/ppermute | solution.py:49
  67.8 4.3 %project.1 = (f32[8,32,1024]{2,1,0:T(8,128)S(1)}, bf16[8,32,1024]{2,1,0:T(8,128)(2,1)S(1)}) custom-call(bf16[256,2048]{1,0:T(8,128)(2,1)S(1)} %get-tuple-element.60.refs_0_, bf16[256,2048]{1,0:T(8,128)(2,1)S(1)} %collective-permute-done.7.refs_1_, bf16[256,3072]{1,0:T(8,128)(2,1)S(1)} %collective-permute-done.6.refs_2_, ...), custom_call_target="tpu_custom_call" | custom-call | flops 3221225472 | bytes 12582912 | tf_op jit(solution)/shard_map/project/pallas_call | solution.py:318
  72.6 6.9 %collective-permute-done.3.refs_0_ = bf16[512,1024]{1,0:T(8,128)(2,1)S(1)} collective-permute-done((bf16[512,1024]{1,0:T(8,128)(2,1)S(1)}, bf16[512,1024]{1,0:T(8,128)(2,1)S(1)}, u32[]{:S(2)}, u32[]{:S(2)}) %collective-permute-start.3) | collective-permute-done | bytes 1048608 | tf_op jit(solution)/shard_map/ppermute | solution.py:52
  79.6 0.8 collective-permute-start.4
  80.5 1.0 collective-permute-start.11
  81.5 7.7 %collective-permute-done.11.refs_1_ = bf16[4,32,1024]{2,1,0:T(8,128)(2,1)S(1)} collective-permute-done((bf16[4,32,1024]{2,1,0:T(8,128)(2,1)S(1)}, bf16[4,32,1024]{2,1,0:T(8,128)(2,1)S(1)}, u32[]{:S(2)}, u32[]{:S(2)}) %collective-permute-start.11) | collective-permute-done | bytes 262176 | tf_op jit(solution)/shard_map/ppermute | solution.py:49
  89.3 1.0 collective-permute-start.12
  90.3 11.1 %collective-permute-done.4.refs_0_ = bf16[512,1024]{1,0:T(8,128)(2,1)S(1)} collective-permute-done((bf16[512,1024]{1,0:T(8,128)(2,1)S(1)}, bf16[512,1024]{1,0:T(8,128)(2,1)S(1)}, u32[]{:S(2)}, u32[]{:S(2)}) %collective-permute-start.4) | collective-permute-done | bytes 1048608 | tf_op jit(solution)/shard_map/ppermute | solution.py:52
  101.5 1.4 collective-permute-done.12.refs_4_
  102.9 2.8 %collective-permute-start.15 = (bf16[1,32,1024]{2,1,0:T(8,128)(2,1)S(1)}, bf16[1,32,1024]{2,1,0:T(8,128)(2,1)S(1)}, u32[]{:S(2)}, u32[]{:S(2)}) collective-permute-start(bf16[1,32,1024]{2,1,0:T(8,128)(2,1)S(1)} %get-tuple-element.75), channel_id=1, source_target_pairs={{0,12},{1,13},{2,14},{3,15},{4,8},{5,9},{6,10},{7,11},{8,4},{9,5},... | collective-permute-start | bytes 196616 | tf_op jit(solution)/shard_map/ppermute | solution.py:49
  105.7 2.0 %collective-permute-start.14 = (bf16[1,32,1024]{2,1,0:T(8,128)(2,1)S(1)}, bf16[1,32,1024]{2,1,0:T(8,128)(2,1)S(1)}, u32[]{:S(2)}, u32[]{:S(2)}) collective-permute-start(bf16[1,32,1024]{2,1,0:T(8,128)(2,1)S(1)} %get-tuple-element.73), channel_id=1, source_target_pairs={{0,8},{1,9},{2,10},{3,11},{4,12},{5,13},{6,14},{7,15},{8,0},{9,1},... | collective-permute-start | bytes 196616 | tf_op jit(solution)/shard_map/ppermute | solution.py:49
  107.8 2.1 %weight.6 = (bf16[256,8192]{1,0:T(8,128)(2,1)}, bf16[256,1024]{1,0:T(8,128)(2,1)S(1)}) custom-call(bf16[512,1024]{1,0:T(8,128)(2,1)S(1)} %collective-permute-done.3.refs_0_, bf16[512,1024]{1,0:T(8,128)(2,1)S(1)} %collective-permute-done.18.refs_1_, bf16[256,1024]{1,0:T(8,128)(2,1)S(1)} %copy-done.1, ...), custom_call_target="tpu_custom_call", output_to_operand_aliasing={{0}: (4, {})} | custom-call | flops 1073741824 | bytes 6291456 | tf_op jit(solution)/shard_map/weight/pallas_call | solution.py:318
  109.9 1.0 collective-permute-start.22
  111.0 1.3 collective-permute-done.14.refs_2_
  113.3 2.1 %weight.7 = (bf16[256,8192]{1,0:T(8,128)(2,1)}, bf16[256,1024]{1,0:T(8,128)(2,1)S(1)}) custom-call(bf16[512,1024]{1,0:T(8,128)(2,1)S(1)} %collective-permute-done.4.refs_0_, bf16[512,1024]{1,0:T(8,128)(2,1)S(1)} %collective-permute-done.17.refs_1_, bf16[256,1024]{1,0:T(8,128)(2,1)S(1)} %copy-done.1, ...), custom_call_target="tpu_custom_call", output_to_operand_aliasing={{0}: (5, {})} | custom-call | flops 1073741824 | bytes 6291456 | tf_op jit(solution)/shard_map/weight/pallas_call | solution.py:318
  115.5 6.6 %collective-permute-done.22.refs_4_ = bf16[256,1024]{1,0:T(8,128)(2,1)S(1)} collective-permute-done((bf16[256,1024]{1,0:T(8,128)(2,1)S(1)}, bf16[256,1024]{1,0:T(8,128)(2,1)S(1)}, u32[]{:S(2)}, u32[]{:S(2)}) %collective-permute-start.22) | collective-permute-done | bytes 524320 | tf_op jit(solution)/shard_map/ppermute | solution.py:49
  122.1 1.1 collective-permute-start.23
  123.2 2.9 %collective-permute-done.16.refs_0_ = bf16[256,1024]{1,0:T(8,128)(2,1)S(1)} collective-permute-done((bf16[256,1024]{1,0:T(8,128)(2,1)S(1)}, bf16[256,1024]{1,0:T(8,128)(2,1)S(1)}, u32[]{:S(2)}, u32[]{:S(2)}) %collective-permute-start.16) | collective-permute-done | bytes 524320 | tf_op jit(solution)/shard_map/ppermute | solution.py:52
  126.1 1.6 collective-permute-start.20
  127.7 2.8 %collective-permute-start.21 = (bf16[1,48,1024]{2,1,0:T(8,128)(2,1)S(1)}, bf16[1,48,1024]{2,1,0:T(8,128)(2,1)S(1)}, u32[]{:S(2)}, u32[]{:S(2)}) collective-permute-start(bf16[1,48,1024]{2,1,0:T(8,128)(2,1)S(1)} %get-tuple-element.84), channel_id=1, source_target_pairs={{0,12},{1,13},{2,14},{3,15},{4,8},{5,9},{6,10},{7,11},{8,4},{9,5},... | collective-permute-start | bytes 294920 | tf_op jit(solution)/shard_map/ppermute | solution.py:49
  130.5 2.0 %collective-permute-done.19 = bf16[1,48,1024]{2,1,0:T(8,128)(2,1)S(1)} collective-permute-done((bf16[1,48,1024]{2,1,0:T(8,128)(2,1)S(1)}, bf16[1,48,1024]{2,1,0:T(8,128)(2,1)S(1)}, u32[]{:S(2)}, u32[]{:S(2)}) %collective-permute-start.19) | collective-permute-done | bytes 98336 | tf_op jit(solution)/shard_map/ppermute | solution.py:49
  132.5 4.3 %collective-permute-done.20 = bf16[1,48,1024]{2,1,0:T(8,128)(2,1)S(1)} collective-permute-done((bf16[1,48,1024]{2,1,0:T(8,128)(2,1)S(1)}, bf16[1,48,1024]{2,1,0:T(8,128)(2,1)S(1)}, u32[]{:S(2)}, u32[]{:S(2)}) %collective-permute-start.20) | collective-permute-done | bytes 98336 | tf_op jit(solution)/shard_map/ppermute | solution.py:49
  136.9 2.3 %collective-permute-start.30 = (bf16[256,1024]{1,0:T(8,128)(2,1)S(1)}, bf16[256,1024]{1,0:T(8,128)(2,1)S(1)}, u32[]{:S(2)}, u32[]{:S(2)}) collective-permute-start(bf16[256,1024]{1,0:T(8,128)(2,1)S(1)} %get-tuple-element.94), channel_id=1, source_target_pairs={{0,4},{1,5},{2,6},{3,7},{4,12},{5,13},{6,14},{7,15},{12,8},{13,9},... | collective-permute-start | bytes 1572872 | tf_op jit(solution)/shard_map/ppermute | solution.py:52
  139.4 2.0 %collective-permute-start.26 = (f32[8,128]{1,0:T(8,128)S(1)}, f32[8,128]{1,0:T(8,128)S(1)}, u32[]{:S(2)}, u32[]{:S(2)}) collective-permute-start(f32[8,128]{1,0:T(8,128)S(1)} %gathered.1.refs_0_), channel_id=1, source_target_pairs={{0,2},{1,3},{2,0},{3,1},{4,6},{5,7},{6,4},{7,5},{8,10},{9,11},{10,... | collective-permute-start | bytes 12296 | tf_op jit(solution)/shard_map/ppermute | solution.py:49
  141.5 1.5 weight.8
  143.1 1.4 collective-permute-done.27.refs_3_
  145.0 5.9 %collective-permute-done.30.refs_0_ = bf16[256,1024]{1,0:T(8,128)(2,1)S(1)} collective-permute-done((bf16[256,1024]{1,0:T(8,128)(2,1)S(1)}, bf16[256,1024]{1,0:T(8,128)(2,1)S(1)}, u32[]{:S(2)}, u32[]{:S(2)}) %collective-permute-start.30) | collective-permute-done | bytes 524320 | tf_op jit(solution)/shard_map/ppermute | solution.py:52
  151.0 2.2 %collective-permute-done.28.refs_0_ = bf16[256,512]{1,0:T(8,128)(2,1)S(1)} collective-permute-done((bf16[256,512]{1,0:T(8,128)(2,1)S(1)}, bf16[256,512]{1,0:T(8,128)(2,1)S(1)}, u32[]{:S(2)}, u32[]{:S(2)}) %collective-permute-start.28) | collective-permute-done | bytes 262176 | tf_op jit(solution)/shard_map/ppermute | solution.py:49
  153.1 1.1 moment.1
  155.0 1.5 weight.9
  156.5 6.4 %collective-permute-done.29 = bf16[4,32,1024]{2,1,0:T(8,128)(2,1)S(1)} collective-permute-done((bf16[4,32,1024]{2,1,0:T(8,128)(2,1)S(1)}, bf16[4,32,1024]{2,1,0:T(8,128)(2,1)S(1)}, u32[]{:S(2)}, u32[]{:S(2)}) %collective-permute-start.29) | collective-permute-done | bytes 262176 | tf_op jit(solution)/shard_map/ppermute | solution.py:49
  163.4 1.5 collective-permute-done.32.other
  164.9 2.2 %back.1 = f32[512,1024]{1,0:T(8,128)} custom-call(bf16[512,512]{1,0:T(8,128)(2,1)S(1)} %copy-done.4, bf16[8,32,1024]{2,1,0:T(8,128)(2,1)S(1)} %constant_dynamic-update-slice_fusion.4.near, bf16[8,32,1024]{2,1,0:T(8,128)(2,1)S(1)} %collective-permute-done.32.other, f32[512,1024]{1,0:T(8,128)S(1)} %copy-done.2), custom_call_target="tpu_custom_call" | custom-call | flops 536870912 | bytes 8388608 | tf_op jit(solution)/shard_map/back/pallas_call | solution.py:318
  167.1 4.6 %collective-permute-done.33.refs_1_ = bf16[256,512]{1,0:T(8,128)(2,1)S(1)} collective-permute-done((bf16[256,512]{1,0:T(8,128)(2,1)S(1)}, bf16[256,512]{1,0:T(8,128)(2,1)S(1)}, u32[]{:S(2)}, u32[]{:S(2)}) %collective-permute-start.33) | collective-permute-done | bytes 262176 | tf_op jit(solution)/shard_map/ppermute | solution.py:49
  171.8 0.8 last.1
  (63 shorter events, 5.1 us)
Async XLA Ops:
  0.6 1.0 copy-start
  1.7 2.2 %copy-start.3 = (bf16[256,8192]{1,0:T(8,128)(2,1)S(1)}, bf16[256,8192]{1,0:T(8,128)(2,1)}, u32[]{:S(2)}) copy-start(bf16[256,8192]{1,0:T(8,128)(2,1)} %act.1) | copy-start | bytes 12582916
  3.9 3.7 %copy-start.6 = (f32[32,1024]{1,0:T(8,128)S(1)}, f32[32,1024]{1,0:T(8,128)}, u32[]{:S(2)}) copy-start(f32[32,1024]{1,0:T(8,128)} %refs_9_.1) | copy-start | bytes 393220
  3.9 3.7 %copy-start.5 = (f32[32,1024]{1,0:T(8,128)S(1)}, f32[32,1024]{1,0:T(8,128)}, u32[]{:S(2)}) copy-start(f32[32,1024]{1,0:T(8,128)} %refs_10_.1) | copy-start | bytes 393220
  3.9 3.8 %copy-start.4 = (bf16[512,512]{1,0:T(8,128)(2,1)S(1)}, bf16[512,512]{1,0:T(8,128)(2,1)}, u32[]{:S(2)}) copy-start(bf16[512,512]{1,0:T(8,128)(2,1)} %basis.1) | copy-start | bytes 1572868
  3.9 21.7 %copy-start.2 = (f32[512,1024]{1,0:T(8,128)S(1)}, f32[512,1024]{1,0:T(8,128)}, u32[]{:S(2)}) copy-start(f32[512,1024]{1,0:T(8,128)} %master.1) | copy-start | bytes 6291460
  4.5 37.4 %collective-permute-start.6 = (bf16[256,3072]{1,0:T(8,128)(2,1)S(1)}, bf16[256,3072]{1,0:T(8,128)(2,1)S(1)}, u32[]{:S(2)}, u32[]{:S(2)}) collective-permute-start(bf16[256,3072]{1,0:T(8,128)(2,1)S(1)} %get-tuple-element.58), channel_id=1, source_target_pairs={{0,2},{1,3},{2,0},{3,1},{4,6},{5,7},{6,4},{7,5},{8,10},{9,11},{10,... | collective-permute-start | bytes 4718600 | tf_op jit(solution)/shard_map/ppermute | solution.py:49
  7.7 17.1 %collective-permute-start = (bf16[640,512]{1,0:T(8,128)(2,1)S(1)}, bf16[640,512]{1,0:T(8,128)(2,1)S(1)}, u32[]{:S(2)}, u32[]{:S(2)}) collective-permute-start(bf16[640,512]{1,0:T(8,128)(2,1)S(1)} %fusion.refs_4_), channel_id=1, source_target_pairs={{0,4},{1,5},{2,6},{3,7},{4,12},{5,13},{6,14},{7,15},{12,8},{13,9},... | collective-permute-start | bytes 1966088 | tf_op jit(solution)/shard_map/ppermute | solution.py:52
  24.8 16.2 %collective-permute-start.1 = (bf16[640,512]{1,0:T(8,128)(2,1)S(1)}, bf16[640,512]{1,0:T(8,128)(2,1)S(1)}, u32[]{:S(2)}, u32[]{:S(2)}) collective-permute-start(bf16[640,512]{1,0:T(8,128)(2,1)S(1)} %collective-permute-done.refs_5_), channel_id=1, source_target_pairs={{0,4},{1,5},{2,6},{3,7},{4,12},{5,13},{6,14},{7,15},{12,8},{13,9},... | collective-permute-start | bytes 1966088 | tf_op jit(solution)/shard_map/ppermute | solution.py:52
  25.8 31.3 %collective-permute-start.5 = (bf16[512,1024]{1,0:T(8,128)(2,1)S(1)}, bf16[512,1024]{1,0:T(8,128)(2,1)S(1)}, u32[]{:S(2)}, u32[]{:S(2)}) collective-permute-start(bf16[512,1024]{1,0:T(8,128)(2,1)S(1)} %convert_element_type.4.refs_0_), channel_id=1, source_target_pairs={{0,1},{1,0},{2,3},{3,2},{4,5},{5,4},{6,7},{7,6},{8,9},{9,8},{10,11... | collective-permute-start | bytes 3145736 | tf_op jit(solution)/shard_map/ppermute | solution.py:49
  41.0 15.3 %collective-permute-start.2 = (bf16[640,512]{1,0:T(8,128)(2,1)S(1)}, bf16[640,512]{1,0:T(8,128)(2,1)S(1)}, u32[]{:S(2)}, u32[]{:S(2)}) collective-permute-start(bf16[640,512]{1,0:T(8,128)(2,1)S(1)} %collective-permute-done.1.refs_6_), channel_id=1, source_target_pairs={{0,4},{1,5},{2,6},{3,7},{4,12},{5,13},{6,14},{7,15},{12,8},{13,9},... | collective-permute-start | bytes 1966088 | tf_op jit(solution)/shard_map/ppermute | solution.py:52
  42.1 17.1 %collective-permute-start.9 = (bf16[512,1024]{1,0:T(8,128)(2,1)S(1)}, bf16[512,1024]{1,0:T(8,128)(2,1)S(1)}, u32[]{:S(2)}, u32[]{:S(2)}) collective-permute-start(bf16[512,1024]{1,0:T(8,128)(2,1)S(1)} %pad_maximum_fusion), channel_id=1, source_target_pairs={{0,1},{1,0},{2,3},{3,2},{4,5},{5,4},{6,7},{7,6},{8,9},{9,8},{10,11... | collective-permute-start | bytes 3145736 | tf_op jit(solution)/shard_map/ppermute | solution.py:49
  42.2 17.1 %collective-permute-start.7 = (bf16[256,2048]{1,0:T(8,128)(2,1)S(1)}, bf16[256,2048]{1,0:T(8,128)(2,1)S(1)}, u32[]{:S(2)}, u32[]{:S(2)}) collective-permute-start(bf16[256,2048]{1,0:T(8,128)(2,1)S(1)} %get-tuple-element.61), channel_id=1, source_target_pairs={{0,1},{1,0},{2,3},{3,2},{4,5},{5,4},{6,7},{7,6},{8,9},{9,8},{10,11... | collective-permute-start | bytes 3145736 | tf_op jit(solution)/shard_map/ppermute | solution.py:49
  42.7 25.2 %copy-start.1 = (bf16[256,1024]{1,0:T(8,128)(2,1)S(1)}, bf16[256,1024]{1,0:T(8,128)(2,1)}, u32[]{:S(2)}) copy-start(bf16[256,1024]{1,0:T(8,128)(2,1)} %refs_2_.9) | copy-start | bytes 1572868
  42.7 25.2 %collective-permute-start.8 = (bf16[256,2048]{1,0:T(8,128)(2,1)S(1)}, bf16[256,2048]{1,0:T(8,128)(2,1)S(1)}, u32[]{:S(2)}, u32[]{:S(2)}) collective-permute-start(bf16[256,2048]{1,0:T(8,128)(2,1)S(1)} %get-tuple-element.62), channel_id=1, source_target_pairs={{0,3},{1,2},{2,1},{3,0},{4,7},{5,6},{6,5},{7,4},{8,11},{9,10},{10,... | collective-permute-start | bytes 3145736 | tf_op jit(solution)/shard_map/ppermute | solution.py:49
  56.3 23.3 %collective-permute-start.3 = (bf16[512,1024]{1,0:T(8,128)(2,1)S(1)}, bf16[512,1024]{1,0:T(8,128)(2,1)S(1)}, u32[]{:S(2)}, u32[]{:S(2)}) collective-permute-start(bf16[512,1024]{1,0:T(8,128)(2,1)S(1)} %convert_element_type.4.refs_0_), channel_id=1, source_target_pairs={{0,4},{1,5},{2,6},{3,7},{4,12},{5,13},{6,14},{7,15},{12,8},{13,9},... | collective-permute-start | bytes 3145736 | tf_op jit(solution)/shard_map/ppermute | solution.py:52
  72.2 8.2 %collective-permute-start.10 = (bf16[8,32,1024]{2,1,0:T(8,128)(2,1)S(1)}, bf16[8,32,1024]{2,1,0:T(8,128)(2,1)S(1)}, u32[]{:S(2)}, u32[]{:S(2)}) collective-permute-start(bf16[8,32,1024]{2,1,0:T(8,128)(2,1)S(1)} %get-tuple-element.64), channel_id=1, source_target_pairs={{0,1},{1,0},{2,3},{3,2},{4,5},{5,4},{6,7},{7,6},{8,9},{9,8},{10,11... | collective-permute-start | bytes 1572872 | tf_op jit(solution)/shard_map/ppermute | solution.py:49
  79.6 21.9 %collective-permute-start.4 = (bf16[512,1024]{1,0:T(8,128)(2,1)S(1)}, bf16[512,1024]{1,0:T(8,128)(2,1)S(1)}, u32[]{:S(2)}, u32[]{:S(2)}) collective-permute-start(bf16[512,1024]{1,0:T(8,128)(2,1)S(1)} %collective-permute-done.3.refs_0_), channel_id=1, source_target_pairs={{0,4},{1,5},{2,6},{3,7},{4,12},{5,13},{6,14},{7,15},{12,8},{13,9},... | collective-permute-start | bytes 3145736 | tf_op jit(solution)/shard_map/ppermute | solution.py:52
  80.4 27.4 %collective-permute-start.18 = (bf16[512,1024]{1,0:T(8,128)(2,1)S(1)}, bf16[512,1024]{1,0:T(8,128)(2,1)S(1)}, u32[]{:S(2)}, u32[]{:S(2)}) collective-permute-start(bf16[512,1024]{1,0:T(8,128)(2,1)S(1)} %collective-permute-done.3.refs_0_), channel_id=1, source_target_pairs={{0,1},{1,0},{2,3},{3,2},{4,5},{5,4},{6,7},{7,6},{8,9},{9,8},{10,11... | collective-permute-start | bytes 3145736 | tf_op jit(solution)/shard_map/ppermute | solution.py:49
  80.5 8.8 %collective-permute-start.11 = (bf16[4,32,1024]{2,1,0:T(8,128)(2,1)S(1)}, bf16[4,32,1024]{2,1,0:T(8,128)(2,1)S(1)}, u32[]{:S(2)}, u32[]{:S(2)}) collective-permute-start(bf16[4,32,1024]{2,1,0:T(8,128)(2,1)S(1)} %get-tuple-element.66), channel_id=1, source_target_pairs={{0,2},{1,3},{2,0},{3,1},{4,6},{5,7},{6,4},{7,5},{8,10},{9,11},{10,... | collective-permute-start | bytes 786440 | tf_op jit(solution)/shard_map/ppermute | solution.py:49
  89.3 13.6 %collective-permute-start.12 = (bf16[256,1024]{1,0:T(8,128)(2,1)S(1)}, bf16[256,1024]{1,0:T(8,128)(2,1)S(1)}, u32[]{:S(2)}, u32[]{:S(2)}) collective-permute-start(bf16[256,1024]{1,0:T(8,128)(2,1)S(1)} %get-tuple-element.70), channel_id=1, source_target_pairs={{0,2},{1,3},{2,0},{3,1},{4,6},{5,7},{6,4},{7,5},{8,10},{9,11},{10,... | collective-permute-start | bytes 1572872 | tf_op jit(solution)/shard_map/ppermute | solution.py:49
  101.5 11.8 %collective-permute-start.17 = (bf16[512,1024]{1,0:T(8,128)(2,1)S(1)}, bf16[512,1024]{1,0:T(8,128)(2,1)S(1)}, u32[]{:S(2)}, u32[]{:S(2)}) collective-permute-start(bf16[512,1024]{1,0:T(8,128)(2,1)S(1)} %collective-permute-done.4.refs_0_), channel_id=1, source_target_pairs={{0,1},{1,0},{2,3},{3,2},{4,5},{5,4},{6,7},{7,6},{8,9},{9,8},{10,11... | collective-permute-start | bytes 3145736 | tf_op jit(solution)/shard_map/ppermute | solution.py:49
  102.9 8.1 %collective-permute-start.15 = (bf16[1,32,1024]{2,1,0:T(8,128)(2,1)S(1)}, bf16[1,32,1024]{2,1,0:T(8,128)(2,1)S(1)}, u32[]{:S(2)}, u32[]{:S(2)}) collective-permute-start(bf16[1,32,1024]{2,1,0:T(8,128)(2,1)S(1)} %get-tuple-element.75), channel_id=1, source_target_pairs={{0,12},{1,13},{2,14},{3,15},{4,8},{5,9},{6,10},{7,11},{8,4},{9,5},... | collective-permute-start | bytes 196616 | tf_op jit(solution)/shard_map/ppermute | solution.py:49
  105.7 6.6 %collective-permute-start.14 = (bf16[1,32,1024]{2,1,0:T(8,128)(2,1)S(1)}, bf16[1,32,1024]{2,1,0:T(8,128)(2,1)S(1)}, u32[]{:S(2)}, u32[]{:S(2)}) collective-permute-start(bf16[1,32,1024]{2,1,0:T(8,128)(2,1)S(1)} %get-tuple-element.73), channel_id=1, source_target_pairs={{0,8},{1,9},{2,10},{3,11},{4,12},{5,13},{6,14},{7,15},{8,0},{9,1},... | collective-permute-start | bytes 196616 | tf_op jit(solution)/shard_map/ppermute | solution.py:49
  107.8 5.0 %collective-permute-start.13 = (bf16[1,32,1024]{2,1,0:T(8,128)(2,1)S(1)}, bf16[1,32,1024]{2,1,0:T(8,128)(2,1)S(1)}, u32[]{:S(2)}, u32[]{:S(2)}) collective-permute-start(bf16[1,32,1024]{2,1,0:T(8,128)(2,1)S(1)} %get-tuple-element.71), channel_id=1, source_target_pairs={{0,4},{1,5},{2,6},{3,7},{4,0},{5,1},{6,2},{7,3},{8,12},{9,13},{10,... | collective-permute-start | bytes 196616 | tf_op jit(solution)/shard_map/ppermute | solution.py:49
  109.9 12.2 %collective-permute-start.22 = (bf16[256,1024]{1,0:T(8,128)(2,1)S(1)}, bf16[256,1024]{1,0:T(8,128)(2,1)S(1)}, u32[]{:S(2)}, u32[]{:S(2)}) collective-permute-start(bf16[256,1024]{1,0:T(8,128)(2,1)S(1)} %get-tuple-element.86), channel_id=1, source_target_pairs={{0,2},{1,3},{2,0},{3,1},{4,6},{5,7},{6,4},{7,5},{8,10},{9,11},{10,... | collective-permute-start | bytes 1572872 | tf_op jit(solution)/shard_map/ppermute | solution.py:49
  112.8 13.3 %collective-permute-start.16 = (bf16[256,1024]{1,0:T(8,128)(2,1)S(1)}, bf16[256,1024]{1,0:T(8,128)(2,1)S(1)}, u32[]{:S(2)}, u32[]{:S(2)}) collective-permute-start(bf16[256,1024]{1,0:T(8,128)(2,1)S(1)} %get-tuple-element.76), channel_id=1, source_target_pairs={{0,4},{1,5},{2,6},{3,7},{4,12},{5,13},{6,14},{7,15},{12,8},{13,9},... | collective-permute-start | bytes 1572872 | tf_op jit(solution)/shard_map/ppermute | solution.py:52
  122.1 17.3 %collective-permute-start.23 = (bf16[256,1024]{1,0:T(8,128)(2,1)S(1)}, bf16[256,1024]{1,0:T(8,128)(2,1)S(1)}, u32[]{:S(2)}, u32[]{:S(2)}) collective-permute-start(bf16[256,1024]{1,0:T(8,128)(2,1)S(1)} %get-tuple-element.87), channel_id=1, source_target_pairs={{0,2},{1,3},{2,0},{3,1},{4,6},{5,7},{6,4},{7,5},{8,10},{9,11},{10,... | collective-permute-start | bytes 1572872 | tf_op jit(solution)/shard_map/ppermute | solution.py:49
  126.1 15.4 %collective-permute-start.24 = (bf16[256,1024]{1,0:T(8,128)(2,1)S(1)}, bf16[256,1024]{1,0:T(8,128)(2,1)S(1)}, u32[]{:S(2)}, u32[]{:S(2)}) collective-permute-start(bf16[256,1024]{1,0:T(8,128)(2,1)S(1)} %collective-permute-done.16.refs_0_), channel_id=1, source_target_pairs={{0,1},{1,0},{2,3},{3,2},{4,5},{5,4},{6,7},{7,6},{8,9},{9,8},{10,11... | collective-permute-start | bytes 1572872 | tf_op jit(solution)/shard_map/ppermute | solution.py:49
  126.1 6.4 %collective-permute-start.19 = (bf16[1,48,1024]{2,1,0:T(8,128)(2,1)S(1)}, bf16[1,48,1024]{2,1,0:T(8,128)(2,1)S(1)}, u32[]{:S(2)}, u32[]{:S(2)}) collective-permute-start(bf16[1,48,1024]{2,1,0:T(8,128)(2,1)S(1)} %get-tuple-element.84), channel_id=1, source_target_pairs={{0,4},{1,5},{2,6},{3,7},{4,0},{5,1},{6,2},{7,3},{8,12},{9,13},{10,... | collective-permute-start | bytes 294920 | tf_op jit(solution)/shard_map/ppermute | solution.py:49
  126.1 10.8 %collective-permute-start.20 = (bf16[1,48,1024]{2,1,0:T(8,128)(2,1)S(1)}, bf16[1,48,1024]{2,1,0:T(8,128)(2,1)S(1)}, u32[]{:S(2)}, u32[]{:S(2)}) collective-permute-start(bf16[1,48,1024]{2,1,0:T(8,128)(2,1)S(1)} %get-tuple-element.84), channel_id=1, source_target_pairs={{0,8},{1,9},{2,10},{3,11},{4,12},{5,13},{6,14},{7,15},{8,0},{9,1},... | collective-permute-start | bytes 294920 | tf_op jit(solution)/shard_map/ppermute | solution.py:49
  127.7 9.2 %collective-permute-start.21 = (bf16[1,48,1024]{2,1,0:T(8,128)(2,1)S(1)}, bf16[1,48,1024]{2,1,0:T(8,128)(2,1)S(1)}, u32[]{:S(2)}, u32[]{:S(2)}) collective-permute-start(bf16[1,48,1024]{2,1,0:T(8,128)(2,1)S(1)} %get-tuple-element.84), channel_id=1, source_target_pairs={{0,12},{1,13},{2,14},{3,15},{4,8},{5,9},{6,10},{7,11},{8,4},{9,5},... | collective-permute-start | bytes 294920 | tf_op jit(solution)/shard_map/ppermute | solution.py:49
  136.9 14.1 %collective-permute-start.30 = (bf16[256,1024]{1,0:T(8,128)(2,1)S(1)}, bf16[256,1024]{1,0:T(8,128)(2,1)S(1)}, u32[]{:S(2)}, u32[]{:S(2)}) collective-permute-start(bf16[256,1024]{1,0:T(8,128)(2,1)S(1)} %get-tuple-element.94), channel_id=1, source_target_pairs={{0,4},{1,5},{2,6},{3,7},{4,12},{5,13},{6,14},{7,15},{12,8},{13,9},... | collective-permute-start | bytes 1572872 | tf_op jit(solution)/shard_map/ppermute | solution.py:52
  139.3 3.7 %collective-permute-start.25 = (f32[8,128]{1,0:T(8,128)S(1)}, f32[8,128]{1,0:T(8,128)S(1)}, u32[]{:S(2)}, u32[]{:S(2)}) collective-permute-start(f32[8,128]{1,0:T(8,128)S(1)} %gathered.1.refs_0_), channel_id=1, source_target_pairs={{0,1},{1,0},{2,3},{3,2},{4,5},{5,4},{6,7},{7,6},{8,9},{9,8},{10,11... | collective-permute-start | bytes 12296 | tf_op jit(solution)/shard_map/ppermute | solution.py:49
  139.4 3.7 %collective-permute-start.26 = (f32[8,128]{1,0:T(8,128)S(1)}, f32[8,128]{1,0:T(8,128)S(1)}, u32[]{:S(2)}, u32[]{:S(2)}) collective-permute-start(f32[8,128]{1,0:T(8,128)S(1)} %gathered.1.refs_0_), channel_id=1, source_target_pairs={{0,2},{1,3},{2,0},{3,1},{4,6},{5,7},{6,4},{7,5},{8,10},{9,11},{10,... | collective-permute-start | bytes 12296 | tf_op jit(solution)/shard_map/ppermute | solution.py:49
  141.4 3.0 %collective-permute-start.27 = (f32[8,128]{1,0:T(8,128)S(1)}, f32[8,128]{1,0:T(8,128)S(1)}, u32[]{:S(2)}, u32[]{:S(2)}) collective-permute-start(f32[8,128]{1,0:T(8,128)S(1)} %gathered.1.refs_0_), channel_id=1, source_target_pairs={{0,3},{1,2},{2,1},{3,0},{4,7},{5,6},{6,5},{7,4},{8,11},{9,10},{10,... | collective-permute-start | bytes 12296 | tf_op jit(solution)/shard_map/ppermute | solution.py:49
  144.4 8.7 %collective-permute-start.28 = (bf16[256,512]{1,0:T(8,128)(2,1)S(1)}, bf16[256,512]{1,0:T(8,128)(2,1)S(1)}, u32[]{:S(2)}, u32[]{:S(2)}) collective-permute-start(bf16[256,512]{1,0:T(8,128)(2,1)S(1)} %get-tuple-element.92), channel_id=1, source_target_pairs={{0,2},{1,3},{2,0},{3,1},{4,6},{5,7},{6,4},{7,5},{8,10},{9,11},{10,... | collective-permute-start | bytes 786440 | tf_op jit(solution)/shard_map/ppermute | solution.py:49
  153.1 1.9 %collective-permute-start.31 = (bf16[256,1024]{1,0:T(8,128)(2,1)S(1)}, bf16[256,1024]{1,0:T(8,128)(2,1)S(1)}, u32[]{:S(2)}, u32[]{:S(2)}) collective-permute-start(bf16[256,1024]{1,0:T(8,128)(2,1)S(1)} %collective-permute-done.30.refs_0_), channel_id=1, source_target_pairs={{0,1},{1,0},{2,3},{3,2},{4,5},{5,4},{6,7},{7,6},{8,9},{9,8},{10,11... | collective-permute-start | bytes 1572872 | tf_op jit(solution)/shard_map/ppermute | solution.py:49
  154.2 8.7 %collective-permute-start.29 = (bf16[4,32,1024]{2,1,0:T(8,128)(2,1)S(1)}, bf16[4,32,1024]{2,1,0:T(8,128)(2,1)S(1)}, u32[]{:S(2)}, u32[]{:S(2)}) collective-permute-start(bf16[4,32,1024]{2,1,0:T(8,128)(2,1)S(1)} %get-tuple-element.93), channel_id=1, source_target_pairs={{0,2},{1,3},{2,0},{3,1},{4,6},{5,7},{6,4},{7,5},{8,10},{9,11},{10,... | collective-permute-start | bytes 786440 | tf_op jit(solution)/shard_map/ppermute | solution.py:49
  163.0 2.0 %collective-permute-start.32 = (bf16[8,32,1024]{2,1,0:T(8,128)(2,1)S(1)}, bf16[8,32,1024]{2,1,0:T(8,128)(2,1)S(1)}, u32[]{:S(2)}, u32[]{:S(2)}) collective-permute-start(bf16[8,32,1024]{2,1,0:T(8,128)(2,1)S(1)} %constant_dynamic-update-slice_fusion.4.near), channel_id=1, source_target_pairs={{0,1},{1,0},{2,3},{3,2},{4,5},{5,4},{6,7},{7,6},{8,9},{9,8},{10,11... | collective-permute-start | bytes 1572872 | tf_op jit(solution)/shard_map/ppermute | solution.py:49
  163.1 8.7 %collective-permute-start.33 = (bf16[256,512]{1,0:T(8,128)(2,1)S(1)}, bf16[256,512]{1,0:T(8,128)(2,1)S(1)}, u32[]{:S(2)}, u32[]{:S(2)}) collective-permute-start(bf16[256,512]{1,0:T(8,128)(2,1)S(1)} %get-tuple-element.97), channel_id=1, source_target_pairs={{0,2},{1,3},{2,0},{3,1},{4,6},{5,7},{6,4},{7,5},{8,10},{9,11},{10,... | collective-permute-start | bytes 786440 | tf_op jit(solution)/shard_map/ppermute | solution.py:49

commit v13 on v11

--- a/solution.py
+++ b/solution.py
@@ -429,12 +429,13 @@
             moved=12 * 2**20,
         )
         weight[1] = after(weight[1], total)
-        weight.append(onward(weight[1]))
+        halves = [weight[1][p * height : (p + 1) * height] for p in range(parts)]
+        second = [onward(halves[0])]
         theirs.append(swap(weight[1], 1))
 
         for k, (bit, radix) in enumerate(rounds):
             if bit == members:
-                gives = [after(give, weight[2], block, sent if sides == 2 else block) for give in gives]
+                gives = [after(give, second[0]) for give in gives]
             came = [swap(give, j * bit) for j, give in zip(range(1, radix), gives)]
             if k == len(rounds) - 1:
                 break
@@ -452,42 +453,40 @@
             if bit == 2:
                 sent = give_back(0, first_block, gate=total)
                 later = give_back(1, block, gate=total)
-                weight[2] = after(weight[2], total, sent)
-
         owned_rows, message = call(
             functools.partial(square_kernel, len(came), lines),
             "square",
             [((owned, outs), f32), ((1, lines + 16, outs), bf16)],
             [total] + came,
         )
-        their_step = swap(weight[2], 1)
-        messages = message
+
+        messages = after(message, sent) if sides == 2 else message
         for bit, radix in reversed(rounds):
             if bit >= members:
                 came = [swap(messages, j * bit) for j in range(1, radix)]
                 messages = jnp.concatenate([messages] + came, axis=0)
-
-        split = [weight[2][p * height : (p + 1) * height] for p in range(parts)] if ring == 4 else []
-        last = [onward(after(piece, *came)) for piece in split[:1]]
-        block = multiply(2, weight[2], their_step, gate=owned_rows)
+        second += [onward(after(half, *came)) for half in halves[1:]]
+        third = []
+        if ring == 4:
+            third = [onward(after(piece, *came) if p == 0 else piece) for p, piece in enumerate(second)]
         (square,) = call(gathered_kernel, "gathered", [((8, 128), f32)], [messages])
         if sides == 2:
-            sent = give_back(2, block, gate=later)
-            square = after(square, sent)
+            square = after(square, later)
         squares = [square] + [swap(square, x) for x in range(1, members)]
-        last += [onward(after(piece, square)) for piece in split[1:]]
         new_first, new_second, update = call(
             functools.partial(moment_kernel, lay, rows),
             "moment",
             [((owned, outs), f32), ((owned, outs), f32), ((ring, owned, outs), bf16)],
             squares + basis + [owned_rows, first_moment, second_moment, messages],
         )
+        piece = after(second[0], owned_rows)
+        block = multiply(2, piece, swap(piece, 1))
+        sent = give_back(2, block, gate=update)
+
         whole = update
         for bit, radix in reversed(rounds[1:]):
             if bit < members:
-                whole = jnp.concatenate(
-                    [whole] + [swap(whole, j * bit) for j in range(1, radix)], axis=0
-                )
+                whole = jnp.concatenate([whole, swap(whole, bit)], axis=0)
         (new_master,) = call(
             functools.partial(back_kernel, lay, owned),
             "back",
@@ -498,21 +497,24 @@
             moved=8 * 2**20,
         )
 
-        for p in range(len(split)):
-            piece = after(last[p], update if p == 0 else sent)
-            block = multiply(3, piece, swap(piece, 1), p * height)
-            sent = give_back(3, block, p * height)
-        if not split:
+        spots = [(2, p, second[p]) for p in range(1, parts)]
+        spots += [(3, p, third[p]) for p in range(len(third))]
+        if ring != 4:
+            spots = []
             for s in range(3, ring):
-                weight.append(onward(weight[s - 1]))
-                give_back(s, multiply(s, weight[s], swap(weight[s], 1)))
+                second = [onward(piece) for piece in second]
+                spots += [(s, p, piece) for p, piece in enumerate(second)]
+        for s, p, piece in spots:
+            piece = after(piece, sent, new_master) if (s, p) == (3, parts - 1) else after(piece, sent)
+            block = multiply(s, piece, swap(piece, 1), p * height)
+            sent = give_back(s, block, p * height)
         activation_grad = state["out"]
         if waiting:
             (activation_grad,) = call(
                 functools.partial(last_kernel, lay, rows, [spot for spot, block in waiting]),
                 "last",
                 [((tokens, width), bf16)],
-                [after(block, new_master) for spot, block in waiting] + [activation_grad],
+                [block for spot, block in waiting] + [activation_grad],
                 [VMEM] * len(waiting) + [HBM],
                 [HBM],
                 scratch=[pltpu.SemaphoreType.DMA((len(waiting), 2))],

time: 177 us -> 185 us (1.045)
  starting transfers between devices: 33.7 us -> 36.8 us
  waiting for transfers between devices: 120 us -> 123 us
    ppermute x7 -> x8, waiting for transfers between devices: 58.2 us -> 73 us  [onward(): return lax.ppermute(value, 'dp', self.forward)]
    ppermute x27 -> x29, waiting for transfers between devices: 61.6 us -> 50.4 us  [swap(): return lax.ppermute(value, 'dp', [(i, i ^ bit) for i in range(self.n)])]
    ppermute x27 -> x29, starting transfers between devices: 24.7 us -> 26.7 us  [swap(): return lax.ppermute(value, 'dp', [(i, i ^ bit) for i in range(self.n)])]
    ppermute x7 -> x8, starting transfers between devices: 9.02 us -> 10.1 us  [onward(): return lax.ppermute(value, 'dp', self.forward)]
    pallas_call x14 -> x15, Pallas kernels: 18.9 us -> 19.7 us  [call(): pl.pallas_call(kernel, name=name, out_shape=[jax.ShapeDtypeStruct(shape,...]
  transfers between devices with their start and end apart: 34 -> 37, of which waited for: 20 -> 20; matrix products, arithmetic and copies ran while one was open for 0% -> 0% of each run, Pallas kernels for 10% -> 9%
where the time goes in v13:
time: 185 us
  waiting for transfers between devices  123 us (66%)
  starting transfers between devices  36.8 us (20%)
  Pallas kernels  19.7 us (11%)
  local copies, waits for them, and re-layouts  3.48 us (2%)
    ppermute x8, waiting for transfers between devices, onward(): return lax.ppermute(value, 'dp', self.forward)  73 us
    ppermute x29, waiting for transfers between devices, swap(): return lax.ppermute(value, 'dp', [(i, i ^ bit) for i in range(self.n)])  50.4 us
    ppermute x29, starting transfers between devices, swap(): return lax.ppermute(value, 'dp', [(i, i ^ bit) for i in range(self.n)])  26.7 us
    pallas_call x15, Pallas kernels, call(): pl.pallas_call(kernel, name=name, out_shape=[jax.ShapeDtypeStruct(shape,...  19.7 us
    ppermute x8, starting transfers between devices, onward(): return lax.ppermute(value, 'dp', self.forward)  10.1 us
  transfers between devices with their start and end apart: 37, of which 20 were waited for; matrix products, arithmetic and copies ran while one was open for 0% of the time, Pallas kernels for 9%

profile of v13, /device:TPU:0, one launch (start us, length us, event | category | flops | bytes accessed | tf_op | source)
XLA Modules:
  0.0 184.7 jit_solution(8651180576342225483)
XLA Ops:
  0.6 1.0 copy-done
  1.7 2.2 %copy-done.3 = bf16[256,8192]{1,0:T(8,128)(2,1)S(1)} copy-done((bf16[256,8192]{1,0:T(8,128)(2,1)S(1)}, bf16[256,8192]{1,0:T(8,128)(2,1)}, u32[]{:S(2)}) %copy-start.3) | copy-done | bytes 4194328
  4.5 3.0 %collective-permute-start.5 = (bf16[256,3072]{1,0:T(8,128)(2,1)S(1)}, bf16[256,3072]{1,0:T(8,128)(2,1)S(1)}, u32[]{:S(2)}, u32[]{:S(2)}) collective-permute-start(bf16[256,3072]{1,0:T(8,128)(2,1)S(1)} %get-tuple-element.57), channel_id=1, source_target_pairs={{0,2},{1,3},{2,0},{3,1},{4,6},{5,7},{6,4},{7,5},{8,10},{9,11},{10,... | collective-permute-start | bytes 4718600 | tf_op jit(solution)/shard_map/ppermute | solution.py:49
  7.7 1.6 collective-permute-start
  9.3 15.5 %collective-permute-done.refs_5_ = bf16[640,512]{1,0:T(8,128)(2,1)S(1)} collective-permute-done((bf16[640,512]{1,0:T(8,128)(2,1)S(1)}, bf16[640,512]{1,0:T(8,128)(2,1)S(1)}, u32[]{:S(2)}, u32[]{:S(2)}) %collective-permute-start) | collective-permute-done | bytes 655392 | tf_op jit(solution)/shard_map/ppermute | solution.py:52
  25.9 16.1 %collective-permute-done.5.refs_2_ = bf16[256,3072]{1,0:T(8,128)(2,1)S(1)} collective-permute-done((bf16[256,3072]{1,0:T(8,128)(2,1)S(1)}, bf16[256,3072]{1,0:T(8,128)(2,1)S(1)}, u32[]{:S(2)}, u32[]{:S(2)}) %collective-permute-start.5) | collective-permute-done | bytes 1572896 | tf_op jit(solution)/shard_map/ppermute | solution.py:49
  42.2 1.9 %collective-permute-start.2 = (bf16[640,512]{1,0:T(8,128)(2,1)S(1)}, bf16[640,512]{1,0:T(8,128)(2,1)S(1)}, u32[]{:S(2)}, u32[]{:S(2)}) collective-permute-start(bf16[640,512]{1,0:T(8,128)(2,1)S(1)} %collective-permute-done.1.refs_6_), channel_id=1, source_target_pairs={{0,4},{1,5},{2,6},{3,7},{4,12},{5,13},{6,14},{7,15},{12,8},{13,9},... | collective-permute-start | bytes 1966088 | tf_op jit(solution)/shard_map/ppermute | solution.py:52
  44.2 1.5 collective-permute-start.7
  45.7 14.7 %collective-permute-done.2.refs_7_ = bf16[640,512]{1,0:T(8,128)(2,1)S(1)} collective-permute-done((bf16[640,512]{1,0:T(8,128)(2,1)S(1)}, bf16[640,512]{1,0:T(8,128)(2,1)S(1)}, u32[]{:S(2)}, u32[]{:S(2)}) %collective-permute-start.2) | collective-permute-done | bytes 655392 | tf_op jit(solution)/shard_map/ppermute | solution.py:52
  60.4 0.8 collective-permute-start.3
  61.2 2.1 %weight.6 = (bf16[256,8192]{1,0:T(8,128)(2,1)}, bf16[256,1024]{1,0:T(8,128)(2,1)S(1)}) custom-call(bf16[512,1024]{1,0:T(8,128)(2,1)S(1)} %convert_element_type.4.refs_0_, bf16[512,1024]{1,0:T(8,128)(2,1)S(1)} %collective-permute-done.4.refs_1_, bf16[256,1024]{1,0:T(8,128)(2,1)S(1)} %copy-done, bf16[256,1024]{1,0:T(8,128)(2,1)S(1)} %slice.30.refs_3_.refs_10_), custom_call_target="tpu_custom_call" | custom-call | flops 1073741824 | bytes 6291456 | tf_op jit(solution)/shard_map/weight/pallas_call | solution.py:318
  63.4 5.8 %collective-permute-done.7.refs_3_ = bf16[256,2048]{1,0:T(8,128)(2,1)S(1)} collective-permute-done((bf16[256,2048]{1,0:T(8,128)(2,1)S(1)}, bf16[256,2048]{1,0:T(8,128)(2,1)S(1)}, u32[]{:S(2)}, u32[]{:S(2)}) %collective-permute-start.7) | collective-permute-done | bytes 1048608 | tf_op jit(solution)/shard_map/ppermute | solution.py:49
  69.2 4.3 %project.1 = (f32[8,32,1024]{2,1,0:T(8,128)S(1)}, bf16[8,32,1024]{2,1,0:T(8,128)(2,1)S(1)}) custom-call(bf16[256,2048]{1,0:T(8,128)(2,1)S(1)} %get-tuple-element.59.refs_0_, bf16[256,2048]{1,0:T(8,128)(2,1)S(1)} %collective-permute-done.6.refs_1_, bf16[256,3072]{1,0:T(8,128)(2,1)S(1)} %collective-permute-done.5.refs_2_, ...), custom_call_target="tpu_custom_call" | custom-call | flops 3221225472 | bytes 12582912 | tf_op jit(solution)/shard_map/project/pallas_call | solution.py:318
  74.2 12.0 %collective-permute-done.3.refs_0_ = bf16[512,1024]{1,0:T(8,128)(2,1)S(1)} collective-permute-done((bf16[512,1024]{1,0:T(8,128)(2,1)S(1)}, bf16[512,1024]{1,0:T(8,128)(2,1)S(1)}, u32[]{:S(2)}, u32[]{:S(2)}) %collective-permute-start.3) | collective-permute-done | bytes 1048608 | tf_op jit(solution)/shard_map/ppermute | solution.py:52
  86.3 1.4 collective-permute-start.11
  87.8 0.8 collective-permute-start.9
  88.6 6.4 %collective-permute-done.11.refs_1_ = bf16[4,32,1024]{2,1,0:T(8,128)(2,1)S(1)} collective-permute-done((bf16[4,32,1024]{2,1,0:T(8,128)(2,1)S(1)}, bf16[4,32,1024]{2,1,0:T(8,128)(2,1)S(1)}, u32[]{:S(2)}, u32[]{:S(2)}) %collective-permute-start.11) | collective-permute-done | bytes 262176 | tf_op jit(solution)/shard_map/ppermute | solution.py:49
  95.1 1.4 collective-permute-start.15
  96.5 6.2 %collective-permute-done.9.refs_0_ = bf16[256,1024]{1,0:T(8,128)(2,1)S(1)} collective-permute-done((bf16[256,1024]{1,0:T(8,128)(2,1)S(1)}, bf16[256,1024]{1,0:T(8,128)(2,1)S(1)}, u32[]{:S(2)}, u32[]{:S(2)}) %collective-permute-start.9) | collective-permute-done | bytes 524320 | tf_op jit(solution)/shard_map/ppermute | solution.py:52
  102.8 3.6 %collective-permute-start.14 = (bf16[1,32,1024]{2,1,0:T(8,128)(2,1)S(1)}, bf16[1,32,1024]{2,1,0:T(8,128)(2,1)S(1)}, u32[]{:S(2)}, u32[]{:S(2)}) collective-permute-start(bf16[1,32,1024]{2,1,0:T(8,128)(2,1)S(1)} %get-tuple-element.73), channel_id=1, source_target_pairs={{0,12},{1,13},{2,14},{3,15},{4,8},{5,9},{6,10},{7,11},{8,4},{9,5},... | collective-permute-start | bytes 196616 | tf_op jit(solution)/shard_map/ppermute | solution.py:49
  107.2 2.1 %weight.7 = (bf16[256,8192]{1,0:T(8,128)(2,1)}, bf16[256,1024]{1,0:T(8,128)(2,1)S(1)}) custom-call(bf16[512,1024]{1,0:T(8,128)(2,1)S(1)} %collective-permute-done.3.refs_0_, bf16[512,1024]{1,0:T(8,128)(2,1)S(1)} %collective-permute-done.22.refs_1_, bf16[256,1024]{1,0:T(8,128)(2,1)S(1)} %copy-done.1, ...), custom_call_target="tpu_custom_call", output_to_operand_aliasing={{0}: (4, {})} | custom-call | flops 1073741824 | bytes 6291456 | tf_op jit(solution)/shard_map/weight/pallas_call | solution.py:318
  110.0 1.6 collective-permute-done.13.refs_2_
  112.9 1.7 collective-permute-start.17
  114.6 2.0 %collective-permute-start.18 = (bf16[1,48,1024]{2,1,0:T(8,128)(2,1)S(1)}, bf16[1,48,1024]{2,1,0:T(8,128)(2,1)S(1)}, u32[]{:S(2)}, u32[]{:S(2)}) collective-permute-start(bf16[1,48,1024]{2,1,0:T(8,128)(2,1)S(1)} %get-tuple-element.76), channel_id=1, source_target_pairs={{0,12},{1,13},{2,14},{3,15},{4,8},{5,9},{6,10},{7,11},{8,4},{9,5},... | collective-permute-start | bytes 294920 | tf_op jit(solution)/shard_map/ppermute | solution.py:49
  116.6 2.3 %collective-permute-done.16 = bf16[1,48,1024]{2,1,0:T(8,128)(2,1)S(1)} collective-permute-done((bf16[1,48,1024]{2,1,0:T(8,128)(2,1)S(1)}, bf16[1,48,1024]{2,1,0:T(8,128)(2,1)S(1)}, u32[]{:S(2)}, u32[]{:S(2)}) %collective-permute-start.16) | collective-permute-done | bytes 98336 | tf_op jit(solution)/shard_map/ppermute | solution.py:49
  119.0 4.8 %collective-permute-done.17 = bf16[1,48,1024]{2,1,0:T(8,128)(2,1)S(1)} collective-permute-done((bf16[1,48,1024]{2,1,0:T(8,128)(2,1)S(1)}, bf16[1,48,1024]{2,1,0:T(8,128)(2,1)S(1)}, u32[]{:S(2)}, u32[]{:S(2)}) %collective-permute-start.17) | collective-permute-done | bytes 98336 | tf_op jit(solution)/shard_map/ppermute | solution.py:49
  123.7 1.9 %collective-permute-start.20 = (bf16[256,1024]{1,0:T(8,128)(2,1)S(1)}, bf16[256,1024]{1,0:T(8,128)(2,1)S(1)}, u32[]{:S(2)}, u32[]{:S(2)}) collective-permute-start(bf16[256,1024]{1,0:T(8,128)(2,1)S(1)} %get-tuple-element.78), channel_id=1, source_target_pairs={{0,4},{1,5},{2,6},{3,7},{4,12},{5,13},{6,14},{7,15},{12,8},{13,9},... | collective-permute-start | bytes 1572872 | tf_op jit(solution)/shard_map/ppermute | solution.py:52
  126.5 1.3 collective-permute-start.26
  127.8 1.5 weight.8
  129.6 1.1 moment.1
  130.7 1.4 collective-permute-start.27
  132.1 6.1 %collective-permute-done.20.refs_0_ = bf16[256,1024]{1,0:T(8,128)(2,1)S(1)} collective-permute-done((bf16[256,1024]{1,0:T(8,128)(2,1)S(1)}, bf16[256,1024]{1,0:T(8,128)(2,1)S(1)}, u32[]{:S(2)}, u32[]{:S(2)}) %collective-permute-start.20) | collective-permute-done | bytes 524320 | tf_op jit(solution)/shard_map/ppermute | solution.py:52
  138.2 1.1 collective-permute-done.27.refs_4_
  139.3 1.1 collective-permute-start.19
  140.4 0.8 collective-permute-done.28.refs_1_
  141.2 1.5 weight.9
  142.7 1.6 collective-permute-start.29
  144.8 9.7 %collective-permute-done.19.refs_0_ = bf16[256,1024]{1,0:T(8,128)(2,1)S(1)} collective-permute-done((bf16[256,1024]{1,0:T(8,128)(2,1)S(1)}, bf16[256,1024]{1,0:T(8,128)(2,1)S(1)}, u32[]{:S(2)}, u32[]{:S(2)}) %collective-permute-start.19) | collective-permute-done | bytes 524320 | tf_op jit(solution)/shard_map/ppermute | solution.py:52
  154.6 2.2 %collective-permute-done.33 = bf16[4,32,1024]{2,1,0:T(8,128)(2,1)S(1)} collective-permute-done((bf16[4,32,1024]{2,1,0:T(8,128)(2,1)S(1)}, bf16[4,32,1024]{2,1,0:T(8,128)(2,1)S(1)}, u32[]{:S(2)}, u32[]{:S(2)}) %collective-permute-start.33) | collective-permute-done | bytes 262176 | tf_op jit(solution)/shard_map/ppermute | solution.py:49
  156.8 1.2 collective-permute-start.32
  158.0 1.5 weight.10
  159.5 1.6 collective-permute-start.31
  161.1 2.2 %back.1 = f32[512,1024]{1,0:T(8,128)} custom-call(bf16[512,512]{1,0:T(8,128)(2,1)S(1)} %copy-done.4, bf16[8,32,1024]{2,1,0:T(8,128)(2,1)S(1)} %constant_dynamic-update-slice_fusion.4.near, bf16[8,32,1024]{2,1,0:T(8,128)(2,1)S(1)} %collective-permute-done.34.other, f32[512,1024]{1,0:T(8,128)S(1)} %copy-done.2), custom_call_target="tpu_custom_call" | custom-call | flops 536870912 | bytes 8388608 | tf_op jit(solution)/shard_map/back/pallas_call | solution.py:318
  163.3 8.8 %collective-permute-done.32.refs_0_ = bf16[256,1024]{1,0:T(8,128)(2,1)S(1)} collective-permute-done((bf16[256,1024]{1,0:T(8,128)(2,1)S(1)}, bf16[256,1024]{1,0:T(8,128)(2,1)S(1)}, u32[]{:S(2)}, u32[]{:S(2)}) %collective-permute-start.32) | collective-permute-done | bytes 524320 | tf_op jit(solution)/shard_map/ppermute | solution.py:52
  172.1 1.9 %collective-permute-done.35.refs_1_ = bf16[256,1024]{1,0:T(8,128)(2,1)S(1)} collective-permute-done((bf16[256,1024]{1,0:T(8,128)(2,1)S(1)}, bf16[256,1024]{1,0:T(8,128)(2,1)S(1)}, u32[]{:S(2)}, u32[]{:S(2)}) %collective-permute-start.35) | collective-permute-done | bytes 524320 | tf_op jit(solution)/shard_map/ppermute | solution.py:49
  174.0 1.5 weight.11
  175.5 1.6 collective-permute-start.36
  177.0 6.8 %collective-permute-done.36.refs_1_ = bf16[256,512]{1,0:T(8,128)(2,1)S(1)} collective-permute-done((bf16[256,512]{1,0:T(8,128)(2,1)S(1)}, bf16[256,512]{1,0:T(8,128)(2,1)S(1)}, u32[]{:S(2)}, u32[]{:S(2)}) %collective-permute-start.36) | collective-permute-done | bytes 262176 | tf_op jit(solution)/shard_map/ppermute | solution.py:49
  (70 shorter events, 8.4 us)
Async XLA Ops:
  0.6 1.0 copy-start
  1.7 2.2 %copy-start.3 = (bf16[256,8192]{1,0:T(8,128)(2,1)S(1)}, bf16[256,8192]{1,0:T(8,128)(2,1)}, u32[]{:S(2)}) copy-start(bf16[256,8192]{1,0:T(8,128)(2,1)} %act.1) | copy-start | bytes 12582916
  3.9 3.7 %copy-start.6 = (f32[32,1024]{1,0:T(8,128)S(1)}, f32[32,1024]{1,0:T(8,128)}, u32[]{:S(2)}) copy-start(f32[32,1024]{1,0:T(8,128)} %refs_9_.1) | copy-start | bytes 393220
  3.9 3.7 %copy-start.5 = (f32[32,1024]{1,0:T(8,128)S(1)}, f32[32,1024]{1,0:T(8,128)}, u32[]{:S(2)}) copy-start(f32[32,1024]{1,0:T(8,128)} %refs_10_.1) | copy-start | bytes 393220
  3.9 3.8 %copy-start.4 = (bf16[512,512]{1,0:T(8,128)(2,1)S(1)}, bf16[512,512]{1,0:T(8,128)(2,1)}, u32[]{:S(2)}) copy-start(bf16[512,512]{1,0:T(8,128)(2,1)} %basis.1) | copy-start | bytes 1572868
  3.9 21.7 %copy-start.2 = (f32[512,1024]{1,0:T(8,128)S(1)}, f32[512,1024]{1,0:T(8,128)}, u32[]{:S(2)}) copy-start(f32[512,1024]{1,0:T(8,128)} %master.1) | copy-start | bytes 6291460
  4.5 37.4 %collective-permute-start.5 = (bf16[256,3072]{1,0:T(8,128)(2,1)S(1)}, bf16[256,3072]{1,0:T(8,128)(2,1)S(1)}, u32[]{:S(2)}, u32[]{:S(2)}) collective-permute-start(bf16[256,3072]{1,0:T(8,128)(2,1)S(1)} %get-tuple-element.57), channel_id=1, source_target_pairs={{0,2},{1,3},{2,0},{3,1},{4,6},{5,7},{6,4},{7,5},{8,10},{9,11},{10,... | collective-permute-start | bytes 4718600 | tf_op jit(solution)/shard_map/ppermute | solution.py:49
  7.7 17.1 %collective-permute-start = (bf16[640,512]{1,0:T(8,128)(2,1)S(1)}, bf16[640,512]{1,0:T(8,128)(2,1)S(1)}, u32[]{:S(2)}, u32[]{:S(2)}) collective-permute-start(bf16[640,512]{1,0:T(8,128)(2,1)S(1)} %fusion.refs_4_), channel_id=1, source_target_pairs={{0,4},{1,5},{2,6},{3,7},{4,12},{5,13},{6,14},{7,15},{12,8},{13,9},... | collective-permute-start | bytes 1966088 | tf_op jit(solution)/shard_map/ppermute | solution.py:52
  24.8 17.3 %collective-permute-start.1 = (bf16[640,512]{1,0:T(8,128)(2,1)S(1)}, bf16[640,512]{1,0:T(8,128)(2,1)S(1)}, u32[]{:S(2)}, u32[]{:S(2)}) collective-permute-start(bf16[640,512]{1,0:T(8,128)(2,1)S(1)} %collective-permute-done.refs_5_), channel_id=1, source_target_pairs={{0,4},{1,5},{2,6},{3,7},{4,12},{5,13},{6,14},{7,15},{12,8},{13,9},... | collective-permute-start | bytes 1966088 | tf_op jit(solution)/shard_map/ppermute | solution.py:52
  25.8 35.4 %collective-permute-start.4 = (bf16[512,1024]{1,0:T(8,128)(2,1)S(1)}, bf16[512,1024]{1,0:T(8,128)(2,1)S(1)}, u32[]{:S(2)}, u32[]{:S(2)}) collective-permute-start(bf16[512,1024]{1,0:T(8,128)(2,1)S(1)} %convert_element_type.4.refs_0_), channel_id=1, source_target_pairs={{0,1},{1,0},{2,3},{3,2},{4,5},{5,4},{6,7},{7,6},{8,9},{9,8},{10,11... | collective-permute-start | bytes 3145736 | tf_op jit(solution)/shard_map/ppermute | solution.py:49
  42.1 21.2 %collective-permute-start.8 = (bf16[512,1024]{1,0:T(8,128)(2,1)S(1)}, bf16[512,1024]{1,0:T(8,128)(2,1)S(1)}, u32[]{:S(2)}, u32[]{:S(2)}) collective-permute-start(bf16[512,1024]{1,0:T(8,128)(2,1)S(1)} %pad_maximum_fusion), channel_id=1, source_target_pairs={{0,1},{1,0},{2,3},{3,2},{4,5},{5,4},{6,7},{7,6},{8,9},{9,8},{10,11... | collective-permute-start | bytes 3145736 | tf_op jit(solution)/shard_map/ppermute | solution.py:49
  42.2 18.2 %collective-permute-start.2 = (bf16[640,512]{1,0:T(8,128)(2,1)S(1)}, bf16[640,512]{1,0:T(8,128)(2,1)S(1)}, u32[]{:S(2)}, u32[]{:S(2)}) collective-permute-start(bf16[640,512]{1,0:T(8,128)(2,1)S(1)} %collective-permute-done.1.refs_6_), channel_id=1, source_target_pairs={{0,4},{1,5},{2,6},{3,7},{4,12},{5,13},{6,14},{7,15},{12,8},{13,9},... | collective-permute-start | bytes 1966088 | tf_op jit(solution)/shard_map/ppermute | solution.py:52
  44.0 19.4 %collective-permute-start.6 = (bf16[256,2048]{1,0:T(8,128)(2,1)S(1)}, bf16[256,2048]{1,0:T(8,128)(2,1)S(1)}, u32[]{:S(2)}, u32[]{:S(2)}) collective-permute-start(bf16[256,2048]{1,0:T(8,128)(2,1)S(1)} %get-tuple-element.60), channel_id=1, source_target_pairs={{0,1},{1,0},{2,3},{3,2},{4,5},{5,4},{6,7},{7,6},{8,9},{9,8},{10,11... | collective-permute-start | bytes 3145736 | tf_op jit(solution)/shard_map/ppermute | solution.py:49
  44.2 25.0 %copy-start.1 = (bf16[256,1024]{1,0:T(8,128)(2,1)S(1)}, bf16[256,1024]{1,0:T(8,128)(2,1)}, u32[]{:S(2)}) copy-start(bf16[256,1024]{1,0:T(8,128)(2,1)} %refs_2_.11) | copy-start | bytes 1572868
  44.2 25.0 %collective-permute-start.7 = (bf16[256,2048]{1,0:T(8,128)(2,1)S(1)}, bf16[256,2048]{1,0:T(8,128)(2,1)S(1)}, u32[]{:S(2)}, u32[]{:S(2)}) collective-permute-start(bf16[256,2048]{1,0:T(8,128)(2,1)S(1)} %get-tuple-element.61), channel_id=1, source_target_pairs={{0,3},{1,2},{2,1},{3,0},{4,7},{5,6},{6,5},{7,4},{8,11},{9,10},{10,... | collective-permute-start | bytes 3145736 | tf_op jit(solution)/shard_map/ppermute | solution.py:49
  60.4 25.8 %collective-permute-start.3 = (bf16[512,1024]{1,0:T(8,128)(2,1)S(1)}, bf16[512,1024]{1,0:T(8,128)(2,1)S(1)}, u32[]{:S(2)}, u32[]{:S(2)}) collective-permute-start(bf16[512,1024]{1,0:T(8,128)(2,1)S(1)} %convert_element_type.4.refs_0_), channel_id=1, source_target_pairs={{0,4},{1,5},{2,6},{3,7},{4,12},{5,13},{6,14},{7,15},{12,8},{13,9},... | collective-permute-start | bytes 3145736 | tf_op jit(solution)/shard_map/ppermute | solution.py:52
  73.5 12.7 %collective-permute-start.10 = (bf16[8,32,1024]{2,1,0:T(8,128)(2,1)S(1)}, bf16[8,32,1024]{2,1,0:T(8,128)(2,1)S(1)}, u32[]{:S(2)}, u32[]{:S(2)}) collective-permute-start(bf16[8,32,1024]{2,1,0:T(8,128)(2,1)S(1)} %get-tuple-element.64), channel_id=1, source_target_pairs={{0,1},{1,0},{2,3},{3,2},{4,5},{5,4},{6,7},{7,6},{8,9},{9,8},{10,11... | collective-permute-start | bytes 1572872 | tf_op jit(solution)/shard_map/ppermute | solution.py:49
  86.2 21.0 %collective-permute-start.22 = (bf16[512,1024]{1,0:T(8,128)(2,1)S(1)}, bf16[512,1024]{1,0:T(8,128)(2,1)S(1)}, u32[]{:S(2)}, u32[]{:S(2)}) collective-permute-start(bf16[512,1024]{1,0:T(8,128)(2,1)S(1)} %collective-permute-done.3.refs_0_), channel_id=1, source_target_pairs={{0,1},{1,0},{2,3},{3,2},{4,5},{5,4},{6,7},{7,6},{8,9},{9,8},{10,11... | collective-permute-start | bytes 3145736 | tf_op jit(solution)/shard_map/ppermute | solution.py:49
  86.3 8.8 %collective-permute-start.11 = (bf16[4,32,1024]{2,1,0:T(8,128)(2,1)S(1)}, bf16[4,32,1024]{2,1,0:T(8,128)(2,1)S(1)}, u32[]{:S(2)}, u32[]{:S(2)}) collective-permute-start(bf16[4,32,1024]{2,1,0:T(8,128)(2,1)S(1)} %get-tuple-element.66), channel_id=1, source_target_pairs={{0,2},{1,3},{2,0},{3,1},{4,6},{5,7},{6,4},{7,5},{8,10},{9,11},{10,... | collective-permute-start | bytes 786440 | tf_op jit(solution)/shard_map/ppermute | solution.py:49
  87.8 15.0 %collective-permute-start.9 = (bf16[256,1024]{1,0:T(8,128)(2,1)S(1)}, bf16[256,1024]{1,0:T(8,128)(2,1)S(1)}, u32[]{:S(2)}, u32[]{:S(2)}) collective-permute-start(bf16[256,1024]{1,0:T(8,128)(2,1)S(1)} %get-tuple-element.103), channel_id=1, source_target_pairs={{0,4},{1,5},{2,6},{3,7},{4,12},{5,13},{6,14},{7,15},{12,8},{13,9},... | collective-permute-start | bytes 1572872 | tf_op jit(solution)/shard_map/ppermute | solution.py:52
  95.1 17.1 %collective-permute-start.15 = (bf16[256,1024]{1,0:T(8,128)(2,1)S(1)}, bf16[256,1024]{1,0:T(8,128)(2,1)S(1)}, u32[]{:S(2)}, u32[]{:S(2)}) collective-permute-start(bf16[256,1024]{1,0:T(8,128)(2,1)S(1)} %get-tuple-element.75), channel_id=1, source_target_pairs={{0,2},{1,3},{2,0},{3,1},{4,6},{5,7},{6,4},{7,5},{8,10},{9,11},{10,... | collective-permute-start | bytes 1572872 | tf_op jit(solution)/shard_map/ppermute | solution.py:49
  102.8 7.2 %collective-permute-start.14 = (bf16[1,32,1024]{2,1,0:T(8,128)(2,1)S(1)}, bf16[1,32,1024]{2,1,0:T(8,128)(2,1)S(1)}, u32[]{:S(2)}, u32[]{:S(2)}) collective-permute-start(bf16[1,32,1024]{2,1,0:T(8,128)(2,1)S(1)} %get-tuple-element.73), channel_id=1, source_target_pairs={{0,12},{1,13},{2,14},{3,15},{4,8},{5,9},{6,10},{7,11},{8,4},{9,5},... | collective-permute-start | bytes 196616 | tf_op jit(solution)/shard_map/ppermute | solution.py:49
  106.4 5.2 %collective-permute-start.13 = (bf16[1,32,1024]{2,1,0:T(8,128)(2,1)S(1)}, bf16[1,32,1024]{2,1,0:T(8,128)(2,1)S(1)}, u32[]{:S(2)}, u32[]{:S(2)}) collective-permute-start(bf16[1,32,1024]{2,1,0:T(8,128)(2,1)S(1)} %get-tuple-element.71), channel_id=1, source_target_pairs={{0,8},{1,9},{2,10},{3,11},{4,12},{5,13},{6,14},{7,15},{8,0},{9,1},... | collective-permute-start | bytes 196616 | tf_op jit(solution)/shard_map/ppermute | solution.py:49
  106.4 5.5 %collective-permute-start.12 = (bf16[1,32,1024]{2,1,0:T(8,128)(2,1)S(1)}, bf16[1,32,1024]{2,1,0:T(8,128)(2,1)S(1)}, u32[]{:S(2)}, u32[]{:S(2)}) collective-permute-start(bf16[1,32,1024]{2,1,0:T(8,128)(2,1)S(1)} %get-tuple-element.69), channel_id=1, source_target_pairs={{0,4},{1,5},{2,6},{3,7},{4,0},{5,1},{6,2},{7,3},{8,12},{9,13},{10,... | collective-permute-start | bytes 196616 | tf_op jit(solution)/shard_map/ppermute | solution.py:49
  109.3 16.5 %collective-permute-start.23 = (bf16[256,1024]{1,0:T(8,128)(2,1)S(1)}, bf16[256,1024]{1,0:T(8,128)(2,1)S(1)}, u32[]{:S(2)}, u32[]{:S(2)}) collective-permute-start(bf16[256,1024]{1,0:T(8,128)(2,1)S(1)} %get-tuple-element.86), channel_id=1, source_target_pairs={{0,2},{1,3},{2,0},{3,1},{4,6},{5,7},{6,4},{7,5},{8,10},{9,11},{10,... | collective-permute-start | bytes 1572872 | tf_op jit(solution)/shard_map/ppermute | solution.py:49
  112.1 15.7 %collective-permute-start.21 = (bf16[256,1024]{1,0:T(8,128)(2,1)S(1)}, bf16[256,1024]{1,0:T(8,128)(2,1)S(1)}, u32[]{:S(2)}, u32[]{:S(2)}) collective-permute-start(bf16[256,1024]{1,0:T(8,128)(2,1)S(1)} %collective-permute-done.9.refs_0_), channel_id=1, source_target_pairs={{0,1},{1,0},{2,3},{3,2},{4,5},{5,4},{6,7},{7,6},{8,9},{9,8},{10,11... | collective-permute-start | bytes 1572872 | tf_op jit(solution)/shard_map/ppermute | solution.py:49
  112.2 6.8 %collective-permute-start.16 = (bf16[1,48,1024]{2,1,0:T(8,128)(2,1)S(1)}, bf16[1,48,1024]{2,1,0:T(8,128)(2,1)S(1)}, u32[]{:S(2)}, u32[]{:S(2)}) collective-permute-start(bf16[1,48,1024]{2,1,0:T(8,128)(2,1)S(1)} %get-tuple-element.76), channel_id=1, source_target_pairs={{0,4},{1,5},{2,6},{3,7},{4,0},{5,1},{6,2},{7,3},{8,12},{9,13},{10,... | collective-permute-start | bytes 294920 | tf_op jit(solution)/shard_map/ppermute | solution.py:49
  112.9 10.8 %collective-permute-start.17 = (bf16[1,48,1024]{2,1,0:T(8,128)(2,1)S(1)}, bf16[1,48,1024]{2,1,0:T(8,128)(2,1)S(1)}, u32[]{:S(2)}, u32[]{:S(2)}) collective-permute-start(bf16[1,48,1024]{2,1,0:T(8,128)(2,1)S(1)} %get-tuple-element.76), channel_id=1, source_target_pairs={{0,8},{1,9},{2,10},{3,11},{4,12},{5,13},{6,14},{7,15},{8,0},{9,1},... | collective-permute-start | bytes 294920 | tf_op jit(solution)/shard_map/ppermute | solution.py:49
  114.6 9.1 %collective-permute-start.18 = (bf16[1,48,1024]{2,1,0:T(8,128)(2,1)S(1)}, bf16[1,48,1024]{2,1,0:T(8,128)(2,1)S(1)}, u32[]{:S(2)}, u32[]{:S(2)}) collective-permute-start(bf16[1,48,1024]{2,1,0:T(8,128)(2,1)S(1)} %get-tuple-element.76), channel_id=1, source_target_pairs={{0,12},{1,13},{2,14},{3,15},{4,8},{5,9},{6,10},{7,11},{8,4},{9,5},... | collective-permute-start | bytes 294920 | tf_op jit(solution)/shard_map/ppermute | solution.py:49
  123.7 14.4 %collective-permute-start.20 = (bf16[256,1024]{1,0:T(8,128)(2,1)S(1)}, bf16[256,1024]{1,0:T(8,128)(2,1)S(1)}, u32[]{:S(2)}, u32[]{:S(2)}) collective-permute-start(bf16[256,1024]{1,0:T(8,128)(2,1)S(1)} %get-tuple-element.78), channel_id=1, source_target_pairs={{0,4},{1,5},{2,6},{3,7},{4,12},{5,13},{6,14},{7,15},{12,8},{13,9},... | collective-permute-start | bytes 1572872 | tf_op jit(solution)/shard_map/ppermute | solution.py:52
  125.8 3.5 %collective-permute-start.24 = (f32[8,128]{1,0:T(8,128)S(1)}, f32[8,128]{1,0:T(8,128)S(1)}, u32[]{:S(2)}, u32[]{:S(2)}) collective-permute-start(f32[8,128]{1,0:T(8,128)S(1)} %gathered.1.refs_0_), channel_id=1, source_target_pairs={{0,1},{1,0},{2,3},{3,2},{4,5},{5,4},{6,7},{7,6},{8,9},{9,8},{10,11... | collective-permute-start | bytes 12296 | tf_op jit(solution)/shard_map/ppermute | solution.py:49
  125.9 3.7 %collective-permute-start.25 = (f32[8,128]{1,0:T(8,128)S(1)}, f32[8,128]{1,0:T(8,128)S(1)}, u32[]{:S(2)}, u32[]{:S(2)}) collective-permute-start(f32[8,128]{1,0:T(8,128)S(1)} %gathered.1.refs_0_), channel_id=1, source_target_pairs={{0,2},{1,3},{2,0},{3,1},{4,6},{5,7},{6,4},{7,5},{8,10},{9,11},{10,... | collective-permute-start | bytes 12296 | tf_op jit(solution)/shard_map/ppermute | solution.py:49
  126.5 3.1 %collective-permute-start.26 = (f32[8,128]{1,0:T(8,128)S(1)}, f32[8,128]{1,0:T(8,128)S(1)}, u32[]{:S(2)}, u32[]{:S(2)}) collective-permute-start(f32[8,128]{1,0:T(8,128)S(1)} %gathered.1.refs_0_), channel_id=1, source_target_pairs={{0,3},{1,2},{2,1},{3,0},{4,7},{5,6},{6,5},{7,4},{8,11},{9,10},{10,... | collective-permute-start | bytes 12296 | tf_op jit(solution)/shard_map/ppermute | solution.py:49
  130.7 8.6 %collective-permute-start.27 = (bf16[256,512]{1,0:T(8,128)(2,1)S(1)}, bf16[256,512]{1,0:T(8,128)(2,1)S(1)}, u32[]{:S(2)}, u32[]{:S(2)}) collective-permute-start(bf16[256,512]{1,0:T(8,128)(2,1)S(1)} %get-tuple-element.89), channel_id=1, source_target_pairs={{0,2},{1,3},{2,0},{3,1},{4,6},{5,7},{6,4},{7,5},{8,10},{9,11},{10,... | collective-permute-start | bytes 786440 | tf_op jit(solution)/shard_map/ppermute | solution.py:49
  139.3 1.9 %collective-permute-start.28 = (bf16[256,1024]{1,0:T(8,128)(2,1)S(1)}, bf16[256,1024]{1,0:T(8,128)(2,1)S(1)}, u32[]{:S(2)}, u32[]{:S(2)}) collective-permute-start(bf16[256,1024]{1,0:T(8,128)(2,1)S(1)} %collective-permute-done.20.refs_0_), channel_id=1, source_target_pairs={{0,1},{1,0},{2,3},{3,2},{4,5},{5,4},{6,7},{7,6},{8,9},{9,8},{10,11... | collective-permute-start | bytes 1572872 | tf_op jit(solution)/shard_map/ppermute | solution.py:49
  139.3 15.2 %collective-permute-start.19 = (bf16[256,1024]{1,0:T(8,128)(2,1)S(1)}, bf16[256,1024]{1,0:T(8,128)(2,1)S(1)}, u32[]{:S(2)}, u32[]{:S(2)}) collective-permute-start(bf16[256,1024]{1,0:T(8,128)(2,1)S(1)} %collective-permute-done.9.refs_0_), channel_id=1, source_target_pairs={{0,4},{1,5},{2,6},{3,7},{4,12},{5,13},{6,14},{7,15},{12,8},{13,9},... | collective-permute-start | bytes 1572872 | tf_op jit(solution)/shard_map/ppermute | solution.py:52
  142.7 11.8 %collective-permute-start.29 = (bf16[256,512]{1,0:T(8,128)(2,1)S(1)}, bf16[256,512]{1,0:T(8,128)(2,1)S(1)}, u32[]{:S(2)}, u32[]{:S(2)}) collective-permute-start(bf16[256,512]{1,0:T(8,128)(2,1)S(1)} %get-tuple-element.92), channel_id=1, source_target_pairs={{0,2},{1,3},{2,0},{3,1},{4,6},{5,7},{6,4},{7,5},{8,10},{9,11},{10,... | collective-permute-start | bytes 786440 | tf_op jit(solution)/shard_map/ppermute | solution.py:49
  144.3 12.4 %collective-permute-start.33 = (bf16[4,32,1024]{2,1,0:T(8,128)(2,1)S(1)}, bf16[4,32,1024]{2,1,0:T(8,128)(2,1)S(1)}, u32[]{:S(2)}, u32[]{:S(2)}) collective-permute-start(bf16[4,32,1024]{2,1,0:T(8,128)(2,1)S(1)} %get-tuple-element.88), channel_id=1, source_target_pairs={{0,2},{1,3},{2,0},{3,1},{4,6},{5,7},{6,4},{7,5},{8,10},{9,11},{10,... | collective-permute-start | bytes 786440 | tf_op jit(solution)/shard_map/ppermute | solution.py:49
  154.5 3.5 %collective-permute-start.30 = (bf16[256,1024]{1,0:T(8,128)(2,1)S(1)}, bf16[256,1024]{1,0:T(8,128)(2,1)S(1)}, u32[]{:S(2)}, u32[]{:S(2)}) collective-permute-start(bf16[256,1024]{1,0:T(8,128)(2,1)S(1)} %collective-permute-done.19.refs_0_), channel_id=1, source_target_pairs={{0,1},{1,0},{2,3},{3,2},{4,5},{5,4},{6,7},{7,6},{8,9},{9,8},{10,11... | collective-permute-start | bytes 1572872 | tf_op jit(solution)/shard_map/ppermute | solution.py:49
  156.8 4.3 %collective-permute-start.34 = (bf16[8,32,1024]{2,1,0:T(8,128)(2,1)S(1)}, bf16[8,32,1024]{2,1,0:T(8,128)(2,1)S(1)}, u32[]{:S(2)}, u32[]{:S(2)}) collective-permute-start(bf16[8,32,1024]{2,1,0:T(8,128)(2,1)S(1)} %constant_dynamic-update-slice_fusion.4.near), channel_id=1, source_target_pairs={{0,1},{1,0},{2,3},{3,2},{4,5},{5,4},{6,7},{7,6},{8,9},{9,8},{10,11... | collective-permute-start | bytes 1572872 | tf_op jit(solution)/shard_map/ppermute | solution.py:49
  156.8 15.2 %collective-permute-start.32 = (bf16[256,1024]{1,0:T(8,128)(2,1)S(1)}, bf16[256,1024]{1,0:T(8,128)(2,1)S(1)}, u32[]{:S(2)}, u32[]{:S(2)}) collective-permute-start(bf16[256,1024]{1,0:T(8,128)(2,1)S(1)} %collective-permute-done.20.refs_0_), channel_id=1, source_target_pairs={{0,4},{1,5},{2,6},{3,7},{4,12},{5,13},{6,14},{7,15},{12,8},{13,9},... | collective-permute-start | bytes 1572872 | tf_op jit(solution)/shard_map/ppermute | solution.py:52
  159.5 12.5 %collective-permute-start.31 = (bf16[256,512]{1,0:T(8,128)(2,1)S(1)}, bf16[256,512]{1,0:T(8,128)(2,1)S(1)}, u32[]{:S(2)}, u32[]{:S(2)}) collective-permute-start(bf16[256,512]{1,0:T(8,128)(2,1)S(1)} %get-tuple-element.95), channel_id=1, source_target_pairs={{0,2},{1,3},{2,0},{3,1},{4,6},{5,7},{6,4},{7,5},{8,10},{9,11},{10,... | collective-permute-start | bytes 786440 | tf_op jit(solution)/shard_map/ppermute | solution.py:49
  172.1 1.9 %collective-permute-start.35 = (bf16[256,1024]{1,0:T(8,128)(2,1)S(1)}, bf16[256,1024]{1,0:T(8,128)(2,1)S(1)}, u32[]{:S(2)}, u32[]{:S(2)}) collective-permute-start(bf16[256,1024]{1,0:T(8,128)(2,1)S(1)} %collective-permute-done.32.refs_0_), channel_id=1, source_target_pairs={{0,1},{1,0},{2,3},{3,2},{4,5},{5,4},{6,7},{7,6},{8,9},{9,8},{10,11... | collective-permute-start | bytes 1572872 | tf_op jit(solution)/shard_map/ppermute | solution.py:49
  175.5 8.4 %collective-permute-start.36 = (bf16[256,512]{1,0:T(8,128)(2,1)S(1)}, bf16[256,512]{1,0:T(8,128)(2,1)S(1)}, u32[]{:S(2)}, u32[]{:S(2)}) collective-permute-start(bf16[256,512]{1,0:T(8,128)(2,1)S(1)} %get-tuple-element.98), channel_id=1, source_target_pairs={{0,2},{1,3},{2,0},{3,1},{4,6},{5,7},{6,4},{7,5},{8,10},{9,11},{10,... | collective-permute-start | bytes 786440 | tf_op jit(solution)/shard_map/ppermute | solution.py:49

commit v14 on v11

--- a/solution.py
+++ b/solution.py
@@ -364,6 +364,7 @@
         weight.append(onward(after(weight[0], basis[-1])))
 
         if sides == 2:
+            acts[2] = after(acts[2], basis[2])
             far_grad = acts[2][:, ring * rows :]
             near = swap(jnp.concatenate([key_grad, far_grad], axis=0), 1)
             grads = [key_grad, near[:tokens], far_grad, near[tokens:]]
@@ -434,7 +435,7 @@
 
         for k, (bit, radix) in enumerate(rounds):
             if bit == members:
-                gives = [after(give, weight[2], block, sent if sides == 2 else block) for give in gives]
+                gives = [after(give, weight[2], sent if sides == 2 else block) for give in gives]
             came = [swap(give, j * bit) for j, give in zip(range(1, radix), gives)]
             if k == len(rounds) - 1:
                 break
@@ -444,7 +445,7 @@
                 functools.partial(fold_kernel, next_bit, next_radix, len(came)),
                 "fold",
                 [(shape, f32)] + [(shape, bf16)] * (next_radix - 1),
-                [total] + came,
+                [after(total, block) if bit == 2 else total] + came,
                 moved=4 * total.size,
             )
             if bit == 1:
@@ -501,7 +502,7 @@
         for p in range(len(split)):
             piece = after(last[p], update if p == 0 else sent)
             block = multiply(3, piece, swap(piece, 1), p * height)
-            sent = give_back(3, block, p * height)
+            sent = give_back(3, block, p * height, whole if p == 0 else None)
         if not split:
             for s in range(3, ring):
                 weight.append(onward(weight[s - 1]))

time: 177 us -> 171 us (0.966)
  waiting for transfers between devices: 120 us -> 113 us
    ppermute x27, waiting for transfers between devices: 61.6 us -> 45.9 us  [swap(): return lax.ppermute(value, 'dp', [(i, i ^ bit) for i in range(self.n)])]
    ppermute x7, waiting for transfers between devices: 58.2 us -> 67.2 us  [onward(): return lax.ppermute(value, 'dp', self.forward)]
    ppermute x27, starting transfers between devices: 24.7 us -> 27.4 us  [swap(): return lax.ppermute(value, 'dp', [(i, i ^ bit) for i in range(self.n)])]
    ppermute x7, starting transfers between devices: 9.02 us -> 7.05 us  [onward(): return lax.ppermute(value, 'dp', self.forward)]
where the time goes in v14:
time: 171 us
  waiting for transfers between devices  113 us (66%)
  starting transfers between devices  34.5 us (20%)
  Pallas kernels  18.9 us (11%)
  local copies, waits for them, and re-layouts  3.49 us (2%)
    ppermute x7, waiting for transfers between devices, onward(): return lax.ppermute(value, 'dp', self.forward)  67.2 us
    ppermute x27, waiting for transfers between devices, swap(): return lax.ppermute(value, 'dp', [(i, i ^ bit) for i in range(self.n)])  45.9 us
    ppermute x27, starting transfers between devices, swap(): return lax.ppermute(value, 'dp', [(i, i ^ bit) for i in range(self.n)])  27.4 us
    pallas_call x14, Pallas kernels, call(): pl.pallas_call(kernel, name=name, out_shape=[jax.ShapeDtypeStruct(shape,...  18.9 us
    ppermute x7, starting transfers between devices, onward(): return lax.ppermute(value, 'dp', self.forward)  7.05 us
  transfers between devices with their start and end apart: 34, of which 20 were waited for; matrix products, arithmetic and copies ran while one was open for 0% of the time, Pallas kernels for 10%

profile of v14, /device:TPU:0, one launch (start us, length us, event | category | flops | bytes accessed | tf_op | source)
XLA Modules:
  0.0 171.1 jit_solution(10105882160084453012)
XLA Ops:
  0.6 1.0 copy-done
  1.7 2.2 %copy-done.3 = bf16[256,8192]{1,0:T(8,128)(2,1)S(1)} copy-done((bf16[256,8192]{1,0:T(8,128)(2,1)S(1)}, bf16[256,8192]{1,0:T(8,128)(2,1)}, u32[]{:S(2)}) %copy-start.3) | copy-done | bytes 4194328
  4.5 3.0 %collective-permute-start.5 = (bf16[256,3072]{1,0:T(8,128)(2,1)S(1)}, bf16[256,3072]{1,0:T(8,128)(2,1)S(1)}, u32[]{:S(2)}, u32[]{:S(2)}) collective-permute-start(bf16[256,3072]{1,0:T(8,128)(2,1)S(1)} %get-tuple-element.59), channel_id=1, source_target_pairs={{0,2},{1,3},{2,0},{3,1},{4,6},{5,7},{6,4},{7,5},{8,10},{9,11},{10,... | collective-permute-start | bytes 4718600 | tf_op jit(solution)/shard_map/ppermute | solution.py:49
  7.7 1.6 collective-permute-start
  9.3 15.5 %collective-permute-done.refs_5_ = bf16[640,512]{1,0:T(8,128)(2,1)S(1)} collective-permute-done((bf16[640,512]{1,0:T(8,128)(2,1)S(1)}, bf16[640,512]{1,0:T(8,128)(2,1)S(1)}, u32[]{:S(2)}, u32[]{:S(2)}) %collective-permute-start) | collective-permute-done | bytes 655392 | tf_op jit(solution)/shard_map/ppermute | solution.py:52
  24.8 0.8 collective-permute-start.1
  25.9 15.1 %collective-permute-done.1.refs_6_ = bf16[640,512]{1,0:T(8,128)(2,1)S(1)} collective-permute-done((bf16[640,512]{1,0:T(8,128)(2,1)S(1)}, bf16[640,512]{1,0:T(8,128)(2,1)S(1)}, u32[]{:S(2)}, u32[]{:S(2)}) %collective-permute-start.1) | collective-permute-done | bytes 655392 | tf_op jit(solution)/shard_map/ppermute | solution.py:52
  41.0 0.8 collective-permute-start.2
  42.7 1.4 collective-permute-start.7
  44.1 12.2 %collective-permute-done.2.refs_7_ = bf16[640,512]{1,0:T(8,128)(2,1)S(1)} collective-permute-done((bf16[640,512]{1,0:T(8,128)(2,1)S(1)}, bf16[640,512]{1,0:T(8,128)(2,1)S(1)}, u32[]{:S(2)}, u32[]{:S(2)}) %collective-permute-start.2) | collective-permute-done | bytes 655392 | tf_op jit(solution)/shard_map/ppermute | solution.py:52
  56.3 0.8 collective-permute-start.3
  57.1 2.1 %weight.5 = (bf16[256,8192]{1,0:T(8,128)(2,1)}, bf16[256,1024]{1,0:T(8,128)(2,1)S(1)}) custom-call(bf16[512,1024]{1,0:T(8,128)(2,1)S(1)} %convert_element_type.4.refs_0_, bf16[512,1024]{1,0:T(8,128)(2,1)S(1)} %collective-permute-done.4.refs_1_, bf16[256,1024]{1,0:T(8,128)(2,1)S(1)} %copy-done, bf16[256,1024]{1,0:T(8,128)(2,1)S(1)} %slice.23.refs_3_.refs_10_), custom_call_target="tpu_custom_call" | custom-call | flops 1073741824 | bytes 6291456 | tf_op jit(solution)/shard_map/weight/pallas_call | solution.py:318
  59.3 8.6 %collective-permute-done.7.refs_3_ = bf16[256,2048]{1,0:T(8,128)(2,1)S(1)} collective-permute-done((bf16[256,2048]{1,0:T(8,128)(2,1)S(1)}, bf16[256,2048]{1,0:T(8,128)(2,1)S(1)}, u32[]{:S(2)}, u32[]{:S(2)}) %collective-permute-start.7) | collective-permute-done | bytes 1048608 | tf_op jit(solution)/shard_map/ppermute | solution.py:49
  67.8 4.3 %project.1 = (f32[8,32,1024]{2,1,0:T(8,128)S(1)}, bf16[8,32,1024]{2,1,0:T(8,128)(2,1)S(1)}) custom-call(bf16[256,2048]{1,0:T(8,128)(2,1)S(1)} %get-tuple-element.62.refs_0_, bf16[256,2048]{1,0:T(8,128)(2,1)S(1)} %collective-permute-done.6.refs_1_, bf16[256,3072]{1,0:T(8,128)(2,1)S(1)} %collective-permute-done.5.refs_2_, ...), custom_call_target="tpu_custom_call" | custom-call | flops 3221225472 | bytes 12582912 | tf_op jit(solution)/shard_map/project/pallas_call | solution.py:318
  72.2 6.9 %collective-permute-done.3.refs_0_ = bf16[512,1024]{1,0:T(8,128)(2,1)S(1)} collective-permute-done((bf16[512,1024]{1,0:T(8,128)(2,1)S(1)}, bf16[512,1024]{1,0:T(8,128)(2,1)S(1)}, u32[]{:S(2)}, u32[]{:S(2)}) %collective-permute-start.3) | collective-permute-done | bytes 1048608 | tf_op jit(solution)/shard_map/ppermute | solution.py:52
  80.3 2.1 %collective-permute-done.10.refs_1_ = bf16[8,32,1024]{2,1,0:T(8,128)(2,1)S(1)} collective-permute-done((bf16[8,32,1024]{2,1,0:T(8,128)(2,1)S(1)}, bf16[8,32,1024]{2,1,0:T(8,128)(2,1)S(1)}, u32[]{:S(2)}, u32[]{:S(2)}) %collective-permute-start.10) | collective-permute-done | bytes 524320 | tf_op jit(solution)/shard_map/ppermute | solution.py:49
  82.5 1.7 collective-permute-start.12
  84.2 2.1 %weight.6 = (bf16[256,8192]{1,0:T(8,128)(2,1)}, bf16[256,1024]{1,0:T(8,128)(2,1)S(1)}) custom-call(bf16[512,1024]{1,0:T(8,128)(2,1)S(1)} %collective-permute-done.3.refs_0_, bf16[512,1024]{1,0:T(8,128)(2,1)S(1)} %collective-permute-done.11.refs_1_, bf16[256,1024]{1,0:T(8,128)(2,1)S(1)} %copy-done.1, ...), custom_call_target="tpu_custom_call", output_to_operand_aliasing={{0}: (4, {})} | custom-call | flops 1073741824 | bytes 6291456 | tf_op jit(solution)/shard_map/weight/pallas_call | solution.py:318
  86.3 4.6 %collective-permute-done.12.refs_1_ = bf16[4,32,1024]{2,1,0:T(8,128)(2,1)S(1)} collective-permute-done((bf16[4,32,1024]{2,1,0:T(8,128)(2,1)S(1)}, bf16[4,32,1024]{2,1,0:T(8,128)(2,1)S(1)}, u32[]{:S(2)}, u32[]{:S(2)}) %collective-permute-start.12) | collective-permute-done | bytes 262176 | tf_op jit(solution)/shard_map/ppermute | solution.py:49
  91.0 1.7 collective-permute-start.13
  92.7 12.8 %collective-permute-done.9.refs_0_ = bf16[512,1024]{1,0:T(8,128)(2,1)S(1)} collective-permute-done((bf16[512,1024]{1,0:T(8,128)(2,1)S(1)}, bf16[512,1024]{1,0:T(8,128)(2,1)S(1)}, u32[]{:S(2)}, u32[]{:S(2)}) %collective-permute-start.9) | collective-permute-done | bytes 1048608 | tf_op jit(solution)/shard_map/ppermute | solution.py:52
  105.5 1.6 collective-permute-start.22
  107.1 3.1 %collective-permute-start.16 = (bf16[1,32,1024]{2,1,0:T(8,128)(2,1)S(1)}, bf16[1,32,1024]{2,1,0:T(8,128)(2,1)S(1)}, u32[]{:S(2)}, u32[]{:S(2)}) collective-permute-start(bf16[1,32,1024]{2,1,0:T(8,128)(2,1)S(1)} %get-tuple-element.82), channel_id=1, source_target_pairs={{0,12},{1,13},{2,14},{3,15},{4,8},{5,9},{6,10},{7,11},{8,4},{9,5},... | collective-permute-start | bytes 196616 | tf_op jit(solution)/shard_map/ppermute | solution.py:49
  110.3 1.3 collective-permute-start.14
  111.5 2.4 %collective-permute-done.16.refs_3_ = bf16[1,32,1024]{2,1,0:T(8,128)(2,1)S(1)} collective-permute-done((bf16[1,32,1024]{2,1,0:T(8,128)(2,1)S(1)}, bf16[1,32,1024]{2,1,0:T(8,128)(2,1)S(1)}, u32[]{:S(2)}, u32[]{:S(2)}) %collective-permute-start.16) | collective-permute-done | bytes 65568 | tf_op jit(solution)/shard_map/ppermute | solution.py:49
  113.9 2.1 %collective-permute-done.15.refs_2_ = bf16[1,32,1024]{2,1,0:T(8,128)(2,1)S(1)} collective-permute-done((bf16[1,32,1024]{2,1,0:T(8,128)(2,1)S(1)}, bf16[1,32,1024]{2,1,0:T(8,128)(2,1)S(1)}, u32[]{:S(2)}, u32[]{:S(2)}) %collective-permute-start.15) | collective-permute-done | bytes 65568 | tf_op jit(solution)/shard_map/ppermute | solution.py:49
  116.3 1.3 collective-permute-start.17
  117.6 1.8 %collective-permute-start.18 = (bf16[1,48,1024]{2,1,0:T(8,128)(2,1)S(1)}, bf16[1,48,1024]{2,1,0:T(8,128)(2,1)S(1)}, u32[]{:S(2)}, u32[]{:S(2)}) collective-permute-start(bf16[1,48,1024]{2,1,0:T(8,128)(2,1)S(1)} %get-tuple-element.83), channel_id=1, source_target_pairs={{0,8},{1,9},{2,10},{3,11},{4,12},{5,13},{6,14},{7,15},{8,0},{9,1},... | collective-permute-start | bytes 294920 | tf_op jit(solution)/shard_map/ppermute | solution.py:49
  119.4 1.3 collective-permute-start.19
  120.8 2.1 %weight.7 = (bf16[256,8192]{1,0:T(8,128)(2,1)}, bf16[256,1024]{1,0:T(8,128)(2,1)S(1)}) custom-call(bf16[512,1024]{1,0:T(8,128)(2,1)S(1)} %collective-permute-done.9.refs_0_, bf16[512,1024]{1,0:T(8,128)(2,1)S(1)} %collective-permute-done.21.refs_1_, bf16[256,1024]{1,0:T(8,128)(2,1)S(1)} %copy-done.1, ...), custom_call_target="tpu_custom_call", output_to_operand_aliasing={{0}: (5, {})} | custom-call | flops 1073741824 | bytes 6291456 | tf_op jit(solution)/shard_map/weight/pallas_call | solution.py:318
  123.7 3.8 %collective-permute-done.18 = bf16[1,48,1024]{2,1,0:T(8,128)(2,1)S(1)} collective-permute-done((bf16[1,48,1024]{2,1,0:T(8,128)(2,1)S(1)}, bf16[1,48,1024]{2,1,0:T(8,128)(2,1)S(1)}, u32[]{:S(2)}, u32[]{:S(2)}) %collective-permute-start.18) | collective-permute-done | bytes 98336 | tf_op jit(solution)/shard_map/ppermute | solution.py:49
  127.6 1.6 collective-permute-start.20
  129.4 6.4 %collective-permute-done.23.refs_4_ = bf16[256,1024]{1,0:T(8,128)(2,1)S(1)} collective-permute-done((bf16[256,1024]{1,0:T(8,128)(2,1)S(1)}, bf16[256,1024]{1,0:T(8,128)(2,1)S(1)}, u32[]{:S(2)}, u32[]{:S(2)}) %collective-permute-start.23) | collective-permute-done | bytes 524320 | tf_op jit(solution)/shard_map/ppermute | solution.py:49
  136.1 1.6 collective-permute-start.26
  137.6 1.7 %collective-permute-done.25.refs_2_ = f32[8,128]{1,0:T(8,128)S(1)} collective-permute-done((f32[8,128]{1,0:T(8,128)S(1)}, f32[8,128]{1,0:T(8,128)S(1)}, u32[]{:S(2)}, u32[]{:S(2)}) %collective-permute-start.25) | collective-permute-done | bytes 4128 | tf_op jit(solution)/shard_map/ppermute | solution.py:49
  139.4 1.1 moment.1
  140.8 1.7 %collective-permute-start.28 = (bf16[4,32,1024]{2,1,0:T(8,128)(2,1)S(1)}, bf16[4,32,1024]{2,1,0:T(8,128)(2,1)S(1)}, u32[]{:S(2)}, u32[]{:S(2)}) collective-permute-start(bf16[4,32,1024]{2,1,0:T(8,128)(2,1)S(1)} %get-tuple-element.92), channel_id=1, source_target_pairs={{0,2},{1,3},{2,0},{3,1},{4,6},{5,7},{6,4},{7,5},{8,10},{9,11},{10,... | collective-permute-start | bytes 786440 | tf_op jit(solution)/shard_map/ppermute | solution.py:49
  143.2 6.1 %collective-permute-done.28 = bf16[4,32,1024]{2,1,0:T(8,128)(2,1)S(1)} collective-permute-done((bf16[4,32,1024]{2,1,0:T(8,128)(2,1)S(1)}, bf16[4,32,1024]{2,1,0:T(8,128)(2,1)S(1)}, u32[]{:S(2)}, u32[]{:S(2)}) %collective-permute-start.28) | collective-permute-done | bytes 262176 | tf_op jit(solution)/shard_map/ppermute | solution.py:49
  149.3 1.5 weight.8
  150.8 1.6 collective-permute-start.29
  152.3 4.6 %collective-permute-done.31.refs_0_ = bf16[256,1024]{1,0:T(8,128)(2,1)S(1)} collective-permute-done((bf16[256,1024]{1,0:T(8,128)(2,1)S(1)}, bf16[256,1024]{1,0:T(8,128)(2,1)S(1)}, u32[]{:S(2)}, u32[]{:S(2)}) %collective-permute-start.31) | collective-permute-done | bytes 524320 | tf_op jit(solution)/shard_map/ppermute | solution.py:52
  157.0 1.5 collective-permute-done.29.refs_0_
  159.0 1.4 collective-permute-done.32.refs_1_
  160.4 1.5 weight.9
  161.9 1.3 collective-permute-start.33
  163.2 2.2 %back.1 = f32[512,1024]{1,0:T(8,128)} custom-call(bf16[512,512]{1,0:T(8,128)(2,1)S(1)} %copy-done.4, bf16[8,32,1024]{2,1,0:T(8,128)(2,1)S(1)} %constant_dynamic-update-slice_fusion.4.near, bf16[8,32,1024]{2,1,0:T(8,128)(2,1)S(1)} %collective-permute-done.30.other, f32[512,1024]{1,0:T(8,128)S(1)} %copy-done.2), custom_call_target="tpu_custom_call" | custom-call | flops 536870912 | bytes 8388608 | tf_op jit(solution)/shard_map/back/pallas_call | solution.py:318
  165.4 4.9 %collective-permute-done.33.refs_1_ = bf16[256,512]{1,0:T(8,128)(2,1)S(1)} collective-permute-done((bf16[256,512]{1,0:T(8,128)(2,1)S(1)}, bf16[256,512]{1,0:T(8,128)(2,1)S(1)}, u32[]{:S(2)}, u32[]{:S(2)}) %collective-permute-start.33) | collective-permute-done | bytes 262176 | tf_op jit(solution)/shard_map/ppermute | solution.py:49
  170.3 0.8 last.1
  (63 shorter events, 6.4 us)
Async XLA Ops:
  0.6 1.0 copy-start
  1.7 2.2 %copy-start.3 = (bf16[256,8192]{1,0:T(8,128)(2,1)S(1)}, bf16[256,8192]{1,0:T(8,128)(2,1)}, u32[]{:S(2)}) copy-start(bf16[256,8192]{1,0:T(8,128)(2,1)} %act.1) | copy-start | bytes 12582916
  3.9 3.7 %copy-start.6 = (f32[32,1024]{1,0:T(8,128)S(1)}, f32[32,1024]{1,0:T(8,128)}, u32[]{:S(2)}) copy-start(f32[32,1024]{1,0:T(8,128)} %refs_9_.1) | copy-start | bytes 393220
  3.9 3.7 %copy-start.5 = (f32[32,1024]{1,0:T(8,128)S(1)}, f32[32,1024]{1,0:T(8,128)}, u32[]{:S(2)}) copy-start(f32[32,1024]{1,0:T(8,128)} %refs_10_.1) | copy-start | bytes 393220
  3.9 3.8 %copy-start.4 = (bf16[512,512]{1,0:T(8,128)(2,1)S(1)}, bf16[512,512]{1,0:T(8,128)(2,1)}, u32[]{:S(2)}) copy-start(bf16[512,512]{1,0:T(8,128)(2,1)} %basis.1) | copy-start | bytes 1572868
  3.9 21.7 %copy-start.2 = (f32[512,1024]{1,0:T(8,128)S(1)}, f32[512,1024]{1,0:T(8,128)}, u32[]{:S(2)}) copy-start(f32[512,1024]{1,0:T(8,128)} %master.1) | copy-start | bytes 6291460
  4.5 37.4 %collective-permute-start.5 = (bf16[256,3072]{1,0:T(8,128)(2,1)S(1)}, bf16[256,3072]{1,0:T(8,128)(2,1)S(1)}, u32[]{:S(2)}, u32[]{:S(2)}) collective-permute-start(bf16[256,3072]{1,0:T(8,128)(2,1)S(1)} %get-tuple-element.59), channel_id=1, source_target_pairs={{0,2},{1,3},{2,0},{3,1},{4,6},{5,7},{6,4},{7,5},{8,10},{9,11},{10,... | collective-permute-start | bytes 4718600 | tf_op jit(solution)/shard_map/ppermute | solution.py:49
  7.7 17.1 %collective-permute-start = (bf16[640,512]{1,0:T(8,128)(2,1)S(1)}, bf16[640,512]{1,0:T(8,128)(2,1)S(1)}, u32[]{:S(2)}, u32[]{:S(2)}) collective-permute-start(bf16[640,512]{1,0:T(8,128)(2,1)S(1)} %fusion.refs_4_), channel_id=1, source_target_pairs={{0,4},{1,5},{2,6},{3,7},{4,12},{5,13},{6,14},{7,15},{12,8},{13,9},... | collective-permute-start | bytes 1966088 | tf_op jit(solution)/shard_map/ppermute | solution.py:52
  24.8 16.2 %collective-permute-start.1 = (bf16[640,512]{1,0:T(8,128)(2,1)S(1)}, bf16[640,512]{1,0:T(8,128)(2,1)S(1)}, u32[]{:S(2)}, u32[]{:S(2)}) collective-permute-start(bf16[640,512]{1,0:T(8,128)(2,1)S(1)} %collective-permute-done.refs_5_), channel_id=1, source_target_pairs={{0,4},{1,5},{2,6},{3,7},{4,12},{5,13},{6,14},{7,15},{12,8},{13,9},... | collective-permute-start | bytes 1966088 | tf_op jit(solution)/shard_map/ppermute | solution.py:52
  25.8 31.3 %collective-permute-start.4 = (bf16[512,1024]{1,0:T(8,128)(2,1)S(1)}, bf16[512,1024]{1,0:T(8,128)(2,1)S(1)}, u32[]{:S(2)}, u32[]{:S(2)}) collective-permute-start(bf16[512,1024]{1,0:T(8,128)(2,1)S(1)} %convert_element_type.4.refs_0_), channel_id=1, source_target_pairs={{0,1},{1,0},{2,3},{3,2},{4,5},{5,4},{6,7},{7,6},{8,9},{9,8},{10,11... | collective-permute-start | bytes 3145736 | tf_op jit(solution)/shard_map/ppermute | solution.py:49
  41.0 15.3 %collective-permute-start.2 = (bf16[640,512]{1,0:T(8,128)(2,1)S(1)}, bf16[640,512]{1,0:T(8,128)(2,1)S(1)}, u32[]{:S(2)}, u32[]{:S(2)}) collective-permute-start(bf16[640,512]{1,0:T(8,128)(2,1)S(1)} %collective-permute-done.1.refs_6_), channel_id=1, source_target_pairs={{0,4},{1,5},{2,6},{3,7},{4,12},{5,13},{6,14},{7,15},{12,8},{13,9},... | collective-permute-start | bytes 1966088 | tf_op jit(solution)/shard_map/ppermute | solution.py:52
  42.1 17.1 %collective-permute-start.8 = (bf16[512,1024]{1,0:T(8,128)(2,1)S(1)}, bf16[512,1024]{1,0:T(8,128)(2,1)S(1)}, u32[]{:S(2)}, u32[]{:S(2)}) collective-permute-start(bf16[512,1024]{1,0:T(8,128)(2,1)S(1)} %pad_maximum_fusion), channel_id=1, source_target_pairs={{0,1},{1,0},{2,3},{3,2},{4,5},{5,4},{6,7},{7,6},{8,9},{9,8},{10,11... | collective-permute-start | bytes 3145736 | tf_op jit(solution)/shard_map/ppermute | solution.py:49
  42.2 17.1 %collective-permute-start.6 = (bf16[256,2048]{1,0:T(8,128)(2,1)S(1)}, bf16[256,2048]{1,0:T(8,128)(2,1)S(1)}, u32[]{:S(2)}, u32[]{:S(2)}) collective-permute-start(bf16[256,2048]{1,0:T(8,128)(2,1)S(1)} %get-tuple-element.63), channel_id=1, source_target_pairs={{0,1},{1,0},{2,3},{3,2},{4,5},{5,4},{6,7},{7,6},{8,9},{9,8},{10,11... | collective-permute-start | bytes 3145736 | tf_op jit(solution)/shard_map/ppermute | solution.py:49
  42.7 25.2 %copy-start.1 = (bf16[256,1024]{1,0:T(8,128)(2,1)S(1)}, bf16[256,1024]{1,0:T(8,128)(2,1)}, u32[]{:S(2)}) copy-start(bf16[256,1024]{1,0:T(8,128)(2,1)} %refs_2_.9) | copy-start | bytes 1572868
  42.7 25.2 %collective-permute-start.7 = (bf16[256,2048]{1,0:T(8,128)(2,1)S(1)}, bf16[256,2048]{1,0:T(8,128)(2,1)S(1)}, u32[]{:S(2)}, u32[]{:S(2)}) collective-permute-start(bf16[256,2048]{1,0:T(8,128)(2,1)S(1)} %get-tuple-element.64), channel_id=1, source_target_pairs={{0,3},{1,2},{2,1},{3,0},{4,7},{5,6},{6,5},{7,4},{8,11},{9,10},{10,... | collective-permute-start | bytes 3145736 | tf_op jit(solution)/shard_map/ppermute | solution.py:49
  56.3 22.8 %collective-permute-start.3 = (bf16[512,1024]{1,0:T(8,128)(2,1)S(1)}, bf16[512,1024]{1,0:T(8,128)(2,1)S(1)}, u32[]{:S(2)}, u32[]{:S(2)}) collective-permute-start(bf16[512,1024]{1,0:T(8,128)(2,1)S(1)} %convert_element_type.4.refs_0_), channel_id=1, source_target_pairs={{0,4},{1,5},{2,6},{3,7},{4,12},{5,13},{6,14},{7,15},{12,8},{13,9},... | collective-permute-start | bytes 3145736 | tf_op jit(solution)/shard_map/ppermute | solution.py:52
  79.0 5.2 %collective-permute-start.11 = (bf16[512,1024]{1,0:T(8,128)(2,1)S(1)}, bf16[512,1024]{1,0:T(8,128)(2,1)S(1)}, u32[]{:S(2)}, u32[]{:S(2)}) collective-permute-start(bf16[512,1024]{1,0:T(8,128)(2,1)S(1)} %collective-permute-done.3.refs_0_), channel_id=1, source_target_pairs={{0,1},{1,0},{2,3},{3,2},{4,5},{5,4},{6,7},{7,6},{8,9},{9,8},{10,11... | collective-permute-start | bytes 3145736 | tf_op jit(solution)/shard_map/ppermute | solution.py:49
  79.0 3.4 %collective-permute-start.10 = (bf16[8,32,1024]{2,1,0:T(8,128)(2,1)S(1)}, bf16[8,32,1024]{2,1,0:T(8,128)(2,1)S(1)}, u32[]{:S(2)}, u32[]{:S(2)}) collective-permute-start(bf16[8,32,1024]{2,1,0:T(8,128)(2,1)S(1)} %get-tuple-element.67), channel_id=1, source_target_pairs={{0,1},{1,0},{2,3},{3,2},{4,5},{5,4},{6,7},{7,6},{8,9},{9,8},{10,11... | collective-permute-start | bytes 1572872 | tf_op jit(solution)/shard_map/ppermute | solution.py:49
  79.5 26.0 %collective-permute-start.9 = (bf16[512,1024]{1,0:T(8,128)(2,1)S(1)}, bf16[512,1024]{1,0:T(8,128)(2,1)S(1)}, u32[]{:S(2)}, u32[]{:S(2)}) collective-permute-start(bf16[512,1024]{1,0:T(8,128)(2,1)S(1)} %collective-permute-done.3.refs_0_), channel_id=1, source_target_pairs={{0,4},{1,5},{2,6},{3,7},{4,12},{5,13},{6,14},{7,15},{12,8},{13,9},... | collective-permute-start | bytes 3145736 | tf_op jit(solution)/shard_map/ppermute | solution.py:52
  82.5 8.4 %collective-permute-start.12 = (bf16[4,32,1024]{2,1,0:T(8,128)(2,1)S(1)}, bf16[4,32,1024]{2,1,0:T(8,128)(2,1)S(1)}, u32[]{:S(2)}, u32[]{:S(2)}) collective-permute-start(bf16[4,32,1024]{2,1,0:T(8,128)(2,1)S(1)} %get-tuple-element.73), channel_id=1, source_target_pairs={{0,2},{1,3},{2,0},{3,1},{4,6},{5,7},{6,4},{7,5},{8,10},{9,11},{10,... | collective-permute-start | bytes 786440 | tf_op jit(solution)/shard_map/ppermute | solution.py:49
  91.0 14.5 %collective-permute-start.13 = (bf16[256,1024]{1,0:T(8,128)(2,1)S(1)}, bf16[256,1024]{1,0:T(8,128)(2,1)S(1)}, u32[]{:S(2)}, u32[]{:S(2)}) collective-permute-start(bf16[256,1024]{1,0:T(8,128)(2,1)S(1)} %get-tuple-element.75), channel_id=1, source_target_pairs={{0,2},{1,3},{2,0},{3,1},{4,6},{5,7},{6,4},{7,5},{8,10},{9,11},{10,... | collective-permute-start | bytes 1572872 | tf_op jit(solution)/shard_map/ppermute | solution.py:49
  105.5 15.3 %collective-permute-start.21 = (bf16[512,1024]{1,0:T(8,128)(2,1)S(1)}, bf16[512,1024]{1,0:T(8,128)(2,1)S(1)}, u32[]{:S(2)}, u32[]{:S(2)}) collective-permute-start(bf16[512,1024]{1,0:T(8,128)(2,1)S(1)} %collective-permute-done.9.refs_0_), channel_id=1, source_target_pairs={{0,1},{1,0},{2,3},{3,2},{4,5},{5,4},{6,7},{7,6},{8,9},{9,8},{10,11... | collective-permute-start | bytes 3145736 | tf_op jit(solution)/shard_map/ppermute | solution.py:49
  105.5 17.4 %collective-permute-start.22 = (bf16[256,1024]{1,0:T(8,128)(2,1)S(1)}, bf16[256,1024]{1,0:T(8,128)(2,1)S(1)}, u32[]{:S(2)}, u32[]{:S(2)}) collective-permute-start(bf16[256,1024]{1,0:T(8,128)(2,1)S(1)} %get-tuple-element.89), channel_id=1, source_target_pairs={{0,2},{1,3},{2,0},{3,1},{4,6},{5,7},{6,4},{7,5},{8,10},{9,11},{10,... | collective-permute-start | bytes 1572872 | tf_op jit(solution)/shard_map/ppermute | solution.py:49
  107.1 6.8 %collective-permute-start.16 = (bf16[1,32,1024]{2,1,0:T(8,128)(2,1)S(1)}, bf16[1,32,1024]{2,1,0:T(8,128)(2,1)S(1)}, u32[]{:S(2)}, u32[]{:S(2)}) collective-permute-start(bf16[1,32,1024]{2,1,0:T(8,128)(2,1)S(1)} %get-tuple-element.82), channel_id=1, source_target_pairs={{0,12},{1,13},{2,14},{3,15},{4,8},{5,9},{6,10},{7,11},{8,4},{9,5},... | collective-permute-start | bytes 196616 | tf_op jit(solution)/shard_map/ppermute | solution.py:49
  110.3 5.8 %collective-permute-start.15 = (bf16[1,32,1024]{2,1,0:T(8,128)(2,1)S(1)}, bf16[1,32,1024]{2,1,0:T(8,128)(2,1)S(1)}, u32[]{:S(2)}, u32[]{:S(2)}) collective-permute-start(bf16[1,32,1024]{2,1,0:T(8,128)(2,1)S(1)} %get-tuple-element.80), channel_id=1, source_target_pairs={{0,8},{1,9},{2,10},{3,11},{4,12},{5,13},{6,14},{7,15},{8,0},{9,1},... | collective-permute-start | bytes 196616 | tf_op jit(solution)/shard_map/ppermute | solution.py:49
  110.3 5.9 %collective-permute-start.14 = (bf16[1,32,1024]{2,1,0:T(8,128)(2,1)S(1)}, bf16[1,32,1024]{2,1,0:T(8,128)(2,1)S(1)}, u32[]{:S(2)}, u32[]{:S(2)}) collective-permute-start(bf16[1,32,1024]{2,1,0:T(8,128)(2,1)S(1)} %get-tuple-element.78), channel_id=1, source_target_pairs={{0,4},{1,5},{2,6},{3,7},{4,0},{5,1},{6,2},{7,3},{8,12},{9,13},{10,... | collective-permute-start | bytes 196616 | tf_op jit(solution)/shard_map/ppermute | solution.py:49
  116.3 7.4 %collective-permute-start.17 = (bf16[1,48,1024]{2,1,0:T(8,128)(2,1)S(1)}, bf16[1,48,1024]{2,1,0:T(8,128)(2,1)S(1)}, u32[]{:S(2)}, u32[]{:S(2)}) collective-permute-start(bf16[1,48,1024]{2,1,0:T(8,128)(2,1)S(1)} %get-tuple-element.83), channel_id=1, source_target_pairs={{0,4},{1,5},{2,6},{3,7},{4,0},{5,1},{6,2},{7,3},{8,12},{9,13},{10,... | collective-permute-start | bytes 294920 | tf_op jit(solution)/shard_map/ppermute | solution.py:49
  117.6 10.0 %collective-permute-start.18 = (bf16[1,48,1024]{2,1,0:T(8,128)(2,1)S(1)}, bf16[1,48,1024]{2,1,0:T(8,128)(2,1)S(1)}, u32[]{:S(2)}, u32[]{:S(2)}) collective-permute-start(bf16[1,48,1024]{2,1,0:T(8,128)(2,1)S(1)} %get-tuple-element.83), channel_id=1, source_target_pairs={{0,8},{1,9},{2,10},{3,11},{4,12},{5,13},{6,14},{7,15},{8,0},{9,1},... | collective-permute-start | bytes 294920 | tf_op jit(solution)/shard_map/ppermute | solution.py:49
  119.4 8.2 %collective-permute-start.19 = (bf16[1,48,1024]{2,1,0:T(8,128)(2,1)S(1)}, bf16[1,48,1024]{2,1,0:T(8,128)(2,1)S(1)}, u32[]{:S(2)}, u32[]{:S(2)}) collective-permute-start(bf16[1,48,1024]{2,1,0:T(8,128)(2,1)S(1)} %get-tuple-element.83), channel_id=1, source_target_pairs={{0,12},{1,13},{2,14},{3,15},{4,8},{5,9},{6,10},{7,11},{8,4},{9,5},... | collective-permute-start | bytes 294920 | tf_op jit(solution)/shard_map/ppermute | solution.py:49
  122.9 12.8 %collective-permute-start.23 = (bf16[256,1024]{1,0:T(8,128)(2,1)S(1)}, bf16[256,1024]{1,0:T(8,128)(2,1)S(1)}, u32[]{:S(2)}, u32[]{:S(2)}) collective-permute-start(bf16[256,1024]{1,0:T(8,128)(2,1)S(1)} %get-tuple-element.90), channel_id=1, source_target_pairs={{0,2},{1,3},{2,0},{3,1},{4,6},{5,7},{6,4},{7,5},{8,10},{9,11},{10,... | collective-permute-start | bytes 1572872 | tf_op jit(solution)/shard_map/ppermute | solution.py:49
  127.6 12.9 %collective-permute-start.20 = (bf16[256,1024]{1,0:T(8,128)(2,1)S(1)}, bf16[256,1024]{1,0:T(8,128)(2,1)S(1)}, u32[]{:S(2)}, u32[]{:S(2)}) collective-permute-start(bf16[256,1024]{1,0:T(8,128)(2,1)S(1)} %get-tuple-element.84), channel_id=1, source_target_pairs={{0,4},{1,5},{2,6},{3,7},{4,12},{5,13},{6,14},{7,15},{12,8},{13,9},... | collective-permute-start | bytes 1572872 | tf_op jit(solution)/shard_map/ppermute | solution.py:52
  135.8 1.9 %collective-permute-start.24 = (f32[8,128]{1,0:T(8,128)S(1)}, f32[8,128]{1,0:T(8,128)S(1)}, u32[]{:S(2)}, u32[]{:S(2)}) collective-permute-start(f32[8,128]{1,0:T(8,128)S(1)} %gathered.1.refs_0_), channel_id=1, source_target_pairs={{0,1},{1,0},{2,3},{3,2},{4,5},{5,4},{6,7},{7,6},{8,9},{9,8},{10,11... | collective-permute-start | bytes 12296 | tf_op jit(solution)/shard_map/ppermute | solution.py:49
  135.8 3.6 %collective-permute-start.25 = (f32[8,128]{1,0:T(8,128)S(1)}, f32[8,128]{1,0:T(8,128)S(1)}, u32[]{:S(2)}, u32[]{:S(2)}) collective-permute-start(f32[8,128]{1,0:T(8,128)S(1)} %gathered.1.refs_0_), channel_id=1, source_target_pairs={{0,2},{1,3},{2,0},{3,1},{4,6},{5,7},{6,4},{7,5},{8,10},{9,11},{10,... | collective-permute-start | bytes 12296 | tf_op jit(solution)/shard_map/ppermute | solution.py:49
  136.1 3.3 %collective-permute-start.26 = (f32[8,128]{1,0:T(8,128)S(1)}, f32[8,128]{1,0:T(8,128)S(1)}, u32[]{:S(2)}, u32[]{:S(2)}) collective-permute-start(f32[8,128]{1,0:T(8,128)S(1)} %gathered.1.refs_0_), channel_id=1, source_target_pairs={{0,3},{1,2},{2,1},{3,0},{4,7},{5,6},{6,5},{7,4},{8,11},{9,10},{10,... | collective-permute-start | bytes 12296 | tf_op jit(solution)/shard_map/ppermute | solution.py:49
  140.5 8.7 %collective-permute-start.27 = (bf16[256,1024]{1,0:T(8,128)(2,1)S(1)}, bf16[256,1024]{1,0:T(8,128)(2,1)S(1)}, u32[]{:S(2)}, u32[]{:S(2)}) collective-permute-start(bf16[256,1024]{1,0:T(8,128)(2,1)S(1)} %collective-permute-done.20.refs_0_), channel_id=1, source_target_pairs={{0,1},{1,0},{2,3},{3,2},{4,5},{5,4},{6,7},{7,6},{8,9},{9,8},{10,11... | collective-permute-start | bytes 1572872 | tf_op jit(solution)/shard_map/ppermute | solution.py:49
  140.8 8.5 %collective-permute-start.28 = (bf16[4,32,1024]{2,1,0:T(8,128)(2,1)S(1)}, bf16[4,32,1024]{2,1,0:T(8,128)(2,1)S(1)}, u32[]{:S(2)}, u32[]{:S(2)}) collective-permute-start(bf16[4,32,1024]{2,1,0:T(8,128)(2,1)S(1)} %get-tuple-element.92), channel_id=1, source_target_pairs={{0,2},{1,3},{2,0},{3,1},{4,6},{5,7},{6,4},{7,5},{8,10},{9,11},{10,... | collective-permute-start | bytes 786440 | tf_op jit(solution)/shard_map/ppermute | solution.py:49
  142.5 14.5 %collective-permute-start.31 = (bf16[256,1024]{1,0:T(8,128)(2,1)S(1)}, bf16[256,1024]{1,0:T(8,128)(2,1)S(1)}, u32[]{:S(2)}, u32[]{:S(2)}) collective-permute-start(bf16[256,1024]{1,0:T(8,128)(2,1)S(1)} %get-tuple-element.98), channel_id=1, source_target_pairs={{0,4},{1,5},{2,6},{3,7},{4,12},{5,13},{6,14},{7,15},{12,8},{13,9},... | collective-permute-start | bytes 1572872 | tf_op jit(solution)/shard_map/ppermute | solution.py:52
  150.8 7.7 %collective-permute-start.29 = (bf16[256,512]{1,0:T(8,128)(2,1)S(1)}, bf16[256,512]{1,0:T(8,128)(2,1)S(1)}, u32[]{:S(2)}, u32[]{:S(2)}) collective-permute-start(bf16[256,512]{1,0:T(8,128)(2,1)S(1)} %get-tuple-element.96), channel_id=1, source_target_pairs={{0,2},{1,3},{2,0},{3,1},{4,6},{5,7},{6,4},{7,5},{8,10},{9,11},{10,... | collective-permute-start | bytes 786440 | tf_op jit(solution)/shard_map/ppermute | solution.py:49
  158.5 1.9 %collective-permute-start.32 = (bf16[256,1024]{1,0:T(8,128)(2,1)S(1)}, bf16[256,1024]{1,0:T(8,128)(2,1)S(1)}, u32[]{:S(2)}, u32[]{:S(2)}) collective-permute-start(bf16[256,1024]{1,0:T(8,128)(2,1)S(1)} %collective-permute-done.31.refs_0_), channel_id=1, source_target_pairs={{0,1},{1,0},{2,3},{3,2},{4,5},{5,4},{6,7},{7,6},{8,9},{9,8},{10,11... | collective-permute-start | bytes 1572872 | tf_op jit(solution)/shard_map/ppermute | solution.py:49
  158.5 4.7 %collective-permute-start.30 = (bf16[8,32,1024]{2,1,0:T(8,128)(2,1)S(1)}, bf16[8,32,1024]{2,1,0:T(8,128)(2,1)S(1)}, u32[]{:S(2)}, u32[]{:S(2)}) collective-permute-start(bf16[8,32,1024]{2,1,0:T(8,128)(2,1)S(1)} %constant_dynamic-update-slice_fusion.4.near), channel_id=1, source_target_pairs={{0,1},{1,0},{2,3},{3,2},{4,5},{5,4},{6,7},{7,6},{8,9},{9,8},{10,11... | collective-permute-start | bytes 1572872 | tf_op jit(solution)/shard_map/ppermute | solution.py:49
  161.9 8.4 %collective-permute-start.33 = (bf16[256,512]{1,0:T(8,128)(2,1)S(1)}, bf16[256,512]{1,0:T(8,128)(2,1)S(1)}, u32[]{:S(2)}, u32[]{:S(2)}) collective-permute-start(bf16[256,512]{1,0:T(8,128)(2,1)S(1)} %get-tuple-element.101), channel_id=1, source_target_pairs={{0,2},{1,3},{2,0},{3,1},{4,6},{5,7},{6,4},{7,5},{8,10},{9,11},{10,... | collective-permute-start | bytes 786440 | tf_op jit(solution)/shard_map/ppermute | solution.py:49

commit v15 on v14

--- a/solution.py
+++ b/solution.py
@@ -470,25 +470,28 @@
 
         split = [weight[2][p * height : (p + 1) * height] for p in range(parts)] if ring == 4 else []
         last = [onward(after(piece, *came)) for piece in split[:1]]
-        block = multiply(2, weight[2], their_step, gate=owned_rows)
+        block = multiply(2, weight[2], their_step, gate=gives[0])
         (square,) = call(gathered_kernel, "gathered", [((8, 128), f32)], [messages])
+        last += [onward(after(piece, square)) for piece in split[1:]]
         if sides == 2:
             sent = give_back(2, block, gate=later)
             square = after(square, sent)
         squares = [square] + [swap(square, x) for x in range(1, members)]
-        last += [onward(after(piece, square)) for piece in split[1:]]
         new_first, new_second, update = call(
             functools.partial(moment_kernel, lay, rows),
             "moment",
             [((owned, outs), f32), ((owned, outs), f32), ((ring, owned, outs), bf16)],
             squares + basis + [owned_rows, first_moment, second_moment, messages],
         )
+        if split:
+            piece = after(last[0], update)
+            block = multiply(3, piece, swap(piece, 1))
         whole = update
         for bit, radix in reversed(rounds[1:]):
             if bit < members:
-                whole = jnp.concatenate(
-                    [whole] + [swap(whole, j * bit) for j in range(1, radix)], axis=0
-                )
+                whole = jnp.concatenate([whole, after(swap(whole, bit), block)], axis=0)
+        if split:
+            sent = give_back(3, block, 0, whole)
         (new_master,) = call(
             functools.partial(back_kernel, lay, owned),
             "back",
@@ -499,10 +502,10 @@
             moved=8 * 2**20,
         )
 
-        for p in range(len(split)):
-            piece = after(last[p], update if p == 0 else sent)
+        for p in range(1, len(split)):
+            piece = after(last[p], sent)
             block = multiply(3, piece, swap(piece, 1), p * height)
-            sent = give_back(3, block, p * height, whole if p == 0 else None)
+            sent = give_back(3, block, p * height)
         if not split:
             for s in range(3, ring):
                 weight.append(onward(weight[s - 1]))

time: 171 us -> 171 us (level)
  starting transfers between devices: 34.5 us -> 31 us
  waiting for transfers between devices: 113 us -> 116 us
    ppermute x7, waiting for transfers between devices: 67.2 us -> 69.6 us  [onward(): return lax.ppermute(value, 'dp', self.forward)]
    ppermute x27, starting transfers between devices: 27.4 us -> 25.5 us  [swap(): return lax.ppermute(value, 'dp', [(i, i ^ bit) for i in range(self.n)])]
  transfers between devices with their start and end apart: 34 -> 34, of which waited for: 20 -> 22; matrix products, arithmetic and copies ran while one was open for 0% -> 0% of each run, Pallas kernels for 10% -> 10%
where the time goes in v15:
time: 171 us; the launch traced here: 170 us
  waiting for transfers between devices  116 us (68%)
  starting transfers between devices  31 us (18%)
  Pallas kernels  18.9 us (11%)
  local copies, waits for them, and re-layouts  3.49 us (2%)
    ppermute x7, waiting for transfers between devices, onward(): return lax.ppermute(value, 'dp', self.forward)  69.6 us
    ppermute x27, waiting for transfers between devices, swap(): return lax.ppermute(value, 'dp', [(i, i ^ bit) for i in range(self.n)])  46.3 us
    ppermute x27, starting transfers between devices, swap(): return lax.ppermute(value, 'dp', [(i, i ^ bit) for i in range(self.n)])  25.5 us
    pallas_call x14, Pallas kernels, call(): pl.pallas_call(kernel, name=name, out_shape=[jax.ShapeDtypeStruct(shape,...  18.9 us
    ppermute x7, starting transfers between devices, onward(): return lax.ppermute(value, 'dp', self.forward)  5.44 us
  transfers between devices with their start and end apart: 34, of which 22 were waited for; matrix products, arithmetic and copies ran while one was open for 0% of the time, Pallas kernels for 10%

profile of v15, /device:TPU:0, one launch (start us, length us, event | category | flops | bytes accessed | tf_op | source)
XLA Modules:
  0.0 170.5 jit_solution(70269720432617822)
XLA Ops:
  0.6 1.0 copy-done
  1.7 2.2 %copy-done.3 = bf16[256,8192]{1,0:T(8,128)(2,1)S(1)} copy-done((bf16[256,8192]{1,0:T(8,128)(2,1)S(1)}, bf16[256,8192]{1,0:T(8,128)(2,1)}, u32[]{:S(2)}) %copy-start.3) | copy-done | bytes 4194328
  4.5 3.0 %collective-permute-start.5 = (bf16[256,3072]{1,0:T(8,128)(2,1)S(1)}, bf16[256,3072]{1,0:T(8,128)(2,1)S(1)}, u32[]{:S(2)}, u32[]{:S(2)}) collective-permute-start(bf16[256,3072]{1,0:T(8,128)(2,1)S(1)} %get-tuple-element.60), channel_id=1, source_target_pairs={{0,2},{1,3},{2,0},{3,1},{4,6},{5,7},{6,4},{7,5},{8,10},{9,11},{10,... | collective-permute-start | bytes 4718600 | tf_op jit(solution)/shard_map/ppermute | solution.py:49
  7.7 1.6 collective-permute-start
  9.3 15.5 %collective-permute-done.refs_5_ = bf16[640,512]{1,0:T(8,128)(2,1)S(1)} collective-permute-done((bf16[640,512]{1,0:T(8,128)(2,1)S(1)}, bf16[640,512]{1,0:T(8,128)(2,1)S(1)}, u32[]{:S(2)}, u32[]{:S(2)}) %collective-permute-start) | collective-permute-done | bytes 655392 | tf_op jit(solution)/shard_map/ppermute | solution.py:52
  24.8 0.8 collective-permute-start.1
  25.9 15.1 %collective-permute-done.1.refs_6_ = bf16[640,512]{1,0:T(8,128)(2,1)S(1)} collective-permute-done((bf16[640,512]{1,0:T(8,128)(2,1)S(1)}, bf16[640,512]{1,0:T(8,128)(2,1)S(1)}, u32[]{:S(2)}, u32[]{:S(2)}) %collective-permute-start.1) | collective-permute-done | bytes 655392 | tf_op jit(solution)/shard_map/ppermute | solution.py:52
  41.0 0.8 collective-permute-start.2
  42.7 1.4 collective-permute-start.7
  44.1 12.2 %collective-permute-done.2.refs_7_ = bf16[640,512]{1,0:T(8,128)(2,1)S(1)} collective-permute-done((bf16[640,512]{1,0:T(8,128)(2,1)S(1)}, bf16[640,512]{1,0:T(8,128)(2,1)S(1)}, u32[]{:S(2)}, u32[]{:S(2)}) %collective-permute-start.2) | collective-permute-done | bytes 655392 | tf_op jit(solution)/shard_map/ppermute | solution.py:52
  56.3 0.8 collective-permute-start.3
  57.1 2.1 %weight.5 = (bf16[256,8192]{1,0:T(8,128)(2,1)}, bf16[256,1024]{1,0:T(8,128)(2,1)S(1)}) custom-call(bf16[512,1024]{1,0:T(8,128)(2,1)S(1)} %convert_element_type.4.refs_0_, bf16[512,1024]{1,0:T(8,128)(2,1)S(1)} %collective-permute-done.4.refs_1_, bf16[256,1024]{1,0:T(8,128)(2,1)S(1)} %copy-done, bf16[256,1024]{1,0:T(8,128)(2,1)S(1)} %slice.23.refs_3_.refs_10_), custom_call_target="tpu_custom_call" | custom-call | flops 1073741824 | bytes 6291456 | tf_op jit(solution)/shard_map/weight/pallas_call | solution.py:318
  59.3 8.6 %collective-permute-done.7.refs_3_ = bf16[256,2048]{1,0:T(8,128)(2,1)S(1)} collective-permute-done((bf16[256,2048]{1,0:T(8,128)(2,1)S(1)}, bf16[256,2048]{1,0:T(8,128)(2,1)S(1)}, u32[]{:S(2)}, u32[]{:S(2)}) %collective-permute-start.7) | collective-permute-done | bytes 1048608 | tf_op jit(solution)/shard_map/ppermute | solution.py:49
  67.8 4.3 %project.1 = (f32[8,32,1024]{2,1,0:T(8,128)S(1)}, bf16[8,32,1024]{2,1,0:T(8,128)(2,1)S(1)}) custom-call(bf16[256,2048]{1,0:T(8,128)(2,1)S(1)} %get-tuple-element.63.refs_0_, bf16[256,2048]{1,0:T(8,128)(2,1)S(1)} %collective-permute-done.6.refs_1_, bf16[256,3072]{1,0:T(8,128)(2,1)S(1)} %collective-permute-done.5.refs_2_, ...), custom_call_target="tpu_custom_call" | custom-call | flops 3221225472 | bytes 12582912 | tf_op jit(solution)/shard_map/project/pallas_call | solution.py:318
  72.2 6.9 %collective-permute-done.3.refs_0_ = bf16[512,1024]{1,0:T(8,128)(2,1)S(1)} collective-permute-done((bf16[512,1024]{1,0:T(8,128)(2,1)S(1)}, bf16[512,1024]{1,0:T(8,128)(2,1)S(1)}, u32[]{:S(2)}, u32[]{:S(2)}) %collective-permute-start.3) | collective-permute-done | bytes 1048608 | tf_op jit(solution)/shard_map/ppermute | solution.py:52
  80.3 2.1 %collective-permute-done.10.refs_1_ = bf16[8,32,1024]{2,1,0:T(8,128)(2,1)S(1)} collective-permute-done((bf16[8,32,1024]{2,1,0:T(8,128)(2,1)S(1)}, bf16[8,32,1024]{2,1,0:T(8,128)(2,1)S(1)}, u32[]{:S(2)}, u32[]{:S(2)}) %collective-permute-start.10) | collective-permute-done | bytes 524320 | tf_op jit(solution)/shard_map/ppermute | solution.py:49
  82.5 1.7 collective-permute-start.12
  84.2 2.1 %weight.6 = (bf16[256,8192]{1,0:T(8,128)(2,1)}, bf16[256,1024]{1,0:T(8,128)(2,1)S(1)}) custom-call(bf16[512,1024]{1,0:T(8,128)(2,1)S(1)} %collective-permute-done.3.refs_0_, bf16[512,1024]{1,0:T(8,128)(2,1)S(1)} %collective-permute-done.11.refs_1_, bf16[256,1024]{1,0:T(8,128)(2,1)S(1)} %copy-done.1, ...), custom_call_target="tpu_custom_call", output_to_operand_aliasing={{0}: (4, {})} | custom-call | flops 1073741824 | bytes 6291456 | tf_op jit(solution)/shard_map/weight/pallas_call | solution.py:318
  86.3 4.6 %collective-permute-done.12.refs_1_ = bf16[4,32,1024]{2,1,0:T(8,128)(2,1)S(1)} collective-permute-done((bf16[4,32,1024]{2,1,0:T(8,128)(2,1)S(1)}, bf16[4,32,1024]{2,1,0:T(8,128)(2,1)S(1)}, u32[]{:S(2)}, u32[]{:S(2)}) %collective-permute-start.12) | collective-permute-done | bytes 262176 | tf_op jit(solution)/shard_map/ppermute | solution.py:49
  91.0 1.7 collective-permute-start.13
  92.7 12.8 %collective-permute-done.9.refs_0_ = bf16[512,1024]{1,0:T(8,128)(2,1)S(1)} collective-permute-done((bf16[512,1024]{1,0:T(8,128)(2,1)S(1)}, bf16[512,1024]{1,0:T(8,128)(2,1)S(1)}, u32[]{:S(2)}, u32[]{:S(2)}) %collective-permute-start.9) | collective-permute-done | bytes 1048608 | tf_op jit(solution)/shard_map/ppermute | solution.py:52
  105.5 1.6 collective-permute-start.22
  107.4 3.4 %collective-permute-start.15 = (bf16[1,32,1024]{2,1,0:T(8,128)(2,1)S(1)}, bf16[1,32,1024]{2,1,0:T(8,128)(2,1)S(1)}, u32[]{:S(2)}, u32[]{:S(2)}) collective-permute-start(bf16[1,32,1024]{2,1,0:T(8,128)(2,1)S(1)} %get-tuple-element.81), channel_id=1, source_target_pairs={{0,8},{1,9},{2,10},{3,11},{4,12},{5,13},{6,14},{7,15},{8,0},{9,1},... | collective-permute-start | bytes 196616 | tf_op jit(solution)/shard_map/ppermute | solution.py:49
  111.5 3.4 %collective-permute-done.15.refs_2_ = bf16[1,32,1024]{2,1,0:T(8,128)(2,1)S(1)} collective-permute-done((bf16[1,32,1024]{2,1,0:T(8,128)(2,1)S(1)}, bf16[1,32,1024]{2,1,0:T(8,128)(2,1)S(1)}, u32[]{:S(2)}, u32[]{:S(2)}) %collective-permute-start.15) | collective-permute-done | bytes 65568 | tf_op jit(solution)/shard_map/ppermute | solution.py:49
  115.0 2.0 %collective-permute-done.16.refs_3_ = bf16[1,32,1024]{2,1,0:T(8,128)(2,1)S(1)} collective-permute-done((bf16[1,32,1024]{2,1,0:T(8,128)(2,1)S(1)}, bf16[1,32,1024]{2,1,0:T(8,128)(2,1)S(1)}, u32[]{:S(2)}, u32[]{:S(2)}) %collective-permute-start.16) | collective-permute-done | bytes 65568 | tf_op jit(solution)/shard_map/ppermute | solution.py:49
  117.2 2.0 %collective-permute-start.19 = (bf16[1,48,1024]{2,1,0:T(8,128)(2,1)S(1)}, bf16[1,48,1024]{2,1,0:T(8,128)(2,1)S(1)}, u32[]{:S(2)}, u32[]{:S(2)}) collective-permute-start(bf16[1,48,1024]{2,1,0:T(8,128)(2,1)S(1)} %get-tuple-element.84), channel_id=1, source_target_pairs={{0,12},{1,13},{2,14},{3,15},{4,8},{5,9},{6,10},{7,11},{8,4},{9,5},... | collective-permute-start | bytes 294920 | tf_op jit(solution)/shard_map/ppermute | solution.py:49
  119.6 2.1 %collective-permute-start.17 = (bf16[1,48,1024]{2,1,0:T(8,128)(2,1)S(1)}, bf16[1,48,1024]{2,1,0:T(8,128)(2,1)S(1)}, u32[]{:S(2)}, u32[]{:S(2)}) collective-permute-start(bf16[1,48,1024]{2,1,0:T(8,128)(2,1)S(1)} %get-tuple-element.84), channel_id=1, source_target_pairs={{0,4},{1,5},{2,6},{3,7},{4,0},{5,1},{6,2},{7,3},{8,12},{9,13},{10,... | collective-permute-start | bytes 294920 | tf_op jit(solution)/shard_map/ppermute | solution.py:49
  121.6 2.1 %weight.7 = (bf16[256,8192]{1,0:T(8,128)(2,1)}, bf16[256,1024]{1,0:T(8,128)(2,1)S(1)}) custom-call(bf16[512,1024]{1,0:T(8,128)(2,1)S(1)} %collective-permute-done.9.refs_0_, bf16[512,1024]{1,0:T(8,128)(2,1)S(1)} %collective-permute-done.21.refs_1_, bf16[256,1024]{1,0:T(8,128)(2,1)S(1)} %copy-done.1, ...), custom_call_target="tpu_custom_call", output_to_operand_aliasing={{0}: (5, {})} | custom-call | flops 1073741824 | bytes 6291456 | tf_op jit(solution)/shard_map/weight/pallas_call | solution.py:318
  123.8 0.9 collective-permute-start.23
  124.8 2.8 %collective-permute-done.18 = bf16[1,48,1024]{2,1,0:T(8,128)(2,1)S(1)} collective-permute-done((bf16[1,48,1024]{2,1,0:T(8,128)(2,1)S(1)}, bf16[1,48,1024]{2,1,0:T(8,128)(2,1)S(1)}, u32[]{:S(2)}, u32[]{:S(2)}) %collective-permute-start.18) | collective-permute-done | bytes 98336 | tf_op jit(solution)/shard_map/ppermute | solution.py:49
  127.8 7.5 %collective-permute-done.23.refs_4_ = bf16[256,1024]{1,0:T(8,128)(2,1)S(1)} collective-permute-done((bf16[256,1024]{1,0:T(8,128)(2,1)S(1)}, bf16[256,1024]{1,0:T(8,128)(2,1)S(1)}, u32[]{:S(2)}, u32[]{:S(2)}) %collective-permute-start.23) | collective-permute-done | bytes 524320 | tf_op jit(solution)/shard_map/ppermute | solution.py:49
  135.4 0.9 collective-permute-start.25
  136.3 0.9 collective-permute-start.24
  137.2 1.2 collective-permute-done.26.refs_3_
  139.0 1.1 moment.1
  140.2 0.9 collective-permute-done.20.refs_0_
  141.1 0.9 collective-permute-start.28
  143.0 1.5 weight.8
  144.5 5.3 %collective-permute-done.28 = bf16[4,32,1024]{2,1,0:T(8,128)(2,1)S(1)} collective-permute-done((bf16[4,32,1024]{2,1,0:T(8,128)(2,1)S(1)}, bf16[4,32,1024]{2,1,0:T(8,128)(2,1)S(1)}, u32[]{:S(2)}, u32[]{:S(2)}) %collective-permute-start.28) | collective-permute-done | bytes 262176 | tf_op jit(solution)/shard_map/ppermute | solution.py:49
  149.8 0.9 collective-permute-start.29
  150.8 6.1 %collective-permute-done.31.refs_0_ = bf16[256,1024]{1,0:T(8,128)(2,1)S(1)} collective-permute-done((bf16[256,1024]{1,0:T(8,128)(2,1)S(1)}, bf16[256,1024]{1,0:T(8,128)(2,1)S(1)}, u32[]{:S(2)}, u32[]{:S(2)}) %collective-permute-start.31) | collective-permute-done | bytes 524320 | tf_op jit(solution)/shard_map/ppermute | solution.py:52
  156.9 0.9 collective-permute-done.29.refs_0_
  158.3 1.4 collective-permute-done.32.refs_1_
  159.7 1.5 weight.9
  161.2 0.9 collective-permute-start.33
  162.2 2.2 %back.1 = f32[512,1024]{1,0:T(8,128)} custom-call(bf16[512,512]{1,0:T(8,128)(2,1)S(1)} %copy-done.4, bf16[8,32,1024]{2,1,0:T(8,128)(2,1)S(1)} %constant_dynamic-update-slice_fusion.4.near, bf16[8,32,1024]{2,1,0:T(8,128)(2,1)S(1)} %collective-permute-done.30.other, f32[512,1024]{1,0:T(8,128)S(1)} %copy-done.2), custom_call_target="tpu_custom_call" | custom-call | flops 536870912 | bytes 8388608 | tf_op jit(solution)/shard_map/back/pallas_call | solution.py:318
  164.4 5.3 %collective-permute-done.33.refs_1_ = bf16[256,512]{1,0:T(8,128)(2,1)S(1)} collective-permute-done((bf16[256,512]{1,0:T(8,128)(2,1)S(1)}, bf16[256,512]{1,0:T(8,128)(2,1)S(1)}, u32[]{:S(2)}, u32[]{:S(2)}) %collective-permute-start.33) | collective-permute-done | bytes 262176 | tf_op jit(solution)/shard_map/ppermute | solution.py:49
  169.7 0.8 last.1
  (63 shorter events, 7.4 us)
Async XLA Ops:
  0.6 1.0 copy-start
  1.7 2.2 %copy-start.3 = (bf16[256,8192]{1,0:T(8,128)(2,1)S(1)}, bf16[256,8192]{1,0:T(8,128)(2,1)}, u32[]{:S(2)}) copy-start(bf16[256,8192]{1,0:T(8,128)(2,1)} %act.1) | copy-start | bytes 12582916
  3.9 3.7 %copy-start.6 = (f32[32,1024]{1,0:T(8,128)S(1)}, f32[32,1024]{1,0:T(8,128)}, u32[]{:S(2)}) copy-start(f32[32,1024]{1,0:T(8,128)} %refs_9_.1) | copy-start | bytes 393220
  3.9 3.7 %copy-start.5 = (f32[32,1024]{1,0:T(8,128)S(1)}, f32[32,1024]{1,0:T(8,128)}, u32[]{:S(2)}) copy-start(f32[32,1024]{1,0:T(8,128)} %refs_10_.1) | copy-start | bytes 393220
  3.9 3.8 %copy-start.4 = (bf16[512,512]{1,0:T(8,128)(2,1)S(1)}, bf16[512,512]{1,0:T(8,128)(2,1)}, u32[]{:S(2)}) copy-start(bf16[512,512]{1,0:T(8,128)(2,1)} %basis.1) | copy-start | bytes 1572868
  3.9 21.7 %copy-start.2 = (f32[512,1024]{1,0:T(8,128)S(1)}, f32[512,1024]{1,0:T(8,128)}, u32[]{:S(2)}) copy-start(f32[512,1024]{1,0:T(8,128)} %master.1) | copy-start | bytes 6291460
  4.5 37.4 %collective-permute-start.5 = (bf16[256,3072]{1,0:T(8,128)(2,1)S(1)}, bf16[256,3072]{1,0:T(8,128)(2,1)S(1)}, u32[]{:S(2)}, u32[]{:S(2)}) collective-permute-start(bf16[256,3072]{1,0:T(8,128)(2,1)S(1)} %get-tuple-element.60), channel_id=1, source_target_pairs={{0,2},{1,3},{2,0},{3,1},{4,6},{5,7},{6,4},{7,5},{8,10},{9,11},{10,... | collective-permute-start | bytes 4718600 | tf_op jit(solution)/shard_map/ppermute | solution.py:49
  7.7 17.1 %collective-permute-start = (bf16[640,512]{1,0:T(8,128)(2,1)S(1)}, bf16[640,512]{1,0:T(8,128)(2,1)S(1)}, u32[]{:S(2)}, u32[]{:S(2)}) collective-permute-start(bf16[640,512]{1,0:T(8,128)(2,1)S(1)} %fusion.refs_4_), channel_id=1, source_target_pairs={{0,4},{1,5},{2,6},{3,7},{4,12},{5,13},{6,14},{7,15},{12,8},{13,9},... | collective-permute-start | bytes 1966088 | tf_op jit(solution)/shard_map/ppermute | solution.py:52
  24.8 16.2 %collective-permute-start.1 = (bf16[640,512]{1,0:T(8,128)(2,1)S(1)}, bf16[640,512]{1,0:T(8,128)(2,1)S(1)}, u32[]{:S(2)}, u32[]{:S(2)}) collective-permute-start(bf16[640,512]{1,0:T(8,128)(2,1)S(1)} %collective-permute-done.refs_5_), channel_id=1, source_target_pairs={{0,4},{1,5},{2,6},{3,7},{4,12},{5,13},{6,14},{7,15},{12,8},{13,9},... | collective-permute-start | bytes 1966088 | tf_op jit(solution)/shard_map/ppermute | solution.py:52
  25.8 31.3 %collective-permute-start.4 = (bf16[512,1024]{1,0:T(8,128)(2,1)S(1)}, bf16[512,1024]{1,0:T(8,128)(2,1)S(1)}, u32[]{:S(2)}, u32[]{:S(2)}) collective-permute-start(bf16[512,1024]{1,0:T(8,128)(2,1)S(1)} %convert_element_type.4.refs_0_), channel_id=1, source_target_pairs={{0,1},{1,0},{2,3},{3,2},{4,5},{5,4},{6,7},{7,6},{8,9},{9,8},{10,11... | collective-permute-start | bytes 3145736 | tf_op jit(solution)/shard_map/ppermute | solution.py:49
  41.0 15.3 %collective-permute-start.2 = (bf16[640,512]{1,0:T(8,128)(2,1)S(1)}, bf16[640,512]{1,0:T(8,128)(2,1)S(1)}, u32[]{:S(2)}, u32[]{:S(2)}) collective-permute-start(bf16[640,512]{1,0:T(8,128)(2,1)S(1)} %collective-permute-done.1.refs_6_), channel_id=1, source_target_pairs={{0,4},{1,5},{2,6},{3,7},{4,12},{5,13},{6,14},{7,15},{12,8},{13,9},... | collective-permute-start | bytes 1966088 | tf_op jit(solution)/shard_map/ppermute | solution.py:52
  42.1 17.1 %collective-permute-start.8 = (bf16[512,1024]{1,0:T(8,128)(2,1)S(1)}, bf16[512,1024]{1,0:T(8,128)(2,1)S(1)}, u32[]{:S(2)}, u32[]{:S(2)}) collective-permute-start(bf16[512,1024]{1,0:T(8,128)(2,1)S(1)} %pad_maximum_fusion), channel_id=1, source_target_pairs={{0,1},{1,0},{2,3},{3,2},{4,5},{5,4},{6,7},{7,6},{8,9},{9,8},{10,11... | collective-permute-start | bytes 3145736 | tf_op jit(solution)/shard_map/ppermute | solution.py:49
  42.2 17.1 %collective-permute-start.6 = (bf16[256,2048]{1,0:T(8,128)(2,1)S(1)}, bf16[256,2048]{1,0:T(8,128)(2,1)S(1)}, u32[]{:S(2)}, u32[]{:S(2)}) collective-permute-start(bf16[256,2048]{1,0:T(8,128)(2,1)S(1)} %get-tuple-element.64), channel_id=1, source_target_pairs={{0,1},{1,0},{2,3},{3,2},{4,5},{5,4},{6,7},{7,6},{8,9},{9,8},{10,11... | collective-permute-start | bytes 3145736 | tf_op jit(solution)/shard_map/ppermute | solution.py:49
  42.7 25.2 %copy-start.1 = (bf16[256,1024]{1,0:T(8,128)(2,1)S(1)}, bf16[256,1024]{1,0:T(8,128)(2,1)}, u32[]{:S(2)}) copy-start(bf16[256,1024]{1,0:T(8,128)(2,1)} %refs_2_.9) | copy-start | bytes 1572868
  42.7 25.2 %collective-permute-start.7 = (bf16[256,2048]{1,0:T(8,128)(2,1)S(1)}, bf16[256,2048]{1,0:T(8,128)(2,1)S(1)}, u32[]{:S(2)}, u32[]{:S(2)}) collective-permute-start(bf16[256,2048]{1,0:T(8,128)(2,1)S(1)} %get-tuple-element.65), channel_id=1, source_target_pairs={{0,3},{1,2},{2,1},{3,0},{4,7},{5,6},{6,5},{7,4},{8,11},{9,10},{10,... | collective-permute-start | bytes 3145736 | tf_op jit(solution)/shard_map/ppermute | solution.py:49
  56.3 22.8 %collective-permute-start.3 = (bf16[512,1024]{1,0:T(8,128)(2,1)S(1)}, bf16[512,1024]{1,0:T(8,128)(2,1)S(1)}, u32[]{:S(2)}, u32[]{:S(2)}) collective-permute-start(bf16[512,1024]{1,0:T(8,128)(2,1)S(1)} %convert_element_type.4.refs_0_), channel_id=1, source_target_pairs={{0,4},{1,5},{2,6},{3,7},{4,12},{5,13},{6,14},{7,15},{12,8},{13,9},... | collective-permute-start | bytes 3145736 | tf_op jit(solution)/shard_map/ppermute | solution.py:52
  79.0 5.2 %collective-permute-start.11 = (bf16[512,1024]{1,0:T(8,128)(2,1)S(1)}, bf16[512,1024]{1,0:T(8,128)(2,1)S(1)}, u32[]{:S(2)}, u32[]{:S(2)}) collective-permute-start(bf16[512,1024]{1,0:T(8,128)(2,1)S(1)} %collective-permute-done.3.refs_0_), channel_id=1, source_target_pairs={{0,1},{1,0},{2,3},{3,2},{4,5},{5,4},{6,7},{7,6},{8,9},{9,8},{10,11... | collective-permute-start | bytes 3145736 | tf_op jit(solution)/shard_map/ppermute | solution.py:49
  79.0 3.4 %collective-permute-start.10 = (bf16[8,32,1024]{2,1,0:T(8,128)(2,1)S(1)}, bf16[8,32,1024]{2,1,0:T(8,128)(2,1)S(1)}, u32[]{:S(2)}, u32[]{:S(2)}) collective-permute-start(bf16[8,32,1024]{2,1,0:T(8,128)(2,1)S(1)} %get-tuple-element.68), channel_id=1, source_target_pairs={{0,1},{1,0},{2,3},{3,2},{4,5},{5,4},{6,7},{7,6},{8,9},{9,8},{10,11... | collective-permute-start | bytes 1572872 | tf_op jit(solution)/shard_map/ppermute | solution.py:49
  79.5 26.0 %collective-permute-start.9 = (bf16[512,1024]{1,0:T(8,128)(2,1)S(1)}, bf16[512,1024]{1,0:T(8,128)(2,1)S(1)}, u32[]{:S(2)}, u32[]{:S(2)}) collective-permute-start(bf16[512,1024]{1,0:T(8,128)(2,1)S(1)} %collective-permute-done.3.refs_0_), channel_id=1, source_target_pairs={{0,4},{1,5},{2,6},{3,7},{4,12},{5,13},{6,14},{7,15},{12,8},{13,9},... | collective-permute-start | bytes 3145736 | tf_op jit(solution)/shard_map/ppermute | solution.py:52
  82.5 8.4 %collective-permute-start.12 = (bf16[4,32,1024]{2,1,0:T(8,128)(2,1)S(1)}, bf16[4,32,1024]{2,1,0:T(8,128)(2,1)S(1)}, u32[]{:S(2)}, u32[]{:S(2)}) collective-permute-start(bf16[4,32,1024]{2,1,0:T(8,128)(2,1)S(1)} %get-tuple-element.74), channel_id=1, source_target_pairs={{0,2},{1,3},{2,0},{3,1},{4,6},{5,7},{6,4},{7,5},{8,10},{9,11},{10,... | collective-permute-start | bytes 786440 | tf_op jit(solution)/shard_map/ppermute | solution.py:49
  91.0 14.5 %collective-permute-start.13 = (bf16[256,1024]{1,0:T(8,128)(2,1)S(1)}, bf16[256,1024]{1,0:T(8,128)(2,1)S(1)}, u32[]{:S(2)}, u32[]{:S(2)}) collective-permute-start(bf16[256,1024]{1,0:T(8,128)(2,1)S(1)} %get-tuple-element.76), channel_id=1, source_target_pairs={{0,2},{1,3},{2,0},{3,1},{4,6},{5,7},{6,4},{7,5},{8,10},{9,11},{10,... | collective-permute-start | bytes 1572872 | tf_op jit(solution)/shard_map/ppermute | solution.py:49
  105.5 16.1 %collective-permute-start.21 = (bf16[512,1024]{1,0:T(8,128)(2,1)S(1)}, bf16[512,1024]{1,0:T(8,128)(2,1)S(1)}, u32[]{:S(2)}, u32[]{:S(2)}) collective-permute-start(bf16[512,1024]{1,0:T(8,128)(2,1)S(1)} %collective-permute-done.9.refs_0_), channel_id=1, source_target_pairs={{0,1},{1,0},{2,3},{3,2},{4,5},{5,4},{6,7},{7,6},{8,9},{9,8},{10,11... | collective-permute-start | bytes 3145736 | tf_op jit(solution)/shard_map/ppermute | solution.py:49
  105.5 18.3 %collective-permute-start.22 = (bf16[256,1024]{1,0:T(8,128)(2,1)S(1)}, bf16[256,1024]{1,0:T(8,128)(2,1)S(1)}, u32[]{:S(2)}, u32[]{:S(2)}) collective-permute-start(bf16[256,1024]{1,0:T(8,128)(2,1)S(1)} %get-tuple-element.89), channel_id=1, source_target_pairs={{0,2},{1,3},{2,0},{3,1},{4,6},{5,7},{6,4},{7,5},{8,10},{9,11},{10,... | collective-permute-start | bytes 1572872 | tf_op jit(solution)/shard_map/ppermute | solution.py:49
  107.1 4.4 %collective-permute-start.14 = (bf16[1,32,1024]{2,1,0:T(8,128)(2,1)S(1)}, bf16[1,32,1024]{2,1,0:T(8,128)(2,1)S(1)}, u32[]{:S(2)}, u32[]{:S(2)}) collective-permute-start(bf16[1,32,1024]{2,1,0:T(8,128)(2,1)S(1)} %get-tuple-element.79), channel_id=1, source_target_pairs={{0,4},{1,5},{2,6},{3,7},{4,0},{5,1},{6,2},{7,3},{8,12},{9,13},{10,... | collective-permute-start | bytes 196616 | tf_op jit(solution)/shard_map/ppermute | solution.py:49
  107.4 7.5 %collective-permute-start.15 = (bf16[1,32,1024]{2,1,0:T(8,128)(2,1)S(1)}, bf16[1,32,1024]{2,1,0:T(8,128)(2,1)S(1)}, u32[]{:S(2)}, u32[]{:S(2)}) collective-permute-start(bf16[1,32,1024]{2,1,0:T(8,128)(2,1)S(1)} %get-tuple-element.81), channel_id=1, source_target_pairs={{0,8},{1,9},{2,10},{3,11},{4,12},{5,13},{6,14},{7,15},{8,0},{9,1},... | collective-permute-start | bytes 196616 | tf_op jit(solution)/shard_map/ppermute | solution.py:49
  110.8 6.2 %collective-permute-start.16 = (bf16[1,32,1024]{2,1,0:T(8,128)(2,1)S(1)}, bf16[1,32,1024]{2,1,0:T(8,128)(2,1)S(1)}, u32[]{:S(2)}, u32[]{:S(2)}) collective-permute-start(bf16[1,32,1024]{2,1,0:T(8,128)(2,1)S(1)} %get-tuple-element.83), channel_id=1, source_target_pairs={{0,12},{1,13},{2,14},{3,15},{4,8},{5,9},{6,10},{7,11},{8,4},{9,5},... | collective-permute-start | bytes 196616 | tf_op jit(solution)/shard_map/ppermute | solution.py:49
  117.2 7.6 %collective-permute-start.19 = (bf16[1,48,1024]{2,1,0:T(8,128)(2,1)S(1)}, bf16[1,48,1024]{2,1,0:T(8,128)(2,1)S(1)}, u32[]{:S(2)}, u32[]{:S(2)}) collective-permute-start(bf16[1,48,1024]{2,1,0:T(8,128)(2,1)S(1)} %get-tuple-element.84), channel_id=1, source_target_pairs={{0,12},{1,13},{2,14},{3,15},{4,8},{5,9},{6,10},{7,11},{8,4},{9,5},... | collective-permute-start | bytes 294920 | tf_op jit(solution)/shard_map/ppermute | solution.py:49
  119.2 8.5 %collective-permute-start.18 = (bf16[1,48,1024]{2,1,0:T(8,128)(2,1)S(1)}, bf16[1,48,1024]{2,1,0:T(8,128)(2,1)S(1)}, u32[]{:S(2)}, u32[]{:S(2)}) collective-permute-start(bf16[1,48,1024]{2,1,0:T(8,128)(2,1)S(1)} %get-tuple-element.84), channel_id=1, source_target_pairs={{0,8},{1,9},{2,10},{3,11},{4,12},{5,13},{6,14},{7,15},{8,0},{9,1},... | collective-permute-start | bytes 294920 | tf_op jit(solution)/shard_map/ppermute | solution.py:49
  119.6 8.1 %collective-permute-start.17 = (bf16[1,48,1024]{2,1,0:T(8,128)(2,1)S(1)}, bf16[1,48,1024]{2,1,0:T(8,128)(2,1)S(1)}, u32[]{:S(2)}, u32[]{:S(2)}) collective-permute-start(bf16[1,48,1024]{2,1,0:T(8,128)(2,1)S(1)} %get-tuple-element.84), channel_id=1, source_target_pairs={{0,4},{1,5},{2,6},{3,7},{4,0},{5,1},{6,2},{7,3},{8,12},{9,13},{10,... | collective-permute-start | bytes 294920 | tf_op jit(solution)/shard_map/ppermute | solution.py:49
  123.8 11.6 %collective-permute-start.23 = (bf16[256,1024]{1,0:T(8,128)(2,1)S(1)}, bf16[256,1024]{1,0:T(8,128)(2,1)S(1)}, u32[]{:S(2)}, u32[]{:S(2)}) collective-permute-start(bf16[256,1024]{1,0:T(8,128)(2,1)S(1)} %get-tuple-element.90), channel_id=1, source_target_pairs={{0,2},{1,3},{2,0},{3,1},{4,6},{5,7},{6,4},{7,5},{8,10},{9,11},{10,... | collective-permute-start | bytes 1572872 | tf_op jit(solution)/shard_map/ppermute | solution.py:49
  127.6 13.4 %collective-permute-start.20 = (bf16[256,1024]{1,0:T(8,128)(2,1)S(1)}, bf16[256,1024]{1,0:T(8,128)(2,1)S(1)}, u32[]{:S(2)}, u32[]{:S(2)}) collective-permute-start(bf16[256,1024]{1,0:T(8,128)(2,1)S(1)} %get-tuple-element.85), channel_id=1, source_target_pairs={{0,4},{1,5},{2,6},{3,7},{4,12},{5,13},{6,14},{7,15},{12,8},{13,9},... | collective-permute-start | bytes 1572872 | tf_op jit(solution)/shard_map/ppermute | solution.py:52
  135.4 3.0 %collective-permute-start.26 = (f32[8,128]{1,0:T(8,128)S(1)}, f32[8,128]{1,0:T(8,128)S(1)}, u32[]{:S(2)}, u32[]{:S(2)}) collective-permute-start(f32[8,128]{1,0:T(8,128)S(1)} %gathered.1.refs_0_), channel_id=1, source_target_pairs={{0,3},{1,2},{2,1},{3,0},{4,7},{5,6},{6,5},{7,4},{8,11},{9,10},{10,... | collective-permute-start | bytes 12296 | tf_op jit(solution)/shard_map/ppermute | solution.py:49
  135.4 3.7 %collective-permute-start.25 = (f32[8,128]{1,0:T(8,128)S(1)}, f32[8,128]{1,0:T(8,128)S(1)}, u32[]{:S(2)}, u32[]{:S(2)}) collective-permute-start(f32[8,128]{1,0:T(8,128)S(1)} %gathered.1.refs_0_), channel_id=1, source_target_pairs={{0,2},{1,3},{2,0},{3,1},{4,6},{5,7},{6,4},{7,5},{8,10},{9,11},{10,... | collective-permute-start | bytes 12296 | tf_op jit(solution)/shard_map/ppermute | solution.py:49
  136.3 2.8 %collective-permute-start.24 = (f32[8,128]{1,0:T(8,128)S(1)}, f32[8,128]{1,0:T(8,128)S(1)}, u32[]{:S(2)}, u32[]{:S(2)}) collective-permute-start(f32[8,128]{1,0:T(8,128)S(1)} %gathered.1.refs_0_), channel_id=1, source_target_pairs={{0,1},{1,0},{2,3},{3,2},{4,5},{5,4},{6,7},{7,6},{8,9},{9,8},{10,11... | collective-permute-start | bytes 12296 | tf_op jit(solution)/shard_map/ppermute | solution.py:49
  141.1 1.9 %collective-permute-start.27 = (bf16[256,1024]{1,0:T(8,128)(2,1)S(1)}, bf16[256,1024]{1,0:T(8,128)(2,1)S(1)}, u32[]{:S(2)}, u32[]{:S(2)}) collective-permute-start(bf16[256,1024]{1,0:T(8,128)(2,1)S(1)} %collective-permute-done.20.refs_0_), channel_id=1, source_target_pairs={{0,1},{1,0},{2,3},{3,2},{4,5},{5,4},{6,7},{7,6},{8,9},{9,8},{10,11... | collective-permute-start | bytes 1572872 | tf_op jit(solution)/shard_map/ppermute | solution.py:49
  141.1 8.7 %collective-permute-start.28 = (bf16[4,32,1024]{2,1,0:T(8,128)(2,1)S(1)}, bf16[4,32,1024]{2,1,0:T(8,128)(2,1)S(1)}, u32[]{:S(2)}, u32[]{:S(2)}) collective-permute-start(bf16[4,32,1024]{2,1,0:T(8,128)(2,1)S(1)} %get-tuple-element.93), channel_id=1, source_target_pairs={{0,2},{1,3},{2,0},{3,1},{4,6},{5,7},{6,4},{7,5},{8,10},{9,11},{10,... | collective-permute-start | bytes 786440 | tf_op jit(solution)/shard_map/ppermute | solution.py:49
  142.0 15.0 %collective-permute-start.31 = (bf16[256,1024]{1,0:T(8,128)(2,1)S(1)}, bf16[256,1024]{1,0:T(8,128)(2,1)S(1)}, u32[]{:S(2)}, u32[]{:S(2)}) collective-permute-start(bf16[256,1024]{1,0:T(8,128)(2,1)S(1)} %get-tuple-element.100), channel_id=1, source_target_pairs={{0,4},{1,5},{2,6},{3,7},{4,12},{5,13},{6,14},{7,15},{12,8},{13,9},... | collective-permute-start | bytes 1572872 | tf_op jit(solution)/shard_map/ppermute | solution.py:52
  149.8 8.0 %collective-permute-start.29 = (bf16[256,512]{1,0:T(8,128)(2,1)S(1)}, bf16[256,512]{1,0:T(8,128)(2,1)S(1)}, u32[]{:S(2)}, u32[]{:S(2)}) collective-permute-start(bf16[256,512]{1,0:T(8,128)(2,1)S(1)} %get-tuple-element.98), channel_id=1, source_target_pairs={{0,2},{1,3},{2,0},{3,1},{4,6},{5,7},{6,4},{7,5},{8,10},{9,11},{10,... | collective-permute-start | bytes 786440 | tf_op jit(solution)/shard_map/ppermute | solution.py:49
  157.8 1.9 %collective-permute-start.32 = (bf16[256,1024]{1,0:T(8,128)(2,1)S(1)}, bf16[256,1024]{1,0:T(8,128)(2,1)S(1)}, u32[]{:S(2)}, u32[]{:S(2)}) collective-permute-start(bf16[256,1024]{1,0:T(8,128)(2,1)S(1)} %collective-permute-done.31.refs_0_), channel_id=1, source_target_pairs={{0,1},{1,0},{2,3},{3,2},{4,5},{5,4},{6,7},{7,6},{8,9},{9,8},{10,11... | collective-permute-start | bytes 1572872 | tf_op jit(solution)/shard_map/ppermute | solution.py:49
  157.8 4.4 %collective-permute-start.30 = (bf16[8,32,1024]{2,1,0:T(8,128)(2,1)S(1)}, bf16[8,32,1024]{2,1,0:T(8,128)(2,1)S(1)}, u32[]{:S(2)}, u32[]{:S(2)}) collective-permute-start(bf16[8,32,1024]{2,1,0:T(8,128)(2,1)S(1)} %constant_dynamic-update-slice_fusion.4.near), channel_id=1, source_target_pairs={{0,1},{1,0},{2,3},{3,2},{4,5},{5,4},{6,7},{7,6},{8,9},{9,8},{10,11... | collective-permute-start | bytes 1572872 | tf_op jit(solution)/shard_map/ppermute | solution.py:49
  161.2 8.4 %collective-permute-start.33 = (bf16[256,512]{1,0:T(8,128)(2,1)S(1)}, bf16[256,512]{1,0:T(8,128)(2,1)S(1)}, u32[]{:S(2)}, u32[]{:S(2)}) collective-permute-start(bf16[256,512]{1,0:T(8,128)(2,1)S(1)} %get-tuple-element.103), channel_id=1, source_target_pairs={{0,2},{1,3},{2,0},{3,1},{4,6},{5,7},{6,4},{7,5},{8,10},{9,11},{10,... | collective-permute-start | bytes 786440 | tf_op jit(solution)/shard_map/ppermute | solution.py:49

commit v16 on v14

--- a/solution.py
+++ b/solution.py
@@ -238,7 +238,7 @@
     return copies
 
 
-def weight_kernel(lay, rows, s, low, parts, came, first, *refs):
+def weight_kernel(lay, rows, s, low, height, parts, came, first, *refs):
     sides = lay.sides
     mine, refs = refs[:parts], refs[parts:]
     theirs, refs = refs[:parts], refs[parts:]
@@ -251,7 +251,6 @@
     if sides == 2:
         far, refs = refs[0], refs[1:]
     own, sems, came_sems = refs
-    height = mine[0].shape[0]
     width = parts * height
     side = (lax.axis_index("dp") // 2) % sides
     copies = []
@@ -267,7 +266,7 @@
             for p, piece in enumerate(group):
                 target[:, k * width + p * height : k * width + (p + 1) * height] = lax.dot_general(
                     grads[x][...],
-                    piece[...],
+                    piece[...] if piece.shape[0] == height else piece[low : low + height, :],
                     (((1,), (1,)), ((), ())),
                     preferred_element_type=f32,
                 ).astype(bf16)
@@ -377,10 +376,9 @@
         state = {"out": None}
         waiting = []
 
-        def multiply(s, mine, theirs, low=0, gate=None):
+        def multiply(s, mine, theirs, low=0, gate=None, wide=rows):
             args = [mine if gate is None else after(mine, gate), theirs] + side_grads
             in_specs = [VMEM] * len(args)
-            wide = mine.shape[0]
             came = None
             if len(waiting) > 1:
                 (came, block) = waiting.pop(0)
@@ -395,7 +393,7 @@
                 shapes.append(((tokens, 2 * wide), bf16))
                 out_specs.append(VMEM)
             result = call(
-                functools.partial(weight_kernel, lay, rows, s, low, 1, came, first),
+                functools.partial(weight_kernel, lay, rows, s, low, wide, 1, came, first),
                 "weight",
                 shapes,
                 args,
@@ -462,33 +460,30 @@
             [total] + came,
         )
         their_step = swap(weight[2], 1)
-        messages = message
+        messages = after(message, later) if sides == 2 else message
         for bit, radix in reversed(rounds):
             if bit >= members:
                 came = [swap(messages, j * bit) for j in range(1, radix)]
                 messages = jnp.concatenate([messages] + came, axis=0)
 
-        split = [weight[2][p * height : (p + 1) * height] for p in range(parts)] if ring == 4 else []
-        last = [onward(after(piece, *came)) for piece in split[:1]]
-        block = multiply(2, weight[2], their_step, gate=owned_rows)
+        block = multiply(2, weight[2], their_step, gate=gives[0])
+        if ring == 4:
+            weight.append(onward(after(weight[2], *came)))
         (square,) = call(gathered_kernel, "gathered", [((8, 128), f32)], [messages])
         if sides == 2:
-            sent = give_back(2, block, gate=later)
-            square = after(square, sent)
+            square = after(square, block)
         squares = [square] + [swap(square, x) for x in range(1, members)]
-        last += [onward(after(piece, square)) for piece in split[1:]]
         new_first, new_second, update = call(
             functools.partial(moment_kernel, lay, rows),
             "moment",
             [((owned, outs), f32), ((owned, outs), f32), ((ring, owned, outs), bf16)],
             squares + basis + [owned_rows, first_moment, second_moment, messages],
         )
+        sent = give_back(2, block, gate=squares[-1])
         whole = update
         for bit, radix in reversed(rounds[1:]):
             if bit < members:
-                whole = jnp.concatenate(
-                    [whole] + [swap(whole, j * bit) for j in range(1, radix)], axis=0
-                )
+                whole = jnp.concatenate([whole, swap(whole, bit)], axis=0)
         (new_master,) = call(
             functools.partial(back_kernel, lay, owned),
             "back",
@@ -499,14 +494,14 @@
             moved=8 * 2**20,
         )
 
-        for p in range(len(split)):
-            piece = after(last[p], update if p == 0 else sent)
-            block = multiply(3, piece, swap(piece, 1), p * height)
-            sent = give_back(3, block, p * height, whole if p == 0 else None)
-        if not split:
-            for s in range(3, ring):
+        for s in range(3, ring):
+            if len(weight) <= s:
                 weight.append(onward(weight[s - 1]))
-                give_back(s, multiply(s, weight[s], swap(weight[s], 1)))
+            mine = after(weight[s], whole, sent)
+            other = swap(mine, 1)
+            for p in range(parts):
+                block = multiply(s, mine, other, p * height, wide=height)
+                give_back(s, block, p * height)
         activation_grad = state["out"]
         if waiting:
             (activation_grad,) = call(

time: 171 us -> 178 us (1.041)
  waiting for transfers between devices: 113 us -> 123 us
  starting transfers between devices: 34.5 us -> 30.4 us
    ppermute x27 -> x26, waiting for transfers between devices: 45.9 us -> 61.4 us  [swap(): return lax.ppermute(value, 'dp', [(i, i ^ bit) for i in range(self.n)])]
    ppermute x7 -> x6, waiting for transfers between devices: 67.2 us -> 62.1 us  [onward(): return lax.ppermute(value, 'dp', self.forward)]
    ppermute x27 -> x26, starting transfers between devices: 27.4 us -> 23.7 us  [swap(): return lax.ppermute(value, 'dp', [(i, i ^ bit) for i in range(self.n)])]
    ppermute x7 -> x6, starting transfers between devices: 7.05 us -> 6.71 us  [onward(): return lax.ppermute(value, 'dp', self.forward)]
  transfers between devices with their start and end apart: 34 -> 32, of which waited for: 20 -> 22; matrix products, arithmetic and copies ran while one was open for 0% -> 0% of each run, Pallas kernels for 10% -> 10%
where the time goes in v16:
time: 178 us
  waiting for transfers between devices  123 us (69%)
  starting transfers between devices  30.4 us (17%)
  Pallas kernels  18.9 us (11%)
  local copies, waits for them, and re-layouts  3.42 us (2%)
    ppermute x6, waiting for transfers between devices, onward(): return lax.ppermute(value, 'dp', self.forward)  62.1 us
    ppermute x26, waiting for transfers between devices, swap(): return lax.ppermute(value, 'dp', [(i, i ^ bit) for i in range(self.n)])  61.4 us
    ppermute x26, starting transfers between devices, swap(): return lax.ppermute(value, 'dp', [(i, i ^ bit) for i in range(self.n)])  23.7 us
    pallas_call x14, Pallas kernels, call(): pl.pallas_call(kernel, name=name, out_shape=[jax.ShapeDtypeStruct(shape,...  18.9 us
    ppermute x6, starting transfers between devices, onward(): return lax.ppermute(value, 'dp', self.forward)  6.71 us
  transfers between devices with their start and end apart: 32, of which 22 were waited for; matrix products, arithmetic and copies ran while one was open for 0% of the time, Pallas kernels for 10%

profile of v16, /device:TPU:0, one launch (start us, length us, event | category | flops | bytes accessed | tf_op | source)
XLA Modules:
  0.0 177.6 jit_solution(2207930143434934494)
XLA Ops:
  0.6 1.0 copy-done
  1.7 2.2 %copy-done.3 = bf16[256,8192]{1,0:T(8,128)(2,1)S(1)} copy-done((bf16[256,8192]{1,0:T(8,128)(2,1)S(1)}, bf16[256,8192]{1,0:T(8,128)(2,1)}, u32[]{:S(2)}) %copy-start.3) | copy-done | bytes 4194328
  3.9 0.7 cut.1
  4.5 3.0 %collective-permute-start.5 = (bf16[256,3072]{1,0:T(8,128)(2,1)S(1)}, bf16[256,3072]{1,0:T(8,128)(2,1)S(1)}, u32[]{:S(2)}, u32[]{:S(2)}) collective-permute-start(bf16[256,3072]{1,0:T(8,128)(2,1)S(1)} %get-tuple-element.57), channel_id=1, source_target_pairs={{0,2},{1,3},{2,0},{3,1},{4,6},{5,7},{6,4},{7,5},{8,10},{9,11},{10,... | collective-permute-start | bytes 4718600 | tf_op jit(solution)/shard_map/ppermute | solution.py:49
  7.7 1.6 collective-permute-start
  9.3 15.5 %collective-permute-done.refs_5_ = bf16[640,512]{1,0:T(8,128)(2,1)S(1)} collective-permute-done((bf16[640,512]{1,0:T(8,128)(2,1)S(1)}, bf16[640,512]{1,0:T(8,128)(2,1)S(1)}, u32[]{:S(2)}, u32[]{:S(2)}) %collective-permute-start) | collective-permute-done | bytes 655392 | tf_op jit(solution)/shard_map/ppermute | solution.py:52
  24.8 0.8 collective-permute-start.1
  25.9 15.1 %collective-permute-done.1.refs_6_ = bf16[640,512]{1,0:T(8,128)(2,1)S(1)} collective-permute-done((bf16[640,512]{1,0:T(8,128)(2,1)S(1)}, bf16[640,512]{1,0:T(8,128)(2,1)S(1)}, u32[]{:S(2)}, u32[]{:S(2)}) %collective-permute-start.1) | collective-permute-done | bytes 655392 | tf_op jit(solution)/shard_map/ppermute | solution.py:52
  41.0 0.8 collective-permute-start.2
  42.7 1.4 collective-permute-start.7
  44.1 12.2 %collective-permute-done.2.refs_7_ = bf16[640,512]{1,0:T(8,128)(2,1)S(1)} collective-permute-done((bf16[640,512]{1,0:T(8,128)(2,1)S(1)}, bf16[640,512]{1,0:T(8,128)(2,1)S(1)}, u32[]{:S(2)}, u32[]{:S(2)}) %collective-permute-start.2) | collective-permute-done | bytes 655392 | tf_op jit(solution)/shard_map/ppermute | solution.py:52
  56.3 0.8 collective-permute-start.3
  57.1 2.1 %weight.5 = (bf16[256,8192]{1,0:T(8,128)(2,1)}, bf16[256,1024]{1,0:T(8,128)(2,1)S(1)}) custom-call(bf16[512,1024]{1,0:T(8,128)(2,1)S(1)} %convert_element_type.4.refs_0_, bf16[512,1024]{1,0:T(8,128)(2,1)S(1)} %collective-permute-done.4.refs_1_, bf16[256,1024]{1,0:T(8,128)(2,1)S(1)} %copy-done, bf16[256,1024]{1,0:T(8,128)(2,1)S(1)} %slice.17.refs_3_.refs_10_), custom_call_target="tpu_custom_call" | custom-call | flops 1073741824 | bytes 6291456 | tf_op jit(solution)/shard_map/weight/pallas_call | solution.py:317
  59.3 8.5 %collective-permute-done.7.refs_3_ = bf16[256,2048]{1,0:T(8,128)(2,1)S(1)} collective-permute-done((bf16[256,2048]{1,0:T(8,128)(2,1)S(1)}, bf16[256,2048]{1,0:T(8,128)(2,1)S(1)}, u32[]{:S(2)}, u32[]{:S(2)}) %collective-permute-start.7) | collective-permute-done | bytes 1048608 | tf_op jit(solution)/shard_map/ppermute | solution.py:49
  67.8 4.3 %project.1 = (f32[8,32,1024]{2,1,0:T(8,128)S(1)}, bf16[8,32,1024]{2,1,0:T(8,128)(2,1)S(1)}) custom-call(bf16[256,2048]{1,0:T(8,128)(2,1)S(1)} %get-tuple-element.60.refs_0_, bf16[256,2048]{1,0:T(8,128)(2,1)S(1)} %collective-permute-done.6.refs_1_, bf16[256,3072]{1,0:T(8,128)(2,1)S(1)} %collective-permute-done.5.refs_2_, ...), custom_call_target="tpu_custom_call" | custom-call | flops 3221225472 | bytes 12582912 | tf_op jit(solution)/shard_map/project/pallas_call | solution.py:317
  72.2 6.9 %collective-permute-done.3.refs_0_ = bf16[512,1024]{1,0:T(8,128)(2,1)S(1)} collective-permute-done((bf16[512,1024]{1,0:T(8,128)(2,1)S(1)}, bf16[512,1024]{1,0:T(8,128)(2,1)S(1)}, u32[]{:S(2)}, u32[]{:S(2)}) %collective-permute-start.3) | collective-permute-done | bytes 1048608 | tf_op jit(solution)/shard_map/ppermute | solution.py:52
  79.0 0.5 collective-permute-start.10
  79.5 0.8 collective-permute-start.9
  80.3 2.1 %collective-permute-done.10.refs_1_ = bf16[8,32,1024]{2,1,0:T(8,128)(2,1)S(1)} collective-permute-done((bf16[8,32,1024]{2,1,0:T(8,128)(2,1)S(1)}, bf16[8,32,1024]{2,1,0:T(8,128)(2,1)S(1)}, u32[]{:S(2)}, u32[]{:S(2)}) %collective-permute-start.10) | collective-permute-done | bytes 524320 | tf_op jit(solution)/shard_map/ppermute | solution.py:49
  82.5 1.7 collective-permute-start.12
  84.2 2.1 %weight.6 = (bf16[256,8192]{1,0:T(8,128)(2,1)}, bf16[256,1024]{1,0:T(8,128)(2,1)S(1)}) custom-call(bf16[512,1024]{1,0:T(8,128)(2,1)S(1)} %collective-permute-done.3.refs_0_, bf16[512,1024]{1,0:T(8,128)(2,1)S(1)} %collective-permute-done.11.refs_1_, bf16[256,1024]{1,0:T(8,128)(2,1)S(1)} %copy-done.1, ...), custom_call_target="tpu_custom_call", output_to_operand_aliasing={{0}: (4, {})} | custom-call | flops 1073741824 | bytes 6291456 | tf_op jit(solution)/shard_map/weight/pallas_call | solution.py:317
  86.3 4.6 %collective-permute-done.12.refs_1_ = bf16[4,32,1024]{2,1,0:T(8,128)(2,1)S(1)} collective-permute-done((bf16[4,32,1024]{2,1,0:T(8,128)(2,1)S(1)}, bf16[4,32,1024]{2,1,0:T(8,128)(2,1)S(1)}, u32[]{:S(2)}, u32[]{:S(2)}) %collective-permute-start.12) | collective-permute-done | bytes 262176 | tf_op jit(solution)/shard_map/ppermute | solution.py:49
  91.0 1.7 collective-permute-start.13
  93.1 12.4 %collective-permute-done.9.refs_0_ = bf16[512,1024]{1,0:T(8,128)(2,1)S(1)} collective-permute-done((bf16[512,1024]{1,0:T(8,128)(2,1)S(1)}, bf16[512,1024]{1,0:T(8,128)(2,1)S(1)}, u32[]{:S(2)}, u32[]{:S(2)}) %collective-permute-start.9) | collective-permute-done | bytes 1048608 | tf_op jit(solution)/shard_map/ppermute | solution.py:52
  105.9 3.6 %collective-permute-start.16 = (bf16[1,32,1024]{2,1,0:T(8,128)(2,1)S(1)}, bf16[1,32,1024]{2,1,0:T(8,128)(2,1)S(1)}, u32[]{:S(2)}, u32[]{:S(2)}) collective-permute-start(bf16[1,32,1024]{2,1,0:T(8,128)(2,1)S(1)} %get-tuple-element.80), channel_id=1, source_target_pairs={{0,12},{1,13},{2,14},{3,15},{4,8},{5,9},{6,10},{7,11},{8,4},{9,5},... | collective-permute-start | bytes 196616 | tf_op jit(solution)/shard_map/ppermute | solution.py:49
  109.5 0.8 collective-permute-start.14
  110.3 2.3 %collective-permute-done.16.refs_3_ = bf16[1,32,1024]{2,1,0:T(8,128)(2,1)S(1)} collective-permute-done((bf16[1,32,1024]{2,1,0:T(8,128)(2,1)S(1)}, bf16[1,32,1024]{2,1,0:T(8,128)(2,1)S(1)}, u32[]{:S(2)}, u32[]{:S(2)}) %collective-permute-start.16) | collective-permute-done | bytes 65568 | tf_op jit(solution)/shard_map/ppermute | solution.py:49
  112.6 2.6 %collective-permute-done.15.refs_2_ = bf16[1,32,1024]{2,1,0:T(8,128)(2,1)S(1)} collective-permute-done((bf16[1,32,1024]{2,1,0:T(8,128)(2,1)S(1)}, bf16[1,32,1024]{2,1,0:T(8,128)(2,1)S(1)}, u32[]{:S(2)}, u32[]{:S(2)}) %collective-permute-start.15) | collective-permute-done | bytes 65568 | tf_op jit(solution)/shard_map/ppermute | solution.py:49
  115.5 1.7 collective-permute-start.18
  117.1 2.4 %collective-permute-start.19 = (bf16[1,48,1024]{2,1,0:T(8,128)(2,1)S(1)}, bf16[1,48,1024]{2,1,0:T(8,128)(2,1)S(1)}, u32[]{:S(2)}, u32[]{:S(2)}) collective-permute-start(bf16[1,48,1024]{2,1,0:T(8,128)(2,1)S(1)} %get-tuple-element.83), channel_id=1, source_target_pairs={{0,8},{1,9},{2,10},{3,11},{4,12},{5,13},{6,14},{7,15},{8,0},{9,1},... | collective-permute-start | bytes 294920 | tf_op jit(solution)/shard_map/ppermute | solution.py:49
  120.3 6.7 %collective-permute-done.19 = bf16[1,48,1024]{2,1,0:T(8,128)(2,1)S(1)} collective-permute-done((bf16[1,48,1024]{2,1,0:T(8,128)(2,1)S(1)}, bf16[1,48,1024]{2,1,0:T(8,128)(2,1)S(1)}, u32[]{:S(2)}, u32[]{:S(2)}) %collective-permute-start.19) | collective-permute-done | bytes 98336 | tf_op jit(solution)/shard_map/ppermute | solution.py:49
  126.9 1.9 %collective-permute-start.21 = (bf16[512,1024]{1,0:T(8,128)(2,1)S(1)}, bf16[512,1024]{1,0:T(8,128)(2,1)S(1)}, u32[]{:S(2)}, u32[]{:S(2)}) collective-permute-start(bf16[512,1024]{1,0:T(8,128)(2,1)S(1)} %collective-permute-done.9.refs_0_), channel_id=1, source_target_pairs={{0,4},{1,5},{2,6},{3,7},{4,12},{5,13},{6,14},{7,15},{12,8},{13,9},... | collective-permute-start | bytes 3145736 | tf_op jit(solution)/shard_map/ppermute | solution.py:52
  129.1 2.1 %weight.7 = (bf16[256,8192]{1,0:T(8,128)(2,1)}, bf16[256,1024]{1,0:T(8,128)(2,1)S(1)}) custom-call(bf16[512,1024]{1,0:T(8,128)(2,1)S(1)} %collective-permute-done.9.refs_0_, bf16[512,1024]{1,0:T(8,128)(2,1)S(1)} %collective-permute-done.22.refs_1_, bf16[256,1024]{1,0:T(8,128)(2,1)S(1)} %copy-done.1, ...), custom_call_target="tpu_custom_call", output_to_operand_aliasing={{0}: (5, {})} | custom-call | flops 1073741824 | bytes 6291456 | tf_op jit(solution)/shard_map/weight/pallas_call | solution.py:317
  131.3 3.0 %collective-permute-done.25.refs_3_ = f32[8,128]{1,0:T(8,128)S(1)} collective-permute-done((f32[8,128]{1,0:T(8,128)S(1)}, f32[8,128]{1,0:T(8,128)S(1)}, u32[]{:S(2)}, u32[]{:S(2)}) %collective-permute-start.25) | collective-permute-done | bytes 4128 | tf_op jit(solution)/shard_map/ppermute | solution.py:49
  134.3 1.4 collective-permute-start.27
  135.7 0.7 collective-permute-start.24
  136.8 11.4 %collective-permute-done.24.refs_2_ = f32[8,128]{1,0:T(8,128)S(1)} collective-permute-done((f32[8,128]{1,0:T(8,128)S(1)}, f32[8,128]{1,0:T(8,128)S(1)}, u32[]{:S(2)}, u32[]{:S(2)}) %collective-permute-start.24) | collective-permute-done | bytes 4128 | tf_op jit(solution)/shard_map/ppermute | solution.py:49
  148.3 1.1 moment.1
  149.4 0.7 collective-permute-start.26
  150.1 6.7 %collective-permute-done.26 = bf16[4,32,1024]{2,1,0:T(8,128)(2,1)S(1)} collective-permute-done((bf16[4,32,1024]{2,1,0:T(8,128)(2,1)S(1)}, bf16[4,32,1024]{2,1,0:T(8,128)(2,1)S(1)}, u32[]{:S(2)}, u32[]{:S(2)}) %collective-permute-start.26) | collective-permute-done | bytes 262176 | tf_op jit(solution)/shard_map/ppermute | solution.py:49
  157.4 2.1 %collective-permute-done.28.refs_1_ = bf16[512,1024]{1,0:T(8,128)(2,1)S(1)} collective-permute-done((bf16[512,1024]{1,0:T(8,128)(2,1)S(1)}, bf16[512,1024]{1,0:T(8,128)(2,1)S(1)}, u32[]{:S(2)}, u32[]{:S(2)}) %collective-permute-start.28) | collective-permute-done | bytes 1048608 | tf_op jit(solution)/shard_map/ppermute | solution.py:49
  159.5 1.5 weight.8
  161.0 1.5 weight.9
  162.9 1.7 collective-permute-start.29
  164.6 2.2 %back.1 = f32[512,1024]{1,0:T(8,128)} custom-call(bf16[512,512]{1,0:T(8,128)(2,1)S(1)} %copy-done.4, bf16[8,32,1024]{2,1,0:T(8,128)(2,1)S(1)} %constant_dynamic-update-slice_fusion.4.near, bf16[8,32,1024]{2,1,0:T(8,128)(2,1)S(1)} %collective-permute-done.30.other, f32[512,1024]{1,0:T(8,128)S(1)} %copy-done.2), custom_call_target="tpu_custom_call" | custom-call | flops 536870912 | bytes 8388608 | tf_op jit(solution)/shard_map/back/pallas_call | solution.py:317
  166.8 4.9 %collective-permute-done.31.refs_1_ = bf16[256,512]{1,0:T(8,128)(2,1)S(1)} collective-permute-done((bf16[256,512]{1,0:T(8,128)(2,1)S(1)}, bf16[256,512]{1,0:T(8,128)(2,1)S(1)}, u32[]{:S(2)}, u32[]{:S(2)}) %collective-permute-start.31) | collective-permute-done | bytes 262176 | tf_op jit(solution)/shard_map/ppermute | solution.py:49
  171.8 4.8 %collective-permute-done.29.refs_0_ = bf16[256,512]{1,0:T(8,128)(2,1)S(1)} collective-permute-done((bf16[256,512]{1,0:T(8,128)(2,1)S(1)}, bf16[256,512]{1,0:T(8,128)(2,1)S(1)}, u32[]{:S(2)}, u32[]{:S(2)}) %collective-permute-start.29) | collective-permute-done | bytes 262176 | tf_op jit(solution)/shard_map/ppermute | solution.py:49
  176.6 0.8 last.1
  (58 shorter events, 4.8 us)
Async XLA Ops:
  0.6 1.0 copy-start
  1.7 2.2 %copy-start.3 = (bf16[256,8192]{1,0:T(8,128)(2,1)S(1)}, bf16[256,8192]{1,0:T(8,128)(2,1)}, u32[]{:S(2)}) copy-start(bf16[256,8192]{1,0:T(8,128)(2,1)} %act.1) | copy-start | bytes 12582916
  3.9 3.7 %copy-start.6 = (f32[32,1024]{1,0:T(8,128)S(1)}, f32[32,1024]{1,0:T(8,128)}, u32[]{:S(2)}) copy-start(f32[32,1024]{1,0:T(8,128)} %refs_9_.1) | copy-start | bytes 393220
  3.9 3.7 %copy-start.5 = (f32[32,1024]{1,0:T(8,128)S(1)}, f32[32,1024]{1,0:T(8,128)}, u32[]{:S(2)}) copy-start(f32[32,1024]{1,0:T(8,128)} %refs_10_.1) | copy-start | bytes 393220
  3.9 3.8 %copy-start.4 = (bf16[512,512]{1,0:T(8,128)(2,1)S(1)}, bf16[512,512]{1,0:T(8,128)(2,1)}, u32[]{:S(2)}) copy-start(bf16[512,512]{1,0:T(8,128)(2,1)} %basis.1) | copy-start | bytes 1572868
  3.9 21.7 %copy-start.2 = (f32[512,1024]{1,0:T(8,128)S(1)}, f32[512,1024]{1,0:T(8,128)}, u32[]{:S(2)}) copy-start(f32[512,1024]{1,0:T(8,128)} %master.1) | copy-start | bytes 6291460
  4.5 37.4 %collective-permute-start.5 = (bf16[256,3072]{1,0:T(8,128)(2,1)S(1)}, bf16[256,3072]{1,0:T(8,128)(2,1)S(1)}, u32[]{:S(2)}, u32[]{:S(2)}) collective-permute-start(bf16[256,3072]{1,0:T(8,128)(2,1)S(1)} %get-tuple-element.57), channel_id=1, source_target_pairs={{0,2},{1,3},{2,0},{3,1},{4,6},{5,7},{6,4},{7,5},{8,10},{9,11},{10,... | collective-permute-start | bytes 4718600 | tf_op jit(solution)/shard_map/ppermute | solution.py:49
  7.7 17.1 %collective-permute-start = (bf16[640,512]{1,0:T(8,128)(2,1)S(1)}, bf16[640,512]{1,0:T(8,128)(2,1)S(1)}, u32[]{:S(2)}, u32[]{:S(2)}) collective-permute-start(bf16[640,512]{1,0:T(8,128)(2,1)S(1)} %fusion.refs_4_), channel_id=1, source_target_pairs={{0,4},{1,5},{2,6},{3,7},{4,12},{5,13},{6,14},{7,15},{12,8},{13,9},... | collective-permute-start | bytes 1966088 | tf_op jit(solution)/shard_map/ppermute | solution.py:52
  24.8 16.2 %collective-permute-start.1 = (bf16[640,512]{1,0:T(8,128)(2,1)S(1)}, bf16[640,512]{1,0:T(8,128)(2,1)S(1)}, u32[]{:S(2)}, u32[]{:S(2)}) collective-permute-start(bf16[640,512]{1,0:T(8,128)(2,1)S(1)} %collective-permute-done.refs_5_), channel_id=1, source_target_pairs={{0,4},{1,5},{2,6},{3,7},{4,12},{5,13},{6,14},{7,15},{12,8},{13,9},... | collective-permute-start | bytes 1966088 | tf_op jit(solution)/shard_map/ppermute | solution.py:52
  25.8 31.3 %collective-permute-start.4 = (bf16[512,1024]{1,0:T(8,128)(2,1)S(1)}, bf16[512,1024]{1,0:T(8,128)(2,1)S(1)}, u32[]{:S(2)}, u32[]{:S(2)}) collective-permute-start(bf16[512,1024]{1,0:T(8,128)(2,1)S(1)} %convert_element_type.4.refs_0_), channel_id=1, source_target_pairs={{0,1},{1,0},{2,3},{3,2},{4,5},{5,4},{6,7},{7,6},{8,9},{9,8},{10,11... | collective-permute-start | bytes 3145736 | tf_op jit(solution)/shard_map/ppermute | solution.py:49
  41.0 15.3 %collective-permute-start.2 = (bf16[640,512]{1,0:T(8,128)(2,1)S(1)}, bf16[640,512]{1,0:T(8,128)(2,1)S(1)}, u32[]{:S(2)}, u32[]{:S(2)}) collective-permute-start(bf16[640,512]{1,0:T(8,128)(2,1)S(1)} %collective-permute-done.1.refs_6_), channel_id=1, source_target_pairs={{0,4},{1,5},{2,6},{3,7},{4,12},{5,13},{6,14},{7,15},{12,8},{13,9},... | collective-permute-start | bytes 1966088 | tf_op jit(solution)/shard_map/ppermute | solution.py:52
  42.1 17.1 %collective-permute-start.8 = (bf16[512,1024]{1,0:T(8,128)(2,1)S(1)}, bf16[512,1024]{1,0:T(8,128)(2,1)S(1)}, u32[]{:S(2)}, u32[]{:S(2)}) collective-permute-start(bf16[512,1024]{1,0:T(8,128)(2,1)S(1)} %pad_maximum_fusion), channel_id=1, source_target_pairs={{0,1},{1,0},{2,3},{3,2},{4,5},{5,4},{6,7},{7,6},{8,9},{9,8},{10,11... | collective-permute-start | bytes 3145736 | tf_op jit(solution)/shard_map/ppermute | solution.py:49
  42.2 17.1 %collective-permute-start.6 = (bf16[256,2048]{1,0:T(8,128)(2,1)S(1)}, bf16[256,2048]{1,0:T(8,128)(2,1)S(1)}, u32[]{:S(2)}, u32[]{:S(2)}) collective-permute-start(bf16[256,2048]{1,0:T(8,128)(2,1)S(1)} %get-tuple-element.61), channel_id=1, source_target_pairs={{0,1},{1,0},{2,3},{3,2},{4,5},{5,4},{6,7},{7,6},{8,9},{9,8},{10,11... | collective-permute-start | bytes 3145736 | tf_op jit(solution)/shard_map/ppermute | solution.py:49
  42.7 25.2 %copy-start.1 = (bf16[256,1024]{1,0:T(8,128)(2,1)S(1)}, bf16[256,1024]{1,0:T(8,128)(2,1)}, u32[]{:S(2)}) copy-start(bf16[256,1024]{1,0:T(8,128)(2,1)} %refs_2_.9) | copy-start | bytes 1572868
  42.7 25.2 %collective-permute-start.7 = (bf16[256,2048]{1,0:T(8,128)(2,1)S(1)}, bf16[256,2048]{1,0:T(8,128)(2,1)S(1)}, u32[]{:S(2)}, u32[]{:S(2)}) collective-permute-start(bf16[256,2048]{1,0:T(8,128)(2,1)S(1)} %get-tuple-element.62), channel_id=1, source_target_pairs={{0,3},{1,2},{2,1},{3,0},{4,7},{5,6},{6,5},{7,4},{8,11},{9,10},{10,... | collective-permute-start | bytes 3145736 | tf_op jit(solution)/shard_map/ppermute | solution.py:49
  56.3 22.8 %collective-permute-start.3 = (bf16[512,1024]{1,0:T(8,128)(2,1)S(1)}, bf16[512,1024]{1,0:T(8,128)(2,1)S(1)}, u32[]{:S(2)}, u32[]{:S(2)}) collective-permute-start(bf16[512,1024]{1,0:T(8,128)(2,1)S(1)} %convert_element_type.4.refs_0_), channel_id=1, source_target_pairs={{0,4},{1,5},{2,6},{3,7},{4,12},{5,13},{6,14},{7,15},{12,8},{13,9},... | collective-permute-start | bytes 3145736 | tf_op jit(solution)/shard_map/ppermute | solution.py:52
  79.0 5.2 %collective-permute-start.11 = (bf16[512,1024]{1,0:T(8,128)(2,1)S(1)}, bf16[512,1024]{1,0:T(8,128)(2,1)S(1)}, u32[]{:S(2)}, u32[]{:S(2)}) collective-permute-start(bf16[512,1024]{1,0:T(8,128)(2,1)S(1)} %collective-permute-done.3.refs_0_), channel_id=1, source_target_pairs={{0,1},{1,0},{2,3},{3,2},{4,5},{5,4},{6,7},{7,6},{8,9},{9,8},{10,11... | collective-permute-start | bytes 3145736 | tf_op jit(solution)/shard_map/ppermute | solution.py:49
  79.0 3.4 %collective-permute-start.10 = (bf16[8,32,1024]{2,1,0:T(8,128)(2,1)S(1)}, bf16[8,32,1024]{2,1,0:T(8,128)(2,1)S(1)}, u32[]{:S(2)}, u32[]{:S(2)}) collective-permute-start(bf16[8,32,1024]{2,1,0:T(8,128)(2,1)S(1)} %get-tuple-element.65), channel_id=1, source_target_pairs={{0,1},{1,0},{2,3},{3,2},{4,5},{5,4},{6,7},{7,6},{8,9},{9,8},{10,11... | collective-permute-start | bytes 1572872 | tf_op jit(solution)/shard_map/ppermute | solution.py:49
  79.5 26.0 %collective-permute-start.9 = (bf16[512,1024]{1,0:T(8,128)(2,1)S(1)}, bf16[512,1024]{1,0:T(8,128)(2,1)S(1)}, u32[]{:S(2)}, u32[]{:S(2)}) collective-permute-start(bf16[512,1024]{1,0:T(8,128)(2,1)S(1)} %collective-permute-done.3.refs_0_), channel_id=1, source_target_pairs={{0,4},{1,5},{2,6},{3,7},{4,12},{5,13},{6,14},{7,15},{12,8},{13,9},... | collective-permute-start | bytes 3145736 | tf_op jit(solution)/shard_map/ppermute | solution.py:52
  82.5 8.4 %collective-permute-start.12 = (bf16[4,32,1024]{2,1,0:T(8,128)(2,1)S(1)}, bf16[4,32,1024]{2,1,0:T(8,128)(2,1)S(1)}, u32[]{:S(2)}, u32[]{:S(2)}) collective-permute-start(bf16[4,32,1024]{2,1,0:T(8,128)(2,1)S(1)} %get-tuple-element.71), channel_id=1, source_target_pairs={{0,2},{1,3},{2,0},{3,1},{4,6},{5,7},{6,4},{7,5},{8,10},{9,11},{10,... | collective-permute-start | bytes 786440 | tf_op jit(solution)/shard_map/ppermute | solution.py:49
  91.0 14.9 %collective-permute-start.13 = (bf16[256,1024]{1,0:T(8,128)(2,1)S(1)}, bf16[256,1024]{1,0:T(8,128)(2,1)S(1)}, u32[]{:S(2)}, u32[]{:S(2)}) collective-permute-start(bf16[256,1024]{1,0:T(8,128)(2,1)S(1)} %get-tuple-element.73), channel_id=1, source_target_pairs={{0,2},{1,3},{2,0},{3,1},{4,6},{5,7},{6,4},{7,5},{8,10},{9,11},{10,... | collective-permute-start | bytes 1572872 | tf_op jit(solution)/shard_map/ppermute | solution.py:49
  92.7 22.8 %collective-permute-start.17 = (bf16[256,1024]{1,0:T(8,128)(2,1)S(1)}, bf16[256,1024]{1,0:T(8,128)(2,1)S(1)}, u32[]{:S(2)}, u32[]{:S(2)}) collective-permute-start(bf16[256,1024]{1,0:T(8,128)(2,1)S(1)} %get-tuple-element.82), channel_id=1, source_target_pairs={{0,2},{1,3},{2,0},{3,1},{4,6},{5,7},{6,4},{7,5},{8,10},{9,11},{10,... | collective-permute-start | bytes 1572872 | tf_op jit(solution)/shard_map/ppermute | solution.py:49
  105.9 23.2 %collective-permute-start.22 = (bf16[512,1024]{1,0:T(8,128)(2,1)S(1)}, bf16[512,1024]{1,0:T(8,128)(2,1)S(1)}, u32[]{:S(2)}, u32[]{:S(2)}) collective-permute-start(bf16[512,1024]{1,0:T(8,128)(2,1)S(1)} %collective-permute-done.9.refs_0_), channel_id=1, source_target_pairs={{0,1},{1,0},{2,3},{3,2},{4,5},{5,4},{6,7},{7,6},{8,9},{9,8},{10,11... | collective-permute-start | bytes 3145736 | tf_op jit(solution)/shard_map/ppermute | solution.py:49
  105.9 6.7 %collective-permute-start.16 = (bf16[1,32,1024]{2,1,0:T(8,128)(2,1)S(1)}, bf16[1,32,1024]{2,1,0:T(8,128)(2,1)S(1)}, u32[]{:S(2)}, u32[]{:S(2)}) collective-permute-start(bf16[1,32,1024]{2,1,0:T(8,128)(2,1)S(1)} %get-tuple-element.80), channel_id=1, source_target_pairs={{0,12},{1,13},{2,14},{3,15},{4,8},{5,9},{6,10},{7,11},{8,4},{9,5},... | collective-permute-start | bytes 196616 | tf_op jit(solution)/shard_map/ppermute | solution.py:49
  109.5 5.7 %collective-permute-start.15 = (bf16[1,32,1024]{2,1,0:T(8,128)(2,1)S(1)}, bf16[1,32,1024]{2,1,0:T(8,128)(2,1)S(1)}, u32[]{:S(2)}, u32[]{:S(2)}) collective-permute-start(bf16[1,32,1024]{2,1,0:T(8,128)(2,1)S(1)} %get-tuple-element.78), channel_id=1, source_target_pairs={{0,8},{1,9},{2,10},{3,11},{4,12},{5,13},{6,14},{7,15},{8,0},{9,1},... | collective-permute-start | bytes 196616 | tf_op jit(solution)/shard_map/ppermute | solution.py:49
  109.5 5.8 %collective-permute-start.14 = (bf16[1,32,1024]{2,1,0:T(8,128)(2,1)S(1)}, bf16[1,32,1024]{2,1,0:T(8,128)(2,1)S(1)}, u32[]{:S(2)}, u32[]{:S(2)}) collective-permute-start(bf16[1,32,1024]{2,1,0:T(8,128)(2,1)S(1)} %get-tuple-element.76), channel_id=1, source_target_pairs={{0,4},{1,5},{2,6},{3,7},{4,0},{5,1},{6,2},{7,3},{8,12},{9,13},{10,... | collective-permute-start | bytes 196616 | tf_op jit(solution)/shard_map/ppermute | solution.py:49
  115.5 4.8 %collective-permute-start.18 = (bf16[1,48,1024]{2,1,0:T(8,128)(2,1)S(1)}, bf16[1,48,1024]{2,1,0:T(8,128)(2,1)S(1)}, u32[]{:S(2)}, u32[]{:S(2)}) collective-permute-start(bf16[1,48,1024]{2,1,0:T(8,128)(2,1)S(1)} %get-tuple-element.83), channel_id=1, source_target_pairs={{0,4},{1,5},{2,6},{3,7},{4,0},{5,1},{6,2},{7,3},{8,12},{9,13},{10,... | collective-permute-start | bytes 294920 | tf_op jit(solution)/shard_map/ppermute | solution.py:49
  117.1 9.8 %collective-permute-start.19 = (bf16[1,48,1024]{2,1,0:T(8,128)(2,1)S(1)}, bf16[1,48,1024]{2,1,0:T(8,128)(2,1)S(1)}, u32[]{:S(2)}, u32[]{:S(2)}) collective-permute-start(bf16[1,48,1024]{2,1,0:T(8,128)(2,1)S(1)} %get-tuple-element.83), channel_id=1, source_target_pairs={{0,8},{1,9},{2,10},{3,11},{4,12},{5,13},{6,14},{7,15},{8,0},{9,1},... | collective-permute-start | bytes 294920 | tf_op jit(solution)/shard_map/ppermute | solution.py:49
  119.6 7.4 %collective-permute-start.20 = (bf16[1,48,1024]{2,1,0:T(8,128)(2,1)S(1)}, bf16[1,48,1024]{2,1,0:T(8,128)(2,1)S(1)}, u32[]{:S(2)}, u32[]{:S(2)}) collective-permute-start(bf16[1,48,1024]{2,1,0:T(8,128)(2,1)S(1)} %get-tuple-element.83), channel_id=1, source_target_pairs={{0,12},{1,13},{2,14},{3,15},{4,8},{5,9},{6,10},{7,11},{8,4},{9,5},... | collective-permute-start | bytes 294920 | tf_op jit(solution)/shard_map/ppermute | solution.py:49
  126.9 29.9 %collective-permute-start.21 = (bf16[512,1024]{1,0:T(8,128)(2,1)S(1)}, bf16[512,1024]{1,0:T(8,128)(2,1)S(1)}, u32[]{:S(2)}, u32[]{:S(2)}) collective-permute-start(bf16[512,1024]{1,0:T(8,128)(2,1)S(1)} %collective-permute-done.9.refs_0_), channel_id=1, source_target_pairs={{0,4},{1,5},{2,6},{3,7},{4,12},{5,13},{6,14},{7,15},{12,8},{13,9},... | collective-permute-start | bytes 3145736 | tf_op jit(solution)/shard_map/ppermute | solution.py:52
  131.2 3.1 %collective-permute-start.25 = (f32[8,128]{1,0:T(8,128)S(1)}, f32[8,128]{1,0:T(8,128)S(1)}, u32[]{:S(2)}, u32[]{:S(2)}) collective-permute-start(f32[8,128]{1,0:T(8,128)S(1)} %gathered.1.refs_0_), channel_id=1, source_target_pairs={{0,3},{1,2},{2,1},{3,0},{4,7},{5,6},{6,5},{7,4},{8,11},{9,10},{10,... | collective-permute-start | bytes 12296 | tf_op jit(solution)/shard_map/ppermute | solution.py:49
  134.3 22.5 %collective-permute-start.27 = (bf16[256,1024]{1,0:T(8,128)(2,1)S(1)}, bf16[256,1024]{1,0:T(8,128)(2,1)S(1)}, u32[]{:S(2)}, u32[]{:S(2)}) collective-permute-start(bf16[256,1024]{1,0:T(8,128)(2,1)S(1)} %get-tuple-element.91), channel_id=1, source_target_pairs={{0,2},{1,3},{2,0},{3,1},{4,6},{5,7},{6,4},{7,5},{8,10},{9,11},{10,... | collective-permute-start | bytes 1572872 | tf_op jit(solution)/shard_map/ppermute | solution.py:49
  135.7 1.2 collective-permute-start.23
  135.7 12.6 %collective-permute-start.24 = (f32[8,128]{1,0:T(8,128)S(1)}, f32[8,128]{1,0:T(8,128)S(1)}, u32[]{:S(2)}, u32[]{:S(2)}) collective-permute-start(f32[8,128]{1,0:T(8,128)S(1)} %gathered.1.refs_0_), channel_id=1, source_target_pairs={{0,2},{1,3},{2,0},{3,1},{4,6},{5,7},{6,4},{7,5},{8,10},{9,11},{10,... | collective-permute-start | bytes 12296 | tf_op jit(solution)/shard_map/ppermute | solution.py:49
  149.4 7.4 %collective-permute-start.26 = (bf16[4,32,1024]{2,1,0:T(8,128)(2,1)S(1)}, bf16[4,32,1024]{2,1,0:T(8,128)(2,1)S(1)}, u32[]{:S(2)}, u32[]{:S(2)}) collective-permute-start(bf16[4,32,1024]{2,1,0:T(8,128)(2,1)S(1)} %get-tuple-element.90), channel_id=1, source_target_pairs={{0,2},{1,3},{2,0},{3,1},{4,6},{5,7},{6,4},{7,5},{8,10},{9,11},{10,... | collective-permute-start | bytes 786440 | tf_op jit(solution)/shard_map/ppermute | solution.py:49
  156.8 2.7 %collective-permute-start.28 = (bf16[512,1024]{1,0:T(8,128)(2,1)S(1)}, bf16[512,1024]{1,0:T(8,128)(2,1)S(1)}, u32[]{:S(2)}, u32[]{:S(2)}) collective-permute-start(bf16[512,1024]{1,0:T(8,128)(2,1)S(1)} %collective-permute-done.21.refs_0_), channel_id=1, source_target_pairs={{0,1},{1,0},{2,3},{3,2},{4,5},{5,4},{6,7},{7,6},{8,9},{9,8},{10,11... | collective-permute-start | bytes 3145736 | tf_op jit(solution)/shard_map/ppermute | solution.py:49
  156.9 7.8 %collective-permute-start.30 = (bf16[8,32,1024]{2,1,0:T(8,128)(2,1)S(1)}, bf16[8,32,1024]{2,1,0:T(8,128)(2,1)S(1)}, u32[]{:S(2)}, u32[]{:S(2)}) collective-permute-start(bf16[8,32,1024]{2,1,0:T(8,128)(2,1)S(1)} %constant_dynamic-update-slice_fusion.4.near), channel_id=1, source_target_pairs={{0,1},{1,0},{2,3},{3,2},{4,5},{5,4},{6,7},{7,6},{8,9},{9,8},{10,11... | collective-permute-start | bytes 1572872 | tf_op jit(solution)/shard_map/ppermute | solution.py:49
  162.5 9.2 %collective-permute-start.31 = (bf16[256,512]{1,0:T(8,128)(2,1)S(1)}, bf16[256,512]{1,0:T(8,128)(2,1)S(1)}, u32[]{:S(2)}, u32[]{:S(2)}) collective-permute-start(bf16[256,512]{1,0:T(8,128)(2,1)S(1)} %get-tuple-element.97), channel_id=1, source_target_pairs={{0,2},{1,3},{2,0},{3,1},{4,6},{5,7},{6,4},{7,5},{8,10},{9,11},{10,... | collective-permute-start | bytes 786440 | tf_op jit(solution)/shard_map/ppermute | solution.py:49
  162.9 13.7 %collective-permute-start.29 = (bf16[256,512]{1,0:T(8,128)(2,1)S(1)}, bf16[256,512]{1,0:T(8,128)(2,1)S(1)}, u32[]{:S(2)}, u32[]{:S(2)}) collective-permute-start(bf16[256,512]{1,0:T(8,128)(2,1)S(1)} %get-tuple-element.94), channel_id=1, source_target_pairs={{0,2},{1,3},{2,0},{3,1},{4,6},{5,7},{6,4},{7,5},{8,10},{9,11},{10,... | collective-permute-start | bytes 786440 | tf_op jit(solution)/shard_map/ppermute | solution.py:49
